TPU v7x, 32 devices: a whole 2x2x4 slice. The times are simulated.
32 devices in a mesh: groups: 2 (over x), wide: 4 (over y, core), narrow: 4 (over z).
Axes of the slice: x: 2, y: 2, z: 4, core: 2. Of those that a mesh axis runs over, the one named last changes fastest.
Arguments:
- activations: bfloat16 [128, 18432], P('groups', 'wide'), parts along dimension 0, may hold values from -160 to 160
- norm_gain: float32 [18432], P('wide'), may hold values from 0.1 to 1.9
- query_weight: bfloat16 [18432, 12288], P('wide', 'narrow'), may hold values from -0.046875 to 0.046875
- kv_weight: bfloat16 [18432, 512], P(('wide', 'narrow')), may hold values from -0.046875 to 0.046875
- out_weight: bfloat16 [12288, 18432], P('narrow', 'wide'), may hold values from -0.375 to 0.375
- kv_cache: bfloat16 [128, 1024, 512], P(('groups', 'wide', 'narrow')), parts along dimension 0, may hold values from -128 to 128
- lengths: int32 [128], P(('groups', 'wide', 'narrow')), parts along dimension 0, may hold values from 1 to 1024, as said below
Outputs:
- attended: bfloat16 [128, 18432], P(('groups', 'narrow'), 'wide'), parts along dimension 0
There are 2 independent parts, one for each index of `groups`. A program takes and returns all parts, laid end to end along the dimension named above; an argument that names none is the same for every part. Nothing has to cross between parts.
Inputs may be any that keep to these rules, and one draw needn't show every extreme that they name: `lengths`: each row names how many leading cache positions hold its history; some row uses all 1024.
All inputs are finite; a program needn't handle non-finite values.
Results may differ from a plain program's by a relative error of at most 0.00585.
The roundings to bfloat16 on the way count: a program that leaves them out, or rounds other values in their place, can miss the bound.
Values may be sent and summed in bfloat16 or wider, within the bound.
No kernel may reach another device: no remote copies, remote signals or barrier semaphores. Data moves between devices by JAX's collectives and lax.ppermute only.
A program may use at most 128 MiB of HBM per device.

v0:
```python
import math

import jax
import jax.numpy as jnp
from jax import lax
from jax.sharding import PartitionSpec as P


def attend(queries, kv_cache, fresh, lengths):
    row_count = queries.shape[0]
    head_dim = kv_cache.shape[2] // 2
    head_count = queries.shape[1] // head_dim
    scaling = 1.0 / math.sqrt(head_dim)
    query_heads = queries.reshape(row_count, head_count, head_dim)
    new_keys = fresh[:, :head_dim]
    new_values = fresh[:, head_dim:]
    own_score = (
        jnp.einsum("rhd,rd->rh", query_heads, new_keys, preferred_element_type=jnp.float32)
        * scaling
    )

    def block_scores(block):
        width = block.shape[1]
        scores = (
            jnp.einsum(
                "rhd,rld->rhl",
                query_heads,
                block[:, :, :head_dim],
                preferred_element_type=jnp.float32,
            )
            * scaling
        )
        positions = jnp.arange(width, dtype=jnp.int32)
        valid = positions[None, :] < lengths[:, None]
        return (scores, valid[:, None, :])

    scores, valid = block_scores(kv_cache)
    top = jnp.maximum(jnp.max(jnp.where(valid, scores, -jnp.inf), axis=2), own_score)
    scores, valid = block_scores(kv_cache)
    weights = jnp.where(valid, jnp.exp(scores - top[..., None]), 0.0)
    numer = jnp.einsum(
        "rhl,rld->rhd",
        weights.astype(jnp.bfloat16),
        kv_cache[:, :, head_dim:],
        preferred_element_type=jnp.float32,
    )
    total, numer = (jnp.sum(weights, axis=2), numer)
    own_weight = jnp.exp(own_score - top)
    total = total + own_weight
    own_rounded = lax.optimization_barrier(own_weight.astype(jnp.bfloat16)).astype(jnp.float32)
    numer = numer + own_rounded[..., None] * new_values.astype(jnp.float32)[:, None, :]
    return (numer / total[..., None]).astype(jnp.bfloat16).reshape(row_count, head_count * head_dim)


def local(activations, norm_gain, query_weight, kv_weight, out_weight, kv_cache, lengths):
    wide_count = lax.axis_size("wide")
    narrow_count = lax.axis_size("narrow")
    values = activations.astype(jnp.float32)
    width_all = activations.shape[1] * wide_count
    sums, squares = lax.psum((jnp.sum(values, axis=1), jnp.sum(values * values, axis=1)), "wide")
    center = sums / width_all
    spread = squares / width_all - center * center
    normed = (
        (values - center[:, None]) * lax.rsqrt(spread + 1e-05)[:, None] * norm_gain[None, :]
    ).astype(jnp.bfloat16)
    summed = lax.psum_scatter(
        jnp.dot(normed, query_weight, preferred_element_type=jnp.float32),
        "wide",
        scatter_dimension=0,
        tiled=True,
    ).astype(jnp.bfloat16)
    queries = lax.all_to_all(summed, "narrow", split_axis=0, concat_axis=1, tiled=True)
    sub_width = normed.shape[1] // narrow_count
    own_columns = lax.dynamic_slice_in_dim(
        normed, lax.axis_index("narrow") * sub_width, sub_width, 1
    )
    fresh = lax.psum_scatter(
        jnp.dot(own_columns, kv_weight, preferred_element_type=jnp.float32),
        ("wide", "narrow"),
        scatter_dimension=0,
        tiled=True,
    ).astype(jnp.bfloat16)
    context = attend(queries, kv_cache, fresh, lengths)
    returned = lax.all_to_all(context, "narrow", split_axis=1, concat_axis=0, tiled=True)
    gathered = lax.all_gather(returned, "wide", axis=0, tiled=True)
    return lax.psum_scatter(
        jnp.dot(gathered, out_weight, preferred_element_type=jnp.float32),
        "narrow",
        scatter_dimension=0,
        tiled=True,
    ).astype(jnp.bfloat16)


def solution(mesh):
    return jax.shard_map(
        local,
        mesh=mesh,
        in_specs=(
            P("groups", "wide"),
            P("wide"),
            P("wide", "narrow"),
            P(("wide", "narrow"), None),
            P("narrow", "wide"),
            P(("groups", "wide", "narrow"), None, None),
            P(("groups", "wide", "narrow")),
        ),
        out_specs=P(("groups", "narrow"), "wide"),
        check_vma=False,
    )
```

profile of v0, /device:TPU:0, one launch (start us, length us, event | category | flops | bytes accessed | tf_op | source)
XLA Modules:
  0.0 173.3 jit_solution(4696629181915925910)
XLA Ops:
  6.5 0.0 copy-start
  6.5 0.0 reduce-scatter.3.cloned.1.call-start
  6.5 1.4 convert_reduce_fusion
  8.0 8.4 %all-reduce.1 = (f32[64]{0:T(128)S(1)}, f32[64]{0:T(128)S(1)}) all-reduce(f32[64]{0:T(128)S(1)} %get-tuple-element.6, f32[64]{0:T(128)S(1)} %get-tuple-element.5), channel_id=1, replica_groups=mesh['groups'=2,'wide'=4,'narrow'=4] {'wide'}, use_global_device_ids=true, to_apply=%region_3.0 | all-reduce | flops 128 | bytes 1024 | tf_op jit(solution)/shard_map/psum | solution.py:60
  16.3 1.3 fusion.9
  17.6 12.6 %fusion.34 = f32[64,3072]{1,0:T(8,128)} fusion(bf16[64,4608]{1,0:T(8,128)(2,1)S(1)} %fusion.9, bf16[4608,3072]{1,0:T(8,128)(2,1)} %param.9), kind=kOutput, calls=%fused_computation.38 | convolution fusion | flops 1811939328 | bytes 29687808 | tf_op jit(solution)/shard_map/dot_general | solution.py:67
  30.2 0.0 reduce-scatter.3.cloned.1.call-update
  30.3 0.0 copy-done
  30.3 0.3 fusion.26
  30.6 0.3 copy-done.3
  30.9 0.6 dynamic-slice
  32.1 62.1 %all-reduce.3 = bf16[64,512]{1,0:T(8,128)(2,1)S(1)} all-reduce(f32[64,512]{1,0:T(8,128)S(1)} %fusion.26), channel_id=3, replica_groups=mesh['groups'=2,'wide'=4,'narrow'=4] {'wide','narrow'}, use_global_device_ids=true, to_apply=%region_6.7.clone | all-reduce | flops 32768 | bytes 196608
  94.3 0.0 reduce-scatter.3.cloned.1.call-done
  94.3 0.9 convert_element_type.32
  95.3 0.7 all_to_all.26
  96.0 3.3 %all-to-all-start = ((bf16[4,4,3072]{2,1,0:T(4,128)(2,1)}), bf16[4,4,3072]{2,1,0:T(4,128)(2,1)S(1)}, u32[]{:S(2)}, u32[]{:S(2)}) async-start(bf16[4,4,3072]{2,1,0:T(4,128)(2,1)} %all_to_all.26), calls=%async_computation.1 | async-start | bytes 196608 | tf_op jit(solution)/shard_map/all_to_all | solution.py:72
  99.3 0.0 reduce-scatter.5.cloned.1.call-start
  99.3 0.1 iota_compare_fusion
  99.4 5.7 %all-to-all-done = bf16[4,4,3072]{2,1,0:T(4,128)(2,1)S(1)} async-done(((bf16[4,4,3072]{2,1,0:T(4,128)(2,1)}), bf16[4,4,3072]{2,1,0:T(4,128)(2,1)S(1)}, u32[]{:S(2)}, u32[]{:S(2)}) %all-to-all-start) | async-done | bytes 98336 | tf_op jit(solution)/shard_map/all_to_all | solution.py:72
  105.1 0.1 copy.11
  105.1 0.1 reshape.36
  105.2 0.1 fusion.28
  105.3 2.4 %select_reduce_fusion = (f32[4,48]{1,0:T(4,128)S(1)}, f32[4,48,1024]{2,1,0:T(8,128)S(1)}) fusion(pred[4,1024]{1,0:T(4,128)(4,1)S(1)} %iota_compare_fusion, bf16[4,48,256]{2,1,0:T(8,128)(2,1)S(1)} %reshape.36, bf16[4,1024,512]{2,1,0:T(8,128)(2,1)} %param.12), kind=kOutput, calls=%fused_computation.16 | convolution fusion | flops 101252928 | bytes 2986752 | tf_op jit(solution)/shard_map/rhd,rld->rhl/dot_general | solution.py:25
  107.8 0.3 fusion.20
  108.1 2.1 %fusion.17 = bf16[4,48,256]{2,1,0:T(8,128)(2,1)S(1)} fusion(bf16[4,1024,512]{2,1,0:T(8,128)(2,1)} %param.12, f32[4,48,1024]{2,1,0:T(8,128)S(1)} %get-tuple-element.16, f32[4,48]{1,0:T(4,128)S(1)} %multiply_maximum_fusion, pred[4,1024]{1,0:T(4,128)(4,1)S(1)} %iota_compare_fusion, f32[4,48]{1,0:T(4,128)S(1)} %get-tuple-element.10, ...), kind=kOutput, calls=%fused_computation.14 | convolution fusion | flops 101449728 | bytes 2992384 | tf_op jit(solution)/shard_map/rhl,rld->rhd/dot_general | solution.py:41
  110.3 0.1 copy.12
  110.3 8.2 %all_to_all.35 = bf16[4,4,3072]{2,0,1:T(4,128)(2,1)S(1)} all-to-all(bf16[4,4,3072]{2,0,1:T(4,128)(2,1)S(1)} %copy.12), channel_id=1, replica_groups=mesh['groups'=2,'wide'=4,'narrow'=4] {'narrow'}, dimensions={1} | all-to-all | bytes 196608 | tf_op jit(solution)/shard_map/all_to_all | solution.py:84
  118.6 6.1 %all_gather.3 = bf16[64,3072]{1,0:T(8,128)(2,1)S(1)} all-gather(bf16[16,3072]{1,0:T(8,128)(2,1)S(1)} %all_to_all.32), channel_id=1, replica_groups=mesh['groups'=2,'wide'=4,'narrow'=4] {'wide'}, dimensions={0}, use_global_device_ids=true | all-gather | bytes 491520 | tf_op jit(solution)/shard_map/all_gather | solution.py:85
  124.7 12.7 %fusion.35 = f32[64,4608]{1,0:T(8,128)} fusion(bf16[64,3072]{1,0:T(8,128)(2,1)S(1)} %all_gather.3, bf16[3072,4608]{1,0:T(8,128)(2,1)} %param.11), kind=kOutput, calls=%fused_computation.39 | convolution fusion | flops 1811939328 | bytes 29884416 | tf_op jit(solution)/shard_map/dot_general | solution.py:87
  137.4 0.0 reduce-scatter.5.cloned.1.call-update
  137.4 27.3 %reduce-scatter.5.cloned.1.call-done = f32[16,4608]{1,0:T(8,128)} async-done(((f32[64,4608]{1,0:T(8,128)}), f32[16,4608]{1,0:T(8,128)}) %reduce-scatter.5.cloned.1.call-update) | async-done | bytes 294928 | tf_op jit(solution)/shard_map/reduce_scatter | solution.py:86
  164.8 1.6 convert_element_type.39
  (13 shorter events, 0.1 us)
Async XLA Ops:
  6.5 23.8 %copy-start = (bf16[1152,512]{1,0:T(8,128)(2,1)S(1)}, bf16[1152,512]{1,0:T(8,128)(2,1)}, u32[]{:S(2)}) copy-start(bf16[1152,512]{1,0:T(8,128)(2,1)} %param.10) | copy-start | bytes 3538948
  6.5 87.8 %reduce-scatter.3.cloned.1.call-start = ((), (), s32[]{:S(2)}) async-start(), calls=%async_computation.4 | async-start | bytes 983040 | tf_op jit(solution)/shard_map/reduce_scatter | solution.py:66
  30.2 0.7 copy-start.3
  30.2 69.1 %copy-start.2 = (s32[4]{0:T(128)S(1)}, s32[4]{0:T(128)}, u32[]{:S(2)}) copy-start(s32[4]{0:T(128)} %param.13) | copy-start | bytes 52
  96.0 9.1 %all-to-all-start = ((bf16[4,4,3072]{2,1,0:T(4,128)(2,1)}), bf16[4,4,3072]{2,1,0:T(4,128)(2,1)S(1)}, u32[]{:S(2)}, u32[]{:S(2)}) async-start(bf16[4,4,3072]{2,1,0:T(4,128)(2,1)} %all_to_all.26), calls=%async_computation.1 | async-start | bytes 196608 | tf_op jit(solution)/shard_map/all_to_all | solution.py:72
  99.3 65.5 %reduce-scatter.5.cloned.1.call-start = ((), (), s32[]{:S(2)}) async-start(), calls=%async_computation.5 | async-start | bytes 1474560 | tf_op jit(solution)/shard_map/reduce_scatter | solution.py:86
  124.7 41.7 %copy-start.1 = (bf16[1152,512]{1,0:T(8,128)(2,1)S(1)}, bf16[1152,512]{1,0:T(8,128)(2,1)}, u32[]{:S(2)}) copy-start(bf16[1152,512]{1,0:T(8,128)(2,1)} %param.10) | copy-start | bytes 3538948
Sparse Core Ops, SparseCore 0:
  30.4 23.6 reduce-scatter.2
  137.5 27.1 reduce-scatter.4
where the time goes:
time: 174 us; the launch traced here: 173 us
  blocking collectives  84.9 us (49%)
  waiting for transfers between devices  33.1 us (19%)
  matrix products  30.3 us (17%)
  between operations  14.2 us (8%)
  other arithmetic  5.71 us (3%)
  starting transfers between devices  3.35 us (2%)
  local copies, waits for them, and re-layouts  1.8 us (1%)
    unnamed x1, blocking collectives  62.1 us
    reduce_scatter x1, waiting for transfers between devices, local(): lax.psum_scatter(jnp.dot(gathered, out_weight, preferred_element_type=jnp...  27.3 us
    dot_general x1, matrix products, local(): jnp.dot(gathered, out_weight, preferred_element_type=jnp.float32)  12.7 us
    dot_general x1, matrix products, local(): jnp.dot(normed, query_weight, preferred_element_type=jnp.float32)  12.6 us
    psum x1, blocking collectives, local(): lax.psum((jnp.sum(values, axis=1), jnp.sum(values * values, axis=1)), 'wi...  8.37 us
    all_to_all x1, blocking collectives, local(): lax.all_to_all(context, 'narrow', split_axis=1, concat_axis=0, tiled=True)  8.21 us
    all_gather x1, blocking collectives, local(): gathered = lax.all_gather(returned, 'wide', axis=0, tiled=True)  6.15 us
    all_to_all x1, waiting for transfers between devices, local(): lax.all_to_all(summed, 'narrow', split_axis=0, concat_axis=1, tiled=True)  5.66 us
  transfers between devices with their start and end apart: 3, of which 2 were waited for; matrix products, arithmetic and copies ran while one was open for 1% of the time, Pallas kernels for 0%

commit v1 on v0

v1 whole, which is shorter than its diff:
```python
import math

import jax
import jax.numpy as jnp
from jax import lax
from jax.sharding import PartitionSpec as P


def swap(x, axis, distance):
    count = lax.axis_size(axis)
    return lax.ppermute(x, axis, [(i, i ^ distance) for i in range(count)])


def sum_over(x, axis):
    count = lax.axis_size(axis)
    if count <= 4:
        parts = [swap(x, axis, d) for d in range(1, count)]
        for part in parts:
            x = x + part
        return x
    d = 1
    while d < count:
        x = x + swap(x, axis, d)
        d *= 2
    return x


def scatter_sum(x, axis):
    count = lax.axis_size(axis)
    me = lax.axis_index(axis)
    rows, columns = x.shape[0] // count, x.shape[1]
    left, d = count, 1
    while d < count:
        bit = (me // d) % 2
        x = x.reshape(left // 2, 2, rows, columns)
        sent = lax.dynamic_index_in_dim(x, 1 - bit, 1, keepdims=False)
        kept = lax.dynamic_index_in_dim(x, bit, 1, keepdims=False)
        x = kept + swap(sent, axis, d)
        left //= 2
        d *= 2
    return x.reshape(rows, columns)


def exchange(blocks, axis):
    return [blocks[0]] + [swap(b, axis, d) for d, b in enumerate(blocks) if d]


def in_order(blocks, axis):
    me = lax.axis_index(axis)
    out = jnp.zeros((len(blocks),) + blocks[0].shape, blocks[0].dtype)
    for d, b in enumerate(blocks):
        out = lax.dynamic_update_index_in_dim(out, b, me ^ d, 0)
    return out.reshape((-1,) + blocks[0].shape[1:])


def gather(x, axis):
    count = lax.axis_size(axis)
    blocks = {0: x}
    d = count // 2
    while d:
        blocks |= {k ^ d: swap(b, axis, d) for k, b in blocks.items()}
        d //= 2
    return in_order([blocks[k] for k in range(count)], axis)


def attend(query_heads, kv_cache, fresh, lengths):
    row_count, head_count, head_dim = query_heads.shape
    scaling = 1.0 / math.sqrt(head_dim)
    new_keys = fresh[:, :head_dim]
    new_values = fresh[:, head_dim:]
    own_score = (
        jnp.einsum("rhd,rd->rh", query_heads, new_keys, preferred_element_type=jnp.float32)
        * scaling
    )
    scores = (
        jnp.einsum("rhd,rld->rhl", query_heads, kv_cache[:, :, :head_dim], preferred_element_type=jnp.float32)
        * scaling
    )
    positions = jnp.arange(kv_cache.shape[1], dtype=jnp.int32)
    valid = (positions[None, :] < lengths[:, None])[:, None, :]
    top = jnp.maximum(jnp.max(jnp.where(valid, scores, -jnp.inf), axis=2), own_score)
    weights = jnp.where(valid, jnp.exp(scores - top[..., None]), 0.0)
    numer = jnp.einsum(
        "rhl,rld->rhd",
        weights.astype(jnp.bfloat16),
        kv_cache[:, :, head_dim:],
        preferred_element_type=jnp.float32,
    )
    own_weight = jnp.exp(own_score - top)
    total = jnp.sum(weights, axis=2) + own_weight
    own_rounded = lax.optimization_barrier(own_weight.astype(jnp.bfloat16)).astype(jnp.float32)
    numer = numer + own_rounded[..., None] * new_values.astype(jnp.float32)[:, None, :]
    return (numer / total[..., None]).astype(jnp.bfloat16)


def local(activations, norm_gain, query_weight, kv_weight, out_weight, kv_cache, lengths):
    wide_count = lax.axis_size("wide")
    narrow_count = lax.axis_size("narrow")
    narrow = lax.axis_index("narrow")
    own_rows, head_dim = kv_cache.shape[0], kv_cache.shape[2] // 2
    values = activations.astype(jnp.float32)
    width_all = activations.shape[1] * wide_count
    sums = jnp.stack([jnp.sum(values, axis=1), jnp.sum(values * values, axis=1)])
    sums, squares = sum_over(sums, "wide")
    center = sums / width_all
    spread = squares / width_all - center * center
    normed = (
        (values - center[:, None]) * lax.rsqrt(spread + 1e-05)[:, None] * norm_gain[None, :]
    ).astype(jnp.bfloat16)
    sub_width = normed.shape[1] // narrow_count
    own_columns = lax.dynamic_slice_in_dim(normed, narrow * sub_width, sub_width, 1)
    fresh_part = jnp.dot(own_columns, kv_weight, preferred_element_type=jnp.float32)
    query_part = jnp.dot(normed, query_weight, preferred_element_type=jnp.float32)
    fresh_part = scatter_sum(fresh_part, "wide")
    summed = scatter_sum(query_part, "wide").astype(jnp.bfloat16)
    fresh = scatter_sum(fresh_part, "narrow").astype(jnp.bfloat16)
    by_owner = summed.reshape(narrow_count, own_rows, -1, head_dim)
    blocks = [lax.dynamic_index_in_dim(by_owner, narrow ^ d, 0, keepdims=False) for d in range(narrow_count)]
    heads = jnp.concatenate(exchange(blocks, "narrow"), axis=1)
    context = attend(heads, kv_cache, fresh, lengths)
    context = context.reshape(own_rows, narrow_count, -1)
    returned = in_order(exchange([context[:, d] for d in range(narrow_count)], "narrow"), "narrow")
    gathered = gather(returned, "wide")
    columns = out_weight.shape[1]
    cuts = 2
    outs = []
    for c in range(cuts):
        part = out_weight[:, c * columns // cuts : (c + 1) * columns // cuts]
        product = jnp.dot(gathered, part, preferred_element_type=jnp.float32)
        outs.append(scatter_sum(product, "narrow").astype(jnp.bfloat16))
    return jnp.concatenate(outs, axis=1)


def solution(mesh):
    return jax.shard_map(
        local,
        mesh=mesh,
        in_specs=(
            P("groups", "wide"),
            P("wide"),
            P("wide", "narrow"),
            P(("wide", "narrow"), None),
            P("narrow", "wide"),
            P(("groups", "wide", "narrow"), None, None),
            P(("groups", "wide", "narrow")),
        ),
        out_specs=P(("groups", "narrow"), "wide"),
        check_vma=False,
    )
```

time: 174 us -> 105 us (0.60)
  blocking collectives: 84.9 us -> 0 us
  starting transfers between devices: 3.35 us -> 21.4 us
  waiting for transfers between devices: 33.1 us -> 50.2 us
  between operations: 14.2 us -> 0.4 us
  matrix products: 30.3 us -> 27.9 us
    unnamed x1 -> x0, blocking collectives: 62.1 us -> none
    ppermute x0 -> x22, waiting for transfers between devices: none -> 50.2 us  [swap(): return lax.ppermute(x, axis, [(i, i ^ distance) for i in range(count)])]
    reduce_scatter x2 -> x0, waiting for transfers between devices: 27.4 us -> none  [the longest x1 27.3 us: local(): lax.psum_scatter(jnp.dot(gathered, out_weight, preferred_element_type=jnp...]
    ppermute x0 -> x22, starting transfers between devices: none -> 21.4 us  [swap(): return lax.ppermute(x, axis, [(i, i ^ distance) for i in range(count)])]
    psum x1 -> x0, blocking collectives: 8.37 us -> none  [local(): lax.psum((jnp.sum(values, axis=1), jnp.sum(values * values, axis=1)), 'wi...]
    all_to_all x1 -> x0, blocking collectives: 8.21 us -> none  [local(): lax.all_to_all(context, 'narrow', split_axis=1, concat_axis=0, tiled=True)]
    all_gather x1 -> x0, blocking collectives: 6.15 us -> none  [local(): gathered = lax.all_gather(returned, 'wide', axis=0, tiled=True)]
    all_to_all x1 -> x0, waiting for transfers between devices: 5.66 us -> none  [local(): lax.all_to_all(summed, 'narrow', split_axis=0, concat_axis=1, tiled=True)]
  transfers between devices with their start and end apart: 3 -> 22, of which waited for: 2 -> 16; matrix products, arithmetic and copies ran while one was open for 1% -> 12% of each run, Pallas kernels for 0% -> 0%
where the time goes in v1:
time: 105 us
  waiting for transfers between devices  50.2 us (48%)
  matrix products  27.9 us (27%)
  starting transfers between devices  21.4 us (20%)
  other arithmetic  4.05 us (4%)
    ppermute x22, waiting for transfers between devices, swap(): return lax.ppermute(x, axis, [(i, i ^ distance) for i in range(count)])  50.2 us
    ppermute x22, starting transfers between devices, swap(): return lax.ppermute(x, axis, [(i, i ^ distance) for i in range(count)])  21.4 us
    dot_general x2, matrix products, local(): product = jnp.dot(gathered, part, preferred_element_type=jnp.float32)  12.8 us
    dot_general x1, matrix products, local(): jnp.dot(normed, query_weight, preferred_element_type=jnp.float32)  11.6 us
    dot_general x1, matrix products, attend(): jnp.einsum('rhd,rld->rhl', query_heads, kv_cache[:, :, :head_dim], prefer...  2.42 us
  transfers between devices with their start and end apart: 22, of which 16 were waited for; matrix products, arithmetic and copies ran while one was open for 12% of the time, Pallas kernels for 0%

profile of v1, /device:TPU:0, one launch (start us, length us, event | category | flops | bytes accessed | tf_op | source)
XLA Modules:
  0.0 104.8 jit_solution(15189383920556797814)
XLA Ops:
  0.0 1.4 %convert_reduce_fusion = (f32[64]{0:T(128)S(1)}, f32[64]{0:T(128)S(1)}) fusion(bf16[64,4608]{1,0:T(8,128)(2,1)} %param.7), kind=kLoop, calls=%fused_computation.12 | loop fusion | flops 1179520 | bytes 590336 | tf_op jit(solution)/shard_map/reduce_sum | solution.py:103
  2.0 2.6 %collective-permute-start.1 = (f32[2,64]{1,0:T(2,128)S(1)}, f32[2,64]{1,0:T(2,128)S(1)}, u32[]{:S(2)}, u32[]{:S(2)}) collective-permute-start(f32[2,64]{1,0:T(2,128)S(1)} %pad_maximum_fusion.2), channel_id=1, source_target_pairs={{0,8},{4,12},{8,0},{12,4},{1,9},{5,13},{9,1},{13,5},{2,10},{6,14},... | collective-permute-start | bytes 1544 | tf_op jit(solution)/shard_map/ppermute | solution.py:11
  4.6 1.5 %collective-permute-done.1 = f32[2,64]{1,0:T(2,128)S(1)} collective-permute-done((f32[2,64]{1,0:T(2,128)S(1)}, f32[2,64]{1,0:T(2,128)S(1)}, u32[]{:S(2)}, u32[]{:S(2)}) %collective-permute-start.1) | collective-permute-done | bytes 544 | tf_op jit(solution)/shard_map/ppermute | solution.py:11
  6.1 1.4 %collective-permute-done.2 = f32[2,64]{1,0:T(2,128)S(1)} collective-permute-done((f32[2,64]{1,0:T(2,128)S(1)}, f32[2,64]{1,0:T(2,128)S(1)}, u32[]{:S(2)}, u32[]{:S(2)}) %collective-permute-start.2) | collective-permute-done | bytes 544 | tf_op jit(solution)/shard_map/ppermute | solution.py:11
  7.6 1.3 %fusion.16 = bf16[64,4608]{1,0:T(8,128)(2,1)S(1)} fusion(bf16[64,4608]{1,0:T(8,128)(2,1)} %param.7, f32[4608]{0:T(1024)} %param.8, f32[64]{0:T(128)S(1)} %fusion.44, f32[64]{0:T(128)S(1)} %multiply_bitcast_fusion), kind=kLoop, calls=%fused_computation.17 | loop fusion | flops 1474560 | bytes 1198592 | tf_op jit(solution)/shard_map/convert_element_type | solution.py:109
  9.5 11.6 %fusion.51 = f32[64,3072]{1,0:T(8,128)S(1)} fusion(bf16[64,4608]{1,0:T(8,128)(2,1)S(1)} %fusion.16, bf16[4608,3072]{1,0:T(8,128)(2,1)} %param.9), kind=kOutput, calls=%fused_computation.93 | convolution fusion | flops 1811939328 | bytes 29687808 | tf_op jit(solution)/shard_map/dot_general | solution.py:113
  21.2 0.6 collective-permute-start.9
  22.0 3.1 %collective-permute-done.9 = f32[1,16,512]{2,1,0:T(8,128)S(1)} collective-permute-done((f32[1,16,512]{2,1,0:T(8,128)S(1)}, f32[1,16,512]{2,1,0:T(8,128)S(1)}, u32[]{:S(2)}, u32[]{:S(2)}) %collective-permute-start.9) | collective-permute-done | bytes 32800 | tf_op jit(solution)/shard_map/ppermute | solution.py:11
  25.2 1.6 %collective-permute-start.10 = (f32[2,4,512]{2,1,0:T(4,128)S(1)}, f32[2,4,512]{2,1,0:T(4,128)S(1)}, u32[]{:S(2)}, u32[]{:S(2)}) collective-permute-start(f32[2,4,512]{2,1,0:T(4,128)S(1)} %dynamic-slice_bitcast_fusion.8), channel_id=1, source_target_pairs={{0,1},{1,0},{2,3},{3,2},{4,5},{5,4},{6,7},{7,6},{8,9},{9,8},{10,11... | collective-permute-start | bytes 49160 | tf_op jit(solution)/shard_map/ppermute | solution.py:11
  26.9 2.1 %collective-permute-done.10 = f32[2,4,512]{2,1,0:T(4,128)S(1)} collective-permute-done((f32[2,4,512]{2,1,0:T(4,128)S(1)}, f32[2,4,512]{2,1,0:T(4,128)S(1)}, u32[]{:S(2)}, u32[]{:S(2)}) %collective-permute-start.10) | collective-permute-done | bytes 16416 | tf_op jit(solution)/shard_map/ppermute | solution.py:11
  29.0 2.7 %collective-permute-start.11 = (f32[1,4,512]{2,1,0:T(4,128)S(1)}, f32[1,4,512]{2,1,0:T(4,128)S(1)}, u32[]{:S(2)}, u32[]{:S(2)}) collective-permute-start(f32[1,4,512]{2,1,0:T(4,128)S(1)} %constant_dynamic-slice_fusion.2), channel_id=1, source_target_pairs={{0,2},{1,3},{2,0},{3,1},{4,6},{5,7},{6,4},{7,5},{8,10},{9,11},{10,... | collective-permute-start | bytes 24584 | tf_op jit(solution)/shard_map/ppermute | solution.py:11
  32.3 1.3 %collective-permute-done.11 = f32[1,4,512]{2,1,0:T(4,128)S(1)} collective-permute-done((f32[1,4,512]{2,1,0:T(4,128)S(1)}, f32[1,4,512]{2,1,0:T(4,128)S(1)}, u32[]{:S(2)}, u32[]{:S(2)}) %collective-permute-start.11) | collective-permute-done | bytes 8224 | tf_op jit(solution)/shard_map/ppermute | solution.py:11
  33.6 3.9 %collective-permute-done.4 = f32[1,16,3072]{2,1,0:T(8,128)S(1)} collective-permute-done((f32[1,16,3072]{2,1,0:T(8,128)S(1)}, f32[1,16,3072]{2,1,0:T(8,128)S(1)}, u32[]{:S(2)}, u32[]{:S(2)}) %collective-permute-start.4) | collective-permute-done | bytes 196640 | tf_op jit(solution)/shard_map/ppermute | solution.py:11
  37.6 1.6 %collective-permute-start.5 = (bf16[4,12,256]{2,1,0:T(8,128)(2,1)S(1)}, bf16[4,12,256]{2,1,0:T(8,128)(2,1)S(1)}, u32[]{:S(2)}, u32[]{:S(2)}) collective-permute-start(bf16[4,12,256]{2,1,0:T(8,128)(2,1)S(1)} %get-tuple-element.10), channel_id=1, source_target_pairs={{0,1},{1,0},{2,3},{3,2},{4,5},{5,4},{6,7},{7,6},{8,9},{9,8},{10,11... | collective-permute-start | bytes 73736 | tf_op jit(solution)/shard_map/ppermute | solution.py:11
  39.6 2.5 %collective-permute-start.7 = (bf16[4,12,256]{2,1,0:T(8,128)(2,1)S(1)}, bf16[4,12,256]{2,1,0:T(8,128)(2,1)S(1)}, u32[]{:S(2)}, u32[]{:S(2)}) collective-permute-start(bf16[4,12,256]{2,1,0:T(8,128)(2,1)S(1)} %get-tuple-element.8), channel_id=1, source_target_pairs={{0,3},{1,2},{2,1},{3,0},{4,7},{5,6},{6,5},{7,4},{8,11},{9,10},{10,... | collective-permute-start | bytes 73736 | tf_op jit(solution)/shard_map/ppermute | solution.py:11
  42.1 2.2 %collective-permute-done.6 = bf16[4,12,256]{2,1,0:T(8,128)(2,1)S(1)} collective-permute-done((bf16[4,12,256]{2,1,0:T(8,128)(2,1)S(1)}, bf16[4,12,256]{2,1,0:T(8,128)(2,1)S(1)}, u32[]{:S(2)}, u32[]{:S(2)}) %collective-permute-start.6) | collective-permute-done | bytes 24608 | tf_op jit(solution)/shard_map/ppermute | solution.py:11
  44.3 1.0 collective-permute-done.7
  45.5 2.4 %select_reduce_fusion = (f32[4,48]{1,0:T(4,128)S(1)}, f32[4,48,1024]{2,1,0:T(8,128)S(1)}) fusion(pred[4,1024]{1,0:T(4,128)(4,1)S(1)} %iota_compare_fusion, bf16[4,1024,512]{2,1,0:T(8,128)(2,1)} %param.12, bf16[4,12,256]{2,1,0:T(8,128)(2,1)S(1)} %collective-permute-done.7, bf16[4,12,256]{2,1,0:T(8,128)(2,1)S(1)} %collective-permute-done.6, ...), kind=kOutput, calls=%fused_computation.22 | convolution fusion | flops 101646144 | bytes 2986752 | tf_op jit(solution)/shard_map/rhd,rld->rhl/dot_general | solution.py:76
  49.1 3.1 %collective-permute-start.13 = (bf16[4,3072]{1,0:T(4,128)(2,1)S(1)}, bf16[4,3072]{1,0:T(4,128)(2,1)S(1)}, u32[]{:S(2)}, u32[]{:S(2)}) collective-permute-start(bf16[4,3072]{1,0:T(4,128)(2,1)S(1)} %bitcast.100), channel_id=1, source_target_pairs={{0,2},{1,3},{2,0},{3,1},{4,6},{5,7},{6,4},{7,5},{8,10},{9,11},{10,... | collective-permute-start | bytes 73736 | tf_op jit(solution)/shard_map/ppermute | solution.py:11
  52.2 1.4 %collective-permute-start.14 = (bf16[4,3072]{1,0:T(4,128)(2,1)S(1)}, bf16[4,3072]{1,0:T(4,128)(2,1)S(1)}, u32[]{:S(2)}, u32[]{:S(2)}) collective-permute-start(bf16[4,3072]{1,0:T(4,128)(2,1)S(1)} %bitcast.99), channel_id=1, source_target_pairs={{0,3},{1,2},{2,1},{3,0},{4,7},{5,6},{6,5},{7,4},{8,11},{9,10},{10,... | collective-permute-start | bytes 73736 | tf_op jit(solution)/shard_map/ppermute | solution.py:11
  54.0 3.9 %collective-permute-done.14 = bf16[4,3072]{1,0:T(4,128)(2,1)S(1)} collective-permute-done((bf16[4,3072]{1,0:T(4,128)(2,1)S(1)}, bf16[4,3072]{1,0:T(4,128)(2,1)S(1)}, u32[]{:S(2)}, u32[]{:S(2)}) %collective-permute-start.14) | collective-permute-done | bytes 24608 | tf_op jit(solution)/shard_map/ppermute | solution.py:11
  58.1 0.6 collective-permute-start.16
  58.7 4.6 %collective-permute-done.16 = bf16[16,3072]{1,0:T(8,128)(2,1)S(1)} collective-permute-done((bf16[16,3072]{1,0:T(8,128)(2,1)S(1)}, bf16[16,3072]{1,0:T(8,128)(2,1)S(1)}, u32[]{:S(2)}, u32[]{:S(2)}) %collective-permute-start.16) | collective-permute-done | bytes 98336 | tf_op jit(solution)/shard_map/ppermute | solution.py:11
  63.3 1.3 %collective-permute-done.17 = bf16[16,3072]{1,0:T(8,128)(2,1)S(1)} collective-permute-done((bf16[16,3072]{1,0:T(8,128)(2,1)S(1)}, bf16[16,3072]{1,0:T(8,128)(2,1)S(1)}, u32[]{:S(2)}, u32[]{:S(2)}) %collective-permute-start.17) | collective-permute-done | bytes 98336 | tf_op jit(solution)/shard_map/ppermute | solution.py:11
  64.6 6.4 %fusion.2 = f32[2,2,16,2304]{3,2,1,0:T(8,128)S(1)} fusion(bf16[2,2,16,3072]{3,2,1,0:T(8,128)(2,1)S(1)} %bitcast.97, bf16[3072,4608]{1,0:T(8,128)(2,1)} %param.11), kind=kOutput, calls=%fused_computation.2 | convolution fusion | flops 905969664 | bytes 15138816 | tf_op jit(solution)/shard_map/dot_general | solution.py:129
  71.0 6.5 %fusion = f32[2,2,16,2304]{3,2,1,0:T(8,128)S(1)} fusion(bf16[2,2,16,3072]{3,2,1,0:T(8,128)(2,1)S(1)} %bitcast.98, bf16[3072,4608]{1,0:T(8,128)(2,1)} %param.11), kind=kOutput, calls=%fused_computation | convolution fusion | flops 905969664 | bytes 15138816 | tf_op jit(solution)/shard_map/dot_general | solution.py:129
  77.6 2.1 %collective-permute-start.20 = (f32[2,16,2304]{2,1,0:T(8,128)S(1)}, f32[2,16,2304]{2,1,0:T(8,128)S(1)}, u32[]{:S(2)}, u32[]{:S(2)}) collective-permute-start(f32[2,16,2304]{2,1,0:T(8,128)S(1)} %dynamic-slice_bitcast_fusion.1), channel_id=1, source_target_pairs={{0,1},{1,0},{2,3},{3,2},{4,5},{5,4},{6,7},{7,6},{8,9},{9,8},{10,11... | collective-permute-start | bytes 884744 | tf_op jit(solution)/shard_map/ppermute | solution.py:11
  79.7 7.7 %collective-permute-done.18 = f32[2,16,2304]{2,1,0:T(8,128)S(1)} collective-permute-done((f32[2,16,2304]{2,1,0:T(8,128)S(1)}, f32[2,16,2304]{2,1,0:T(8,128)S(1)}, u32[]{:S(2)}, u32[]{:S(2)}) %collective-permute-start.18) | collective-permute-done | bytes 294944 | tf_op jit(solution)/shard_map/ppermute | solution.py:11
  87.6 7.6 %collective-permute-done.20 = f32[2,16,2304]{2,1,0:T(8,128)S(1)} collective-permute-done((f32[2,16,2304]{2,1,0:T(8,128)S(1)}, f32[2,16,2304]{2,1,0:T(8,128)S(1)}, u32[]{:S(2)}, u32[]{:S(2)}) %collective-permute-start.20) | collective-permute-done | bytes 294944 | tf_op jit(solution)/shard_map/ppermute | solution.py:11
  95.7 1.1 %collective-permute-done.19 = f32[1,16,2304]{2,1,0:T(8,128)S(1)} collective-permute-done((f32[1,16,2304]{2,1,0:T(8,128)S(1)}, f32[1,16,2304]{2,1,0:T(8,128)S(1)}, u32[]{:S(2)}, u32[]{:S(2)}) %collective-permute-start.19) | collective-permute-done | bytes 147488 | tf_op jit(solution)/shard_map/ppermute | solution.py:11
  96.8 7.3 %collective-permute-done.21 = f32[1,16,2304]{2,1,0:T(8,128)S(1)} collective-permute-done((f32[1,16,2304]{2,1,0:T(8,128)S(1)}, f32[1,16,2304]{2,1,0:T(8,128)S(1)}, u32[]{:S(2)}, u32[]{:S(2)}) %collective-permute-start.21) | collective-permute-done | bytes 147488 | tf_op jit(solution)/shard_map/ppermute | solution.py:11
  104.1 0.7 pad_maximum_fusion
  (80 shorter events, 5.5 us)
Async XLA Ops:
  0.0 8.9 %copy-start = (bf16[1152,512]{1,0:T(8,128)(2,1)S(1)}, bf16[1152,512]{1,0:T(8,128)(2,1)}, u32[]{:S(2)}) copy-start(bf16[1152,512]{1,0:T(8,128)(2,1)} %param.10) | copy-start | bytes 3538948
  1.4 3.2 %collective-permute-start = (f32[2,64]{1,0:T(2,128)S(1)}, f32[2,64]{1,0:T(2,128)S(1)}, u32[]{:S(2)}, u32[]{:S(2)}) collective-permute-start(f32[2,64]{1,0:T(2,128)S(1)} %pad_maximum_fusion.2), channel_id=1, source_target_pairs={{0,4},{4,0},{8,12},{12,8},{1,5},{5,1},{9,13},{13,9},{2,6},{6,2},{1... | collective-permute-start | bytes 1544 | tf_op jit(solution)/shard_map/ppermute | solution.py:11
  2.0 4.1 %collective-permute-start.1 = (f32[2,64]{1,0:T(2,128)S(1)}, f32[2,64]{1,0:T(2,128)S(1)}, u32[]{:S(2)}, u32[]{:S(2)}) collective-permute-start(f32[2,64]{1,0:T(2,128)S(1)} %pad_maximum_fusion.2), channel_id=1, source_target_pairs={{0,8},{4,12},{8,0},{12,4},{1,9},{5,13},{9,1},{13,5},{2,10},{6,14},... | collective-permute-start | bytes 1544 | tf_op jit(solution)/shard_map/ppermute | solution.py:11
  4.5 3.0 %collective-permute-start.2 = (f32[2,64]{1,0:T(2,128)S(1)}, f32[2,64]{1,0:T(2,128)S(1)}, u32[]{:S(2)}, u32[]{:S(2)}) collective-permute-start(f32[2,64]{1,0:T(2,128)S(1)} %pad_maximum_fusion.2), channel_id=1, source_target_pairs={{0,12},{4,8},{8,4},{12,0},{1,13},{5,9},{9,5},{13,1},{2,14},{6,10},... | collective-permute-start | bytes 1544 | tf_op jit(solution)/shard_map/ppermute | solution.py:11
  9.2 17.6 %copy-start.2 = (s32[4]{0:T(128)S(1)}, s32[4]{0:T(128)}, u32[]{:S(2)}) copy-start(s32[4]{0:T(128)} %param.13) | copy-start | bytes 52
  9.3 11.9 %collective-permute-start.8 = (f32[2,16,512]{2,1,0:T(8,128)S(1)}, f32[2,16,512]{2,1,0:T(8,128)S(1)}, u32[]{:S(2)}, u32[]{:S(2)}) collective-permute-start(f32[2,16,512]{2,1,0:T(8,128)S(1)} %dynamic-slice_bitcast_fusion.3), channel_id=1, source_target_pairs={{0,4},{4,0},{8,12},{12,8},{1,5},{5,1},{9,13},{13,9},{2,6},{6,2},{1... | collective-permute-start | bytes 196616 | tf_op jit(solution)/shard_map/ppermute | solution.py:11
  21.2 4.0 %collective-permute-start.9 = (f32[1,16,512]{2,1,0:T(8,128)S(1)}, f32[1,16,512]{2,1,0:T(8,128)S(1)}, u32[]{:S(2)}, u32[]{:S(2)}) collective-permute-start(f32[1,16,512]{2,1,0:T(8,128)S(1)} %constant_dynamic-slice_fusion.4), channel_id=1, source_target_pairs={{0,8},{4,12},{8,0},{12,4},{1,9},{5,13},{9,1},{13,5},{2,10},{6,14},... | collective-permute-start | bytes 98312 | tf_op jit(solution)/shard_map/ppermute | solution.py:11
  21.8 9.9 %collective-permute-start.3 = (f32[2,16,3072]{2,1,0:T(8,128)S(1)}, f32[2,16,3072]{2,1,0:T(8,128)S(1)}, u32[]{:S(2)}, u32[]{:S(2)}) collective-permute-start(f32[2,16,3072]{2,1,0:T(8,128)S(1)} %dynamic-slice_bitcast_fusion), channel_id=1, source_target_pairs={{0,4},{4,0},{8,12},{12,8},{1,5},{5,1},{9,13},{13,9},{2,6},{6,2},{1... | collective-permute-start | bytes 1179656 | tf_op jit(solution)/shard_map/ppermute | solution.py:11
  25.2 3.8 %collective-permute-start.10 = (f32[2,4,512]{2,1,0:T(4,128)S(1)}, f32[2,4,512]{2,1,0:T(4,128)S(1)}, u32[]{:S(2)}, u32[]{:S(2)}) collective-permute-start(f32[2,4,512]{2,1,0:T(4,128)S(1)} %dynamic-slice_bitcast_fusion.8), channel_id=1, source_target_pairs={{0,1},{1,0},{2,3},{3,2},{4,5},{5,4},{6,7},{7,6},{8,9},{9,8},{10,11... | collective-permute-start | bytes 49160 | tf_op jit(solution)/shard_map/ppermute | solution.py:11
  29.0 4.6 %collective-permute-start.11 = (f32[1,4,512]{2,1,0:T(4,128)S(1)}, f32[1,4,512]{2,1,0:T(4,128)S(1)}, u32[]{:S(2)}, u32[]{:S(2)}) collective-permute-start(f32[1,4,512]{2,1,0:T(4,128)S(1)} %constant_dynamic-slice_fusion.2), channel_id=1, source_target_pairs={{0,2},{1,3},{2,0},{3,1},{4,6},{5,7},{6,4},{7,5},{8,10},{9,11},{10,... | collective-permute-start | bytes 24584 | tf_op jit(solution)/shard_map/ppermute | solution.py:11
  31.7 5.7 %collective-permute-start.4 = (f32[1,16,3072]{2,1,0:T(8,128)S(1)}, f32[1,16,3072]{2,1,0:T(8,128)S(1)}, u32[]{:S(2)}, u32[]{:S(2)}) collective-permute-start(f32[1,16,3072]{2,1,0:T(8,128)S(1)} %constant_dynamic-slice_fusion.5), channel_id=1, source_target_pairs={{0,8},{4,12},{8,0},{12,4},{1,9},{5,13},{9,1},{13,5},{2,10},{6,14},... | collective-permute-start | bytes 589832 | tf_op jit(solution)/shard_map/ppermute | solution.py:11
  37.6 10.6 %copy-start.3 = (bf16[4,1024,512]{2,1,0:T(8,128)(2,1)S(1)}, bf16[4,1024,512]{2,1,0:T(8,128)(2,1)}, u32[]{:S(2)}) copy-start(bf16[4,1024,512]{2,1,0:T(8,128)(2,1)} %param.12) | copy-start | bytes 12582916
  37.6 4.5 %collective-permute-start.5 = (bf16[4,12,256]{2,1,0:T(8,128)(2,1)S(1)}, bf16[4,12,256]{2,1,0:T(8,128)(2,1)S(1)}, u32[]{:S(2)}, u32[]{:S(2)}) collective-permute-start(bf16[4,12,256]{2,1,0:T(8,128)(2,1)S(1)} %get-tuple-element.10), channel_id=1, source_target_pairs={{0,1},{1,0},{2,3},{3,2},{4,5},{5,4},{6,7},{7,6},{8,9},{9,8},{10,11... | collective-permute-start | bytes 73736 | tf_op jit(solution)/shard_map/ppermute | solution.py:11
  39.3 5.1 %collective-permute-start.6 = (bf16[4,12,256]{2,1,0:T(8,128)(2,1)S(1)}, bf16[4,12,256]{2,1,0:T(8,128)(2,1)S(1)}, u32[]{:S(2)}, u32[]{:S(2)}) collective-permute-start(bf16[4,12,256]{2,1,0:T(8,128)(2,1)S(1)} %get-tuple-element.9), channel_id=1, source_target_pairs={{0,2},{1,3},{2,0},{3,1},{4,6},{5,7},{6,4},{7,5},{8,10},{9,11},{10,... | collective-permute-start | bytes 73736 | tf_op jit(solution)/shard_map/ppermute | solution.py:11
  39.6 5.7 %collective-permute-start.7 = (bf16[4,12,256]{2,1,0:T(8,128)(2,1)S(1)}, bf16[4,12,256]{2,1,0:T(8,128)(2,1)S(1)}, u32[]{:S(2)}, u32[]{:S(2)}) collective-permute-start(bf16[4,12,256]{2,1,0:T(8,128)(2,1)S(1)} %get-tuple-element.8), channel_id=1, source_target_pairs={{0,3},{1,2},{2,1},{3,0},{4,7},{5,6},{6,5},{7,4},{8,11},{9,10},{10,... | collective-permute-start | bytes 73736 | tf_op jit(solution)/shard_map/ppermute | solution.py:11
  49.0 4.7 %collective-permute-start.12 = (bf16[4,3072]{1,0:T(4,128)(2,1)S(1)}, bf16[4,3072]{1,0:T(4,128)(2,1)S(1)}, u32[]{:S(2)}, u32[]{:S(2)}) collective-permute-start(bf16[4,3072]{1,0:T(4,128)(2,1)S(1)} %bitcast.101), channel_id=1, source_target_pairs={{0,1},{1,0},{2,3},{3,2},{4,5},{5,4},{6,7},{7,6},{8,9},{9,8},{10,11... | collective-permute-start | bytes 73736 | tf_op jit(solution)/shard_map/ppermute | solution.py:11
  49.1 4.9 %collective-permute-start.13 = (bf16[4,3072]{1,0:T(4,128)(2,1)S(1)}, bf16[4,3072]{1,0:T(4,128)(2,1)S(1)}, u32[]{:S(2)}, u32[]{:S(2)}) collective-permute-start(bf16[4,3072]{1,0:T(4,128)(2,1)S(1)} %bitcast.100), channel_id=1, source_target_pairs={{0,2},{1,3},{2,0},{3,1},{4,6},{5,7},{6,4},{7,5},{8,10},{9,11},{10,... | collective-permute-start | bytes 73736 | tf_op jit(solution)/shard_map/ppermute | solution.py:11
  52.2 5.7 %collective-permute-start.14 = (bf16[4,3072]{1,0:T(4,128)(2,1)S(1)}, bf16[4,3072]{1,0:T(4,128)(2,1)S(1)}, u32[]{:S(2)}, u32[]{:S(2)}) collective-permute-start(bf16[4,3072]{1,0:T(4,128)(2,1)S(1)} %bitcast.99), channel_id=1, source_target_pairs={{0,3},{1,2},{2,1},{3,0},{4,7},{5,6},{6,5},{7,4},{8,11},{9,10},{10,... | collective-permute-start | bytes 73736 | tf_op jit(solution)/shard_map/ppermute | solution.py:11
  58.0 5.3 %collective-permute-start.15 = (bf16[16,3072]{1,0:T(8,128)(2,1)S(1)}, bf16[16,3072]{1,0:T(8,128)(2,1)S(1)}, u32[]{:S(2)}, u32[]{:S(2)}) collective-permute-start(bf16[16,3072]{1,0:T(8,128)(2,1)S(1)} %reshape.102), channel_id=1, source_target_pairs={{0,4},{4,0},{8,12},{12,8},{1,5},{5,1},{9,13},{13,9},{2,6},{6,2},{1... | collective-permute-start | bytes 294920 | tf_op jit(solution)/shard_map/ppermute | solution.py:11
  58.1 5.2 %collective-permute-start.16 = (bf16[16,3072]{1,0:T(8,128)(2,1)S(1)}, bf16[16,3072]{1,0:T(8,128)(2,1)S(1)}, u32[]{:S(2)}, u32[]{:S(2)}) collective-permute-start(bf16[16,3072]{1,0:T(8,128)(2,1)S(1)} %reshape.102), channel_id=1, source_target_pairs={{0,8},{4,12},{8,0},{12,4},{1,9},{5,13},{9,1},{13,5},{2,10},{6,14},... | collective-permute-start | bytes 294920 | tf_op jit(solution)/shard_map/ppermute | solution.py:11
  63.3 1.3 %collective-permute-start.17 = (bf16[16,3072]{1,0:T(8,128)(2,1)S(1)}, bf16[16,3072]{1,0:T(8,128)(2,1)S(1)}, u32[]{:S(2)}, u32[]{:S(2)}) collective-permute-start(bf16[16,3072]{1,0:T(8,128)(2,1)S(1)} %collective-permute-done.16), channel_id=1, source_target_pairs={{0,4},{4,0},{8,12},{12,8},{1,5},{5,1},{9,13},{13,9},{2,6},{6,2},{1... | collective-permute-start | bytes 294920 | tf_op jit(solution)/shard_map/ppermute | solution.py:11
  71.0 33.8 %copy-start.1 = (bf16[1152,512]{1,0:T(8,128)(2,1)S(1)}, bf16[1152,512]{1,0:T(8,128)(2,1)}, u32[]{:S(2)}) copy-start(bf16[1152,512]{1,0:T(8,128)(2,1)} %param.10) | copy-start | bytes 3538948
  77.5 9.9 %collective-permute-start.18 = (f32[2,16,2304]{2,1,0:T(8,128)S(1)}, f32[2,16,2304]{2,1,0:T(8,128)S(1)}, u32[]{:S(2)}, u32[]{:S(2)}) collective-permute-start(f32[2,16,2304]{2,1,0:T(8,128)S(1)} %dynamic-slice_bitcast_fusion.2), channel_id=1, source_target_pairs={{0,1},{1,0},{2,3},{3,2},{4,5},{5,4},{6,7},{7,6},{8,9},{9,8},{10,11... | collective-permute-start | bytes 884744 | tf_op jit(solution)/shard_map/ppermute | solution.py:11
  77.6 17.6 %collective-permute-start.20 = (f32[2,16,2304]{2,1,0:T(8,128)S(1)}, f32[2,16,2304]{2,1,0:T(8,128)S(1)}, u32[]{:S(2)}, u32[]{:S(2)}) collective-permute-start(f32[2,16,2304]{2,1,0:T(8,128)S(1)} %dynamic-slice_bitcast_fusion.1), channel_id=1, source_target_pairs={{0,1},{1,0},{2,3},{3,2},{4,5},{5,4},{6,7},{7,6},{8,9},{9,8},{10,11... | collective-permute-start | bytes 884744 | tf_op jit(solution)/shard_map/ppermute | solution.py:11
  87.5 9.3 %collective-permute-start.19 = (f32[1,16,2304]{2,1,0:T(8,128)S(1)}, f32[1,16,2304]{2,1,0:T(8,128)S(1)}, u32[]{:S(2)}, u32[]{:S(2)}) collective-permute-start(f32[1,16,2304]{2,1,0:T(8,128)S(1)} %constant_dynamic-slice_fusion.1), channel_id=1, source_target_pairs={{0,2},{1,3},{2,0},{3,1},{4,6},{5,7},{6,4},{7,5},{8,10},{9,11},{10,... | collective-permute-start | bytes 442376 | tf_op jit(solution)/shard_map/ppermute | solution.py:11
  95.3 8.8 %collective-permute-start.21 = (f32[1,16,2304]{2,1,0:T(8,128)S(1)}, f32[1,16,2304]{2,1,0:T(8,128)S(1)}, u32[]{:S(2)}, u32[]{:S(2)}) collective-permute-start(f32[1,16,2304]{2,1,0:T(8,128)S(1)} %constant_dynamic-slice_fusion), channel_id=1, source_target_pairs={{0,2},{1,3},{2,0},{3,1},{4,6},{5,7},{6,4},{7,5},{8,10},{9,11},{10,... | collective-permute-start | bytes 442376 | tf_op jit(solution)/shard_map/ppermute | solution.py:11

commit v2 on v1

v2 whole, which is shorter than its diff:
```python
import functools
import math

import jax
import jax.numpy as jnp
from jax import lax
from jax.experimental import pallas as pl
from jax.experimental.pallas import tpu as pltpu
from jax.sharding import PartitionSpec as P

MIB = 1 << 20
FULL = pl.BlockSpec(memory_space=pltpu.VMEM)
ANY = pl.BlockSpec(memory_space=pl.ANY)
SCALAR = pl.BlockSpec(memory_space=pltpu.SMEM)
STEPS = 32700.0
TINY = 1e-37
LANES = 128


def call(kernel, outs, ins, specs, name, scratch=(), limit=4, flops=0, moved=0):
    return pl.pallas_call(
        kernel,
        out_shape=outs,
        in_specs=specs,
        out_specs=jax.tree.map(lambda _: FULL, outs),
        scratch_shapes=list(scratch),
        compiler_params=pltpu.CompilerParams(vmem_limit_bytes=limit * MIB),
        cost_estimate=pl.CostEstimate(flops=flops, bytes_accessed=moved, transcendentals=0),
        name=name,
    )(*ins)


def held(shape, dtype):
    return pltpu.VMEM(shape, dtype)


def in_vmem(x):
    return pltpu.with_memory_space_constraint(x, pltpu.VMEM)


def in_hbm(x):
    return pltpu.with_memory_space_constraint(x, pltpu.HBM)


def swap(x, axis, distance):
    count = lax.axis_size(axis)
    return lax.ppermute(x, axis, [(i, i ^ distance) for i in range(count)])


def sent_apart(x, axis):
    count = lax.axis_size(axis)
    if count <= 4:
        return [x] + [swap(x, axis, d) for d in range(1, count)]
    d = 1
    while d < count:
        x = x + swap(x, axis, d)
        d *= 2
    return [x]


def exchange(blocks, axis):
    return [blocks[0]] + [swap(b, axis, d) for d, b in enumerate(blocks) if d]


def gather(x, axis):
    count = lax.axis_size(axis)
    blocks = {0: x}
    d = count // 2
    while d:
        blocks |= {k ^ d: swap(b, axis, d) for k, b in blocks.items()}
        d //= 2
    return [blocks[k] for k in range(count)]


def halving_order(count):
    bits = count.bit_length() - 1
    return [sum(((k >> b) & 1) << (bits - 1 - b) for b in range(bits)) for k in range(count)]


def thirds(tiles):
    first, second = tiles // 6, tiles // 2
    return first, second, tiles - first - second


def stats_kernel(me_ref, gain_ref, x_ref, w_ref, out_ref, part_ref, sem):
    rows, width = x_ref.shape
    fetch = pltpu.make_async_copy(w_ref.at[:, : part_ref.shape[1]], part_ref, sem)
    fetch.start()
    total = jnp.zeros((rows, LANES), jnp.float32)
    squares = jnp.zeros((rows, LANES), jnp.float32)
    for c in range(0, width, LANES):
        part = x_ref[:, c : c + LANES].astype(jnp.float32)
        total += part
        squares += part * part
    total = jnp.sum(total, axis=1, keepdims=True)
    squares = jnp.sum(squares, axis=1, keepdims=True)
    row = lax.broadcasted_iota(jnp.int32, (rows, rows), 0)
    column = lax.broadcasted_iota(jnp.int32, (rows, rows), 1)
    out_ref[0:1, :] = jnp.sum(jnp.where(row == column, total, 0.0), axis=0, keepdims=True)
    out_ref[1:2, :] = jnp.sum(jnp.where(row == column, squares, 0.0), axis=0, keepdims=True)
    fetch.wait()


def fetch_kernel(starts, *refs):
    count = len(starts)
    sources, shares, sems = refs[:count], refs[count + 1 : 2 * count + 1], refs[-1]
    fetches = []
    for k, start in enumerate(starts):
        source = sources[k] if start is None else sources[k].at[:, pl.ds(start, shares[k].shape[1])]
        fetches.append(pltpu.make_async_copy(source, shares[k], sems.at[k]))
    for fetch in fetches:
        fetch.start()
    for fetch in fetches:
        fetch.wait()


def fetch(items, after, name):
    shapes = [x.shape if start is None else (x.shape[0], width) for x, start, width in items]
    return call(
        functools.partial(fetch_kernel, [start for _, start, _ in items]),
        [held(shape, x.dtype) for shape, (x, _, _) in zip(shapes, items)],
        (*[in_hbm(x) for x, _, _ in items], after),
        [ANY] * (len(items) + 1),
        name,
        scratch=[pltpu.SemaphoreType.DMA((len(items),))],
        moved=sum(2 * math.prod(shape) for shape in shapes),
    )


def project_kernel(width_all, count, narrow_count, tile, me_ref, *refs):
    stat_refs = refs[:-12]
    x_ref, gain_ref, w_ref, kv_ref, first_ref, second_ref, kept_ref, sent_ref, normed, own, rest, sems = refs[-12:]
    rows, width = x_ref.shape
    half = rows // 2
    block = rows // count
    sub_width = width // narrow_count
    done = first_ref.shape[1] + second_ref.shape[1]
    fetches = [
        pltpu.make_async_copy(
            w_ref.at[:, done + t * tile : done + (t + 1) * tile], rest.at[:, t * tile : (t + 1) * tile], sems.at[t]
        )
        for t in range(rest.shape[1] // tile)
    ]
    for fetch in fetches:
        fetch.start()
    me, narrow = me_ref[0], me_ref[1]
    stats = stat_refs[0][...]
    for ref in stat_refs[1:]:
        stats = stats + ref[...]
    row = lax.broadcasted_iota(jnp.int32, (rows, rows), 0)
    column = lax.broadcasted_iota(jnp.int32, (rows, rows), 1)
    sums = jnp.sum(jnp.where(row == column, stats[0:1, :], 0.0), axis=1, keepdims=True)
    squares = jnp.sum(jnp.where(row == column, stats[1:2, :], 0.0), axis=1, keepdims=True)
    center = sums / width_all
    spread = squares / width_all - center * center
    inverse = lax.rsqrt(spread + 1e-05)
    order = halving_order(count)
    for j in range(count):
        pick = slice(j * block, (j + 1) * block)
        place = jnp.int32(0)
        for k, d in enumerate(order):
            place = jnp.where((me ^ d) == j, k, place)
        place = pl.multiple_of(place * block, 16)
        scaled = (x_ref[pick, :].astype(jnp.float32) - center[pick]) * inverse[pick] * gain_ref[...]
        normed[pl.ds(place, block), :] = scaled.astype(jnp.bfloat16)
    for j in range(narrow_count):
        @pl.when(narrow == j)
        def _(j=j):
            own[...] = normed[:, j * sub_width : (j + 1) * sub_width]

    def put(got, at):
        kept_ref[:, at] = got[:half, :]
        sent_ref[:, at] = got[half:, :]

    def products(source, start):
        @pl.loop(0, source.shape[1] // tile)
        def _(t):
            got = jnp.dot(
                normed[...], source[:, pl.ds(pl.multiple_of(t * tile, tile), tile)], preferred_element_type=jnp.float32
            )
            put(got, pl.ds(pl.multiple_of(start + t * tile, tile), tile))

    put(jnp.dot(own[...], kv_ref[...], preferred_element_type=jnp.float32), slice(w_ref.shape[1], kept_ref.shape[1]))
    products(first_ref, 0)
    products(second_ref, first_ref.shape[1])
    for fetch in fetches:
        fetch.wait()
    products(rest, done)


def project(me, stats, x, gain, w, kv, first, second, width_all, count, narrow_count, tile):
    rows, width = x.shape
    queries = w.shape[1]
    rest = queries - first.shape[1] - second.shape[1]
    half = jax.ShapeDtypeStruct((rows // 2, queries + kv.shape[1]), jnp.float32)
    return call(
        functools.partial(project_kernel, width_all, count, narrow_count, tile),
        (half, half),
        (me, *stats, x, gain, in_hbm(w), in_vmem(kv), in_vmem(first), in_vmem(second)),
        [SCALAR] + [FULL] * (len(stats) + 2) + [ANY] + [FULL] * 3,
        "project",
        scratch=[
            pltpu.VMEM((rows, width), jnp.bfloat16),
            pltpu.VMEM((rows, width // narrow_count), jnp.bfloat16),
            pltpu.VMEM((width, rest), jnp.bfloat16),
            pltpu.SemaphoreType.DMA((rest // tile,)),
        ],
        limit=18,
        flops=2 * rows * width * queries,
        moved=2 * width * rest,
    )


def fold_kernel(guards, kept_ref, came_ref, *refs):
    still_ref, sent_ref = refs[guards:]
    half = still_ref.shape[0]
    still_ref[...] = kept_ref[:half, :] + came_ref[:half, :]
    sent_ref[...] = kept_ref[half:, :] + came_ref[half:, :]


def fold(kept, came, guards):
    half = jax.ShapeDtypeStruct((kept.shape[0] // 2, kept.shape[1]), jnp.float32)
    return call(
        functools.partial(fold_kernel, len(guards)),
        (half, half),
        (kept, came, *map(in_vmem, guards)),
        [FULL] * (2 + len(guards)),
        "fold",
        moved=16 * kept.size,
    )


def split_kernel(queries, guards, me_ref, kept_ref, came_ref, *refs):
    out_refs = refs[guards:]
    count, rows = len(out_refs), out_refs[0].shape[0]
    narrow = me_ref[1]
    total = kept_ref[...] + came_ref[...]
    parts = [total[j * rows : (j + 1) * rows, :] for j in range(count)]
    for d, out_ref in enumerate(out_refs):
        mine = parts[0]
        for j in range(1, count):
            mine = jnp.where((narrow ^ d) == j, parts[j], mine)
        out_ref[:, :queries] = mine[:, :queries].astype(jnp.bfloat16)
        left = mine[:, queries:]
        width = left.shape[1]
        for term in range(3):
            high = left.astype(jnp.bfloat16)
            out_ref[:, queries + term * width : queries + (term + 1) * width] = high
            left = left - high.astype(jnp.float32)


PAD = 8


def attend_kernel(head_dim, guards, lengths_ref, *refs):
    count = (len(refs) - guards - 3) // 2
    came_refs, kv_ref = refs[:count], refs[count]
    out_refs, heads, contexts = refs[count + 1 + guards : -2], refs[-2], refs[-1]
    rows, positions = kv_ref.shape[0], kv_ref.shape[1]
    queries = out_refs[0].shape[1]
    each = queries // head_dim
    total_heads = each * count
    slabs = head_dim // LANES
    scaling = 1.0 / math.sqrt(head_dim)
    for d, ref in enumerate(came_refs):
        for h in range(each):
            at = (d * each + h) * PAD
            for k in range(slabs):
                start = h * head_dim + k * LANES
                heads[k, at : at + rows, :] = ref[:, start : start + LANES].astype(jnp.float32)
    terms = came_refs[0][:, queries:].astype(jnp.float32)
    for ref in came_refs[1:]:
        terms = terms + ref[:, queries:].astype(jnp.float32)
    pair = 2 * head_dim
    fresh = terms[:, :pair] + (terms[:, pair : 2 * pair] + terms[:, 2 * pair :])
    fresh = fresh.astype(jnp.bfloat16).astype(jnp.float32)
    place = lax.broadcasted_iota(jnp.int32, (total_heads, positions), 1)
    for r in range(rows):
        query = jnp.concatenate([heads[k, pl.ds(r, total_heads, stride=PAD), :] for k in range(slabs)], axis=1)
        scores = (
            lax.dot_general(
                query.astype(jnp.bfloat16),
                kv_ref[r, :, :head_dim],
                (((1,), (1,)), ((), ())),
                preferred_element_type=jnp.float32,
            )
            * scaling
        )
        own_score = jnp.sum(query * fresh[r : r + 1, :head_dim], axis=1, keepdims=True) * scaling
        valid = place < lengths_ref[r]
        top = jnp.maximum(jnp.max(jnp.where(valid, scores, -jnp.inf), axis=1, keepdims=True), own_score)
        weights = jnp.where(valid, jnp.exp(scores - top), 0.0)
        own_weight = jnp.exp(own_score - top)
        total = jnp.sum(weights, axis=1, keepdims=True) + own_weight
        numer = jnp.dot(weights.astype(jnp.bfloat16), kv_ref[r, :, head_dim:], preferred_element_type=jnp.float32)
        numer = numer + own_weight.astype(jnp.bfloat16).astype(jnp.float32) * fresh[r : r + 1, head_dim:]
        context = numer / total
        for k in range(slabs):
            contexts[k, pl.ds(r, total_heads, stride=PAD), :] = context[:, k * LANES : (k + 1) * LANES]
    for d, ref in enumerate(out_refs):
        for h in range(each):
            at = (d * each + h) * PAD
            for k in range(slabs):
                start = h * head_dim + k * LANES
                ref[:, start : start + LANES] = contexts[k, at : at + rows, :].astype(jnp.bfloat16)


def attend(lengths, came, kv, head_dim, queries, guards):
    rows = kv.shape[0]
    count = len(came)
    all_heads = count * queries // head_dim
    scratch = pltpu.VMEM((head_dim // LANES, all_heads * PAD, LANES), jnp.float32)
    return call(
        functools.partial(attend_kernel, head_dim, len(guards)),
        [jax.ShapeDtypeStruct((rows, queries), jnp.bfloat16)] * count,
        (lengths, *came, in_vmem(kv), *map(in_vmem, guards)),
        [SCALAR] + [FULL] * (count + 1 + len(guards)),
        "attend",
        scratch=[scratch, scratch],
        limit=8,
        flops=4 * rows * count * queries * kv.shape[1],
    )


def join_kernel(me_ref, *refs):
    came_refs, out_ref, joined = refs[:-2], refs[-2], refs[-1]
    rows = came_refs[0].shape[0]
    narrow = me_ref[1]
    came = [ref[...].astype(jnp.float32) for ref in came_refs]
    for j in range(len(came)):
        mine = came[0]
        for d in range(1, len(came)):
            mine = jnp.where((narrow ^ j) == d, came[d], mine)
        joined[j * rows : (j + 1) * rows, :] = mine
    out_ref[...] = joined[...].astype(jnp.bfloat16)


def arrange_kernel(narrow_count, me_ref, *refs):
    came_refs, out_ref, natural = refs[:-2], refs[-2], refs[-1]
    block = came_refs[0].shape[0]
    for d, ref in enumerate(came_refs):
        natural[pl.ds(pl.multiple_of((me_ref[0] ^ d) * block, 16), block), :] = ref[...]
    block = out_ref.shape[0] // narrow_count
    for k, d in enumerate(halving_order(narrow_count)):
        at = pl.ds(pl.multiple_of((me_ref[1] ^ d) * block, 16), block)
        out_ref[k * block : (k + 1) * block, :] = natural[at, :]


def code(x, ref):
    largest = jnp.maximum(jnp.max(jnp.abs(x), axis=1, keepdims=True), TINY)
    power = jnp.floor(jnp.log2(largest)) + 1.0
    steps = jnp.round(x * (STEPS * jnp.exp2(-power)))
    ref[:, : x.shape[1]] = steps.astype(jnp.int32).astype(jnp.int16)
    ref[:, x.shape[1] :] = jnp.broadcast_to(power, (x.shape[0], LANES)).astype(jnp.int32).astype(jnp.int16)


def decode(ref, width):
    power = ref[:, width:].astype(jnp.int32).astype(jnp.float32)[:, 0:1]
    return ref[:, :width].astype(jnp.int32).astype(jnp.float32) * (jnp.exp2(power) * (1.0 / STEPS))


def output_kernel(tile, x_ref, w_ref, kept_ref, sent_ref, product):
    half = kept_ref.shape[0]

    @pl.loop(0, w_ref.shape[1] // tile)
    def _(t):
        at = pl.ds(pl.multiple_of(t * tile, tile), tile)
        product[:, at] = jnp.dot(x_ref[...], w_ref[:, at], preferred_element_type=jnp.float32)

    kept_ref[...] = product[:half, :]
    code(product[half:, :], sent_ref)


def output_part(x, w):
    rows, columns = x.shape[0], w.shape[1]
    return call(
        functools.partial(output_kernel, 256 if columns % 256 == 0 else LANES),
        (
            jax.ShapeDtypeStruct((rows // 2, columns), jnp.float32),
            jax.ShapeDtypeStruct((rows // 2, columns + LANES), jnp.int16),
        ),
        (x, in_vmem(w)),
        [FULL, FULL],
        "output_part",
        scratch=[pltpu.VMEM((rows, columns), jnp.float32)],
        limit=6,
        flops=2 * rows * w.size,
        moved=2 * x.size,
    )


def halve_kernel(kept_ref, came_ref, still_ref, sent_ref):
    half = still_ref.shape[0]
    total = kept_ref[...] + decode(came_ref, kept_ref.shape[1])
    still_ref[...] = total[:half, :]
    code(total[half:, :], sent_ref)


def halve(kept, came):
    rows, columns = kept.shape
    return call(
        halve_kernel,
        (
            jax.ShapeDtypeStruct((rows // 2, columns), jnp.float32),
            jax.ShapeDtypeStruct((rows // 2, columns + LANES), jnp.int16),
        ),
        (kept, came),
        [FULL, FULL],
        "halve",
        moved=16 * kept.size,
    )


def finish_kernel(*refs):
    out_ref = refs[-1]
    at = 0
    for kept_ref, came_ref in zip(refs[:-1:2], refs[1:-1:2]):
        width = kept_ref.shape[1]
        out_ref[:, at : at + width] = (kept_ref[...] + decode(came_ref, width)).astype(jnp.bfloat16)
        at += width


def local(activations, norm_gain, query_weight, kv_weight, out_weight, kv_cache, lengths):
    wide_count = lax.axis_size("wide")
    narrow_count = lax.axis_size("narrow")
    me = jnp.stack([lax.axis_index("wide"), lax.axis_index("narrow")]).astype(jnp.int32)
    own_rows, head_dim = kv_cache.shape[0], kv_cache.shape[2] // 2
    rows, width = activations.shape
    queries = query_weight.shape[1]
    columns = out_weight.shape[1]
    cuts = 3
    cut = columns // cuts
    tile = 256
    first, second, _ = thirds(queries // tile)
    gain = norm_gain[None]
    stats, first_part = call(
        stats_kernel,
        (jax.ShapeDtypeStruct((2, rows), jnp.float32), held((width, first * tile), jnp.bfloat16)),
        (me, gain, activations, in_hbm(query_weight)),
        [SCALAR, FULL, FULL, ANY],
        "row_sums",
        scratch=[pltpu.SemaphoreType.DMA],
        moved=2 * width * first * tile,
    )
    second_part, kv_part = fetch(
        [(query_weight, first * tile, second * tile), (kv_weight, None, None)], stats, "fetch_query_weight"
    )
    kept, sent = project(
        me,
        sent_apart(stats, "wide"),
        activations,
        gain,
        query_weight,
        kv_part,
        first_part,
        second_part,
        width * wide_count,
        wide_count,
        narrow_count,
        tile,
    )
    out_parts = list(fetch([(out_weight, 0, cut)], sent, "fetch_out_weight_0"))
    guards = [out_parts[0]]
    d = 1
    while 2 * d < wide_count:
        kept, sent = fold(kept, swap(sent, "wide", d), guards)
        guards = []
        d *= 2
    fetched = fetch([(out_weight, cut, cut), (kv_cache, None, None)], sent, "fetch_out_weight_1")
    out_parts.append(fetched[0])
    split = call(
        functools.partial(split_kernel, queries, 1),
        [jax.ShapeDtypeStruct((own_rows, queries + 6 * head_dim), jnp.bfloat16)] * narrow_count,
        (me, kept, swap(sent, "wide", d), in_vmem(fetched[0])),
        [SCALAR] + [FULL] * 3,
        "split",
        moved=16 * kept.size,
    )
    out_parts += fetch([(out_weight, 2 * cut, cut)], split[0], "fetch_out_weight_2")
    context = attend(lengths, exchange(split, "narrow"), fetched[1], head_dim, queries, [out_parts[2]])
    returned = call(
        join_kernel,
        jax.ShapeDtypeStruct((narrow_count * own_rows, queries), jnp.bfloat16),
        (me, *exchange(context, "narrow")),
        [SCALAR] + [FULL] * narrow_count,
        "join",
        scratch=[pltpu.VMEM((narrow_count * own_rows, queries), jnp.float32)],
        moved=4 * narrow_count * own_rows * queries,
    )
    arranged = call(
        functools.partial(arrange_kernel, narrow_count),
        jax.ShapeDtypeStruct((rows, queries), jnp.bfloat16),
        (me, *gather(returned, "wide")),
        [SCALAR] + [FULL] * wide_count,
        "arrange",
        scratch=[pltpu.VMEM((rows, queries), jnp.bfloat16)],
        moved=4 * rows * queries,
    )
    pairs = []
    for part in out_parts:
        kept, sent = output_part(arranged, part)
        d = 1
        while d < narrow_count:
            came = swap(sent, "narrow", d)
            d *= 2
            if d < narrow_count:
                kept, sent = halve(kept, came)
        pairs += [kept, came]
    return call(
        finish_kernel,
        jax.ShapeDtypeStruct((rows // narrow_count, columns), jnp.bfloat16),
        pairs,
        [FULL] * len(pairs),
        "finish",
        moved=8 * columns * rows // narrow_count,
    )


def solution(mesh):
    return jax.shard_map(
        local,
        mesh=mesh,
        in_specs=(
            P("groups", "wide"),
            P("wide"),
            P("wide", "narrow"),
            P(("wide", "narrow"), None),
            P("narrow", "wide"),
            P(("groups", "wide", "narrow"), None, None),
            P(("groups", "wide", "narrow")),
        ),
        out_specs=P(("groups", "narrow"), "wide"),
        check_vma=False,
    )
```

time: 105 us -> 84.1 us (0.80)
  Pallas kernels: 0 us -> 41.7 us
  waiting for transfers between devices: 50.2 us -> 18.5 us
  matrix products: 27.9 us -> 0 us
  other arithmetic: 4.05 us -> 0.08 us
    pallas_call x0 -> x18, Pallas kernels: none -> 41.7 us  [call(): pl.pallas_call(kernel, out_shape=outs, in_specs=specs, out_specs=jax.tree...]
    ppermute x22 -> x20, waiting for transfers between devices: 50.2 us -> 18.5 us  [swap(): return lax.ppermute(x, axis, [(i, i ^ distance) for i in range(count)])]
    dot_general x7 -> x0, matrix products: 27.9 us -> none  [the longest x2 12.8 us: local(): product = jnp.dot(gathered, part, preferred_element_type=jnp.float32)]
    reduce_sum x2 -> x0, other arithmetic: 1.72 us -> none  [the longest x1 1.41 us: local(): jnp.sum(values, axis=1)]
    convert_element_type x8 -> x0, other arithmetic: 1.38 us -> none  [the longest x1 1.31 us: local(): normed = ((values - center[:, None]) * lax.rsqrt(spread + 1e-05)[:, None]...]
    ppermute x22 -> x20, starting transfers between devices: 21.4 us -> 21.5 us  [swap(): return lax.ppermute(x, axis, [(i, i ^ distance) for i in range(count)])]
  transfers between devices with their start and end apart: 22 -> 20, of which waited for: 16 -> 12; matrix products, arithmetic and copies ran while one was open for 12% -> 0% of each run, Pallas kernels for 0% -> 25%
where the time goes in v2:
time: 84.1 us; the launch traced here: 83.8 us
  Pallas kernels  41.7 us (50%)
  starting transfers between devices  21.5 us (26%)
  waiting for transfers between devices  18.5 us (22%)
  local copies, waits for them, and re-layouts  1.81 us (2%)
    pallas_call x18, Pallas kernels, call(): pl.pallas_call(kernel, out_shape=outs, in_specs=specs, out_specs=jax.tree...  41.7 us
    ppermute x20, starting transfers between devices, swap(): return lax.ppermute(x, axis, [(i, i ^ distance) for i in range(count)])  21.5 us
    ppermute x20, waiting for transfers between devices, swap(): return lax.ppermute(x, axis, [(i, i ^ distance) for i in range(count)])  18.5 us
  transfers between devices with their start and end apart: 20, of which 12 were waited for; matrix products, arithmetic and copies ran while one was open for 0% of the time, Pallas kernels for 25%

profile of v2, /device:TPU:0, one launch (start us, length us, event | category | flops | bytes accessed | tf_op | source)
XLA Modules:
  0.0 83.8 jit_solution(11246850937788696819)
XLA Ops:
  0.8 1.1 %copy-done = bf16[64,4608]{1,0:T(8,128)(2,1)S(1)} copy-done((bf16[64,4608]{1,0:T(8,128)(2,1)S(1)}, bf16[64,4608]{1,0:T(8,128)(2,1)}, u32[]{:S(2)}) %copy-start) | copy-done | bytes 589848
  1.9 2.9 %row_sums.1 = (f32[2,64]{1,0:T(2,128)S(1)}, bf16[4608,512]{1,0:T(8,128)(2,1)S(1)}) custom-call(s32[2]{0:T(128)S(1)} %pad_add_fusion.me_ref, f32[1,4608]{1,0:T(1,128)S(1)} %broadcast_in_dim.3.gain_ref.refs_5_, bf16[64,4608]{1,0:T(8,128)(2,1)S(1)} %copy-done, bf16[4608,3072]{1,0:T(8,128)(2,1)} %refs_6_.1), custom_call_target="tpu_custom_call" | custom-call | bytes 4718592 | tf_op jit(solution)/shard_map/row_sums/pallas_call | solution.py:21
  4.8 2.5 %collective-permute-start.2 = (f32[2,64]{1,0:T(2,128)S(1)}, f32[2,64]{1,0:T(2,128)S(1)}, u32[]{:S(2)}, u32[]{:S(2)}) collective-permute-start(f32[2,64]{1,0:T(2,128)S(1)} %get-tuple-element.35.refs_2_.refs_0_), channel_id=1, source_target_pairs={{0,12},{4,8},{8,4},{12,0},{1,13},{5,9},{9,5},{13,1},{2,14},{6,10},... | collective-permute-start | bytes 1544 | tf_op jit(solution)/shard_map/ppermute | solution.py:47
  7.9 5.5 %fetch_query_weight.1 = (bf16[4608,1536]{1,0:T(8,128)(2,1)S(1)}, bf16[1152,512]{1,0:T(8,128)(2,1)S(1)}) custom-call(bf16[4608,3072]{1,0:T(8,128)(2,1)} %refs_6_.1, bf16[1152,512]{1,0:T(8,128)(2,1)} %refs_1_.2, f32[2,64]{1,0:T(2,128)S(1)} %get-tuple-element.35.refs_2_.refs_0_), custom_call_target="tpu_custom_call" | custom-call | bytes 15335424 | tf_op jit(solution)/shard_map/fetch_query_weight/pallas_call | solution.py:21
  13.5 7.8 %project.1 = (f32[32,3584]{1,0:T(8,128)S(1)}, f32[32,3584]{1,0:T(8,128)S(1)}) custom-call(s32[2]{0:T(128)S(1)} %pad_add_fusion.me_ref, f32[2,64]{1,0:T(2,128)S(1)} %get-tuple-element.35.refs_2_.refs_0_, f32[2,64]{1,0:T(2,128)S(1)} %collective-permute-done.refs_1_, f32[2,64]{1,0:T(2,128)S(1)} %collective-permute-done.1.refs_2_, ...), custom_call_target="tpu_custom_call" | custom-call | flops 1811939328 | bytes 9437184 | tf_op jit(solution)/shard_map/project/pallas_call | solution.py:21
  21.9 3.7 %fetch_out_weight_0.1.refs_0_.w_ref = bf16[3072,1536]{1,0:T(8,128)(2,1)S(1)} custom-call(bf16[3072,4608]{1,0:T(8,128)(2,1)} %refs_0_.7, f32[32,3584]{1,0:T(8,128)S(1)} %get-tuple-element.40.refs_1_), custom_call_target="tpu_custom_call" | custom-call | bytes 9437184 | tf_op jit(solution)/shard_map/fetch_out_weight_0/pallas_call | solution.py:21
  25.7 1.4 %collective-permute-start.4 = (f32[16,3584]{1,0:T(8,128)S(1)}, f32[16,3584]{1,0:T(8,128)S(1)}, u32[]{:S(2)}, u32[]{:S(2)}) collective-permute-start(f32[16,3584]{1,0:T(8,128)S(1)} %get-tuple-element.42.refs_2_), channel_id=1, source_target_pairs={{0,8},{4,12},{8,0},{12,4},{1,9},{5,13},{9,1},{13,5},{2,10},{6,14},... | collective-permute-start | bytes 688136 | tf_op jit(solution)/shard_map/ppermute | solution.py:47
  27.1 4.9 %fetch_out_weight_1.1 = (bf16[3072,1536]{1,0:T(8,128)(2,1)S(1)}, bf16[4,1024,512]{2,1,0:T(8,128)(2,1)S(1)}) custom-call(bf16[3072,4608]{1,0:T(8,128)(2,1)} %refs_0_.7, bf16[4,1024,512]{2,1,0:T(8,128)(2,1)} %refs_1_.3, f32[16,3584]{1,0:T(8,128)S(1)} %get-tuple-element.42.refs_2_), custom_call_target="tpu_custom_call" | custom-call | bytes 13631488 | tf_op jit(solution)/shard_map/fetch_out_weight_1/pallas_call | solution.py:21
  32.1 1.3 %collective-permute-done.4.came_ref = f32[16,3584]{1,0:T(8,128)S(1)} collective-permute-done((f32[16,3584]{1,0:T(8,128)S(1)}, f32[16,3584]{1,0:T(8,128)S(1)}, u32[]{:S(2)}, u32[]{:S(2)}) %collective-permute-start.4) | collective-permute-done | bytes 229408 | tf_op jit(solution)/shard_map/ppermute | solution.py:47
  34.0 1.9 %collective-permute-start.5 = (bf16[4,4608]{1,0:T(4,128)(2,1)S(1)}, bf16[4,4608]{1,0:T(4,128)(2,1)S(1)}, u32[]{:S(2)}, u32[]{:S(2)}) collective-permute-start(bf16[4,4608]{1,0:T(4,128)(2,1)S(1)} %get-tuple-element.45), channel_id=1, source_target_pairs={{0,1},{1,0},{2,3},{3,2},{4,5},{5,4},{6,7},{7,6},{8,9},{9,8},{10,11... | collective-permute-start | bytes 110600 | tf_op jit(solution)/shard_map/ppermute | solution.py:47
  35.9 2.6 %collective-permute-start.6 = (bf16[4,4608]{1,0:T(4,128)(2,1)S(1)}, bf16[4,4608]{1,0:T(4,128)(2,1)S(1)}, u32[]{:S(2)}, u32[]{:S(2)}) collective-permute-start(bf16[4,4608]{1,0:T(4,128)(2,1)S(1)} %get-tuple-element.46), channel_id=1, source_target_pairs={{0,2},{1,3},{2,0},{3,1},{4,6},{5,7},{6,4},{7,5},{8,10},{9,11},{10,... | collective-permute-start | bytes 110600 | tf_op jit(solution)/shard_map/ppermute | solution.py:47
  38.4 3.7 %fetch_out_weight_2.1.refs_5_.w_ref = bf16[3072,1536]{1,0:T(8,128)(2,1)S(1)} custom-call(bf16[3072,4608]{1,0:T(8,128)(2,1)} %refs_0_.7, bf16[4,4608]{1,0:T(4,128)(2,1)S(1)} %get-tuple-element.44.refs_1_.refs_0_), custom_call_target="tpu_custom_call" | custom-call | bytes 9437184 | tf_op jit(solution)/shard_map/fetch_out_weight_2/pallas_call | solution.py:21
  42.2 2.0 %collective-permute-done.7.refs_3_ = bf16[4,4608]{1,0:T(4,128)(2,1)S(1)} collective-permute-done((bf16[4,4608]{1,0:T(4,128)(2,1)S(1)}, bf16[4,4608]{1,0:T(4,128)(2,1)S(1)}, u32[]{:S(2)}, u32[]{:S(2)}) %collective-permute-start.7) | collective-permute-done | bytes 36896 | tf_op jit(solution)/shard_map/ppermute | solution.py:47
  44.2 2.4 %attend.1 = (bf16[4,3072]{1,0:T(4,128)(2,1)S(1)}, bf16[4,3072]{1,0:T(4,128)(2,1)S(1)}, bf16[4,3072]{1,0:T(4,128)(2,1)S(1)}, bf16[4,3072]{1,0:T(4,128)(2,1)S(1)}) custom-call(s32[4]{0:T(128)S(1)} %copy-done.2, bf16[4,4608]{1,0:T(4,128)(2,1)S(1)} %get-tuple-element.44.refs_1_.refs_0_, bf16[4,4608]{1,0:T(4,128)(2,1)S(1)} %collective-permute-done.5.refs_1_, ...), custom_call_target="tpu_custom_call" | custom-call | flops 201326592 | tf_op jit(solution)/shard_map/attend/pallas_call | solution.py:21
  46.7 2.4 %collective-permute-start.9 = (bf16[4,3072]{1,0:T(4,128)(2,1)S(1)}, bf16[4,3072]{1,0:T(4,128)(2,1)S(1)}, u32[]{:S(2)}, u32[]{:S(2)}) collective-permute-start(bf16[4,3072]{1,0:T(4,128)(2,1)S(1)} %get-tuple-element.51), channel_id=1, source_target_pairs={{0,2},{1,3},{2,0},{3,1},{4,6},{5,7},{6,4},{7,5},{8,10},{9,11},{10,... | collective-permute-start | bytes 73736 | tf_op jit(solution)/shard_map/ppermute | solution.py:47
  49.1 2.0 %collective-permute-start.10 = (bf16[4,3072]{1,0:T(4,128)(2,1)S(1)}, bf16[4,3072]{1,0:T(4,128)(2,1)S(1)}, u32[]{:S(2)}, u32[]{:S(2)}) collective-permute-start(bf16[4,3072]{1,0:T(4,128)(2,1)S(1)} %get-tuple-element.52), channel_id=1, source_target_pairs={{0,3},{1,2},{2,1},{3,0},{4,7},{5,6},{6,5},{7,4},{8,11},{9,10},{10,... | collective-permute-start | bytes 73736 | tf_op jit(solution)/shard_map/ppermute | solution.py:47
  51.5 3.2 %collective-permute-done.10.refs_3_ = bf16[4,3072]{1,0:T(4,128)(2,1)S(1)} collective-permute-done((bf16[4,3072]{1,0:T(4,128)(2,1)S(1)}, bf16[4,3072]{1,0:T(4,128)(2,1)S(1)}, u32[]{:S(2)}, u32[]{:S(2)}) %collective-permute-start.10) | collective-permute-done | bytes 24608 | tf_op jit(solution)/shard_map/ppermute | solution.py:47
  55.3 1.6 %collective-permute-start.12 = (bf16[16,3072]{1,0:T(8,128)(2,1)S(1)}, bf16[16,3072]{1,0:T(8,128)(2,1)S(1)}, u32[]{:S(2)}, u32[]{:S(2)}) collective-permute-start(bf16[16,3072]{1,0:T(8,128)(2,1)S(1)} %join.1.refs_0_), channel_id=1, source_target_pairs={{0,8},{4,12},{8,0},{12,4},{1,9},{5,13},{9,1},{13,5},{2,10},{6,14},... | collective-permute-start | bytes 294920 | tf_op jit(solution)/shard_map/ppermute | solution.py:47
  56.9 3.1 %collective-permute-done.12.refs_2_ = bf16[16,3072]{1,0:T(8,128)(2,1)S(1)} collective-permute-done((bf16[16,3072]{1,0:T(8,128)(2,1)S(1)}, bf16[16,3072]{1,0:T(8,128)(2,1)S(1)}, u32[]{:S(2)}, u32[]{:S(2)}) %collective-permute-start.12) | collective-permute-done | bytes 98336 | tf_op jit(solution)/shard_map/ppermute | solution.py:47
  60.0 1.3 %collective-permute-done.13.refs_3_ = bf16[16,3072]{1,0:T(8,128)(2,1)S(1)} collective-permute-done((bf16[16,3072]{1,0:T(8,128)(2,1)S(1)}, bf16[16,3072]{1,0:T(8,128)(2,1)S(1)}, u32[]{:S(2)}, u32[]{:S(2)}) %collective-permute-start.13) | collective-permute-done | bytes 98336 | tf_op jit(solution)/shard_map/ppermute | solution.py:47
  61.9 2.5 %output_part.5 = (f32[32,1536]{1,0:T(8,128)S(1)}, s16[32,1664]{1,0:T(8,128)(2,1)S(1)}) custom-call(bf16[64,3072]{1,0:T(8,128)(2,1)S(1)} %arrange.1.x_ref, bf16[3072,1536]{1,0:T(8,128)(2,1)S(1)} %fetch_out_weight_2.1.refs_5_.w_ref), custom_call_target="tpu_custom_call" | custom-call | flops 603979776 | bytes 393216 | tf_op jit(solution)/shard_map/output_part/pallas_call | solution.py:21
  64.4 2.5 %output_part.4 = (f32[32,1536]{1,0:T(8,128)S(1)}, s16[32,1664]{1,0:T(8,128)(2,1)S(1)}) custom-call(bf16[64,3072]{1,0:T(8,128)(2,1)S(1)} %arrange.1.x_ref, bf16[3072,1536]{1,0:T(8,128)(2,1)S(1)} %get-tuple-element.43.refs_0_.w_ref), custom_call_target="tpu_custom_call" | custom-call | flops 603979776 | bytes 393216 | tf_op jit(solution)/shard_map/output_part/pallas_call | solution.py:21
  67.0 2.0 %collective-permute-start.16 = (s16[32,1664]{1,0:T(8,128)(2,1)S(1)}, s16[32,1664]{1,0:T(8,128)(2,1)S(1)}, u32[]{:S(2)}, u32[]{:S(2)}) collective-permute-start(s16[32,1664]{1,0:T(8,128)(2,1)S(1)} %get-tuple-element.58), channel_id=1, source_target_pairs={{0,1},{1,0},{2,3},{3,2},{4,5},{5,4},{6,7},{7,6},{8,9},{9,8},{10,11... | collective-permute-start | bytes 319496 | tf_op jit(solution)/shard_map/ppermute | solution.py:47
  69.0 2.5 %output_part.3 = (f32[32,1536]{1,0:T(8,128)S(1)}, s16[32,1664]{1,0:T(8,128)(2,1)S(1)}) custom-call(bf16[64,3072]{1,0:T(8,128)(2,1)S(1)} %arrange.1.x_ref, bf16[3072,1536]{1,0:T(8,128)(2,1)S(1)} %fetch_out_weight_0.1.refs_0_.w_ref), custom_call_target="tpu_custom_call" | custom-call | flops 603979776 | bytes 393216 | tf_op jit(solution)/shard_map/output_part/pallas_call | solution.py:21
  71.7 1.1 %collective-permute-done.18.came_ref = s16[32,1664]{1,0:T(8,128)(2,1)S(1)} collective-permute-done((s16[32,1664]{1,0:T(8,128)(2,1)S(1)}, s16[32,1664]{1,0:T(8,128)(2,1)S(1)}, u32[]{:S(2)}, u32[]{:S(2)}) %collective-permute-start.18) | collective-permute-done | bytes 106528 | tf_op jit(solution)/shard_map/ppermute | solution.py:47
  73.0 1.4 %collective-permute-start.19 = (s16[16,1664]{1,0:T(8,128)(2,1)S(1)}, s16[16,1664]{1,0:T(8,128)(2,1)S(1)}, u32[]{:S(2)}, u32[]{:S(2)}) collective-permute-start(s16[16,1664]{1,0:T(8,128)(2,1)S(1)} %get-tuple-element.64), channel_id=1, source_target_pairs={{0,2},{1,3},{2,0},{3,1},{4,6},{5,7},{6,4},{7,5},{8,10},{9,11},{10,... | collective-permute-start | bytes 159752 | tf_op jit(solution)/shard_map/ppermute | solution.py:47
  74.9 1.3 %collective-permute-start.17 = (s16[16,1664]{1,0:T(8,128)(2,1)S(1)}, s16[16,1664]{1,0:T(8,128)(2,1)S(1)}, u32[]{:S(2)}, u32[]{:S(2)}) collective-permute-start(s16[16,1664]{1,0:T(8,128)(2,1)S(1)} %get-tuple-element.60), channel_id=1, source_target_pairs={{0,2},{1,3},{2,0},{3,1},{4,6},{5,7},{6,4},{7,5},{8,10},{9,11},{10,... | collective-permute-start | bytes 159752 | tf_op jit(solution)/shard_map/ppermute | solution.py:47
  76.2 0.9 %collective-permute-done.14.came_ref = s16[32,1664]{1,0:T(8,128)(2,1)S(1)} collective-permute-done((s16[32,1664]{1,0:T(8,128)(2,1)S(1)}, s16[32,1664]{1,0:T(8,128)(2,1)S(1)}, u32[]{:S(2)}, u32[]{:S(2)}) %collective-permute-start.14) | collective-permute-done | bytes 106528 | tf_op jit(solution)/shard_map/ppermute | solution.py:47
  77.3 0.9 %collective-permute-start.15 = (s16[16,1664]{1,0:T(8,128)(2,1)S(1)}, s16[16,1664]{1,0:T(8,128)(2,1)S(1)}, u32[]{:S(2)}, u32[]{:S(2)}) collective-permute-start(s16[16,1664]{1,0:T(8,128)(2,1)S(1)} %get-tuple-element.56), channel_id=1, source_target_pairs={{0,2},{1,3},{2,0},{3,1},{4,6},{5,7},{6,4},{7,5},{8,10},{9,11},{10,... | collective-permute-start | bytes 159752 | tf_op jit(solution)/shard_map/ppermute | solution.py:47
  78.2 2.6 %collective-permute-done.19.refs_5_ = s16[16,1664]{1,0:T(8,128)(2,1)S(1)} collective-permute-done((s16[16,1664]{1,0:T(8,128)(2,1)S(1)}, s16[16,1664]{1,0:T(8,128)(2,1)S(1)}, u32[]{:S(2)}, u32[]{:S(2)}) %collective-permute-start.19) | collective-permute-done | bytes 53280 | tf_op jit(solution)/shard_map/ppermute | solution.py:47
  80.8 1.7 %collective-permute-done.17.refs_3_ = s16[16,1664]{1,0:T(8,128)(2,1)S(1)} collective-permute-done((s16[16,1664]{1,0:T(8,128)(2,1)S(1)}, s16[16,1664]{1,0:T(8,128)(2,1)S(1)}, u32[]{:S(2)}, u32[]{:S(2)}) %collective-permute-start.17) | collective-permute-done | bytes 53280 | tf_op jit(solution)/shard_map/ppermute | solution.py:47
  83.1 0.8 finish.1
  (34 shorter events, 6.2 us)
Async XLA Ops:
  0.8 1.1 %copy-start = (bf16[64,4608]{1,0:T(8,128)(2,1)S(1)}, bf16[64,4608]{1,0:T(8,128)(2,1)}, u32[]{:S(2)}) copy-start(bf16[64,4608]{1,0:T(8,128)(2,1)} %refs_4_.1) | copy-start | bytes 1769476
  4.8 8.7 %copy-start.1 = (bf16[64,4608]{1,0:T(8,128)(2,1)S(1)}, bf16[64,4608]{1,0:T(8,128)(2,1)}, u32[]{:S(2)}) copy-start(bf16[64,4608]{1,0:T(8,128)(2,1)} %refs_4_.1) | copy-start | bytes 1769476
  4.8 8.7 %collective-permute-start.2 = (f32[2,64]{1,0:T(2,128)S(1)}, f32[2,64]{1,0:T(2,128)S(1)}, u32[]{:S(2)}, u32[]{:S(2)}) collective-permute-start(f32[2,64]{1,0:T(2,128)S(1)} %get-tuple-element.35.refs_2_.refs_0_), channel_id=1, source_target_pairs={{0,12},{4,8},{8,4},{12,0},{1,13},{5,9},{9,5},{13,1},{2,14},{6,10},... | collective-permute-start | bytes 1544 | tf_op jit(solution)/shard_map/ppermute | solution.py:47
  7.3 6.2 %collective-permute-start.1 = (f32[2,64]{1,0:T(2,128)S(1)}, f32[2,64]{1,0:T(2,128)S(1)}, u32[]{:S(2)}, u32[]{:S(2)}) collective-permute-start(f32[2,64]{1,0:T(2,128)S(1)} %get-tuple-element.35.refs_2_.refs_0_), channel_id=1, source_target_pairs={{0,8},{4,12},{8,0},{12,4},{1,9},{5,13},{9,1},{13,5},{2,10},{6,14},... | collective-permute-start | bytes 1544 | tf_op jit(solution)/shard_map/ppermute | solution.py:47
  7.9 5.6 %collective-permute-start = (f32[2,64]{1,0:T(2,128)S(1)}, f32[2,64]{1,0:T(2,128)S(1)}, u32[]{:S(2)}, u32[]{:S(2)}) collective-permute-start(f32[2,64]{1,0:T(2,128)S(1)} %get-tuple-element.35.refs_2_.refs_0_), channel_id=1, source_target_pairs={{0,4},{4,0},{8,12},{12,8},{1,5},{5,1},{9,13},{13,9},{2,6},{6,2},{1... | collective-permute-start | bytes 1544 | tf_op jit(solution)/shard_map/ppermute | solution.py:47
  21.4 4.2 %collective-permute-start.3 = (f32[32,3584]{1,0:T(8,128)S(1)}, f32[32,3584]{1,0:T(8,128)S(1)}, u32[]{:S(2)}, u32[]{:S(2)}) collective-permute-start(f32[32,3584]{1,0:T(8,128)S(1)} %get-tuple-element.40.refs_1_), channel_id=1, source_target_pairs={{0,4},{4,0},{8,12},{12,8},{1,5},{5,1},{9,13},{13,9},{2,6},{6,2},{1... | collective-permute-start | bytes 1376264 | tf_op jit(solution)/shard_map/ppermute | solution.py:47
  25.7 7.6 %collective-permute-start.4 = (f32[16,3584]{1,0:T(8,128)S(1)}, f32[16,3584]{1,0:T(8,128)S(1)}, u32[]{:S(2)}, u32[]{:S(2)}) collective-permute-start(f32[16,3584]{1,0:T(8,128)S(1)} %get-tuple-element.42.refs_2_), channel_id=1, source_target_pairs={{0,8},{4,12},{8,0},{12,4},{1,9},{5,13},{9,1},{13,5},{2,10},{6,14},... | collective-permute-start | bytes 688136 | tf_op jit(solution)/shard_map/ppermute | solution.py:47
  34.0 8.2 %collective-permute-start.5 = (bf16[4,4608]{1,0:T(4,128)(2,1)S(1)}, bf16[4,4608]{1,0:T(4,128)(2,1)S(1)}, u32[]{:S(2)}, u32[]{:S(2)}) collective-permute-start(bf16[4,4608]{1,0:T(4,128)(2,1)S(1)} %get-tuple-element.45), channel_id=1, source_target_pairs={{0,1},{1,0},{2,3},{3,2},{4,5},{5,4},{6,7},{7,6},{8,9},{9,8},{10,11... | collective-permute-start | bytes 110600 | tf_op jit(solution)/shard_map/ppermute | solution.py:47
  35.9 6.3 %collective-permute-start.6 = (bf16[4,4608]{1,0:T(4,128)(2,1)S(1)}, bf16[4,4608]{1,0:T(4,128)(2,1)S(1)}, u32[]{:S(2)}, u32[]{:S(2)}) collective-permute-start(bf16[4,4608]{1,0:T(4,128)(2,1)S(1)} %get-tuple-element.46), channel_id=1, source_target_pairs={{0,2},{1,3},{2,0},{3,1},{4,6},{5,7},{6,4},{7,5},{8,10},{9,11},{10,... | collective-permute-start | bytes 110600 | tf_op jit(solution)/shard_map/ppermute | solution.py:47
  38.4 5.8 %collective-permute-start.7 = (bf16[4,4608]{1,0:T(4,128)(2,1)S(1)}, bf16[4,4608]{1,0:T(4,128)(2,1)S(1)}, u32[]{:S(2)}, u32[]{:S(2)}) collective-permute-start(bf16[4,4608]{1,0:T(4,128)(2,1)S(1)} %get-tuple-element.47), channel_id=1, source_target_pairs={{0,3},{1,2},{2,1},{3,0},{4,7},{5,6},{6,5},{7,4},{8,11},{9,10},{10,... | collective-permute-start | bytes 110600 | tf_op jit(solution)/shard_map/ppermute | solution.py:47
  38.4 5.8 %copy-start.2 = (s32[4]{0:T(128)S(1)}, s32[4]{0:T(128)}, u32[]{:S(2)}) copy-start(s32[4]{0:T(128)} %lengths_ref.1) | copy-start | bytes 52
  46.6 4.5 %collective-permute-start.8 = (bf16[4,3072]{1,0:T(4,128)(2,1)S(1)}, bf16[4,3072]{1,0:T(4,128)(2,1)S(1)}, u32[]{:S(2)}, u32[]{:S(2)}) collective-permute-start(bf16[4,3072]{1,0:T(4,128)(2,1)S(1)} %get-tuple-element.50), channel_id=1, source_target_pairs={{0,1},{1,0},{2,3},{3,2},{4,5},{5,4},{6,7},{7,6},{8,9},{9,8},{10,11... | collective-permute-start | bytes 73736 | tf_op jit(solution)/shard_map/ppermute | solution.py:47
  46.7 4.8 %collective-permute-start.9 = (bf16[4,3072]{1,0:T(4,128)(2,1)S(1)}, bf16[4,3072]{1,0:T(4,128)(2,1)S(1)}, u32[]{:S(2)}, u32[]{:S(2)}) collective-permute-start(bf16[4,3072]{1,0:T(4,128)(2,1)S(1)} %get-tuple-element.51), channel_id=1, source_target_pairs={{0,2},{1,3},{2,0},{3,1},{4,6},{5,7},{6,4},{7,5},{8,10},{9,11},{10,... | collective-permute-start | bytes 73736 | tf_op jit(solution)/shard_map/ppermute | solution.py:47
  49.1 5.6 %collective-permute-start.10 = (bf16[4,3072]{1,0:T(4,128)(2,1)S(1)}, bf16[4,3072]{1,0:T(4,128)(2,1)S(1)}, u32[]{:S(2)}, u32[]{:S(2)}) collective-permute-start(bf16[4,3072]{1,0:T(4,128)(2,1)S(1)} %get-tuple-element.52), channel_id=1, source_target_pairs={{0,3},{1,2},{2,1},{3,0},{4,7},{5,6},{6,5},{7,4},{8,11},{9,10},{10,... | collective-permute-start | bytes 73736 | tf_op jit(solution)/shard_map/ppermute | solution.py:47
  55.3 4.7 %collective-permute-start.12 = (bf16[16,3072]{1,0:T(8,128)(2,1)S(1)}, bf16[16,3072]{1,0:T(8,128)(2,1)S(1)}, u32[]{:S(2)}, u32[]{:S(2)}) collective-permute-start(bf16[16,3072]{1,0:T(8,128)(2,1)S(1)} %join.1.refs_0_), channel_id=1, source_target_pairs={{0,8},{4,12},{8,0},{12,4},{1,9},{5,13},{9,1},{13,5},{2,10},{6,14},... | collective-permute-start | bytes 294920 | tf_op jit(solution)/shard_map/ppermute | solution.py:47
  56.9 3.1 %collective-permute-start.11 = (bf16[16,3072]{1,0:T(8,128)(2,1)S(1)}, bf16[16,3072]{1,0:T(8,128)(2,1)S(1)}, u32[]{:S(2)}, u32[]{:S(2)}) collective-permute-start(bf16[16,3072]{1,0:T(8,128)(2,1)S(1)} %join.1.refs_0_), channel_id=1, source_target_pairs={{0,4},{4,0},{8,12},{12,8},{1,5},{5,1},{9,13},{13,9},{2,6},{6,2},{1... | collective-permute-start | bytes 294920 | tf_op jit(solution)/shard_map/ppermute | solution.py:47
  60.0 1.3 %collective-permute-start.13 = (bf16[16,3072]{1,0:T(8,128)(2,1)S(1)}, bf16[16,3072]{1,0:T(8,128)(2,1)S(1)}, u32[]{:S(2)}, u32[]{:S(2)}) collective-permute-start(bf16[16,3072]{1,0:T(8,128)(2,1)S(1)} %collective-permute-done.12.refs_2_), channel_id=1, source_target_pairs={{0,4},{4,0},{8,12},{12,8},{1,5},{5,1},{9,13},{13,9},{2,6},{6,2},{1... | collective-permute-start | bytes 294920 | tf_op jit(solution)/shard_map/ppermute | solution.py:47
  66.9 5.9 %collective-permute-start.18 = (s16[32,1664]{1,0:T(8,128)(2,1)S(1)}, s16[32,1664]{1,0:T(8,128)(2,1)S(1)}, u32[]{:S(2)}, u32[]{:S(2)}) collective-permute-start(s16[32,1664]{1,0:T(8,128)(2,1)S(1)} %get-tuple-element.62), channel_id=1, source_target_pairs={{0,1},{1,0},{2,3},{3,2},{4,5},{5,4},{6,7},{7,6},{8,9},{9,8},{10,11... | collective-permute-start | bytes 319496 | tf_op jit(solution)/shard_map/ppermute | solution.py:47
  67.0 7.8 %collective-permute-start.16 = (s16[32,1664]{1,0:T(8,128)(2,1)S(1)}, s16[32,1664]{1,0:T(8,128)(2,1)S(1)}, u32[]{:S(2)}, u32[]{:S(2)}) collective-permute-start(s16[32,1664]{1,0:T(8,128)(2,1)S(1)} %get-tuple-element.58), channel_id=1, source_target_pairs={{0,1},{1,0},{2,3},{3,2},{4,5},{5,4},{6,7},{7,6},{8,9},{9,8},{10,11... | collective-permute-start | bytes 319496 | tf_op jit(solution)/shard_map/ppermute | solution.py:47
  71.5 5.6 %collective-permute-start.14 = (s16[32,1664]{1,0:T(8,128)(2,1)S(1)}, s16[32,1664]{1,0:T(8,128)(2,1)S(1)}, u32[]{:S(2)}, u32[]{:S(2)}) collective-permute-start(s16[32,1664]{1,0:T(8,128)(2,1)S(1)} %get-tuple-element.54), channel_id=1, source_target_pairs={{0,1},{1,0},{2,3},{3,2},{4,5},{5,4},{6,7},{7,6},{8,9},{9,8},{10,11... | collective-permute-start | bytes 319496 | tf_op jit(solution)/shard_map/ppermute | solution.py:47
  73.0 7.8 %collective-permute-start.19 = (s16[16,1664]{1,0:T(8,128)(2,1)S(1)}, s16[16,1664]{1,0:T(8,128)(2,1)S(1)}, u32[]{:S(2)}, u32[]{:S(2)}) collective-permute-start(s16[16,1664]{1,0:T(8,128)(2,1)S(1)} %get-tuple-element.64), channel_id=1, source_target_pairs={{0,2},{1,3},{2,0},{3,1},{4,6},{5,7},{6,4},{7,5},{8,10},{9,11},{10,... | collective-permute-start | bytes 159752 | tf_op jit(solution)/shard_map/ppermute | solution.py:47
  74.9 7.5 %collective-permute-start.17 = (s16[16,1664]{1,0:T(8,128)(2,1)S(1)}, s16[16,1664]{1,0:T(8,128)(2,1)S(1)}, u32[]{:S(2)}, u32[]{:S(2)}) collective-permute-start(s16[16,1664]{1,0:T(8,128)(2,1)S(1)} %get-tuple-element.60), channel_id=1, source_target_pairs={{0,2},{1,3},{2,0},{3,1},{4,6},{5,7},{6,4},{7,5},{8,10},{9,11},{10,... | collective-permute-start | bytes 159752 | tf_op jit(solution)/shard_map/ppermute | solution.py:47
  77.3 5.7 %collective-permute-start.15 = (s16[16,1664]{1,0:T(8,128)(2,1)S(1)}, s16[16,1664]{1,0:T(8,128)(2,1)S(1)}, u32[]{:S(2)}, u32[]{:S(2)}) collective-permute-start(s16[16,1664]{1,0:T(8,128)(2,1)S(1)} %get-tuple-element.56), channel_id=1, source_target_pairs={{0,2},{1,3},{2,0},{3,1},{4,6},{5,7},{6,4},{7,5},{8,10},{9,11},{10,... | collective-permute-start | bytes 159752 | tf_op jit(solution)/shard_map/ppermute | solution.py:47

commit v3 on v2

--- a/solution.py
+++ b/solution.py
@@ -15,6 +15,8 @@
 STEPS = 32700.0
 TINY = 1e-37
 LANES = 128
+PAD = 8
+PIECES = 4
 
 
 def call(kernel, outs, ins, specs, name, scratch=(), limit=4, flops=0, moved=0):
@@ -77,37 +79,19 @@
     return [sum(((k >> b) & 1) << (bits - 1 - b) for b in range(bits)) for k in range(count)]
 
 
-def thirds(tiles):
-    first, second = tiles // 6, tiles // 2
-    return first, second, tiles - first - second
-
-
-def stats_kernel(me_ref, gain_ref, x_ref, w_ref, out_ref, part_ref, sem):
-    rows, width = x_ref.shape
-    fetch = pltpu.make_async_copy(w_ref.at[:, : part_ref.shape[1]], part_ref, sem)
-    fetch.start()
-    total = jnp.zeros((rows, LANES), jnp.float32)
-    squares = jnp.zeros((rows, LANES), jnp.float32)
-    for c in range(0, width, LANES):
-        part = x_ref[:, c : c + LANES].astype(jnp.float32)
-        total += part
-        squares += part * part
-    total = jnp.sum(total, axis=1, keepdims=True)
-    squares = jnp.sum(squares, axis=1, keepdims=True)
-    row = lax.broadcasted_iota(jnp.int32, (rows, rows), 0)
-    column = lax.broadcasted_iota(jnp.int32, (rows, rows), 1)
-    out_ref[0:1, :] = jnp.sum(jnp.where(row == column, total, 0.0), axis=0, keepdims=True)
-    out_ref[1:2, :] = jnp.sum(jnp.where(row == column, squares, 0.0), axis=0, keepdims=True)
-    fetch.wait()
-
-
 def fetch_kernel(starts, *refs):
     count = len(starts)
-    sources, shares, sems = refs[:count], refs[count + 1 : 2 * count + 1], refs[-1]
+    sources, shares, sems = refs[:count], refs[-count - 1 : -1], refs[-1]
     fetches = []
     for k, start in enumerate(starts):
-        source = sources[k] if start is None else sources[k].at[:, pl.ds(start, shares[k].shape[1])]
-        fetches.append(pltpu.make_async_copy(source, shares[k], sems.at[k]))
+        source, share = sources[k], shares[k]
+        if start is not None:
+            source = source.at[:, pl.ds(start, share.shape[1])]
+        pieces = PIECES if len(share.shape) > 2 or share.shape[0] % (16 * PIECES) == 0 else 1
+        step = share.shape[0] // pieces
+        for p in range(pieces):
+            at = pl.ds(p * step, step)
+            fetches.append(pltpu.make_async_copy(source.at[at], share.at[at], sems.at[k, p]))
     for fetch in fetches:
         fetch.start()
     for fetch in fetches:
@@ -119,22 +103,22 @@
     return call(
         functools.partial(fetch_kernel, [start for _, start, _ in items]),
         [held(shape, x.dtype) for shape, (x, _, _) in zip(shapes, items)],
-        (*[in_hbm(x) for x, _, _ in items], after),
-        [ANY] * (len(items) + 1),
+        (*[in_hbm(x) for x, _, _ in items], *after),
+        [ANY] * (len(items) + len(after)),
         name,
-        scratch=[pltpu.SemaphoreType.DMA((len(items),))],
+        scratch=[pltpu.SemaphoreType.DMA((len(items), PIECES))],
         moved=sum(2 * math.prod(shape) for shape in shapes),
     )
 
 
 def project_kernel(width_all, count, narrow_count, tile, me_ref, *refs):
-    stat_refs = refs[:-12]
-    x_ref, gain_ref, w_ref, kv_ref, first_ref, second_ref, kept_ref, sent_ref, normed, own, rest, sems = refs[-12:]
+    stat_refs = refs[:-11]
+    x_ref, gain_ref, w_ref, kv_ref, first_ref, kept_ref, sent_ref, normed, own, rest, sems = refs[-11:]
     rows, width = x_ref.shape
     half = rows // 2
     block = rows // count
     sub_width = width // narrow_count
-    done = first_ref.shape[1] + second_ref.shape[1]
+    done = first_ref.shape[1]
     fetches = [
         pltpu.make_async_copy(
             w_ref.at[:, done + t * tile : done + (t + 1) * tile], rest.at[:, t * tile : (t + 1) * tile], sems.at[t]
@@ -154,6 +138,7 @@
     center = sums / width_all
     spread = squares / width_all - center * center
     inverse = lax.rsqrt(spread + 1e-05)
+    gain = gain_ref[...].reshape(1, width)
     order = halving_order(count)
     for j in range(count):
         pick = slice(j * block, (j + 1) * block)
@@ -161,7 +146,7 @@
         for k, d in enumerate(order):
             place = jnp.where((me ^ d) == j, k, place)
         place = pl.multiple_of(place * block, 16)
-        scaled = (x_ref[pick, :].astype(jnp.float32) - center[pick]) * inverse[pick] * gain_ref[...]
+        scaled = (x_ref[pick, :].astype(jnp.float32) - center[pick]) * inverse[pick] * gain
         normed[pl.ds(place, block), :] = scaled.astype(jnp.bfloat16)
     for j in range(narrow_count):
         @pl.when(narrow == j)
@@ -172,32 +157,32 @@
         kept_ref[:, at] = got[:half, :]
         sent_ref[:, at] = got[half:, :]
 
-    def products(source, start):
-        @pl.loop(0, source.shape[1] // tile)
-        def _(t):
-            got = jnp.dot(
-                normed[...], source[:, pl.ds(pl.multiple_of(t * tile, tile), tile)], preferred_element_type=jnp.float32
-            )
-            put(got, pl.ds(pl.multiple_of(start + t * tile, tile), tile))
+    def products(source, t, start):
+        at = pl.ds(pl.multiple_of(t * tile, tile), tile)
+        got = jnp.dot(normed[...], source[:, at], preferred_element_type=jnp.float32)
+        put(got, pl.ds(pl.multiple_of(start + t * tile, tile), tile))
 
     put(jnp.dot(own[...], kv_ref[...], preferred_element_type=jnp.float32), slice(w_ref.shape[1], kept_ref.shape[1]))
-    products(first_ref, 0)
-    products(second_ref, first_ref.shape[1])
-    for fetch in fetches:
+
+    @pl.loop(0, done // tile)
+    def _(t):
+        products(first_ref, t, 0)
+
+    for t, fetch in enumerate(fetches):
         fetch.wait()
-    products(rest, done)
-
-
-def project(me, stats, x, gain, w, kv, first, second, width_all, count, narrow_count, tile):
+        products(rest, t, done)
+
+
+def project(me, stats, x, gain, w, kv, first, width_all, count, narrow_count, tile):
     rows, width = x.shape
     queries = w.shape[1]
-    rest = queries - first.shape[1] - second.shape[1]
+    rest = queries - first.shape[1]
     half = jax.ShapeDtypeStruct((rows // 2, queries + kv.shape[1]), jnp.float32)
     return call(
         functools.partial(project_kernel, width_all, count, narrow_count, tile),
         (half, half),
-        (me, *stats, x, gain, in_hbm(w), in_vmem(kv), in_vmem(first), in_vmem(second)),
-        [SCALAR] + [FULL] * (len(stats) + 2) + [ANY] + [FULL] * 3,
+        (me, *stats, x, gain, in_hbm(w), in_vmem(kv), in_vmem(first)),
+        [SCALAR] + [FULL] * (len(stats) + 2) + [ANY] + [FULL] * 2,
         "project",
         scratch=[
             pltpu.VMEM((rows, width), jnp.bfloat16),
@@ -205,7 +190,7 @@
             pltpu.VMEM((width, rest), jnp.bfloat16),
             pltpu.SemaphoreType.DMA((rest // tile,)),
         ],
-        limit=18,
+        limit=30,
         flops=2 * rows * width * queries,
         moved=2 * width * rest,
     )
@@ -243,13 +228,10 @@
         out_ref[:, :queries] = mine[:, :queries].astype(jnp.bfloat16)
         left = mine[:, queries:]
         width = left.shape[1]
-        for term in range(3):
+        for term in range(2):
             high = left.astype(jnp.bfloat16)
             out_ref[:, queries + term * width : queries + (term + 1) * width] = high
             left = left - high.astype(jnp.float32)
-
-
-PAD = 8
 
 
 def attend_kernel(head_dim, guards, lengths_ref, *refs):
@@ -272,7 +254,7 @@
     for ref in came_refs[1:]:
         terms = terms + ref[:, queries:].astype(jnp.float32)
     pair = 2 * head_dim
-    fresh = terms[:, :pair] + (terms[:, pair : 2 * pair] + terms[:, 2 * pair :])
+    fresh = terms[:, :pair] + terms[:, pair:]
     fresh = fresh.astype(jnp.bfloat16).astype(jnp.float32)
     place = lax.broadcasted_iota(jnp.int32, (total_heads, positions), 1)
     for r in range(rows):
@@ -322,28 +304,30 @@
     )
 
 
-def join_kernel(me_ref, *refs):
-    came_refs, out_ref, joined = refs[:-2], refs[-2], refs[-1]
-    rows = came_refs[0].shape[0]
-    narrow = me_ref[1]
-    came = [ref[...].astype(jnp.float32) for ref in came_refs]
-    for j in range(len(came)):
-        mine = came[0]
-        for d in range(1, len(came)):
-            mine = jnp.where((narrow ^ j) == d, came[d], mine)
-        joined[j * rows : (j + 1) * rows, :] = mine
-    out_ref[...] = joined[...].astype(jnp.bfloat16)
-
-
-def arrange_kernel(narrow_count, me_ref, *refs):
-    came_refs, out_ref, natural = refs[:-2], refs[-2], refs[-1]
-    block = came_refs[0].shape[0]
-    for d, ref in enumerate(came_refs):
-        natural[pl.ds(pl.multiple_of((me_ref[0] ^ d) * block, 16), block), :] = ref[...]
-    block = out_ref.shape[0] // narrow_count
-    for k, d in enumerate(halving_order(narrow_count)):
-        at = pl.ds(pl.multiple_of((me_ref[1] ^ d) * block, 16), block)
-        out_ref[k * block : (k + 1) * block, :] = natural[at, :]
+def join_kernel(guards, me_ref, *refs):
+    count = len(refs) - guards - 2
+    out_ref, joined = refs[-2:]
+    rows = refs[0].shape[0]
+    for d in range(count):
+        at = pl.ds(pl.multiple_of((me_ref[1] ^ d) * PAD, PAD), rows)
+        joined[at, :] = refs[d][...].astype(jnp.float32)
+    came = [joined[j * PAD : j * PAD + rows, :] for j in range(count)]
+    out_ref[...] = jnp.concatenate(came, axis=0).astype(jnp.bfloat16)
+
+
+def arrange_kernel(narrow_count, guards, me_ref, *refs):
+    count = len(refs) - guards - 1
+    out_ref = refs[-1]
+    block = refs[0].shape[0]
+    ratio = count // narrow_count
+    for d in range(count):
+        block_of = me_ref[0] ^ d
+        apart = (block_of // ratio) ^ me_ref[1]
+        place = jnp.int32(0)
+        for k, distance in enumerate(halving_order(narrow_count)):
+            place = jnp.where(apart == distance, k, place)
+        place = place * ratio + block_of % ratio
+        out_ref[pl.ds(pl.multiple_of(place * block, 16), block), :] = refs[d][...]
 
 
 def code(x, ref):
@@ -359,7 +343,8 @@
     return ref[:, :width].astype(jnp.int32).astype(jnp.float32) * (jnp.exp2(power) * (1.0 / STEPS))
 
 
-def output_kernel(tile, x_ref, w_ref, kept_ref, sent_ref, product):
+def output_kernel(tile, x_ref, w_ref, *refs):
+    kept_ref, sent_ref, product = refs[-3:]
     half = kept_ref.shape[0]
 
     @pl.loop(0, w_ref.shape[1] // tile)
@@ -371,7 +356,7 @@
     code(product[half:, :], sent_ref)
 
 
-def output_part(x, w):
+def output_part(x, w, after):
     rows, columns = x.shape[0], w.shape[1]
     return call(
         functools.partial(output_kernel, 256 if columns % 256 == 0 else LANES),
@@ -379,8 +364,8 @@
             jax.ShapeDtypeStruct((rows // 2, columns), jnp.float32),
             jax.ShapeDtypeStruct((rows // 2, columns + LANES), jnp.int16),
         ),
-        (x, in_vmem(w)),
-        [FULL, FULL],
+        (x, in_vmem(w), *after),
+        [FULL, FULL] + [ANY] * len(after),
         "output_part",
         scratch=[pltpu.VMEM((rows, columns), jnp.float32)],
         limit=6,
@@ -389,14 +374,15 @@
     )
 
 
-def halve_kernel(kept_ref, came_ref, still_ref, sent_ref):
+def halve_kernel(kept_ref, came_ref, *refs):
+    still_ref, sent_ref = refs[-2:]
     half = still_ref.shape[0]
     total = kept_ref[...] + decode(came_ref, kept_ref.shape[1])
     still_ref[...] = total[:half, :]
     code(total[half:, :], sent_ref)
 
 
-def halve(kept, came):
+def halve(kept, came, after):
     rows, columns = kept.shape
     return call(
         halve_kernel,
@@ -404,20 +390,45 @@
             jax.ShapeDtypeStruct((rows // 2, columns), jnp.float32),
             jax.ShapeDtypeStruct((rows // 2, columns + LANES), jnp.int16),
         ),
-        (kept, came),
-        [FULL, FULL],
+        (kept, came, *after),
+        [FULL, FULL] + [ANY] * len(after),
         "halve",
         moved=16 * kept.size,
     )
 
 
-def finish_kernel(*refs):
+def finish_kernel(kinds, *refs):
     out_ref = refs[-1]
-    at = 0
-    for kept_ref, came_ref in zip(refs[:-1:2], refs[1:-1:2]):
-        width = kept_ref.shape[1]
-        out_ref[:, at : at + width] = (kept_ref[...] + decode(came_ref, width)).astype(jnp.bfloat16)
+    at = k = 0
+    for kind in kinds:
+        width = refs[k].shape[1]
+        done = refs[k][...]
+        if kind == 2:
+            done = (done + decode(refs[k + 1], width)).astype(jnp.bfloat16)
+        out_ref[:, at : at + width] = done
         at += width
+        k += kind
+
+
+def finish(cuts, after=()):
+    parts = [x for cut in cuts for x in cut]
+    rows, columns = parts[0].shape[0], sum(cut[0].shape[1] for cut in cuts)
+    return call(
+        functools.partial(finish_kernel, [len(cut) for cut in cuts]),
+        jax.ShapeDtypeStruct((rows, columns), jnp.bfloat16),
+        (*parts, *after),
+        [FULL] * len(parts) + [ANY] * len(after),
+        "finish",
+        moved=8 * columns * rows,
+    )
+
+
+def cut_widths(columns):
+    tile = 256 if columns % 256 == 0 else LANES
+    tiles = columns // tile
+    outer = tiles // 4
+    inner = (tiles - 2 * outer + 1) // 2
+    return [tile * n for n in (outer, inner, tiles - 2 * outer - inner, outer)]
 
 
 def local(activations, norm_gain, query_weight, kv_weight, out_weight, kv_cache, lengths):
@@ -428,92 +439,88 @@
     rows, width = activations.shape
     queries = query_weight.shape[1]
     columns = out_weight.shape[1]
-    cuts = 3
-    cut = columns // cuts
     tile = 256
-    first, second, _ = thirds(queries // tile)
-    gain = norm_gain[None]
-    stats, first_part = call(
-        stats_kernel,
-        (jax.ShapeDtypeStruct((2, rows), jnp.float32), held((width, first * tile), jnp.bfloat16)),
-        (me, gain, activations, in_hbm(query_weight)),
-        [SCALAR, FULL, FULL, ANY],
-        "row_sums",
-        scratch=[pltpu.SemaphoreType.DMA],
-        moved=2 * width * first * tile,
-    )
-    second_part, kv_part = fetch(
-        [(query_weight, first * tile, second * tile), (kv_weight, None, None)], stats, "fetch_query_weight"
+    values = activations.astype(jnp.float32)
+    stats = jnp.stack([jnp.sum(values, axis=1), jnp.sum(values * values, axis=1)])
+    first_part, kv_part = fetch(
+        [(query_weight, 0, queries // tile // 3 * tile), (kv_weight, None, None)], [stats, me], "fetch_query_weight"
     )
     kept, sent = project(
         me,
         sent_apart(stats, "wide"),
         activations,
-        gain,
+        norm_gain,
         query_weight,
         kv_part,
         first_part,
-        second_part,
         width * wide_count,
         wide_count,
         narrow_count,
         tile,
     )
-    out_parts = list(fetch([(out_weight, 0, cut)], sent, "fetch_out_weight_0"))
-    guards = [out_parts[0]]
+    widths = cut_widths(columns)
+    cuts = [(out_weight, sum(widths[:k]), w) for k, w in enumerate(widths)]
     d = 1
     while 2 * d < wide_count:
-        kept, sent = fold(kept, swap(sent, "wide", d), guards)
-        guards = []
+        kept, sent = fold(kept, swap(sent, "wide", d), [])
         d *= 2
-    fetched = fetch([(out_weight, cut, cut), (kv_cache, None, None)], sent, "fetch_out_weight_1")
-    out_parts.append(fetched[0])
+    out_parts = [None] * 4
+    out_parts[0], cache = fetch([cuts[0], (kv_cache, None, None)], [sent], "fetch_out_weight_0")
     split = call(
         functools.partial(split_kernel, queries, 1),
-        [jax.ShapeDtypeStruct((own_rows, queries + 6 * head_dim), jnp.bfloat16)] * narrow_count,
-        (me, kept, swap(sent, "wide", d), in_vmem(fetched[0])),
+        [jax.ShapeDtypeStruct((own_rows, queries + 4 * head_dim), jnp.bfloat16)] * narrow_count,
+        (me, kept, swap(sent, "wide", d), in_vmem(out_parts[0])),
         [SCALAR] + [FULL] * 3,
         "split",
         moved=16 * kept.size,
     )
-    out_parts += fetch([(out_weight, 2 * cut, cut)], split[0], "fetch_out_weight_2")
-    context = attend(lengths, exchange(split, "narrow"), fetched[1], head_dim, queries, [out_parts[2]])
+    [out_parts[1]] = fetch([cuts[1]], [split[0]], "fetch_out_weight_1")
+    context = attend(lengths, exchange(split, "narrow"), cache, head_dim, queries, [out_parts[1]])
+    [out_parts[2]] = fetch([cuts[2]], [context[0]], "fetch_out_weight_2")
     returned = call(
-        join_kernel,
+        functools.partial(join_kernel, 1),
         jax.ShapeDtypeStruct((narrow_count * own_rows, queries), jnp.bfloat16),
-        (me, *exchange(context, "narrow")),
-        [SCALAR] + [FULL] * narrow_count,
+        (me, *exchange(context, "narrow"), in_vmem(out_parts[2])),
+        [SCALAR] + [FULL] * (narrow_count + 1),
         "join",
-        scratch=[pltpu.VMEM((narrow_count * own_rows, queries), jnp.float32)],
+        scratch=[pltpu.VMEM((narrow_count * PAD, queries), jnp.float32)],
         moved=4 * narrow_count * own_rows * queries,
     )
+    [out_parts[3]] = fetch([cuts[3]], [returned], "fetch_out_weight_3")
     arranged = call(
-        functools.partial(arrange_kernel, narrow_count),
+        functools.partial(arrange_kernel, narrow_count, 1),
         jax.ShapeDtypeStruct((rows, queries), jnp.bfloat16),
-        (me, *gather(returned, "wide")),
-        [SCALAR] + [FULL] * wide_count,
+        (me, *gather(returned, "wide"), in_vmem(out_parts[3])),
+        [SCALAR] + [FULL] * (wide_count + 1),
         "arrange",
-        scratch=[pltpu.VMEM((rows, queries), jnp.bfloat16)],
         moved=4 * rows * queries,
     )
-    pairs = []
-    for part in out_parts:
-        kept, sent = output_part(arranged, part)
-        d = 1
-        while d < narrow_count:
-            came = swap(sent, "narrow", d)
+    kepts, sents, halved, summed = [], [], [], []
+
+    def exchange_cut(k, after):
+        kept, sent, d = kepts[k], sents[k], 1
+        while 2 * d < narrow_count:
+            kept, sent = halve(kept, swap(sent, "narrow", d), after)
+            after = []
             d *= 2
-            if d < narrow_count:
-                kept, sent = halve(kept, came)
-        pairs += [kept, came]
-    return call(
-        finish_kernel,
-        jax.ShapeDtypeStruct((rows // narrow_count, columns), jnp.bfloat16),
-        pairs,
-        [FULL] * len(pairs),
-        "finish",
-        moved=8 * columns * rows // narrow_count,
-    )
+        halved.append(kept)
+        summed.append((kept, swap(sent, "narrow", d)))
+
+    def finish_cut(k, after):
+        summed[k] = (finish([summed[k]], after),)
+        return [summed[k][0]]
+
+    for k, part in enumerate(out_parts):
+        kept, sent = output_part(arranged, part, halved[-1:])
+        kepts.append(kept)
+        sents.append(sent)
+        after = [kept]
+        if k > 2:
+            after = after + finish_cut(k - 3, [kept])
+        if k:
+            exchange_cut(k - 1, after)
+    exchange_cut(len(out_parts) - 1, finish_cut(len(out_parts) - 3, []))
+    return finish(summed)
 
 
 def solution(mesh):

time: 84.1 us -> 84 us (level)
  starting transfers between devices: 21.5 us -> 26.1 us
  waiting for transfers between devices: 18.5 us -> 14.6 us
  local copies, waits for them, and re-layouts: 1.81 us -> 0.02 us
  other arithmetic: 0.08 us -> 1.4 us
    ppermute x20 -> x22, starting transfers between devices: 21.5 us -> 26.1 us  [swap(): return lax.ppermute(x, axis, [(i, i ^ distance) for i in range(count)])]
    ppermute x20 -> x22, waiting for transfers between devices: 18.5 us -> 14.6 us  [swap(): return lax.ppermute(x, axis, [(i, i ^ distance) for i in range(count)])]
    reduce_sum x0 -> x1, other arithmetic: none -> 1.31 us  [local(): jnp.sum(values, axis=1)]
    unnamed x6, local copies, waits for them, and re-layouts: 1.07 us -> 0.02 us
    pallas_call x18 -> x22, Pallas kernels: 41.7 us -> 41.5 us  [call(): pl.pallas_call(kernel, out_shape=outs, in_specs=specs, out_specs=jax.tree...]
  transfers between devices with their start and end apart: 20 -> 22, of which waited for: 12 -> 7; matrix products, arithmetic and copies ran while one was open for 0% -> 0% of each run, Pallas kernels for 25% -> 29%
where the time goes in v3:
time: 84 us; the launch traced here: 83.8 us
  Pallas kernels  41.5 us (49%)
  starting transfers between devices  26.1 us (31%)
  waiting for transfers between devices  14.6 us (17%)
  other arithmetic  1.4 us (2%)
    pallas_call x22, Pallas kernels, call(): pl.pallas_call(kernel, out_shape=outs, in_specs=specs, out_specs=jax.tree...  41.5 us
    ppermute x22, starting transfers between devices, swap(): return lax.ppermute(x, axis, [(i, i ^ distance) for i in range(count)])  26.1 us
    ppermute x22, waiting for transfers between devices, swap(): return lax.ppermute(x, axis, [(i, i ^ distance) for i in range(count)])  14.6 us
  transfers between devices with their start and end apart: 22, of which 7 were waited for; matrix products, arithmetic and copies ran while one was open for 0% of the time, Pallas kernels for 29%

profile of v3, /device:TPU:0, one launch (start us, length us, event | category | flops | bytes accessed | tf_op | source)
XLA Modules:
  0.0 83.8 jit_solution(4473245867017782033)
XLA Ops:
  0.0 1.3 %convert_reduce_fusion = (f32[64]{0:T(128)S(1)}, f32[64]{0:T(128)S(1)}) fusion(bf16[64,4608]{1,0:T(8,128)(2,1)} %refs_4_.1), kind=kLoop, calls=%fused_computation.1 | loop fusion | flops 1179520 | bytes 590336 | tf_op jit(solution)/shard_map/reduce_sum | solution.py:444
  1.3 2.5 %collective-permute-start.2 = (f32[2,64]{1,0:T(2,128)S(1)}, f32[2,64]{1,0:T(2,128)S(1)}, u32[]{:S(2)}, u32[]{:S(2)}) collective-permute-start(f32[2,64]{1,0:T(2,128)S(1)} %pad_maximum_fusion.refs_2_.refs_0_), channel_id=1, source_target_pairs={{0,12},{4,8},{8,4},{12,0},{1,13},{5,9},{9,5},{13,1},{2,14},{6,10},... | collective-permute-start | bytes 1544 | tf_op jit(solution)/shard_map/ppermute | solution.py:49
  4.6 4.1 %fetch_query_weight.1 = (bf16[4608,1024]{1,0:T(8,128)(2,1)S(1)}, bf16[1152,512]{1,0:T(8,128)(2,1)S(1)}) custom-call(bf16[4608,3072]{1,0:T(8,128)(2,1)} %refs_6_.1, bf16[1152,512]{1,0:T(8,128)(2,1)} %refs_1_.2, f32[2,64]{1,0:T(2,128)S(1)} %pad_maximum_fusion.refs_2_.refs_0_, s32[2]{0:T(128)S(1)} %pad_add_fusion.refs_3_.me_ref), custom_call_target="tpu_custom_call" | custom-call | bytes 10616832 | tf_op jit(solution)/shard_map/fetch_query_weight/pallas_call | solution.py:23
  8.8 9.9 %project.1 = (f32[32,3584]{1,0:T(8,128)S(1)}, f32[32,3584]{1,0:T(8,128)S(1)}) custom-call(s32[2]{0:T(128)S(1)} %pad_add_fusion.refs_3_.me_ref, f32[2,64]{1,0:T(2,128)S(1)} %pad_maximum_fusion.refs_2_.refs_0_, f32[2,64]{1,0:T(2,128)S(1)} %collective-permute-done.refs_1_, f32[2,64]{1,0:T(2,128)S(1)} %collective-permute-done.1.refs_2_, ...), custom_call_target="tpu_custom_call" | custom-call | flops 1811939328 | bytes 18874368 | tf_op jit(solution)/shard_map/project/pallas_call | solution.py:23
  19.2 1.4 %collective-permute-done.3.came_ref = f32[32,3584]{1,0:T(8,128)S(1)} collective-permute-done((f32[32,3584]{1,0:T(8,128)S(1)}, f32[32,3584]{1,0:T(8,128)S(1)}, u32[]{:S(2)}, u32[]{:S(2)}) %collective-permute-start.3) | collective-permute-done | bytes 458784 | tf_op jit(solution)/shard_map/ppermute | solution.py:49
  20.7 1.7 %collective-permute-start.4 = (f32[16,3584]{1,0:T(8,128)S(1)}, f32[16,3584]{1,0:T(8,128)S(1)}, u32[]{:S(2)}, u32[]{:S(2)}) collective-permute-start(f32[16,3584]{1,0:T(8,128)S(1)} %get-tuple-element.42.refs_2_), channel_id=1, source_target_pairs={{0,8},{4,12},{8,0},{12,4},{1,9},{5,13},{9,1},{13,5},{2,10},{6,14},... | collective-permute-start | bytes 688136 | tf_op jit(solution)/shard_map/ppermute | solution.py:49
  22.4 4.1 %fetch_out_weight_0.1 = (bf16[3072,1024]{1,0:T(8,128)(2,1)S(1)}, bf16[4,1024,512]{2,1,0:T(8,128)(2,1)S(1)}) custom-call(bf16[3072,4608]{1,0:T(8,128)(2,1)} %refs_0_.9, bf16[4,1024,512]{2,1,0:T(8,128)(2,1)} %refs_1_.3, f32[16,3584]{1,0:T(8,128)S(1)} %get-tuple-element.42.refs_2_), custom_call_target="tpu_custom_call" | custom-call | bytes 10485760 | tf_op jit(solution)/shard_map/fetch_out_weight_0/pallas_call | solution.py:23
  26.5 2.1 %collective-permute-done.4.came_ref = f32[16,3584]{1,0:T(8,128)S(1)} collective-permute-done((f32[16,3584]{1,0:T(8,128)S(1)}, f32[16,3584]{1,0:T(8,128)S(1)}, u32[]{:S(2)}, u32[]{:S(2)}) %collective-permute-start.4) | collective-permute-done | bytes 229408 | tf_op jit(solution)/shard_map/ppermute | solution.py:49
  28.7 0.7 split.1
  29.3 1.6 %collective-permute-start.5 = (bf16[4,4096]{1,0:T(4,128)(2,1)S(1)}, bf16[4,4096]{1,0:T(4,128)(2,1)S(1)}, u32[]{:S(2)}, u32[]{:S(2)}) collective-permute-start(bf16[4,4096]{1,0:T(4,128)(2,1)S(1)} %get-tuple-element.45), channel_id=1, source_target_pairs={{0,1},{1,0},{2,3},{3,2},{4,5},{5,4},{6,7},{7,6},{8,9},{9,8},{10,11... | collective-permute-start | bytes 98312 | tf_op jit(solution)/shard_map/ppermute | solution.py:49
  31.0 2.6 %collective-permute-start.6 = (bf16[4,4096]{1,0:T(4,128)(2,1)S(1)}, bf16[4,4096]{1,0:T(4,128)(2,1)S(1)}, u32[]{:S(2)}, u32[]{:S(2)}) collective-permute-start(bf16[4,4096]{1,0:T(4,128)(2,1)S(1)} %get-tuple-element.46), channel_id=1, source_target_pairs={{0,2},{1,3},{2,0},{3,1},{4,6},{5,7},{6,4},{7,5},{8,10},{9,11},{10,... | collective-permute-start | bytes 98312 | tf_op jit(solution)/shard_map/ppermute | solution.py:49
  33.8 3.4 %fetch_out_weight_1.1.refs_5_.w_ref = bf16[3072,1280]{1,0:T(8,128)(2,1)S(1)} custom-call(bf16[3072,4608]{1,0:T(8,128)(2,1)} %refs_0_.9, bf16[4,4096]{1,0:T(4,128)(2,1)S(1)} %get-tuple-element.44.refs_1_.refs_0_), custom_call_target="tpu_custom_call" | custom-call | bytes 7864320 | tf_op jit(solution)/shard_map/fetch_out_weight_1/pallas_call | solution.py:23
  37.2 2.1 %collective-permute-done.7.refs_3_ = bf16[4,4096]{1,0:T(4,128)(2,1)S(1)} collective-permute-done((bf16[4,4096]{1,0:T(4,128)(2,1)S(1)}, bf16[4,4096]{1,0:T(4,128)(2,1)S(1)}, u32[]{:S(2)}, u32[]{:S(2)}) %collective-permute-start.7) | collective-permute-done | bytes 32800 | tf_op jit(solution)/shard_map/ppermute | solution.py:49
  39.3 2.4 %attend.1 = (bf16[4,3072]{1,0:T(4,128)(2,1)S(1)}, bf16[4,3072]{1,0:T(4,128)(2,1)S(1)}, bf16[4,3072]{1,0:T(4,128)(2,1)S(1)}, bf16[4,3072]{1,0:T(4,128)(2,1)S(1)}) custom-call(s32[4]{0:T(128)S(1)} %copy-done.2, bf16[4,4096]{1,0:T(4,128)(2,1)S(1)} %get-tuple-element.44.refs_1_.refs_0_, bf16[4,4096]{1,0:T(4,128)(2,1)S(1)} %collective-permute-done.5.refs_1_, ...), custom_call_target="tpu_custom_call" | custom-call | flops 201326592 | tf_op jit(solution)/shard_map/attend/pallas_call | solution.py:23
  41.8 2.1 %collective-permute-start.9 = (bf16[4,3072]{1,0:T(4,128)(2,1)S(1)}, bf16[4,3072]{1,0:T(4,128)(2,1)S(1)}, u32[]{:S(2)}, u32[]{:S(2)}) collective-permute-start(bf16[4,3072]{1,0:T(4,128)(2,1)S(1)} %get-tuple-element.51), channel_id=1, source_target_pairs={{0,2},{1,3},{2,0},{3,1},{4,6},{5,7},{6,4},{7,5},{8,10},{9,11},{10,... | collective-permute-start | bytes 73736 | tf_op jit(solution)/shard_map/ppermute | solution.py:49
  43.9 2.3 %collective-permute-start.10 = (bf16[4,3072]{1,0:T(4,128)(2,1)S(1)}, bf16[4,3072]{1,0:T(4,128)(2,1)S(1)}, u32[]{:S(2)}, u32[]{:S(2)}) collective-permute-start(bf16[4,3072]{1,0:T(4,128)(2,1)S(1)} %get-tuple-element.52), channel_id=1, source_target_pairs={{0,3},{1,2},{2,1},{3,0},{4,7},{5,6},{6,5},{7,4},{8,11},{9,10},{10,... | collective-permute-start | bytes 73736 | tf_op jit(solution)/shard_map/ppermute | solution.py:49
  46.2 3.4 %fetch_out_weight_2.1.refs_4_.w_ref = bf16[3072,1280]{1,0:T(8,128)(2,1)S(1)} custom-call(bf16[3072,4608]{1,0:T(8,128)(2,1)} %refs_0_.9, bf16[4,3072]{1,0:T(4,128)(2,1)S(1)} %get-tuple-element.49.refs_1_.refs_0_), custom_call_target="tpu_custom_call" | custom-call | bytes 7864320 | tf_op jit(solution)/shard_map/fetch_out_weight_2/pallas_call | solution.py:23
  50.2 1.5 %collective-permute-start.12 = (bf16[16,3072]{1,0:T(8,128)(2,1)S(1)}, bf16[16,3072]{1,0:T(8,128)(2,1)S(1)}, u32[]{:S(2)}, u32[]{:S(2)}) collective-permute-start(bf16[16,3072]{1,0:T(8,128)(2,1)S(1)} %join.1.refs_1_.refs_0_), channel_id=1, source_target_pairs={{0,8},{4,12},{8,0},{12,4},{1,9},{5,13},{9,1},{13,5},{2,10},{6,14},... | collective-permute-start | bytes 294920 | tf_op jit(solution)/shard_map/ppermute | solution.py:49
  51.6 3.2 %collective-permute-done.12.refs_2_ = bf16[16,3072]{1,0:T(8,128)(2,1)S(1)} collective-permute-done((bf16[16,3072]{1,0:T(8,128)(2,1)S(1)}, bf16[16,3072]{1,0:T(8,128)(2,1)S(1)}, u32[]{:S(2)}, u32[]{:S(2)}) %collective-permute-start.12) | collective-permute-done | bytes 98336 | tf_op jit(solution)/shard_map/ppermute | solution.py:49
  54.9 2.9 %fetch_out_weight_3.1.refs_4_.w_ref = bf16[3072,1024]{1,0:T(8,128)(2,1)S(1)} custom-call(bf16[3072,4608]{1,0:T(8,128)(2,1)} %refs_0_.9, bf16[16,3072]{1,0:T(8,128)(2,1)S(1)} %join.1.refs_1_.refs_0_), custom_call_target="tpu_custom_call" | custom-call | bytes 6291456 | tf_op jit(solution)/shard_map/fetch_out_weight_3/pallas_call | solution.py:23
  58.4 1.8 %output_part.4 = (f32[32,1024]{1,0:T(8,128)S(1)}, s16[32,1152]{1,0:T(8,128)(2,1)S(1)}) custom-call(bf16[64,3072]{1,0:T(8,128)(2,1)S(1)} %arrange.1.x_ref, bf16[3072,1024]{1,0:T(8,128)(2,1)S(1)} %get-tuple-element.43.refs_0_.w_ref), custom_call_target="tpu_custom_call" | custom-call | flops 402653184 | bytes 393216 | tf_op jit(solution)/shard_map/output_part/pallas_call | solution.py:23
  60.2 2.1 %output_part.5 = (f32[32,1280]{1,0:T(8,128)S(1)}, s16[32,1408]{1,0:T(8,128)(2,1)S(1)}) custom-call(bf16[64,3072]{1,0:T(8,128)(2,1)S(1)} %arrange.1.x_ref, bf16[3072,1280]{1,0:T(8,128)(2,1)S(1)} %fetch_out_weight_1.1.refs_5_.w_ref), custom_call_target="tpu_custom_call" | custom-call | flops 503316480 | bytes 393216 | tf_op jit(solution)/shard_map/output_part/pallas_call | solution.py:23
  62.3 2.1 %collective-permute-start.16 = (s16[32,1408]{1,0:T(8,128)(2,1)S(1)}, s16[32,1408]{1,0:T(8,128)(2,1)S(1)}, u32[]{:S(2)}, u32[]{:S(2)}) collective-permute-start(s16[32,1408]{1,0:T(8,128)(2,1)S(1)} %get-tuple-element.58), channel_id=1, source_target_pairs={{0,1},{1,0},{2,3},{3,2},{4,5},{5,4},{6,7},{7,6},{8,9},{9,8},{10,11... | collective-permute-start | bytes 270344 | tf_op jit(solution)/shard_map/ppermute | solution.py:49
  65.1 2.1 %output_part.6 = (f32[32,1280]{1,0:T(8,128)S(1)}, s16[32,1408]{1,0:T(8,128)(2,1)S(1)}) custom-call(bf16[64,3072]{1,0:T(8,128)(2,1)S(1)} %arrange.1.x_ref, bf16[3072,1280]{1,0:T(8,128)(2,1)S(1)} %fetch_out_weight_2.1.refs_4_.w_ref, f32[16,1024]{1,0:T(8,128)S(1)} %get-tuple-element.56.refs_0_), custom_call_target="tpu_custom_call" | custom-call | flops 503316480 | bytes 393216 | tf_op jit(solution)/shard_map/output_part/pallas_call | solution.py:23
  67.7 1.8 %output_part.7 = (f32[32,1024]{1,0:T(8,128)S(1)}, s16[32,1152]{1,0:T(8,128)(2,1)S(1)}) custom-call(bf16[64,3072]{1,0:T(8,128)(2,1)S(1)} %arrange.1.x_ref, bf16[3072,1024]{1,0:T(8,128)(2,1)S(1)} %fetch_out_weight_3.1.refs_4_.w_ref, f32[16,1280]{1,0:T(8,128)S(1)} %get-tuple-element.60.refs_0_), custom_call_target="tpu_custom_call" | custom-call | flops 402653184 | bytes 393216 | tf_op jit(solution)/shard_map/output_part/pallas_call | solution.py:23
  69.5 1.8 %collective-permute-start.20 = (s16[32,1152]{1,0:T(8,128)(2,1)S(1)}, s16[32,1152]{1,0:T(8,128)(2,1)S(1)}, u32[]{:S(2)}, u32[]{:S(2)}) collective-permute-start(s16[32,1152]{1,0:T(8,128)(2,1)S(1)} %get-tuple-element.66), channel_id=1, source_target_pairs={{0,1},{1,0},{2,3},{3,2},{4,5},{5,4},{6,7},{7,6},{8,9},{9,8},{10,11... | collective-permute-start | bytes 221192 | tf_op jit(solution)/shard_map/ppermute | solution.py:49
  71.3 1.0 %collective-permute-start.15 = (s16[16,1152]{1,0:T(8,128)(2,1)S(1)}, s16[16,1152]{1,0:T(8,128)(2,1)S(1)}, u32[]{:S(2)}, u32[]{:S(2)}) collective-permute-start(s16[16,1152]{1,0:T(8,128)(2,1)S(1)} %get-tuple-element.57), channel_id=1, source_target_pairs={{0,2},{1,3},{2,0},{3,1},{4,6},{5,7},{6,4},{7,5},{8,10},{9,11},{10,... | collective-permute-start | bytes 110600 | tf_op jit(solution)/shard_map/ppermute | solution.py:49
  72.4 1.9 %collective-permute-start.17 = (s16[16,1408]{1,0:T(8,128)(2,1)S(1)}, s16[16,1408]{1,0:T(8,128)(2,1)S(1)}, u32[]{:S(2)}, u32[]{:S(2)}) collective-permute-start(s16[16,1408]{1,0:T(8,128)(2,1)S(1)} %get-tuple-element.62), channel_id=1, source_target_pairs={{0,2},{1,3},{2,0},{3,1},{4,6},{5,7},{6,4},{7,5},{8,10},{9,11},{10,... | collective-permute-start | bytes 135176 | tf_op jit(solution)/shard_map/ppermute | solution.py:49
  74.2 2.8 %collective-permute-done.15.refs_1_ = s16[16,1152]{1,0:T(8,128)(2,1)S(1)} collective-permute-done((s16[16,1152]{1,0:T(8,128)(2,1)S(1)}, s16[16,1152]{1,0:T(8,128)(2,1)S(1)}, u32[]{:S(2)}, u32[]{:S(2)}) %collective-permute-start.15) | collective-permute-done | bytes 36896 | tf_op jit(solution)/shard_map/ppermute | solution.py:49
  78.2 2.5 %collective-permute-start.21 = (s16[16,1152]{1,0:T(8,128)(2,1)S(1)}, s16[16,1152]{1,0:T(8,128)(2,1)S(1)}, u32[]{:S(2)}, u32[]{:S(2)}) collective-permute-start(s16[16,1152]{1,0:T(8,128)(2,1)S(1)} %get-tuple-element.68), channel_id=1, source_target_pairs={{0,2},{1,3},{2,0},{3,1},{4,6},{5,7},{6,4},{7,5},{8,10},{9,11},{10,... | collective-permute-start | bytes 110600 | tf_op jit(solution)/shard_map/ppermute | solution.py:49
  80.7 2.4 %collective-permute-done.21.refs_5_ = s16[16,1152]{1,0:T(8,128)(2,1)S(1)} collective-permute-done((s16[16,1152]{1,0:T(8,128)(2,1)S(1)}, s16[16,1152]{1,0:T(8,128)(2,1)S(1)}, u32[]{:S(2)}, u32[]{:S(2)}) %collective-permute-start.21) | collective-permute-done | bytes 36896 | tf_op jit(solution)/shard_map/ppermute | solution.py:49
  83.1 0.8 finish.5
  (43 shorter events, 5.3 us)
Async XLA Ops:
  1.3 7.4 %collective-permute-start.2 = (f32[2,64]{1,0:T(2,128)S(1)}, f32[2,64]{1,0:T(2,128)S(1)}, u32[]{:S(2)}, u32[]{:S(2)}) collective-permute-start(f32[2,64]{1,0:T(2,128)S(1)} %pad_maximum_fusion.refs_2_.refs_0_), channel_id=1, source_target_pairs={{0,12},{4,8},{8,4},{12,0},{1,13},{5,9},{9,5},{13,1},{2,14},{6,10},... | collective-permute-start | bytes 1544 | tf_op jit(solution)/shard_map/ppermute | solution.py:49
  3.8 4.9 %collective-permute-start.1 = (f32[2,64]{1,0:T(2,128)S(1)}, f32[2,64]{1,0:T(2,128)S(1)}, u32[]{:S(2)}, u32[]{:S(2)}) collective-permute-start(f32[2,64]{1,0:T(2,128)S(1)} %pad_maximum_fusion.refs_2_.refs_0_), channel_id=1, source_target_pairs={{0,8},{4,12},{8,0},{12,4},{1,9},{5,13},{9,1},{13,5},{2,10},{6,14},... | collective-permute-start | bytes 1544 | tf_op jit(solution)/shard_map/ppermute | solution.py:49
  4.4 4.3 %collective-permute-start = (f32[2,64]{1,0:T(2,128)S(1)}, f32[2,64]{1,0:T(2,128)S(1)}, u32[]{:S(2)}, u32[]{:S(2)}) collective-permute-start(f32[2,64]{1,0:T(2,128)S(1)} %pad_maximum_fusion.refs_2_.refs_0_), channel_id=1, source_target_pairs={{0,4},{4,0},{8,12},{12,8},{1,5},{5,1},{9,13},{13,9},{2,6},{6,2},{1... | collective-permute-start | bytes 1544 | tf_op jit(solution)/shard_map/ppermute | solution.py:49
  4.6 4.2 %copy-start = (bf16[64,4608]{1,0:T(8,128)(2,1)S(1)}, bf16[64,4608]{1,0:T(8,128)(2,1)}, u32[]{:S(2)}) copy-start(bf16[64,4608]{1,0:T(8,128)(2,1)} %refs_4_.1) | copy-start | bytes 1769476
  4.6 4.2 %copy-start.1 = (f32[4608]{0:T(1024)S(1)}, f32[4608]{0:T(1024)}, u32[]{:S(2)}) copy-start(f32[4608]{0:T(1024)} %refs_5_.1) | copy-start | bytes 55300
  18.7 2.0 %collective-permute-start.3 = (f32[32,3584]{1,0:T(8,128)S(1)}, f32[32,3584]{1,0:T(8,128)S(1)}, u32[]{:S(2)}, u32[]{:S(2)}) collective-permute-start(f32[32,3584]{1,0:T(8,128)S(1)} %get-tuple-element.40), channel_id=1, source_target_pairs={{0,4},{4,0},{8,12},{12,8},{1,5},{5,1},{9,13},{13,9},{2,6},{6,2},{1... | collective-permute-start | bytes 1376264 | tf_op jit(solution)/shard_map/ppermute | solution.py:49
  20.7 7.9 %collective-permute-start.4 = (f32[16,3584]{1,0:T(8,128)S(1)}, f32[16,3584]{1,0:T(8,128)S(1)}, u32[]{:S(2)}, u32[]{:S(2)}) collective-permute-start(f32[16,3584]{1,0:T(8,128)S(1)} %get-tuple-element.42.refs_2_), channel_id=1, source_target_pairs={{0,8},{4,12},{8,0},{12,4},{1,9},{5,13},{9,1},{13,5},{2,10},{6,14},... | collective-permute-start | bytes 688136 | tf_op jit(solution)/shard_map/ppermute | solution.py:49
  29.3 7.8 %collective-permute-start.5 = (bf16[4,4096]{1,0:T(4,128)(2,1)S(1)}, bf16[4,4096]{1,0:T(4,128)(2,1)S(1)}, u32[]{:S(2)}, u32[]{:S(2)}) collective-permute-start(bf16[4,4096]{1,0:T(4,128)(2,1)S(1)} %get-tuple-element.45), channel_id=1, source_target_pairs={{0,1},{1,0},{2,3},{3,2},{4,5},{5,4},{6,7},{7,6},{8,9},{9,8},{10,11... | collective-permute-start | bytes 98312 | tf_op jit(solution)/shard_map/ppermute | solution.py:49
  31.0 6.2 %collective-permute-start.6 = (bf16[4,4096]{1,0:T(4,128)(2,1)S(1)}, bf16[4,4096]{1,0:T(4,128)(2,1)S(1)}, u32[]{:S(2)}, u32[]{:S(2)}) collective-permute-start(bf16[4,4096]{1,0:T(4,128)(2,1)S(1)} %get-tuple-element.46), channel_id=1, source_target_pairs={{0,2},{1,3},{2,0},{3,1},{4,6},{5,7},{6,4},{7,5},{8,10},{9,11},{10,... | collective-permute-start | bytes 98312 | tf_op jit(solution)/shard_map/ppermute | solution.py:49
  33.6 5.7 %collective-permute-start.7 = (bf16[4,4096]{1,0:T(4,128)(2,1)S(1)}, bf16[4,4096]{1,0:T(4,128)(2,1)S(1)}, u32[]{:S(2)}, u32[]{:S(2)}) collective-permute-start(bf16[4,4096]{1,0:T(4,128)(2,1)S(1)} %get-tuple-element.47), channel_id=1, source_target_pairs={{0,3},{1,2},{2,1},{3,0},{4,7},{5,6},{6,5},{7,4},{8,11},{9,10},{10,... | collective-permute-start | bytes 98312 | tf_op jit(solution)/shard_map/ppermute | solution.py:49
  33.8 5.5 %copy-start.2 = (s32[4]{0:T(128)S(1)}, s32[4]{0:T(128)}, u32[]{:S(2)}) copy-start(s32[4]{0:T(128)} %lengths_ref.1) | copy-start | bytes 52
  41.7 7.8 %collective-permute-start.8 = (bf16[4,3072]{1,0:T(4,128)(2,1)S(1)}, bf16[4,3072]{1,0:T(4,128)(2,1)S(1)}, u32[]{:S(2)}, u32[]{:S(2)}) collective-permute-start(bf16[4,3072]{1,0:T(4,128)(2,1)S(1)} %get-tuple-element.50), channel_id=1, source_target_pairs={{0,1},{1,0},{2,3},{3,2},{4,5},{5,4},{6,7},{7,6},{8,9},{9,8},{10,11... | collective-permute-start | bytes 73736 | tf_op jit(solution)/shard_map/ppermute | solution.py:49
  41.8 7.8 %collective-permute-start.9 = (bf16[4,3072]{1,0:T(4,128)(2,1)S(1)}, bf16[4,3072]{1,0:T(4,128)(2,1)S(1)}, u32[]{:S(2)}, u32[]{:S(2)}) collective-permute-start(bf16[4,3072]{1,0:T(4,128)(2,1)S(1)} %get-tuple-element.51), channel_id=1, source_target_pairs={{0,2},{1,3},{2,0},{3,1},{4,6},{5,7},{6,4},{7,5},{8,10},{9,11},{10,... | collective-permute-start | bytes 73736 | tf_op jit(solution)/shard_map/ppermute | solution.py:49
  43.9 5.7 %collective-permute-start.10 = (bf16[4,3072]{1,0:T(4,128)(2,1)S(1)}, bf16[4,3072]{1,0:T(4,128)(2,1)S(1)}, u32[]{:S(2)}, u32[]{:S(2)}) collective-permute-start(bf16[4,3072]{1,0:T(4,128)(2,1)S(1)} %get-tuple-element.52), channel_id=1, source_target_pairs={{0,3},{1,2},{2,1},{3,0},{4,7},{5,6},{6,5},{7,4},{8,11},{9,10},{10,... | collective-permute-start | bytes 73736 | tf_op jit(solution)/shard_map/ppermute | solution.py:49
  50.2 4.7 %collective-permute-start.12 = (bf16[16,3072]{1,0:T(8,128)(2,1)S(1)}, bf16[16,3072]{1,0:T(8,128)(2,1)S(1)}, u32[]{:S(2)}, u32[]{:S(2)}) collective-permute-start(bf16[16,3072]{1,0:T(8,128)(2,1)S(1)} %join.1.refs_1_.refs_0_), channel_id=1, source_target_pairs={{0,8},{4,12},{8,0},{12,4},{1,9},{5,13},{9,1},{13,5},{2,10},{6,14},... | collective-permute-start | bytes 294920 | tf_op jit(solution)/shard_map/ppermute | solution.py:49
  51.6 6.1 %collective-permute-start.11 = (bf16[16,3072]{1,0:T(8,128)(2,1)S(1)}, bf16[16,3072]{1,0:T(8,128)(2,1)S(1)}, u32[]{:S(2)}, u32[]{:S(2)}) collective-permute-start(bf16[16,3072]{1,0:T(8,128)(2,1)S(1)} %join.1.refs_1_.refs_0_), channel_id=1, source_target_pairs={{0,4},{4,0},{8,12},{12,8},{1,5},{5,1},{9,13},{13,9},{2,6},{6,2},{1... | collective-permute-start | bytes 294920 | tf_op jit(solution)/shard_map/ppermute | solution.py:49
  54.9 2.9 %collective-permute-start.13 = (bf16[16,3072]{1,0:T(8,128)(2,1)S(1)}, bf16[16,3072]{1,0:T(8,128)(2,1)S(1)}, u32[]{:S(2)}, u32[]{:S(2)}) collective-permute-start(bf16[16,3072]{1,0:T(8,128)(2,1)S(1)} %collective-permute-done.12.refs_2_), channel_id=1, source_target_pairs={{0,4},{4,0},{8,12},{12,8},{1,5},{5,1},{9,13},{13,9},{2,6},{6,2},{1... | collective-permute-start | bytes 294920 | tf_op jit(solution)/shard_map/ppermute | solution.py:49
  60.1 4.7 %collective-permute-start.14 = (s16[32,1152]{1,0:T(8,128)(2,1)S(1)}, s16[32,1152]{1,0:T(8,128)(2,1)S(1)}, u32[]{:S(2)}, u32[]{:S(2)}) collective-permute-start(s16[32,1152]{1,0:T(8,128)(2,1)S(1)} %get-tuple-element.54), channel_id=1, source_target_pairs={{0,1},{1,0},{2,3},{3,2},{4,5},{5,4},{6,7},{7,6},{8,9},{9,8},{10,11... | collective-permute-start | bytes 221192 | tf_op jit(solution)/shard_map/ppermute | solution.py:49
  62.3 5.2 %collective-permute-start.16 = (s16[32,1408]{1,0:T(8,128)(2,1)S(1)}, s16[32,1408]{1,0:T(8,128)(2,1)S(1)}, u32[]{:S(2)}, u32[]{:S(2)}) collective-permute-start(s16[32,1408]{1,0:T(8,128)(2,1)S(1)} %get-tuple-element.58), channel_id=1, source_target_pairs={{0,1},{1,0},{2,3},{3,2},{4,5},{5,4},{6,7},{7,6},{8,9},{9,8},{10,11... | collective-permute-start | bytes 270344 | tf_op jit(solution)/shard_map/ppermute | solution.py:49
  67.2 10.0 %collective-permute-start.18 = (s16[32,1408]{1,0:T(8,128)(2,1)S(1)}, s16[32,1408]{1,0:T(8,128)(2,1)S(1)}, u32[]{:S(2)}, u32[]{:S(2)}) collective-permute-start(s16[32,1408]{1,0:T(8,128)(2,1)S(1)} %get-tuple-element.63), channel_id=1, source_target_pairs={{0,1},{1,0},{2,3},{3,2},{4,5},{5,4},{6,7},{7,6},{8,9},{9,8},{10,11... | collective-permute-start | bytes 270344 | tf_op jit(solution)/shard_map/ppermute | solution.py:49
  69.5 8.5 %collective-permute-start.20 = (s16[32,1152]{1,0:T(8,128)(2,1)S(1)}, s16[32,1152]{1,0:T(8,128)(2,1)S(1)}, u32[]{:S(2)}, u32[]{:S(2)}) collective-permute-start(s16[32,1152]{1,0:T(8,128)(2,1)S(1)} %get-tuple-element.66), channel_id=1, source_target_pairs={{0,1},{1,0},{2,3},{3,2},{4,5},{5,4},{6,7},{7,6},{8,9},{9,8},{10,11... | collective-permute-start | bytes 221192 | tf_op jit(solution)/shard_map/ppermute | solution.py:49
  71.3 5.7 %collective-permute-start.15 = (s16[16,1152]{1,0:T(8,128)(2,1)S(1)}, s16[16,1152]{1,0:T(8,128)(2,1)S(1)}, u32[]{:S(2)}, u32[]{:S(2)}) collective-permute-start(s16[16,1152]{1,0:T(8,128)(2,1)S(1)} %get-tuple-element.57), channel_id=1, source_target_pairs={{0,2},{1,3},{2,0},{3,1},{4,6},{5,7},{6,4},{7,5},{8,10},{9,11},{10,... | collective-permute-start | bytes 110600 | tf_op jit(solution)/shard_map/ppermute | solution.py:49
  72.4 5.5 %collective-permute-start.17 = (s16[16,1408]{1,0:T(8,128)(2,1)S(1)}, s16[16,1408]{1,0:T(8,128)(2,1)S(1)}, u32[]{:S(2)}, u32[]{:S(2)}) collective-permute-start(s16[16,1408]{1,0:T(8,128)(2,1)S(1)} %get-tuple-element.62), channel_id=1, source_target_pairs={{0,2},{1,3},{2,0},{3,1},{4,6},{5,7},{6,4},{7,5},{8,10},{9,11},{10,... | collective-permute-start | bytes 135176 | tf_op jit(solution)/shard_map/ppermute | solution.py:49
  77.3 5.8 %collective-permute-start.19 = (s16[16,1408]{1,0:T(8,128)(2,1)S(1)}, s16[16,1408]{1,0:T(8,128)(2,1)S(1)}, u32[]{:S(2)}, u32[]{:S(2)}) collective-permute-start(s16[16,1408]{1,0:T(8,128)(2,1)S(1)} %get-tuple-element.65), channel_id=1, source_target_pairs={{0,2},{1,3},{2,0},{3,1},{4,6},{5,7},{6,4},{7,5},{8,10},{9,11},{10,... | collective-permute-start | bytes 135176 | tf_op jit(solution)/shard_map/ppermute | solution.py:49
  78.2 4.9 %collective-permute-start.21 = (s16[16,1152]{1,0:T(8,128)(2,1)S(1)}, s16[16,1152]{1,0:T(8,128)(2,1)S(1)}, u32[]{:S(2)}, u32[]{:S(2)}) collective-permute-start(s16[16,1152]{1,0:T(8,128)(2,1)S(1)} %get-tuple-element.68), channel_id=1, source_target_pairs={{0,2},{1,3},{2,0},{3,1},{4,6},{5,7},{6,4},{7,5},{8,10},{9,11},{10,... | collective-permute-start | bytes 110600 | tf_op jit(solution)/shard_map/ppermute | solution.py:49

commit v4 on v3

--- a/solution.py
+++ b/solution.py
@@ -79,9 +79,7 @@
     return [sum(((k >> b) & 1) << (bits - 1 - b) for b in range(bits)) for k in range(count)]
 
 
-def fetch_kernel(starts, *refs):
-    count = len(starts)
-    sources, shares, sems = refs[:count], refs[-count - 1 : -1], refs[-1]
+def fetches_of(starts, sources, shares, sems):
     fetches = []
     for k, start in enumerate(starts):
         source, share = sources[k], shares[k]
@@ -92,6 +90,12 @@
         for p in range(pieces):
             at = pl.ds(p * step, step)
             fetches.append(pltpu.make_async_copy(source.at[at], share.at[at], sems.at[k, p]))
+    return fetches
+
+
+def fetch_kernel(starts, *refs):
+    count = len(starts)
+    fetches = fetches_of(starts, refs[:count], refs[-count - 1 : -1], refs[-1])
     for fetch in fetches:
         fetch.start()
     for fetch in fetches:
@@ -111,22 +115,19 @@
     )
 
 
-def project_kernel(width_all, count, narrow_count, tile, me_ref, *refs):
-    stat_refs = refs[:-11]
-    x_ref, gain_ref, w_ref, kv_ref, first_ref, kept_ref, sent_ref, normed, own, rest, sems = refs[-11:]
+def project_kernel(many, width_all, count, narrow_count, tile, me_ref, *refs):
+    stat_refs, refs = refs[:many], refs[many:]
+    x_ref, gain_ref, w_ref, kv_ref, first_ref, kept_ref, sent_ref, normed, own, *groups, sems = refs
     rows, width = x_ref.shape
     half = rows // 2
     block = rows // count
     sub_width = width // narrow_count
     done = first_ref.shape[1]
-    fetches = [
-        pltpu.make_async_copy(
-            w_ref.at[:, done + t * tile : done + (t + 1) * tile], rest.at[:, t * tile : (t + 1) * tile], sems.at[t]
-        )
-        for t in range(rest.shape[1] // tile)
-    ]
+    starts = [done + sum(ref.shape[1] for ref in groups[:g]) for g in range(len(groups))]
+    fetches = [fetches_of([start], [w_ref], [ref], sems.at[pl.ds(g, 1)]) for g, (start, ref) in enumerate(zip(starts, groups))]
     for fetch in fetches:
-        fetch.start()
+        for piece in fetch:
+            piece.start()
     me, narrow = me_ref[0], me_ref[1]
     stats = stat_refs[0][...]
     for ref in stat_refs[1:]:
@@ -157,29 +158,30 @@
         kept_ref[:, at] = got[:half, :]
         sent_ref[:, at] = got[half:, :]
 
-    def products(source, t, start):
-        at = pl.ds(pl.multiple_of(t * tile, tile), tile)
-        got = jnp.dot(normed[...], source[:, at], preferred_element_type=jnp.float32)
-        put(got, pl.ds(pl.multiple_of(start + t * tile, tile), tile))
+    def products(source, start):
+        @pl.loop(0, source.shape[1] // tile)
+        def _(t):
+            at = pl.ds(pl.multiple_of(t * tile, tile), tile)
+            got = jnp.dot(normed[...], source[:, at], preferred_element_type=jnp.float32)
+            put(got, pl.ds(pl.multiple_of(start + t * tile, tile), tile))
 
     put(jnp.dot(own[...], kv_ref[...], preferred_element_type=jnp.float32), slice(w_ref.shape[1], kept_ref.shape[1]))
-
-    @pl.loop(0, done // tile)
-    def _(t):
-        products(first_ref, t, 0)
-
-    for t, fetch in enumerate(fetches):
-        fetch.wait()
-        products(rest, t, done)
+    products(first_ref, 0)
+    for start, fetch, ref in zip(starts, fetches, groups):
+        for piece in fetch:
+            piece.wait()
+        products(ref, start)
 
 
 def project(me, stats, x, gain, w, kv, first, width_all, count, narrow_count, tile):
     rows, width = x.shape
     queries = w.shape[1]
-    rest = queries - first.shape[1]
+    tiles = (queries - first.shape[1]) // tile
+    groups = [tiles * 4 // 9, (tiles - tiles * 4 // 9 + 1) // 2]
+    groups.append(tiles - sum(groups))
     half = jax.ShapeDtypeStruct((rows // 2, queries + kv.shape[1]), jnp.float32)
     return call(
-        functools.partial(project_kernel, width_all, count, narrow_count, tile),
+        functools.partial(project_kernel, len(stats), width_all, count, narrow_count, tile),
         (half, half),
         (me, *stats, x, gain, in_hbm(w), in_vmem(kv), in_vmem(first)),
         [SCALAR] + [FULL] * (len(stats) + 2) + [ANY] + [FULL] * 2,
@@ -187,12 +189,12 @@
         scratch=[
             pltpu.VMEM((rows, width), jnp.bfloat16),
             pltpu.VMEM((rows, width // narrow_count), jnp.bfloat16),
-            pltpu.VMEM((width, rest), jnp.bfloat16),
-            pltpu.SemaphoreType.DMA((rest // tile,)),
+            *[pltpu.VMEM((width, n * tile), jnp.bfloat16) for n in groups],
+            pltpu.SemaphoreType.DMA((len(groups), PIECES)),
         ],
         limit=30,
         flops=2 * rows * width * queries,
-        moved=2 * width * rest,
+        moved=2 * width * tiles * tile,
     )
 
 
@@ -216,28 +218,26 @@
 
 
 def split_kernel(queries, guards, me_ref, kept_ref, came_ref, *refs):
-    out_refs = refs[guards:]
+    out_refs, slots = refs[guards:-1], refs[-1]
     count, rows = len(out_refs), out_refs[0].shape[0]
     narrow = me_ref[1]
     total = kept_ref[...] + came_ref[...]
-    parts = [total[j * rows : (j + 1) * rows, :] for j in range(count)]
+    for j in range(count):
+        slots[j * PAD : j * PAD + rows, :] = total[j * rows : (j + 1) * rows, :]
     for d, out_ref in enumerate(out_refs):
-        mine = parts[0]
-        for j in range(1, count):
-            mine = jnp.where((narrow ^ d) == j, parts[j], mine)
-        out_ref[:, :queries] = mine[:, :queries].astype(jnp.bfloat16)
-        left = mine[:, queries:]
-        width = left.shape[1]
-        for term in range(2):
-            high = left.astype(jnp.bfloat16)
-            out_ref[:, queries + term * width : queries + (term + 1) * width] = high
-            left = left - high.astype(jnp.float32)
-
-
-def attend_kernel(head_dim, guards, lengths_ref, *refs):
-    count = (len(refs) - guards - 3) // 2
-    came_refs, kv_ref = refs[:count], refs[count]
-    out_refs, heads, contexts = refs[count + 1 + guards : -2], refs[-2], refs[-1]
+        mine = slots[pl.ds(pl.multiple_of((narrow ^ d) * PAD, PAD), rows), :]
+        high = mine.astype(jnp.bfloat16)
+        out_ref[:, : mine.shape[1]] = high
+        out_ref[:, mine.shape[1] :] = (mine - high.astype(jnp.float32))[:, queries:].astype(jnp.bfloat16)
+
+
+def attend_kernel(head_dim, count, guards, start, lengths_ref, *refs):
+    came_refs, kv_ref, w_ref = refs[:count], refs[count], refs[count + 1]
+    refs = refs[count + 2 + guards :]
+    out_refs, share, (heads, contexts, sems) = refs[:count], refs[count], refs[count + 1 :]
+    fetches = fetches_of([start], [w_ref], [share], sems)
+    for fetch in fetches:
+        fetch.start()
     rows, positions = kv_ref.shape[0], kv_ref.shape[1]
     queries = out_refs[0].shape[1]
     each = queries // head_dim
@@ -285,20 +285,23 @@
             for k in range(slabs):
                 start = h * head_dim + k * LANES
                 ref[:, start : start + LANES] = contexts[k, at : at + rows, :].astype(jnp.bfloat16)
-
-
-def attend(lengths, came, kv, head_dim, queries, guards):
+    for fetch in fetches:
+        fetch.wait()
+
+
+def attend(lengths, came, kv, cut, head_dim, queries, guards):
     rows = kv.shape[0]
     count = len(came)
     all_heads = count * queries // head_dim
     scratch = pltpu.VMEM((head_dim // LANES, all_heads * PAD, LANES), jnp.float32)
-    return call(
-        functools.partial(attend_kernel, head_dim, len(guards)),
-        [jax.ShapeDtypeStruct((rows, queries), jnp.bfloat16)] * count,
-        (lengths, *came, in_vmem(kv), *map(in_vmem, guards)),
-        [SCALAR] + [FULL] * (count + 1 + len(guards)),
+    w, start, width = cut
+    return call(
+        functools.partial(attend_kernel, head_dim, count, len(guards), start),
+        [jax.ShapeDtypeStruct((rows, queries), jnp.bfloat16)] * count + [held((w.shape[0], width), w.dtype)],
+        (lengths, *came, in_vmem(kv), in_hbm(w), *map(in_vmem, guards)),
+        [SCALAR] + [FULL] * (count + 1) + [ANY] + [FULL] * len(guards),
         "attend",
-        scratch=[scratch, scratch],
+        scratch=[scratch, scratch, pltpu.SemaphoreType.DMA((1, PIECES))],
         limit=8,
         flops=4 * rows * count * queries * kv.shape[1],
     )
@@ -315,21 +318,6 @@
     out_ref[...] = jnp.concatenate(came, axis=0).astype(jnp.bfloat16)
 
 
-def arrange_kernel(narrow_count, guards, me_ref, *refs):
-    count = len(refs) - guards - 1
-    out_ref = refs[-1]
-    block = refs[0].shape[0]
-    ratio = count // narrow_count
-    for d in range(count):
-        block_of = me_ref[0] ^ d
-        apart = (block_of // ratio) ^ me_ref[1]
-        place = jnp.int32(0)
-        for k, distance in enumerate(halving_order(narrow_count)):
-            place = jnp.where(apart == distance, k, place)
-        place = place * ratio + block_of % ratio
-        out_ref[pl.ds(pl.multiple_of(place * block, 16), block), :] = refs[d][...]
-
-
 def code(x, ref):
     largest = jnp.maximum(jnp.max(jnp.abs(x), axis=1, keepdims=True), TINY)
     power = jnp.floor(jnp.log2(largest)) + 1.0
@@ -343,34 +331,47 @@
     return ref[:, :width].astype(jnp.int32).astype(jnp.float32) * (jnp.exp2(power) * (1.0 / STEPS))
 
 
-def output_kernel(tile, x_ref, w_ref, *refs):
-    kept_ref, sent_ref, product = refs[-3:]
-    half = kept_ref.shape[0]
+def output_kernel(count, narrow_count, tile, me_ref, *refs):
+    x_refs, w_ref = refs[:count], refs[count]
+    kept_ref, sent_ref, x, product = refs[-4:]
+    block = x_refs[0].shape[0]
+    ratio = count // narrow_count
+    for d, ref in enumerate(x_refs):
+        x[d * block : (d + 1) * block, :] = ref[...]
 
     @pl.loop(0, w_ref.shape[1] // tile)
     def _(t):
         at = pl.ds(pl.multiple_of(t * tile, tile), tile)
-        product[:, at] = jnp.dot(x_ref[...], w_ref[:, at], preferred_element_type=jnp.float32)
-
-    kept_ref[...] = product[:half, :]
-    code(product[half:, :], sent_ref)
-
-
-def output_part(x, w, after):
-    rows, columns = x.shape[0], w.shape[1]
-    return call(
-        functools.partial(output_kernel, 256 if columns % 256 == 0 else LANES),
+        product[:, at] = jnp.dot(x[...], w_ref[:, at], preferred_element_type=jnp.float32)
+
+    parts = []
+    for distance in halving_order(narrow_count):
+        for k in range(ratio):
+            wide = (me_ref[1] ^ distance) * ratio + k
+            parts.append(product[pl.ds(pl.multiple_of((wide ^ me_ref[0]) * block, block), block), :])
+    half = count // 2
+    for k, part in enumerate(parts[:half]):
+        kept_ref[k * block : (k + 1) * block, :] = part
+    code(jnp.concatenate(parts[half:], axis=0), sent_ref)
+
+
+def output_part(me, blocks, w, narrow_count, after):
+    count = len(blocks)
+    block, depth = blocks[0].shape
+    rows, columns = count * block, w.shape[1]
+    return call(
+        functools.partial(output_kernel, count, narrow_count, 256 if columns % 256 == 0 else LANES),
         (
             jax.ShapeDtypeStruct((rows // 2, columns), jnp.float32),
             jax.ShapeDtypeStruct((rows // 2, columns + LANES), jnp.int16),
         ),
-        (x, in_vmem(w), *after),
-        [FULL, FULL] + [ANY] * len(after),
+        (me, *blocks, in_vmem(w), *after),
+        [SCALAR] + [FULL] * (count + 1) + [ANY] * len(after),
         "output_part",
-        scratch=[pltpu.VMEM((rows, columns), jnp.float32)],
+        scratch=[pltpu.VMEM((rows, depth), jnp.bfloat16), pltpu.VMEM((rows, columns), jnp.float32)],
         limit=6,
         flops=2 * rows * w.size,
-        moved=2 * x.size,
+        moved=2 * rows * depth,
     )
 
 
@@ -397,38 +398,26 @@
     )
 
 
-def finish_kernel(kinds, *refs):
+def finish_kernel(*refs):
     out_ref = refs[-1]
-    at = k = 0
-    for kind in kinds:
-        width = refs[k].shape[1]
-        done = refs[k][...]
-        if kind == 2:
-            done = (done + decode(refs[k + 1], width)).astype(jnp.bfloat16)
-        out_ref[:, at : at + width] = done
+    at = 0
+    for kept_ref, came_ref in zip(refs[:-1:2], refs[1:-1:2]):
+        width = kept_ref.shape[1]
+        out_ref[:, at : at + width] = (kept_ref[...] + decode(came_ref, width)).astype(jnp.bfloat16)
         at += width
-        k += kind
-
-
-def finish(cuts, after=()):
+
+
+def finish(cuts):
     parts = [x for cut in cuts for x in cut]
     rows, columns = parts[0].shape[0], sum(cut[0].shape[1] for cut in cuts)
     return call(
-        functools.partial(finish_kernel, [len(cut) for cut in cuts]),
+        finish_kernel,
         jax.ShapeDtypeStruct((rows, columns), jnp.bfloat16),
-        (*parts, *after),
-        [FULL] * len(parts) + [ANY] * len(after),
+        parts,
+        [FULL] * len(parts),
         "finish",
         moved=8 * columns * rows,
     )
-
-
-def cut_widths(columns):
-    tile = 256 if columns % 256 == 0 else LANES
-    tiles = columns // tile
-    outer = tiles // 4
-    inner = (tiles - 2 * outer + 1) // 2
-    return [tile * n for n in (outer, inner, tiles - 2 * outer - inner, outer)]
 
 
 def local(activations, norm_gain, query_weight, kv_weight, out_weight, kv_cache, lengths):
@@ -443,7 +432,7 @@
     values = activations.astype(jnp.float32)
     stats = jnp.stack([jnp.sum(values, axis=1), jnp.sum(values * values, axis=1)])
     first_part, kv_part = fetch(
-        [(query_weight, 0, queries // tile // 3 * tile), (kv_weight, None, None)], [stats, me], "fetch_query_weight"
+        [(query_weight, 0, queries // tile // 4 * tile), (kv_weight, None, None)], [stats, me], "fetch_query_weight"
     )
     kept, sent = project(
         me,
@@ -458,13 +447,13 @@
         narrow_count,
         tile,
     )
-    widths = cut_widths(columns)
-    cuts = [(out_weight, sum(widths[:k]), w) for k, w in enumerate(widths)]
+    cut = columns // 3
+    cuts = [(out_weight, k * cut, cut) for k in range(3)]
     d = 1
     while 2 * d < wide_count:
         kept, sent = fold(kept, swap(sent, "wide", d), [])
         d *= 2
-    out_parts = [None] * 4
+    out_parts = [None] * 3
     out_parts[0], cache = fetch([cuts[0], (kv_cache, None, None)], [sent], "fetch_out_weight_0")
     split = call(
         functools.partial(split_kernel, queries, 1),
@@ -472,55 +461,41 @@
         (me, kept, swap(sent, "wide", d), in_vmem(out_parts[0])),
         [SCALAR] + [FULL] * 3,
         "split",
+        scratch=[pltpu.VMEM((narrow_count * PAD, queries + 2 * head_dim), jnp.float32)],
         moved=16 * kept.size,
     )
     [out_parts[1]] = fetch([cuts[1]], [split[0]], "fetch_out_weight_1")
-    context = attend(lengths, exchange(split, "narrow"), cache, head_dim, queries, [out_parts[1]])
-    [out_parts[2]] = fetch([cuts[2]], [context[0]], "fetch_out_weight_2")
+    *context, out_parts[2] = attend(
+        lengths, exchange(split, "narrow"), cache, cuts[2], head_dim, queries, [out_parts[1]]
+    )
     returned = call(
-        functools.partial(join_kernel, 1),
+        functools.partial(join_kernel, 0),
         jax.ShapeDtypeStruct((narrow_count * own_rows, queries), jnp.bfloat16),
-        (me, *exchange(context, "narrow"), in_vmem(out_parts[2])),
-        [SCALAR] + [FULL] * (narrow_count + 1),
+        (me, *exchange(context, "narrow")),
+        [SCALAR] + [FULL] * narrow_count,
         "join",
         scratch=[pltpu.VMEM((narrow_count * PAD, queries), jnp.float32)],
         moved=4 * narrow_count * own_rows * queries,
     )
-    [out_parts[3]] = fetch([cuts[3]], [returned], "fetch_out_weight_3")
-    arranged = call(
-        functools.partial(arrange_kernel, narrow_count, 1),
-        jax.ShapeDtypeStruct((rows, queries), jnp.bfloat16),
-        (me, *gather(returned, "wide"), in_vmem(out_parts[3])),
-        [SCALAR] + [FULL] * (wide_count + 1),
-        "arrange",
-        moved=4 * rows * queries,
-    )
-    kepts, sents, halved, summed = [], [], [], []
-
-    def exchange_cut(k, after):
-        kept, sent, d = kepts[k], sents[k], 1
+    gathered = gather(returned, "wide")
+    cut_sums, halved, last = [], [], []
+
+    def exchange_cut(kept, sent, after):
+        d = 1
         while 2 * d < narrow_count:
             kept, sent = halve(kept, swap(sent, "narrow", d), after)
             after = []
             d *= 2
         halved.append(kept)
-        summed.append((kept, swap(sent, "narrow", d)))
-
-    def finish_cut(k, after):
-        summed[k] = (finish([summed[k]], after),)
-        return [summed[k][0]]
-
-    for k, part in enumerate(out_parts):
-        kept, sent = output_part(arranged, part, halved[-1:])
-        kepts.append(kept)
-        sents.append(sent)
-        after = [kept]
-        if k > 2:
-            after = after + finish_cut(k - 3, [kept])
-        if k:
-            exchange_cut(k - 1, after)
-    exchange_cut(len(out_parts) - 1, finish_cut(len(out_parts) - 3, []))
-    return finish(summed)
+        cut_sums.append((kept, swap(sent, "narrow", d)))
+
+    for part in out_parts:
+        kept, sent = output_part(me, gathered, part, narrow_count, halved[-1:])
+        if last:
+            exchange_cut(*last, [kept])
+        last = (kept, sent)
+    exchange_cut(*last, [])
+    return finish(cut_sums)
 
 
 def solution(mesh):

time: 84 us -> 80.9 us (0.963)
  waiting for transfers between devices: 14.6 us -> 19.5 us
  starting transfers between devices: 26.1 us -> 21.4 us
  Pallas kernels: 41.5 us -> 38.1 us
    ppermute x22 -> x20, waiting for transfers between devices: 14.6 us -> 19.5 us  [swap(): return lax.ppermute(x, axis, [(i, i ^ distance) for i in range(count)])]
    ppermute x22 -> x20, starting transfers between devices: 26.1 us -> 21.4 us  [swap(): return lax.ppermute(x, axis, [(i, i ^ distance) for i in range(count)])]
    pallas_call x22 -> x15, Pallas kernels: 41.5 us -> 38.1 us  [call(): pl.pallas_call(kernel, out_shape=outs, in_specs=specs, out_specs=jax.tree...]
  transfers between devices with their start and end apart: 22 -> 20, of which waited for: 7 -> 11; matrix products, arithmetic and copies ran while one was open for 0% -> 0% of each run, Pallas kernels for 29% -> 24%
where the time goes in v4:
time: 80.9 us; the launch traced here: 80.7 us
  Pallas kernels  38.1 us (47%)
  starting transfers between devices  21.4 us (26%)
  waiting for transfers between devices  19.5 us (24%)
  other arithmetic  1.4 us (2%)
    pallas_call x15, Pallas kernels, call(): pl.pallas_call(kernel, out_shape=outs, in_specs=specs, out_specs=jax.tree...  38.1 us
    ppermute x20, starting transfers between devices, swap(): return lax.ppermute(x, axis, [(i, i ^ distance) for i in range(count)])  21.4 us
    ppermute x20, waiting for transfers between devices, swap(): return lax.ppermute(x, axis, [(i, i ^ distance) for i in range(count)])  19.5 us
  transfers between devices with their start and end apart: 20, of which 11 were waited for; matrix products, arithmetic and copies ran while one was open for 0% of the time, Pallas kernels for 24%

profile of v4, /device:TPU:0, one launch (start us, length us, event | category | flops | bytes accessed | tf_op | source)
XLA Modules:
  0.0 80.7 jit_solution(742366945261771789)
XLA Ops:
  0.0 1.3 %convert_reduce_fusion = (f32[64]{0:T(128)S(1)}, f32[64]{0:T(128)S(1)}) fusion(bf16[64,4608]{1,0:T(8,128)(2,1)} %refs_4_.1), kind=kLoop, calls=%fused_computation.1 | loop fusion | flops 1179520 | bytes 590336 | tf_op jit(solution)/shard_map/reduce_sum | solution.py:433
  1.3 2.5 %collective-permute-start.2 = (f32[2,64]{1,0:T(2,128)S(1)}, f32[2,64]{1,0:T(2,128)S(1)}, u32[]{:S(2)}, u32[]{:S(2)}) collective-permute-start(f32[2,64]{1,0:T(2,128)S(1)} %pad_maximum_fusion.refs_2_.refs_0_), channel_id=1, source_target_pairs={{0,12},{4,8},{8,4},{12,0},{1,13},{5,9},{9,5},{13,1},{2,14},{6,10},... | collective-permute-start | bytes 1544 | tf_op jit(solution)/shard_map/ppermute | solution.py:49
  3.8 0.6 collective-permute-start.1
  4.6 3.5 %fetch_query_weight.1 = (bf16[4608,768]{1,0:T(8,128)(2,1)S(1)}, bf16[1152,512]{1,0:T(8,128)(2,1)S(1)}) custom-call(bf16[4608,3072]{1,0:T(8,128)(2,1)} %refs_6_.1, bf16[1152,512]{1,0:T(8,128)(2,1)} %refs_1_.2, f32[2,64]{1,0:T(2,128)S(1)} %pad_maximum_fusion.refs_2_.refs_0_, s32[2]{0:T(128)S(1)} %pad_add_fusion.refs_3_.me_ref), custom_call_target="tpu_custom_call" | custom-call | bytes 8257536 | tf_op jit(solution)/shard_map/fetch_query_weight/pallas_call | solution.py:23
  8.1 9.5 %project.1 = (f32[32,3584]{1,0:T(8,128)S(1)}, f32[32,3584]{1,0:T(8,128)S(1)}) custom-call(s32[2]{0:T(128)S(1)} %pad_add_fusion.refs_3_.me_ref, f32[2,64]{1,0:T(2,128)S(1)} %pad_maximum_fusion.refs_2_.refs_0_, f32[2,64]{1,0:T(2,128)S(1)} %collective-permute-done.refs_1_, f32[2,64]{1,0:T(2,128)S(1)} %collective-permute-done.1.refs_2_, ...), custom_call_target="tpu_custom_call" | custom-call | flops 1811939328 | bytes 21233664 | tf_op jit(solution)/shard_map/project/pallas_call | solution.py:23
  18.1 1.4 %collective-permute-done.3.came_ref = f32[32,3584]{1,0:T(8,128)S(1)} collective-permute-done((f32[32,3584]{1,0:T(8,128)S(1)}, f32[32,3584]{1,0:T(8,128)S(1)}, u32[]{:S(2)}, u32[]{:S(2)}) %collective-permute-start.3) | collective-permute-done | bytes 458784 | tf_op jit(solution)/shard_map/ppermute | solution.py:49
  19.6 1.7 %collective-permute-start.4 = (f32[16,3584]{1,0:T(8,128)S(1)}, f32[16,3584]{1,0:T(8,128)S(1)}, u32[]{:S(2)}, u32[]{:S(2)}) collective-permute-start(f32[16,3584]{1,0:T(8,128)S(1)} %get-tuple-element.39.refs_2_), channel_id=1, source_target_pairs={{0,8},{4,12},{8,0},{12,4},{1,9},{5,13},{9,1},{13,5},{2,10},{6,14},... | collective-permute-start | bytes 688136 | tf_op jit(solution)/shard_map/ppermute | solution.py:49
  21.3 5.0 %fetch_out_weight_0.1 = (bf16[3072,1536]{1,0:T(8,128)(2,1)S(1)}, bf16[4,1024,512]{2,1,0:T(8,128)(2,1)S(1)}) custom-call(bf16[3072,4608]{1,0:T(8,128)(2,1)} %refs_5_.3, bf16[4,1024,512]{2,1,0:T(8,128)(2,1)} %refs_1_.3, f32[16,3584]{1,0:T(8,128)S(1)} %get-tuple-element.39.refs_2_), custom_call_target="tpu_custom_call" | custom-call | bytes 13631488 | tf_op jit(solution)/shard_map/fetch_out_weight_0/pallas_call | solution.py:23
  26.3 1.3 %collective-permute-done.4.came_ref = f32[16,3584]{1,0:T(8,128)S(1)} collective-permute-done((f32[16,3584]{1,0:T(8,128)S(1)}, f32[16,3584]{1,0:T(8,128)S(1)}, u32[]{:S(2)}, u32[]{:S(2)}) %collective-permute-start.4) | collective-permute-done | bytes 229408 | tf_op jit(solution)/shard_map/ppermute | solution.py:49
  27.6 0.6 split.1
  28.2 1.6 %collective-permute-start.5 = (bf16[4,4096]{1,0:T(4,128)(2,1)S(1)}, bf16[4,4096]{1,0:T(4,128)(2,1)S(1)}, u32[]{:S(2)}, u32[]{:S(2)}) collective-permute-start(bf16[4,4096]{1,0:T(4,128)(2,1)S(1)} %get-tuple-element.42), channel_id=1, source_target_pairs={{0,1},{1,0},{2,3},{3,2},{4,5},{5,4},{6,7},{7,6},{8,9},{9,8},{10,11... | collective-permute-start | bytes 98312 | tf_op jit(solution)/shard_map/ppermute | solution.py:49
  29.8 2.6 %collective-permute-start.6 = (bf16[4,4096]{1,0:T(4,128)(2,1)S(1)}, bf16[4,4096]{1,0:T(4,128)(2,1)S(1)}, u32[]{:S(2)}, u32[]{:S(2)}) collective-permute-start(bf16[4,4096]{1,0:T(4,128)(2,1)S(1)} %get-tuple-element.43), channel_id=1, source_target_pairs={{0,2},{1,3},{2,0},{3,1},{4,6},{5,7},{6,4},{7,5},{8,10},{9,11},{10,... | collective-permute-start | bytes 98312 | tf_op jit(solution)/shard_map/ppermute | solution.py:49
  32.6 3.8 %fetch_out_weight_1.1.refs_6_.refs_4_ = bf16[3072,1536]{1,0:T(8,128)(2,1)S(1)} custom-call(bf16[3072,4608]{1,0:T(8,128)(2,1)} %refs_5_.3, bf16[4,4096]{1,0:T(4,128)(2,1)S(1)} %get-tuple-element.41.refs_1_.refs_0_), custom_call_target="tpu_custom_call" | custom-call | bytes 9437184 | tf_op jit(solution)/shard_map/fetch_out_weight_1/pallas_call | solution.py:23
  36.5 1.6 %collective-permute-done.7.refs_3_ = bf16[4,4096]{1,0:T(4,128)(2,1)S(1)} collective-permute-done((bf16[4,4096]{1,0:T(4,128)(2,1)S(1)}, bf16[4,4096]{1,0:T(4,128)(2,1)S(1)}, u32[]{:S(2)}, u32[]{:S(2)}) %collective-permute-start.7) | collective-permute-done | bytes 32800 | tf_op jit(solution)/shard_map/ppermute | solution.py:49
  38.1 4.6 %attend.1 = (bf16[4,3072]{1,0:T(4,128)(2,1)S(1)}, bf16[4,3072]{1,0:T(4,128)(2,1)S(1)}, bf16[4,3072]{1,0:T(4,128)(2,1)S(1)}, bf16[4,3072]{1,0:T(4,128)(2,1)S(1)}, bf16[3072,1536]{1,0:T(8,128)(2,1)S(1)}) custom-call(s32[4]{0:T(128)S(1)} %copy-done.2, bf16[4,4096]{1,0:T(4,128)(2,1)S(1)} %get-tuple-element.41.refs_1_.refs_0_, ...), custom_call_target="tpu_custom_call" | custom-call | flops 201326592 | tf_op jit(solution)/shard_map/attend/pallas_call | solution.py:23
  42.8 2.5 %collective-permute-start.9 = (bf16[4,3072]{1,0:T(4,128)(2,1)S(1)}, bf16[4,3072]{1,0:T(4,128)(2,1)S(1)}, u32[]{:S(2)}, u32[]{:S(2)}) collective-permute-start(bf16[4,3072]{1,0:T(4,128)(2,1)S(1)} %get-tuple-element.48), channel_id=1, source_target_pairs={{0,2},{1,3},{2,0},{3,1},{4,6},{5,7},{6,4},{7,5},{8,10},{9,11},{10,... | collective-permute-start | bytes 73736 | tf_op jit(solution)/shard_map/ppermute | solution.py:49
  45.3 1.8 %collective-permute-start.10 = (bf16[4,3072]{1,0:T(4,128)(2,1)S(1)}, bf16[4,3072]{1,0:T(4,128)(2,1)S(1)}, u32[]{:S(2)}, u32[]{:S(2)}) collective-permute-start(bf16[4,3072]{1,0:T(4,128)(2,1)S(1)} %get-tuple-element.49), channel_id=1, source_target_pairs={{0,3},{1,2},{2,1},{3,0},{4,7},{5,6},{6,5},{7,4},{8,11},{9,10},{10,... | collective-permute-start | bytes 73736 | tf_op jit(solution)/shard_map/ppermute | solution.py:49
  47.6 3.4 %collective-permute-done.10.refs_3_ = bf16[4,3072]{1,0:T(4,128)(2,1)S(1)} collective-permute-done((bf16[4,3072]{1,0:T(4,128)(2,1)S(1)}, bf16[4,3072]{1,0:T(4,128)(2,1)S(1)}, u32[]{:S(2)}, u32[]{:S(2)}) %collective-permute-start.10) | collective-permute-done | bytes 24608 | tf_op jit(solution)/shard_map/ppermute | solution.py:49
  51.6 1.5 %collective-permute-start.12 = (bf16[16,3072]{1,0:T(8,128)(2,1)S(1)}, bf16[16,3072]{1,0:T(8,128)(2,1)S(1)}, u32[]{:S(2)}, u32[]{:S(2)}) collective-permute-start(bf16[16,3072]{1,0:T(8,128)(2,1)S(1)} %join.1.refs_0_), channel_id=1, source_target_pairs={{0,8},{4,12},{8,0},{12,4},{1,9},{5,13},{9,1},{13,5},{2,10},{6,14},... | collective-permute-start | bytes 294920 | tf_op jit(solution)/shard_map/ppermute | solution.py:49
  53.1 3.2 %collective-permute-done.12.refs_2_ = bf16[16,3072]{1,0:T(8,128)(2,1)S(1)} collective-permute-done((bf16[16,3072]{1,0:T(8,128)(2,1)S(1)}, bf16[16,3072]{1,0:T(8,128)(2,1)S(1)}, u32[]{:S(2)}, u32[]{:S(2)}) %collective-permute-start.12) | collective-permute-done | bytes 98336 | tf_op jit(solution)/shard_map/ppermute | solution.py:49
  56.3 1.3 %collective-permute-done.13.refs_3_ = bf16[16,3072]{1,0:T(8,128)(2,1)S(1)} collective-permute-done((bf16[16,3072]{1,0:T(8,128)(2,1)S(1)}, bf16[16,3072]{1,0:T(8,128)(2,1)S(1)}, u32[]{:S(2)}, u32[]{:S(2)}) %collective-permute-start.13) | collective-permute-done | bytes 98336 | tf_op jit(solution)/shard_map/ppermute | solution.py:49
  57.6 3.1 %output_part.3 = (f32[32,1536]{1,0:T(8,128)S(1)}, s16[32,1664]{1,0:T(8,128)(2,1)S(1)}) custom-call(s32[2]{0:T(128)S(1)} %pad_add_fusion.refs_3_.me_ref, bf16[16,3072]{1,0:T(8,128)(2,1)S(1)} %join.1.refs_0_, bf16[16,3072]{1,0:T(8,128)(2,1)S(1)} %collective-permute-done.11.refs_1_, bf16[16,3072]{1,0:T(8,128)(2,1)S(1)} %collective-permute-done.12.refs_2_, ...), custom_call_target="tpu_custom_call" | custom-call | flops 603979776 | bytes 393216 | tf_op jit(solution)/shard_map/output_part/pallas_call | solution.py:23
  60.7 3.1 %output_part.4 = (f32[32,1536]{1,0:T(8,128)S(1)}, s16[32,1664]{1,0:T(8,128)(2,1)S(1)}) custom-call(s32[2]{0:T(128)S(1)} %pad_add_fusion.refs_3_.me_ref, bf16[16,3072]{1,0:T(8,128)(2,1)S(1)} %join.1.refs_0_, bf16[16,3072]{1,0:T(8,128)(2,1)S(1)} %collective-permute-done.11.refs_1_, bf16[16,3072]{1,0:T(8,128)(2,1)S(1)} %collective-permute-done.12.refs_2_, ...), custom_call_target="tpu_custom_call" | custom-call | flops 603979776 | bytes 393216 | tf_op jit(solution)/shard_map/output_part/pallas_call | solution.py:23
  63.8 2.1 %collective-permute-start.16 = (s16[32,1664]{1,0:T(8,128)(2,1)S(1)}, s16[32,1664]{1,0:T(8,128)(2,1)S(1)}, u32[]{:S(2)}, u32[]{:S(2)}) collective-permute-start(s16[32,1664]{1,0:T(8,128)(2,1)S(1)} %get-tuple-element.55), channel_id=1, source_target_pairs={{0,1},{1,0},{2,3},{3,2},{4,5},{5,4},{6,7},{7,6},{8,9},{9,8},{10,11... | collective-permute-start | bytes 319496 | tf_op jit(solution)/shard_map/ppermute | solution.py:49
  66.1 3.1 %output_part.5 = (f32[32,1536]{1,0:T(8,128)S(1)}, s16[32,1664]{1,0:T(8,128)(2,1)S(1)}) custom-call(s32[2]{0:T(128)S(1)} %pad_add_fusion.refs_3_.me_ref, bf16[16,3072]{1,0:T(8,128)(2,1)S(1)} %join.1.refs_0_, bf16[16,3072]{1,0:T(8,128)(2,1)S(1)} %collective-permute-done.11.refs_1_, bf16[16,3072]{1,0:T(8,128)(2,1)S(1)} %collective-permute-done.12.refs_2_, ...), custom_call_target="tpu_custom_call" | custom-call | flops 603979776 | bytes 393216 | tf_op jit(solution)/shard_map/output_part/pallas_call | solution.py:23
  69.3 2.3 %collective-permute-start.15 = (s16[16,1664]{1,0:T(8,128)(2,1)S(1)}, s16[16,1664]{1,0:T(8,128)(2,1)S(1)}, u32[]{:S(2)}, u32[]{:S(2)}) collective-permute-start(s16[16,1664]{1,0:T(8,128)(2,1)S(1)} %get-tuple-element.54), channel_id=1, source_target_pairs={{0,2},{1,3},{2,0},{3,1},{4,6},{5,7},{6,4},{7,5},{8,10},{9,11},{10,... | collective-permute-start | bytes 159752 | tf_op jit(solution)/shard_map/ppermute | solution.py:49
  71.8 0.7 collective-permute-start.17
  72.5 2.0 %collective-permute-done.18.came_ref = s16[32,1664]{1,0:T(8,128)(2,1)S(1)} collective-permute-done((s16[32,1664]{1,0:T(8,128)(2,1)S(1)}, s16[32,1664]{1,0:T(8,128)(2,1)S(1)}, u32[]{:S(2)}, u32[]{:S(2)}) %collective-permute-start.18) | collective-permute-done | bytes 106528 | tf_op jit(solution)/shard_map/ppermute | solution.py:49
  75.1 2.2 %collective-permute-done.15.refs_1_ = s16[16,1664]{1,0:T(8,128)(2,1)S(1)} collective-permute-done((s16[16,1664]{1,0:T(8,128)(2,1)S(1)}, s16[16,1664]{1,0:T(8,128)(2,1)S(1)}, u32[]{:S(2)}, u32[]{:S(2)}) %collective-permute-start.15) | collective-permute-done | bytes 53280 | tf_op jit(solution)/shard_map/ppermute | solution.py:49
  77.3 1.1 %collective-permute-done.17.refs_3_ = s16[16,1664]{1,0:T(8,128)(2,1)S(1)} collective-permute-done((s16[16,1664]{1,0:T(8,128)(2,1)S(1)}, s16[16,1664]{1,0:T(8,128)(2,1)S(1)}, u32[]{:S(2)}, u32[]{:S(2)}) %collective-permute-start.17) | collective-permute-done | bytes 53280 | tf_op jit(solution)/shard_map/ppermute | solution.py:49
  78.4 1.5 %collective-permute-done.19.refs_5_ = s16[16,1664]{1,0:T(8,128)(2,1)S(1)} collective-permute-done((s16[16,1664]{1,0:T(8,128)(2,1)S(1)}, s16[16,1664]{1,0:T(8,128)(2,1)S(1)}, u32[]{:S(2)}, u32[]{:S(2)}) %collective-permute-start.19) | collective-permute-done | bytes 53280 | tf_op jit(solution)/shard_map/ppermute | solution.py:49
  79.9 0.8 finish.1
  (32 shorter events, 3.3 us)
Async XLA Ops:
  1.3 6.7 %collective-permute-start.2 = (f32[2,64]{1,0:T(2,128)S(1)}, f32[2,64]{1,0:T(2,128)S(1)}, u32[]{:S(2)}, u32[]{:S(2)}) collective-permute-start(f32[2,64]{1,0:T(2,128)S(1)} %pad_maximum_fusion.refs_2_.refs_0_), channel_id=1, source_target_pairs={{0,12},{4,8},{8,4},{12,0},{1,13},{5,9},{9,5},{13,1},{2,14},{6,10},... | collective-permute-start | bytes 1544 | tf_op jit(solution)/shard_map/ppermute | solution.py:49
  3.8 4.3 %collective-permute-start.1 = (f32[2,64]{1,0:T(2,128)S(1)}, f32[2,64]{1,0:T(2,128)S(1)}, u32[]{:S(2)}, u32[]{:S(2)}) collective-permute-start(f32[2,64]{1,0:T(2,128)S(1)} %pad_maximum_fusion.refs_2_.refs_0_), channel_id=1, source_target_pairs={{0,8},{4,12},{8,0},{12,4},{1,9},{5,13},{9,1},{13,5},{2,10},{6,14},... | collective-permute-start | bytes 1544 | tf_op jit(solution)/shard_map/ppermute | solution.py:49
  4.4 3.6 %collective-permute-start = (f32[2,64]{1,0:T(2,128)S(1)}, f32[2,64]{1,0:T(2,128)S(1)}, u32[]{:S(2)}, u32[]{:S(2)}) collective-permute-start(f32[2,64]{1,0:T(2,128)S(1)} %pad_maximum_fusion.refs_2_.refs_0_), channel_id=1, source_target_pairs={{0,4},{4,0},{8,12},{12,8},{1,5},{5,1},{9,13},{13,9},{2,6},{6,2},{1... | collective-permute-start | bytes 1544 | tf_op jit(solution)/shard_map/ppermute | solution.py:49
  4.6 3.5 %copy-start = (bf16[64,4608]{1,0:T(8,128)(2,1)S(1)}, bf16[64,4608]{1,0:T(8,128)(2,1)}, u32[]{:S(2)}) copy-start(bf16[64,4608]{1,0:T(8,128)(2,1)} %refs_4_.1) | copy-start | bytes 1769476
  4.6 3.5 %copy-start.1 = (f32[4608]{0:T(1024)S(1)}, f32[4608]{0:T(1024)}, u32[]{:S(2)}) copy-start(f32[4608]{0:T(1024)} %refs_5_.2) | copy-start | bytes 55300
  17.6 2.0 %collective-permute-start.3 = (f32[32,3584]{1,0:T(8,128)S(1)}, f32[32,3584]{1,0:T(8,128)S(1)}, u32[]{:S(2)}, u32[]{:S(2)}) collective-permute-start(f32[32,3584]{1,0:T(8,128)S(1)} %get-tuple-element.37), channel_id=1, source_target_pairs={{0,4},{4,0},{8,12},{12,8},{1,5},{5,1},{9,13},{13,9},{2,6},{6,2},{1... | collective-permute-start | bytes 1376264 | tf_op jit(solution)/shard_map/ppermute | solution.py:49
  19.6 7.9 %collective-permute-start.4 = (f32[16,3584]{1,0:T(8,128)S(1)}, f32[16,3584]{1,0:T(8,128)S(1)}, u32[]{:S(2)}, u32[]{:S(2)}) collective-permute-start(f32[16,3584]{1,0:T(8,128)S(1)} %get-tuple-element.39.refs_2_), channel_id=1, source_target_pairs={{0,8},{4,12},{8,0},{12,4},{1,9},{5,13},{9,1},{13,5},{2,10},{6,14},... | collective-permute-start | bytes 688136 | tf_op jit(solution)/shard_map/ppermute | solution.py:49
  28.2 8.3 %collective-permute-start.5 = (bf16[4,4096]{1,0:T(4,128)(2,1)S(1)}, bf16[4,4096]{1,0:T(4,128)(2,1)S(1)}, u32[]{:S(2)}, u32[]{:S(2)}) collective-permute-start(bf16[4,4096]{1,0:T(4,128)(2,1)S(1)} %get-tuple-element.42), channel_id=1, source_target_pairs={{0,1},{1,0},{2,3},{3,2},{4,5},{5,4},{6,7},{7,6},{8,9},{9,8},{10,11... | collective-permute-start | bytes 98312 | tf_op jit(solution)/shard_map/ppermute | solution.py:49
  29.8 6.7 %collective-permute-start.6 = (bf16[4,4096]{1,0:T(4,128)(2,1)S(1)}, bf16[4,4096]{1,0:T(4,128)(2,1)S(1)}, u32[]{:S(2)}, u32[]{:S(2)}) collective-permute-start(bf16[4,4096]{1,0:T(4,128)(2,1)S(1)} %get-tuple-element.43), channel_id=1, source_target_pairs={{0,2},{1,3},{2,0},{3,1},{4,6},{5,7},{6,4},{7,5},{8,10},{9,11},{10,... | collective-permute-start | bytes 98312 | tf_op jit(solution)/shard_map/ppermute | solution.py:49
  32.4 5.7 %collective-permute-start.7 = (bf16[4,4096]{1,0:T(4,128)(2,1)S(1)}, bf16[4,4096]{1,0:T(4,128)(2,1)S(1)}, u32[]{:S(2)}, u32[]{:S(2)}) collective-permute-start(bf16[4,4096]{1,0:T(4,128)(2,1)S(1)} %get-tuple-element.44), channel_id=1, source_target_pairs={{0,3},{1,2},{2,1},{3,0},{4,7},{5,6},{6,5},{7,4},{8,11},{9,10},{10,... | collective-permute-start | bytes 98312 | tf_op jit(solution)/shard_map/ppermute | solution.py:49
  32.6 5.5 %copy-start.2 = (s32[4]{0:T(128)S(1)}, s32[4]{0:T(128)}, u32[]{:S(2)}) copy-start(s32[4]{0:T(128)} %lengths_ref.1) | copy-start | bytes 52
  42.7 4.5 %collective-permute-start.8 = (bf16[4,3072]{1,0:T(4,128)(2,1)S(1)}, bf16[4,3072]{1,0:T(4,128)(2,1)S(1)}, u32[]{:S(2)}, u32[]{:S(2)}) collective-permute-start(bf16[4,3072]{1,0:T(4,128)(2,1)S(1)} %get-tuple-element.47), channel_id=1, source_target_pairs={{0,1},{1,0},{2,3},{3,2},{4,5},{5,4},{6,7},{7,6},{8,9},{9,8},{10,11... | collective-permute-start | bytes 73736 | tf_op jit(solution)/shard_map/ppermute | solution.py:49
  42.8 4.8 %collective-permute-start.9 = (bf16[4,3072]{1,0:T(4,128)(2,1)S(1)}, bf16[4,3072]{1,0:T(4,128)(2,1)S(1)}, u32[]{:S(2)}, u32[]{:S(2)}) collective-permute-start(bf16[4,3072]{1,0:T(4,128)(2,1)S(1)} %get-tuple-element.48), channel_id=1, source_target_pairs={{0,2},{1,3},{2,0},{3,1},{4,6},{5,7},{6,4},{7,5},{8,10},{9,11},{10,... | collective-permute-start | bytes 73736 | tf_op jit(solution)/shard_map/ppermute | solution.py:49
  45.3 5.6 %collective-permute-start.10 = (bf16[4,3072]{1,0:T(4,128)(2,1)S(1)}, bf16[4,3072]{1,0:T(4,128)(2,1)S(1)}, u32[]{:S(2)}, u32[]{:S(2)}) collective-permute-start(bf16[4,3072]{1,0:T(4,128)(2,1)S(1)} %get-tuple-element.49), channel_id=1, source_target_pairs={{0,3},{1,2},{2,1},{3,0},{4,7},{5,6},{6,5},{7,4},{8,11},{9,10},{10,... | collective-permute-start | bytes 73736 | tf_op jit(solution)/shard_map/ppermute | solution.py:49
  51.6 4.7 %collective-permute-start.12 = (bf16[16,3072]{1,0:T(8,128)(2,1)S(1)}, bf16[16,3072]{1,0:T(8,128)(2,1)S(1)}, u32[]{:S(2)}, u32[]{:S(2)}) collective-permute-start(bf16[16,3072]{1,0:T(8,128)(2,1)S(1)} %join.1.refs_0_), channel_id=1, source_target_pairs={{0,8},{4,12},{8,0},{12,4},{1,9},{5,13},{9,1},{13,5},{2,10},{6,14},... | collective-permute-start | bytes 294920 | tf_op jit(solution)/shard_map/ppermute | solution.py:49
  53.0 3.2 %collective-permute-start.11 = (bf16[16,3072]{1,0:T(8,128)(2,1)S(1)}, bf16[16,3072]{1,0:T(8,128)(2,1)S(1)}, u32[]{:S(2)}, u32[]{:S(2)}) collective-permute-start(bf16[16,3072]{1,0:T(8,128)(2,1)S(1)} %join.1.refs_0_), channel_id=1, source_target_pairs={{0,4},{4,0},{8,12},{12,8},{1,5},{5,1},{9,13},{13,9},{2,6},{6,2},{1... | collective-permute-start | bytes 294920 | tf_op jit(solution)/shard_map/ppermute | solution.py:49
  56.3 1.3 %collective-permute-start.13 = (bf16[16,3072]{1,0:T(8,128)(2,1)S(1)}, bf16[16,3072]{1,0:T(8,128)(2,1)S(1)}, u32[]{:S(2)}, u32[]{:S(2)}) collective-permute-start(bf16[16,3072]{1,0:T(8,128)(2,1)S(1)} %collective-permute-done.12.refs_2_), channel_id=1, source_target_pairs={{0,4},{4,0},{8,12},{12,8},{1,5},{5,1},{9,13},{13,9},{2,6},{6,2},{1... | collective-permute-start | bytes 294920 | tf_op jit(solution)/shard_map/ppermute | solution.py:49
  60.6 5.2 %collective-permute-start.14 = (s16[32,1664]{1,0:T(8,128)(2,1)S(1)}, s16[32,1664]{1,0:T(8,128)(2,1)S(1)}, u32[]{:S(2)}, u32[]{:S(2)}) collective-permute-start(s16[32,1664]{1,0:T(8,128)(2,1)S(1)} %get-tuple-element.51), channel_id=1, source_target_pairs={{0,1},{1,0},{2,3},{3,2},{4,5},{5,4},{6,7},{7,6},{8,9},{9,8},{10,11... | collective-permute-start | bytes 319496 | tf_op jit(solution)/shard_map/ppermute | solution.py:49
  63.8 7.8 %collective-permute-start.16 = (s16[32,1664]{1,0:T(8,128)(2,1)S(1)}, s16[32,1664]{1,0:T(8,128)(2,1)S(1)}, u32[]{:S(2)}, u32[]{:S(2)}) collective-permute-start(s16[32,1664]{1,0:T(8,128)(2,1)S(1)} %get-tuple-element.55), channel_id=1, source_target_pairs={{0,1},{1,0},{2,3},{3,2},{4,5},{5,4},{6,7},{7,6},{8,9},{9,8},{10,11... | collective-permute-start | bytes 319496 | tf_op jit(solution)/shard_map/ppermute | solution.py:49
  69.1 5.4 %collective-permute-start.18 = (s16[32,1664]{1,0:T(8,128)(2,1)S(1)}, s16[32,1664]{1,0:T(8,128)(2,1)S(1)}, u32[]{:S(2)}, u32[]{:S(2)}) collective-permute-start(s16[32,1664]{1,0:T(8,128)(2,1)S(1)} %get-tuple-element.60), channel_id=1, source_target_pairs={{0,1},{1,0},{2,3},{3,2},{4,5},{5,4},{6,7},{7,6},{8,9},{9,8},{10,11... | collective-permute-start | bytes 319496 | tf_op jit(solution)/shard_map/ppermute | solution.py:49
  69.3 7.9 %collective-permute-start.15 = (s16[16,1664]{1,0:T(8,128)(2,1)S(1)}, s16[16,1664]{1,0:T(8,128)(2,1)S(1)}, u32[]{:S(2)}, u32[]{:S(2)}) collective-permute-start(s16[16,1664]{1,0:T(8,128)(2,1)S(1)} %get-tuple-element.54), channel_id=1, source_target_pairs={{0,2},{1,3},{2,0},{3,1},{4,6},{5,7},{6,4},{7,5},{8,10},{9,11},{10,... | collective-permute-start | bytes 159752 | tf_op jit(solution)/shard_map/ppermute | solution.py:49
  71.8 6.6 %collective-permute-start.17 = (s16[16,1664]{1,0:T(8,128)(2,1)S(1)}, s16[16,1664]{1,0:T(8,128)(2,1)S(1)}, u32[]{:S(2)}, u32[]{:S(2)}) collective-permute-start(s16[16,1664]{1,0:T(8,128)(2,1)S(1)} %get-tuple-element.59), channel_id=1, source_target_pairs={{0,2},{1,3},{2,0},{3,1},{4,6},{5,7},{6,4},{7,5},{8,10},{9,11},{10,... | collective-permute-start | bytes 159752 | tf_op jit(solution)/shard_map/ppermute | solution.py:49
  74.8 5.2 %collective-permute-start.19 = (s16[16,1664]{1,0:T(8,128)(2,1)S(1)}, s16[16,1664]{1,0:T(8,128)(2,1)S(1)}, u32[]{:S(2)}, u32[]{:S(2)}) collective-permute-start(s16[16,1664]{1,0:T(8,128)(2,1)S(1)} %get-tuple-element.62), channel_id=1, source_target_pairs={{0,2},{1,3},{2,0},{3,1},{4,6},{5,7},{6,4},{7,5},{8,10},{9,11},{10,... | collective-permute-start | bytes 159752 | tf_op jit(solution)/shard_map/ppermute | solution.py:49

commit v5 on v4

--- a/solution.py
+++ b/solution.py
@@ -61,7 +61,8 @@
 
 
 def exchange(blocks, axis):
-    return [blocks[0]] + [swap(b, axis, d) for d, b in enumerate(blocks) if d]
+    far_first = {d: swap(blocks[d], axis, d) for d in range(len(blocks) - 1, 0, -1)}
+    return [blocks[0]] + [far_first[d] for d in range(1, len(blocks))]
 
 
 def gather(x, axis):
@@ -159,11 +160,8 @@
         sent_ref[:, at] = got[half:, :]
 
     def products(source, start):
-        @pl.loop(0, source.shape[1] // tile)
-        def _(t):
-            at = pl.ds(pl.multiple_of(t * tile, tile), tile)
-            got = jnp.dot(normed[...], source[:, at], preferred_element_type=jnp.float32)
-            put(got, pl.ds(pl.multiple_of(start + t * tile, tile), tile))
+        got = jnp.dot(normed[...], source[...], preferred_element_type=jnp.float32)
+        put(got, slice(start, start + source.shape[1]))
 
     put(jnp.dot(own[...], kv_ref[...], preferred_element_type=jnp.float32), slice(w_ref.shape[1], kept_ref.shape[1]))
     products(first_ref, 0)
@@ -177,8 +175,7 @@
     rows, width = x.shape
     queries = w.shape[1]
     tiles = (queries - first.shape[1]) // tile
-    groups = [tiles * 4 // 9, (tiles - tiles * 4 // 9 + 1) // 2]
-    groups.append(tiles - sum(groups))
+    groups = [2] * (tiles // 2) + [1] * (tiles % 2)
     half = jax.ShapeDtypeStruct((rows // 2, queries + kv.shape[1]), jnp.float32)
     return call(
         functools.partial(project_kernel, len(stats), width_all, count, narrow_count, tile),
@@ -232,7 +229,7 @@
 
 
 def attend_kernel(head_dim, count, guards, start, lengths_ref, *refs):
-    came_refs, kv_ref, w_ref = refs[:count], refs[count], refs[count + 1]
+    came_refs, kv_ref, w_ref = refs[:count][::-1], refs[count], refs[count + 1]
     refs = refs[count + 2 + guards :]
     out_refs, share, (heads, contexts, sems) = refs[:count], refs[count], refs[count + 1 :]
     fetches = fetches_of([start], [w_ref], [share], sems)
@@ -298,7 +295,7 @@
     return call(
         functools.partial(attend_kernel, head_dim, count, len(guards), start),
         [jax.ShapeDtypeStruct((rows, queries), jnp.bfloat16)] * count + [held((w.shape[0], width), w.dtype)],
-        (lengths, *came, in_vmem(kv), in_hbm(w), *map(in_vmem, guards)),
+        (lengths, *came[::-1], in_vmem(kv), in_hbm(w), *map(in_vmem, guards)),
         [SCALAR] + [FULL] * (count + 1) + [ANY] + [FULL] * len(guards),
         "attend",
         scratch=[scratch, scratch, pltpu.SemaphoreType.DMA((1, PIECES))],
@@ -313,7 +310,7 @@
     rows = refs[0].shape[0]
     for d in range(count):
         at = pl.ds(pl.multiple_of((me_ref[1] ^ d) * PAD, PAD), rows)
-        joined[at, :] = refs[d][...].astype(jnp.float32)
+        joined[at, :] = refs[count - 1 - d][...].astype(jnp.float32)
     came = [joined[j * PAD : j * PAD + rows, :] for j in range(count)]
     out_ref[...] = jnp.concatenate(came, axis=0).astype(jnp.bfloat16)
 
@@ -331,87 +328,83 @@
     return ref[:, :width].astype(jnp.int32).astype(jnp.float32) * (jnp.exp2(power) * (1.0 / STEPS))
 
 
-def output_kernel(count, narrow_count, tile, me_ref, *refs):
-    x_refs, w_ref = refs[:count], refs[count]
-    kept_ref, sent_ref, x, product = refs[-4:]
+def output_kernel(count, weights, narrow_count, me_ref, *refs):
+    x_refs, w_refs, (sums_ref, sent_ref) = refs[:count], refs[count : count + weights], refs[-2:]
     block = x_refs[0].shape[0]
     ratio = count // narrow_count
-    for d, ref in enumerate(x_refs):
-        x[d * block : (d + 1) * block, :] = ref[...]
-
-    @pl.loop(0, w_ref.shape[1] // tile)
-    def _(t):
-        at = pl.ds(pl.multiple_of(t * tile, tile), tile)
-        product[:, at] = jnp.dot(x[...], w_ref[:, at], preferred_element_type=jnp.float32)
-
-    parts = []
-    for distance in halving_order(narrow_count):
-        for k in range(ratio):
-            wide = (me_ref[1] ^ distance) * ratio + k
-            parts.append(product[pl.ds(pl.multiple_of((wide ^ me_ref[0]) * block, block), block), :])
-    half = count // 2
-    for k, part in enumerate(parts[:half]):
-        kept_ref[k * block : (k + 1) * block, :] = part
-    code(jnp.concatenate(parts[half:], axis=0), sent_ref)
-
-
-def output_part(me, blocks, w, narrow_count, after):
+    places = []
+    for d in range(count):
+        wide = me_ref[0] ^ d
+        apart = (wide // ratio) ^ me_ref[1]
+        place = jnp.int32(0)
+        for k, distance in enumerate(halving_order(narrow_count)):
+            place = jnp.where(apart == distance, k, place)
+        places.append(pl.multiple_of((place * ratio + wide % ratio) * block, block))
+    x = jnp.concatenate([ref[...] for ref in x_refs], axis=0)
+    at = 0
+    for w_ref in w_refs:
+        width = w_ref.shape[1]
+        got = jnp.dot(x, w_ref[...], preferred_element_type=jnp.float32)
+        for d, place in enumerate(places):
+            sums_ref[pl.ds(place, block), at : at + width] = got[d * block : (d + 1) * block, :]
+        at += width
+    code(sums_ref[sums_ref.shape[0] // 2 :, :], sent_ref)
+
+
+def output_part(me, blocks, ws, narrow_count, after):
     count = len(blocks)
     block, depth = blocks[0].shape
-    rows, columns = count * block, w.shape[1]
-    return call(
-        functools.partial(output_kernel, count, narrow_count, 256 if columns % 256 == 0 else LANES),
+    rows, columns = count * block, sum(w.shape[1] for w in ws)
+    return call(
+        functools.partial(output_kernel, count, len(ws), narrow_count),
         (
-            jax.ShapeDtypeStruct((rows // 2, columns), jnp.float32),
+            jax.ShapeDtypeStruct((rows, columns), jnp.float32),
             jax.ShapeDtypeStruct((rows // 2, columns + LANES), jnp.int16),
         ),
-        (me, *blocks, in_vmem(w), *after),
-        [SCALAR] + [FULL] * (count + 1) + [ANY] * len(after),
+        (me, *blocks, *map(in_vmem, ws), *after),
+        [SCALAR] + [FULL] * (count + len(ws)) + [ANY] * len(after),
         "output_part",
-        scratch=[pltpu.VMEM((rows, depth), jnp.bfloat16), pltpu.VMEM((rows, columns), jnp.float32)],
-        limit=6,
-        flops=2 * rows * w.size,
+        limit=8,
+        flops=2 * rows * depth * columns,
         moved=2 * rows * depth,
     )
 
 
-def halve_kernel(kept_ref, came_ref, *refs):
+def halve_kernel(sums_ref, came_ref, *refs):
     still_ref, sent_ref = refs[-2:]
     half = still_ref.shape[0]
-    total = kept_ref[...] + decode(came_ref, kept_ref.shape[1])
+    total = sums_ref[: 2 * half, :] + decode(came_ref, sums_ref.shape[1])
     still_ref[...] = total[:half, :]
     code(total[half:, :], sent_ref)
 
 
-def halve(kept, came, after):
-    rows, columns = kept.shape
+def halve(sums, came, after):
+    rows, columns = came.shape[0], sums.shape[1]
     return call(
         halve_kernel,
         (
             jax.ShapeDtypeStruct((rows // 2, columns), jnp.float32),
             jax.ShapeDtypeStruct((rows // 2, columns + LANES), jnp.int16),
         ),
-        (kept, came, *after),
+        (sums, came, *after),
         [FULL, FULL] + [ANY] * len(after),
         "halve",
-        moved=16 * kept.size,
-    )
-
-
-def finish_kernel(*refs):
+        moved=16 * rows * columns,
+    )
+
+
+def finish_kernel(starts, *refs):
     out_ref = refs[-1]
-    at = 0
-    for kept_ref, came_ref in zip(refs[:-1:2], refs[1:-1:2]):
+    for at, kept_ref, came_ref in zip(starts, refs[:-1:2], refs[1:-1:2]):
         width = kept_ref.shape[1]
         out_ref[:, at : at + width] = (kept_ref[...] + decode(came_ref, width)).astype(jnp.bfloat16)
-        at += width
-
-
-def finish(cuts):
+
+
+def finish(starts, cuts):
     parts = [x for cut in cuts for x in cut]
     rows, columns = parts[0].shape[0], sum(cut[0].shape[1] for cut in cuts)
     return call(
-        finish_kernel,
+        functools.partial(finish_kernel, starts),
         jax.ShapeDtypeStruct((rows, columns), jnp.bfloat16),
         parts,
         [FULL] * len(parts),
@@ -447,13 +440,13 @@
         narrow_count,
         tile,
     )
-    cut = columns // 3
-    cuts = [(out_weight, k * cut, cut) for k in range(3)]
+    ends = [columns // LANES * k // 18 * LANES for k in (0, 6, 11, 13, 18)]
+    cuts = [(out_weight, start, end - start) for start, end in zip(ends, ends[1:])]
     d = 1
     while 2 * d < wide_count:
         kept, sent = fold(kept, swap(sent, "wide", d), [])
         d *= 2
-    out_parts = [None] * 3
+    out_parts = [None] * 4
     out_parts[0], cache = fetch([cuts[0], (kv_cache, None, None)], [sent], "fetch_out_weight_0")
     split = call(
         functools.partial(split_kernel, queries, 1),
@@ -468,11 +461,12 @@
     *context, out_parts[2] = attend(
         lengths, exchange(split, "narrow"), cache, cuts[2], head_dim, queries, [out_parts[1]]
     )
+    [out_parts[3]] = fetch([cuts[3]], [context[0]], "fetch_out_weight_3")
     returned = call(
-        functools.partial(join_kernel, 0),
+        functools.partial(join_kernel, 1),
         jax.ShapeDtypeStruct((narrow_count * own_rows, queries), jnp.bfloat16),
-        (me, *exchange(context, "narrow")),
-        [SCALAR] + [FULL] * narrow_count,
+        (me, *exchange(context, "narrow")[::-1], in_vmem(out_parts[3])),
+        [SCALAR] + [FULL] * (narrow_count + 1),
         "join",
         scratch=[pltpu.VMEM((narrow_count * PAD, queries), jnp.float32)],
         moved=4 * narrow_count * own_rows * queries,
@@ -489,13 +483,13 @@
         halved.append(kept)
         cut_sums.append((kept, swap(sent, "narrow", d)))
 
-    for part in out_parts:
-        kept, sent = output_part(me, gathered, part, narrow_count, halved[-1:])
+    for parts in (out_parts[:1], out_parts[2:], out_parts[1:2]):
+        kept, sent = output_part(me, gathered, parts, narrow_count, halved[-1:])
         if last:
             exchange_cut(*last, [kept])
         last = (kept, sent)
     exchange_cut(*last, [])
-    return finish(cut_sums)
+    return finish([ends[0], ends[2], ends[1]], cut_sums)
 
 
 def solution(mesh):

time: 80.9 us -> 76.5 us (0.946)
  waiting for transfers between devices: 19.5 us -> 13.4 us
  starting transfers between devices: 21.4 us -> 23.7 us
    ppermute x20, waiting for transfers between devices: 19.5 us -> 13.4 us  [swap(): return lax.ppermute(x, axis, [(i, i ^ distance) for i in range(count)])]
    ppermute x20, starting transfers between devices: 21.4 us -> 23.7 us  [swap(): return lax.ppermute(x, axis, [(i, i ^ distance) for i in range(count)])]
    pallas_call x15 -> x16, Pallas kernels: 38.1 us -> 37.5 us  [call(): pl.pallas_call(kernel, out_shape=outs, in_specs=specs, out_specs=jax.tree...]
  transfers between devices with their start and end apart: 20 -> 20, of which waited for: 11 -> 10; matrix products, arithmetic and copies ran while one was open for 0% -> 0% of each run, Pallas kernels for 24% -> 27%
where the time goes in v5:
time: 76.5 us; the launch traced here: 76.3 us
  Pallas kernels  37.5 us (49%)
  starting transfers between devices  23.7 us (31%)
  waiting for transfers between devices  13.4 us (18%)
  other arithmetic  1.4 us (2%)
    pallas_call x16, Pallas kernels, call(): pl.pallas_call(kernel, out_shape=outs, in_specs=specs, out_specs=jax.tree...  37.5 us
    ppermute x20, starting transfers between devices, swap(): return lax.ppermute(x, axis, [(i, i ^ distance) for i in range(count)])  23.7 us
    ppermute x20, waiting for transfers between devices, swap(): return lax.ppermute(x, axis, [(i, i ^ distance) for i in range(count)])  13.4 us
  transfers between devices with their start and end apart: 20, of which 10 were waited for; matrix products, arithmetic and copies ran while one was open for 0% of the time, Pallas kernels for 27%

profile of v5, /device:TPU:0, one launch (start us, length us, event | category | flops | bytes accessed | tf_op | source)
XLA Modules:
  0.0 76.3 jit_solution(14971579367235391438)
XLA Ops:
  0.0 1.3 %convert_reduce_fusion = (f32[64]{0:T(128)S(1)}, f32[64]{0:T(128)S(1)}) fusion(bf16[64,4608]{1,0:T(8,128)(2,1)} %refs_4_.1), kind=kLoop, calls=%fused_computation.1 | loop fusion | flops 1179520 | bytes 590336 | tf_op jit(solution)/shard_map/reduce_sum | solution.py:426
  1.9 2.6 %collective-permute-start.1 = (f32[2,64]{1,0:T(2,128)S(1)}, f32[2,64]{1,0:T(2,128)S(1)}, u32[]{:S(2)}, u32[]{:S(2)}) collective-permute-start(f32[2,64]{1,0:T(2,128)S(1)} %pad_maximum_fusion.refs_2_.refs_0_), channel_id=1, source_target_pairs={{0,8},{4,12},{8,0},{12,4},{1,9},{5,13},{9,1},{13,5},{2,10},{6,14},... | collective-permute-start | bytes 1544 | tf_op jit(solution)/shard_map/ppermute | solution.py:49
  4.6 3.5 %fetch_query_weight.1 = (bf16[4608,768]{1,0:T(8,128)(2,1)S(1)}, bf16[1152,512]{1,0:T(8,128)(2,1)S(1)}) custom-call(bf16[4608,3072]{1,0:T(8,128)(2,1)} %refs_6_.1, bf16[1152,512]{1,0:T(8,128)(2,1)} %refs_1_.2, f32[2,64]{1,0:T(2,128)S(1)} %pad_maximum_fusion.refs_2_.refs_0_, s32[2]{0:T(128)S(1)} %pad_add_fusion.refs_3_.me_ref), custom_call_target="tpu_custom_call" | custom-call | bytes 8257536 | tf_op jit(solution)/shard_map/fetch_query_weight/pallas_call | solution.py:23
  8.1 9.1 %project.1 = (f32[32,3584]{1,0:T(8,128)S(1)}, f32[32,3584]{1,0:T(8,128)S(1)}) custom-call(s32[2]{0:T(128)S(1)} %pad_add_fusion.refs_3_.me_ref, f32[2,64]{1,0:T(2,128)S(1)} %pad_maximum_fusion.refs_2_.refs_0_, f32[2,64]{1,0:T(2,128)S(1)} %collective-permute-done.refs_1_, f32[2,64]{1,0:T(2,128)S(1)} %collective-permute-done.1.refs_2_, ...), custom_call_target="tpu_custom_call" | custom-call | flops 1811939328 | bytes 21233664 | tf_op jit(solution)/shard_map/project/pallas_call | solution.py:23
  17.4 1.7 %collective-permute-done.3.came_ref = f32[32,3584]{1,0:T(8,128)S(1)} collective-permute-done((f32[32,3584]{1,0:T(8,128)S(1)}, f32[32,3584]{1,0:T(8,128)S(1)}, u32[]{:S(2)}, u32[]{:S(2)}) %collective-permute-start.3) | collective-permute-done | bytes 458784 | tf_op jit(solution)/shard_map/ppermute | solution.py:49
  19.2 1.8 %collective-permute-start.4 = (f32[16,3584]{1,0:T(8,128)S(1)}, f32[16,3584]{1,0:T(8,128)S(1)}, u32[]{:S(2)}, u32[]{:S(2)}) collective-permute-start(f32[16,3584]{1,0:T(8,128)S(1)} %get-tuple-element.39.refs_2_), channel_id=1, source_target_pairs={{0,8},{4,12},{8,0},{12,4},{1,9},{5,13},{9,1},{13,5},{2,10},{6,14},... | collective-permute-start | bytes 688136 | tf_op jit(solution)/shard_map/ppermute | solution.py:49
  20.9 5.0 %fetch_out_weight_0.1 = (bf16[3072,1536]{1,0:T(8,128)(2,1)S(1)}, bf16[4,1024,512]{2,1,0:T(8,128)(2,1)S(1)}) custom-call(bf16[3072,4608]{1,0:T(8,128)(2,1)} %refs_0_.7, bf16[4,1024,512]{2,1,0:T(8,128)(2,1)} %refs_1_.3, f32[16,3584]{1,0:T(8,128)S(1)} %get-tuple-element.39.refs_2_), custom_call_target="tpu_custom_call" | custom-call | bytes 13631488 | tf_op jit(solution)/shard_map/fetch_out_weight_0/pallas_call | solution.py:23
  25.9 1.1 %collective-permute-done.4.came_ref = f32[16,3584]{1,0:T(8,128)S(1)} collective-permute-done((f32[16,3584]{1,0:T(8,128)S(1)}, f32[16,3584]{1,0:T(8,128)S(1)}, u32[]{:S(2)}, u32[]{:S(2)}) %collective-permute-start.4) | collective-permute-done | bytes 229408 | tf_op jit(solution)/shard_map/ppermute | solution.py:49
  27.1 0.6 split.1
  27.7 3.9 %collective-permute-start.5 = (bf16[4,4096]{1,0:T(4,128)(2,1)S(1)}, bf16[4,4096]{1,0:T(4,128)(2,1)S(1)}, u32[]{:S(2)}, u32[]{:S(2)}) collective-permute-start(bf16[4,4096]{1,0:T(4,128)(2,1)S(1)} %get-tuple-element.41), channel_id=1, source_target_pairs={{0,3},{1,2},{2,1},{3,0},{4,7},{5,6},{6,5},{7,4},{8,11},{9,10},{10,... | collective-permute-start | bytes 98312 | tf_op jit(solution)/shard_map/ppermute | solution.py:49
  31.6 0.6 collective-permute-start.7
  32.2 3.4 %fetch_out_weight_1.1.refs_6_.refs_4_ = bf16[3072,1280]{1,0:T(8,128)(2,1)S(1)} custom-call(bf16[3072,4608]{1,0:T(8,128)(2,1)} %refs_0_.7, bf16[4,4096]{1,0:T(4,128)(2,1)S(1)} %get-tuple-element.44.refs_1_.refs_3_), custom_call_target="tpu_custom_call" | custom-call | bytes 7864320 | tf_op jit(solution)/shard_map/fetch_out_weight_1/pallas_call | solution.py:23
  35.6 0.8 %collective-permute-done.6.refs_1_ = bf16[4,4096]{1,0:T(4,128)(2,1)S(1)} collective-permute-done((bf16[4,4096]{1,0:T(4,128)(2,1)S(1)}, bf16[4,4096]{1,0:T(4,128)(2,1)S(1)}, u32[]{:S(2)}, u32[]{:S(2)}) %collective-permute-start.6) | collective-permute-done | bytes 32800 | tf_op jit(solution)/shard_map/ppermute | solution.py:49
  36.4 3.4 %attend.1 = (bf16[4,3072]{1,0:T(4,128)(2,1)S(1)}, bf16[4,3072]{1,0:T(4,128)(2,1)S(1)}, bf16[4,3072]{1,0:T(4,128)(2,1)S(1)}, bf16[4,3072]{1,0:T(4,128)(2,1)S(1)}, bf16[3072,512]{1,0:T(8,128)(2,1)S(1)}) custom-call(s32[4]{0:T(128)S(1)} %copy-done.2, bf16[4,4096]{1,0:T(4,128)(2,1)S(1)} %collective-permute-done.5.refs_0_, ...), custom_call_target="tpu_custom_call" | custom-call | flops 201326592 | tf_op jit(solution)/shard_map/attend/pallas_call | solution.py:23
  39.8 3.1 %collective-permute-start.8 = (bf16[4,3072]{1,0:T(4,128)(2,1)S(1)}, bf16[4,3072]{1,0:T(4,128)(2,1)S(1)}, u32[]{:S(2)}, u32[]{:S(2)}) collective-permute-start(bf16[4,3072]{1,0:T(4,128)(2,1)S(1)} %get-tuple-element.46), channel_id=1, source_target_pairs={{0,3},{1,2},{2,1},{3,0},{4,7},{5,6},{6,5},{7,4},{8,11},{9,10},{10,... | collective-permute-start | bytes 73736 | tf_op jit(solution)/shard_map/ppermute | solution.py:49
  42.9 1.4 %collective-permute-start.10 = (bf16[4,3072]{1,0:T(4,128)(2,1)S(1)}, bf16[4,3072]{1,0:T(4,128)(2,1)S(1)}, u32[]{:S(2)}, u32[]{:S(2)}) collective-permute-start(bf16[4,3072]{1,0:T(4,128)(2,1)S(1)} %get-tuple-element.48), channel_id=1, source_target_pairs={{0,1},{1,0},{2,3},{3,2},{4,5},{5,4},{6,7},{7,6},{8,9},{9,8},{10,11... | collective-permute-start | bytes 73736 | tf_op jit(solution)/shard_map/ppermute | solution.py:49
  44.3 3.4 %fetch_out_weight_3.1.refs_4_.refs_5_ = bf16[3072,1280]{1,0:T(8,128)(2,1)S(1)} custom-call(bf16[3072,4608]{1,0:T(8,128)(2,1)} %refs_0_.7, bf16[4,3072]{1,0:T(4,128)(2,1)S(1)} %get-tuple-element.49.refs_1_.refs_3_), custom_call_target="tpu_custom_call" | custom-call | bytes 7864320 | tf_op jit(solution)/shard_map/fetch_out_weight_3/pallas_call | solution.py:23
  48.3 1.6 %collective-permute-start.12 = (bf16[16,3072]{1,0:T(8,128)(2,1)S(1)}, bf16[16,3072]{1,0:T(8,128)(2,1)S(1)}, u32[]{:S(2)}, u32[]{:S(2)}) collective-permute-start(bf16[16,3072]{1,0:T(8,128)(2,1)S(1)} %join.1.refs_0_), channel_id=1, source_target_pairs={{0,8},{4,12},{8,0},{12,4},{1,9},{5,13},{9,1},{13,5},{2,10},{6,14},... | collective-permute-start | bytes 294920 | tf_op jit(solution)/shard_map/ppermute | solution.py:49
  49.9 3.1 %collective-permute-done.12.refs_2_ = bf16[16,3072]{1,0:T(8,128)(2,1)S(1)} collective-permute-done((bf16[16,3072]{1,0:T(8,128)(2,1)S(1)}, bf16[16,3072]{1,0:T(8,128)(2,1)S(1)}, u32[]{:S(2)}, u32[]{:S(2)}) %collective-permute-start.12) | collective-permute-done | bytes 98336 | tf_op jit(solution)/shard_map/ppermute | solution.py:49
  53.0 1.3 %collective-permute-done.13.refs_3_ = bf16[16,3072]{1,0:T(8,128)(2,1)S(1)} collective-permute-done((bf16[16,3072]{1,0:T(8,128)(2,1)S(1)}, bf16[16,3072]{1,0:T(8,128)(2,1)S(1)}, u32[]{:S(2)}, u32[]{:S(2)}) %collective-permute-start.13) | collective-permute-done | bytes 98336 | tf_op jit(solution)/shard_map/ppermute | solution.py:49
  54.3 2.4 %output_part.3 = (f32[64,1536]{1,0:T(8,128)S(1)}, s16[32,1664]{1,0:T(8,128)(2,1)S(1)}) custom-call(s32[2]{0:T(128)S(1)} %pad_add_fusion.refs_3_.me_ref, bf16[16,3072]{1,0:T(8,128)(2,1)S(1)} %join.1.refs_0_, bf16[16,3072]{1,0:T(8,128)(2,1)S(1)} %collective-permute-done.11.refs_1_, bf16[16,3072]{1,0:T(8,128)(2,1)S(1)} %collective-permute-done.12.refs_2_, ...), custom_call_target="tpu_custom_call" | custom-call | flops 603979776 | bytes 393216 | tf_op jit(solution)/shard_map/output_part/pallas_call | solution.py:23
  56.7 0.7 collective-permute-start.14
  57.4 2.7 %output_part.4 = (f32[64,1792]{1,0:T(8,128)S(1)}, s16[32,1920]{1,0:T(8,128)(2,1)S(1)}) custom-call(s32[2]{0:T(128)S(1)} %pad_add_fusion.refs_3_.me_ref, bf16[16,3072]{1,0:T(8,128)(2,1)S(1)} %join.1.refs_0_, bf16[16,3072]{1,0:T(8,128)(2,1)S(1)} %collective-permute-done.11.refs_1_, bf16[16,3072]{1,0:T(8,128)(2,1)S(1)} %collective-permute-done.12.refs_2_, ...), custom_call_target="tpu_custom_call" | custom-call | flops 704643072 | bytes 393216 | tf_op jit(solution)/shard_map/output_part/pallas_call | solution.py:23
  60.1 1.5 %collective-permute-start.16 = (s16[32,1920]{1,0:T(8,128)(2,1)S(1)}, s16[32,1920]{1,0:T(8,128)(2,1)S(1)}, u32[]{:S(2)}, u32[]{:S(2)}) collective-permute-start(s16[32,1920]{1,0:T(8,128)(2,1)S(1)} %get-tuple-element.56), channel_id=1, source_target_pairs={{0,1},{1,0},{2,3},{3,2},{4,5},{5,4},{6,7},{7,6},{8,9},{9,8},{10,11... | collective-permute-start | bytes 368648 | tf_op jit(solution)/shard_map/ppermute | solution.py:49
  62.0 2.1 %output_part.5 = (f32[64,1280]{1,0:T(8,128)S(1)}, s16[32,1408]{1,0:T(8,128)(2,1)S(1)}) custom-call(s32[2]{0:T(128)S(1)} %pad_add_fusion.refs_3_.me_ref, bf16[16,3072]{1,0:T(8,128)(2,1)S(1)} %join.1.refs_0_, bf16[16,3072]{1,0:T(8,128)(2,1)S(1)} %collective-permute-done.11.refs_1_, bf16[16,3072]{1,0:T(8,128)(2,1)S(1)} %collective-permute-done.12.refs_2_, ...), custom_call_target="tpu_custom_call" | custom-call | flops 503316480 | bytes 393216 | tf_op jit(solution)/shard_map/output_part/pallas_call | solution.py:23
  64.1 0.7 collective-permute-start.18
  65.4 3.0 %collective-permute-start.17 = (s16[16,1920]{1,0:T(8,128)(2,1)S(1)}, s16[16,1920]{1,0:T(8,128)(2,1)S(1)}, u32[]{:S(2)}, u32[]{:S(2)}) collective-permute-start(s16[16,1920]{1,0:T(8,128)(2,1)S(1)} %get-tuple-element.59), channel_id=1, source_target_pairs={{0,2},{1,3},{2,0},{3,1},{4,6},{5,7},{6,4},{7,5},{8,10},{9,11},{10,... | collective-permute-start | bytes 184328 | tf_op jit(solution)/shard_map/ppermute | solution.py:49
  68.5 0.9 %collective-permute-done.18.came_ref = s16[32,1408]{1,0:T(8,128)(2,1)S(1)} collective-permute-done((s16[32,1408]{1,0:T(8,128)(2,1)S(1)}, s16[32,1408]{1,0:T(8,128)(2,1)S(1)}, u32[]{:S(2)}, u32[]{:S(2)}) %collective-permute-start.18) | collective-permute-done | bytes 90144 | tf_op jit(solution)/shard_map/ppermute | solution.py:49
  69.6 2.1 %collective-permute-start.19 = (s16[16,1408]{1,0:T(8,128)(2,1)S(1)}, s16[16,1408]{1,0:T(8,128)(2,1)S(1)}, u32[]{:S(2)}, u32[]{:S(2)}) collective-permute-start(s16[16,1408]{1,0:T(8,128)(2,1)S(1)} %get-tuple-element.62), channel_id=1, source_target_pairs={{0,2},{1,3},{2,0},{3,1},{4,6},{5,7},{6,4},{7,5},{8,10},{9,11},{10,... | collective-permute-start | bytes 135176 | tf_op jit(solution)/shard_map/ppermute | solution.py:49
  71.6 2.9 %collective-permute-done.15.refs_1_ = s16[16,1664]{1,0:T(8,128)(2,1)S(1)} collective-permute-done((s16[16,1664]{1,0:T(8,128)(2,1)S(1)}, s16[16,1664]{1,0:T(8,128)(2,1)S(1)}, u32[]{:S(2)}, u32[]{:S(2)}) %collective-permute-start.15) | collective-permute-done | bytes 53280 | tf_op jit(solution)/shard_map/ppermute | solution.py:49
  74.5 1.0 %collective-permute-done.19.refs_5_ = s16[16,1408]{1,0:T(8,128)(2,1)S(1)} collective-permute-done((s16[16,1408]{1,0:T(8,128)(2,1)S(1)}, s16[16,1408]{1,0:T(8,128)(2,1)S(1)}, u32[]{:S(2)}, u32[]{:S(2)}) %collective-permute-start.19) | collective-permute-done | bytes 45088 | tf_op jit(solution)/shard_map/ppermute | solution.py:49
  75.5 0.8 %finish.1 = bf16[16,4608]{1,0:T(8,128)(2,1)} custom-call(f32[16,1536]{1,0:T(8,128)S(1)} %get-tuple-element.54.refs_5_.refs_0_, s16[16,1664]{1,0:T(8,128)(2,1)S(1)} %collective-permute-done.15.refs_1_, f32[16,1792]{1,0:T(8,128)S(1)} %get-tuple-element.58.refs_2_, s16[16,1920]{1,0:T(8,128)(2,1)S(1)} %collective-permute-done.17.refs_3_, ...), custom_call_target="tpu_custom_call" | custom-call | bytes 589824 | tf_op jit(solution)/shard_map/finish/pallas_call | solution.py:23
  (33 shorter events, 2.9 us)
Async XLA Ops:
  1.3 6.7 %collective-permute-start = (f32[2,64]{1,0:T(2,128)S(1)}, f32[2,64]{1,0:T(2,128)S(1)}, u32[]{:S(2)}, u32[]{:S(2)}) collective-permute-start(f32[2,64]{1,0:T(2,128)S(1)} %pad_maximum_fusion.refs_2_.refs_0_), channel_id=1, source_target_pairs={{0,4},{4,0},{8,12},{12,8},{1,5},{5,1},{9,13},{13,9},{2,6},{6,2},{1... | collective-permute-start | bytes 1544 | tf_op jit(solution)/shard_map/ppermute | solution.py:49
  1.9 6.2 %collective-permute-start.1 = (f32[2,64]{1,0:T(2,128)S(1)}, f32[2,64]{1,0:T(2,128)S(1)}, u32[]{:S(2)}, u32[]{:S(2)}) collective-permute-start(f32[2,64]{1,0:T(2,128)S(1)} %pad_maximum_fusion.refs_2_.refs_0_), channel_id=1, source_target_pairs={{0,8},{4,12},{8,0},{12,4},{1,9},{5,13},{9,1},{13,5},{2,10},{6,14},... | collective-permute-start | bytes 1544 | tf_op jit(solution)/shard_map/ppermute | solution.py:49
  4.4 3.7 %collective-permute-start.2 = (f32[2,64]{1,0:T(2,128)S(1)}, f32[2,64]{1,0:T(2,128)S(1)}, u32[]{:S(2)}, u32[]{:S(2)}) collective-permute-start(f32[2,64]{1,0:T(2,128)S(1)} %pad_maximum_fusion.refs_2_.refs_0_), channel_id=1, source_target_pairs={{0,12},{4,8},{8,4},{12,0},{1,13},{5,9},{9,5},{13,1},{2,14},{6,10},... | collective-permute-start | bytes 1544 | tf_op jit(solution)/shard_map/ppermute | solution.py:49
  4.6 3.5 %copy-start = (bf16[64,4608]{1,0:T(8,128)(2,1)S(1)}, bf16[64,4608]{1,0:T(8,128)(2,1)}, u32[]{:S(2)}) copy-start(bf16[64,4608]{1,0:T(8,128)(2,1)} %refs_4_.1) | copy-start | bytes 1769476
  4.6 3.5 %copy-start.1 = (f32[4608]{0:T(1024)S(1)}, f32[4608]{0:T(1024)}, u32[]{:S(2)}) copy-start(f32[4608]{0:T(1024)} %refs_5_.2) | copy-start | bytes 55300
  17.2 1.9 %collective-permute-start.3 = (f32[32,3584]{1,0:T(8,128)S(1)}, f32[32,3584]{1,0:T(8,128)S(1)}, u32[]{:S(2)}, u32[]{:S(2)}) collective-permute-start(f32[32,3584]{1,0:T(8,128)S(1)} %get-tuple-element.37), channel_id=1, source_target_pairs={{0,4},{4,0},{8,12},{12,8},{1,5},{5,1},{9,13},{13,9},{2,6},{6,2},{1... | collective-permute-start | bytes 1376264 | tf_op jit(solution)/shard_map/ppermute | solution.py:49
  19.2 7.9 %collective-permute-start.4 = (f32[16,3584]{1,0:T(8,128)S(1)}, f32[16,3584]{1,0:T(8,128)S(1)}, u32[]{:S(2)}, u32[]{:S(2)}) collective-permute-start(f32[16,3584]{1,0:T(8,128)S(1)} %get-tuple-element.39.refs_2_), channel_id=1, source_target_pairs={{0,8},{4,12},{8,0},{12,4},{1,9},{5,13},{9,1},{13,5},{2,10},{6,14},... | collective-permute-start | bytes 688136 | tf_op jit(solution)/shard_map/ppermute | solution.py:49
  27.7 7.9 %collective-permute-start.5 = (bf16[4,4096]{1,0:T(4,128)(2,1)S(1)}, bf16[4,4096]{1,0:T(4,128)(2,1)S(1)}, u32[]{:S(2)}, u32[]{:S(2)}) collective-permute-start(bf16[4,4096]{1,0:T(4,128)(2,1)S(1)} %get-tuple-element.41), channel_id=1, source_target_pairs={{0,3},{1,2},{2,1},{3,0},{4,7},{5,6},{6,5},{7,4},{8,11},{9,10},{10,... | collective-permute-start | bytes 98312 | tf_op jit(solution)/shard_map/ppermute | solution.py:49
  31.6 4.8 %collective-permute-start.6 = (bf16[4,4096]{1,0:T(4,128)(2,1)S(1)}, bf16[4,4096]{1,0:T(4,128)(2,1)S(1)}, u32[]{:S(2)}, u32[]{:S(2)}) collective-permute-start(bf16[4,4096]{1,0:T(4,128)(2,1)S(1)} %get-tuple-element.42), channel_id=1, source_target_pairs={{0,2},{1,3},{2,0},{3,1},{4,6},{5,7},{6,4},{7,5},{8,10},{9,11},{10,... | collective-permute-start | bytes 98312 | tf_op jit(solution)/shard_map/ppermute | solution.py:49
  31.6 4.8 %collective-permute-start.7 = (bf16[4,4096]{1,0:T(4,128)(2,1)S(1)}, bf16[4,4096]{1,0:T(4,128)(2,1)S(1)}, u32[]{:S(2)}, u32[]{:S(2)}) collective-permute-start(bf16[4,4096]{1,0:T(4,128)(2,1)S(1)} %get-tuple-element.43), channel_id=1, source_target_pairs={{0,1},{1,0},{2,3},{3,2},{4,5},{5,4},{6,7},{7,6},{8,9},{9,8},{10,11... | collective-permute-start | bytes 98312 | tf_op jit(solution)/shard_map/ppermute | solution.py:49
  32.2 4.2 %copy-start.2 = (s32[4]{0:T(128)S(1)}, s32[4]{0:T(128)}, u32[]{:S(2)}) copy-start(s32[4]{0:T(128)} %lengths_ref.1) | copy-start | bytes 52
  39.8 7.8 %collective-permute-start.8 = (bf16[4,3072]{1,0:T(4,128)(2,1)S(1)}, bf16[4,3072]{1,0:T(4,128)(2,1)S(1)}, u32[]{:S(2)}, u32[]{:S(2)}) collective-permute-start(bf16[4,3072]{1,0:T(4,128)(2,1)S(1)} %get-tuple-element.46), channel_id=1, source_target_pairs={{0,3},{1,2},{2,1},{3,0},{4,7},{5,6},{6,5},{7,4},{8,11},{9,10},{10,... | collective-permute-start | bytes 73736 | tf_op jit(solution)/shard_map/ppermute | solution.py:49
  42.9 4.8 %collective-permute-start.9 = (bf16[4,3072]{1,0:T(4,128)(2,1)S(1)}, bf16[4,3072]{1,0:T(4,128)(2,1)S(1)}, u32[]{:S(2)}, u32[]{:S(2)}) collective-permute-start(bf16[4,3072]{1,0:T(4,128)(2,1)S(1)} %get-tuple-element.47), channel_id=1, source_target_pairs={{0,2},{1,3},{2,0},{3,1},{4,6},{5,7},{6,4},{7,5},{8,10},{9,11},{10,... | collective-permute-start | bytes 73736 | tf_op jit(solution)/shard_map/ppermute | solution.py:49
  42.9 4.8 %collective-permute-start.10 = (bf16[4,3072]{1,0:T(4,128)(2,1)S(1)}, bf16[4,3072]{1,0:T(4,128)(2,1)S(1)}, u32[]{:S(2)}, u32[]{:S(2)}) collective-permute-start(bf16[4,3072]{1,0:T(4,128)(2,1)S(1)} %get-tuple-element.48), channel_id=1, source_target_pairs={{0,1},{1,0},{2,3},{3,2},{4,5},{5,4},{6,7},{7,6},{8,9},{9,8},{10,11... | collective-permute-start | bytes 73736 | tf_op jit(solution)/shard_map/ppermute | solution.py:49
  48.3 4.7 %collective-permute-start.12 = (bf16[16,3072]{1,0:T(8,128)(2,1)S(1)}, bf16[16,3072]{1,0:T(8,128)(2,1)S(1)}, u32[]{:S(2)}, u32[]{:S(2)}) collective-permute-start(bf16[16,3072]{1,0:T(8,128)(2,1)S(1)} %join.1.refs_0_), channel_id=1, source_target_pairs={{0,8},{4,12},{8,0},{12,4},{1,9},{5,13},{9,1},{13,5},{2,10},{6,14},... | collective-permute-start | bytes 294920 | tf_op jit(solution)/shard_map/ppermute | solution.py:49
  49.9 3.1 %collective-permute-start.11 = (bf16[16,3072]{1,0:T(8,128)(2,1)S(1)}, bf16[16,3072]{1,0:T(8,128)(2,1)S(1)}, u32[]{:S(2)}, u32[]{:S(2)}) collective-permute-start(bf16[16,3072]{1,0:T(8,128)(2,1)S(1)} %join.1.refs_0_), channel_id=1, source_target_pairs={{0,4},{4,0},{8,12},{12,8},{1,5},{5,1},{9,13},{13,9},{2,6},{6,2},{1... | collective-permute-start | bytes 294920 | tf_op jit(solution)/shard_map/ppermute | solution.py:49
  53.0 1.3 %collective-permute-start.13 = (bf16[16,3072]{1,0:T(8,128)(2,1)S(1)}, bf16[16,3072]{1,0:T(8,128)(2,1)S(1)}, u32[]{:S(2)}, u32[]{:S(2)}) collective-permute-start(bf16[16,3072]{1,0:T(8,128)(2,1)S(1)} %collective-permute-done.12.refs_2_), channel_id=1, source_target_pairs={{0,4},{4,0},{8,12},{12,8},{1,5},{5,1},{9,13},{13,9},{2,6},{6,2},{1... | collective-permute-start | bytes 294920 | tf_op jit(solution)/shard_map/ppermute | solution.py:49
  56.7 5.1 %collective-permute-start.14 = (s16[32,1664]{1,0:T(8,128)(2,1)S(1)}, s16[32,1664]{1,0:T(8,128)(2,1)S(1)}, u32[]{:S(2)}, u32[]{:S(2)}) collective-permute-start(s16[32,1664]{1,0:T(8,128)(2,1)S(1)} %get-tuple-element.51), channel_id=1, source_target_pairs={{0,1},{1,0},{2,3},{3,2},{4,5},{5,4},{6,7},{7,6},{8,9},{9,8},{10,11... | collective-permute-start | bytes 319496 | tf_op jit(solution)/shard_map/ppermute | solution.py:49
  60.1 5.2 %collective-permute-start.16 = (s16[32,1920]{1,0:T(8,128)(2,1)S(1)}, s16[32,1920]{1,0:T(8,128)(2,1)S(1)}, u32[]{:S(2)}, u32[]{:S(2)}) collective-permute-start(s16[32,1920]{1,0:T(8,128)(2,1)S(1)} %get-tuple-element.56), channel_id=1, source_target_pairs={{0,1},{1,0},{2,3},{3,2},{4,5},{5,4},{6,7},{7,6},{8,9},{9,8},{10,11... | collective-permute-start | bytes 368648 | tf_op jit(solution)/shard_map/ppermute | solution.py:49
  64.1 5.3 %collective-permute-start.18 = (s16[32,1408]{1,0:T(8,128)(2,1)S(1)}, s16[32,1408]{1,0:T(8,128)(2,1)S(1)}, u32[]{:S(2)}, u32[]{:S(2)}) collective-permute-start(s16[32,1408]{1,0:T(8,128)(2,1)S(1)} %get-tuple-element.60), channel_id=1, source_target_pairs={{0,1},{1,0},{2,3},{3,2},{4,5},{5,4},{6,7},{7,6},{8,9},{9,8},{10,11... | collective-permute-start | bytes 270344 | tf_op jit(solution)/shard_map/ppermute | solution.py:49
  65.4 9.1 %collective-permute-start.17 = (s16[16,1920]{1,0:T(8,128)(2,1)S(1)}, s16[16,1920]{1,0:T(8,128)(2,1)S(1)}, u32[]{:S(2)}, u32[]{:S(2)}) collective-permute-start(s16[16,1920]{1,0:T(8,128)(2,1)S(1)} %get-tuple-element.59), channel_id=1, source_target_pairs={{0,2},{1,3},{2,0},{3,1},{4,6},{5,7},{6,4},{7,5},{8,10},{9,11},{10,... | collective-permute-start | bytes 184328 | tf_op jit(solution)/shard_map/ppermute | solution.py:49
  68.4 6.1 %collective-permute-start.15 = (s16[16,1664]{1,0:T(8,128)(2,1)S(1)}, s16[16,1664]{1,0:T(8,128)(2,1)S(1)}, u32[]{:S(2)}, u32[]{:S(2)}) collective-permute-start(s16[16,1664]{1,0:T(8,128)(2,1)S(1)} %get-tuple-element.55), channel_id=1, source_target_pairs={{0,2},{1,3},{2,0},{3,1},{4,6},{5,7},{6,4},{7,5},{8,10},{9,11},{10,... | collective-permute-start | bytes 159752 | tf_op jit(solution)/shard_map/ppermute | solution.py:49
  69.6 5.9 %collective-permute-start.19 = (s16[16,1408]{1,0:T(8,128)(2,1)S(1)}, s16[16,1408]{1,0:T(8,128)(2,1)S(1)}, u32[]{:S(2)}, u32[]{:S(2)}) collective-permute-start(s16[16,1408]{1,0:T(8,128)(2,1)S(1)} %get-tuple-element.62), channel_id=1, source_target_pairs={{0,2},{1,3},{2,0},{3,1},{4,6},{5,7},{6,4},{7,5},{8,10},{9,11},{10,... | collective-permute-start | bytes 135176 | tf_op jit(solution)/shard_map/ppermute | solution.py:49

commit v6 on v5

--- a/solution.py
+++ b/solution.py
@@ -17,6 +17,7 @@
 LANES = 128
 PAD = 8
 PIECES = 4
+BESIDE = 5 * 10**9
 
 
 def call(kernel, outs, ins, specs, name, scratch=(), limit=4, flops=0, moved=0):
@@ -126,7 +127,8 @@
     done = first_ref.shape[1]
     starts = [done + sum(ref.shape[1] for ref in groups[:g]) for g in range(len(groups))]
     fetches = [fetches_of([start], [w_ref], [ref], sems.at[pl.ds(g, 1)]) for g, (start, ref) in enumerate(zip(starts, groups))]
-    for fetch in fetches:
+    ahead = 2
+    for fetch in fetches[:ahead]:
         for piece in fetch:
             piece.start()
     me, narrow = me_ref[0], me_ref[1]
@@ -165,10 +167,12 @@
 
     put(jnp.dot(own[...], kv_ref[...], preferred_element_type=jnp.float32), slice(w_ref.shape[1], kept_ref.shape[1]))
     products(first_ref, 0)
-    for start, fetch, ref in zip(starts, fetches, groups):
+    for g, fetch in enumerate(fetches):
         for piece in fetch:
             piece.wait()
-        products(ref, start)
+        for piece in fetches[g + ahead] if g + ahead < len(fetches) else ():
+            piece.start()
+        products(groups[g], starts[g])
 
 
 def project(me, stats, x, gain, w, kv, first, width_all, count, narrow_count, tile):
@@ -195,27 +199,26 @@
     )
 
 
-def fold_kernel(guards, kept_ref, came_ref, *refs):
-    still_ref, sent_ref = refs[guards:]
+def fold_kernel(kept_ref, came_ref, still_ref, sent_ref):
     half = still_ref.shape[0]
     still_ref[...] = kept_ref[:half, :] + came_ref[:half, :]
     sent_ref[...] = kept_ref[half:, :] + came_ref[half:, :]
 
 
-def fold(kept, came, guards):
+def fold(kept, came):
     half = jax.ShapeDtypeStruct((kept.shape[0] // 2, kept.shape[1]), jnp.float32)
     return call(
-        functools.partial(fold_kernel, len(guards)),
+        fold_kernel,
         (half, half),
-        (kept, came, *map(in_vmem, guards)),
-        [FULL] * (2 + len(guards)),
+        (kept, came),
+        [FULL] * 2,
         "fold",
-        moved=16 * kept.size,
-    )
-
-
-def split_kernel(queries, guards, me_ref, kept_ref, came_ref, *refs):
-    out_refs, slots = refs[guards:-1], refs[-1]
+        flops=BESIDE,
+    )
+
+
+def split_kernel(queries, me_ref, kept_ref, came_ref, *refs):
+    out_refs, slots = refs[:-1], refs[-1]
     count, rows = len(out_refs), out_refs[0].shape[0]
     narrow = me_ref[1]
     total = kept_ref[...] + came_ref[...]
@@ -228,13 +231,10 @@
         out_ref[:, mine.shape[1] :] = (mine - high.astype(jnp.float32))[:, queries:].astype(jnp.bfloat16)
 
 
-def attend_kernel(head_dim, count, guards, start, lengths_ref, *refs):
-    came_refs, kv_ref, w_ref = refs[:count][::-1], refs[count], refs[count + 1]
-    refs = refs[count + 2 + guards :]
-    out_refs, share, (heads, contexts, sems) = refs[:count], refs[count], refs[count + 1 :]
-    fetches = fetches_of([start], [w_ref], [share], sems)
-    for fetch in fetches:
-        fetch.start()
+def attend_kernel(head_dim, count, lengths_ref, *refs):
+    came_refs, kv_ref = refs[:count][::-1], refs[count]
+    refs = refs[count + 1 :]
+    out_refs, (heads, contexts) = refs[:count], refs[count:]
     rows, positions = kv_ref.shape[0], kv_ref.shape[1]
     queries = out_refs[0].shape[1]
     each = queries // head_dim
@@ -282,30 +282,27 @@
             for k in range(slabs):
                 start = h * head_dim + k * LANES
                 ref[:, start : start + LANES] = contexts[k, at : at + rows, :].astype(jnp.bfloat16)
-    for fetch in fetches:
-        fetch.wait()
-
-
-def attend(lengths, came, kv, cut, head_dim, queries, guards):
+
+
+def attend(lengths, came, kv, head_dim, queries):
     rows = kv.shape[0]
     count = len(came)
     all_heads = count * queries // head_dim
     scratch = pltpu.VMEM((head_dim // LANES, all_heads * PAD, LANES), jnp.float32)
-    w, start, width = cut
-    return call(
-        functools.partial(attend_kernel, head_dim, count, len(guards), start),
-        [jax.ShapeDtypeStruct((rows, queries), jnp.bfloat16)] * count + [held((w.shape[0], width), w.dtype)],
-        (lengths, *came[::-1], in_vmem(kv), in_hbm(w), *map(in_vmem, guards)),
-        [SCALAR] + [FULL] * (count + 1) + [ANY] + [FULL] * len(guards),
+    return call(
+        functools.partial(attend_kernel, head_dim, count),
+        [jax.ShapeDtypeStruct((rows, queries), jnp.bfloat16)] * count,
+        (lengths, *came[::-1], in_vmem(kv)),
+        [SCALAR] + [FULL] * (count + 1),
         "attend",
-        scratch=[scratch, scratch, pltpu.SemaphoreType.DMA((1, PIECES))],
+        scratch=[scratch, scratch],
         limit=8,
-        flops=4 * rows * count * queries * kv.shape[1],
-    )
-
-
-def join_kernel(guards, me_ref, *refs):
-    count = len(refs) - guards - 2
+        flops=BESIDE,
+    )
+
+
+def join_kernel(me_ref, *refs):
+    count = len(refs) - 2
     out_ref, joined = refs[-2:]
     rows = refs[0].shape[0]
     for d in range(count):
@@ -328,8 +325,8 @@
     return ref[:, :width].astype(jnp.int32).astype(jnp.float32) * (jnp.exp2(power) * (1.0 / STEPS))
 
 
-def output_kernel(count, weights, narrow_count, me_ref, *refs):
-    x_refs, w_refs, (sums_ref, sent_ref) = refs[:count], refs[count : count + weights], refs[-2:]
+def output_kernel(start, count, narrow_count, me_ref, *refs):
+    x_refs, w_ref, (sums_ref, sent_ref) = refs[:count], refs[count], refs[-2:]
     block = x_refs[0].shape[0]
     ratio = count // narrow_count
     places = []
@@ -341,28 +338,24 @@
             place = jnp.where(apart == distance, k, place)
         places.append(pl.multiple_of((place * ratio + wide % ratio) * block, block))
     x = jnp.concatenate([ref[...] for ref in x_refs], axis=0)
-    at = 0
-    for w_ref in w_refs:
-        width = w_ref.shape[1]
-        got = jnp.dot(x, w_ref[...], preferred_element_type=jnp.float32)
-        for d, place in enumerate(places):
-            sums_ref[pl.ds(place, block), at : at + width] = got[d * block : (d + 1) * block, :]
-        at += width
+    got = jnp.dot(x, w_ref[:, start : start + sums_ref.shape[1]], preferred_element_type=jnp.float32)
+    for d, place in enumerate(places):
+        sums_ref[pl.ds(place, block), :] = got[d * block : (d + 1) * block, :]
     code(sums_ref[sums_ref.shape[0] // 2 :, :], sent_ref)
 
 
-def output_part(me, blocks, ws, narrow_count, after):
+def output_part(me, blocks, w, start, columns, narrow_count, after):
     count = len(blocks)
     block, depth = blocks[0].shape
-    rows, columns = count * block, sum(w.shape[1] for w in ws)
-    return call(
-        functools.partial(output_kernel, count, len(ws), narrow_count),
+    rows = count * block
+    return call(
+        functools.partial(output_kernel, start, count, narrow_count),
         (
             jax.ShapeDtypeStruct((rows, columns), jnp.float32),
             jax.ShapeDtypeStruct((rows // 2, columns + LANES), jnp.int16),
         ),
-        (me, *blocks, *map(in_vmem, ws), *after),
-        [SCALAR] + [FULL] * (count + len(ws)) + [ANY] * len(after),
+        (me, *blocks, in_vmem(w), *after),
+        [SCALAR] + [FULL] * (count + 1) + [ANY] * len(after),
         "output_part",
         limit=8,
         flops=2 * rows * depth * columns,
@@ -393,18 +386,23 @@
     )
 
 
-def finish_kernel(starts, *refs):
+def finish_kernel(starts, kinds, *refs):
     out_ref = refs[-1]
-    for at, kept_ref, came_ref in zip(starts, refs[:-1:2], refs[1:-1:2]):
-        width = kept_ref.shape[1]
-        out_ref[:, at : at + width] = (kept_ref[...] + decode(came_ref, width)).astype(jnp.bfloat16)
+    k = 0
+    for at, kind in zip(starts, kinds):
+        width = refs[k].shape[1]
+        done = refs[k][...]
+        if kind == 2:
+            done = (done + decode(refs[k + 1], width)).astype(jnp.bfloat16)
+        out_ref[:, at : at + width] = done
+        k += kind
 
 
 def finish(starts, cuts):
     parts = [x for cut in cuts for x in cut]
     rows, columns = parts[0].shape[0], sum(cut[0].shape[1] for cut in cuts)
     return call(
-        functools.partial(finish_kernel, starts),
+        functools.partial(finish_kernel, starts, [len(cut) for cut in cuts]),
         jax.ShapeDtypeStruct((rows, columns), jnp.bfloat16),
         parts,
         [FULL] * len(parts),
@@ -440,38 +438,31 @@
         narrow_count,
         tile,
     )
-    ends = [columns // LANES * k // 18 * LANES for k in (0, 6, 11, 13, 18)]
-    cuts = [(out_weight, start, end - start) for start, end in zip(ends, ends[1:])]
     d = 1
     while 2 * d < wide_count:
-        kept, sent = fold(kept, swap(sent, "wide", d), [])
+        kept, sent = fold(kept, swap(sent, "wide", d))
         d *= 2
-    out_parts = [None] * 4
-    out_parts[0], cache = fetch([cuts[0], (kv_cache, None, None)], [sent], "fetch_out_weight_0")
     split = call(
-        functools.partial(split_kernel, queries, 1),
+        functools.partial(split_kernel, queries),
         [jax.ShapeDtypeStruct((own_rows, queries + 4 * head_dim), jnp.bfloat16)] * narrow_count,
-        (me, kept, swap(sent, "wide", d), in_vmem(out_parts[0])),
-        [SCALAR] + [FULL] * 3,
+        (me, kept, swap(sent, "wide", d)),
+        [SCALAR] + [FULL] * 2,
         "split",
         scratch=[pltpu.VMEM((narrow_count * PAD, queries + 2 * head_dim), jnp.float32)],
-        moved=16 * kept.size,
-    )
-    [out_parts[1]] = fetch([cuts[1]], [split[0]], "fetch_out_weight_1")
-    *context, out_parts[2] = attend(
-        lengths, exchange(split, "narrow"), cache, cuts[2], head_dim, queries, [out_parts[1]]
-    )
-    [out_parts[3]] = fetch([cuts[3]], [context[0]], "fetch_out_weight_3")
+        flops=BESIDE,
+    )
+    context = attend(lengths, exchange(split, "narrow"), kv_cache, head_dim, queries)
     returned = call(
-        functools.partial(join_kernel, 1),
+        join_kernel,
         jax.ShapeDtypeStruct((narrow_count * own_rows, queries), jnp.bfloat16),
-        (me, *exchange(context, "narrow")[::-1], in_vmem(out_parts[3])),
-        [SCALAR] + [FULL] * (narrow_count + 1),
+        (me, *exchange(context, "narrow")[::-1]),
+        [SCALAR] + [FULL] * narrow_count,
         "join",
         scratch=[pltpu.VMEM((narrow_count * PAD, queries), jnp.float32)],
-        moved=4 * narrow_count * own_rows * queries,
+        flops=BESIDE,
     )
     gathered = gather(returned, "wide")
+    ends = [columns // LANES * k // 18 * LANES for k in (0,7,15,18)]
     cut_sums, halved, last = [], [], []
 
     def exchange_cut(kept, sent, after):
@@ -483,13 +474,15 @@
         halved.append(kept)
         cut_sums.append((kept, swap(sent, "narrow", d)))
 
-    for parts in (out_parts[:1], out_parts[2:], out_parts[1:2]):
-        kept, sent = output_part(me, gathered, parts, narrow_count, halved[-1:])
+    for start, end in zip(ends, ends[1:]):
+        kept, sent = output_part(me, gathered, out_weight, start, end - start, narrow_count, halved[-1:])
         if last:
             exchange_cut(*last, [kept])
         last = (kept, sent)
-    exchange_cut(*last, [])
-    return finish([ends[0], ends[2], ends[1]], cut_sums)
+    early = finish([0], cut_sums[:1])
+    exchange_cut(*last, [early])
+    cut_sums[0] = (early,)
+    return finish(ends[:-1], cut_sums)
 
 
 def solution(mesh):

time: 76.5 us -> 74 us (0.967)
  Pallas kernels: 37.5 us -> 25 us
  waiting for transfers between devices: 13.4 us -> 23.9 us
    pallas_call x16 -> x14, Pallas kernels: 37.5 us -> 25 us  [call(): pl.pallas_call(kernel, out_shape=outs, in_specs=specs, out_specs=jax.tree...]
    ppermute x20, waiting for transfers between devices: 13.4 us -> 23.9 us  [swap(): return lax.ppermute(x, axis, [(i, i ^ distance) for i in range(count)])]
  transfers between devices with their start and end apart: 20 -> 20, of which waited for: 10 -> 14; matrix products, arithmetic and copies ran while one was open for 0% -> 0% of each run, Pallas kernels for 27% -> 12%
where the time goes in v6:
time: 74 us; the launch traced here: 73.8 us
  Pallas kernels  25 us (34%)
  waiting for transfers between devices  23.9 us (32%)
  starting transfers between devices  23.3 us (31%)
  other arithmetic  1.4 us (2%)
    pallas_call x14, Pallas kernels, call(): pl.pallas_call(kernel, out_shape=outs, in_specs=specs, out_specs=jax.tree...  25 us
    ppermute x20, waiting for transfers between devices, swap(): return lax.ppermute(x, axis, [(i, i ^ distance) for i in range(count)])  23.9 us
    ppermute x20, starting transfers between devices, swap(): return lax.ppermute(x, axis, [(i, i ^ distance) for i in range(count)])  23.3 us
  transfers between devices with their start and end apart: 20, of which 14 were waited for; matrix products, arithmetic and copies ran while one was open for 0% of the time, Pallas kernels for 12%

profile of v6, /device:TPU:0, one launch (start us, length us, event | category | flops | bytes accessed | tf_op | source)
XLA Modules:
  0.0 73.8 jit_solution(1889404302490542613)
XLA Ops:
  0.0 1.3 %convert_reduce_fusion = (f32[64]{0:T(128)S(1)}, f32[64]{0:T(128)S(1)}) fusion(bf16[64,4608]{1,0:T(8,128)(2,1)} %refs_4_.5), kind=kLoop, calls=%fused_computation.1 | loop fusion | flops 1179520 | bytes 590336 | tf_op jit(solution)/shard_map/reduce_sum | solution.py:424
  1.3 2.5 %collective-permute-start.2 = (f32[2,64]{1,0:T(2,128)S(1)}, f32[2,64]{1,0:T(2,128)S(1)}, u32[]{:S(2)}, u32[]{:S(2)}) collective-permute-start(f32[2,64]{1,0:T(2,128)S(1)} %pad_maximum_fusion.refs_2_.refs_0_), channel_id=1, source_target_pairs={{0,12},{4,8},{8,4},{12,0},{1,13},{5,9},{9,5},{13,1},{2,14},{6,10},... | collective-permute-start | bytes 1544 | tf_op jit(solution)/shard_map/ppermute | solution.py:50
  3.8 0.6 collective-permute-start.1
  4.6 3.5 %fetch_query_weight.1 = (bf16[4608,768]{1,0:T(8,128)(2,1)S(1)}, bf16[1152,512]{1,0:T(8,128)(2,1)S(1)}) custom-call(bf16[4608,3072]{1,0:T(8,128)(2,1)} %refs_6_.1, bf16[1152,512]{1,0:T(8,128)(2,1)} %refs_1_.1, f32[2,64]{1,0:T(2,128)S(1)} %pad_maximum_fusion.refs_2_.refs_0_, s32[2]{0:T(128)S(1)} %pad_add_fusion.refs_3_.me_ref), custom_call_target="tpu_custom_call" | custom-call | bytes 8257536 | tf_op jit(solution)/shard_map/fetch_query_weight/pallas_call | solution.py:24
  8.1 9.2 %project.1 = (f32[32,3584]{1,0:T(8,128)S(1)}, f32[32,3584]{1,0:T(8,128)S(1)}) custom-call(s32[2]{0:T(128)S(1)} %pad_add_fusion.refs_3_.me_ref, f32[2,64]{1,0:T(2,128)S(1)} %pad_maximum_fusion.refs_2_.refs_0_, f32[2,64]{1,0:T(2,128)S(1)} %collective-permute-done.refs_1_, f32[2,64]{1,0:T(2,128)S(1)} %collective-permute-done.1.refs_2_, ...), custom_call_target="tpu_custom_call" | custom-call | flops 1811939328 | bytes 21233664 | tf_op jit(solution)/shard_map/project/pallas_call | solution.py:24
  17.9 1.4 %collective-permute-done.3.came_ref = f32[32,3584]{1,0:T(8,128)S(1)} collective-permute-done((f32[32,3584]{1,0:T(8,128)S(1)}, f32[32,3584]{1,0:T(8,128)S(1)}, u32[]{:S(2)}, u32[]{:S(2)}) %collective-permute-start.3) | collective-permute-done | bytes 458784 | tf_op jit(solution)/shard_map/ppermute | solution.py:50
  19.4 1.7 %collective-permute-start.4 = (f32[16,3584]{1,0:T(8,128)S(1)}, f32[16,3584]{1,0:T(8,128)S(1)}, u32[]{:S(2)}, u32[]{:S(2)}) collective-permute-start(f32[16,3584]{1,0:T(8,128)S(1)} %get-tuple-element.36), channel_id=1, source_target_pairs={{0,8},{4,12},{8,0},{12,4},{1,9},{5,13},{9,1},{13,5},{2,10},{6,14},... | collective-permute-start | bytes 688136 | tf_op jit(solution)/shard_map/ppermute | solution.py:50
  21.1 6.2 %collective-permute-done.4.came_ref = f32[16,3584]{1,0:T(8,128)S(1)} collective-permute-done((f32[16,3584]{1,0:T(8,128)S(1)}, f32[16,3584]{1,0:T(8,128)S(1)}, u32[]{:S(2)}, u32[]{:S(2)}) %collective-permute-start.4) | collective-permute-done | bytes 229408 | tf_op jit(solution)/shard_map/ppermute | solution.py:50
  27.3 0.6 split.1
  27.9 3.7 %collective-permute-start.5 = (bf16[4,4096]{1,0:T(4,128)(2,1)S(1)}, bf16[4,4096]{1,0:T(4,128)(2,1)S(1)}, u32[]{:S(2)}, u32[]{:S(2)}) collective-permute-start(bf16[4,4096]{1,0:T(4,128)(2,1)S(1)} %get-tuple-element.37), channel_id=1, source_target_pairs={{0,3},{1,2},{2,1},{3,0},{4,7},{5,6},{6,5},{7,4},{8,11},{9,10},{10,... | collective-permute-start | bytes 98312 | tf_op jit(solution)/shard_map/ppermute | solution.py:50
  31.6 0.8 %collective-permute-start.7 = (bf16[4,4096]{1,0:T(4,128)(2,1)S(1)}, bf16[4,4096]{1,0:T(4,128)(2,1)S(1)}, u32[]{:S(2)}, u32[]{:S(2)}) collective-permute-start(bf16[4,4096]{1,0:T(4,128)(2,1)S(1)} %get-tuple-element.39), channel_id=1, source_target_pairs={{0,1},{1,0},{2,3},{3,2},{4,5},{5,4},{6,7},{7,6},{8,9},{9,8},{10,11... | collective-permute-start | bytes 98312 | tf_op jit(solution)/shard_map/ppermute | solution.py:50
  32.4 1.7 %collective-permute-done.5.refs_0_ = bf16[4,4096]{1,0:T(4,128)(2,1)S(1)} collective-permute-done((bf16[4,4096]{1,0:T(4,128)(2,1)S(1)}, bf16[4,4096]{1,0:T(4,128)(2,1)S(1)}, u32[]{:S(2)}, u32[]{:S(2)}) %collective-permute-start.5) | collective-permute-done | bytes 32800 | tf_op jit(solution)/shard_map/ppermute | solution.py:50
  34.1 2.4 %collective-permute-done.6.refs_1_ = bf16[4,4096]{1,0:T(4,128)(2,1)S(1)} collective-permute-done((bf16[4,4096]{1,0:T(4,128)(2,1)S(1)}, bf16[4,4096]{1,0:T(4,128)(2,1)S(1)}, u32[]{:S(2)}, u32[]{:S(2)}) %collective-permute-start.6) | collective-permute-done | bytes 32800 | tf_op jit(solution)/shard_map/ppermute | solution.py:50
  36.5 2.4 %attend.1 = (bf16[4,3072]{1,0:T(4,128)(2,1)S(1)}, bf16[4,3072]{1,0:T(4,128)(2,1)S(1)}, bf16[4,3072]{1,0:T(4,128)(2,1)S(1)}, bf16[4,3072]{1,0:T(4,128)(2,1)S(1)}) custom-call(s32[4]{0:T(128)S(1)} %copy-done.3, bf16[4,4096]{1,0:T(4,128)(2,1)S(1)} %collective-permute-done.5.refs_0_, bf16[4,4096]{1,0:T(4,128)(2,1)S(1)} %collective-permute-done.6.refs_1_, ...), custom_call_target="tpu_custom_call" | custom-call | flops 5000000000 | tf_op jit(solution)/shard_map/attend/pallas_call | solution.py:24
  38.9 1.5 %collective-permute-start.8 = (bf16[4,3072]{1,0:T(4,128)(2,1)S(1)}, bf16[4,3072]{1,0:T(4,128)(2,1)S(1)}, u32[]{:S(2)}, u32[]{:S(2)}) collective-permute-start(bf16[4,3072]{1,0:T(4,128)(2,1)S(1)} %get-tuple-element.41), channel_id=1, source_target_pairs={{0,3},{1,2},{2,1},{3,0},{4,7},{5,6},{6,5},{7,4},{8,11},{9,10},{10,... | collective-permute-start | bytes 73736 | tf_op jit(solution)/shard_map/ppermute | solution.py:50
  40.4 0.6 collective-permute-start.9
  41.1 2.3 %collective-permute-start.10 = (bf16[4,3072]{1,0:T(4,128)(2,1)S(1)}, bf16[4,3072]{1,0:T(4,128)(2,1)S(1)}, u32[]{:S(2)}, u32[]{:S(2)}) collective-permute-start(bf16[4,3072]{1,0:T(4,128)(2,1)S(1)} %get-tuple-element.43), channel_id=1, source_target_pairs={{0,1},{1,0},{2,3},{3,2},{4,5},{5,4},{6,7},{7,6},{8,9},{9,8},{10,11... | collective-permute-start | bytes 73736 | tf_op jit(solution)/shard_map/ppermute | solution.py:50
  43.4 1.2 %collective-permute-done.8.refs_0_ = bf16[4,3072]{1,0:T(4,128)(2,1)S(1)} collective-permute-done((bf16[4,3072]{1,0:T(4,128)(2,1)S(1)}, bf16[4,3072]{1,0:T(4,128)(2,1)S(1)}, u32[]{:S(2)}, u32[]{:S(2)}) %collective-permute-start.8) | collective-permute-done | bytes 24608 | tf_op jit(solution)/shard_map/ppermute | solution.py:50
  46.0 1.5 %collective-permute-start.12 = (bf16[16,3072]{1,0:T(8,128)(2,1)S(1)}, bf16[16,3072]{1,0:T(8,128)(2,1)S(1)}, u32[]{:S(2)}, u32[]{:S(2)}) collective-permute-start(bf16[16,3072]{1,0:T(8,128)(2,1)S(1)} %join.1.refs_0_), channel_id=1, source_target_pairs={{0,8},{4,12},{8,0},{12,4},{1,9},{5,13},{9,1},{13,5},{2,10},{6,14},... | collective-permute-start | bytes 294920 | tf_op jit(solution)/shard_map/ppermute | solution.py:50
  47.5 3.2 %collective-permute-done.12.refs_2_ = bf16[16,3072]{1,0:T(8,128)(2,1)S(1)} collective-permute-done((bf16[16,3072]{1,0:T(8,128)(2,1)S(1)}, bf16[16,3072]{1,0:T(8,128)(2,1)S(1)}, u32[]{:S(2)}, u32[]{:S(2)}) %collective-permute-start.12) | collective-permute-done | bytes 98336 | tf_op jit(solution)/shard_map/ppermute | solution.py:50
  50.7 1.3 %collective-permute-done.13.refs_3_ = bf16[16,3072]{1,0:T(8,128)(2,1)S(1)} collective-permute-done((bf16[16,3072]{1,0:T(8,128)(2,1)S(1)}, bf16[16,3072]{1,0:T(8,128)(2,1)S(1)}, u32[]{:S(2)}, u32[]{:S(2)}) %collective-permute-start.13) | collective-permute-done | bytes 98336 | tf_op jit(solution)/shard_map/ppermute | solution.py:50
  52.1 2.7 %output_part.3 = (f32[64,1792]{1,0:T(8,128)S(1)}, s16[32,1920]{1,0:T(8,128)(2,1)S(1)}) custom-call(s32[2]{0:T(128)S(1)} %pad_add_fusion.refs_3_.me_ref, bf16[16,3072]{1,0:T(8,128)(2,1)S(1)} %join.1.refs_0_, bf16[16,3072]{1,0:T(8,128)(2,1)S(1)} %collective-permute-done.11.refs_1_, bf16[16,3072]{1,0:T(8,128)(2,1)S(1)} %collective-permute-done.12.refs_2_, ...), custom_call_target="tpu_custom_call" | custom-call | flops 704643072 | bytes 393216 | tf_op jit(solution)/shard_map/output_part/pallas_call | solution.py:24
  54.8 1.8 %collective-permute-start.14 = (s16[32,1920]{1,0:T(8,128)(2,1)S(1)}, s16[32,1920]{1,0:T(8,128)(2,1)S(1)}, u32[]{:S(2)}, u32[]{:S(2)}) collective-permute-start(s16[32,1920]{1,0:T(8,128)(2,1)S(1)} %get-tuple-element.46), channel_id=1, source_target_pairs={{0,1},{1,0},{2,3},{3,2},{4,5},{5,4},{6,7},{7,6},{8,9},{9,8},{10,11... | collective-permute-start | bytes 368648 | tf_op jit(solution)/shard_map/ppermute | solution.py:50
  56.6 2.9 %output_part.4 = (f32[64,2048]{1,0:T(8,128)S(1)}, s16[32,2176]{1,0:T(8,128)(2,1)S(1)}) custom-call(s32[2]{0:T(128)S(1)} %pad_add_fusion.refs_3_.me_ref, bf16[16,3072]{1,0:T(8,128)(2,1)S(1)} %join.1.refs_0_, bf16[16,3072]{1,0:T(8,128)(2,1)S(1)} %collective-permute-done.11.refs_1_, bf16[16,3072]{1,0:T(8,128)(2,1)S(1)} %collective-permute-done.12.refs_2_, ...), custom_call_target="tpu_custom_call" | custom-call | flops 805306368 | bytes 393216 | tf_op jit(solution)/shard_map/output_part/pallas_call | solution.py:24
  60.5 1.8 %collective-permute-start.15 = (s16[16,1920]{1,0:T(8,128)(2,1)S(1)}, s16[16,1920]{1,0:T(8,128)(2,1)S(1)}, u32[]{:S(2)}, u32[]{:S(2)}) collective-permute-start(s16[16,1920]{1,0:T(8,128)(2,1)S(1)} %get-tuple-element.49), channel_id=1, source_target_pairs={{0,2},{1,3},{2,0},{3,1},{4,6},{5,7},{6,4},{7,5},{8,10},{9,11},{10,... | collective-permute-start | bytes 184328 | tf_op jit(solution)/shard_map/ppermute | solution.py:50
  62.2 1.6 %output_part.5 = (f32[64,768]{1,0:T(8,128)S(1)}, s16[32,896]{1,0:T(8,128)(2,1)S(1)}) custom-call(s32[2]{0:T(128)S(1)} %pad_add_fusion.refs_3_.me_ref, bf16[16,3072]{1,0:T(8,128)(2,1)S(1)} %join.1.refs_0_, bf16[16,3072]{1,0:T(8,128)(2,1)S(1)} %collective-permute-done.11.refs_1_, bf16[16,3072]{1,0:T(8,128)(2,1)S(1)} %collective-permute-done.12.refs_2_, ...), custom_call_target="tpu_custom_call" | custom-call | flops 301989888 | bytes 393216 | tf_op jit(solution)/shard_map/output_part/pallas_call | solution.py:24
  63.8 1.2 %collective-permute-start.18 = (s16[32,896]{1,0:T(8,128)(2,1)S(1)}, s16[32,896]{1,0:T(8,128)(2,1)S(1)}, u32[]{:S(2)}, u32[]{:S(2)}) collective-permute-start(s16[32,896]{1,0:T(8,128)(2,1)S(1)} %get-tuple-element.54), channel_id=1, source_target_pairs={{0,1},{1,0},{2,3},{3,2},{4,5},{5,4},{6,7},{7,6},{8,9},{9,8},{10,11... | collective-permute-start | bytes 172040 | tf_op jit(solution)/shard_map/ppermute | solution.py:50
  65.1 1.7 %collective-permute-done.16.came_ref = s16[32,2176]{1,0:T(8,128)(2,1)S(1)} collective-permute-done((s16[32,2176]{1,0:T(8,128)(2,1)S(1)}, s16[32,2176]{1,0:T(8,128)(2,1)S(1)}, u32[]{:S(2)}, u32[]{:S(2)}) %collective-permute-start.16) | collective-permute-done | bytes 139296 | tf_op jit(solution)/shard_map/ppermute | solution.py:50
  67.3 0.8 %collective-permute-done.18.came_ref = s16[32,896]{1,0:T(8,128)(2,1)S(1)} collective-permute-done((s16[32,896]{1,0:T(8,128)(2,1)S(1)}, s16[32,896]{1,0:T(8,128)(2,1)S(1)}, u32[]{:S(2)}, u32[]{:S(2)}) %collective-permute-start.18) | collective-permute-done | bytes 57376 | tf_op jit(solution)/shard_map/ppermute | solution.py:50
  68.3 2.1 %collective-permute-start.19 = (s16[16,896]{1,0:T(8,128)(2,1)S(1)}, s16[16,896]{1,0:T(8,128)(2,1)S(1)}, u32[]{:S(2)}, u32[]{:S(2)}) collective-permute-start(s16[16,896]{1,0:T(8,128)(2,1)S(1)} %get-tuple-element.56), channel_id=1, source_target_pairs={{0,2},{1,3},{2,0},{3,1},{4,6},{5,7},{6,4},{7,5},{8,10},{9,11},{10,... | collective-permute-start | bytes 86024 | tf_op jit(solution)/shard_map/ppermute | solution.py:50
  70.4 2.1 %collective-permute-done.17.refs_2_ = s16[16,2176]{1,0:T(8,128)(2,1)S(1)} collective-permute-done((s16[16,2176]{1,0:T(8,128)(2,1)S(1)}, s16[16,2176]{1,0:T(8,128)(2,1)S(1)}, u32[]{:S(2)}, u32[]{:S(2)}) %collective-permute-start.17) | collective-permute-done | bytes 69664 | tf_op jit(solution)/shard_map/ppermute | solution.py:50
  73.1 0.8 %finish.3 = bf16[16,4608]{1,0:T(8,128)(2,1)} custom-call(bf16[16,1792]{1,0:T(8,128)(2,1)S(1)} %finish.2.refs_0_, f32[16,2048]{1,0:T(8,128)S(1)} %get-tuple-element.52.refs_1_, s16[16,2176]{1,0:T(8,128)(2,1)S(1)} %collective-permute-done.17.refs_2_, f32[16,768]{1,0:T(8,128)S(1)} %get-tuple-element.55.refs_3_, s16[16,896]{1,0:T(8,128)(2,1)S(1)} %collective-permute-done.19.refs_4_), custom_call_target="tpu_custom_call" | custom-call | bytes 589824 | tf_op jit(solution)/shard_map/finish/pallas_call | solution.py:24
  (48 shorter events, 4.4 us)
Async XLA Ops:
  1.3 6.7 %collective-permute-start.2 = (f32[2,64]{1,0:T(2,128)S(1)}, f32[2,64]{1,0:T(2,128)S(1)}, u32[]{:S(2)}, u32[]{:S(2)}) collective-permute-start(f32[2,64]{1,0:T(2,128)S(1)} %pad_maximum_fusion.refs_2_.refs_0_), channel_id=1, source_target_pairs={{0,12},{4,8},{8,4},{12,0},{1,13},{5,9},{9,5},{13,1},{2,14},{6,10},... | collective-permute-start | bytes 1544 | tf_op jit(solution)/shard_map/ppermute | solution.py:50
  3.8 4.3 %collective-permute-start.1 = (f32[2,64]{1,0:T(2,128)S(1)}, f32[2,64]{1,0:T(2,128)S(1)}, u32[]{:S(2)}, u32[]{:S(2)}) collective-permute-start(f32[2,64]{1,0:T(2,128)S(1)} %pad_maximum_fusion.refs_2_.refs_0_), channel_id=1, source_target_pairs={{0,8},{4,12},{8,0},{12,4},{1,9},{5,13},{9,1},{13,5},{2,10},{6,14},... | collective-permute-start | bytes 1544 | tf_op jit(solution)/shard_map/ppermute | solution.py:50
  4.4 3.6 %collective-permute-start = (f32[2,64]{1,0:T(2,128)S(1)}, f32[2,64]{1,0:T(2,128)S(1)}, u32[]{:S(2)}, u32[]{:S(2)}) collective-permute-start(f32[2,64]{1,0:T(2,128)S(1)} %pad_maximum_fusion.refs_2_.refs_0_), channel_id=1, source_target_pairs={{0,4},{4,0},{8,12},{12,8},{1,5},{5,1},{9,13},{13,9},{2,6},{6,2},{1... | collective-permute-start | bytes 1544 | tf_op jit(solution)/shard_map/ppermute | solution.py:50
  4.6 3.5 %copy-start = (bf16[64,4608]{1,0:T(8,128)(2,1)S(1)}, bf16[64,4608]{1,0:T(8,128)(2,1)}, u32[]{:S(2)}) copy-start(bf16[64,4608]{1,0:T(8,128)(2,1)} %refs_4_.5) | copy-start | bytes 1769476
  4.6 3.5 %copy-start.1 = (f32[4608]{0:T(1024)S(1)}, f32[4608]{0:T(1024)}, u32[]{:S(2)}) copy-start(f32[4608]{0:T(1024)} %refs_5_.1) | copy-start | bytes 55300
  17.3 2.0 %collective-permute-start.3 = (f32[32,3584]{1,0:T(8,128)S(1)}, f32[32,3584]{1,0:T(8,128)S(1)}, u32[]{:S(2)}, u32[]{:S(2)}) collective-permute-start(f32[32,3584]{1,0:T(8,128)S(1)} %get-tuple-element.34), channel_id=1, source_target_pairs={{0,4},{4,0},{8,12},{12,8},{1,5},{5,1},{9,13},{13,9},{2,6},{6,2},{1... | collective-permute-start | bytes 1376264 | tf_op jit(solution)/shard_map/ppermute | solution.py:50
  19.4 7.9 %collective-permute-start.4 = (f32[16,3584]{1,0:T(8,128)S(1)}, f32[16,3584]{1,0:T(8,128)S(1)}, u32[]{:S(2)}, u32[]{:S(2)}) collective-permute-start(f32[16,3584]{1,0:T(8,128)S(1)} %get-tuple-element.36), channel_id=1, source_target_pairs={{0,8},{4,12},{8,0},{12,4},{1,9},{5,13},{9,1},{13,5},{2,10},{6,14},... | collective-permute-start | bytes 688136 | tf_op jit(solution)/shard_map/ppermute | solution.py:50
  27.3 9.1 %copy-start.2 = (bf16[4,1024,512]{2,1,0:T(8,128)(2,1)S(1)}, bf16[4,1024,512]{2,1,0:T(8,128)(2,1)}, u32[]{:S(2)}) copy-start(bf16[4,1024,512]{2,1,0:T(8,128)(2,1)} %refs_4_.6) | copy-start | bytes 12582916
  27.3 9.1 %copy-start.3 = (s32[4]{0:T(128)S(1)}, s32[4]{0:T(128)}, u32[]{:S(2)}) copy-start(s32[4]{0:T(128)} %lengths_ref.1) | copy-start | bytes 52
  27.3 24.7 %slice-start = ((s8[28311552]{0:T(1024)(128)(4,1)}), s8[4194304]{0:T(1024)(128)(4,1)S(1)}, s32[]{:S(2)}) async-start(s8[28311552]{0:T(1024)(128)(4,1)} %bitcast.4), calls=%async_computation | async-start | bytes 8388608
  27.3 24.7 %slice-start.1 = ((s8[28311552]{0:T(1024)(128)(4,1)}), s8[4194304]{0:T(1024)(128)(4,1)S(1)}, s32[]{:S(2)}) async-start(s8[28311552]{0:T(1024)(128)(4,1)} %bitcast.4), calls=%async_computation.1 | async-start | bytes 8388608
  27.3 24.7 %slice-start.2 = ((s8[28311552]{0:T(1024)(128)(4,1)}), s8[4194304]{0:T(1024)(128)(4,1)S(1)}, s32[]{:S(2)}) async-start(s8[28311552]{0:T(1024)(128)(4,1)} %bitcast.4), calls=%async_computation.2 | async-start | bytes 8388608
  27.9 6.1 %collective-permute-start.5 = (bf16[4,4096]{1,0:T(4,128)(2,1)S(1)}, bf16[4,4096]{1,0:T(4,128)(2,1)S(1)}, u32[]{:S(2)}, u32[]{:S(2)}) collective-permute-start(bf16[4,4096]{1,0:T(4,128)(2,1)S(1)} %get-tuple-element.37), channel_id=1, source_target_pairs={{0,3},{1,2},{2,1},{3,0},{4,7},{5,6},{6,5},{7,4},{8,11},{9,10},{10,... | collective-permute-start | bytes 98312 | tf_op jit(solution)/shard_map/ppermute | solution.py:50
  31.6 4.8 %collective-permute-start.6 = (bf16[4,4096]{1,0:T(4,128)(2,1)S(1)}, bf16[4,4096]{1,0:T(4,128)(2,1)S(1)}, u32[]{:S(2)}, u32[]{:S(2)}) collective-permute-start(bf16[4,4096]{1,0:T(4,128)(2,1)S(1)} %get-tuple-element.38), channel_id=1, source_target_pairs={{0,2},{1,3},{2,0},{3,1},{4,6},{5,7},{6,4},{7,5},{8,10},{9,11},{10,... | collective-permute-start | bytes 98312 | tf_op jit(solution)/shard_map/ppermute | solution.py:50
  31.6 4.8 %collective-permute-start.7 = (bf16[4,4096]{1,0:T(4,128)(2,1)S(1)}, bf16[4,4096]{1,0:T(4,128)(2,1)S(1)}, u32[]{:S(2)}, u32[]{:S(2)}) collective-permute-start(bf16[4,4096]{1,0:T(4,128)(2,1)S(1)} %get-tuple-element.39), channel_id=1, source_target_pairs={{0,1},{1,0},{2,3},{3,2},{4,5},{5,4},{6,7},{7,6},{8,9},{9,8},{10,11... | collective-permute-start | bytes 98312 | tf_op jit(solution)/shard_map/ppermute | solution.py:50
  36.4 15.6 %slice-start.3 = ((s8[28311552]{0:T(1024)(128)(4,1)}), s8[4194304]{0:T(1024)(128)(4,1)S(1)}, s32[]{:S(2)}) async-start(s8[28311552]{0:T(1024)(128)(4,1)} %bitcast.4), calls=%async_computation.3 | async-start | bytes 8388608
  36.5 15.6 %slice-start.4 = ((s8[28311552]{0:T(1024)(128)(4,1)}), s8[4194304]{0:T(1024)(128)(4,1)S(1)}, s32[]{:S(2)}) async-start(s8[28311552]{0:T(1024)(128)(4,1)} %bitcast.4), calls=%async_computation.4 | async-start | bytes 8388608
  38.9 5.7 %collective-permute-start.8 = (bf16[4,3072]{1,0:T(4,128)(2,1)S(1)}, bf16[4,3072]{1,0:T(4,128)(2,1)S(1)}, u32[]{:S(2)}, u32[]{:S(2)}) collective-permute-start(bf16[4,3072]{1,0:T(4,128)(2,1)S(1)} %get-tuple-element.41), channel_id=1, source_target_pairs={{0,3},{1,2},{2,1},{3,0},{4,7},{5,6},{6,5},{7,4},{8,11},{9,10},{10,... | collective-permute-start | bytes 73736 | tf_op jit(solution)/shard_map/ppermute | solution.py:50
  40.4 4.7 %collective-permute-start.9 = (bf16[4,3072]{1,0:T(4,128)(2,1)S(1)}, bf16[4,3072]{1,0:T(4,128)(2,1)S(1)}, u32[]{:S(2)}, u32[]{:S(2)}) collective-permute-start(bf16[4,3072]{1,0:T(4,128)(2,1)S(1)} %get-tuple-element.42), channel_id=1, source_target_pairs={{0,2},{1,3},{2,0},{3,1},{4,6},{5,7},{6,4},{7,5},{8,10},{9,11},{10,... | collective-permute-start | bytes 73736 | tf_op jit(solution)/shard_map/ppermute | solution.py:50
  41.1 4.3 %collective-permute-start.10 = (bf16[4,3072]{1,0:T(4,128)(2,1)S(1)}, bf16[4,3072]{1,0:T(4,128)(2,1)S(1)}, u32[]{:S(2)}, u32[]{:S(2)}) collective-permute-start(bf16[4,3072]{1,0:T(4,128)(2,1)S(1)} %get-tuple-element.43), channel_id=1, source_target_pairs={{0,1},{1,0},{2,3},{3,2},{4,5},{5,4},{6,7},{7,6},{8,9},{9,8},{10,11... | collective-permute-start | bytes 73736 | tf_op jit(solution)/shard_map/ppermute | solution.py:50
  45.4 6.6 %slice-start.5 = ((s8[28311552]{0:T(1024)(128)(4,1)}), s8[4194304]{0:T(1024)(128)(4,1)S(1)}, s32[]{:S(2)}) async-start(s8[28311552]{0:T(1024)(128)(4,1)} %bitcast.4), calls=%async_computation.5 | async-start | bytes 8388608
  45.4 6.6 %slice-start.6 = ((s8[28311552]{0:T(1024)(128)(4,1)}), s8[3145728]{0:T(1024)(128)(4,1)S(1)}, s32[]{:S(2)}) async-start(s8[28311552]{0:T(1024)(128)(4,1)} %bitcast.4), calls=%async_computation.6 | async-start | bytes 6291456
  46.0 4.7 %collective-permute-start.12 = (bf16[16,3072]{1,0:T(8,128)(2,1)S(1)}, bf16[16,3072]{1,0:T(8,128)(2,1)S(1)}, u32[]{:S(2)}, u32[]{:S(2)}) collective-permute-start(bf16[16,3072]{1,0:T(8,128)(2,1)S(1)} %join.1.refs_0_), channel_id=1, source_target_pairs={{0,8},{4,12},{8,0},{12,4},{1,9},{5,13},{9,1},{13,5},{2,10},{6,14},... | collective-permute-start | bytes 294920 | tf_op jit(solution)/shard_map/ppermute | solution.py:50
  47.5 3.2 %collective-permute-start.11 = (bf16[16,3072]{1,0:T(8,128)(2,1)S(1)}, bf16[16,3072]{1,0:T(8,128)(2,1)S(1)}, u32[]{:S(2)}, u32[]{:S(2)}) collective-permute-start(bf16[16,3072]{1,0:T(8,128)(2,1)S(1)} %join.1.refs_0_), channel_id=1, source_target_pairs={{0,4},{4,0},{8,12},{12,8},{1,5},{5,1},{9,13},{13,9},{2,6},{6,2},{1... | collective-permute-start | bytes 294920 | tf_op jit(solution)/shard_map/ppermute | solution.py:50
  50.7 1.3 %collective-permute-start.13 = (bf16[16,3072]{1,0:T(8,128)(2,1)S(1)}, bf16[16,3072]{1,0:T(8,128)(2,1)S(1)}, u32[]{:S(2)}, u32[]{:S(2)}) collective-permute-start(bf16[16,3072]{1,0:T(8,128)(2,1)S(1)} %collective-permute-done.12.refs_2_), channel_id=1, source_target_pairs={{0,4},{4,0},{8,12},{12,8},{1,5},{5,1},{9,13},{13,9},{2,6},{6,2},{1... | collective-permute-start | bytes 294920 | tf_op jit(solution)/shard_map/ppermute | solution.py:50
  54.8 5.5 %collective-permute-start.14 = (s16[32,1920]{1,0:T(8,128)(2,1)S(1)}, s16[32,1920]{1,0:T(8,128)(2,1)S(1)}, u32[]{:S(2)}, u32[]{:S(2)}) collective-permute-start(s16[32,1920]{1,0:T(8,128)(2,1)S(1)} %get-tuple-element.46), channel_id=1, source_target_pairs={{0,1},{1,0},{2,3},{3,2},{4,5},{5,4},{6,7},{7,6},{8,9},{9,8},{10,11... | collective-permute-start | bytes 368648 | tf_op jit(solution)/shard_map/ppermute | solution.py:50
  59.6 7.2 %collective-permute-start.16 = (s16[32,2176]{1,0:T(8,128)(2,1)S(1)}, s16[32,2176]{1,0:T(8,128)(2,1)S(1)}, u32[]{:S(2)}, u32[]{:S(2)}) collective-permute-start(s16[32,2176]{1,0:T(8,128)(2,1)S(1)} %get-tuple-element.50), channel_id=1, source_target_pairs={{0,1},{1,0},{2,3},{3,2},{4,5},{5,4},{6,7},{7,6},{8,9},{9,8},{10,11... | collective-permute-start | bytes 417800 | tf_op jit(solution)/shard_map/ppermute | solution.py:50
  60.5 6.8 %collective-permute-start.15 = (s16[16,1920]{1,0:T(8,128)(2,1)S(1)}, s16[16,1920]{1,0:T(8,128)(2,1)S(1)}, u32[]{:S(2)}, u32[]{:S(2)}) collective-permute-start(s16[16,1920]{1,0:T(8,128)(2,1)S(1)} %get-tuple-element.49), channel_id=1, source_target_pairs={{0,2},{1,3},{2,0},{3,1},{4,6},{5,7},{6,4},{7,5},{8,10},{9,11},{10,... | collective-permute-start | bytes 184328 | tf_op jit(solution)/shard_map/ppermute | solution.py:50
  63.8 4.2 %collective-permute-start.18 = (s16[32,896]{1,0:T(8,128)(2,1)S(1)}, s16[32,896]{1,0:T(8,128)(2,1)S(1)}, u32[]{:S(2)}, u32[]{:S(2)}) collective-permute-start(s16[32,896]{1,0:T(8,128)(2,1)S(1)} %get-tuple-element.54), channel_id=1, source_target_pairs={{0,1},{1,0},{2,3},{3,2},{4,5},{5,4},{6,7},{7,6},{8,9},{9,8},{10,11... | collective-permute-start | bytes 172040 | tf_op jit(solution)/shard_map/ppermute | solution.py:50
  67.0 5.5 %collective-permute-start.17 = (s16[16,2176]{1,0:T(8,128)(2,1)S(1)}, s16[16,2176]{1,0:T(8,128)(2,1)S(1)}, u32[]{:S(2)}, u32[]{:S(2)}) collective-permute-start(s16[16,2176]{1,0:T(8,128)(2,1)S(1)} %get-tuple-element.53), channel_id=1, source_target_pairs={{0,2},{1,3},{2,0},{3,1},{4,6},{5,7},{6,4},{7,5},{8,10},{9,11},{10,... | collective-permute-start | bytes 208904 | tf_op jit(solution)/shard_map/ppermute | solution.py:50
  68.3 4.8 %collective-permute-start.19 = (s16[16,896]{1,0:T(8,128)(2,1)S(1)}, s16[16,896]{1,0:T(8,128)(2,1)S(1)}, u32[]{:S(2)}, u32[]{:S(2)}) collective-permute-start(s16[16,896]{1,0:T(8,128)(2,1)S(1)} %get-tuple-element.56), channel_id=1, source_target_pairs={{0,2},{1,3},{2,0},{3,1},{4,6},{5,7},{6,4},{7,5},{8,10},{9,11},{10,... | collective-permute-start | bytes 86024 | tf_op jit(solution)/shard_map/ppermute | solution.py:50

commit v7 on v6

--- a/solution.py
+++ b/solution.py
@@ -16,7 +16,6 @@
 TINY = 1e-37
 LANES = 128
 PAD = 8
-PIECES = 4
 BESIDE = 5 * 10**9
 
 
@@ -81,56 +80,50 @@
     return [sum(((k >> b) & 1) << (bits - 1 - b) for b in range(bits)) for k in range(count)]
 
 
-def fetches_of(starts, sources, shares, sems):
-    fetches = []
-    for k, start in enumerate(starts):
-        source, share = sources[k], shares[k]
-        if start is not None:
-            source = source.at[:, pl.ds(start, share.shape[1])]
-        pieces = PIECES if len(share.shape) > 2 or share.shape[0] % (16 * PIECES) == 0 else 1
-        step = share.shape[0] // pieces
-        for p in range(pieces):
-            at = pl.ds(p * step, step)
-            fetches.append(pltpu.make_async_copy(source.at[at], share.at[at], sems.at[k, p]))
-    return fetches
-
-
-def fetch_kernel(starts, *refs):
-    count = len(starts)
-    fetches = fetches_of(starts, refs[:count], refs[-count - 1 : -1], refs[-1])
+def fetch_kernel(w_ref, kv_ref, *refs):
+    share_ref, kv_share_ref, sems = refs[-3:]
+    fetches = [
+        pltpu.make_async_copy(w_ref.at[: share_ref.shape[0]], share_ref, sems.at[0]),
+        pltpu.make_async_copy(kv_ref, kv_share_ref, sems.at[1]),
+    ]
     for fetch in fetches:
         fetch.start()
     for fetch in fetches:
         fetch.wait()
 
 
-def fetch(items, after, name):
-    shapes = [x.shape if start is None else (x.shape[0], width) for x, start, width in items]
-    return call(
-        functools.partial(fetch_kernel, [start for _, start, _ in items]),
-        [held(shape, x.dtype) for shape, (x, _, _) in zip(shapes, items)],
-        (*[in_hbm(x) for x, _, _ in items], *after),
-        [ANY] * (len(items) + len(after)),
-        name,
-        scratch=[pltpu.SemaphoreType.DMA((len(items), PIECES))],
-        moved=sum(2 * math.prod(shape) for shape in shapes),
-    )
-
-
-def project_kernel(many, width_all, count, narrow_count, tile, me_ref, *refs):
+def fetch(w, kv, rows, after):
+    return call(
+        fetch_kernel,
+        [held((rows, w.shape[1]), w.dtype), held(kv.shape, kv.dtype)],
+        (in_hbm(w), in_hbm(kv), *after),
+        [ANY] * (2 + len(after)),
+        "fetch_query_weight",
+        scratch=[pltpu.SemaphoreType.DMA((2,))],
+        moved=2 * (rows * w.shape[1] + kv.size),
+    )
+
+
+def row_block(rows):
+    return LANES * max(1, rows // LANES // 6)
+
+
+def project_kernel(many, width_all, count, narrow_count, me_ref, *refs):
     stat_refs, refs = refs[:many], refs[many:]
-    x_ref, gain_ref, w_ref, kv_ref, first_ref, kept_ref, sent_ref, normed, own, *groups, sems = refs
+    x_ref, gain_ref, w_ref, kv_ref, first_ref, kept_ref, sent_ref, normed, own, *blocks, sems = refs
     rows, width = x_ref.shape
     half = rows // 2
     block = rows // count
     sub_width = width // narrow_count
-    done = first_ref.shape[1]
-    starts = [done + sum(ref.shape[1] for ref in groups[:g]) for g in range(len(groups))]
-    fetches = [fetches_of([start], [w_ref], [ref], sems.at[pl.ds(g, 1)]) for g, (start, ref) in enumerate(zip(starts, groups))]
-    ahead = 2
+    done = first_ref.shape[0]
+    step = blocks[0].shape[0]
+    fetches = [
+        pltpu.make_async_copy(w_ref.at[done + g * step : done + (g + 1) * step], ref, sems.at[g])
+        for g, ref in enumerate(blocks)
+    ]
+    ahead = 3
     for fetch in fetches[:ahead]:
-        for piece in fetch:
-            piece.start()
+        fetch.start()
     me, narrow = me_ref[0], me_ref[1]
     stats = stat_refs[0][...]
     for ref in stat_refs[1:]:
@@ -157,32 +150,36 @@
         def _(j=j):
             own[...] = normed[:, j * sub_width : (j + 1) * sub_width]
 
-    def put(got, at):
-        kept_ref[:, at] = got[:half, :]
-        sent_ref[:, at] = got[half:, :]
+    queries = w_ref.shape[1]
 
     def products(source, start):
-        got = jnp.dot(normed[...], source[...], preferred_element_type=jnp.float32)
-        put(got, slice(start, start + source.shape[1]))
-
-    put(jnp.dot(own[...], kv_ref[...], preferred_element_type=jnp.float32), slice(w_ref.shape[1], kept_ref.shape[1]))
+        got = jnp.dot(normed[:, start : start + source.shape[0]], source[...], preferred_element_type=jnp.float32)
+        if start:
+            kept_ref[:, :queries] += got[:half, :]
+            sent_ref[:, :queries] += got[half:, :]
+        else:
+            kept_ref[:, :queries] = got[:half, :]
+            sent_ref[:, :queries] = got[half:, :]
+
+    fresh = jnp.dot(own[...], kv_ref[...], preferred_element_type=jnp.float32)
+    kept_ref[:, queries:] = fresh[:half, :]
+    sent_ref[:, queries:] = fresh[half:, :]
     products(first_ref, 0)
     for g, fetch in enumerate(fetches):
-        for piece in fetch:
-            piece.wait()
-        for piece in fetches[g + ahead] if g + ahead < len(fetches) else ():
-            piece.start()
-        products(groups[g], starts[g])
-
-
-def project(me, stats, x, gain, w, kv, first, width_all, count, narrow_count, tile):
+        fetch.wait()
+        if g + ahead < len(fetches):
+            fetches[g + ahead].start()
+        products(blocks[g], done + g * step)
+
+
+def project(me, stats, x, gain, w, kv, first, width_all, count, narrow_count):
     rows, width = x.shape
     queries = w.shape[1]
-    tiles = (queries - first.shape[1]) // tile
-    groups = [2] * (tiles // 2) + [1] * (tiles % 2)
+    step = row_block(width)
+    blocks = (width - first.shape[0]) // step
     half = jax.ShapeDtypeStruct((rows // 2, queries + kv.shape[1]), jnp.float32)
     return call(
-        functools.partial(project_kernel, len(stats), width_all, count, narrow_count, tile),
+        functools.partial(project_kernel, len(stats), width_all, count, narrow_count),
         (half, half),
         (me, *stats, x, gain, in_hbm(w), in_vmem(kv), in_vmem(first)),
         [SCALAR] + [FULL] * (len(stats) + 2) + [ANY] + [FULL] * 2,
@@ -190,12 +187,12 @@
         scratch=[
             pltpu.VMEM((rows, width), jnp.bfloat16),
             pltpu.VMEM((rows, width // narrow_count), jnp.bfloat16),
-            *[pltpu.VMEM((width, n * tile), jnp.bfloat16) for n in groups],
-            pltpu.SemaphoreType.DMA((len(groups), PIECES)),
+            *[pltpu.VMEM((step, queries), jnp.bfloat16)] * blocks,
+            pltpu.SemaphoreType.DMA((blocks,)),
         ],
-        limit=30,
+        limit=32,
         flops=2 * rows * width * queries,
-        moved=2 * width * tiles * tile,
+        moved=2 * blocks * step * queries,
     )
 
 
@@ -419,12 +416,10 @@
     rows, width = activations.shape
     queries = query_weight.shape[1]
     columns = out_weight.shape[1]
-    tile = 256
     values = activations.astype(jnp.float32)
     stats = jnp.stack([jnp.sum(values, axis=1), jnp.sum(values * values, axis=1)])
-    first_part, kv_part = fetch(
-        [(query_weight, 0, queries // tile // 4 * tile), (kv_weight, None, None)], [stats, me], "fetch_query_weight"
-    )
+    step = row_block(width)
+    first_part, kv_part = fetch(query_weight, kv_weight, width // step // 3 * step, [stats, me])
     kept, sent = project(
         me,
         sent_apart(stats, "wide"),
@@ -436,7 +431,6 @@
         width * wide_count,
         wide_count,
         narrow_count,
-        tile,
     )
     d = 1
     while 2 * d < wide_count:

time: 74 us -> 73.6 us (level)
  transfers between devices with their start and end apart: 20 -> 20, of which waited for: 14 -> 14; matrix products, arithmetic and copies ran while one was open for 0% -> 0% of each run, Pallas kernels for 12% -> 13%
where the time goes in v7:
time: 73.6 us; the launch traced here: 73.4 us
  Pallas kernels  24.6 us (33%)
  waiting for transfers between devices  23.9 us (32%)
  starting transfers between devices  23.3 us (32%)
  other arithmetic  1.4 us (2%)
    pallas_call x14, Pallas kernels, call(): pl.pallas_call(kernel, out_shape=outs, in_specs=specs, out_specs=jax.tree...  24.6 us
    ppermute x20, waiting for transfers between devices, swap(): return lax.ppermute(x, axis, [(i, i ^ distance) for i in range(count)])  23.9 us
    ppermute x20, starting transfers between devices, swap(): return lax.ppermute(x, axis, [(i, i ^ distance) for i in range(count)])  23.3 us
  transfers between devices with their start and end apart: 20, of which 14 were waited for; matrix products, arithmetic and copies ran while one was open for 0% of the time, Pallas kernels for 13%

profile of v7, /device:TPU:0, one launch (start us, length us, event | category | flops | bytes accessed | tf_op | source)
XLA Modules:
  0.0 73.4 jit_solution(1310085697770415675)
XLA Ops:
  0.0 1.3 %convert_reduce_fusion = (f32[64]{0:T(128)S(1)}, f32[64]{0:T(128)S(1)}) fusion(bf16[64,4608]{1,0:T(8,128)(2,1)} %refs_4_.5), kind=kLoop, calls=%fused_computation.1 | loop fusion | flops 1179520 | bytes 590336 | tf_op jit(solution)/shard_map/reduce_sum | solution.py:420
  1.3 2.5 %collective-permute-start.2 = (f32[2,64]{1,0:T(2,128)S(1)}, f32[2,64]{1,0:T(2,128)S(1)}, u32[]{:S(2)}, u32[]{:S(2)}) collective-permute-start(f32[2,64]{1,0:T(2,128)S(1)} %pad_maximum_fusion.refs_0_), channel_id=1, source_target_pairs={{0,12},{4,8},{8,4},{12,0},{1,13},{5,9},{9,5},{13,1},{2,14},{6,10},... | collective-permute-start | bytes 1544 | tf_op jit(solution)/shard_map/ppermute | solution.py:49
  3.8 0.6 collective-permute-start.1
  4.6 4.0 %fetch_query_weight.1 = (bf16[1536,3072]{1,0:T(8,128)(2,1)S(1)}, bf16[1152,512]{1,0:T(8,128)(2,1)S(1)}) custom-call(bf16[4608,3072]{1,0:T(8,128)(2,1)} %refs_6_.1, bf16[1152,512]{1,0:T(8,128)(2,1)} %kv_ref.1, f32[2,64]{1,0:T(2,128)S(1)} %pad_maximum_fusion.refs_0_, s32[2]{0:T(128)S(1)} %pad_add_fusion.refs_1_.me_ref), custom_call_target="tpu_custom_call" | custom-call | bytes 10616832 | tf_op jit(solution)/shard_map/fetch_query_weight/pallas_call | solution.py:23
  8.7 8.2 %project.1 = (f32[32,3584]{1,0:T(8,128)S(1)}, f32[32,3584]{1,0:T(8,128)S(1)}) custom-call(s32[2]{0:T(128)S(1)} %pad_add_fusion.refs_1_.me_ref, f32[2,64]{1,0:T(2,128)S(1)} %pad_maximum_fusion.refs_0_, f32[2,64]{1,0:T(2,128)S(1)} %collective-permute-done.refs_1_, f32[2,64]{1,0:T(2,128)S(1)} %collective-permute-done.1.refs_2_, ...), custom_call_target="tpu_custom_call" | custom-call | flops 1811939328 | bytes 18874368 | tf_op jit(solution)/shard_map/project/pallas_call | solution.py:23
  17.4 1.4 %collective-permute-done.3.came_ref = f32[32,3584]{1,0:T(8,128)S(1)} collective-permute-done((f32[32,3584]{1,0:T(8,128)S(1)}, f32[32,3584]{1,0:T(8,128)S(1)}, u32[]{:S(2)}, u32[]{:S(2)}) %collective-permute-start.3) | collective-permute-done | bytes 458784 | tf_op jit(solution)/shard_map/ppermute | solution.py:49
  18.9 1.7 %collective-permute-start.4 = (f32[16,3584]{1,0:T(8,128)S(1)}, f32[16,3584]{1,0:T(8,128)S(1)}, u32[]{:S(2)}, u32[]{:S(2)}) collective-permute-start(f32[16,3584]{1,0:T(8,128)S(1)} %get-tuple-element.36), channel_id=1, source_target_pairs={{0,8},{4,12},{8,0},{12,4},{1,9},{5,13},{9,1},{13,5},{2,10},{6,14},... | collective-permute-start | bytes 688136 | tf_op jit(solution)/shard_map/ppermute | solution.py:49
  20.6 6.2 %collective-permute-done.4.came_ref = f32[16,3584]{1,0:T(8,128)S(1)} collective-permute-done((f32[16,3584]{1,0:T(8,128)S(1)}, f32[16,3584]{1,0:T(8,128)S(1)}, u32[]{:S(2)}, u32[]{:S(2)}) %collective-permute-start.4) | collective-permute-done | bytes 229408 | tf_op jit(solution)/shard_map/ppermute | solution.py:49
  26.9 0.6 split.1
  27.5 3.7 %collective-permute-start.5 = (bf16[4,4096]{1,0:T(4,128)(2,1)S(1)}, bf16[4,4096]{1,0:T(4,128)(2,1)S(1)}, u32[]{:S(2)}, u32[]{:S(2)}) collective-permute-start(bf16[4,4096]{1,0:T(4,128)(2,1)S(1)} %get-tuple-element.37), channel_id=1, source_target_pairs={{0,3},{1,2},{2,1},{3,0},{4,7},{5,6},{6,5},{7,4},{8,11},{9,10},{10,... | collective-permute-start | bytes 98312 | tf_op jit(solution)/shard_map/ppermute | solution.py:49
  31.2 0.8 %collective-permute-start.7 = (bf16[4,4096]{1,0:T(4,128)(2,1)S(1)}, bf16[4,4096]{1,0:T(4,128)(2,1)S(1)}, u32[]{:S(2)}, u32[]{:S(2)}) collective-permute-start(bf16[4,4096]{1,0:T(4,128)(2,1)S(1)} %get-tuple-element.39), channel_id=1, source_target_pairs={{0,1},{1,0},{2,3},{3,2},{4,5},{5,4},{6,7},{7,6},{8,9},{9,8},{10,11... | collective-permute-start | bytes 98312 | tf_op jit(solution)/shard_map/ppermute | solution.py:49
  32.0 1.7 %collective-permute-done.5.refs_0_ = bf16[4,4096]{1,0:T(4,128)(2,1)S(1)} collective-permute-done((bf16[4,4096]{1,0:T(4,128)(2,1)S(1)}, bf16[4,4096]{1,0:T(4,128)(2,1)S(1)}, u32[]{:S(2)}, u32[]{:S(2)}) %collective-permute-start.5) | collective-permute-done | bytes 32800 | tf_op jit(solution)/shard_map/ppermute | solution.py:49
  33.6 2.4 %collective-permute-done.6.refs_1_ = bf16[4,4096]{1,0:T(4,128)(2,1)S(1)} collective-permute-done((bf16[4,4096]{1,0:T(4,128)(2,1)S(1)}, bf16[4,4096]{1,0:T(4,128)(2,1)S(1)}, u32[]{:S(2)}, u32[]{:S(2)}) %collective-permute-start.6) | collective-permute-done | bytes 32800 | tf_op jit(solution)/shard_map/ppermute | solution.py:49
  36.0 2.4 %attend.1 = (bf16[4,3072]{1,0:T(4,128)(2,1)S(1)}, bf16[4,3072]{1,0:T(4,128)(2,1)S(1)}, bf16[4,3072]{1,0:T(4,128)(2,1)S(1)}, bf16[4,3072]{1,0:T(4,128)(2,1)S(1)}) custom-call(s32[4]{0:T(128)S(1)} %copy-done.3, bf16[4,4096]{1,0:T(4,128)(2,1)S(1)} %collective-permute-done.5.refs_0_, bf16[4,4096]{1,0:T(4,128)(2,1)S(1)} %collective-permute-done.6.refs_1_, ...), custom_call_target="tpu_custom_call" | custom-call | flops 5000000000 | tf_op jit(solution)/shard_map/attend/pallas_call | solution.py:23
  38.5 1.5 %collective-permute-start.8 = (bf16[4,3072]{1,0:T(4,128)(2,1)S(1)}, bf16[4,3072]{1,0:T(4,128)(2,1)S(1)}, u32[]{:S(2)}, u32[]{:S(2)}) collective-permute-start(bf16[4,3072]{1,0:T(4,128)(2,1)S(1)} %get-tuple-element.41), channel_id=1, source_target_pairs={{0,3},{1,2},{2,1},{3,0},{4,7},{5,6},{6,5},{7,4},{8,11},{9,10},{10,... | collective-permute-start | bytes 73736 | tf_op jit(solution)/shard_map/ppermute | solution.py:49
  40.0 0.6 collective-permute-start.9
  40.6 2.3 %collective-permute-start.10 = (bf16[4,3072]{1,0:T(4,128)(2,1)S(1)}, bf16[4,3072]{1,0:T(4,128)(2,1)S(1)}, u32[]{:S(2)}, u32[]{:S(2)}) collective-permute-start(bf16[4,3072]{1,0:T(4,128)(2,1)S(1)} %get-tuple-element.43), channel_id=1, source_target_pairs={{0,1},{1,0},{2,3},{3,2},{4,5},{5,4},{6,7},{7,6},{8,9},{9,8},{10,11... | collective-permute-start | bytes 73736 | tf_op jit(solution)/shard_map/ppermute | solution.py:49
  42.9 1.2 %collective-permute-done.8.refs_0_ = bf16[4,3072]{1,0:T(4,128)(2,1)S(1)} collective-permute-done((bf16[4,3072]{1,0:T(4,128)(2,1)S(1)}, bf16[4,3072]{1,0:T(4,128)(2,1)S(1)}, u32[]{:S(2)}, u32[]{:S(2)}) %collective-permute-start.8) | collective-permute-done | bytes 24608 | tf_op jit(solution)/shard_map/ppermute | solution.py:49
  45.6 1.5 %collective-permute-start.12 = (bf16[16,3072]{1,0:T(8,128)(2,1)S(1)}, bf16[16,3072]{1,0:T(8,128)(2,1)S(1)}, u32[]{:S(2)}, u32[]{:S(2)}) collective-permute-start(bf16[16,3072]{1,0:T(8,128)(2,1)S(1)} %join.1.refs_0_), channel_id=1, source_target_pairs={{0,8},{4,12},{8,0},{12,4},{1,9},{5,13},{9,1},{13,5},{2,10},{6,14},... | collective-permute-start | bytes 294920 | tf_op jit(solution)/shard_map/ppermute | solution.py:49
  47.1 3.2 %collective-permute-done.12.refs_2_ = bf16[16,3072]{1,0:T(8,128)(2,1)S(1)} collective-permute-done((bf16[16,3072]{1,0:T(8,128)(2,1)S(1)}, bf16[16,3072]{1,0:T(8,128)(2,1)S(1)}, u32[]{:S(2)}, u32[]{:S(2)}) %collective-permute-start.12) | collective-permute-done | bytes 98336 | tf_op jit(solution)/shard_map/ppermute | solution.py:49
  50.3 1.3 %collective-permute-done.13.refs_3_ = bf16[16,3072]{1,0:T(8,128)(2,1)S(1)} collective-permute-done((bf16[16,3072]{1,0:T(8,128)(2,1)S(1)}, bf16[16,3072]{1,0:T(8,128)(2,1)S(1)}, u32[]{:S(2)}, u32[]{:S(2)}) %collective-permute-start.13) | collective-permute-done | bytes 98336 | tf_op jit(solution)/shard_map/ppermute | solution.py:49
  51.7 2.7 %output_part.3 = (f32[64,1792]{1,0:T(8,128)S(1)}, s16[32,1920]{1,0:T(8,128)(2,1)S(1)}) custom-call(s32[2]{0:T(128)S(1)} %pad_add_fusion.refs_1_.me_ref, bf16[16,3072]{1,0:T(8,128)(2,1)S(1)} %join.1.refs_0_, bf16[16,3072]{1,0:T(8,128)(2,1)S(1)} %collective-permute-done.11.refs_1_, bf16[16,3072]{1,0:T(8,128)(2,1)S(1)} %collective-permute-done.12.refs_2_, ...), custom_call_target="tpu_custom_call" | custom-call | flops 704643072 | bytes 393216 | tf_op jit(solution)/shard_map/output_part/pallas_call | solution.py:23
  54.3 1.8 %collective-permute-start.14 = (s16[32,1920]{1,0:T(8,128)(2,1)S(1)}, s16[32,1920]{1,0:T(8,128)(2,1)S(1)}, u32[]{:S(2)}, u32[]{:S(2)}) collective-permute-start(s16[32,1920]{1,0:T(8,128)(2,1)S(1)} %get-tuple-element.46), channel_id=1, source_target_pairs={{0,1},{1,0},{2,3},{3,2},{4,5},{5,4},{6,7},{7,6},{8,9},{9,8},{10,11... | collective-permute-start | bytes 368648 | tf_op jit(solution)/shard_map/ppermute | solution.py:49
  56.2 2.9 %output_part.4 = (f32[64,2048]{1,0:T(8,128)S(1)}, s16[32,2176]{1,0:T(8,128)(2,1)S(1)}) custom-call(s32[2]{0:T(128)S(1)} %pad_add_fusion.refs_1_.me_ref, bf16[16,3072]{1,0:T(8,128)(2,1)S(1)} %join.1.refs_0_, bf16[16,3072]{1,0:T(8,128)(2,1)S(1)} %collective-permute-done.11.refs_1_, bf16[16,3072]{1,0:T(8,128)(2,1)S(1)} %collective-permute-done.12.refs_2_, ...), custom_call_target="tpu_custom_call" | custom-call | flops 805306368 | bytes 393216 | tf_op jit(solution)/shard_map/output_part/pallas_call | solution.py:23
  60.0 1.8 %collective-permute-start.15 = (s16[16,1920]{1,0:T(8,128)(2,1)S(1)}, s16[16,1920]{1,0:T(8,128)(2,1)S(1)}, u32[]{:S(2)}, u32[]{:S(2)}) collective-permute-start(s16[16,1920]{1,0:T(8,128)(2,1)S(1)} %get-tuple-element.49), channel_id=1, source_target_pairs={{0,2},{1,3},{2,0},{3,1},{4,6},{5,7},{6,4},{7,5},{8,10},{9,11},{10,... | collective-permute-start | bytes 184328 | tf_op jit(solution)/shard_map/ppermute | solution.py:49
  61.8 1.6 %output_part.5 = (f32[64,768]{1,0:T(8,128)S(1)}, s16[32,896]{1,0:T(8,128)(2,1)S(1)}) custom-call(s32[2]{0:T(128)S(1)} %pad_add_fusion.refs_1_.me_ref, bf16[16,3072]{1,0:T(8,128)(2,1)S(1)} %join.1.refs_0_, bf16[16,3072]{1,0:T(8,128)(2,1)S(1)} %collective-permute-done.11.refs_1_, bf16[16,3072]{1,0:T(8,128)(2,1)S(1)} %collective-permute-done.12.refs_2_, ...), custom_call_target="tpu_custom_call" | custom-call | flops 301989888 | bytes 393216 | tf_op jit(solution)/shard_map/output_part/pallas_call | solution.py:23
  63.4 1.2 %collective-permute-start.18 = (s16[32,896]{1,0:T(8,128)(2,1)S(1)}, s16[32,896]{1,0:T(8,128)(2,1)S(1)}, u32[]{:S(2)}, u32[]{:S(2)}) collective-permute-start(s16[32,896]{1,0:T(8,128)(2,1)S(1)} %get-tuple-element.54), channel_id=1, source_target_pairs={{0,1},{1,0},{2,3},{3,2},{4,5},{5,4},{6,7},{7,6},{8,9},{9,8},{10,11... | collective-permute-start | bytes 172040 | tf_op jit(solution)/shard_map/ppermute | solution.py:49
  64.6 1.7 %collective-permute-done.16.came_ref = s16[32,2176]{1,0:T(8,128)(2,1)S(1)} collective-permute-done((s16[32,2176]{1,0:T(8,128)(2,1)S(1)}, s16[32,2176]{1,0:T(8,128)(2,1)S(1)}, u32[]{:S(2)}, u32[]{:S(2)}) %collective-permute-start.16) | collective-permute-done | bytes 139296 | tf_op jit(solution)/shard_map/ppermute | solution.py:49
  66.9 0.8 %collective-permute-done.18.came_ref = s16[32,896]{1,0:T(8,128)(2,1)S(1)} collective-permute-done((s16[32,896]{1,0:T(8,128)(2,1)S(1)}, s16[32,896]{1,0:T(8,128)(2,1)S(1)}, u32[]{:S(2)}, u32[]{:S(2)}) %collective-permute-start.18) | collective-permute-done | bytes 57376 | tf_op jit(solution)/shard_map/ppermute | solution.py:49
  67.8 2.1 %collective-permute-start.19 = (s16[16,896]{1,0:T(8,128)(2,1)S(1)}, s16[16,896]{1,0:T(8,128)(2,1)S(1)}, u32[]{:S(2)}, u32[]{:S(2)}) collective-permute-start(s16[16,896]{1,0:T(8,128)(2,1)S(1)} %get-tuple-element.56), channel_id=1, source_target_pairs={{0,2},{1,3},{2,0},{3,1},{4,6},{5,7},{6,4},{7,5},{8,10},{9,11},{10,... | collective-permute-start | bytes 86024 | tf_op jit(solution)/shard_map/ppermute | solution.py:49
  69.9 2.1 %collective-permute-done.17.refs_2_ = s16[16,2176]{1,0:T(8,128)(2,1)S(1)} collective-permute-done((s16[16,2176]{1,0:T(8,128)(2,1)S(1)}, s16[16,2176]{1,0:T(8,128)(2,1)S(1)}, u32[]{:S(2)}, u32[]{:S(2)}) %collective-permute-start.17) | collective-permute-done | bytes 69664 | tf_op jit(solution)/shard_map/ppermute | solution.py:49
  72.7 0.8 %finish.3 = bf16[16,4608]{1,0:T(8,128)(2,1)} custom-call(bf16[16,1792]{1,0:T(8,128)(2,1)S(1)} %finish.2.refs_0_, f32[16,2048]{1,0:T(8,128)S(1)} %get-tuple-element.52.refs_1_, s16[16,2176]{1,0:T(8,128)(2,1)S(1)} %collective-permute-done.17.refs_2_, f32[16,768]{1,0:T(8,128)S(1)} %get-tuple-element.55.refs_3_, s16[16,896]{1,0:T(8,128)(2,1)S(1)} %collective-permute-done.19.refs_4_), custom_call_target="tpu_custom_call" | custom-call | bytes 589824 | tf_op jit(solution)/shard_map/finish/pallas_call | solution.py:23
  (48 shorter events, 4.4 us)
Async XLA Ops:
  1.3 7.3 %collective-permute-start.2 = (f32[2,64]{1,0:T(2,128)S(1)}, f32[2,64]{1,0:T(2,128)S(1)}, u32[]{:S(2)}, u32[]{:S(2)}) collective-permute-start(f32[2,64]{1,0:T(2,128)S(1)} %pad_maximum_fusion.refs_0_), channel_id=1, source_target_pairs={{0,12},{4,8},{8,4},{12,0},{1,13},{5,9},{9,5},{13,1},{2,14},{6,10},... | collective-permute-start | bytes 1544 | tf_op jit(solution)/shard_map/ppermute | solution.py:49
  3.8 4.8 %collective-permute-start.1 = (f32[2,64]{1,0:T(2,128)S(1)}, f32[2,64]{1,0:T(2,128)S(1)}, u32[]{:S(2)}, u32[]{:S(2)}) collective-permute-start(f32[2,64]{1,0:T(2,128)S(1)} %pad_maximum_fusion.refs_0_), channel_id=1, source_target_pairs={{0,8},{4,12},{8,0},{12,4},{1,9},{5,13},{9,1},{13,5},{2,10},{6,14},... | collective-permute-start | bytes 1544 | tf_op jit(solution)/shard_map/ppermute | solution.py:49
  4.4 4.2 %collective-permute-start = (f32[2,64]{1,0:T(2,128)S(1)}, f32[2,64]{1,0:T(2,128)S(1)}, u32[]{:S(2)}, u32[]{:S(2)}) collective-permute-start(f32[2,64]{1,0:T(2,128)S(1)} %pad_maximum_fusion.refs_0_), channel_id=1, source_target_pairs={{0,4},{4,0},{8,12},{12,8},{1,5},{5,1},{9,13},{13,9},{2,6},{6,2},{1... | collective-permute-start | bytes 1544 | tf_op jit(solution)/shard_map/ppermute | solution.py:49
  4.6 4.1 %copy-start = (bf16[64,4608]{1,0:T(8,128)(2,1)S(1)}, bf16[64,4608]{1,0:T(8,128)(2,1)}, u32[]{:S(2)}) copy-start(bf16[64,4608]{1,0:T(8,128)(2,1)} %refs_4_.5) | copy-start | bytes 1769476
  4.6 4.1 %copy-start.1 = (f32[4608]{0:T(1024)S(1)}, f32[4608]{0:T(1024)}, u32[]{:S(2)}) copy-start(f32[4608]{0:T(1024)} %refs_5_.1) | copy-start | bytes 55300
  16.9 2.0 %collective-permute-start.3 = (f32[32,3584]{1,0:T(8,128)S(1)}, f32[32,3584]{1,0:T(8,128)S(1)}, u32[]{:S(2)}, u32[]{:S(2)}) collective-permute-start(f32[32,3584]{1,0:T(8,128)S(1)} %get-tuple-element.34), channel_id=1, source_target_pairs={{0,4},{4,0},{8,12},{12,8},{1,5},{5,1},{9,13},{13,9},{2,6},{6,2},{1... | collective-permute-start | bytes 1376264 | tf_op jit(solution)/shard_map/ppermute | solution.py:49
  18.9 7.9 %collective-permute-start.4 = (f32[16,3584]{1,0:T(8,128)S(1)}, f32[16,3584]{1,0:T(8,128)S(1)}, u32[]{:S(2)}, u32[]{:S(2)}) collective-permute-start(f32[16,3584]{1,0:T(8,128)S(1)} %get-tuple-element.36), channel_id=1, source_target_pairs={{0,8},{4,12},{8,0},{12,4},{1,9},{5,13},{9,1},{13,5},{2,10},{6,14},... | collective-permute-start | bytes 688136 | tf_op jit(solution)/shard_map/ppermute | solution.py:49
  26.9 9.1 %copy-start.2 = (bf16[4,1024,512]{2,1,0:T(8,128)(2,1)S(1)}, bf16[4,1024,512]{2,1,0:T(8,128)(2,1)}, u32[]{:S(2)}) copy-start(bf16[4,1024,512]{2,1,0:T(8,128)(2,1)} %refs_4_.6) | copy-start | bytes 12582916
  26.9 9.1 %copy-start.3 = (s32[4]{0:T(128)S(1)}, s32[4]{0:T(128)}, u32[]{:S(2)}) copy-start(s32[4]{0:T(128)} %lengths_ref.1) | copy-start | bytes 52
  26.9 24.7 %slice-start = ((s8[28311552]{0:T(1024)(128)(4,1)}), s8[4194304]{0:T(1024)(128)(4,1)S(1)}, s32[]{:S(2)}) async-start(s8[28311552]{0:T(1024)(128)(4,1)} %bitcast.4), calls=%async_computation | async-start | bytes 8388608
  26.9 24.7 %slice-start.1 = ((s8[28311552]{0:T(1024)(128)(4,1)}), s8[4194304]{0:T(1024)(128)(4,1)S(1)}, s32[]{:S(2)}) async-start(s8[28311552]{0:T(1024)(128)(4,1)} %bitcast.4), calls=%async_computation.1 | async-start | bytes 8388608
  26.9 24.7 %slice-start.2 = ((s8[28311552]{0:T(1024)(128)(4,1)}), s8[4194304]{0:T(1024)(128)(4,1)S(1)}, s32[]{:S(2)}) async-start(s8[28311552]{0:T(1024)(128)(4,1)} %bitcast.4), calls=%async_computation.2 | async-start | bytes 8388608
  27.5 6.1 %collective-permute-start.5 = (bf16[4,4096]{1,0:T(4,128)(2,1)S(1)}, bf16[4,4096]{1,0:T(4,128)(2,1)S(1)}, u32[]{:S(2)}, u32[]{:S(2)}) collective-permute-start(bf16[4,4096]{1,0:T(4,128)(2,1)S(1)} %get-tuple-element.37), channel_id=1, source_target_pairs={{0,3},{1,2},{2,1},{3,0},{4,7},{5,6},{6,5},{7,4},{8,11},{9,10},{10,... | collective-permute-start | bytes 98312 | tf_op jit(solution)/shard_map/ppermute | solution.py:49
  31.2 4.8 %collective-permute-start.6 = (bf16[4,4096]{1,0:T(4,128)(2,1)S(1)}, bf16[4,4096]{1,0:T(4,128)(2,1)S(1)}, u32[]{:S(2)}, u32[]{:S(2)}) collective-permute-start(bf16[4,4096]{1,0:T(4,128)(2,1)S(1)} %get-tuple-element.38), channel_id=1, source_target_pairs={{0,2},{1,3},{2,0},{3,1},{4,6},{5,7},{6,4},{7,5},{8,10},{9,11},{10,... | collective-permute-start | bytes 98312 | tf_op jit(solution)/shard_map/ppermute | solution.py:49
  31.2 4.8 %collective-permute-start.7 = (bf16[4,4096]{1,0:T(4,128)(2,1)S(1)}, bf16[4,4096]{1,0:T(4,128)(2,1)S(1)}, u32[]{:S(2)}, u32[]{:S(2)}) collective-permute-start(bf16[4,4096]{1,0:T(4,128)(2,1)S(1)} %get-tuple-element.39), channel_id=1, source_target_pairs={{0,1},{1,0},{2,3},{3,2},{4,5},{5,4},{6,7},{7,6},{8,9},{9,8},{10,11... | collective-permute-start | bytes 98312 | tf_op jit(solution)/shard_map/ppermute | solution.py:49
  36.0 15.6 %slice-start.3 = ((s8[28311552]{0:T(1024)(128)(4,1)}), s8[4194304]{0:T(1024)(128)(4,1)S(1)}, s32[]{:S(2)}) async-start(s8[28311552]{0:T(1024)(128)(4,1)} %bitcast.4), calls=%async_computation.3 | async-start | bytes 8388608
  36.0 15.6 %slice-start.4 = ((s8[28311552]{0:T(1024)(128)(4,1)}), s8[4194304]{0:T(1024)(128)(4,1)S(1)}, s32[]{:S(2)}) async-start(s8[28311552]{0:T(1024)(128)(4,1)} %bitcast.4), calls=%async_computation.4 | async-start | bytes 8388608
  38.5 5.7 %collective-permute-start.8 = (bf16[4,3072]{1,0:T(4,128)(2,1)S(1)}, bf16[4,3072]{1,0:T(4,128)(2,1)S(1)}, u32[]{:S(2)}, u32[]{:S(2)}) collective-permute-start(bf16[4,3072]{1,0:T(4,128)(2,1)S(1)} %get-tuple-element.41), channel_id=1, source_target_pairs={{0,3},{1,2},{2,1},{3,0},{4,7},{5,6},{6,5},{7,4},{8,11},{9,10},{10,... | collective-permute-start | bytes 73736 | tf_op jit(solution)/shard_map/ppermute | solution.py:49
  40.0 4.7 %collective-permute-start.9 = (bf16[4,3072]{1,0:T(4,128)(2,1)S(1)}, bf16[4,3072]{1,0:T(4,128)(2,1)S(1)}, u32[]{:S(2)}, u32[]{:S(2)}) collective-permute-start(bf16[4,3072]{1,0:T(4,128)(2,1)S(1)} %get-tuple-element.42), channel_id=1, source_target_pairs={{0,2},{1,3},{2,0},{3,1},{4,6},{5,7},{6,4},{7,5},{8,10},{9,11},{10,... | collective-permute-start | bytes 73736 | tf_op jit(solution)/shard_map/ppermute | solution.py:49
  40.6 4.3 %collective-permute-start.10 = (bf16[4,3072]{1,0:T(4,128)(2,1)S(1)}, bf16[4,3072]{1,0:T(4,128)(2,1)S(1)}, u32[]{:S(2)}, u32[]{:S(2)}) collective-permute-start(bf16[4,3072]{1,0:T(4,128)(2,1)S(1)} %get-tuple-element.43), channel_id=1, source_target_pairs={{0,1},{1,0},{2,3},{3,2},{4,5},{5,4},{6,7},{7,6},{8,9},{9,8},{10,11... | collective-permute-start | bytes 73736 | tf_op jit(solution)/shard_map/ppermute | solution.py:49
  45.0 6.6 %slice-start.5 = ((s8[28311552]{0:T(1024)(128)(4,1)}), s8[4194304]{0:T(1024)(128)(4,1)S(1)}, s32[]{:S(2)}) async-start(s8[28311552]{0:T(1024)(128)(4,1)} %bitcast.4), calls=%async_computation.5 | async-start | bytes 8388608
  45.0 6.6 %slice-start.6 = ((s8[28311552]{0:T(1024)(128)(4,1)}), s8[3145728]{0:T(1024)(128)(4,1)S(1)}, s32[]{:S(2)}) async-start(s8[28311552]{0:T(1024)(128)(4,1)} %bitcast.4), calls=%async_computation.6 | async-start | bytes 6291456
  45.6 4.7 %collective-permute-start.12 = (bf16[16,3072]{1,0:T(8,128)(2,1)S(1)}, bf16[16,3072]{1,0:T(8,128)(2,1)S(1)}, u32[]{:S(2)}, u32[]{:S(2)}) collective-permute-start(bf16[16,3072]{1,0:T(8,128)(2,1)S(1)} %join.1.refs_0_), channel_id=1, source_target_pairs={{0,8},{4,12},{8,0},{12,4},{1,9},{5,13},{9,1},{13,5},{2,10},{6,14},... | collective-permute-start | bytes 294920 | tf_op jit(solution)/shard_map/ppermute | solution.py:49
  47.1 3.2 %collective-permute-start.11 = (bf16[16,3072]{1,0:T(8,128)(2,1)S(1)}, bf16[16,3072]{1,0:T(8,128)(2,1)S(1)}, u32[]{:S(2)}, u32[]{:S(2)}) collective-permute-start(bf16[16,3072]{1,0:T(8,128)(2,1)S(1)} %join.1.refs_0_), channel_id=1, source_target_pairs={{0,4},{4,0},{8,12},{12,8},{1,5},{5,1},{9,13},{13,9},{2,6},{6,2},{1... | collective-permute-start | bytes 294920 | tf_op jit(solution)/shard_map/ppermute | solution.py:49
  50.3 1.3 %collective-permute-start.13 = (bf16[16,3072]{1,0:T(8,128)(2,1)S(1)}, bf16[16,3072]{1,0:T(8,128)(2,1)S(1)}, u32[]{:S(2)}, u32[]{:S(2)}) collective-permute-start(bf16[16,3072]{1,0:T(8,128)(2,1)S(1)} %collective-permute-done.12.refs_2_), channel_id=1, source_target_pairs={{0,4},{4,0},{8,12},{12,8},{1,5},{5,1},{9,13},{13,9},{2,6},{6,2},{1... | collective-permute-start | bytes 294920 | tf_op jit(solution)/shard_map/ppermute | solution.py:49
  54.3 5.5 %collective-permute-start.14 = (s16[32,1920]{1,0:T(8,128)(2,1)S(1)}, s16[32,1920]{1,0:T(8,128)(2,1)S(1)}, u32[]{:S(2)}, u32[]{:S(2)}) collective-permute-start(s16[32,1920]{1,0:T(8,128)(2,1)S(1)} %get-tuple-element.46), channel_id=1, source_target_pairs={{0,1},{1,0},{2,3},{3,2},{4,5},{5,4},{6,7},{7,6},{8,9},{9,8},{10,11... | collective-permute-start | bytes 368648 | tf_op jit(solution)/shard_map/ppermute | solution.py:49
  59.1 7.2 %collective-permute-start.16 = (s16[32,2176]{1,0:T(8,128)(2,1)S(1)}, s16[32,2176]{1,0:T(8,128)(2,1)S(1)}, u32[]{:S(2)}, u32[]{:S(2)}) collective-permute-start(s16[32,2176]{1,0:T(8,128)(2,1)S(1)} %get-tuple-element.50), channel_id=1, source_target_pairs={{0,1},{1,0},{2,3},{3,2},{4,5},{5,4},{6,7},{7,6},{8,9},{9,8},{10,11... | collective-permute-start | bytes 417800 | tf_op jit(solution)/shard_map/ppermute | solution.py:49
  60.0 6.8 %collective-permute-start.15 = (s16[16,1920]{1,0:T(8,128)(2,1)S(1)}, s16[16,1920]{1,0:T(8,128)(2,1)S(1)}, u32[]{:S(2)}, u32[]{:S(2)}) collective-permute-start(s16[16,1920]{1,0:T(8,128)(2,1)S(1)} %get-tuple-element.49), channel_id=1, source_target_pairs={{0,2},{1,3},{2,0},{3,1},{4,6},{5,7},{6,4},{7,5},{8,10},{9,11},{10,... | collective-permute-start | bytes 184328 | tf_op jit(solution)/shard_map/ppermute | solution.py:49
  63.4 4.2 %collective-permute-start.18 = (s16[32,896]{1,0:T(8,128)(2,1)S(1)}, s16[32,896]{1,0:T(8,128)(2,1)S(1)}, u32[]{:S(2)}, u32[]{:S(2)}) collective-permute-start(s16[32,896]{1,0:T(8,128)(2,1)S(1)} %get-tuple-element.54), channel_id=1, source_target_pairs={{0,1},{1,0},{2,3},{3,2},{4,5},{5,4},{6,7},{7,6},{8,9},{9,8},{10,11... | collective-permute-start | bytes 172040 | tf_op jit(solution)/shard_map/ppermute | solution.py:49
  66.6 5.5 %collective-permute-start.17 = (s16[16,2176]{1,0:T(8,128)(2,1)S(1)}, s16[16,2176]{1,0:T(8,128)(2,1)S(1)}, u32[]{:S(2)}, u32[]{:S(2)}) collective-permute-start(s16[16,2176]{1,0:T(8,128)(2,1)S(1)} %get-tuple-element.53), channel_id=1, source_target_pairs={{0,2},{1,3},{2,0},{3,1},{4,6},{5,7},{6,4},{7,5},{8,10},{9,11},{10,... | collective-permute-start | bytes 208904 | tf_op jit(solution)/shard_map/ppermute | solution.py:49
  67.8 4.8 %collective-permute-start.19 = (s16[16,896]{1,0:T(8,128)(2,1)S(1)}, s16[16,896]{1,0:T(8,128)(2,1)S(1)}, u32[]{:S(2)}, u32[]{:S(2)}) collective-permute-start(s16[16,896]{1,0:T(8,128)(2,1)S(1)} %get-tuple-element.56), channel_id=1, source_target_pairs={{0,2},{1,3},{2,0},{3,1},{4,6},{5,7},{6,4},{7,5},{8,10},{9,11},{10,... | collective-permute-start | bytes 86024 | tf_op jit(solution)/shard_map/ppermute | solution.py:49

commit v8 on v7

--- a/solution.py
+++ b/solution.py
@@ -16,6 +16,7 @@
 TINY = 1e-37
 LANES = 128
 PAD = 8
+PIECES = 4
 BESIDE = 5 * 10**9
 
 
@@ -80,27 +81,43 @@
     return [sum(((k >> b) & 1) << (bits - 1 - b) for b in range(bits)) for k in range(count)]
 
 
-def fetch_kernel(w_ref, kv_ref, *refs):
-    share_ref, kv_share_ref, sems = refs[-3:]
-    fetches = [
-        pltpu.make_async_copy(w_ref.at[: share_ref.shape[0]], share_ref, sems.at[0]),
-        pltpu.make_async_copy(kv_ref, kv_share_ref, sems.at[1]),
-    ]
-    for fetch in fetches:
-        fetch.start()
-    for fetch in fetches:
-        fetch.wait()
-
-
-def fetch(w, kv, rows, after):
-    return call(
-        fetch_kernel,
-        [held((rows, w.shape[1]), w.dtype), held(kv.shape, kv.dtype)],
-        (in_hbm(w), in_hbm(kv), *after),
-        [ANY] * (2 + len(after)),
-        "fetch_query_weight",
-        scratch=[pltpu.SemaphoreType.DMA((2,))],
-        moved=2 * (rows * w.shape[1] + kv.size),
+def stats_kernel(me_ref, x_ref, w_ref, out_ref, share_ref, copied, sems):
+    rows, width = x_ref.shape
+    step = rows // PIECES
+    pieces = [pl.ds(p * step, step) for p in range(PIECES)]
+    copies = [pltpu.make_async_copy(x_ref.at[at], copied.at[at], sems.at[p]) for p, at in enumerate(pieces)]
+    for copy in copies:
+        copy.start()
+    fetch = pltpu.make_async_copy(w_ref.at[: share_ref.shape[0]], share_ref, sems.at[PIECES])
+    fetch.start()
+    totals, squares = [], []
+    for copy, at in zip(copies, pieces):
+        copy.wait()
+        total = jnp.zeros((step, LANES), jnp.float32)
+        square = jnp.zeros((step, LANES), jnp.float32)
+        for c in range(0, width, LANES):
+            part = copied[at, c : c + LANES].astype(jnp.float32)
+            total += part
+            square += part * part
+        totals.append(jnp.sum(total, axis=1, keepdims=True))
+        squares.append(jnp.sum(square, axis=1, keepdims=True))
+    row = lax.broadcasted_iota(jnp.int32, (rows, rows), 0)
+    column = lax.broadcasted_iota(jnp.int32, (rows, rows), 1)
+    for k, sums in enumerate((totals, squares)):
+        sums = jnp.where(row == column, jnp.concatenate(sums, axis=0), 0.0)
+        out_ref[k : k + 1, :] = jnp.sum(sums, axis=0, keepdims=True)
+    fetch.wait()
+
+
+def row_sums(me, x, w, share):
+    return call(
+        stats_kernel,
+        (jax.ShapeDtypeStruct((2, x.shape[0]), jnp.float32), held((share, w.shape[1]), w.dtype)),
+        (me, in_hbm(x), in_hbm(w)),
+        [SCALAR, ANY, ANY],
+        "row_sums",
+        scratch=[pltpu.VMEM(x.shape, x.dtype), pltpu.SemaphoreType.DMA((PIECES + 1,))],
+        moved=2 * share * w.shape[1],
     )
 
 
@@ -416,17 +433,15 @@
     rows, width = activations.shape
     queries = query_weight.shape[1]
     columns = out_weight.shape[1]
-    values = activations.astype(jnp.float32)
-    stats = jnp.stack([jnp.sum(values, axis=1), jnp.sum(values * values, axis=1)])
     step = row_block(width)
-    first_part, kv_part = fetch(query_weight, kv_weight, width // step // 3 * step, [stats, me])
+    stats, first_part = row_sums(me, activations, query_weight, width // step // 3 * step)
     kept, sent = project(
         me,
         sent_apart(stats, "wide"),
         activations,
         norm_gain,
         query_weight,
-        kv_part,
+        kv_weight,
         first_part,
         width * wide_count,
         wide_count,

time: 73.6 us -> 75.3 us (1.023)
  waiting for transfers between devices: 23.9 us -> 28.6 us
  starting transfers between devices: 23.3 us -> 21 us
  other arithmetic: 1.4 us -> 0.08 us
    ppermute x20, waiting for transfers between devices: 23.9 us -> 28.6 us  [swap(): return lax.ppermute(x, axis, [(i, i ^ distance) for i in range(count)])]
    ppermute x20, starting transfers between devices: 23.3 us -> 21 us  [swap(): return lax.ppermute(x, axis, [(i, i ^ distance) for i in range(count)])]
    reduce_sum x1 -> x0, other arithmetic: 1.31 us -> none  [local(): jnp.sum(values, axis=1)]
  transfers between devices with their start and end apart: 20 -> 20, of which waited for: 14 -> 16; matrix products, arithmetic and copies ran while one was open for 0% -> 0% of each run, Pallas kernels for 13% -> 7%
where the time goes in v8:
time: 75.3 us; the launch traced here: 75.2 us
  waiting for transfers between devices  28.6 us (38%)
  Pallas kernels  25.1 us (33%)
  starting transfers between devices  21 us (28%)
    ppermute x20, waiting for transfers between devices, swap(): return lax.ppermute(x, axis, [(i, i ^ distance) for i in range(count)])  28.6 us
    pallas_call x14, Pallas kernels, call(): pl.pallas_call(kernel, out_shape=outs, in_specs=specs, out_specs=jax.tree...  25.1 us
    ppermute x20, starting transfers between devices, swap(): return lax.ppermute(x, axis, [(i, i ^ distance) for i in range(count)])  21 us
  transfers between devices with their start and end apart: 20, of which 16 were waited for; matrix products, arithmetic and copies ran while one was open for 0% of the time, Pallas kernels for 7%

profile of v8, /device:TPU:0, one launch (start us, length us, event | category | flops | bytes accessed | tf_op | source)
XLA Modules:
  0.0 75.2 jit_solution(13579328542539485392)
XLA Ops:
  0.1 4.6 %row_sums.1 = (f32[2,64]{1,0:T(2,128)S(1)}, bf16[1536,3072]{1,0:T(8,128)(2,1)S(1)}) custom-call(s32[2]{0:T(128)S(1)} %pad_add_fusion.me_ref, bf16[64,4608]{1,0:T(8,128)(2,1)} %refs_4_.5, bf16[4608,3072]{1,0:T(8,128)(2,1)} %refs_6_.1), custom_call_target="tpu_custom_call" | custom-call | bytes 9437184 | tf_op jit(solution)/shard_map/row_sums/pallas_call | solution.py:24
  4.7 2.5 %collective-permute-start.2 = (f32[2,64]{1,0:T(2,128)S(1)}, f32[2,64]{1,0:T(2,128)S(1)}, u32[]{:S(2)}, u32[]{:S(2)}) collective-permute-start(f32[2,64]{1,0:T(2,128)S(1)} %get-tuple-element.31.refs_0_), channel_id=1, source_target_pairs={{0,12},{4,8},{8,4},{12,0},{1,13},{5,9},{9,5},{13,1},{2,14},{6,10},... | collective-permute-start | bytes 1544 | tf_op jit(solution)/shard_map/ppermute | solution.py:50
  7.1 0.6 collective-permute-start.1
  7.8 0.6 collective-permute-done.2.refs_3_
  8.4 2.3 %collective-permute-done.1.refs_2_ = f32[2,64]{1,0:T(2,128)S(1)} collective-permute-done((f32[2,64]{1,0:T(2,128)S(1)}, f32[2,64]{1,0:T(2,128)S(1)}, u32[]{:S(2)}, u32[]{:S(2)}) %collective-permute-start.1) | collective-permute-done | bytes 544 | tf_op jit(solution)/shard_map/ppermute | solution.py:50
  10.7 8.2 %project.1 = (f32[32,3584]{1,0:T(8,128)S(1)}, f32[32,3584]{1,0:T(8,128)S(1)}) custom-call(s32[2]{0:T(128)S(1)} %pad_add_fusion.me_ref, f32[2,64]{1,0:T(2,128)S(1)} %get-tuple-element.31.refs_0_, f32[2,64]{1,0:T(2,128)S(1)} %collective-permute-done.refs_1_, f32[2,64]{1,0:T(2,128)S(1)} %collective-permute-done.1.refs_2_, ...), custom_call_target="tpu_custom_call" | custom-call | flops 1811939328 | bytes 18874368 | tf_op jit(solution)/shard_map/project/pallas_call | solution.py:24
  19.0 1.8 %collective-permute-done.3.came_ref = f32[32,3584]{1,0:T(8,128)S(1)} collective-permute-done((f32[32,3584]{1,0:T(8,128)S(1)}, f32[32,3584]{1,0:T(8,128)S(1)}, u32[]{:S(2)}, u32[]{:S(2)}) %collective-permute-start.3) | collective-permute-done | bytes 458784 | tf_op jit(solution)/shard_map/ppermute | solution.py:50
  20.9 0.7 collective-permute-start.4
  21.6 7.0 %collective-permute-done.4.came_ref = f32[16,3584]{1,0:T(8,128)S(1)} collective-permute-done((f32[16,3584]{1,0:T(8,128)S(1)}, f32[16,3584]{1,0:T(8,128)S(1)}, u32[]{:S(2)}, u32[]{:S(2)}) %collective-permute-start.4) | collective-permute-done | bytes 229408 | tf_op jit(solution)/shard_map/ppermute | solution.py:50
  29.3 3.7 %collective-permute-start.5 = (bf16[4,4096]{1,0:T(4,128)(2,1)S(1)}, bf16[4,4096]{1,0:T(4,128)(2,1)S(1)}, u32[]{:S(2)}, u32[]{:S(2)}) collective-permute-start(bf16[4,4096]{1,0:T(4,128)(2,1)S(1)} %get-tuple-element.37), channel_id=1, source_target_pairs={{0,3},{1,2},{2,1},{3,0},{4,7},{5,6},{6,5},{7,4},{8,11},{9,10},{10,... | collective-permute-start | bytes 98312 | tf_op jit(solution)/shard_map/ppermute | solution.py:50
  32.9 0.8 %collective-permute-start.7 = (bf16[4,4096]{1,0:T(4,128)(2,1)S(1)}, bf16[4,4096]{1,0:T(4,128)(2,1)S(1)}, u32[]{:S(2)}, u32[]{:S(2)}) collective-permute-start(bf16[4,4096]{1,0:T(4,128)(2,1)S(1)} %get-tuple-element.39), channel_id=1, source_target_pairs={{0,1},{1,0},{2,3},{3,2},{4,5},{5,4},{6,7},{7,6},{8,9},{9,8},{10,11... | collective-permute-start | bytes 98312 | tf_op jit(solution)/shard_map/ppermute | solution.py:50
  33.7 1.5 %collective-permute-done.5.refs_0_ = bf16[4,4096]{1,0:T(4,128)(2,1)S(1)} collective-permute-done((bf16[4,4096]{1,0:T(4,128)(2,1)S(1)}, bf16[4,4096]{1,0:T(4,128)(2,1)S(1)}, u32[]{:S(2)}, u32[]{:S(2)}) %collective-permute-start.5) | collective-permute-done | bytes 32800 | tf_op jit(solution)/shard_map/ppermute | solution.py:50
  35.3 2.5 %collective-permute-done.6.refs_1_ = bf16[4,4096]{1,0:T(4,128)(2,1)S(1)} collective-permute-done((bf16[4,4096]{1,0:T(4,128)(2,1)S(1)}, bf16[4,4096]{1,0:T(4,128)(2,1)S(1)}, u32[]{:S(2)}, u32[]{:S(2)}) %collective-permute-start.6) | collective-permute-done | bytes 32800 | tf_op jit(solution)/shard_map/ppermute | solution.py:50
  37.8 2.4 %attend.1 = (bf16[4,3072]{1,0:T(4,128)(2,1)S(1)}, bf16[4,3072]{1,0:T(4,128)(2,1)S(1)}, bf16[4,3072]{1,0:T(4,128)(2,1)S(1)}, bf16[4,3072]{1,0:T(4,128)(2,1)S(1)}) custom-call(s32[4]{0:T(128)S(1)} %copy-done.4, bf16[4,4096]{1,0:T(4,128)(2,1)S(1)} %collective-permute-done.5.refs_0_, bf16[4,4096]{1,0:T(4,128)(2,1)S(1)} %collective-permute-done.6.refs_1_, ...), custom_call_target="tpu_custom_call" | custom-call | flops 5000000000 | tf_op jit(solution)/shard_map/attend/pallas_call | solution.py:24
  40.2 1.5 %collective-permute-start.8 = (bf16[4,3072]{1,0:T(4,128)(2,1)S(1)}, bf16[4,3072]{1,0:T(4,128)(2,1)S(1)}, u32[]{:S(2)}, u32[]{:S(2)}) collective-permute-start(bf16[4,3072]{1,0:T(4,128)(2,1)S(1)} %get-tuple-element.41), channel_id=1, source_target_pairs={{0,3},{1,2},{2,1},{3,0},{4,7},{5,6},{6,5},{7,4},{8,11},{9,10},{10,... | collective-permute-start | bytes 73736 | tf_op jit(solution)/shard_map/ppermute | solution.py:50
  41.8 0.6 collective-permute-start.9
  42.4 2.3 %collective-permute-start.10 = (bf16[4,3072]{1,0:T(4,128)(2,1)S(1)}, bf16[4,3072]{1,0:T(4,128)(2,1)S(1)}, u32[]{:S(2)}, u32[]{:S(2)}) collective-permute-start(bf16[4,3072]{1,0:T(4,128)(2,1)S(1)} %get-tuple-element.43), channel_id=1, source_target_pairs={{0,1},{1,0},{2,3},{3,2},{4,5},{5,4},{6,7},{7,6},{8,9},{9,8},{10,11... | collective-permute-start | bytes 73736 | tf_op jit(solution)/shard_map/ppermute | solution.py:50
  44.7 1.2 %collective-permute-done.8.refs_0_ = bf16[4,3072]{1,0:T(4,128)(2,1)S(1)} collective-permute-done((bf16[4,3072]{1,0:T(4,128)(2,1)S(1)}, bf16[4,3072]{1,0:T(4,128)(2,1)S(1)}, u32[]{:S(2)}, u32[]{:S(2)}) %collective-permute-start.8) | collective-permute-done | bytes 24608 | tf_op jit(solution)/shard_map/ppermute | solution.py:50
  47.4 0.7 collective-permute-start.12
  48.1 4.0 %collective-permute-done.12.refs_2_ = bf16[16,3072]{1,0:T(8,128)(2,1)S(1)} collective-permute-done((bf16[16,3072]{1,0:T(8,128)(2,1)S(1)}, bf16[16,3072]{1,0:T(8,128)(2,1)S(1)}, u32[]{:S(2)}, u32[]{:S(2)}) %collective-permute-start.12) | collective-permute-done | bytes 98336 | tf_op jit(solution)/shard_map/ppermute | solution.py:50
  52.0 1.3 %collective-permute-done.13.refs_3_ = bf16[16,3072]{1,0:T(8,128)(2,1)S(1)} collective-permute-done((bf16[16,3072]{1,0:T(8,128)(2,1)S(1)}, bf16[16,3072]{1,0:T(8,128)(2,1)S(1)}, u32[]{:S(2)}, u32[]{:S(2)}) %collective-permute-start.13) | collective-permute-done | bytes 98336 | tf_op jit(solution)/shard_map/ppermute | solution.py:50
  53.4 2.7 %output_part.3 = (f32[64,1792]{1,0:T(8,128)S(1)}, s16[32,1920]{1,0:T(8,128)(2,1)S(1)}) custom-call(s32[2]{0:T(128)S(1)} %pad_add_fusion.me_ref, bf16[16,3072]{1,0:T(8,128)(2,1)S(1)} %join.1.refs_0_, bf16[16,3072]{1,0:T(8,128)(2,1)S(1)} %collective-permute-done.11.refs_1_, bf16[16,3072]{1,0:T(8,128)(2,1)S(1)} %collective-permute-done.12.refs_2_, ...), custom_call_target="tpu_custom_call" | custom-call | flops 704643072 | bytes 393216 | tf_op jit(solution)/shard_map/output_part/pallas_call | solution.py:24
  56.1 1.8 %collective-permute-start.14 = (s16[32,1920]{1,0:T(8,128)(2,1)S(1)}, s16[32,1920]{1,0:T(8,128)(2,1)S(1)}, u32[]{:S(2)}, u32[]{:S(2)}) collective-permute-start(s16[32,1920]{1,0:T(8,128)(2,1)S(1)} %get-tuple-element.46), channel_id=1, source_target_pairs={{0,1},{1,0},{2,3},{3,2},{4,5},{5,4},{6,7},{7,6},{8,9},{9,8},{10,11... | collective-permute-start | bytes 368648 | tf_op jit(solution)/shard_map/ppermute | solution.py:50
  57.9 2.9 %output_part.4 = (f32[64,2048]{1,0:T(8,128)S(1)}, s16[32,2176]{1,0:T(8,128)(2,1)S(1)}) custom-call(s32[2]{0:T(128)S(1)} %pad_add_fusion.me_ref, bf16[16,3072]{1,0:T(8,128)(2,1)S(1)} %join.1.refs_0_, bf16[16,3072]{1,0:T(8,128)(2,1)S(1)} %collective-permute-done.11.refs_1_, bf16[16,3072]{1,0:T(8,128)(2,1)S(1)} %collective-permute-done.12.refs_2_, ...), custom_call_target="tpu_custom_call" | custom-call | flops 805306368 | bytes 393216 | tf_op jit(solution)/shard_map/output_part/pallas_call | solution.py:24
  61.8 1.8 %collective-permute-start.15 = (s16[16,1920]{1,0:T(8,128)(2,1)S(1)}, s16[16,1920]{1,0:T(8,128)(2,1)S(1)}, u32[]{:S(2)}, u32[]{:S(2)}) collective-permute-start(s16[16,1920]{1,0:T(8,128)(2,1)S(1)} %get-tuple-element.49), channel_id=1, source_target_pairs={{0,2},{1,3},{2,0},{3,1},{4,6},{5,7},{6,4},{7,5},{8,10},{9,11},{10,... | collective-permute-start | bytes 184328 | tf_op jit(solution)/shard_map/ppermute | solution.py:50
  63.6 1.6 %output_part.5 = (f32[64,768]{1,0:T(8,128)S(1)}, s16[32,896]{1,0:T(8,128)(2,1)S(1)}) custom-call(s32[2]{0:T(128)S(1)} %pad_add_fusion.me_ref, bf16[16,3072]{1,0:T(8,128)(2,1)S(1)} %join.1.refs_0_, bf16[16,3072]{1,0:T(8,128)(2,1)S(1)} %collective-permute-done.11.refs_1_, bf16[16,3072]{1,0:T(8,128)(2,1)S(1)} %collective-permute-done.12.refs_2_, ...), custom_call_target="tpu_custom_call" | custom-call | flops 301989888 | bytes 393216 | tf_op jit(solution)/shard_map/output_part/pallas_call | solution.py:24
  65.1 1.2 %collective-permute-start.18 = (s16[32,896]{1,0:T(8,128)(2,1)S(1)}, s16[32,896]{1,0:T(8,128)(2,1)S(1)}, u32[]{:S(2)}, u32[]{:S(2)}) collective-permute-start(s16[32,896]{1,0:T(8,128)(2,1)S(1)} %get-tuple-element.54), channel_id=1, source_target_pairs={{0,1},{1,0},{2,3},{3,2},{4,5},{5,4},{6,7},{7,6},{8,9},{9,8},{10,11... | collective-permute-start | bytes 172040 | tf_op jit(solution)/shard_map/ppermute | solution.py:50
  66.4 1.7 %collective-permute-done.16.came_ref = s16[32,2176]{1,0:T(8,128)(2,1)S(1)} collective-permute-done((s16[32,2176]{1,0:T(8,128)(2,1)S(1)}, s16[32,2176]{1,0:T(8,128)(2,1)S(1)}, u32[]{:S(2)}, u32[]{:S(2)}) %collective-permute-start.16) | collective-permute-done | bytes 139296 | tf_op jit(solution)/shard_map/ppermute | solution.py:50
  68.6 0.8 %collective-permute-done.18.came_ref = s16[32,896]{1,0:T(8,128)(2,1)S(1)} collective-permute-done((s16[32,896]{1,0:T(8,128)(2,1)S(1)}, s16[32,896]{1,0:T(8,128)(2,1)S(1)}, u32[]{:S(2)}, u32[]{:S(2)}) %collective-permute-start.18) | collective-permute-done | bytes 57376 | tf_op jit(solution)/shard_map/ppermute | solution.py:50
  69.6 2.1 %collective-permute-start.19 = (s16[16,896]{1,0:T(8,128)(2,1)S(1)}, s16[16,896]{1,0:T(8,128)(2,1)S(1)}, u32[]{:S(2)}, u32[]{:S(2)}) collective-permute-start(s16[16,896]{1,0:T(8,128)(2,1)S(1)} %get-tuple-element.56), channel_id=1, source_target_pairs={{0,2},{1,3},{2,0},{3,1},{4,6},{5,7},{6,4},{7,5},{8,10},{9,11},{10,... | collective-permute-start | bytes 86024 | tf_op jit(solution)/shard_map/ppermute | solution.py:50
  71.7 2.1 %collective-permute-done.17.refs_2_ = s16[16,2176]{1,0:T(8,128)(2,1)S(1)} collective-permute-done((s16[16,2176]{1,0:T(8,128)(2,1)S(1)}, s16[16,2176]{1,0:T(8,128)(2,1)S(1)}, u32[]{:S(2)}, u32[]{:S(2)}) %collective-permute-start.17) | collective-permute-done | bytes 69664 | tf_op jit(solution)/shard_map/ppermute | solution.py:50
  74.4 0.8 %finish.3 = bf16[16,4608]{1,0:T(8,128)(2,1)} custom-call(bf16[16,1792]{1,0:T(8,128)(2,1)S(1)} %finish.2.refs_0_, f32[16,2048]{1,0:T(8,128)S(1)} %get-tuple-element.52.refs_1_, s16[16,2176]{1,0:T(8,128)(2,1)S(1)} %collective-permute-done.17.refs_2_, f32[16,768]{1,0:T(8,128)S(1)} %get-tuple-element.55.refs_3_, s16[16,896]{1,0:T(8,128)(2,1)S(1)} %collective-permute-done.19.refs_4_), custom_call_target="tpu_custom_call" | custom-call | bytes 589824 | tf_op jit(solution)/shard_map/finish/pallas_call | solution.py:24
  (48 shorter events, 4.5 us)
Async XLA Ops:
  0.1 10.6 %copy-start = (bf16[64,4608]{1,0:T(8,128)(2,1)S(1)}, bf16[64,4608]{1,0:T(8,128)(2,1)}, u32[]{:S(2)}) copy-start(bf16[64,4608]{1,0:T(8,128)(2,1)} %refs_4_.5) | copy-start | bytes 1769476
  0.1 10.6 %copy-start.1 = (bf16[1152,512]{1,0:T(8,128)(2,1)S(1)}, bf16[1152,512]{1,0:T(8,128)(2,1)}, u32[]{:S(2)}) copy-start(bf16[1152,512]{1,0:T(8,128)(2,1)} %refs_7_.1) | copy-start | bytes 3538948
  0.1 10.7 %copy-start.2 = (f32[4608]{0:T(1024)S(1)}, f32[4608]{0:T(1024)}, u32[]{:S(2)}) copy-start(f32[4608]{0:T(1024)} %refs_5_.1) | copy-start | bytes 55300
  4.7 3.8 %collective-permute-start.2 = (f32[2,64]{1,0:T(2,128)S(1)}, f32[2,64]{1,0:T(2,128)S(1)}, u32[]{:S(2)}, u32[]{:S(2)}) collective-permute-start(f32[2,64]{1,0:T(2,128)S(1)} %get-tuple-element.31.refs_0_), channel_id=1, source_target_pairs={{0,12},{4,8},{8,4},{12,0},{1,13},{5,9},{9,5},{13,1},{2,14},{6,10},... | collective-permute-start | bytes 1544 | tf_op jit(solution)/shard_map/ppermute | solution.py:50
  7.1 3.6 %collective-permute-start.1 = (f32[2,64]{1,0:T(2,128)S(1)}, f32[2,64]{1,0:T(2,128)S(1)}, u32[]{:S(2)}, u32[]{:S(2)}) collective-permute-start(f32[2,64]{1,0:T(2,128)S(1)} %get-tuple-element.31.refs_0_), channel_id=1, source_target_pairs={{0,8},{4,12},{8,0},{12,4},{1,9},{5,13},{9,1},{13,5},{2,10},{6,14},... | collective-permute-start | bytes 1544 | tf_op jit(solution)/shard_map/ppermute | solution.py:50
  7.8 2.9 %collective-permute-start = (f32[2,64]{1,0:T(2,128)S(1)}, f32[2,64]{1,0:T(2,128)S(1)}, u32[]{:S(2)}, u32[]{:S(2)}) collective-permute-start(f32[2,64]{1,0:T(2,128)S(1)} %get-tuple-element.31.refs_0_), channel_id=1, source_target_pairs={{0,4},{4,0},{8,12},{12,8},{1,5},{5,1},{9,13},{13,9},{2,6},{6,2},{1... | collective-permute-start | bytes 1544 | tf_op jit(solution)/shard_map/ppermute | solution.py:50
  19.0 1.9 %collective-permute-start.3 = (f32[32,3584]{1,0:T(8,128)S(1)}, f32[32,3584]{1,0:T(8,128)S(1)}, u32[]{:S(2)}, u32[]{:S(2)}) collective-permute-start(f32[32,3584]{1,0:T(8,128)S(1)} %get-tuple-element.34), channel_id=1, source_target_pairs={{0,4},{4,0},{8,12},{12,8},{1,5},{5,1},{9,13},{13,9},{2,6},{6,2},{1... | collective-permute-start | bytes 1376264 | tf_op jit(solution)/shard_map/ppermute | solution.py:50
  20.9 16.8 %copy-start.3 = (bf16[4,1024,512]{2,1,0:T(8,128)(2,1)S(1)}, bf16[4,1024,512]{2,1,0:T(8,128)(2,1)}, u32[]{:S(2)}) copy-start(bf16[4,1024,512]{2,1,0:T(8,128)(2,1)} %refs_4_.6) | copy-start | bytes 12582916
  20.9 16.8 %copy-start.4 = (s32[4]{0:T(128)S(1)}, s32[4]{0:T(128)}, u32[]{:S(2)}) copy-start(s32[4]{0:T(128)} %lengths_ref.1) | copy-start | bytes 52
  20.9 7.7 %collective-permute-start.4 = (f32[16,3584]{1,0:T(8,128)S(1)}, f32[16,3584]{1,0:T(8,128)S(1)}, u32[]{:S(2)}, u32[]{:S(2)}) collective-permute-start(f32[16,3584]{1,0:T(8,128)S(1)} %get-tuple-element.36), channel_id=1, source_target_pairs={{0,8},{4,12},{8,0},{12,4},{1,9},{5,13},{9,1},{13,5},{2,10},{6,14},... | collective-permute-start | bytes 688136 | tf_op jit(solution)/shard_map/ppermute | solution.py:50
  28.6 24.7 %slice-start = ((s8[28311552]{0:T(1024)(128)(4,1)}), s8[4194304]{0:T(1024)(128)(4,1)S(1)}, s32[]{:S(2)}) async-start(s8[28311552]{0:T(1024)(128)(4,1)} %bitcast.2), calls=%async_computation | async-start | bytes 8388608
  28.7 24.7 %slice-start.1 = ((s8[28311552]{0:T(1024)(128)(4,1)}), s8[4194304]{0:T(1024)(128)(4,1)S(1)}, s32[]{:S(2)}) async-start(s8[28311552]{0:T(1024)(128)(4,1)} %bitcast.2), calls=%async_computation.1 | async-start | bytes 8388608
  28.7 24.7 %slice-start.2 = ((s8[28311552]{0:T(1024)(128)(4,1)}), s8[4194304]{0:T(1024)(128)(4,1)S(1)}, s32[]{:S(2)}) async-start(s8[28311552]{0:T(1024)(128)(4,1)} %bitcast.2), calls=%async_computation.2 | async-start | bytes 8388608
  29.3 6.0 %collective-permute-start.5 = (bf16[4,4096]{1,0:T(4,128)(2,1)S(1)}, bf16[4,4096]{1,0:T(4,128)(2,1)S(1)}, u32[]{:S(2)}, u32[]{:S(2)}) collective-permute-start(bf16[4,4096]{1,0:T(4,128)(2,1)S(1)} %get-tuple-element.37), channel_id=1, source_target_pairs={{0,3},{1,2},{2,1},{3,0},{4,7},{5,6},{6,5},{7,4},{8,11},{9,10},{10,... | collective-permute-start | bytes 98312 | tf_op jit(solution)/shard_map/ppermute | solution.py:50
  32.9 4.8 %collective-permute-start.6 = (bf16[4,4096]{1,0:T(4,128)(2,1)S(1)}, bf16[4,4096]{1,0:T(4,128)(2,1)S(1)}, u32[]{:S(2)}, u32[]{:S(2)}) collective-permute-start(bf16[4,4096]{1,0:T(4,128)(2,1)S(1)} %get-tuple-element.38), channel_id=1, source_target_pairs={{0,2},{1,3},{2,0},{3,1},{4,6},{5,7},{6,4},{7,5},{8,10},{9,11},{10,... | collective-permute-start | bytes 98312 | tf_op jit(solution)/shard_map/ppermute | solution.py:50
  32.9 4.8 %collective-permute-start.7 = (bf16[4,4096]{1,0:T(4,128)(2,1)S(1)}, bf16[4,4096]{1,0:T(4,128)(2,1)S(1)}, u32[]{:S(2)}, u32[]{:S(2)}) collective-permute-start(bf16[4,4096]{1,0:T(4,128)(2,1)S(1)} %get-tuple-element.39), channel_id=1, source_target_pairs={{0,1},{1,0},{2,3},{3,2},{4,5},{5,4},{6,7},{7,6},{8,9},{9,8},{10,11... | collective-permute-start | bytes 98312 | tf_op jit(solution)/shard_map/ppermute | solution.py:50
  37.8 15.6 %slice-start.3 = ((s8[28311552]{0:T(1024)(128)(4,1)}), s8[4194304]{0:T(1024)(128)(4,1)S(1)}, s32[]{:S(2)}) async-start(s8[28311552]{0:T(1024)(128)(4,1)} %bitcast.2), calls=%async_computation.3 | async-start | bytes 8388608
  37.8 15.6 %slice-start.4 = ((s8[28311552]{0:T(1024)(128)(4,1)}), s8[4194304]{0:T(1024)(128)(4,1)S(1)}, s32[]{:S(2)}) async-start(s8[28311552]{0:T(1024)(128)(4,1)} %bitcast.2), calls=%async_computation.4 | async-start | bytes 8388608
  40.2 5.7 %collective-permute-start.8 = (bf16[4,3072]{1,0:T(4,128)(2,1)S(1)}, bf16[4,3072]{1,0:T(4,128)(2,1)S(1)}, u32[]{:S(2)}, u32[]{:S(2)}) collective-permute-start(bf16[4,3072]{1,0:T(4,128)(2,1)S(1)} %get-tuple-element.41), channel_id=1, source_target_pairs={{0,3},{1,2},{2,1},{3,0},{4,7},{5,6},{6,5},{7,4},{8,11},{9,10},{10,... | collective-permute-start | bytes 73736 | tf_op jit(solution)/shard_map/ppermute | solution.py:50
  41.8 4.7 %collective-permute-start.9 = (bf16[4,3072]{1,0:T(4,128)(2,1)S(1)}, bf16[4,3072]{1,0:T(4,128)(2,1)S(1)}, u32[]{:S(2)}, u32[]{:S(2)}) collective-permute-start(bf16[4,3072]{1,0:T(4,128)(2,1)S(1)} %get-tuple-element.42), channel_id=1, source_target_pairs={{0,2},{1,3},{2,0},{3,1},{4,6},{5,7},{6,4},{7,5},{8,10},{9,11},{10,... | collective-permute-start | bytes 73736 | tf_op jit(solution)/shard_map/ppermute | solution.py:50
  42.4 4.3 %collective-permute-start.10 = (bf16[4,3072]{1,0:T(4,128)(2,1)S(1)}, bf16[4,3072]{1,0:T(4,128)(2,1)S(1)}, u32[]{:S(2)}, u32[]{:S(2)}) collective-permute-start(bf16[4,3072]{1,0:T(4,128)(2,1)S(1)} %get-tuple-element.43), channel_id=1, source_target_pairs={{0,1},{1,0},{2,3},{3,2},{4,5},{5,4},{6,7},{7,6},{8,9},{9,8},{10,11... | collective-permute-start | bytes 73736 | tf_op jit(solution)/shard_map/ppermute | solution.py:50
  46.7 6.6 %slice-start.5 = ((s8[28311552]{0:T(1024)(128)(4,1)}), s8[4194304]{0:T(1024)(128)(4,1)S(1)}, s32[]{:S(2)}) async-start(s8[28311552]{0:T(1024)(128)(4,1)} %bitcast.2), calls=%async_computation.5 | async-start | bytes 8388608
  46.7 6.6 %slice-start.6 = ((s8[28311552]{0:T(1024)(128)(4,1)}), s8[3145728]{0:T(1024)(128)(4,1)S(1)}, s32[]{:S(2)}) async-start(s8[28311552]{0:T(1024)(128)(4,1)} %bitcast.2), calls=%async_computation.6 | async-start | bytes 6291456
  47.4 4.7 %collective-permute-start.12 = (bf16[16,3072]{1,0:T(8,128)(2,1)S(1)}, bf16[16,3072]{1,0:T(8,128)(2,1)S(1)}, u32[]{:S(2)}, u32[]{:S(2)}) collective-permute-start(bf16[16,3072]{1,0:T(8,128)(2,1)S(1)} %join.1.refs_0_), channel_id=1, source_target_pairs={{0,8},{4,12},{8,0},{12,4},{1,9},{5,13},{9,1},{13,5},{2,10},{6,14},... | collective-permute-start | bytes 294920 | tf_op jit(solution)/shard_map/ppermute | solution.py:50
  48.1 4.0 %collective-permute-start.11 = (bf16[16,3072]{1,0:T(8,128)(2,1)S(1)}, bf16[16,3072]{1,0:T(8,128)(2,1)S(1)}, u32[]{:S(2)}, u32[]{:S(2)}) collective-permute-start(bf16[16,3072]{1,0:T(8,128)(2,1)S(1)} %join.1.refs_0_), channel_id=1, source_target_pairs={{0,4},{4,0},{8,12},{12,8},{1,5},{5,1},{9,13},{13,9},{2,6},{6,2},{1... | collective-permute-start | bytes 294920 | tf_op jit(solution)/shard_map/ppermute | solution.py:50
  52.0 1.3 %collective-permute-start.13 = (bf16[16,3072]{1,0:T(8,128)(2,1)S(1)}, bf16[16,3072]{1,0:T(8,128)(2,1)S(1)}, u32[]{:S(2)}, u32[]{:S(2)}) collective-permute-start(bf16[16,3072]{1,0:T(8,128)(2,1)S(1)} %collective-permute-done.12.refs_2_), channel_id=1, source_target_pairs={{0,4},{4,0},{8,12},{12,8},{1,5},{5,1},{9,13},{13,9},{2,6},{6,2},{1... | collective-permute-start | bytes 294920 | tf_op jit(solution)/shard_map/ppermute | solution.py:50
  56.1 5.5 %collective-permute-start.14 = (s16[32,1920]{1,0:T(8,128)(2,1)S(1)}, s16[32,1920]{1,0:T(8,128)(2,1)S(1)}, u32[]{:S(2)}, u32[]{:S(2)}) collective-permute-start(s16[32,1920]{1,0:T(8,128)(2,1)S(1)} %get-tuple-element.46), channel_id=1, source_target_pairs={{0,1},{1,0},{2,3},{3,2},{4,5},{5,4},{6,7},{7,6},{8,9},{9,8},{10,11... | collective-permute-start | bytes 368648 | tf_op jit(solution)/shard_map/ppermute | solution.py:50
  60.9 7.2 %collective-permute-start.16 = (s16[32,2176]{1,0:T(8,128)(2,1)S(1)}, s16[32,2176]{1,0:T(8,128)(2,1)S(1)}, u32[]{:S(2)}, u32[]{:S(2)}) collective-permute-start(s16[32,2176]{1,0:T(8,128)(2,1)S(1)} %get-tuple-element.50), channel_id=1, source_target_pairs={{0,1},{1,0},{2,3},{3,2},{4,5},{5,4},{6,7},{7,6},{8,9},{9,8},{10,11... | collective-permute-start | bytes 417800 | tf_op jit(solution)/shard_map/ppermute | solution.py:50
  61.8 6.8 %collective-permute-start.15 = (s16[16,1920]{1,0:T(8,128)(2,1)S(1)}, s16[16,1920]{1,0:T(8,128)(2,1)S(1)}, u32[]{:S(2)}, u32[]{:S(2)}) collective-permute-start(s16[16,1920]{1,0:T(8,128)(2,1)S(1)} %get-tuple-element.49), channel_id=1, source_target_pairs={{0,2},{1,3},{2,0},{3,1},{4,6},{5,7},{6,4},{7,5},{8,10},{9,11},{10,... | collective-permute-start | bytes 184328 | tf_op jit(solution)/shard_map/ppermute | solution.py:50
  65.1 4.2 %collective-permute-start.18 = (s16[32,896]{1,0:T(8,128)(2,1)S(1)}, s16[32,896]{1,0:T(8,128)(2,1)S(1)}, u32[]{:S(2)}, u32[]{:S(2)}) collective-permute-start(s16[32,896]{1,0:T(8,128)(2,1)S(1)} %get-tuple-element.54), channel_id=1, source_target_pairs={{0,1},{1,0},{2,3},{3,2},{4,5},{5,4},{6,7},{7,6},{8,9},{9,8},{10,11... | collective-permute-start | bytes 172040 | tf_op jit(solution)/shard_map/ppermute | solution.py:50
  68.3 5.5 %collective-permute-start.17 = (s16[16,2176]{1,0:T(8,128)(2,1)S(1)}, s16[16,2176]{1,0:T(8,128)(2,1)S(1)}, u32[]{:S(2)}, u32[]{:S(2)}) collective-permute-start(s16[16,2176]{1,0:T(8,128)(2,1)S(1)} %get-tuple-element.53), channel_id=1, source_target_pairs={{0,2},{1,3},{2,0},{3,1},{4,6},{5,7},{6,4},{7,5},{8,10},{9,11},{10,... | collective-permute-start | bytes 208904 | tf_op jit(solution)/shard_map/ppermute | solution.py:50
  69.6 4.8 %collective-permute-start.19 = (s16[16,896]{1,0:T(8,128)(2,1)S(1)}, s16[16,896]{1,0:T(8,128)(2,1)S(1)}, u32[]{:S(2)}, u32[]{:S(2)}) collective-permute-start(s16[16,896]{1,0:T(8,128)(2,1)S(1)} %get-tuple-element.56), channel_id=1, source_target_pairs={{0,2},{1,3},{2,0},{3,1},{4,6},{5,7},{6,4},{7,5},{8,10},{9,11},{10,... | collective-permute-start | bytes 86024 | tf_op jit(solution)/shard_map/ppermute | solution.py:50

commit v9 on v7

--- a/solution.py
+++ b/solution.py
@@ -80,32 +80,34 @@
     return [sum(((k >> b) & 1) << (bits - 1 - b) for b in range(bits)) for k in range(count)]
 
 
-def fetch_kernel(w_ref, kv_ref, *refs):
-    share_ref, kv_share_ref, sems = refs[-3:]
-    fetches = [
-        pltpu.make_async_copy(w_ref.at[: share_ref.shape[0]], share_ref, sems.at[0]),
-        pltpu.make_async_copy(kv_ref, kv_share_ref, sems.at[1]),
-    ]
-    for fetch in fetches:
-        fetch.start()
-    for fetch in fetches:
-        fetch.wait()
-
-
-def fetch(w, kv, rows, after):
+def fetch_kernel(w_ref, *refs):
+    share_ref, sem = refs[-2:]
+    fetch = pltpu.make_async_copy(w_ref.at[: share_ref.shape[0]], share_ref, sem)
+    fetch.start()
+    fetch.wait()
+
+
+def fetch(w, rows, after):
     return call(
         fetch_kernel,
-        [held((rows, w.shape[1]), w.dtype), held(kv.shape, kv.dtype)],
-        (in_hbm(w), in_hbm(kv), *after),
-        [ANY] * (2 + len(after)),
+        held((rows, w.shape[1]), w.dtype),
+        (in_hbm(w), *after),
+        [ANY] * (1 + len(after)),
         "fetch_query_weight",
-        scratch=[pltpu.SemaphoreType.DMA((2,))],
-        moved=2 * (rows * w.shape[1] + kv.size),
-    )
-
-
-def row_block(rows):
-    return LANES * max(1, rows // LANES // 6)
+        scratch=[pltpu.SemaphoreType.DMA],
+        moved=2 * rows * w.shape[1],
+    )
+
+
+def row_blocks(rows):
+    tiles = rows // LANES
+    step = max(1, tiles // 6)
+    blocks = [step]
+    while tiles - sum(blocks) > step:
+        blocks.append(step)
+    last = tiles - sum(blocks)
+    blocks += [last - last // 3, last // 3] if last > 2 else [last]
+    return [LANES * n for n in blocks]
 
 
 def project_kernel(many, width_all, count, narrow_count, me_ref, *refs):
@@ -115,11 +117,11 @@
     half = rows // 2
     block = rows // count
     sub_width = width // narrow_count
-    done = first_ref.shape[0]
-    step = blocks[0].shape[0]
+    sizes = [ref.shape[0] for ref in (first_ref, *blocks)]
+    starts = [sum(sizes[:g]) for g in range(len(sizes))]
     fetches = [
-        pltpu.make_async_copy(w_ref.at[done + g * step : done + (g + 1) * step], ref, sems.at[g])
-        for g, ref in enumerate(blocks)
+        pltpu.make_async_copy(w_ref.at[start : start + size], ref, sems.at[g])
+        for g, (start, size, ref) in enumerate(zip(starts[1:], sizes[1:], blocks))
     ]
     ahead = 3
     for fetch in fetches[:ahead]:
@@ -169,14 +171,13 @@
         fetch.wait()
         if g + ahead < len(fetches):
             fetches[g + ahead].start()
-        products(blocks[g], done + g * step)
+        products(blocks[g], starts[g + 1])
 
 
 def project(me, stats, x, gain, w, kv, first, width_all, count, narrow_count):
     rows, width = x.shape
     queries = w.shape[1]
-    step = row_block(width)
-    blocks = (width - first.shape[0]) // step
+    blocks = row_blocks(width)[1:]
     half = jax.ShapeDtypeStruct((rows // 2, queries + kv.shape[1]), jnp.float32)
     return call(
         functools.partial(project_kernel, len(stats), width_all, count, narrow_count),
@@ -187,12 +188,12 @@
         scratch=[
             pltpu.VMEM((rows, width), jnp.bfloat16),
             pltpu.VMEM((rows, width // narrow_count), jnp.bfloat16),
-            *[pltpu.VMEM((step, queries), jnp.bfloat16)] * blocks,
-            pltpu.SemaphoreType.DMA((blocks,)),
+            *[pltpu.VMEM((n, queries), jnp.bfloat16) for n in blocks],
+            pltpu.SemaphoreType.DMA((len(blocks),)),
         ],
-        limit=32,
+        limit=36,
         flops=2 * rows * width * queries,
-        moved=2 * blocks * step * queries,
+        moved=2 * sum(blocks) * queries,
     )
 
 
@@ -418,15 +419,14 @@
     columns = out_weight.shape[1]
     values = activations.astype(jnp.float32)
     stats = jnp.stack([jnp.sum(values, axis=1), jnp.sum(values * values, axis=1)])
-    step = row_block(width)
-    first_part, kv_part = fetch(query_weight, kv_weight, width // step // 3 * step, [stats, me])
+    first_part = fetch(query_weight, row_blocks(width)[0], [stats, me])
     kept, sent = project(
         me,
         sent_apart(stats, "wide"),
         activations,
         norm_gain,
         query_weight,
-        kv_part,
+        kv_weight,
         first_part,
         width * wide_count,
         wide_count,

time: 73.6 us -> 73.3 us (level)
  transfers between devices with their start and end apart: 20 -> 20, of which waited for: 14 -> 15; matrix products, arithmetic and copies ran while one was open for 0% -> 0% of each run, Pallas kernels for 13% -> 10%
where the time goes in v9:
time: 73.3 us; the launch traced here: 73.1 us
  waiting for transfers between devices  24.2 us (33%)
  Pallas kernels  24 us (33%)
  starting transfers between devices  23.3 us (32%)
  other arithmetic  1.4 us (2%)
    ppermute x20, waiting for transfers between devices, swap(): return lax.ppermute(x, axis, [(i, i ^ distance) for i in range(count)])  24.2 us
    pallas_call x14, Pallas kernels, call(): pl.pallas_call(kernel, out_shape=outs, in_specs=specs, out_specs=jax.tree...  24 us
    ppermute x20, starting transfers between devices, swap(): return lax.ppermute(x, axis, [(i, i ^ distance) for i in range(count)])  23.3 us
  transfers between devices with their start and end apart: 20, of which 15 were waited for; matrix products, arithmetic and copies ran while one was open for 0% of the time, Pallas kernels for 10%

profile of v9, /device:TPU:0, one launch (start us, length us, event | category | flops | bytes accessed | tf_op | source)
XLA Modules:
  0.0 73.1 jit_solution(6824131282256952371)
XLA Ops:
  0.0 1.3 %convert_reduce_fusion = (f32[64]{0:T(128)S(1)}, f32[64]{0:T(128)S(1)}) fusion(bf16[64,4608]{1,0:T(8,128)(2,1)} %refs_4_.5), kind=kLoop, calls=%fused_computation.1 | loop fusion | flops 1179520 | bytes 590336 | tf_op jit(solution)/shard_map/reduce_sum | solution.py:421
  1.3 2.5 %collective-permute-start.2 = (f32[2,64]{1,0:T(2,128)S(1)}, f32[2,64]{1,0:T(2,128)S(1)}, u32[]{:S(2)}, u32[]{:S(2)}) collective-permute-start(f32[2,64]{1,0:T(2,128)S(1)} %pad_maximum_fusion.refs_0_), channel_id=1, source_target_pairs={{0,12},{4,8},{8,4},{12,0},{1,13},{5,9},{9,5},{13,1},{2,14},{6,10},... | collective-permute-start | bytes 1544 | tf_op jit(solution)/shard_map/ppermute | solution.py:49
  3.8 0.6 collective-permute-start.1
  4.6 2.5 %fetch_query_weight.1.refs_8_ = bf16[768,3072]{1,0:T(8,128)(2,1)S(1)} custom-call(bf16[4608,3072]{1,0:T(8,128)(2,1)} %refs_6_.1, f32[2,64]{1,0:T(2,128)S(1)} %pad_maximum_fusion.refs_0_, s32[2]{0:T(128)S(1)} %pad_add_fusion.refs_1_.me_ref), custom_call_target="tpu_custom_call" | custom-call | bytes 4718592 | tf_op jit(solution)/shard_map/fetch_query_weight/pallas_call | solution.py:23
  7.4 9.2 %project.1 = (f32[32,3584]{1,0:T(8,128)S(1)}, f32[32,3584]{1,0:T(8,128)S(1)}) custom-call(s32[2]{0:T(128)S(1)} %pad_add_fusion.refs_1_.me_ref, f32[2,64]{1,0:T(2,128)S(1)} %pad_maximum_fusion.refs_0_, f32[2,64]{1,0:T(2,128)S(1)} %collective-permute-done.refs_1_, f32[2,64]{1,0:T(2,128)S(1)} %collective-permute-done.1.refs_2_, ...), custom_call_target="tpu_custom_call" | custom-call | flops 1811939328 | bytes 23592960 | tf_op jit(solution)/shard_map/project/pallas_call | solution.py:23
  17.2 1.4 %collective-permute-done.3.came_ref = f32[32,3584]{1,0:T(8,128)S(1)} collective-permute-done((f32[32,3584]{1,0:T(8,128)S(1)}, f32[32,3584]{1,0:T(8,128)S(1)}, u32[]{:S(2)}, u32[]{:S(2)}) %collective-permute-start.3) | collective-permute-done | bytes 458784 | tf_op jit(solution)/shard_map/ppermute | solution.py:49
  18.7 1.7 %collective-permute-start.4 = (f32[16,3584]{1,0:T(8,128)S(1)}, f32[16,3584]{1,0:T(8,128)S(1)}, u32[]{:S(2)}, u32[]{:S(2)}) collective-permute-start(f32[16,3584]{1,0:T(8,128)S(1)} %get-tuple-element.32), channel_id=1, source_target_pairs={{0,8},{4,12},{8,0},{12,4},{1,9},{5,13},{9,1},{13,5},{2,10},{6,14},... | collective-permute-start | bytes 688136 | tf_op jit(solution)/shard_map/ppermute | solution.py:49
  20.4 6.2 %collective-permute-done.4.came_ref = f32[16,3584]{1,0:T(8,128)S(1)} collective-permute-done((f32[16,3584]{1,0:T(8,128)S(1)}, f32[16,3584]{1,0:T(8,128)S(1)}, u32[]{:S(2)}, u32[]{:S(2)}) %collective-permute-start.4) | collective-permute-done | bytes 229408 | tf_op jit(solution)/shard_map/ppermute | solution.py:49
  26.6 0.6 split.1
  27.2 3.7 %collective-permute-start.5 = (bf16[4,4096]{1,0:T(4,128)(2,1)S(1)}, bf16[4,4096]{1,0:T(4,128)(2,1)S(1)}, u32[]{:S(2)}, u32[]{:S(2)}) collective-permute-start(bf16[4,4096]{1,0:T(4,128)(2,1)S(1)} %get-tuple-element.33), channel_id=1, source_target_pairs={{0,3},{1,2},{2,1},{3,0},{4,7},{5,6},{6,5},{7,4},{8,11},{9,10},{10,... | collective-permute-start | bytes 98312 | tf_op jit(solution)/shard_map/ppermute | solution.py:49
  30.9 0.8 %collective-permute-start.7 = (bf16[4,4096]{1,0:T(4,128)(2,1)S(1)}, bf16[4,4096]{1,0:T(4,128)(2,1)S(1)}, u32[]{:S(2)}, u32[]{:S(2)}) collective-permute-start(bf16[4,4096]{1,0:T(4,128)(2,1)S(1)} %get-tuple-element.35), channel_id=1, source_target_pairs={{0,1},{1,0},{2,3},{3,2},{4,5},{5,4},{6,7},{7,6},{8,9},{9,8},{10,11... | collective-permute-start | bytes 98312 | tf_op jit(solution)/shard_map/ppermute | solution.py:49
  31.7 1.7 %collective-permute-done.5.refs_0_ = bf16[4,4096]{1,0:T(4,128)(2,1)S(1)} collective-permute-done((bf16[4,4096]{1,0:T(4,128)(2,1)S(1)}, bf16[4,4096]{1,0:T(4,128)(2,1)S(1)}, u32[]{:S(2)}, u32[]{:S(2)}) %collective-permute-start.5) | collective-permute-done | bytes 32800 | tf_op jit(solution)/shard_map/ppermute | solution.py:49
  33.4 2.4 %collective-permute-done.6.refs_1_ = bf16[4,4096]{1,0:T(4,128)(2,1)S(1)} collective-permute-done((bf16[4,4096]{1,0:T(4,128)(2,1)S(1)}, bf16[4,4096]{1,0:T(4,128)(2,1)S(1)}, u32[]{:S(2)}, u32[]{:S(2)}) %collective-permute-start.6) | collective-permute-done | bytes 32800 | tf_op jit(solution)/shard_map/ppermute | solution.py:49
  35.8 2.4 %attend.1 = (bf16[4,3072]{1,0:T(4,128)(2,1)S(1)}, bf16[4,3072]{1,0:T(4,128)(2,1)S(1)}, bf16[4,3072]{1,0:T(4,128)(2,1)S(1)}, bf16[4,3072]{1,0:T(4,128)(2,1)S(1)}) custom-call(s32[4]{0:T(128)S(1)} %copy-done.4, bf16[4,4096]{1,0:T(4,128)(2,1)S(1)} %collective-permute-done.5.refs_0_, bf16[4,4096]{1,0:T(4,128)(2,1)S(1)} %collective-permute-done.6.refs_1_, ...), custom_call_target="tpu_custom_call" | custom-call | flops 5000000000 | tf_op jit(solution)/shard_map/attend/pallas_call | solution.py:23
  38.2 1.5 %collective-permute-start.8 = (bf16[4,3072]{1,0:T(4,128)(2,1)S(1)}, bf16[4,3072]{1,0:T(4,128)(2,1)S(1)}, u32[]{:S(2)}, u32[]{:S(2)}) collective-permute-start(bf16[4,3072]{1,0:T(4,128)(2,1)S(1)} %get-tuple-element.37), channel_id=1, source_target_pairs={{0,3},{1,2},{2,1},{3,0},{4,7},{5,6},{6,5},{7,4},{8,11},{9,10},{10,... | collective-permute-start | bytes 73736 | tf_op jit(solution)/shard_map/ppermute | solution.py:49
  39.7 0.6 collective-permute-start.9
  40.4 2.3 %collective-permute-start.10 = (bf16[4,3072]{1,0:T(4,128)(2,1)S(1)}, bf16[4,3072]{1,0:T(4,128)(2,1)S(1)}, u32[]{:S(2)}, u32[]{:S(2)}) collective-permute-start(bf16[4,3072]{1,0:T(4,128)(2,1)S(1)} %get-tuple-element.39), channel_id=1, source_target_pairs={{0,1},{1,0},{2,3},{3,2},{4,5},{5,4},{6,7},{7,6},{8,9},{9,8},{10,11... | collective-permute-start | bytes 73736 | tf_op jit(solution)/shard_map/ppermute | solution.py:49
  42.7 1.2 %collective-permute-done.8.refs_0_ = bf16[4,3072]{1,0:T(4,128)(2,1)S(1)} collective-permute-done((bf16[4,3072]{1,0:T(4,128)(2,1)S(1)}, bf16[4,3072]{1,0:T(4,128)(2,1)S(1)}, u32[]{:S(2)}, u32[]{:S(2)}) %collective-permute-start.8) | collective-permute-done | bytes 24608 | tf_op jit(solution)/shard_map/ppermute | solution.py:49
  45.3 1.5 %collective-permute-start.12 = (bf16[16,3072]{1,0:T(8,128)(2,1)S(1)}, bf16[16,3072]{1,0:T(8,128)(2,1)S(1)}, u32[]{:S(2)}, u32[]{:S(2)}) collective-permute-start(bf16[16,3072]{1,0:T(8,128)(2,1)S(1)} %join.1.refs_0_), channel_id=1, source_target_pairs={{0,8},{4,12},{8,0},{12,4},{1,9},{5,13},{9,1},{13,5},{2,10},{6,14},... | collective-permute-start | bytes 294920 | tf_op jit(solution)/shard_map/ppermute | solution.py:49
  46.8 3.2 %collective-permute-done.12.refs_2_ = bf16[16,3072]{1,0:T(8,128)(2,1)S(1)} collective-permute-done((bf16[16,3072]{1,0:T(8,128)(2,1)S(1)}, bf16[16,3072]{1,0:T(8,128)(2,1)S(1)}, u32[]{:S(2)}, u32[]{:S(2)}) %collective-permute-start.12) | collective-permute-done | bytes 98336 | tf_op jit(solution)/shard_map/ppermute | solution.py:49
  50.0 1.3 %collective-permute-done.13.refs_3_ = bf16[16,3072]{1,0:T(8,128)(2,1)S(1)} collective-permute-done((bf16[16,3072]{1,0:T(8,128)(2,1)S(1)}, bf16[16,3072]{1,0:T(8,128)(2,1)S(1)}, u32[]{:S(2)}, u32[]{:S(2)}) %collective-permute-start.13) | collective-permute-done | bytes 98336 | tf_op jit(solution)/shard_map/ppermute | solution.py:49
  51.4 2.7 %output_part.3 = (f32[64,1792]{1,0:T(8,128)S(1)}, s16[32,1920]{1,0:T(8,128)(2,1)S(1)}) custom-call(s32[2]{0:T(128)S(1)} %pad_add_fusion.refs_1_.me_ref, bf16[16,3072]{1,0:T(8,128)(2,1)S(1)} %join.1.refs_0_, bf16[16,3072]{1,0:T(8,128)(2,1)S(1)} %collective-permute-done.11.refs_1_, bf16[16,3072]{1,0:T(8,128)(2,1)S(1)} %collective-permute-done.12.refs_2_, ...), custom_call_target="tpu_custom_call" | custom-call | flops 704643072 | bytes 393216 | tf_op jit(solution)/shard_map/output_part/pallas_call | solution.py:23
  54.1 1.8 %collective-permute-start.14 = (s16[32,1920]{1,0:T(8,128)(2,1)S(1)}, s16[32,1920]{1,0:T(8,128)(2,1)S(1)}, u32[]{:S(2)}, u32[]{:S(2)}) collective-permute-start(s16[32,1920]{1,0:T(8,128)(2,1)S(1)} %get-tuple-element.42), channel_id=1, source_target_pairs={{0,1},{1,0},{2,3},{3,2},{4,5},{5,4},{6,7},{7,6},{8,9},{9,8},{10,11... | collective-permute-start | bytes 368648 | tf_op jit(solution)/shard_map/ppermute | solution.py:49
  55.9 2.9 %output_part.4 = (f32[64,2048]{1,0:T(8,128)S(1)}, s16[32,2176]{1,0:T(8,128)(2,1)S(1)}) custom-call(s32[2]{0:T(128)S(1)} %pad_add_fusion.refs_1_.me_ref, bf16[16,3072]{1,0:T(8,128)(2,1)S(1)} %join.1.refs_0_, bf16[16,3072]{1,0:T(8,128)(2,1)S(1)} %collective-permute-done.11.refs_1_, bf16[16,3072]{1,0:T(8,128)(2,1)S(1)} %collective-permute-done.12.refs_2_, ...), custom_call_target="tpu_custom_call" | custom-call | flops 805306368 | bytes 393216 | tf_op jit(solution)/shard_map/output_part/pallas_call | solution.py:23
  59.8 1.8 %collective-permute-start.15 = (s16[16,1920]{1,0:T(8,128)(2,1)S(1)}, s16[16,1920]{1,0:T(8,128)(2,1)S(1)}, u32[]{:S(2)}, u32[]{:S(2)}) collective-permute-start(s16[16,1920]{1,0:T(8,128)(2,1)S(1)} %get-tuple-element.45), channel_id=1, source_target_pairs={{0,2},{1,3},{2,0},{3,1},{4,6},{5,7},{6,4},{7,5},{8,10},{9,11},{10,... | collective-permute-start | bytes 184328 | tf_op jit(solution)/shard_map/ppermute | solution.py:49
  61.5 1.6 %output_part.5 = (f32[64,768]{1,0:T(8,128)S(1)}, s16[32,896]{1,0:T(8,128)(2,1)S(1)}) custom-call(s32[2]{0:T(128)S(1)} %pad_add_fusion.refs_1_.me_ref, bf16[16,3072]{1,0:T(8,128)(2,1)S(1)} %join.1.refs_0_, bf16[16,3072]{1,0:T(8,128)(2,1)S(1)} %collective-permute-done.11.refs_1_, bf16[16,3072]{1,0:T(8,128)(2,1)S(1)} %collective-permute-done.12.refs_2_, ...), custom_call_target="tpu_custom_call" | custom-call | flops 301989888 | bytes 393216 | tf_op jit(solution)/shard_map/output_part/pallas_call | solution.py:23
  63.1 1.3 %collective-permute-start.18 = (s16[32,896]{1,0:T(8,128)(2,1)S(1)}, s16[32,896]{1,0:T(8,128)(2,1)S(1)}, u32[]{:S(2)}, u32[]{:S(2)}) collective-permute-start(s16[32,896]{1,0:T(8,128)(2,1)S(1)} %get-tuple-element.50), channel_id=1, source_target_pairs={{0,1},{1,0},{2,3},{3,2},{4,5},{5,4},{6,7},{7,6},{8,9},{9,8},{10,11... | collective-permute-start | bytes 172040 | tf_op jit(solution)/shard_map/ppermute | solution.py:49
  64.4 1.7 %collective-permute-done.16.came_ref = s16[32,2176]{1,0:T(8,128)(2,1)S(1)} collective-permute-done((s16[32,2176]{1,0:T(8,128)(2,1)S(1)}, s16[32,2176]{1,0:T(8,128)(2,1)S(1)}, u32[]{:S(2)}, u32[]{:S(2)}) %collective-permute-start.16) | collective-permute-done | bytes 139296 | tf_op jit(solution)/shard_map/ppermute | solution.py:49
  66.6 0.8 %collective-permute-done.18.came_ref = s16[32,896]{1,0:T(8,128)(2,1)S(1)} collective-permute-done((s16[32,896]{1,0:T(8,128)(2,1)S(1)}, s16[32,896]{1,0:T(8,128)(2,1)S(1)}, u32[]{:S(2)}, u32[]{:S(2)}) %collective-permute-start.18) | collective-permute-done | bytes 57376 | tf_op jit(solution)/shard_map/ppermute | solution.py:49
  67.5 2.1 %collective-permute-start.19 = (s16[16,896]{1,0:T(8,128)(2,1)S(1)}, s16[16,896]{1,0:T(8,128)(2,1)S(1)}, u32[]{:S(2)}, u32[]{:S(2)}) collective-permute-start(s16[16,896]{1,0:T(8,128)(2,1)S(1)} %get-tuple-element.52), channel_id=1, source_target_pairs={{0,2},{1,3},{2,0},{3,1},{4,6},{5,7},{6,4},{7,5},{8,10},{9,11},{10,... | collective-permute-start | bytes 86024 | tf_op jit(solution)/shard_map/ppermute | solution.py:49
  69.7 2.1 %collective-permute-done.17.refs_2_ = s16[16,2176]{1,0:T(8,128)(2,1)S(1)} collective-permute-done((s16[16,2176]{1,0:T(8,128)(2,1)S(1)}, s16[16,2176]{1,0:T(8,128)(2,1)S(1)}, u32[]{:S(2)}, u32[]{:S(2)}) %collective-permute-start.17) | collective-permute-done | bytes 69664 | tf_op jit(solution)/shard_map/ppermute | solution.py:49
  72.4 0.8 %finish.3 = bf16[16,4608]{1,0:T(8,128)(2,1)} custom-call(bf16[16,1792]{1,0:T(8,128)(2,1)S(1)} %finish.2.refs_0_, f32[16,2048]{1,0:T(8,128)S(1)} %get-tuple-element.48.refs_1_, s16[16,2176]{1,0:T(8,128)(2,1)S(1)} %collective-permute-done.17.refs_2_, f32[16,768]{1,0:T(8,128)S(1)} %get-tuple-element.51.refs_3_, s16[16,896]{1,0:T(8,128)(2,1)S(1)} %collective-permute-done.19.refs_4_), custom_call_target="tpu_custom_call" | custom-call | bytes 589824 | tf_op jit(solution)/shard_map/finish/pallas_call | solution.py:23
  (50 shorter events, 4.7 us)
Async XLA Ops:
  1.3 5.7 %collective-permute-start.2 = (f32[2,64]{1,0:T(2,128)S(1)}, f32[2,64]{1,0:T(2,128)S(1)}, u32[]{:S(2)}, u32[]{:S(2)}) collective-permute-start(f32[2,64]{1,0:T(2,128)S(1)} %pad_maximum_fusion.refs_0_), channel_id=1, source_target_pairs={{0,12},{4,8},{8,4},{12,0},{1,13},{5,9},{9,5},{13,1},{2,14},{6,10},... | collective-permute-start | bytes 1544 | tf_op jit(solution)/shard_map/ppermute | solution.py:49
  3.8 3.6 %collective-permute-start.1 = (f32[2,64]{1,0:T(2,128)S(1)}, f32[2,64]{1,0:T(2,128)S(1)}, u32[]{:S(2)}, u32[]{:S(2)}) collective-permute-start(f32[2,64]{1,0:T(2,128)S(1)} %pad_maximum_fusion.refs_0_), channel_id=1, source_target_pairs={{0,8},{4,12},{8,0},{12,4},{1,9},{5,13},{9,1},{13,5},{2,10},{6,14},... | collective-permute-start | bytes 1544 | tf_op jit(solution)/shard_map/ppermute | solution.py:49
  4.4 2.9 %collective-permute-start = (f32[2,64]{1,0:T(2,128)S(1)}, f32[2,64]{1,0:T(2,128)S(1)}, u32[]{:S(2)}, u32[]{:S(2)}) collective-permute-start(f32[2,64]{1,0:T(2,128)S(1)} %pad_maximum_fusion.refs_0_), channel_id=1, source_target_pairs={{0,4},{4,0},{8,12},{12,8},{1,5},{5,1},{9,13},{13,9},{2,6},{6,2},{1... | collective-permute-start | bytes 1544 | tf_op jit(solution)/shard_map/ppermute | solution.py:49
  4.6 2.8 %copy-start = (bf16[64,4608]{1,0:T(8,128)(2,1)S(1)}, bf16[64,4608]{1,0:T(8,128)(2,1)}, u32[]{:S(2)}) copy-start(bf16[64,4608]{1,0:T(8,128)(2,1)} %refs_4_.5) | copy-start | bytes 1769476
  4.6 2.9 %copy-start.1 = (bf16[1152,512]{1,0:T(8,128)(2,1)S(1)}, bf16[1152,512]{1,0:T(8,128)(2,1)}, u32[]{:S(2)}) copy-start(bf16[1152,512]{1,0:T(8,128)(2,1)} %refs_7_.1) | copy-start | bytes 3538948
  4.6 2.9 %copy-start.2 = (f32[4608]{0:T(1024)S(1)}, f32[4608]{0:T(1024)}, u32[]{:S(2)}) copy-start(f32[4608]{0:T(1024)} %refs_5_.1) | copy-start | bytes 55300
  16.6 2.0 %collective-permute-start.3 = (f32[32,3584]{1,0:T(8,128)S(1)}, f32[32,3584]{1,0:T(8,128)S(1)}, u32[]{:S(2)}, u32[]{:S(2)}) collective-permute-start(f32[32,3584]{1,0:T(8,128)S(1)} %get-tuple-element.30), channel_id=1, source_target_pairs={{0,4},{4,0},{8,12},{12,8},{1,5},{5,1},{9,13},{13,9},{2,6},{6,2},{1... | collective-permute-start | bytes 1376264 | tf_op jit(solution)/shard_map/ppermute | solution.py:49
  18.7 7.9 %collective-permute-start.4 = (f32[16,3584]{1,0:T(8,128)S(1)}, f32[16,3584]{1,0:T(8,128)S(1)}, u32[]{:S(2)}, u32[]{:S(2)}) collective-permute-start(f32[16,3584]{1,0:T(8,128)S(1)} %get-tuple-element.32), channel_id=1, source_target_pairs={{0,8},{4,12},{8,0},{12,4},{1,9},{5,13},{9,1},{13,5},{2,10},{6,14},... | collective-permute-start | bytes 688136 | tf_op jit(solution)/shard_map/ppermute | solution.py:49
  26.6 9.1 %copy-start.3 = (bf16[4,1024,512]{2,1,0:T(8,128)(2,1)S(1)}, bf16[4,1024,512]{2,1,0:T(8,128)(2,1)}, u32[]{:S(2)}) copy-start(bf16[4,1024,512]{2,1,0:T(8,128)(2,1)} %refs_4_.6) | copy-start | bytes 12582916
  26.6 9.1 %copy-start.4 = (s32[4]{0:T(128)S(1)}, s32[4]{0:T(128)}, u32[]{:S(2)}) copy-start(s32[4]{0:T(128)} %lengths_ref.1) | copy-start | bytes 52
  26.6 24.7 %slice-start = ((s8[28311552]{0:T(1024)(128)(4,1)}), s8[4194304]{0:T(1024)(128)(4,1)S(1)}, s32[]{:S(2)}) async-start(s8[28311552]{0:T(1024)(128)(4,1)} %bitcast.4), calls=%async_computation | async-start | bytes 8388608
  26.6 24.7 %slice-start.1 = ((s8[28311552]{0:T(1024)(128)(4,1)}), s8[4194304]{0:T(1024)(128)(4,1)S(1)}, s32[]{:S(2)}) async-start(s8[28311552]{0:T(1024)(128)(4,1)} %bitcast.4), calls=%async_computation.1 | async-start | bytes 8388608
  26.6 24.7 %slice-start.2 = ((s8[28311552]{0:T(1024)(128)(4,1)}), s8[4194304]{0:T(1024)(128)(4,1)S(1)}, s32[]{:S(2)}) async-start(s8[28311552]{0:T(1024)(128)(4,1)} %bitcast.4), calls=%async_computation.2 | async-start | bytes 8388608
  27.2 6.1 %collective-permute-start.5 = (bf16[4,4096]{1,0:T(4,128)(2,1)S(1)}, bf16[4,4096]{1,0:T(4,128)(2,1)S(1)}, u32[]{:S(2)}, u32[]{:S(2)}) collective-permute-start(bf16[4,4096]{1,0:T(4,128)(2,1)S(1)} %get-tuple-element.33), channel_id=1, source_target_pairs={{0,3},{1,2},{2,1},{3,0},{4,7},{5,6},{6,5},{7,4},{8,11},{9,10},{10,... | collective-permute-start | bytes 98312 | tf_op jit(solution)/shard_map/ppermute | solution.py:49
  30.9 4.8 %collective-permute-start.6 = (bf16[4,4096]{1,0:T(4,128)(2,1)S(1)}, bf16[4,4096]{1,0:T(4,128)(2,1)S(1)}, u32[]{:S(2)}, u32[]{:S(2)}) collective-permute-start(bf16[4,4096]{1,0:T(4,128)(2,1)S(1)} %get-tuple-element.34), channel_id=1, source_target_pairs={{0,2},{1,3},{2,0},{3,1},{4,6},{5,7},{6,4},{7,5},{8,10},{9,11},{10,... | collective-permute-start | bytes 98312 | tf_op jit(solution)/shard_map/ppermute | solution.py:49
  30.9 4.8 %collective-permute-start.7 = (bf16[4,4096]{1,0:T(4,128)(2,1)S(1)}, bf16[4,4096]{1,0:T(4,128)(2,1)S(1)}, u32[]{:S(2)}, u32[]{:S(2)}) collective-permute-start(bf16[4,4096]{1,0:T(4,128)(2,1)S(1)} %get-tuple-element.35), channel_id=1, source_target_pairs={{0,1},{1,0},{2,3},{3,2},{4,5},{5,4},{6,7},{7,6},{8,9},{9,8},{10,11... | collective-permute-start | bytes 98312 | tf_op jit(solution)/shard_map/ppermute | solution.py:49
  35.7 15.6 %slice-start.3 = ((s8[28311552]{0:T(1024)(128)(4,1)}), s8[4194304]{0:T(1024)(128)(4,1)S(1)}, s32[]{:S(2)}) async-start(s8[28311552]{0:T(1024)(128)(4,1)} %bitcast.4), calls=%async_computation.3 | async-start | bytes 8388608
  35.8 15.6 %slice-start.4 = ((s8[28311552]{0:T(1024)(128)(4,1)}), s8[4194304]{0:T(1024)(128)(4,1)S(1)}, s32[]{:S(2)}) async-start(s8[28311552]{0:T(1024)(128)(4,1)} %bitcast.4), calls=%async_computation.4 | async-start | bytes 8388608
  38.2 5.7 %collective-permute-start.8 = (bf16[4,3072]{1,0:T(4,128)(2,1)S(1)}, bf16[4,3072]{1,0:T(4,128)(2,1)S(1)}, u32[]{:S(2)}, u32[]{:S(2)}) collective-permute-start(bf16[4,3072]{1,0:T(4,128)(2,1)S(1)} %get-tuple-element.37), channel_id=1, source_target_pairs={{0,3},{1,2},{2,1},{3,0},{4,7},{5,6},{6,5},{7,4},{8,11},{9,10},{10,... | collective-permute-start | bytes 73736 | tf_op jit(solution)/shard_map/ppermute | solution.py:49
  39.7 4.7 %collective-permute-start.9 = (bf16[4,3072]{1,0:T(4,128)(2,1)S(1)}, bf16[4,3072]{1,0:T(4,128)(2,1)S(1)}, u32[]{:S(2)}, u32[]{:S(2)}) collective-permute-start(bf16[4,3072]{1,0:T(4,128)(2,1)S(1)} %get-tuple-element.38), channel_id=1, source_target_pairs={{0,2},{1,3},{2,0},{3,1},{4,6},{5,7},{6,4},{7,5},{8,10},{9,11},{10,... | collective-permute-start | bytes 73736 | tf_op jit(solution)/shard_map/ppermute | solution.py:49
  40.4 4.3 %collective-permute-start.10 = (bf16[4,3072]{1,0:T(4,128)(2,1)S(1)}, bf16[4,3072]{1,0:T(4,128)(2,1)S(1)}, u32[]{:S(2)}, u32[]{:S(2)}) collective-permute-start(bf16[4,3072]{1,0:T(4,128)(2,1)S(1)} %get-tuple-element.39), channel_id=1, source_target_pairs={{0,1},{1,0},{2,3},{3,2},{4,5},{5,4},{6,7},{7,6},{8,9},{9,8},{10,11... | collective-permute-start | bytes 73736 | tf_op jit(solution)/shard_map/ppermute | solution.py:49
  44.7 6.6 %slice-start.5 = ((s8[28311552]{0:T(1024)(128)(4,1)}), s8[4194304]{0:T(1024)(128)(4,1)S(1)}, s32[]{:S(2)}) async-start(s8[28311552]{0:T(1024)(128)(4,1)} %bitcast.4), calls=%async_computation.5 | async-start | bytes 8388608
  44.7 6.6 %slice-start.6 = ((s8[28311552]{0:T(1024)(128)(4,1)}), s8[3145728]{0:T(1024)(128)(4,1)S(1)}, s32[]{:S(2)}) async-start(s8[28311552]{0:T(1024)(128)(4,1)} %bitcast.4), calls=%async_computation.6 | async-start | bytes 6291456
  45.3 4.7 %collective-permute-start.12 = (bf16[16,3072]{1,0:T(8,128)(2,1)S(1)}, bf16[16,3072]{1,0:T(8,128)(2,1)S(1)}, u32[]{:S(2)}, u32[]{:S(2)}) collective-permute-start(bf16[16,3072]{1,0:T(8,128)(2,1)S(1)} %join.1.refs_0_), channel_id=1, source_target_pairs={{0,8},{4,12},{8,0},{12,4},{1,9},{5,13},{9,1},{13,5},{2,10},{6,14},... | collective-permute-start | bytes 294920 | tf_op jit(solution)/shard_map/ppermute | solution.py:49
  46.8 3.2 %collective-permute-start.11 = (bf16[16,3072]{1,0:T(8,128)(2,1)S(1)}, bf16[16,3072]{1,0:T(8,128)(2,1)S(1)}, u32[]{:S(2)}, u32[]{:S(2)}) collective-permute-start(bf16[16,3072]{1,0:T(8,128)(2,1)S(1)} %join.1.refs_0_), channel_id=1, source_target_pairs={{0,4},{4,0},{8,12},{12,8},{1,5},{5,1},{9,13},{13,9},{2,6},{6,2},{1... | collective-permute-start | bytes 294920 | tf_op jit(solution)/shard_map/ppermute | solution.py:49
  50.0 1.3 %collective-permute-start.13 = (bf16[16,3072]{1,0:T(8,128)(2,1)S(1)}, bf16[16,3072]{1,0:T(8,128)(2,1)S(1)}, u32[]{:S(2)}, u32[]{:S(2)}) collective-permute-start(bf16[16,3072]{1,0:T(8,128)(2,1)S(1)} %collective-permute-done.12.refs_2_), channel_id=1, source_target_pairs={{0,4},{4,0},{8,12},{12,8},{1,5},{5,1},{9,13},{13,9},{2,6},{6,2},{1... | collective-permute-start | bytes 294920 | tf_op jit(solution)/shard_map/ppermute | solution.py:49
  54.1 5.5 %collective-permute-start.14 = (s16[32,1920]{1,0:T(8,128)(2,1)S(1)}, s16[32,1920]{1,0:T(8,128)(2,1)S(1)}, u32[]{:S(2)}, u32[]{:S(2)}) collective-permute-start(s16[32,1920]{1,0:T(8,128)(2,1)S(1)} %get-tuple-element.42), channel_id=1, source_target_pairs={{0,1},{1,0},{2,3},{3,2},{4,5},{5,4},{6,7},{7,6},{8,9},{9,8},{10,11... | collective-permute-start | bytes 368648 | tf_op jit(solution)/shard_map/ppermute | solution.py:49
  58.9 7.2 %collective-permute-start.16 = (s16[32,2176]{1,0:T(8,128)(2,1)S(1)}, s16[32,2176]{1,0:T(8,128)(2,1)S(1)}, u32[]{:S(2)}, u32[]{:S(2)}) collective-permute-start(s16[32,2176]{1,0:T(8,128)(2,1)S(1)} %get-tuple-element.46), channel_id=1, source_target_pairs={{0,1},{1,0},{2,3},{3,2},{4,5},{5,4},{6,7},{7,6},{8,9},{9,8},{10,11... | collective-permute-start | bytes 417800 | tf_op jit(solution)/shard_map/ppermute | solution.py:49
  59.8 6.8 %collective-permute-start.15 = (s16[16,1920]{1,0:T(8,128)(2,1)S(1)}, s16[16,1920]{1,0:T(8,128)(2,1)S(1)}, u32[]{:S(2)}, u32[]{:S(2)}) collective-permute-start(s16[16,1920]{1,0:T(8,128)(2,1)S(1)} %get-tuple-element.45), channel_id=1, source_target_pairs={{0,2},{1,3},{2,0},{3,1},{4,6},{5,7},{6,4},{7,5},{8,10},{9,11},{10,... | collective-permute-start | bytes 184328 | tf_op jit(solution)/shard_map/ppermute | solution.py:49
  63.1 4.2 %collective-permute-start.18 = (s16[32,896]{1,0:T(8,128)(2,1)S(1)}, s16[32,896]{1,0:T(8,128)(2,1)S(1)}, u32[]{:S(2)}, u32[]{:S(2)}) collective-permute-start(s16[32,896]{1,0:T(8,128)(2,1)S(1)} %get-tuple-element.50), channel_id=1, source_target_pairs={{0,1},{1,0},{2,3},{3,2},{4,5},{5,4},{6,7},{7,6},{8,9},{9,8},{10,11... | collective-permute-start | bytes 172040 | tf_op jit(solution)/shard_map/ppermute | solution.py:49
  66.3 5.5 %collective-permute-start.17 = (s16[16,2176]{1,0:T(8,128)(2,1)S(1)}, s16[16,2176]{1,0:T(8,128)(2,1)S(1)}, u32[]{:S(2)}, u32[]{:S(2)}) collective-permute-start(s16[16,2176]{1,0:T(8,128)(2,1)S(1)} %get-tuple-element.49), channel_id=1, source_target_pairs={{0,2},{1,3},{2,0},{3,1},{4,6},{5,7},{6,4},{7,5},{8,10},{9,11},{10,... | collective-permute-start | bytes 208904 | tf_op jit(solution)/shard_map/ppermute | solution.py:49
  67.5 4.8 %collective-permute-start.19 = (s16[16,896]{1,0:T(8,128)(2,1)S(1)}, s16[16,896]{1,0:T(8,128)(2,1)S(1)}, u32[]{:S(2)}, u32[]{:S(2)}) collective-permute-start(s16[16,896]{1,0:T(8,128)(2,1)S(1)} %get-tuple-element.52), channel_id=1, source_target_pairs={{0,2},{1,3},{2,0},{3,1},{4,6},{5,7},{6,4},{7,5},{8,10},{9,11},{10,... | collective-permute-start | bytes 86024 | tf_op jit(solution)/shard_map/ppermute | solution.py:49

commit v10 on v9

--- a/solution.py
+++ b/solution.py
@@ -217,43 +217,48 @@
 
 def split_kernel(queries, me_ref, kept_ref, came_ref, *refs):
     out_refs, slots = refs[:-1], refs[-1]
-    count, rows = len(out_refs), out_refs[0].shape[0]
-    narrow = me_ref[1]
+    count = len(out_refs)
     total = kept_ref[...] + came_ref[...]
+    rows, columns = total.shape[0] // count, total.shape[1]
+    half = slots.shape[1]
+    fresh = total[:, queries:]
+    low = fresh - fresh.astype(jnp.bfloat16).astype(jnp.float32)
     for j in range(count):
-        slots[j * PAD : j * PAD + rows, :] = total[j * rows : (j + 1) * rows, :]
+        mine = slice(j * rows, (j + 1) * rows)
+        slots[j * PAD : j * PAD + rows, :] = total[mine, :half]
+        slots[j * PAD + rows : (j + 1) * PAD, : columns - half] = total[mine, half:]
+        slots[j * PAD + rows : (j + 1) * PAD, columns - half :] = low[mine, :]
     for d, out_ref in enumerate(out_refs):
-        mine = slots[pl.ds(pl.multiple_of((narrow ^ d) * PAD, PAD), rows), :]
-        high = mine.astype(jnp.bfloat16)
-        out_ref[:, : mine.shape[1]] = high
-        out_ref[:, mine.shape[1] :] = (mine - high.astype(jnp.float32))[:, queries:].astype(jnp.bfloat16)
+        out_ref[...] = slots[pl.ds(pl.multiple_of((me_ref[1] ^ d) * PAD, PAD), PAD), :].astype(jnp.bfloat16)
 
 
 def attend_kernel(head_dim, count, lengths_ref, *refs):
     came_refs, kv_ref = refs[:count][::-1], refs[count]
-    refs = refs[count + 1 :]
-    out_refs, (heads, contexts) = refs[:count], refs[count:]
+    out_refs, (heads, contexts) = refs[count + 1 : 2 * count + 1], refs[2 * count + 1 :]
     rows, positions = kv_ref.shape[0], kv_ref.shape[1]
-    queries = out_refs[0].shape[1]
+    half = came_refs[0].shape[1]
+    queries = 2 * out_refs[0].shape[1]
     each = queries // head_dim
-    total_heads = each * count
     slabs = head_dim // LANES
+    group = each // 2
+    half_heads = count * group
     scaling = 1.0 / math.sqrt(head_dim)
+    terms = 0.0
     for d, ref in enumerate(came_refs):
-        for h in range(each):
-            at = (d * each + h) * PAD
-            for k in range(slabs):
-                start = h * head_dim + k * LANES
-                heads[k, at : at + rows, :] = ref[:, start : start + LANES].astype(jnp.float32)
-    terms = came_refs[0][:, queries:].astype(jnp.float32)
-    for ref in came_refs[1:]:
-        terms = terms + ref[:, queries:].astype(jnp.float32)
+        for c in range(0, half, LANES):
+            both = ref[:, c : c + LANES].astype(jnp.float32)
+            for column, part in ((c, both[:rows, :]), (half + c, both[rows:, :])):
+                if column < queries:
+                    h = column // head_dim
+                    at = ((h // group) * half_heads + d * group + h % group) * PAD
+                    heads[column % head_dim // LANES, at : at + rows, :] = part
+        terms = terms + ref[:, queries - half :].astype(jnp.float32)[rows:, :]
     pair = 2 * head_dim
     fresh = terms[:, :pair] + terms[:, pair:]
     fresh = fresh.astype(jnp.bfloat16).astype(jnp.float32)
-    place = lax.broadcasted_iota(jnp.int32, (total_heads, positions), 1)
+    place = lax.broadcasted_iota(jnp.int32, (2 * half_heads, positions), 1)
     for r in range(rows):
-        query = jnp.concatenate([heads[k, pl.ds(r, total_heads, stride=PAD), :] for k in range(slabs)], axis=1)
+        query = jnp.concatenate([heads[k, pl.ds(r, 2 * half_heads, stride=PAD), :] for k in range(slabs)], axis=1)
         scores = (
             lax.dot_general(
                 query.astype(jnp.bfloat16),
@@ -273,27 +278,32 @@
         numer = numer + own_weight.astype(jnp.bfloat16).astype(jnp.float32) * fresh[r : r + 1, head_dim:]
         context = numer / total
         for k in range(slabs):
-            contexts[k, pl.ds(r, total_heads, stride=PAD), :] = context[:, k * LANES : (k + 1) * LANES]
+            for side in range(2):
+                contexts[k, pl.ds(side * rows + r, half_heads, stride=PAD), :] = context[
+                    side * half_heads : (side + 1) * half_heads, k * LANES : (k + 1) * LANES
+                ]
     for d, ref in enumerate(out_refs):
-        for h in range(each):
-            at = (d * each + h) * PAD
+        for h in range(group):
+            at = (d * group + h) * PAD
             for k in range(slabs):
                 start = h * head_dim + k * LANES
-                ref[:, start : start + LANES] = contexts[k, at : at + rows, :].astype(jnp.bfloat16)
+                ref[:, start : start + LANES] = contexts[k, at : at + PAD, :].astype(jnp.bfloat16)
 
 
 def attend(lengths, came, kv, head_dim, queries):
-    rows = kv.shape[0]
     count = len(came)
     all_heads = count * queries // head_dim
-    scratch = pltpu.VMEM((head_dim // LANES, all_heads * PAD, LANES), jnp.float32)
+    slabs = head_dim // LANES
     return call(
         functools.partial(attend_kernel, head_dim, count),
-        [jax.ShapeDtypeStruct((rows, queries), jnp.bfloat16)] * count,
+        [jax.ShapeDtypeStruct((PAD, queries // 2), jnp.bfloat16)] * count,
         (lengths, *came[::-1], in_vmem(kv)),
         [SCALAR] + [FULL] * (count + 1),
         "attend",
-        scratch=[scratch, scratch],
+        scratch=[
+            pltpu.VMEM((slabs, all_heads * PAD, LANES), jnp.float32),
+            pltpu.VMEM((slabs, all_heads // 2 * PAD, LANES), jnp.float32),
+        ],
         limit=8,
         flops=BESIDE,
     )
@@ -302,12 +312,14 @@
 def join_kernel(me_ref, *refs):
     count = len(refs) - 2
     out_ref, joined = refs[-2:]
-    rows = refs[0].shape[0]
+    half = joined.shape[1]
+    rows = out_ref.shape[0] // count
     for d in range(count):
-        at = pl.ds(pl.multiple_of((me_ref[1] ^ d) * PAD, PAD), rows)
+        at = pl.ds(pl.multiple_of((me_ref[1] ^ d) * PAD, PAD), PAD)
         joined[at, :] = refs[count - 1 - d][...].astype(jnp.float32)
-    came = [joined[j * PAD : j * PAD + rows, :] for j in range(count)]
-    out_ref[...] = jnp.concatenate(came, axis=0).astype(jnp.bfloat16)
+    for side in range(2):
+        came = [joined[j * PAD + side * rows : j * PAD + (side + 1) * rows, :] for j in range(count)]
+        out_ref[:, side * half : (side + 1) * half] = jnp.concatenate(came, axis=0).astype(jnp.bfloat16)
 
 
 def code(x, ref):
@@ -384,29 +396,28 @@
     )
 
 
-def finish_kernel(starts, kinds, *refs):
-    out_ref = refs[-1]
-    k = 0
-    for at, kind in zip(starts, kinds):
-        width = refs[k].shape[1]
-        done = refs[k][...]
-        if kind == 2:
-            done = (done + decode(refs[k + 1], width)).astype(jnp.bfloat16)
-        out_ref[:, at : at + width] = done
-        k += kind
-
-
-def finish(starts, cuts):
-    parts = [x for cut in cuts for x in cut]
-    rows, columns = parts[0].shape[0], sum(cut[0].shape[1] for cut in cuts)
-    return call(
-        functools.partial(finish_kernel, starts, [len(cut) for cut in cuts]),
-        jax.ShapeDtypeStruct((rows, columns), jnp.bfloat16),
-        parts,
-        [FULL] * len(parts),
-        "finish",
-        moved=8 * columns * rows,
-    )
+def finish_kernel(start, kept_ref, came_ref, *refs):
+    out_ref, done, sem = refs[-3:]
+    width = kept_ref.shape[1]
+    done[...] = (kept_ref[...] + decode(came_ref, width)).astype(jnp.bfloat16)
+    copy = pltpu.make_async_copy(done, out_ref.at[:, start : start + width], sem)
+    copy.start()
+    copy.wait()
+
+
+def finish(kept, came, start, columns, result):
+    rows, width = kept.shape
+    return pl.pallas_call(
+        functools.partial(finish_kernel, start),
+        out_shape=pltpu.HBM((rows, columns), jnp.bfloat16),
+        in_specs=[FULL, FULL] + [ANY] * (result is not None),
+        out_specs=ANY,
+        scratch_shapes=[pltpu.VMEM((rows, width), jnp.bfloat16), pltpu.SemaphoreType.DMA],
+        input_output_aliases={} if result is None else {2: 0},
+        compiler_params=pltpu.CompilerParams(vmem_limit_bytes=4 * MIB),
+        cost_estimate=pl.CostEstimate(flops=0, bytes_accessed=8 * rows * width, transcendentals=0),
+        name="finish",
+    )(kept, came, *([] if result is None else [in_hbm(result)]))
 
 
 def local(activations, norm_gain, query_weight, kv_weight, out_weight, kv_cache, lengths):
@@ -414,6 +425,7 @@
     narrow_count = lax.axis_size("narrow")
     me = jnp.stack([lax.axis_index("wide"), lax.axis_index("narrow")]).astype(jnp.int32)
     own_rows, head_dim = kv_cache.shape[0], kv_cache.shape[2] // 2
+    assert PAD == 2 * own_rows
     rows, width = activations.shape
     queries = query_weight.shape[1]
     columns = out_weight.shape[1]
@@ -438,11 +450,11 @@
         d *= 2
     split = call(
         functools.partial(split_kernel, queries),
-        [jax.ShapeDtypeStruct((own_rows, queries + 4 * head_dim), jnp.bfloat16)] * narrow_count,
+        [jax.ShapeDtypeStruct((PAD, queries // 2 + 2 * head_dim), jnp.bfloat16)] * narrow_count,
         (me, kept, swap(sent, "wide", d)),
         [SCALAR] + [FULL] * 2,
         "split",
-        scratch=[pltpu.VMEM((narrow_count * PAD, queries + 2 * head_dim), jnp.float32)],
+        scratch=[pltpu.VMEM((narrow_count * PAD, queries // 2 + 2 * head_dim), jnp.float32)],
         flops=BESIDE,
     )
     context = attend(lengths, exchange(split, "narrow"), kv_cache, head_dim, queries)
@@ -452,7 +464,7 @@
         (me, *exchange(context, "narrow")[::-1]),
         [SCALAR] + [FULL] * narrow_count,
         "join",
-        scratch=[pltpu.VMEM((narrow_count * PAD, queries), jnp.float32)],
+        scratch=[pltpu.VMEM((narrow_count * PAD, queries // 2), jnp.float32)],
         flops=BESIDE,
     )
     gathered = gather(returned, "wide")
@@ -473,10 +485,11 @@
         if last:
             exchange_cut(*last, [kept])
         last = (kept, sent)
-    early = finish([0], cut_sums[:1])
-    exchange_cut(*last, [early])
-    cut_sums[0] = (early,)
-    return finish(ends[:-1], cut_sums)
+    result = finish(*cut_sums[0], ends[0], columns, None)
+    exchange_cut(*last, [in_hbm(result)])
+    for cut, start in zip(cut_sums[1:], ends[1:]):
+        result = finish(*cut, start, columns, result)
+    return result
 
 
 def solution(mesh):

time: 73.3 us -> 73.3 us (level)
  waiting for transfers between devices: 24.2 us -> 22.3 us
  Pallas kernels: 24 us -> 25.2 us
    pallas_call x0 -> x3, Pallas kernels: none -> 2.15 us  [finish(): pl.pallas_call(functools.partial(finish_kernel, start), out_shape=pltpu.H...]
    ppermute x20, waiting for transfers between devices: 24.2 us -> 22.3 us  [swap(): return lax.ppermute(x, axis, [(i, i ^ distance) for i in range(count)])]
    pallas_call x14 -> x12, Pallas kernels: 24 us -> 23.1 us  [call(): pl.pallas_call(kernel, out_shape=outs, in_specs=specs, out_specs=jax.tree...]
  transfers between devices with their start and end apart: 20 -> 20, of which waited for: 15 -> 14; matrix products, arithmetic and copies ran while one was open for 0% -> 0% of each run, Pallas kernels for 10% -> 12%
where the time goes in v10:
time: 73.3 us; the launch traced here: 73.2 us
  Pallas kernels  25.2 us (34%)
  starting transfers between devices  23.9 us (33%)
  waiting for transfers between devices  22.3 us (30%)
  other arithmetic  1.4 us (2%)
    ppermute x20, starting transfers between devices, swap(): return lax.ppermute(x, axis, [(i, i ^ distance) for i in range(count)])  23.9 us
    pallas_call x12, Pallas kernels, call(): pl.pallas_call(kernel, out_shape=outs, in_specs=specs, out_specs=jax.tree...  23.1 us
    ppermute x20, waiting for transfers between devices, swap(): return lax.ppermute(x, axis, [(i, i ^ distance) for i in range(count)])  22.3 us
    pallas_call x3, Pallas kernels, finish(): pl.pallas_call(functools.partial(finish_kernel, start), out_shape=pltpu.H...  2.15 us
  transfers between devices with their start and end apart: 20, of which 14 were waited for; matrix products, arithmetic and copies ran while one was open for 0% of the time, Pallas kernels for 12%

profile of v10, /device:TPU:0, one launch (start us, length us, event | category | flops | bytes accessed | tf_op | source)
XLA Modules:
  0.0 73.2 jit_solution(10513290230227110333)
XLA Ops:
  0.0 1.3 %convert_reduce_fusion = (f32[64]{0:T(128)S(1)}, f32[64]{0:T(128)S(1)}) fusion(bf16[64,4608]{1,0:T(8,128)(2,1)} %refs_4_.5), kind=kLoop, calls=%fused_computation.1 | loop fusion | flops 1179520 | bytes 590336 | tf_op jit(solution)/shard_map/reduce_sum | solution.py:433
  1.3 2.5 %collective-permute-start.2 = (f32[2,64]{1,0:T(2,128)S(1)}, f32[2,64]{1,0:T(2,128)S(1)}, u32[]{:S(2)}, u32[]{:S(2)}) collective-permute-start(f32[2,64]{1,0:T(2,128)S(1)} %pad_maximum_fusion.refs_0_), channel_id=1, source_target_pairs={{0,12},{4,8},{8,4},{12,0},{1,13},{5,9},{9,5},{13,1},{2,14},{6,10},... | collective-permute-start | bytes 1544 | tf_op jit(solution)/shard_map/ppermute | solution.py:49
  3.8 0.6 collective-permute-start.1
  4.6 2.5 %fetch_query_weight.1.refs_8_ = bf16[768,3072]{1,0:T(8,128)(2,1)S(1)} custom-call(bf16[4608,3072]{1,0:T(8,128)(2,1)} %refs_6_.1, f32[2,64]{1,0:T(2,128)S(1)} %pad_maximum_fusion.refs_0_, s32[2]{0:T(128)S(1)} %pad_add_fusion.refs_1_.me_ref), custom_call_target="tpu_custom_call" | custom-call | bytes 4718592 | tf_op jit(solution)/shard_map/fetch_query_weight/pallas_call | solution.py:23
  7.4 9.2 %project.1 = (f32[32,3584]{1,0:T(8,128)S(1)}, f32[32,3584]{1,0:T(8,128)S(1)}) custom-call(s32[2]{0:T(128)S(1)} %pad_add_fusion.refs_1_.me_ref, f32[2,64]{1,0:T(2,128)S(1)} %pad_maximum_fusion.refs_0_, f32[2,64]{1,0:T(2,128)S(1)} %collective-permute-done.refs_1_, f32[2,64]{1,0:T(2,128)S(1)} %collective-permute-done.1.refs_2_, ...), custom_call_target="tpu_custom_call" | custom-call | flops 1811939328 | bytes 23592960 | tf_op jit(solution)/shard_map/project/pallas_call | solution.py:23
  17.2 1.4 %collective-permute-done.3.came_ref = f32[32,3584]{1,0:T(8,128)S(1)} collective-permute-done((f32[32,3584]{1,0:T(8,128)S(1)}, f32[32,3584]{1,0:T(8,128)S(1)}, u32[]{:S(2)}, u32[]{:S(2)}) %collective-permute-start.3) | collective-permute-done | bytes 458784 | tf_op jit(solution)/shard_map/ppermute | solution.py:49
  18.7 1.7 %collective-permute-start.4 = (f32[16,3584]{1,0:T(8,128)S(1)}, f32[16,3584]{1,0:T(8,128)S(1)}, u32[]{:S(2)}, u32[]{:S(2)}) collective-permute-start(f32[16,3584]{1,0:T(8,128)S(1)} %get-tuple-element.32), channel_id=1, source_target_pairs={{0,8},{4,12},{8,0},{12,4},{1,9},{5,13},{9,1},{13,5},{2,10},{6,14},... | collective-permute-start | bytes 688136 | tf_op jit(solution)/shard_map/ppermute | solution.py:49
  20.4 6.2 %collective-permute-done.4.came_ref = f32[16,3584]{1,0:T(8,128)S(1)} collective-permute-done((f32[16,3584]{1,0:T(8,128)S(1)}, f32[16,3584]{1,0:T(8,128)S(1)}, u32[]{:S(2)}, u32[]{:S(2)}) %collective-permute-start.4) | collective-permute-done | bytes 229408 | tf_op jit(solution)/shard_map/ppermute | solution.py:49
  27.2 3.7 %collective-permute-start.5 = (bf16[8,2048]{1,0:T(8,128)(2,1)S(1)}, bf16[8,2048]{1,0:T(8,128)(2,1)S(1)}, u32[]{:S(2)}, u32[]{:S(2)}) collective-permute-start(bf16[8,2048]{1,0:T(8,128)(2,1)S(1)} %get-tuple-element.33), channel_id=1, source_target_pairs={{0,3},{1,2},{2,1},{3,0},{4,7},{5,6},{6,5},{7,4},{8,11},{9,10},{10,... | collective-permute-start | bytes 98312 | tf_op jit(solution)/shard_map/ppermute | solution.py:49
  30.9 0.8 %collective-permute-start.7 = (bf16[8,2048]{1,0:T(8,128)(2,1)S(1)}, bf16[8,2048]{1,0:T(8,128)(2,1)S(1)}, u32[]{:S(2)}, u32[]{:S(2)}) collective-permute-start(bf16[8,2048]{1,0:T(8,128)(2,1)S(1)} %get-tuple-element.35), channel_id=1, source_target_pairs={{0,1},{1,0},{2,3},{3,2},{4,5},{5,4},{6,7},{7,6},{8,9},{9,8},{10,11... | collective-permute-start | bytes 98312 | tf_op jit(solution)/shard_map/ppermute | solution.py:49
  31.7 1.7 %collective-permute-done.5.refs_0_ = bf16[8,2048]{1,0:T(8,128)(2,1)S(1)} collective-permute-done((bf16[8,2048]{1,0:T(8,128)(2,1)S(1)}, bf16[8,2048]{1,0:T(8,128)(2,1)S(1)}, u32[]{:S(2)}, u32[]{:S(2)}) %collective-permute-start.5) | collective-permute-done | bytes 32800 | tf_op jit(solution)/shard_map/ppermute | solution.py:49
  33.3 2.4 %collective-permute-done.6.refs_1_ = bf16[8,2048]{1,0:T(8,128)(2,1)S(1)} collective-permute-done((bf16[8,2048]{1,0:T(8,128)(2,1)S(1)}, bf16[8,2048]{1,0:T(8,128)(2,1)S(1)}, u32[]{:S(2)}, u32[]{:S(2)}) %collective-permute-start.6) | collective-permute-done | bytes 32800 | tf_op jit(solution)/shard_map/ppermute | solution.py:49
  35.8 2.4 %attend.1 = (bf16[8,1536]{1,0:T(8,128)(2,1)S(1)}, bf16[8,1536]{1,0:T(8,128)(2,1)S(1)}, bf16[8,1536]{1,0:T(8,128)(2,1)S(1)}, bf16[8,1536]{1,0:T(8,128)(2,1)S(1)}) custom-call(s32[4]{0:T(128)S(1)} %copy-done.4, bf16[8,2048]{1,0:T(8,128)(2,1)S(1)} %collective-permute-done.5.refs_0_, bf16[8,2048]{1,0:T(8,128)(2,1)S(1)} %collective-permute-done.6.refs_1_, ...), custom_call_target="tpu_custom_call" | custom-call | flops 5000000000 | tf_op jit(solution)/shard_map/attend/pallas_call | solution.py:23
  38.2 1.5 %collective-permute-start.8 = (bf16[8,1536]{1,0:T(8,128)(2,1)S(1)}, bf16[8,1536]{1,0:T(8,128)(2,1)S(1)}, u32[]{:S(2)}, u32[]{:S(2)}) collective-permute-start(bf16[8,1536]{1,0:T(8,128)(2,1)S(1)} %get-tuple-element.37), channel_id=1, source_target_pairs={{0,3},{1,2},{2,1},{3,0},{4,7},{5,6},{6,5},{7,4},{8,11},{9,10},{10,... | collective-permute-start | bytes 73736 | tf_op jit(solution)/shard_map/ppermute | solution.py:49
  39.7 0.6 collective-permute-start.9
  40.3 2.3 %collective-permute-start.10 = (bf16[8,1536]{1,0:T(8,128)(2,1)S(1)}, bf16[8,1536]{1,0:T(8,128)(2,1)S(1)}, u32[]{:S(2)}, u32[]{:S(2)}) collective-permute-start(bf16[8,1536]{1,0:T(8,128)(2,1)S(1)} %get-tuple-element.39), channel_id=1, source_target_pairs={{0,1},{1,0},{2,3},{3,2},{4,5},{5,4},{6,7},{7,6},{8,9},{9,8},{10,11... | collective-permute-start | bytes 73736 | tf_op jit(solution)/shard_map/ppermute | solution.py:49
  42.6 1.2 %collective-permute-done.8.refs_0_ = bf16[8,1536]{1,0:T(8,128)(2,1)S(1)} collective-permute-done((bf16[8,1536]{1,0:T(8,128)(2,1)S(1)}, bf16[8,1536]{1,0:T(8,128)(2,1)S(1)}, u32[]{:S(2)}, u32[]{:S(2)}) %collective-permute-start.8) | collective-permute-done | bytes 24608 | tf_op jit(solution)/shard_map/ppermute | solution.py:49
  45.3 1.5 %collective-permute-start.12 = (bf16[16,3072]{1,0:T(8,128)(2,1)S(1)}, bf16[16,3072]{1,0:T(8,128)(2,1)S(1)}, u32[]{:S(2)}, u32[]{:S(2)}) collective-permute-start(bf16[16,3072]{1,0:T(8,128)(2,1)S(1)} %join.1.refs_0_), channel_id=1, source_target_pairs={{0,8},{4,12},{8,0},{12,4},{1,9},{5,13},{9,1},{13,5},{2,10},{6,14},... | collective-permute-start | bytes 294920 | tf_op jit(solution)/shard_map/ppermute | solution.py:49
  46.8 3.2 %collective-permute-done.12.refs_2_ = bf16[16,3072]{1,0:T(8,128)(2,1)S(1)} collective-permute-done((bf16[16,3072]{1,0:T(8,128)(2,1)S(1)}, bf16[16,3072]{1,0:T(8,128)(2,1)S(1)}, u32[]{:S(2)}, u32[]{:S(2)}) %collective-permute-start.12) | collective-permute-done | bytes 98336 | tf_op jit(solution)/shard_map/ppermute | solution.py:49
  50.0 1.3 %collective-permute-done.13.refs_3_ = bf16[16,3072]{1,0:T(8,128)(2,1)S(1)} collective-permute-done((bf16[16,3072]{1,0:T(8,128)(2,1)S(1)}, bf16[16,3072]{1,0:T(8,128)(2,1)S(1)}, u32[]{:S(2)}, u32[]{:S(2)}) %collective-permute-start.13) | collective-permute-done | bytes 98336 | tf_op jit(solution)/shard_map/ppermute | solution.py:49
  51.3 2.7 %output_part.3 = (f32[64,1792]{1,0:T(8,128)S(1)}, s16[32,1920]{1,0:T(8,128)(2,1)S(1)}) custom-call(s32[2]{0:T(128)S(1)} %pad_add_fusion.refs_1_.me_ref, bf16[16,3072]{1,0:T(8,128)(2,1)S(1)} %join.1.refs_0_, bf16[16,3072]{1,0:T(8,128)(2,1)S(1)} %collective-permute-done.11.refs_1_, bf16[16,3072]{1,0:T(8,128)(2,1)S(1)} %collective-permute-done.12.refs_2_, ...), custom_call_target="tpu_custom_call" | custom-call | flops 704643072 | bytes 393216 | tf_op jit(solution)/shard_map/output_part/pallas_call | solution.py:23
  54.0 1.8 %collective-permute-start.14 = (s16[32,1920]{1,0:T(8,128)(2,1)S(1)}, s16[32,1920]{1,0:T(8,128)(2,1)S(1)}, u32[]{:S(2)}, u32[]{:S(2)}) collective-permute-start(s16[32,1920]{1,0:T(8,128)(2,1)S(1)} %get-tuple-element.42), channel_id=1, source_target_pairs={{0,1},{1,0},{2,3},{3,2},{4,5},{5,4},{6,7},{7,6},{8,9},{9,8},{10,11... | collective-permute-start | bytes 368648 | tf_op jit(solution)/shard_map/ppermute | solution.py:49
  55.9 2.9 %output_part.4 = (f32[64,2048]{1,0:T(8,128)S(1)}, s16[32,2176]{1,0:T(8,128)(2,1)S(1)}) custom-call(s32[2]{0:T(128)S(1)} %pad_add_fusion.refs_1_.me_ref, bf16[16,3072]{1,0:T(8,128)(2,1)S(1)} %join.1.refs_0_, bf16[16,3072]{1,0:T(8,128)(2,1)S(1)} %collective-permute-done.11.refs_1_, bf16[16,3072]{1,0:T(8,128)(2,1)S(1)} %collective-permute-done.12.refs_2_, ...), custom_call_target="tpu_custom_call" | custom-call | flops 805306368 | bytes 393216 | tf_op jit(solution)/shard_map/output_part/pallas_call | solution.py:23
  59.7 1.8 %collective-permute-start.16 = (s16[16,1920]{1,0:T(8,128)(2,1)S(1)}, s16[16,1920]{1,0:T(8,128)(2,1)S(1)}, u32[]{:S(2)}, u32[]{:S(2)}) collective-permute-start(s16[16,1920]{1,0:T(8,128)(2,1)S(1)} %get-tuple-element.47), channel_id=1, source_target_pairs={{0,2},{1,3},{2,0},{3,1},{4,6},{5,7},{6,4},{7,5},{8,10},{9,11},{10,... | collective-permute-start | bytes 184328 | tf_op jit(solution)/shard_map/ppermute | solution.py:49
  61.5 1.6 %output_part.5 = (f32[64,768]{1,0:T(8,128)S(1)}, s16[32,896]{1,0:T(8,128)(2,1)S(1)}) custom-call(s32[2]{0:T(128)S(1)} %pad_add_fusion.refs_1_.me_ref, bf16[16,3072]{1,0:T(8,128)(2,1)S(1)} %join.1.refs_0_, bf16[16,3072]{1,0:T(8,128)(2,1)S(1)} %collective-permute-done.11.refs_1_, bf16[16,3072]{1,0:T(8,128)(2,1)S(1)} %collective-permute-done.12.refs_2_, ...), custom_call_target="tpu_custom_call" | custom-call | flops 301989888 | bytes 393216 | tf_op jit(solution)/shard_map/output_part/pallas_call | solution.py:23
  63.1 1.2 %collective-permute-start.15 = (s16[32,896]{1,0:T(8,128)(2,1)S(1)}, s16[32,896]{1,0:T(8,128)(2,1)S(1)}, u32[]{:S(2)}, u32[]{:S(2)}) collective-permute-start(s16[32,896]{1,0:T(8,128)(2,1)S(1)} %get-tuple-element.46), channel_id=1, source_target_pairs={{0,1},{1,0},{2,3},{3,2},{4,5},{5,4},{6,7},{7,6},{8,9},{9,8},{10,11... | collective-permute-start | bytes 172040 | tf_op jit(solution)/shard_map/ppermute | solution.py:49
  64.3 1.7 %collective-permute-done.18.came_ref = s16[32,2176]{1,0:T(8,128)(2,1)S(1)} collective-permute-done((s16[32,2176]{1,0:T(8,128)(2,1)S(1)}, s16[32,2176]{1,0:T(8,128)(2,1)S(1)}, u32[]{:S(2)}, u32[]{:S(2)}) %collective-permute-start.18) | collective-permute-done | bytes 139296 | tf_op jit(solution)/shard_map/ppermute | solution.py:49
  66.5 0.7 finish.3.refs_0_
  67.5 2.7 %collective-permute-start.17 = (s16[16,896]{1,0:T(8,128)(2,1)S(1)}, s16[16,896]{1,0:T(8,128)(2,1)S(1)}, u32[]{:S(2)}, u32[]{:S(2)}) collective-permute-start(s16[16,896]{1,0:T(8,128)(2,1)S(1)} %get-tuple-element.49), channel_id=1, source_target_pairs={{0,2},{1,3},{2,0},{3,1},{4,6},{5,7},{6,4},{7,5},{8,10},{9,11},{10,... | collective-permute-start | bytes 86024 | tf_op jit(solution)/shard_map/ppermute | solution.py:49
  70.2 1.5 %collective-permute-done.19.came_ref = s16[16,2176]{1,0:T(8,128)(2,1)S(1)} collective-permute-done((s16[16,2176]{1,0:T(8,128)(2,1)S(1)}, s16[16,2176]{1,0:T(8,128)(2,1)S(1)}, u32[]{:S(2)}, u32[]{:S(2)}) %collective-permute-start.19) | collective-permute-done | bytes 69664 | tf_op jit(solution)/shard_map/ppermute | solution.py:49
  71.7 0.7 finish.4.refs_0_
  72.5 0.7 finish.5
  (51 shorter events, 4.7 us)
Async XLA Ops:
  1.3 5.7 %collective-permute-start.2 = (f32[2,64]{1,0:T(2,128)S(1)}, f32[2,64]{1,0:T(2,128)S(1)}, u32[]{:S(2)}, u32[]{:S(2)}) collective-permute-start(f32[2,64]{1,0:T(2,128)S(1)} %pad_maximum_fusion.refs_0_), channel_id=1, source_target_pairs={{0,12},{4,8},{8,4},{12,0},{1,13},{5,9},{9,5},{13,1},{2,14},{6,10},... | collective-permute-start | bytes 1544 | tf_op jit(solution)/shard_map/ppermute | solution.py:49
  3.8 3.6 %collective-permute-start.1 = (f32[2,64]{1,0:T(2,128)S(1)}, f32[2,64]{1,0:T(2,128)S(1)}, u32[]{:S(2)}, u32[]{:S(2)}) collective-permute-start(f32[2,64]{1,0:T(2,128)S(1)} %pad_maximum_fusion.refs_0_), channel_id=1, source_target_pairs={{0,8},{4,12},{8,0},{12,4},{1,9},{5,13},{9,1},{13,5},{2,10},{6,14},... | collective-permute-start | bytes 1544 | tf_op jit(solution)/shard_map/ppermute | solution.py:49
  4.4 2.9 %collective-permute-start = (f32[2,64]{1,0:T(2,128)S(1)}, f32[2,64]{1,0:T(2,128)S(1)}, u32[]{:S(2)}, u32[]{:S(2)}) collective-permute-start(f32[2,64]{1,0:T(2,128)S(1)} %pad_maximum_fusion.refs_0_), channel_id=1, source_target_pairs={{0,4},{4,0},{8,12},{12,8},{1,5},{5,1},{9,13},{13,9},{2,6},{6,2},{1... | collective-permute-start | bytes 1544 | tf_op jit(solution)/shard_map/ppermute | solution.py:49
  4.6 2.8 %copy-start = (bf16[64,4608]{1,0:T(8,128)(2,1)S(1)}, bf16[64,4608]{1,0:T(8,128)(2,1)}, u32[]{:S(2)}) copy-start(bf16[64,4608]{1,0:T(8,128)(2,1)} %refs_4_.5) | copy-start | bytes 1769476
  4.6 2.9 %copy-start.1 = (bf16[1152,512]{1,0:T(8,128)(2,1)S(1)}, bf16[1152,512]{1,0:T(8,128)(2,1)}, u32[]{:S(2)}) copy-start(bf16[1152,512]{1,0:T(8,128)(2,1)} %refs_7_.1) | copy-start | bytes 3538948
  4.6 2.9 %copy-start.2 = (f32[4608]{0:T(1024)S(1)}, f32[4608]{0:T(1024)}, u32[]{:S(2)}) copy-start(f32[4608]{0:T(1024)} %refs_5_.1) | copy-start | bytes 55300
  16.6 2.0 %collective-permute-start.3 = (f32[32,3584]{1,0:T(8,128)S(1)}, f32[32,3584]{1,0:T(8,128)S(1)}, u32[]{:S(2)}, u32[]{:S(2)}) collective-permute-start(f32[32,3584]{1,0:T(8,128)S(1)} %get-tuple-element.30), channel_id=1, source_target_pairs={{0,4},{4,0},{8,12},{12,8},{1,5},{5,1},{9,13},{13,9},{2,6},{6,2},{1... | collective-permute-start | bytes 1376264 | tf_op jit(solution)/shard_map/ppermute | solution.py:49
  18.7 7.9 %collective-permute-start.4 = (f32[16,3584]{1,0:T(8,128)S(1)}, f32[16,3584]{1,0:T(8,128)S(1)}, u32[]{:S(2)}, u32[]{:S(2)}) collective-permute-start(f32[16,3584]{1,0:T(8,128)S(1)} %get-tuple-element.32), channel_id=1, source_target_pairs={{0,8},{4,12},{8,0},{12,4},{1,9},{5,13},{9,1},{13,5},{2,10},{6,14},... | collective-permute-start | bytes 688136 | tf_op jit(solution)/shard_map/ppermute | solution.py:49
  26.6 9.1 %copy-start.3 = (bf16[4,1024,512]{2,1,0:T(8,128)(2,1)S(1)}, bf16[4,1024,512]{2,1,0:T(8,128)(2,1)}, u32[]{:S(2)}) copy-start(bf16[4,1024,512]{2,1,0:T(8,128)(2,1)} %refs_4_.6) | copy-start | bytes 12582916
  26.6 9.1 %copy-start.4 = (s32[4]{0:T(128)S(1)}, s32[4]{0:T(128)}, u32[]{:S(2)}) copy-start(s32[4]{0:T(128)} %lengths_ref.1) | copy-start | bytes 52
  26.6 24.7 %slice-start = ((s8[28311552]{0:T(1024)(128)(4,1)}), s8[4194304]{0:T(1024)(128)(4,1)S(1)}, s32[]{:S(2)}) async-start(s8[28311552]{0:T(1024)(128)(4,1)} %bitcast.4), calls=%async_computation | async-start | bytes 8388608
  26.6 24.7 %slice-start.1 = ((s8[28311552]{0:T(1024)(128)(4,1)}), s8[4194304]{0:T(1024)(128)(4,1)S(1)}, s32[]{:S(2)}) async-start(s8[28311552]{0:T(1024)(128)(4,1)} %bitcast.4), calls=%async_computation.1 | async-start | bytes 8388608
  26.6 24.7 %slice-start.2 = ((s8[28311552]{0:T(1024)(128)(4,1)}), s8[4194304]{0:T(1024)(128)(4,1)S(1)}, s32[]{:S(2)}) async-start(s8[28311552]{0:T(1024)(128)(4,1)} %bitcast.4), calls=%async_computation.2 | async-start | bytes 8388608
  27.2 6.1 %collective-permute-start.5 = (bf16[8,2048]{1,0:T(8,128)(2,1)S(1)}, bf16[8,2048]{1,0:T(8,128)(2,1)S(1)}, u32[]{:S(2)}, u32[]{:S(2)}) collective-permute-start(bf16[8,2048]{1,0:T(8,128)(2,1)S(1)} %get-tuple-element.33), channel_id=1, source_target_pairs={{0,3},{1,2},{2,1},{3,0},{4,7},{5,6},{6,5},{7,4},{8,11},{9,10},{10,... | collective-permute-start | bytes 98312 | tf_op jit(solution)/shard_map/ppermute | solution.py:49
  30.9 4.8 %collective-permute-start.6 = (bf16[8,2048]{1,0:T(8,128)(2,1)S(1)}, bf16[8,2048]{1,0:T(8,128)(2,1)S(1)}, u32[]{:S(2)}, u32[]{:S(2)}) collective-permute-start(bf16[8,2048]{1,0:T(8,128)(2,1)S(1)} %get-tuple-element.34), channel_id=1, source_target_pairs={{0,2},{1,3},{2,0},{3,1},{4,6},{5,7},{6,4},{7,5},{8,10},{9,11},{10,... | collective-permute-start | bytes 98312 | tf_op jit(solution)/shard_map/ppermute | solution.py:49
  30.9 4.8 %collective-permute-start.7 = (bf16[8,2048]{1,0:T(8,128)(2,1)S(1)}, bf16[8,2048]{1,0:T(8,128)(2,1)S(1)}, u32[]{:S(2)}, u32[]{:S(2)}) collective-permute-start(bf16[8,2048]{1,0:T(8,128)(2,1)S(1)} %get-tuple-element.35), channel_id=1, source_target_pairs={{0,1},{1,0},{2,3},{3,2},{4,5},{5,4},{6,7},{7,6},{8,9},{9,8},{10,11... | collective-permute-start | bytes 98312 | tf_op jit(solution)/shard_map/ppermute | solution.py:49
  35.7 15.5 %slice-start.3 = ((s8[28311552]{0:T(1024)(128)(4,1)}), s8[4194304]{0:T(1024)(128)(4,1)S(1)}, s32[]{:S(2)}) async-start(s8[28311552]{0:T(1024)(128)(4,1)} %bitcast.4), calls=%async_computation.3 | async-start | bytes 8388608
  35.7 15.5 %slice-start.4 = ((s8[28311552]{0:T(1024)(128)(4,1)}), s8[4194304]{0:T(1024)(128)(4,1)S(1)}, s32[]{:S(2)}) async-start(s8[28311552]{0:T(1024)(128)(4,1)} %bitcast.4), calls=%async_computation.4 | async-start | bytes 8388608
  38.2 5.7 %collective-permute-start.8 = (bf16[8,1536]{1,0:T(8,128)(2,1)S(1)}, bf16[8,1536]{1,0:T(8,128)(2,1)S(1)}, u32[]{:S(2)}, u32[]{:S(2)}) collective-permute-start(bf16[8,1536]{1,0:T(8,128)(2,1)S(1)} %get-tuple-element.37), channel_id=1, source_target_pairs={{0,3},{1,2},{2,1},{3,0},{4,7},{5,6},{6,5},{7,4},{8,11},{9,10},{10,... | collective-permute-start | bytes 73736 | tf_op jit(solution)/shard_map/ppermute | solution.py:49
  39.7 4.7 %collective-permute-start.9 = (bf16[8,1536]{1,0:T(8,128)(2,1)S(1)}, bf16[8,1536]{1,0:T(8,128)(2,1)S(1)}, u32[]{:S(2)}, u32[]{:S(2)}) collective-permute-start(bf16[8,1536]{1,0:T(8,128)(2,1)S(1)} %get-tuple-element.38), channel_id=1, source_target_pairs={{0,2},{1,3},{2,0},{3,1},{4,6},{5,7},{6,4},{7,5},{8,10},{9,11},{10,... | collective-permute-start | bytes 73736 | tf_op jit(solution)/shard_map/ppermute | solution.py:49
  40.3 4.3 %collective-permute-start.10 = (bf16[8,1536]{1,0:T(8,128)(2,1)S(1)}, bf16[8,1536]{1,0:T(8,128)(2,1)S(1)}, u32[]{:S(2)}, u32[]{:S(2)}) collective-permute-start(bf16[8,1536]{1,0:T(8,128)(2,1)S(1)} %get-tuple-element.39), channel_id=1, source_target_pairs={{0,1},{1,0},{2,3},{3,2},{4,5},{5,4},{6,7},{7,6},{8,9},{9,8},{10,11... | collective-permute-start | bytes 73736 | tf_op jit(solution)/shard_map/ppermute | solution.py:49
  44.7 6.6 %slice-start.5 = ((s8[28311552]{0:T(1024)(128)(4,1)}), s8[4194304]{0:T(1024)(128)(4,1)S(1)}, s32[]{:S(2)}) async-start(s8[28311552]{0:T(1024)(128)(4,1)} %bitcast.4), calls=%async_computation.5 | async-start | bytes 8388608
  44.7 6.6 %slice-start.6 = ((s8[28311552]{0:T(1024)(128)(4,1)}), s8[3145728]{0:T(1024)(128)(4,1)S(1)}, s32[]{:S(2)}) async-start(s8[28311552]{0:T(1024)(128)(4,1)} %bitcast.4), calls=%async_computation.6 | async-start | bytes 6291456
  45.3 4.7 %collective-permute-start.12 = (bf16[16,3072]{1,0:T(8,128)(2,1)S(1)}, bf16[16,3072]{1,0:T(8,128)(2,1)S(1)}, u32[]{:S(2)}, u32[]{:S(2)}) collective-permute-start(bf16[16,3072]{1,0:T(8,128)(2,1)S(1)} %join.1.refs_0_), channel_id=1, source_target_pairs={{0,8},{4,12},{8,0},{12,4},{1,9},{5,13},{9,1},{13,5},{2,10},{6,14},... | collective-permute-start | bytes 294920 | tf_op jit(solution)/shard_map/ppermute | solution.py:49
  46.8 3.2 %collective-permute-start.11 = (bf16[16,3072]{1,0:T(8,128)(2,1)S(1)}, bf16[16,3072]{1,0:T(8,128)(2,1)S(1)}, u32[]{:S(2)}, u32[]{:S(2)}) collective-permute-start(bf16[16,3072]{1,0:T(8,128)(2,1)S(1)} %join.1.refs_0_), channel_id=1, source_target_pairs={{0,4},{4,0},{8,12},{12,8},{1,5},{5,1},{9,13},{13,9},{2,6},{6,2},{1... | collective-permute-start | bytes 294920 | tf_op jit(solution)/shard_map/ppermute | solution.py:49
  50.0 1.3 %collective-permute-start.13 = (bf16[16,3072]{1,0:T(8,128)(2,1)S(1)}, bf16[16,3072]{1,0:T(8,128)(2,1)S(1)}, u32[]{:S(2)}, u32[]{:S(2)}) collective-permute-start(bf16[16,3072]{1,0:T(8,128)(2,1)S(1)} %collective-permute-done.12.refs_2_), channel_id=1, source_target_pairs={{0,4},{4,0},{8,12},{12,8},{1,5},{5,1},{9,13},{13,9},{2,6},{6,2},{1... | collective-permute-start | bytes 294920 | tf_op jit(solution)/shard_map/ppermute | solution.py:49
  54.0 5.5 %collective-permute-start.14 = (s16[32,1920]{1,0:T(8,128)(2,1)S(1)}, s16[32,1920]{1,0:T(8,128)(2,1)S(1)}, u32[]{:S(2)}, u32[]{:S(2)}) collective-permute-start(s16[32,1920]{1,0:T(8,128)(2,1)S(1)} %get-tuple-element.42), channel_id=1, source_target_pairs={{0,1},{1,0},{2,3},{3,2},{4,5},{5,4},{6,7},{7,6},{8,9},{9,8},{10,11... | collective-permute-start | bytes 368648 | tf_op jit(solution)/shard_map/ppermute | solution.py:49
  58.8 7.2 %collective-permute-start.18 = (s16[32,2176]{1,0:T(8,128)(2,1)S(1)}, s16[32,2176]{1,0:T(8,128)(2,1)S(1)}, u32[]{:S(2)}, u32[]{:S(2)}) collective-permute-start(s16[32,2176]{1,0:T(8,128)(2,1)S(1)} %get-tuple-element.50), channel_id=1, source_target_pairs={{0,1},{1,0},{2,3},{3,2},{4,5},{5,4},{6,7},{7,6},{8,9},{9,8},{10,11... | collective-permute-start | bytes 417800 | tf_op jit(solution)/shard_map/ppermute | solution.py:49
  59.7 6.8 %collective-permute-start.16 = (s16[16,1920]{1,0:T(8,128)(2,1)S(1)}, s16[16,1920]{1,0:T(8,128)(2,1)S(1)}, u32[]{:S(2)}, u32[]{:S(2)}) collective-permute-start(s16[16,1920]{1,0:T(8,128)(2,1)S(1)} %get-tuple-element.47), channel_id=1, source_target_pairs={{0,2},{1,3},{2,0},{3,1},{4,6},{5,7},{6,4},{7,5},{8,10},{9,11},{10,... | collective-permute-start | bytes 184328 | tf_op jit(solution)/shard_map/ppermute | solution.py:49
  63.1 4.2 %collective-permute-start.15 = (s16[32,896]{1,0:T(8,128)(2,1)S(1)}, s16[32,896]{1,0:T(8,128)(2,1)S(1)}, u32[]{:S(2)}, u32[]{:S(2)}) collective-permute-start(s16[32,896]{1,0:T(8,128)(2,1)S(1)} %get-tuple-element.46), channel_id=1, source_target_pairs={{0,1},{1,0},{2,3},{3,2},{4,5},{5,4},{6,7},{7,6},{8,9},{9,8},{10,11... | collective-permute-start | bytes 172040 | tf_op jit(solution)/shard_map/ppermute | solution.py:49
  66.3 5.5 %collective-permute-start.19 = (s16[16,2176]{1,0:T(8,128)(2,1)S(1)}, s16[16,2176]{1,0:T(8,128)(2,1)S(1)}, u32[]{:S(2)}, u32[]{:S(2)}) collective-permute-start(s16[16,2176]{1,0:T(8,128)(2,1)S(1)} %get-tuple-element.52), channel_id=1, source_target_pairs={{0,2},{1,3},{2,0},{3,1},{4,6},{5,7},{6,4},{7,5},{8,10},{9,11},{10,... | collective-permute-start | bytes 208904 | tf_op jit(solution)/shard_map/ppermute | solution.py:49
  67.5 5.0 %collective-permute-start.17 = (s16[16,896]{1,0:T(8,128)(2,1)S(1)}, s16[16,896]{1,0:T(8,128)(2,1)S(1)}, u32[]{:S(2)}, u32[]{:S(2)}) collective-permute-start(s16[16,896]{1,0:T(8,128)(2,1)S(1)} %get-tuple-element.49), channel_id=1, source_target_pairs={{0,2},{1,3},{2,0},{3,1},{4,6},{5,7},{6,4},{7,5},{8,10},{9,11},{10,... | collective-permute-start | bytes 86024 | tf_op jit(solution)/shard_map/ppermute | solution.py:49

commit v11 on v10

--- a/solution.py
+++ b/solution.py
@@ -11,7 +11,6 @@
 MIB = 1 << 20
 FULL = pl.BlockSpec(memory_space=pltpu.VMEM)
 ANY = pl.BlockSpec(memory_space=pl.ANY)
-SCALAR = pl.BlockSpec(memory_space=pltpu.SMEM)
 STEPS = 32700.0
 TINY = 1e-37
 LANES = 128
@@ -110,7 +109,7 @@
     return [LANES * n for n in blocks]
 
 
-def project_kernel(many, width_all, count, narrow_count, me_ref, *refs):
+def project_kernel(many, width_all, count, narrow_count, *refs):
     stat_refs, refs = refs[:many], refs[many:]
     x_ref, gain_ref, w_ref, kv_ref, first_ref, kept_ref, sent_ref, normed, own, *blocks, sems = refs
     rows, width = x_ref.shape
@@ -126,7 +125,7 @@
     ahead = 3
     for fetch in fetches[:ahead]:
         fetch.start()
-    me, narrow = me_ref[0], me_ref[1]
+    me, narrow = lax.axis_index("wide"), lax.axis_index("narrow")
     stats = stat_refs[0][...]
     for ref in stat_refs[1:]:
         stats = stats + ref[...]
@@ -174,7 +173,7 @@
         products(blocks[g], starts[g + 1])
 
 
-def project(me, stats, x, gain, w, kv, first, width_all, count, narrow_count):
+def project(stats, x, gain, w, kv, first, width_all, count, narrow_count):
     rows, width = x.shape
     queries = w.shape[1]
     blocks = row_blocks(width)[1:]
@@ -182,8 +181,8 @@
     return call(
         functools.partial(project_kernel, len(stats), width_all, count, narrow_count),
         (half, half),
-        (me, *stats, x, gain, in_hbm(w), in_vmem(kv), in_vmem(first)),
-        [SCALAR] + [FULL] * (len(stats) + 2) + [ANY] + [FULL] * 2,
+        (*stats, x, gain, in_hbm(w), in_vmem(kv), in_vmem(first)),
+        [FULL] * (len(stats) + 2) + [ANY] + [FULL] * 2,
         "project",
         scratch=[
             pltpu.VMEM((rows, width), jnp.bfloat16),
@@ -215,9 +214,10 @@
     )
 
 
-def split_kernel(queries, me_ref, kept_ref, came_ref, *refs):
+def split_kernel(queries, kept_ref, came_ref, *refs):
     out_refs, slots = refs[:-1], refs[-1]
     count = len(out_refs)
+    narrow = lax.axis_index("narrow")
     total = kept_ref[...] + came_ref[...]
     rows, columns = total.shape[0] // count, total.shape[1]
     half = slots.shape[1]
@@ -229,7 +229,7 @@
         slots[j * PAD + rows : (j + 1) * PAD, : columns - half] = total[mine, half:]
         slots[j * PAD + rows : (j + 1) * PAD, columns - half :] = low[mine, :]
     for d, out_ref in enumerate(out_refs):
-        out_ref[...] = slots[pl.ds(pl.multiple_of((me_ref[1] ^ d) * PAD, PAD), PAD), :].astype(jnp.bfloat16)
+        out_ref[...] = slots[pl.ds(pl.multiple_of((narrow ^ d) * PAD, PAD), PAD), :].astype(jnp.bfloat16)
 
 
 def attend_kernel(head_dim, count, lengths_ref, *refs):
@@ -269,7 +269,7 @@
             * scaling
         )
         own_score = jnp.sum(query * fresh[r : r + 1, :head_dim], axis=1, keepdims=True) * scaling
-        valid = place < lengths_ref[r]
+        valid = place < lengths_ref[:, r : r + 1]
         top = jnp.maximum(jnp.max(jnp.where(valid, scores, -jnp.inf), axis=1, keepdims=True), own_score)
         weights = jnp.where(valid, jnp.exp(scores - top), 0.0)
         own_weight = jnp.exp(own_score - top)
@@ -298,7 +298,7 @@
         functools.partial(attend_kernel, head_dim, count),
         [jax.ShapeDtypeStruct((PAD, queries // 2), jnp.bfloat16)] * count,
         (lengths, *came[::-1], in_vmem(kv)),
-        [SCALAR] + [FULL] * (count + 1),
+        [FULL] * (count + 2),
         "attend",
         scratch=[
             pltpu.VMEM((slabs, all_heads * PAD, LANES), jnp.float32),
@@ -309,13 +309,13 @@
     )
 
 
-def join_kernel(me_ref, *refs):
+def join_kernel(*refs):
     count = len(refs) - 2
     out_ref, joined = refs[-2:]
     half = joined.shape[1]
     rows = out_ref.shape[0] // count
     for d in range(count):
-        at = pl.ds(pl.multiple_of((me_ref[1] ^ d) * PAD, PAD), PAD)
+        at = pl.ds(pl.multiple_of((lax.axis_index("narrow") ^ d) * PAD, PAD), PAD)
         joined[at, :] = refs[count - 1 - d][...].astype(jnp.float32)
     for side in range(2):
         came = [joined[j * PAD + side * rows : j * PAD + (side + 1) * rows, :] for j in range(count)]
@@ -335,14 +335,14 @@
     return ref[:, :width].astype(jnp.int32).astype(jnp.float32) * (jnp.exp2(power) * (1.0 / STEPS))
 
 
-def output_kernel(start, count, narrow_count, me_ref, *refs):
+def output_kernel(start, count, narrow_count, *refs):
     x_refs, w_ref, (sums_ref, sent_ref) = refs[:count], refs[count], refs[-2:]
     block = x_refs[0].shape[0]
     ratio = count // narrow_count
     places = []
     for d in range(count):
-        wide = me_ref[0] ^ d
-        apart = (wide // ratio) ^ me_ref[1]
+        wide = lax.axis_index("wide") ^ d
+        apart = (wide // ratio) ^ lax.axis_index("narrow")
         place = jnp.int32(0)
         for k, distance in enumerate(halving_order(narrow_count)):
             place = jnp.where(apart == distance, k, place)
@@ -354,7 +354,7 @@
     code(sums_ref[sums_ref.shape[0] // 2 :, :], sent_ref)
 
 
-def output_part(me, blocks, w, start, columns, narrow_count, after):
+def output_part(blocks, w, start, columns, narrow_count, after):
     count = len(blocks)
     block, depth = blocks[0].shape
     rows = count * block
@@ -364,8 +364,8 @@
             jax.ShapeDtypeStruct((rows, columns), jnp.float32),
             jax.ShapeDtypeStruct((rows // 2, columns + LANES), jnp.int16),
         ),
-        (me, *blocks, in_vmem(w), *after),
-        [SCALAR] + [FULL] * (count + 1) + [ANY] * len(after),
+        (*blocks, in_vmem(w), *after),
+        [FULL] * (count + 1) + [ANY] * len(after),
         "output_part",
         limit=8,
         flops=2 * rows * depth * columns,
@@ -423,7 +423,6 @@
 def local(activations, norm_gain, query_weight, kv_weight, out_weight, kv_cache, lengths):
     wide_count = lax.axis_size("wide")
     narrow_count = lax.axis_size("narrow")
-    me = jnp.stack([lax.axis_index("wide"), lax.axis_index("narrow")]).astype(jnp.int32)
     own_rows, head_dim = kv_cache.shape[0], kv_cache.shape[2] // 2
     assert PAD == 2 * own_rows
     rows, width = activations.shape
@@ -431,9 +430,8 @@
     columns = out_weight.shape[1]
     values = activations.astype(jnp.float32)
     stats = jnp.stack([jnp.sum(values, axis=1), jnp.sum(values * values, axis=1)])
-    first_part = fetch(query_weight, row_blocks(width)[0], [stats, me])
+    first_part = fetch(query_weight, row_blocks(width)[0], [stats])
     kept, sent = project(
-        me,
         sent_apart(stats, "wide"),
         activations,
         norm_gain,
@@ -451,18 +449,18 @@
     split = call(
         functools.partial(split_kernel, queries),
         [jax.ShapeDtypeStruct((PAD, queries // 2 + 2 * head_dim), jnp.bfloat16)] * narrow_count,
-        (me, kept, swap(sent, "wide", d)),
-        [SCALAR] + [FULL] * 2,
+        (kept, swap(sent, "wide", d)),
+        [FULL] * 2,
         "split",
         scratch=[pltpu.VMEM((narrow_count * PAD, queries // 2 + 2 * head_dim), jnp.float32)],
         flops=BESIDE,
     )
-    context = attend(lengths, exchange(split, "narrow"), kv_cache, head_dim, queries)
+    context = attend(lengths[None], exchange(split, "narrow"), kv_cache, head_dim, queries)
     returned = call(
         join_kernel,
         jax.ShapeDtypeStruct((narrow_count * own_rows, queries), jnp.bfloat16),
-        (me, *exchange(context, "narrow")[::-1]),
-        [SCALAR] + [FULL] * narrow_count,
+        exchange(context, "narrow")[::-1],
+        [FULL] * narrow_count,
         "join",
         scratch=[pltpu.VMEM((narrow_count * PAD, queries // 2), jnp.float32)],
         flops=BESIDE,
@@ -481,7 +479,7 @@
         cut_sums.append((kept, swap(sent, "narrow", d)))
 
     for start, end in zip(ends, ends[1:]):
-        kept, sent = output_part(me, gathered, out_weight, start, end - start, narrow_count, halved[-1:])
+        kept, sent = output_part(gathered, out_weight, start, end - start, narrow_count, halved[-1:])
         if last:
             exchange_cut(*last, [kept])
         last = (kept, sent)

time: 73.3 us -> 69.7 us (0.951)
  Pallas kernels: 25.2 us -> 21.3 us
  waiting for transfers between devices: 22.3 us -> 23.9 us
  starting transfers between devices: 23.9 us -> 22.7 us
    pallas_call x12, Pallas kernels: 23.1 us -> 19.1 us  [call(): pl.pallas_call(kernel, out_shape=outs, in_specs=specs, out_specs=jax.tree...]
    ppermute x20, waiting for transfers between devices: 22.3 us -> 23.9 us  [swap(): return lax.ppermute(x, axis, [(i, i ^ distance) for i in range(count)])]
    ppermute x20, starting transfers between devices: 23.9 us -> 22.7 us  [swap(): return lax.ppermute(x, axis, [(i, i ^ distance) for i in range(count)])]
  transfers between devices with their start and end apart: 20 -> 20, of which waited for: 14 -> 14; matrix products, arithmetic and copies ran while one was open for 0% -> 0% of each run, Pallas kernels for 12% -> 11%
where the time goes in v11:
time: 69.7 us; the launch traced here: 69.5 us
  waiting for transfers between devices  23.9 us (34%)
  starting transfers between devices  22.7 us (33%)
  Pallas kernels  21.3 us (31%)
  other arithmetic  1.32 us (2%)
    ppermute x20, waiting for transfers between devices, swap(): return lax.ppermute(x, axis, [(i, i ^ distance) for i in range(count)])  23.9 us
    ppermute x20, starting transfers between devices, swap(): return lax.ppermute(x, axis, [(i, i ^ distance) for i in range(count)])  22.7 us
    pallas_call x12, Pallas kernels, call(): pl.pallas_call(kernel, out_shape=outs, in_specs=specs, out_specs=jax.tree...  19.1 us
    pallas_call x3, Pallas kernels, finish(): pl.pallas_call(functools.partial(finish_kernel, start), out_shape=pltpu.H...  2.15 us
  transfers between devices with their start and end apart: 20, of which 14 were waited for; matrix products, arithmetic and copies ran while one was open for 0% of the time, Pallas kernels for 11%

profile of v11, /device:TPU:0, one launch (start us, length us, event | category | flops | bytes accessed | tf_op | source)
XLA Modules:
  0.0 69.5 jit_solution(9960175851703732368)
XLA Ops:
  0.0 1.3 %convert_reduce_fusion = (f32[64]{0:T(128)S(1)}, f32[64]{0:T(128)S(1)}) fusion(bf16[64,4608]{1,0:T(8,128)(2,1)} %refs_4_.5), kind=kLoop, calls=%fused_computation.1 | loop fusion | flops 1179520 | bytes 590336 | tf_op jit(solution)/shard_map/reduce_sum | solution.py:432
  1.4 2.5 %collective-permute-start.2 = (f32[2,64]{1,0:T(2,128)S(1)}, f32[2,64]{1,0:T(2,128)S(1)}, u32[]{:S(2)}, u32[]{:S(2)}) collective-permute-start(f32[2,64]{1,0:T(2,128)S(1)} %pad_maximum_fusion.refs_0_), channel_id=1, source_target_pairs={{0,12},{4,8},{8,4},{12,0},{1,13},{5,9},{9,5},{13,1},{2,14},{6,10},... | collective-permute-start | bytes 1544 | tf_op jit(solution)/shard_map/ppermute | solution.py:48
  4.5 2.3 %fetch_query_weight.1.refs_8_ = bf16[768,3072]{1,0:T(8,128)(2,1)S(1)} custom-call(bf16[4608,3072]{1,0:T(8,128)(2,1)} %refs_6_.1, f32[2,64]{1,0:T(2,128)S(1)} %pad_maximum_fusion.refs_0_), custom_call_target="tpu_custom_call" | custom-call | bytes 4718592 | tf_op jit(solution)/shard_map/fetch_query_weight/pallas_call | solution.py:22
  7.4 8.6 %project.1 = (f32[32,3584]{1,0:T(8,128)S(1)}, f32[32,3584]{1,0:T(8,128)S(1)}) custom-call(f32[2,64]{1,0:T(2,128)S(1)} %pad_maximum_fusion.refs_0_, f32[2,64]{1,0:T(2,128)S(1)} %collective-permute-done.refs_1_, f32[2,64]{1,0:T(2,128)S(1)} %collective-permute-done.1.refs_2_, f32[2,64]{1,0:T(2,128)S(1)} %collective-permute-done.2.refs_3_, ...), custom_call_target="tpu_custom_call" | custom-call | flops 1811939328 | bytes 23592960 | tf_op jit(solution)/shard_map/project/pallas_call | solution.py:22
  16.2 1.8 %collective-permute-done.3.came_ref = f32[32,3584]{1,0:T(8,128)S(1)} collective-permute-done((f32[32,3584]{1,0:T(8,128)S(1)}, f32[32,3584]{1,0:T(8,128)S(1)}, u32[]{:S(2)}, u32[]{:S(2)}) %collective-permute-start.3) | collective-permute-done | bytes 458784 | tf_op jit(solution)/shard_map/ppermute | solution.py:48
  18.0 1.3 %collective-permute-start.4 = (f32[16,3584]{1,0:T(8,128)S(1)}, f32[16,3584]{1,0:T(8,128)S(1)}, u32[]{:S(2)}, u32[]{:S(2)}) collective-permute-start(f32[16,3584]{1,0:T(8,128)S(1)} %get-tuple-element.32), channel_id=1, source_target_pairs={{0,8},{4,12},{8,0},{12,4},{1,9},{5,13},{9,1},{13,5},{2,10},{6,14},... | collective-permute-start | bytes 688136 | tf_op jit(solution)/shard_map/ppermute | solution.py:48
  19.3 6.4 %collective-permute-done.4.came_ref = f32[16,3584]{1,0:T(8,128)S(1)} collective-permute-done((f32[16,3584]{1,0:T(8,128)S(1)}, f32[16,3584]{1,0:T(8,128)S(1)}, u32[]{:S(2)}, u32[]{:S(2)}) %collective-permute-start.4) | collective-permute-done | bytes 229408 | tf_op jit(solution)/shard_map/ppermute | solution.py:48
  25.8 3.7 %collective-permute-start.5 = (bf16[8,2048]{1,0:T(8,128)(2,1)S(1)}, bf16[8,2048]{1,0:T(8,128)(2,1)S(1)}, u32[]{:S(2)}, u32[]{:S(2)}) collective-permute-start(bf16[8,2048]{1,0:T(8,128)(2,1)S(1)} %get-tuple-element.33), channel_id=1, source_target_pairs={{0,3},{1,2},{2,1},{3,0},{4,7},{5,6},{6,5},{7,4},{8,11},{9,10},{10,... | collective-permute-start | bytes 98312 | tf_op jit(solution)/shard_map/ppermute | solution.py:48
  29.5 0.8 %collective-permute-start.7 = (bf16[8,2048]{1,0:T(8,128)(2,1)S(1)}, bf16[8,2048]{1,0:T(8,128)(2,1)S(1)}, u32[]{:S(2)}, u32[]{:S(2)}) collective-permute-start(bf16[8,2048]{1,0:T(8,128)(2,1)S(1)} %get-tuple-element.35), channel_id=1, source_target_pairs={{0,1},{1,0},{2,3},{3,2},{4,5},{5,4},{6,7},{7,6},{8,9},{9,8},{10,11... | collective-permute-start | bytes 98312 | tf_op jit(solution)/shard_map/ppermute | solution.py:48
  30.3 1.5 %collective-permute-done.5.refs_0_ = bf16[8,2048]{1,0:T(8,128)(2,1)S(1)} collective-permute-done((bf16[8,2048]{1,0:T(8,128)(2,1)S(1)}, bf16[8,2048]{1,0:T(8,128)(2,1)S(1)}, u32[]{:S(2)}, u32[]{:S(2)}) %collective-permute-start.5) | collective-permute-done | bytes 32800 | tf_op jit(solution)/shard_map/ppermute | solution.py:48
  31.8 2.5 %collective-permute-done.6.refs_1_ = bf16[8,2048]{1,0:T(8,128)(2,1)S(1)} collective-permute-done((bf16[8,2048]{1,0:T(8,128)(2,1)S(1)}, bf16[8,2048]{1,0:T(8,128)(2,1)S(1)}, u32[]{:S(2)}, u32[]{:S(2)}) %collective-permute-start.6) | collective-permute-done | bytes 32800 | tf_op jit(solution)/shard_map/ppermute | solution.py:48
  34.3 1.9 %attend.1 = (bf16[8,1536]{1,0:T(8,128)(2,1)S(1)}, bf16[8,1536]{1,0:T(8,128)(2,1)S(1)}, bf16[8,1536]{1,0:T(8,128)(2,1)S(1)}, bf16[8,1536]{1,0:T(8,128)(2,1)S(1)}) custom-call(s32[1,4]{1,0:T(1,128)S(1)} %bitcast.5, bf16[8,2048]{1,0:T(8,128)(2,1)S(1)} %collective-permute-done.5.refs_0_, bf16[8,2048]{1,0:T(8,128)(2,1)S(1)} %collective-permute-done.6.refs_1_, ...), custom_call_target="tpu_custom_call" | custom-call | flops 5000000000 | tf_op jit(solution)/shard_map/attend/pallas_call | solution.py:22
  36.2 1.5 %collective-permute-start.8 = (bf16[8,1536]{1,0:T(8,128)(2,1)S(1)}, bf16[8,1536]{1,0:T(8,128)(2,1)S(1)}, u32[]{:S(2)}, u32[]{:S(2)}) collective-permute-start(bf16[8,1536]{1,0:T(8,128)(2,1)S(1)} %get-tuple-element.37), channel_id=1, source_target_pairs={{0,3},{1,2},{2,1},{3,0},{4,7},{5,6},{6,5},{7,4},{8,11},{9,10},{10,... | collective-permute-start | bytes 73736 | tf_op jit(solution)/shard_map/ppermute | solution.py:48
  38.4 2.3 %collective-permute-start.10 = (bf16[8,1536]{1,0:T(8,128)(2,1)S(1)}, bf16[8,1536]{1,0:T(8,128)(2,1)S(1)}, u32[]{:S(2)}, u32[]{:S(2)}) collective-permute-start(bf16[8,1536]{1,0:T(8,128)(2,1)S(1)} %get-tuple-element.39), channel_id=1, source_target_pairs={{0,1},{1,0},{2,3},{3,2},{4,5},{5,4},{6,7},{7,6},{8,9},{9,8},{10,11... | collective-permute-start | bytes 73736 | tf_op jit(solution)/shard_map/ppermute | solution.py:48
  40.7 1.2 %collective-permute-done.8.refs_0_ = bf16[8,1536]{1,0:T(8,128)(2,1)S(1)} collective-permute-done((bf16[8,1536]{1,0:T(8,128)(2,1)S(1)}, bf16[8,1536]{1,0:T(8,128)(2,1)S(1)}, u32[]{:S(2)}, u32[]{:S(2)}) %collective-permute-start.8) | collective-permute-done | bytes 24608 | tf_op jit(solution)/shard_map/ppermute | solution.py:48
  42.8 1.3 %collective-permute-start.12 = (bf16[16,3072]{1,0:T(8,128)(2,1)S(1)}, bf16[16,3072]{1,0:T(8,128)(2,1)S(1)}, u32[]{:S(2)}, u32[]{:S(2)}) collective-permute-start(bf16[16,3072]{1,0:T(8,128)(2,1)S(1)} %join.1.refs_0_), channel_id=1, source_target_pairs={{0,8},{4,12},{8,0},{12,4},{1,9},{5,13},{9,1},{13,5},{2,10},{6,14},... | collective-permute-start | bytes 294920 | tf_op jit(solution)/shard_map/ppermute | solution.py:48
  44.1 3.4 %collective-permute-done.12.refs_2_ = bf16[16,3072]{1,0:T(8,128)(2,1)S(1)} collective-permute-done((bf16[16,3072]{1,0:T(8,128)(2,1)S(1)}, bf16[16,3072]{1,0:T(8,128)(2,1)S(1)}, u32[]{:S(2)}, u32[]{:S(2)}) %collective-permute-start.12) | collective-permute-done | bytes 98336 | tf_op jit(solution)/shard_map/ppermute | solution.py:48
  47.5 1.3 %collective-permute-done.13.refs_3_ = bf16[16,3072]{1,0:T(8,128)(2,1)S(1)} collective-permute-done((bf16[16,3072]{1,0:T(8,128)(2,1)S(1)}, bf16[16,3072]{1,0:T(8,128)(2,1)S(1)}, u32[]{:S(2)}, u32[]{:S(2)}) %collective-permute-start.13) | collective-permute-done | bytes 98336 | tf_op jit(solution)/shard_map/ppermute | solution.py:48
  48.8 2.1 %output_part.3 = (f32[64,1792]{1,0:T(8,128)S(1)}, s16[32,1920]{1,0:T(8,128)(2,1)S(1)}) custom-call(bf16[16,3072]{1,0:T(8,128)(2,1)S(1)} %join.1.refs_0_, bf16[16,3072]{1,0:T(8,128)(2,1)S(1)} %collective-permute-done.11.refs_1_, bf16[16,3072]{1,0:T(8,128)(2,1)S(1)} %collective-permute-done.12.refs_2_, bf16[16,3072]{1,0:T(8,128)(2,1)S(1)} %collective-permute-done.13.refs_3_, ...), custom_call_target="tpu_custom_call" | custom-call | flops 704643072 | bytes 393216 | tf_op jit(solution)/shard_map/output_part/pallas_call | solution.py:22
  51.0 1.8 %collective-permute-start.14 = (s16[32,1920]{1,0:T(8,128)(2,1)S(1)}, s16[32,1920]{1,0:T(8,128)(2,1)S(1)}, u32[]{:S(2)}, u32[]{:S(2)}) collective-permute-start(s16[32,1920]{1,0:T(8,128)(2,1)S(1)} %get-tuple-element.42), channel_id=1, source_target_pairs={{0,1},{1,0},{2,3},{3,2},{4,5},{5,4},{6,7},{7,6},{8,9},{9,8},{10,11... | collective-permute-start | bytes 368648 | tf_op jit(solution)/shard_map/ppermute | solution.py:48
  52.8 2.4 %output_part.4 = (f32[64,2048]{1,0:T(8,128)S(1)}, s16[32,2176]{1,0:T(8,128)(2,1)S(1)}) custom-call(bf16[16,3072]{1,0:T(8,128)(2,1)S(1)} %join.1.refs_0_, bf16[16,3072]{1,0:T(8,128)(2,1)S(1)} %collective-permute-done.11.refs_1_, bf16[16,3072]{1,0:T(8,128)(2,1)S(1)} %collective-permute-done.12.refs_2_, bf16[16,3072]{1,0:T(8,128)(2,1)S(1)} %collective-permute-done.13.refs_3_, ...), custom_call_target="tpu_custom_call" | custom-call | flops 805306368 | bytes 393216 | tf_op jit(solution)/shard_map/output_part/pallas_call | solution.py:22
  55.5 0.9 %collective-permute-done.14.came_ref = s16[32,1920]{1,0:T(8,128)(2,1)S(1)} collective-permute-done((s16[32,1920]{1,0:T(8,128)(2,1)S(1)}, s16[32,1920]{1,0:T(8,128)(2,1)S(1)}, u32[]{:S(2)}, u32[]{:S(2)}) %collective-permute-start.14) | collective-permute-done | bytes 122912 | tf_op jit(solution)/shard_map/ppermute | solution.py:48
  56.6 1.8 %collective-permute-start.16 = (s16[16,1920]{1,0:T(8,128)(2,1)S(1)}, s16[16,1920]{1,0:T(8,128)(2,1)S(1)}, u32[]{:S(2)}, u32[]{:S(2)}) collective-permute-start(s16[16,1920]{1,0:T(8,128)(2,1)S(1)} %get-tuple-element.47), channel_id=1, source_target_pairs={{0,2},{1,3},{2,0},{3,1},{4,6},{5,7},{6,4},{7,5},{8,10},{9,11},{10,... | collective-permute-start | bytes 184328 | tf_op jit(solution)/shard_map/ppermute | solution.py:48
  58.4 1.0 %output_part.5 = (f32[64,768]{1,0:T(8,128)S(1)}, s16[32,896]{1,0:T(8,128)(2,1)S(1)}) custom-call(bf16[16,3072]{1,0:T(8,128)(2,1)S(1)} %join.1.refs_0_, bf16[16,3072]{1,0:T(8,128)(2,1)S(1)} %collective-permute-done.11.refs_1_, bf16[16,3072]{1,0:T(8,128)(2,1)S(1)} %collective-permute-done.12.refs_2_, bf16[16,3072]{1,0:T(8,128)(2,1)S(1)} %collective-permute-done.13.refs_3_, ...), custom_call_target="tpu_custom_call" | custom-call | flops 301989888 | bytes 393216 | tf_op jit(solution)/shard_map/output_part/pallas_call | solution.py:22
  59.5 1.2 %collective-permute-start.15 = (s16[32,896]{1,0:T(8,128)(2,1)S(1)}, s16[32,896]{1,0:T(8,128)(2,1)S(1)}, u32[]{:S(2)}, u32[]{:S(2)}) collective-permute-start(s16[32,896]{1,0:T(8,128)(2,1)S(1)} %get-tuple-element.46), channel_id=1, source_target_pairs={{0,1},{1,0},{2,3},{3,2},{4,5},{5,4},{6,7},{7,6},{8,9},{9,8},{10,11... | collective-permute-start | bytes 172040 | tf_op jit(solution)/shard_map/ppermute | solution.py:48
  60.7 1.2 %collective-permute-done.18.came_ref = s16[32,2176]{1,0:T(8,128)(2,1)S(1)} collective-permute-done((s16[32,2176]{1,0:T(8,128)(2,1)S(1)}, s16[32,2176]{1,0:T(8,128)(2,1)S(1)}, u32[]{:S(2)}, u32[]{:S(2)}) %collective-permute-start.18) | collective-permute-done | bytes 139296 | tf_op jit(solution)/shard_map/ppermute | solution.py:48
  62.1 0.7 %collective-permute-start.19 = (s16[16,2176]{1,0:T(8,128)(2,1)S(1)}, s16[16,2176]{1,0:T(8,128)(2,1)S(1)}, u32[]{:S(2)}, u32[]{:S(2)}) collective-permute-start(s16[16,2176]{1,0:T(8,128)(2,1)S(1)} %get-tuple-element.52), channel_id=1, source_target_pairs={{0,2},{1,3},{2,0},{3,1},{4,6},{5,7},{6,4},{7,5},{8,10},{9,11},{10,... | collective-permute-start | bytes 208904 | tf_op jit(solution)/shard_map/ppermute | solution.py:48
  62.8 0.7 %finish.3.refs_0_ = bf16[16,4608]{1,0:T(8,128)(2,1)} custom-call(f32[16,1792]{1,0:T(8,128)S(1)} %get-tuple-element.44.refs_5_.kept_ref, s16[16,1920]{1,0:T(8,128)(2,1)S(1)} %collective-permute-done.16.came_ref), custom_call_target="tpu_custom_call" | custom-call | bytes 229376 | tf_op jit(solution)/shard_map/finish/pallas_call | solution.py:410
  64.0 2.0 %collective-permute-start.17 = (s16[16,896]{1,0:T(8,128)(2,1)S(1)}, s16[16,896]{1,0:T(8,128)(2,1)S(1)}, u32[]{:S(2)}, u32[]{:S(2)}) collective-permute-start(s16[16,896]{1,0:T(8,128)(2,1)S(1)} %get-tuple-element.49), channel_id=1, source_target_pairs={{0,2},{1,3},{2,0},{3,1},{4,6},{5,7},{6,4},{7,5},{8,10},{9,11},{10,... | collective-permute-start | bytes 86024 | tf_op jit(solution)/shard_map/ppermute | solution.py:48
  66.1 2.0 %collective-permute-done.19.came_ref = s16[16,2176]{1,0:T(8,128)(2,1)S(1)} collective-permute-done((s16[16,2176]{1,0:T(8,128)(2,1)S(1)}, s16[16,2176]{1,0:T(8,128)(2,1)S(1)}, u32[]{:S(2)}, u32[]{:S(2)}) %collective-permute-start.19) | collective-permute-done | bytes 69664 | tf_op jit(solution)/shard_map/ppermute | solution.py:48
  68.1 0.7 %finish.4.refs_0_ = bf16[16,4608]{1,0:T(8,128)(2,1)} custom-call(f32[16,2048]{1,0:T(8,128)S(1)} %get-tuple-element.51.kept_ref, s16[16,2176]{1,0:T(8,128)(2,1)S(1)} %collective-permute-done.19.came_ref, bf16[16,4608]{1,0:T(8,128)(2,1)} %finish.3.refs_0_), custom_call_target="tpu_custom_call", output_to_operand_aliasing={{}: (2, {})} | custom-call | bytes 262144 | tf_op jit(solution)/shard_map/finish/pallas_call | solution.py:410
  68.8 0.7 %finish.5 = bf16[16,4608]{1,0:T(8,128)(2,1)} custom-call(f32[16,768]{1,0:T(8,128)S(1)} %get-tuple-element.48.kept_ref, s16[16,896]{1,0:T(8,128)(2,1)S(1)} %collective-permute-done.17.came_ref, bf16[16,4608]{1,0:T(8,128)(2,1)} %finish.4.refs_0_), custom_call_target="tpu_custom_call", output_to_operand_aliasing={{}: (2, {})} | custom-call | bytes 98304 | tf_op jit(solution)/shard_map/finish/pallas_call | solution.py:410
  (50 shorter events, 4.1 us)
Async XLA Ops:
  1.3 6.1 %copy-start = (bf16[64,4608]{1,0:T(8,128)(2,1)S(1)}, bf16[64,4608]{1,0:T(8,128)(2,1)}, u32[]{:S(2)}) copy-start(bf16[64,4608]{1,0:T(8,128)(2,1)} %refs_4_.5) | copy-start | bytes 1769476
  1.3 6.1 %copy-start.1 = (bf16[1152,512]{1,0:T(8,128)(2,1)S(1)}, bf16[1152,512]{1,0:T(8,128)(2,1)}, u32[]{:S(2)}) copy-start(bf16[1152,512]{1,0:T(8,128)(2,1)} %refs_7_.1) | copy-start | bytes 3538948
  1.4 6.1 %copy-start.2 = (f32[4608]{0:T(1024)S(1)}, f32[4608]{0:T(1024)}, u32[]{:S(2)}) copy-start(f32[4608]{0:T(1024)} %refs_5_.1) | copy-start | bytes 55300
  1.4 5.5 %collective-permute-start.2 = (f32[2,64]{1,0:T(2,128)S(1)}, f32[2,64]{1,0:T(2,128)S(1)}, u32[]{:S(2)}, u32[]{:S(2)}) collective-permute-start(f32[2,64]{1,0:T(2,128)S(1)} %pad_maximum_fusion.refs_0_), channel_id=1, source_target_pairs={{0,12},{4,8},{8,4},{12,0},{1,13},{5,9},{9,5},{13,1},{2,14},{6,10},... | collective-permute-start | bytes 1544 | tf_op jit(solution)/shard_map/ppermute | solution.py:48
  3.8 3.6 %collective-permute-start.1 = (f32[2,64]{1,0:T(2,128)S(1)}, f32[2,64]{1,0:T(2,128)S(1)}, u32[]{:S(2)}, u32[]{:S(2)}) collective-permute-start(f32[2,64]{1,0:T(2,128)S(1)} %pad_maximum_fusion.refs_0_), channel_id=1, source_target_pairs={{0,8},{4,12},{8,0},{12,4},{1,9},{5,13},{9,1},{13,5},{2,10},{6,14},... | collective-permute-start | bytes 1544 | tf_op jit(solution)/shard_map/ppermute | solution.py:48
  4.5 2.9 %collective-permute-start = (f32[2,64]{1,0:T(2,128)S(1)}, f32[2,64]{1,0:T(2,128)S(1)}, u32[]{:S(2)}, u32[]{:S(2)}) collective-permute-start(f32[2,64]{1,0:T(2,128)S(1)} %pad_maximum_fusion.refs_0_), channel_id=1, source_target_pairs={{0,4},{4,0},{8,12},{12,8},{1,5},{5,1},{9,13},{13,9},{2,6},{6,2},{1... | collective-permute-start | bytes 1544 | tf_op jit(solution)/shard_map/ppermute | solution.py:48
  16.1 1.9 %collective-permute-start.3 = (f32[32,3584]{1,0:T(8,128)S(1)}, f32[32,3584]{1,0:T(8,128)S(1)}, u32[]{:S(2)}, u32[]{:S(2)}) collective-permute-start(f32[32,3584]{1,0:T(8,128)S(1)} %get-tuple-element.30), channel_id=1, source_target_pairs={{0,4},{4,0},{8,12},{12,8},{1,5},{5,1},{9,13},{13,9},{2,6},{6,2},{1... | collective-permute-start | bytes 1376264 | tf_op jit(solution)/shard_map/ppermute | solution.py:48
  18.0 7.7 %collective-permute-start.4 = (f32[16,3584]{1,0:T(8,128)S(1)}, f32[16,3584]{1,0:T(8,128)S(1)}, u32[]{:S(2)}, u32[]{:S(2)}) collective-permute-start(f32[16,3584]{1,0:T(8,128)S(1)} %get-tuple-element.32), channel_id=1, source_target_pairs={{0,8},{4,12},{8,0},{12,4},{1,9},{5,13},{9,1},{13,5},{2,10},{6,14},... | collective-permute-start | bytes 688136 | tf_op jit(solution)/shard_map/ppermute | solution.py:48
  25.7 8.6 %copy-start.3 = (bf16[4,1024,512]{2,1,0:T(8,128)(2,1)S(1)}, bf16[4,1024,512]{2,1,0:T(8,128)(2,1)}, u32[]{:S(2)}) copy-start(bf16[4,1024,512]{2,1,0:T(8,128)(2,1)} %refs_4_.6) | copy-start | bytes 12582916
  25.7 8.6 %copy-start.4 = (s32[4]{0:T(128)S(1)}, s32[4]{0:T(128)}, u32[]{:S(2)}) copy-start(s32[4]{0:T(128)} %param.13) | copy-start | bytes 52
  25.7 23.0 %slice-start = ((s8[28311552]{0:T(1024)(128)(4,1)}), s8[4194304]{0:T(1024)(128)(4,1)S(1)}, s32[]{:S(2)}) async-start(s8[28311552]{0:T(1024)(128)(4,1)} %bitcast.3), calls=%async_computation | async-start | bytes 8388608
  25.7 23.0 %slice-start.1 = ((s8[28311552]{0:T(1024)(128)(4,1)}), s8[4194304]{0:T(1024)(128)(4,1)S(1)}, s32[]{:S(2)}) async-start(s8[28311552]{0:T(1024)(128)(4,1)} %bitcast.3), calls=%async_computation.1 | async-start | bytes 8388608
  25.7 23.0 %slice-start.2 = ((s8[28311552]{0:T(1024)(128)(4,1)}), s8[4194304]{0:T(1024)(128)(4,1)S(1)}, s32[]{:S(2)}) async-start(s8[28311552]{0:T(1024)(128)(4,1)} %bitcast.3), calls=%async_computation.2 | async-start | bytes 8388608
  25.8 6.0 %collective-permute-start.5 = (bf16[8,2048]{1,0:T(8,128)(2,1)S(1)}, bf16[8,2048]{1,0:T(8,128)(2,1)S(1)}, u32[]{:S(2)}, u32[]{:S(2)}) collective-permute-start(bf16[8,2048]{1,0:T(8,128)(2,1)S(1)} %get-tuple-element.33), channel_id=1, source_target_pairs={{0,3},{1,2},{2,1},{3,0},{4,7},{5,6},{6,5},{7,4},{8,11},{9,10},{10,... | collective-permute-start | bytes 98312 | tf_op jit(solution)/shard_map/ppermute | solution.py:48
  29.5 4.8 %collective-permute-start.6 = (bf16[8,2048]{1,0:T(8,128)(2,1)S(1)}, bf16[8,2048]{1,0:T(8,128)(2,1)S(1)}, u32[]{:S(2)}, u32[]{:S(2)}) collective-permute-start(bf16[8,2048]{1,0:T(8,128)(2,1)S(1)} %get-tuple-element.34), channel_id=1, source_target_pairs={{0,2},{1,3},{2,0},{3,1},{4,6},{5,7},{6,4},{7,5},{8,10},{9,11},{10,... | collective-permute-start | bytes 98312 | tf_op jit(solution)/shard_map/ppermute | solution.py:48
  29.5 4.8 %collective-permute-start.7 = (bf16[8,2048]{1,0:T(8,128)(2,1)S(1)}, bf16[8,2048]{1,0:T(8,128)(2,1)S(1)}, u32[]{:S(2)}, u32[]{:S(2)}) collective-permute-start(bf16[8,2048]{1,0:T(8,128)(2,1)S(1)} %get-tuple-element.35), channel_id=1, source_target_pairs={{0,1},{1,0},{2,3},{3,2},{4,5},{5,4},{6,7},{7,6},{8,9},{9,8},{10,11... | collective-permute-start | bytes 98312 | tf_op jit(solution)/shard_map/ppermute | solution.py:48
  34.3 14.5 %slice-start.3 = ((s8[28311552]{0:T(1024)(128)(4,1)}), s8[4194304]{0:T(1024)(128)(4,1)S(1)}, s32[]{:S(2)}) async-start(s8[28311552]{0:T(1024)(128)(4,1)} %bitcast.3), calls=%async_computation.3 | async-start | bytes 8388608
  34.3 14.5 %slice-start.4 = ((s8[28311552]{0:T(1024)(128)(4,1)}), s8[4194304]{0:T(1024)(128)(4,1)S(1)}, s32[]{:S(2)}) async-start(s8[28311552]{0:T(1024)(128)(4,1)} %bitcast.3), calls=%async_computation.4 | async-start | bytes 8388608
  36.2 5.7 %collective-permute-start.8 = (bf16[8,1536]{1,0:T(8,128)(2,1)S(1)}, bf16[8,1536]{1,0:T(8,128)(2,1)S(1)}, u32[]{:S(2)}, u32[]{:S(2)}) collective-permute-start(bf16[8,1536]{1,0:T(8,128)(2,1)S(1)} %get-tuple-element.37), channel_id=1, source_target_pairs={{0,3},{1,2},{2,1},{3,0},{4,7},{5,6},{6,5},{7,4},{8,11},{9,10},{10,... | collective-permute-start | bytes 73736 | tf_op jit(solution)/shard_map/ppermute | solution.py:48
  37.7 4.7 %collective-permute-start.9 = (bf16[8,1536]{1,0:T(8,128)(2,1)S(1)}, bf16[8,1536]{1,0:T(8,128)(2,1)S(1)}, u32[]{:S(2)}, u32[]{:S(2)}) collective-permute-start(bf16[8,1536]{1,0:T(8,128)(2,1)S(1)} %get-tuple-element.38), channel_id=1, source_target_pairs={{0,2},{1,3},{2,0},{3,1},{4,6},{5,7},{6,4},{7,5},{8,10},{9,11},{10,... | collective-permute-start | bytes 73736 | tf_op jit(solution)/shard_map/ppermute | solution.py:48
  38.4 4.3 %collective-permute-start.10 = (bf16[8,1536]{1,0:T(8,128)(2,1)S(1)}, bf16[8,1536]{1,0:T(8,128)(2,1)S(1)}, u32[]{:S(2)}, u32[]{:S(2)}) collective-permute-start(bf16[8,1536]{1,0:T(8,128)(2,1)S(1)} %get-tuple-element.39), channel_id=1, source_target_pairs={{0,1},{1,0},{2,3},{3,2},{4,5},{5,4},{6,7},{7,6},{8,9},{9,8},{10,11... | collective-permute-start | bytes 73736 | tf_op jit(solution)/shard_map/ppermute | solution.py:48
  42.7 6.1 %slice-start.5 = ((s8[28311552]{0:T(1024)(128)(4,1)}), s8[4194304]{0:T(1024)(128)(4,1)S(1)}, s32[]{:S(2)}) async-start(s8[28311552]{0:T(1024)(128)(4,1)} %bitcast.3), calls=%async_computation.5 | async-start | bytes 8388608
  42.7 6.1 %slice-start.6 = ((s8[28311552]{0:T(1024)(128)(4,1)}), s8[3145728]{0:T(1024)(128)(4,1)S(1)}, s32[]{:S(2)}) async-start(s8[28311552]{0:T(1024)(128)(4,1)} %bitcast.3), calls=%async_computation.6 | async-start | bytes 6291456
  42.8 4.7 %collective-permute-start.12 = (bf16[16,3072]{1,0:T(8,128)(2,1)S(1)}, bf16[16,3072]{1,0:T(8,128)(2,1)S(1)}, u32[]{:S(2)}, u32[]{:S(2)}) collective-permute-start(bf16[16,3072]{1,0:T(8,128)(2,1)S(1)} %join.1.refs_0_), channel_id=1, source_target_pairs={{0,8},{4,12},{8,0},{12,4},{1,9},{5,13},{9,1},{13,5},{2,10},{6,14},... | collective-permute-start | bytes 294920 | tf_op jit(solution)/shard_map/ppermute | solution.py:48
  44.1 3.4 %collective-permute-start.11 = (bf16[16,3072]{1,0:T(8,128)(2,1)S(1)}, bf16[16,3072]{1,0:T(8,128)(2,1)S(1)}, u32[]{:S(2)}, u32[]{:S(2)}) collective-permute-start(bf16[16,3072]{1,0:T(8,128)(2,1)S(1)} %join.1.refs_0_), channel_id=1, source_target_pairs={{0,4},{4,0},{8,12},{12,8},{1,5},{5,1},{9,13},{13,9},{2,6},{6,2},{1... | collective-permute-start | bytes 294920 | tf_op jit(solution)/shard_map/ppermute | solution.py:48
  47.4 1.3 %collective-permute-start.13 = (bf16[16,3072]{1,0:T(8,128)(2,1)S(1)}, bf16[16,3072]{1,0:T(8,128)(2,1)S(1)}, u32[]{:S(2)}, u32[]{:S(2)}) collective-permute-start(bf16[16,3072]{1,0:T(8,128)(2,1)S(1)} %collective-permute-done.12.refs_2_), channel_id=1, source_target_pairs={{0,4},{4,0},{8,12},{12,8},{1,5},{5,1},{9,13},{13,9},{2,6},{6,2},{1... | collective-permute-start | bytes 294920 | tf_op jit(solution)/shard_map/ppermute | solution.py:48
  51.0 5.5 %collective-permute-start.14 = (s16[32,1920]{1,0:T(8,128)(2,1)S(1)}, s16[32,1920]{1,0:T(8,128)(2,1)S(1)}, u32[]{:S(2)}, u32[]{:S(2)}) collective-permute-start(s16[32,1920]{1,0:T(8,128)(2,1)S(1)} %get-tuple-element.42), channel_id=1, source_target_pairs={{0,1},{1,0},{2,3},{3,2},{4,5},{5,4},{6,7},{7,6},{8,9},{9,8},{10,11... | collective-permute-start | bytes 368648 | tf_op jit(solution)/shard_map/ppermute | solution.py:48
  55.2 6.7 %collective-permute-start.18 = (s16[32,2176]{1,0:T(8,128)(2,1)S(1)}, s16[32,2176]{1,0:T(8,128)(2,1)S(1)}, u32[]{:S(2)}, u32[]{:S(2)}) collective-permute-start(s16[32,2176]{1,0:T(8,128)(2,1)S(1)} %get-tuple-element.50), channel_id=1, source_target_pairs={{0,1},{1,0},{2,3},{3,2},{4,5},{5,4},{6,7},{7,6},{8,9},{9,8},{10,11... | collective-permute-start | bytes 417800 | tf_op jit(solution)/shard_map/ppermute | solution.py:48
  56.6 6.2 %collective-permute-start.16 = (s16[16,1920]{1,0:T(8,128)(2,1)S(1)}, s16[16,1920]{1,0:T(8,128)(2,1)S(1)}, u32[]{:S(2)}, u32[]{:S(2)}) collective-permute-start(s16[16,1920]{1,0:T(8,128)(2,1)S(1)} %get-tuple-element.47), channel_id=1, source_target_pairs={{0,2},{1,3},{2,0},{3,1},{4,6},{5,7},{6,4},{7,5},{8,10},{9,11},{10,... | collective-permute-start | bytes 184328 | tf_op jit(solution)/shard_map/ppermute | solution.py:48
  59.5 4.4 %collective-permute-start.15 = (s16[32,896]{1,0:T(8,128)(2,1)S(1)}, s16[32,896]{1,0:T(8,128)(2,1)S(1)}, u32[]{:S(2)}, u32[]{:S(2)}) collective-permute-start(s16[32,896]{1,0:T(8,128)(2,1)S(1)} %get-tuple-element.46), channel_id=1, source_target_pairs={{0,1},{1,0},{2,3},{3,2},{4,5},{5,4},{6,7},{7,6},{8,9},{9,8},{10,11... | collective-permute-start | bytes 172040 | tf_op jit(solution)/shard_map/ppermute | solution.py:48
  62.1 6.0 %collective-permute-start.19 = (s16[16,2176]{1,0:T(8,128)(2,1)S(1)}, s16[16,2176]{1,0:T(8,128)(2,1)S(1)}, u32[]{:S(2)}, u32[]{:S(2)}) collective-permute-start(s16[16,2176]{1,0:T(8,128)(2,1)S(1)} %get-tuple-element.52), channel_id=1, source_target_pairs={{0,2},{1,3},{2,0},{3,1},{4,6},{5,7},{6,4},{7,5},{8,10},{9,11},{10,... | collective-permute-start | bytes 208904 | tf_op jit(solution)/shard_map/ppermute | solution.py:48
  64.0 4.8 %collective-permute-start.17 = (s16[16,896]{1,0:T(8,128)(2,1)S(1)}, s16[16,896]{1,0:T(8,128)(2,1)S(1)}, u32[]{:S(2)}, u32[]{:S(2)}) collective-permute-start(s16[16,896]{1,0:T(8,128)(2,1)S(1)} %get-tuple-element.49), channel_id=1, source_target_pairs={{0,2},{1,3},{2,0},{3,1},{4,6},{5,7},{6,4},{7,5},{8,10},{9,11},{10,... | collective-permute-start | bytes 86024 | tf_op jit(solution)/shard_map/ppermute | solution.py:48

commit v12 on v11

--- a/solution.py
+++ b/solution.py
@@ -396,28 +396,29 @@
     )
 
 
-def finish_kernel(start, kept_ref, came_ref, *refs):
-    out_ref, done, sem = refs[-3:]
-    width = kept_ref.shape[1]
-    done[...] = (kept_ref[...] + decode(came_ref, width)).astype(jnp.bfloat16)
-    copy = pltpu.make_async_copy(done, out_ref.at[:, start : start + width], sem)
-    copy.start()
-    copy.wait()
-
-
-def finish(kept, came, start, columns, result):
-    rows, width = kept.shape
-    return pl.pallas_call(
-        functools.partial(finish_kernel, start),
-        out_shape=pltpu.HBM((rows, columns), jnp.bfloat16),
-        in_specs=[FULL, FULL] + [ANY] * (result is not None),
-        out_specs=ANY,
-        scratch_shapes=[pltpu.VMEM((rows, width), jnp.bfloat16), pltpu.SemaphoreType.DMA],
-        input_output_aliases={} if result is None else {2: 0},
-        compiler_params=pltpu.CompilerParams(vmem_limit_bytes=4 * MIB),
-        cost_estimate=pl.CostEstimate(flops=0, bytes_accessed=8 * rows * width, transcendentals=0),
-        name="finish",
-    )(kept, came, *([] if result is None else [in_hbm(result)]))
+def finish_kernel(starts, kinds, *refs):
+    out_ref = refs[-1]
+    k = 0
+    for at, kind in zip(starts, kinds):
+        width = refs[k].shape[1]
+        done = refs[k][...]
+        if kind == 2:
+            done = (done + decode(refs[k + 1], width)).astype(jnp.bfloat16)
+        out_ref[:, at : at + width] = done
+        k += kind
+
+
+def finish(starts, cuts):
+    parts = [x for cut in cuts for x in cut]
+    rows, columns = parts[0].shape[0], sum(cut[0].shape[1] for cut in cuts)
+    return call(
+        functools.partial(finish_kernel, starts, [len(cut) for cut in cuts]),
+        jax.ShapeDtypeStruct((rows, columns), jnp.bfloat16),
+        parts,
+        [FULL] * len(parts),
+        "finish",
+        moved=8 * columns * rows,
+    )
 
 
 def local(activations, norm_gain, query_weight, kv_weight, out_weight, kv_cache, lengths):
@@ -466,7 +467,7 @@
         flops=BESIDE,
     )
     gathered = gather(returned, "wide")
-    ends = [columns // LANES * k // 18 * LANES for k in (0,7,15,18)]
+    ends = [columns // LANES * k // 18 * LANES for k in (0, 8, 16, 18)]
     cut_sums, halved, last = [], [], []
 
     def exchange_cut(kept, sent, after):
@@ -483,11 +484,10 @@
         if last:
             exchange_cut(*last, [kept])
         last = (kept, sent)
-    result = finish(*cut_sums[0], ends[0], columns, None)
-    exchange_cut(*last, [in_hbm(result)])
-    for cut, start in zip(cut_sums[1:], ends[1:]):
-        result = finish(*cut, start, columns, result)
-    return result
+    early = finish([0], cut_sums[:1])
+    exchange_cut(*last, [early])
+    cut_sums[0] = (early,)
+    return finish(ends[:-1], cut_sums)
 
 
 def solution(mesh):

time: 69.7 us -> 72.6 us (1.042)
  waiting for transfers between devices: 23.9 us -> 28.2 us
  Pallas kernels: 21.3 us -> 20 us
    ppermute x20, waiting for transfers between devices: 23.9 us -> 28.2 us  [swap(): return lax.ppermute(x, axis, [(i, i ^ distance) for i in range(count)])]
    pallas_call x3 -> x0, Pallas kernels: 2.15 us -> none  [finish(): pl.pallas_call(functools.partial(finish_kernel, start), out_shape=pltpu.H...]
    pallas_call x12 -> x14, Pallas kernels: 19.1 us -> 20 us  [call(): pl.pallas_call(kernel, out_shape=outs, in_specs=specs, out_specs=jax.tree...]
  transfers between devices with their start and end apart: 20 -> 20, of which waited for: 14 -> 14; matrix products, arithmetic and copies ran while one was open for 0% -> 0% of each run, Pallas kernels for 11% -> 8%
where the time goes in v12:
time: 72.6 us; the launch traced here: 72.5 us
  waiting for transfers between devices  28.2 us (39%)
  starting transfers between devices  22.6 us (31%)
  Pallas kernels  20 us (28%)
  other arithmetic  1.32 us (2%)
    ppermute x20, waiting for transfers between devices, swap(): return lax.ppermute(x, axis, [(i, i ^ distance) for i in range(count)])  28.2 us
    ppermute x20, starting transfers between devices, swap(): return lax.ppermute(x, axis, [(i, i ^ distance) for i in range(count)])  22.6 us
    pallas_call x14, Pallas kernels, call(): pl.pallas_call(kernel, out_shape=outs, in_specs=specs, out_specs=jax.tree...  20 us
  transfers between devices with their start and end apart: 20, of which 14 were waited for; matrix products, arithmetic and copies ran while one was open for 0% of the time, Pallas kernels for 8%

profile of v12, /device:TPU:0, one launch (start us, length us, event | category | flops | bytes accessed | tf_op | source)
XLA Modules:
  0.0 72.5 jit_solution(8024920622573103364)
XLA Ops:
  0.0 1.3 %convert_reduce_fusion = (f32[64]{0:T(128)S(1)}, f32[64]{0:T(128)S(1)}) fusion(bf16[64,4608]{1,0:T(8,128)(2,1)} %refs_4_.5), kind=kLoop, calls=%fused_computation.1 | loop fusion | flops 1179520 | bytes 590336 | tf_op jit(solution)/shard_map/reduce_sum | solution.py:433
  1.4 2.5 %collective-permute-start.2 = (f32[2,64]{1,0:T(2,128)S(1)}, f32[2,64]{1,0:T(2,128)S(1)}, u32[]{:S(2)}, u32[]{:S(2)}) collective-permute-start(f32[2,64]{1,0:T(2,128)S(1)} %pad_maximum_fusion.refs_0_), channel_id=1, source_target_pairs={{0,12},{4,8},{8,4},{12,0},{1,13},{5,9},{9,5},{13,1},{2,14},{6,10},... | collective-permute-start | bytes 1544 | tf_op jit(solution)/shard_map/ppermute | solution.py:48
  4.5 2.3 %fetch_query_weight.1.refs_8_ = bf16[768,3072]{1,0:T(8,128)(2,1)S(1)} custom-call(bf16[4608,3072]{1,0:T(8,128)(2,1)} %refs_6_.1, f32[2,64]{1,0:T(2,128)S(1)} %pad_maximum_fusion.refs_0_), custom_call_target="tpu_custom_call" | custom-call | bytes 4718592 | tf_op jit(solution)/shard_map/fetch_query_weight/pallas_call | solution.py:22
  7.4 8.6 %project.1 = (f32[32,3584]{1,0:T(8,128)S(1)}, f32[32,3584]{1,0:T(8,128)S(1)}) custom-call(f32[2,64]{1,0:T(2,128)S(1)} %pad_maximum_fusion.refs_0_, f32[2,64]{1,0:T(2,128)S(1)} %collective-permute-done.refs_1_, f32[2,64]{1,0:T(2,128)S(1)} %collective-permute-done.1.refs_2_, f32[2,64]{1,0:T(2,128)S(1)} %collective-permute-done.2.refs_3_, ...), custom_call_target="tpu_custom_call" | custom-call | flops 1811939328 | bytes 23592960 | tf_op jit(solution)/shard_map/project/pallas_call | solution.py:22
  16.2 1.8 %collective-permute-done.3.came_ref = f32[32,3584]{1,0:T(8,128)S(1)} collective-permute-done((f32[32,3584]{1,0:T(8,128)S(1)}, f32[32,3584]{1,0:T(8,128)S(1)}, u32[]{:S(2)}, u32[]{:S(2)}) %collective-permute-start.3) | collective-permute-done | bytes 458784 | tf_op jit(solution)/shard_map/ppermute | solution.py:48
  18.0 1.3 %collective-permute-start.4 = (f32[16,3584]{1,0:T(8,128)S(1)}, f32[16,3584]{1,0:T(8,128)S(1)}, u32[]{:S(2)}, u32[]{:S(2)}) collective-permute-start(f32[16,3584]{1,0:T(8,128)S(1)} %get-tuple-element.32), channel_id=1, source_target_pairs={{0,8},{4,12},{8,0},{12,4},{1,9},{5,13},{9,1},{13,5},{2,10},{6,14},... | collective-permute-start | bytes 688136 | tf_op jit(solution)/shard_map/ppermute | solution.py:48
  19.3 6.4 %collective-permute-done.4.came_ref = f32[16,3584]{1,0:T(8,128)S(1)} collective-permute-done((f32[16,3584]{1,0:T(8,128)S(1)}, f32[16,3584]{1,0:T(8,128)S(1)}, u32[]{:S(2)}, u32[]{:S(2)}) %collective-permute-start.4) | collective-permute-done | bytes 229408 | tf_op jit(solution)/shard_map/ppermute | solution.py:48
  25.8 3.7 %collective-permute-start.5 = (bf16[8,2048]{1,0:T(8,128)(2,1)S(1)}, bf16[8,2048]{1,0:T(8,128)(2,1)S(1)}, u32[]{:S(2)}, u32[]{:S(2)}) collective-permute-start(bf16[8,2048]{1,0:T(8,128)(2,1)S(1)} %get-tuple-element.33), channel_id=1, source_target_pairs={{0,3},{1,2},{2,1},{3,0},{4,7},{5,6},{6,5},{7,4},{8,11},{9,10},{10,... | collective-permute-start | bytes 98312 | tf_op jit(solution)/shard_map/ppermute | solution.py:48
  29.5 0.8 %collective-permute-start.7 = (bf16[8,2048]{1,0:T(8,128)(2,1)S(1)}, bf16[8,2048]{1,0:T(8,128)(2,1)S(1)}, u32[]{:S(2)}, u32[]{:S(2)}) collective-permute-start(bf16[8,2048]{1,0:T(8,128)(2,1)S(1)} %get-tuple-element.35), channel_id=1, source_target_pairs={{0,1},{1,0},{2,3},{3,2},{4,5},{5,4},{6,7},{7,6},{8,9},{9,8},{10,11... | collective-permute-start | bytes 98312 | tf_op jit(solution)/shard_map/ppermute | solution.py:48
  30.3 1.5 %collective-permute-done.5.refs_0_ = bf16[8,2048]{1,0:T(8,128)(2,1)S(1)} collective-permute-done((bf16[8,2048]{1,0:T(8,128)(2,1)S(1)}, bf16[8,2048]{1,0:T(8,128)(2,1)S(1)}, u32[]{:S(2)}, u32[]{:S(2)}) %collective-permute-start.5) | collective-permute-done | bytes 32800 | tf_op jit(solution)/shard_map/ppermute | solution.py:48
  31.8 2.5 %collective-permute-done.6.refs_1_ = bf16[8,2048]{1,0:T(8,128)(2,1)S(1)} collective-permute-done((bf16[8,2048]{1,0:T(8,128)(2,1)S(1)}, bf16[8,2048]{1,0:T(8,128)(2,1)S(1)}, u32[]{:S(2)}, u32[]{:S(2)}) %collective-permute-start.6) | collective-permute-done | bytes 32800 | tf_op jit(solution)/shard_map/ppermute | solution.py:48
  34.3 1.9 %attend.1 = (bf16[8,1536]{1,0:T(8,128)(2,1)S(1)}, bf16[8,1536]{1,0:T(8,128)(2,1)S(1)}, bf16[8,1536]{1,0:T(8,128)(2,1)S(1)}, bf16[8,1536]{1,0:T(8,128)(2,1)S(1)}) custom-call(s32[1,4]{1,0:T(1,128)S(1)} %bitcast.5, bf16[8,2048]{1,0:T(8,128)(2,1)S(1)} %collective-permute-done.5.refs_0_, bf16[8,2048]{1,0:T(8,128)(2,1)S(1)} %collective-permute-done.6.refs_1_, ...), custom_call_target="tpu_custom_call" | custom-call | flops 5000000000 | tf_op jit(solution)/shard_map/attend/pallas_call | solution.py:22
  36.2 1.5 %collective-permute-start.8 = (bf16[8,1536]{1,0:T(8,128)(2,1)S(1)}, bf16[8,1536]{1,0:T(8,128)(2,1)S(1)}, u32[]{:S(2)}, u32[]{:S(2)}) collective-permute-start(bf16[8,1536]{1,0:T(8,128)(2,1)S(1)} %get-tuple-element.37), channel_id=1, source_target_pairs={{0,3},{1,2},{2,1},{3,0},{4,7},{5,6},{6,5},{7,4},{8,11},{9,10},{10,... | collective-permute-start | bytes 73736 | tf_op jit(solution)/shard_map/ppermute | solution.py:48
  37.7 0.6 collective-permute-start.9
  38.4 2.3 %collective-permute-start.10 = (bf16[8,1536]{1,0:T(8,128)(2,1)S(1)}, bf16[8,1536]{1,0:T(8,128)(2,1)S(1)}, u32[]{:S(2)}, u32[]{:S(2)}) collective-permute-start(bf16[8,1536]{1,0:T(8,128)(2,1)S(1)} %get-tuple-element.39), channel_id=1, source_target_pairs={{0,1},{1,0},{2,3},{3,2},{4,5},{5,4},{6,7},{7,6},{8,9},{9,8},{10,11... | collective-permute-start | bytes 73736 | tf_op jit(solution)/shard_map/ppermute | solution.py:48
  40.7 1.2 %collective-permute-done.8.refs_0_ = bf16[8,1536]{1,0:T(8,128)(2,1)S(1)} collective-permute-done((bf16[8,1536]{1,0:T(8,128)(2,1)S(1)}, bf16[8,1536]{1,0:T(8,128)(2,1)S(1)}, u32[]{:S(2)}, u32[]{:S(2)}) %collective-permute-start.8) | collective-permute-done | bytes 24608 | tf_op jit(solution)/shard_map/ppermute | solution.py:48
  42.8 1.3 %collective-permute-start.12 = (bf16[16,3072]{1,0:T(8,128)(2,1)S(1)}, bf16[16,3072]{1,0:T(8,128)(2,1)S(1)}, u32[]{:S(2)}, u32[]{:S(2)}) collective-permute-start(bf16[16,3072]{1,0:T(8,128)(2,1)S(1)} %join.1.refs_0_), channel_id=1, source_target_pairs={{0,8},{4,12},{8,0},{12,4},{1,9},{5,13},{9,1},{13,5},{2,10},{6,14},... | collective-permute-start | bytes 294920 | tf_op jit(solution)/shard_map/ppermute | solution.py:48
  44.1 3.4 %collective-permute-done.12.refs_2_ = bf16[16,3072]{1,0:T(8,128)(2,1)S(1)} collective-permute-done((bf16[16,3072]{1,0:T(8,128)(2,1)S(1)}, bf16[16,3072]{1,0:T(8,128)(2,1)S(1)}, u32[]{:S(2)}, u32[]{:S(2)}) %collective-permute-start.12) | collective-permute-done | bytes 98336 | tf_op jit(solution)/shard_map/ppermute | solution.py:48
  47.5 1.3 %collective-permute-done.13.refs_3_ = bf16[16,3072]{1,0:T(8,128)(2,1)S(1)} collective-permute-done((bf16[16,3072]{1,0:T(8,128)(2,1)S(1)}, bf16[16,3072]{1,0:T(8,128)(2,1)S(1)}, u32[]{:S(2)}, u32[]{:S(2)}) %collective-permute-start.13) | collective-permute-done | bytes 98336 | tf_op jit(solution)/shard_map/ppermute | solution.py:48
  48.8 2.4 %output_part.3 = (f32[64,2048]{1,0:T(8,128)S(1)}, s16[32,2176]{1,0:T(8,128)(2,1)S(1)}) custom-call(bf16[16,3072]{1,0:T(8,128)(2,1)S(1)} %join.1.refs_0_, bf16[16,3072]{1,0:T(8,128)(2,1)S(1)} %collective-permute-done.11.refs_1_, bf16[16,3072]{1,0:T(8,128)(2,1)S(1)} %collective-permute-done.12.refs_2_, bf16[16,3072]{1,0:T(8,128)(2,1)S(1)} %collective-permute-done.13.refs_3_, ...), custom_call_target="tpu_custom_call" | custom-call | flops 805306368 | bytes 393216 | tf_op jit(solution)/shard_map/output_part/pallas_call | solution.py:22
  51.2 1.8 %collective-permute-start.14 = (s16[32,2176]{1,0:T(8,128)(2,1)S(1)}, s16[32,2176]{1,0:T(8,128)(2,1)S(1)}, u32[]{:S(2)}, u32[]{:S(2)}) collective-permute-start(s16[32,2176]{1,0:T(8,128)(2,1)S(1)} %get-tuple-element.42), channel_id=1, source_target_pairs={{0,1},{1,0},{2,3},{3,2},{4,5},{5,4},{6,7},{7,6},{8,9},{9,8},{10,11... | collective-permute-start | bytes 417800 | tf_op jit(solution)/shard_map/ppermute | solution.py:48
  53.1 2.4 %output_part.4 = (f32[64,2048]{1,0:T(8,128)S(1)}, s16[32,2176]{1,0:T(8,128)(2,1)S(1)}) custom-call(bf16[16,3072]{1,0:T(8,128)(2,1)S(1)} %join.1.refs_0_, bf16[16,3072]{1,0:T(8,128)(2,1)S(1)} %collective-permute-done.11.refs_1_, bf16[16,3072]{1,0:T(8,128)(2,1)S(1)} %collective-permute-done.12.refs_2_, bf16[16,3072]{1,0:T(8,128)(2,1)S(1)} %collective-permute-done.13.refs_3_, ...), custom_call_target="tpu_custom_call" | custom-call | flops 805306368 | bytes 393216 | tf_op jit(solution)/shard_map/output_part/pallas_call | solution.py:22
  55.8 1.3 %collective-permute-done.14.came_ref = s16[32,2176]{1,0:T(8,128)(2,1)S(1)} collective-permute-done((s16[32,2176]{1,0:T(8,128)(2,1)S(1)}, s16[32,2176]{1,0:T(8,128)(2,1)S(1)}, u32[]{:S(2)}, u32[]{:S(2)}) %collective-permute-start.14) | collective-permute-done | bytes 139296 | tf_op jit(solution)/shard_map/ppermute | solution.py:48
  57.3 1.8 %collective-permute-start.15 = (s16[16,2176]{1,0:T(8,128)(2,1)S(1)}, s16[16,2176]{1,0:T(8,128)(2,1)S(1)}, u32[]{:S(2)}, u32[]{:S(2)}) collective-permute-start(s16[16,2176]{1,0:T(8,128)(2,1)S(1)} %get-tuple-element.45), channel_id=1, source_target_pairs={{0,2},{1,3},{2,0},{3,1},{4,6},{5,7},{6,4},{7,5},{8,10},{9,11},{10,... | collective-permute-start | bytes 208904 | tf_op jit(solution)/shard_map/ppermute | solution.py:48
  59.0 0.8 %output_part.5 = (f32[64,512]{1,0:T(8,128)S(1)}, s16[32,640]{1,0:T(8,128)(2,1)S(1)}) custom-call(bf16[16,3072]{1,0:T(8,128)(2,1)S(1)} %join.1.refs_0_, bf16[16,3072]{1,0:T(8,128)(2,1)S(1)} %collective-permute-done.11.refs_1_, bf16[16,3072]{1,0:T(8,128)(2,1)S(1)} %collective-permute-done.12.refs_2_, bf16[16,3072]{1,0:T(8,128)(2,1)S(1)} %collective-permute-done.13.refs_3_, ...), custom_call_target="tpu_custom_call" | custom-call | flops 201326592 | bytes 393216 | tf_op jit(solution)/shard_map/output_part/pallas_call | solution.py:22
  59.8 1.9 %collective-permute-done.16.came_ref = s16[32,2176]{1,0:T(8,128)(2,1)S(1)} collective-permute-done((s16[32,2176]{1,0:T(8,128)(2,1)S(1)}, s16[32,2176]{1,0:T(8,128)(2,1)S(1)}, u32[]{:S(2)}, u32[]{:S(2)}) %collective-permute-start.16) | collective-permute-done | bytes 139296 | tf_op jit(solution)/shard_map/ppermute | solution.py:48
  61.9 0.7 collective-permute-start.17
  62.6 0.8 %collective-permute-start.18 = (s16[32,640]{1,0:T(8,128)(2,1)S(1)}, s16[32,640]{1,0:T(8,128)(2,1)S(1)}, u32[]{:S(2)}, u32[]{:S(2)}) collective-permute-start(s16[32,640]{1,0:T(8,128)(2,1)S(1)} %get-tuple-element.50), channel_id=1, source_target_pairs={{0,1},{1,0},{2,3},{3,2},{4,5},{5,4},{6,7},{7,6},{8,9},{9,8},{10,11... | collective-permute-start | bytes 122888 | tf_op jit(solution)/shard_map/ppermute | solution.py:48
  63.5 3.2 %collective-permute-done.18.came_ref = s16[32,640]{1,0:T(8,128)(2,1)S(1)} collective-permute-done((s16[32,640]{1,0:T(8,128)(2,1)S(1)}, s16[32,640]{1,0:T(8,128)(2,1)S(1)}, u32[]{:S(2)}, u32[]{:S(2)}) %collective-permute-start.18) | collective-permute-done | bytes 40992 | tf_op jit(solution)/shard_map/ppermute | solution.py:48
  66.9 2.4 %collective-permute-start.19 = (s16[16,640]{1,0:T(8,128)(2,1)S(1)}, s16[16,640]{1,0:T(8,128)(2,1)S(1)}, u32[]{:S(2)}, u32[]{:S(2)}) collective-permute-start(s16[16,640]{1,0:T(8,128)(2,1)S(1)} %get-tuple-element.52), channel_id=1, source_target_pairs={{0,2},{1,3},{2,0},{3,1},{4,6},{5,7},{6,4},{7,5},{8,10},{9,11},{10,... | collective-permute-start | bytes 61448 | tf_op jit(solution)/shard_map/ppermute | solution.py:48
  69.3 2.4 %collective-permute-done.19.refs_4_ = s16[16,640]{1,0:T(8,128)(2,1)S(1)} collective-permute-done((s16[16,640]{1,0:T(8,128)(2,1)S(1)}, s16[16,640]{1,0:T(8,128)(2,1)S(1)}, u32[]{:S(2)}, u32[]{:S(2)}) %collective-permute-start.19) | collective-permute-done | bytes 20512 | tf_op jit(solution)/shard_map/ppermute | solution.py:48
  71.7 0.8 %finish.3 = bf16[16,4608]{1,0:T(8,128)(2,1)} custom-call(bf16[16,2048]{1,0:T(8,128)(2,1)S(1)} %finish.2.refs_0_, f32[16,2048]{1,0:T(8,128)S(1)} %get-tuple-element.48.refs_1_, s16[16,2176]{1,0:T(8,128)(2,1)S(1)} %collective-permute-done.17.refs_2_, f32[16,512]{1,0:T(8,128)S(1)} %get-tuple-element.51.refs_3_, s16[16,640]{1,0:T(8,128)(2,1)S(1)} %collective-permute-done.19.refs_4_), custom_call_target="tpu_custom_call" | custom-call | bytes 589824 | tf_op jit(solution)/shard_map/finish/pallas_call | solution.py:22
  (49 shorter events, 3.3 us)
Async XLA Ops:
  1.3 6.1 %copy-start = (bf16[64,4608]{1,0:T(8,128)(2,1)S(1)}, bf16[64,4608]{1,0:T(8,128)(2,1)}, u32[]{:S(2)}) copy-start(bf16[64,4608]{1,0:T(8,128)(2,1)} %refs_4_.5) | copy-start | bytes 1769476
  1.3 6.1 %copy-start.1 = (bf16[1152,512]{1,0:T(8,128)(2,1)S(1)}, bf16[1152,512]{1,0:T(8,128)(2,1)}, u32[]{:S(2)}) copy-start(bf16[1152,512]{1,0:T(8,128)(2,1)} %refs_7_.1) | copy-start | bytes 3538948
  1.4 6.1 %copy-start.2 = (f32[4608]{0:T(1024)S(1)}, f32[4608]{0:T(1024)}, u32[]{:S(2)}) copy-start(f32[4608]{0:T(1024)} %refs_5_.1) | copy-start | bytes 55300
  1.4 5.5 %collective-permute-start.2 = (f32[2,64]{1,0:T(2,128)S(1)}, f32[2,64]{1,0:T(2,128)S(1)}, u32[]{:S(2)}, u32[]{:S(2)}) collective-permute-start(f32[2,64]{1,0:T(2,128)S(1)} %pad_maximum_fusion.refs_0_), channel_id=1, source_target_pairs={{0,12},{4,8},{8,4},{12,0},{1,13},{5,9},{9,5},{13,1},{2,14},{6,10},... | collective-permute-start | bytes 1544 | tf_op jit(solution)/shard_map/ppermute | solution.py:48
  3.8 3.6 %collective-permute-start.1 = (f32[2,64]{1,0:T(2,128)S(1)}, f32[2,64]{1,0:T(2,128)S(1)}, u32[]{:S(2)}, u32[]{:S(2)}) collective-permute-start(f32[2,64]{1,0:T(2,128)S(1)} %pad_maximum_fusion.refs_0_), channel_id=1, source_target_pairs={{0,8},{4,12},{8,0},{12,4},{1,9},{5,13},{9,1},{13,5},{2,10},{6,14},... | collective-permute-start | bytes 1544 | tf_op jit(solution)/shard_map/ppermute | solution.py:48
  4.5 2.9 %collective-permute-start = (f32[2,64]{1,0:T(2,128)S(1)}, f32[2,64]{1,0:T(2,128)S(1)}, u32[]{:S(2)}, u32[]{:S(2)}) collective-permute-start(f32[2,64]{1,0:T(2,128)S(1)} %pad_maximum_fusion.refs_0_), channel_id=1, source_target_pairs={{0,4},{4,0},{8,12},{12,8},{1,5},{5,1},{9,13},{13,9},{2,6},{6,2},{1... | collective-permute-start | bytes 1544 | tf_op jit(solution)/shard_map/ppermute | solution.py:48
  16.1 1.9 %collective-permute-start.3 = (f32[32,3584]{1,0:T(8,128)S(1)}, f32[32,3584]{1,0:T(8,128)S(1)}, u32[]{:S(2)}, u32[]{:S(2)}) collective-permute-start(f32[32,3584]{1,0:T(8,128)S(1)} %get-tuple-element.30), channel_id=1, source_target_pairs={{0,4},{4,0},{8,12},{12,8},{1,5},{5,1},{9,13},{13,9},{2,6},{6,2},{1... | collective-permute-start | bytes 1376264 | tf_op jit(solution)/shard_map/ppermute | solution.py:48
  18.0 7.7 %collective-permute-start.4 = (f32[16,3584]{1,0:T(8,128)S(1)}, f32[16,3584]{1,0:T(8,128)S(1)}, u32[]{:S(2)}, u32[]{:S(2)}) collective-permute-start(f32[16,3584]{1,0:T(8,128)S(1)} %get-tuple-element.32), channel_id=1, source_target_pairs={{0,8},{4,12},{8,0},{12,4},{1,9},{5,13},{9,1},{13,5},{2,10},{6,14},... | collective-permute-start | bytes 688136 | tf_op jit(solution)/shard_map/ppermute | solution.py:48
  25.7 8.6 %copy-start.3 = (bf16[4,1024,512]{2,1,0:T(8,128)(2,1)S(1)}, bf16[4,1024,512]{2,1,0:T(8,128)(2,1)}, u32[]{:S(2)}) copy-start(bf16[4,1024,512]{2,1,0:T(8,128)(2,1)} %refs_4_.6) | copy-start | bytes 12582916
  25.7 8.6 %copy-start.4 = (s32[4]{0:T(128)S(1)}, s32[4]{0:T(128)}, u32[]{:S(2)}) copy-start(s32[4]{0:T(128)} %param.13) | copy-start | bytes 52
  25.7 23.0 %slice-start = ((s8[28311552]{0:T(1024)(128)(4,1)}), s8[4194304]{0:T(1024)(128)(4,1)S(1)}, s32[]{:S(2)}) async-start(s8[28311552]{0:T(1024)(128)(4,1)} %bitcast.3), calls=%async_computation | async-start | bytes 8388608
  25.7 23.0 %slice-start.1 = ((s8[28311552]{0:T(1024)(128)(4,1)}), s8[4194304]{0:T(1024)(128)(4,1)S(1)}, s32[]{:S(2)}) async-start(s8[28311552]{0:T(1024)(128)(4,1)} %bitcast.3), calls=%async_computation.1 | async-start | bytes 8388608
  25.7 23.0 %slice-start.2 = ((s8[28311552]{0:T(1024)(128)(4,1)}), s8[4194304]{0:T(1024)(128)(4,1)S(1)}, s32[]{:S(2)}) async-start(s8[28311552]{0:T(1024)(128)(4,1)} %bitcast.3), calls=%async_computation.2 | async-start | bytes 8388608
  25.8 6.0 %collective-permute-start.5 = (bf16[8,2048]{1,0:T(8,128)(2,1)S(1)}, bf16[8,2048]{1,0:T(8,128)(2,1)S(1)}, u32[]{:S(2)}, u32[]{:S(2)}) collective-permute-start(bf16[8,2048]{1,0:T(8,128)(2,1)S(1)} %get-tuple-element.33), channel_id=1, source_target_pairs={{0,3},{1,2},{2,1},{3,0},{4,7},{5,6},{6,5},{7,4},{8,11},{9,10},{10,... | collective-permute-start | bytes 98312 | tf_op jit(solution)/shard_map/ppermute | solution.py:48
  29.5 4.8 %collective-permute-start.6 = (bf16[8,2048]{1,0:T(8,128)(2,1)S(1)}, bf16[8,2048]{1,0:T(8,128)(2,1)S(1)}, u32[]{:S(2)}, u32[]{:S(2)}) collective-permute-start(bf16[8,2048]{1,0:T(8,128)(2,1)S(1)} %get-tuple-element.34), channel_id=1, source_target_pairs={{0,2},{1,3},{2,0},{3,1},{4,6},{5,7},{6,4},{7,5},{8,10},{9,11},{10,... | collective-permute-start | bytes 98312 | tf_op jit(solution)/shard_map/ppermute | solution.py:48
  29.5 4.8 %collective-permute-start.7 = (bf16[8,2048]{1,0:T(8,128)(2,1)S(1)}, bf16[8,2048]{1,0:T(8,128)(2,1)S(1)}, u32[]{:S(2)}, u32[]{:S(2)}) collective-permute-start(bf16[8,2048]{1,0:T(8,128)(2,1)S(1)} %get-tuple-element.35), channel_id=1, source_target_pairs={{0,1},{1,0},{2,3},{3,2},{4,5},{5,4},{6,7},{7,6},{8,9},{9,8},{10,11... | collective-permute-start | bytes 98312 | tf_op jit(solution)/shard_map/ppermute | solution.py:48
  34.3 14.5 %slice-start.3 = ((s8[28311552]{0:T(1024)(128)(4,1)}), s8[4194304]{0:T(1024)(128)(4,1)S(1)}, s32[]{:S(2)}) async-start(s8[28311552]{0:T(1024)(128)(4,1)} %bitcast.3), calls=%async_computation.3 | async-start | bytes 8388608
  34.3 14.5 %slice-start.4 = ((s8[28311552]{0:T(1024)(128)(4,1)}), s8[4194304]{0:T(1024)(128)(4,1)S(1)}, s32[]{:S(2)}) async-start(s8[28311552]{0:T(1024)(128)(4,1)} %bitcast.3), calls=%async_computation.4 | async-start | bytes 8388608
  36.2 5.7 %collective-permute-start.8 = (bf16[8,1536]{1,0:T(8,128)(2,1)S(1)}, bf16[8,1536]{1,0:T(8,128)(2,1)S(1)}, u32[]{:S(2)}, u32[]{:S(2)}) collective-permute-start(bf16[8,1536]{1,0:T(8,128)(2,1)S(1)} %get-tuple-element.37), channel_id=1, source_target_pairs={{0,3},{1,2},{2,1},{3,0},{4,7},{5,6},{6,5},{7,4},{8,11},{9,10},{10,... | collective-permute-start | bytes 73736 | tf_op jit(solution)/shard_map/ppermute | solution.py:48
  37.7 4.7 %collective-permute-start.9 = (bf16[8,1536]{1,0:T(8,128)(2,1)S(1)}, bf16[8,1536]{1,0:T(8,128)(2,1)S(1)}, u32[]{:S(2)}, u32[]{:S(2)}) collective-permute-start(bf16[8,1536]{1,0:T(8,128)(2,1)S(1)} %get-tuple-element.38), channel_id=1, source_target_pairs={{0,2},{1,3},{2,0},{3,1},{4,6},{5,7},{6,4},{7,5},{8,10},{9,11},{10,... | collective-permute-start | bytes 73736 | tf_op jit(solution)/shard_map/ppermute | solution.py:48
  38.4 4.3 %collective-permute-start.10 = (bf16[8,1536]{1,0:T(8,128)(2,1)S(1)}, bf16[8,1536]{1,0:T(8,128)(2,1)S(1)}, u32[]{:S(2)}, u32[]{:S(2)}) collective-permute-start(bf16[8,1536]{1,0:T(8,128)(2,1)S(1)} %get-tuple-element.39), channel_id=1, source_target_pairs={{0,1},{1,0},{2,3},{3,2},{4,5},{5,4},{6,7},{7,6},{8,9},{9,8},{10,11... | collective-permute-start | bytes 73736 | tf_op jit(solution)/shard_map/ppermute | solution.py:48
  42.7 6.1 %slice-start.5 = ((s8[28311552]{0:T(1024)(128)(4,1)}), s8[4194304]{0:T(1024)(128)(4,1)S(1)}, s32[]{:S(2)}) async-start(s8[28311552]{0:T(1024)(128)(4,1)} %bitcast.3), calls=%async_computation.5 | async-start | bytes 8388608
  42.7 6.1 %slice-start.6 = ((s8[28311552]{0:T(1024)(128)(4,1)}), s8[3145728]{0:T(1024)(128)(4,1)S(1)}, s32[]{:S(2)}) async-start(s8[28311552]{0:T(1024)(128)(4,1)} %bitcast.3), calls=%async_computation.6 | async-start | bytes 6291456
  42.8 4.7 %collective-permute-start.12 = (bf16[16,3072]{1,0:T(8,128)(2,1)S(1)}, bf16[16,3072]{1,0:T(8,128)(2,1)S(1)}, u32[]{:S(2)}, u32[]{:S(2)}) collective-permute-start(bf16[16,3072]{1,0:T(8,128)(2,1)S(1)} %join.1.refs_0_), channel_id=1, source_target_pairs={{0,8},{4,12},{8,0},{12,4},{1,9},{5,13},{9,1},{13,5},{2,10},{6,14},... | collective-permute-start | bytes 294920 | tf_op jit(solution)/shard_map/ppermute | solution.py:48
  44.1 3.4 %collective-permute-start.11 = (bf16[16,3072]{1,0:T(8,128)(2,1)S(1)}, bf16[16,3072]{1,0:T(8,128)(2,1)S(1)}, u32[]{:S(2)}, u32[]{:S(2)}) collective-permute-start(bf16[16,3072]{1,0:T(8,128)(2,1)S(1)} %join.1.refs_0_), channel_id=1, source_target_pairs={{0,4},{4,0},{8,12},{12,8},{1,5},{5,1},{9,13},{13,9},{2,6},{6,2},{1... | collective-permute-start | bytes 294920 | tf_op jit(solution)/shard_map/ppermute | solution.py:48
  47.4 1.3 %collective-permute-start.13 = (bf16[16,3072]{1,0:T(8,128)(2,1)S(1)}, bf16[16,3072]{1,0:T(8,128)(2,1)S(1)}, u32[]{:S(2)}, u32[]{:S(2)}) collective-permute-start(bf16[16,3072]{1,0:T(8,128)(2,1)S(1)} %collective-permute-done.12.refs_2_), channel_id=1, source_target_pairs={{0,4},{4,0},{8,12},{12,8},{1,5},{5,1},{9,13},{13,9},{2,6},{6,2},{1... | collective-permute-start | bytes 294920 | tf_op jit(solution)/shard_map/ppermute | solution.py:48
  51.2 5.8 %collective-permute-start.14 = (s16[32,2176]{1,0:T(8,128)(2,1)S(1)}, s16[32,2176]{1,0:T(8,128)(2,1)S(1)}, u32[]{:S(2)}, u32[]{:S(2)}) collective-permute-start(s16[32,2176]{1,0:T(8,128)(2,1)S(1)} %get-tuple-element.42), channel_id=1, source_target_pairs={{0,1},{1,0},{2,3},{3,2},{4,5},{5,4},{6,7},{7,6},{8,9},{9,8},{10,11... | collective-permute-start | bytes 417800 | tf_op jit(solution)/shard_map/ppermute | solution.py:48
  55.5 6.3 %collective-permute-start.16 = (s16[32,2176]{1,0:T(8,128)(2,1)S(1)}, s16[32,2176]{1,0:T(8,128)(2,1)S(1)}, u32[]{:S(2)}, u32[]{:S(2)}) collective-permute-start(s16[32,2176]{1,0:T(8,128)(2,1)S(1)} %get-tuple-element.46), channel_id=1, source_target_pairs={{0,1},{1,0},{2,3},{3,2},{4,5},{5,4},{6,7},{7,6},{8,9},{9,8},{10,11... | collective-permute-start | bytes 417800 | tf_op jit(solution)/shard_map/ppermute | solution.py:48
  57.3 6.2 %collective-permute-start.15 = (s16[16,2176]{1,0:T(8,128)(2,1)S(1)}, s16[16,2176]{1,0:T(8,128)(2,1)S(1)}, u32[]{:S(2)}, u32[]{:S(2)}) collective-permute-start(s16[16,2176]{1,0:T(8,128)(2,1)S(1)} %get-tuple-element.45), channel_id=1, source_target_pairs={{0,2},{1,3},{2,0},{3,1},{4,6},{5,7},{6,4},{7,5},{8,10},{9,11},{10,... | collective-permute-start | bytes 208904 | tf_op jit(solution)/shard_map/ppermute | solution.py:48
  61.9 7.4 %collective-permute-start.17 = (s16[16,2176]{1,0:T(8,128)(2,1)S(1)}, s16[16,2176]{1,0:T(8,128)(2,1)S(1)}, u32[]{:S(2)}, u32[]{:S(2)}) collective-permute-start(s16[16,2176]{1,0:T(8,128)(2,1)S(1)} %get-tuple-element.49), channel_id=1, source_target_pairs={{0,2},{1,3},{2,0},{3,1},{4,6},{5,7},{6,4},{7,5},{8,10},{9,11},{10,... | collective-permute-start | bytes 208904 | tf_op jit(solution)/shard_map/ppermute | solution.py:48
  62.6 4.1 %collective-permute-start.18 = (s16[32,640]{1,0:T(8,128)(2,1)S(1)}, s16[32,640]{1,0:T(8,128)(2,1)S(1)}, u32[]{:S(2)}, u32[]{:S(2)}) collective-permute-start(s16[32,640]{1,0:T(8,128)(2,1)S(1)} %get-tuple-element.50), channel_id=1, source_target_pairs={{0,1},{1,0},{2,3},{3,2},{4,5},{5,4},{6,7},{7,6},{8,9},{9,8},{10,11... | collective-permute-start | bytes 122888 | tf_op jit(solution)/shard_map/ppermute | solution.py:48
  66.9 4.8 %collective-permute-start.19 = (s16[16,640]{1,0:T(8,128)(2,1)S(1)}, s16[16,640]{1,0:T(8,128)(2,1)S(1)}, u32[]{:S(2)}, u32[]{:S(2)}) collective-permute-start(s16[16,640]{1,0:T(8,128)(2,1)S(1)} %get-tuple-element.52), channel_id=1, source_target_pairs={{0,2},{1,3},{2,0},{3,1},{4,6},{5,7},{6,4},{7,5},{8,10},{9,11},{10,... | collective-permute-start | bytes 61448 | tf_op jit(solution)/shard_map/ppermute | solution.py:48

commit v13 on v12

--- a/solution.py
+++ b/solution.py
@@ -467,7 +467,7 @@
         flops=BESIDE,
     )
     gathered = gather(returned, "wide")
-    ends = [columns // LANES * k // 18 * LANES for k in (0, 8, 16, 18)]
+    ends = [columns // LANES * k // 18 * LANES for k in (0, 8, 15, 18)]
     cut_sums, halved, last = [], [], []
 
     def exchange_cut(kept, sent, after):

time: 72.6 us -> 70.3 us (0.968)
  waiting for transfers between devices: 28.2 us -> 24.1 us
  starting transfers between devices: 22.6 us -> 24.4 us
    ppermute x20, waiting for transfers between devices: 28.2 us -> 24.1 us  [swap(): return lax.ppermute(x, axis, [(i, i ^ distance) for i in range(count)])]
    ppermute x20, starting transfers between devices: 22.6 us -> 24.4 us  [swap(): return lax.ppermute(x, axis, [(i, i ^ distance) for i in range(count)])]
  transfers between devices with their start and end apart: 20 -> 20, of which waited for: 14 -> 14; matrix products, arithmetic and copies ran while one was open for 0% -> 0% of each run, Pallas kernels for 8% -> 9%
where the time goes in v13:
time: 70.3 us; the launch traced here: 70.1 us
  starting transfers between devices  24.4 us (35%)
  waiting for transfers between devices  24.1 us (34%)
  Pallas kernels  20 us (28%)
  other arithmetic  1.32 us (2%)
    ppermute x20, starting transfers between devices, swap(): return lax.ppermute(x, axis, [(i, i ^ distance) for i in range(count)])  24.4 us
    ppermute x20, waiting for transfers between devices, swap(): return lax.ppermute(x, axis, [(i, i ^ distance) for i in range(count)])  24.1 us
    pallas_call x14, Pallas kernels, call(): pl.pallas_call(kernel, out_shape=outs, in_specs=specs, out_specs=jax.tree...  20 us
  transfers between devices with their start and end apart: 20, of which 14 were waited for; matrix products, arithmetic and copies ran while one was open for 0% of the time, Pallas kernels for 9%

profile of v13, /device:TPU:0, one launch (start us, length us, event | category | flops | bytes accessed | tf_op | source)
XLA Modules:
  0.0 70.1 jit_solution(270092692496028477)
XLA Ops:
  0.0 1.3 %convert_reduce_fusion = (f32[64]{0:T(128)S(1)}, f32[64]{0:T(128)S(1)}) fusion(bf16[64,4608]{1,0:T(8,128)(2,1)} %refs_4_.5), kind=kLoop, calls=%fused_computation.1 | loop fusion | flops 1179520 | bytes 590336 | tf_op jit(solution)/shard_map/reduce_sum | solution.py:433
  1.4 2.5 %collective-permute-start.2 = (f32[2,64]{1,0:T(2,128)S(1)}, f32[2,64]{1,0:T(2,128)S(1)}, u32[]{:S(2)}, u32[]{:S(2)}) collective-permute-start(f32[2,64]{1,0:T(2,128)S(1)} %pad_maximum_fusion.refs_0_), channel_id=1, source_target_pairs={{0,12},{4,8},{8,4},{12,0},{1,13},{5,9},{9,5},{13,1},{2,14},{6,10},... | collective-permute-start | bytes 1544 | tf_op jit(solution)/shard_map/ppermute | solution.py:48
  3.8 0.6 collective-permute-start.1
  4.5 2.3 %fetch_query_weight.1.refs_8_ = bf16[768,3072]{1,0:T(8,128)(2,1)S(1)} custom-call(bf16[4608,3072]{1,0:T(8,128)(2,1)} %refs_6_.1, f32[2,64]{1,0:T(2,128)S(1)} %pad_maximum_fusion.refs_0_), custom_call_target="tpu_custom_call" | custom-call | bytes 4718592 | tf_op jit(solution)/shard_map/fetch_query_weight/pallas_call | solution.py:22
  7.4 8.6 %project.1 = (f32[32,3584]{1,0:T(8,128)S(1)}, f32[32,3584]{1,0:T(8,128)S(1)}) custom-call(f32[2,64]{1,0:T(2,128)S(1)} %pad_maximum_fusion.refs_0_, f32[2,64]{1,0:T(2,128)S(1)} %collective-permute-done.refs_1_, f32[2,64]{1,0:T(2,128)S(1)} %collective-permute-done.1.refs_2_, f32[2,64]{1,0:T(2,128)S(1)} %collective-permute-done.2.refs_3_, ...), custom_call_target="tpu_custom_call" | custom-call | flops 1811939328 | bytes 23592960 | tf_op jit(solution)/shard_map/project/pallas_call | solution.py:22
  16.2 1.8 %collective-permute-done.3.came_ref = f32[32,3584]{1,0:T(8,128)S(1)} collective-permute-done((f32[32,3584]{1,0:T(8,128)S(1)}, f32[32,3584]{1,0:T(8,128)S(1)}, u32[]{:S(2)}, u32[]{:S(2)}) %collective-permute-start.3) | collective-permute-done | bytes 458784 | tf_op jit(solution)/shard_map/ppermute | solution.py:48
  18.0 1.3 %collective-permute-start.4 = (f32[16,3584]{1,0:T(8,128)S(1)}, f32[16,3584]{1,0:T(8,128)S(1)}, u32[]{:S(2)}, u32[]{:S(2)}) collective-permute-start(f32[16,3584]{1,0:T(8,128)S(1)} %get-tuple-element.32), channel_id=1, source_target_pairs={{0,8},{4,12},{8,0},{12,4},{1,9},{5,13},{9,1},{13,5},{2,10},{6,14},... | collective-permute-start | bytes 688136 | tf_op jit(solution)/shard_map/ppermute | solution.py:48
  19.3 6.4 %collective-permute-done.4.came_ref = f32[16,3584]{1,0:T(8,128)S(1)} collective-permute-done((f32[16,3584]{1,0:T(8,128)S(1)}, f32[16,3584]{1,0:T(8,128)S(1)}, u32[]{:S(2)}, u32[]{:S(2)}) %collective-permute-start.4) | collective-permute-done | bytes 229408 | tf_op jit(solution)/shard_map/ppermute | solution.py:48
  25.8 3.7 %collective-permute-start.5 = (bf16[8,2048]{1,0:T(8,128)(2,1)S(1)}, bf16[8,2048]{1,0:T(8,128)(2,1)S(1)}, u32[]{:S(2)}, u32[]{:S(2)}) collective-permute-start(bf16[8,2048]{1,0:T(8,128)(2,1)S(1)} %get-tuple-element.33), channel_id=1, source_target_pairs={{0,3},{1,2},{2,1},{3,0},{4,7},{5,6},{6,5},{7,4},{8,11},{9,10},{10,... | collective-permute-start | bytes 98312 | tf_op jit(solution)/shard_map/ppermute | solution.py:48
  29.5 0.8 %collective-permute-start.7 = (bf16[8,2048]{1,0:T(8,128)(2,1)S(1)}, bf16[8,2048]{1,0:T(8,128)(2,1)S(1)}, u32[]{:S(2)}, u32[]{:S(2)}) collective-permute-start(bf16[8,2048]{1,0:T(8,128)(2,1)S(1)} %get-tuple-element.35), channel_id=1, source_target_pairs={{0,1},{1,0},{2,3},{3,2},{4,5},{5,4},{6,7},{7,6},{8,9},{9,8},{10,11... | collective-permute-start | bytes 98312 | tf_op jit(solution)/shard_map/ppermute | solution.py:48
  30.3 1.5 %collective-permute-done.5.refs_0_ = bf16[8,2048]{1,0:T(8,128)(2,1)S(1)} collective-permute-done((bf16[8,2048]{1,0:T(8,128)(2,1)S(1)}, bf16[8,2048]{1,0:T(8,128)(2,1)S(1)}, u32[]{:S(2)}, u32[]{:S(2)}) %collective-permute-start.5) | collective-permute-done | bytes 32800 | tf_op jit(solution)/shard_map/ppermute | solution.py:48
  31.8 2.5 %collective-permute-done.6.refs_1_ = bf16[8,2048]{1,0:T(8,128)(2,1)S(1)} collective-permute-done((bf16[8,2048]{1,0:T(8,128)(2,1)S(1)}, bf16[8,2048]{1,0:T(8,128)(2,1)S(1)}, u32[]{:S(2)}, u32[]{:S(2)}) %collective-permute-start.6) | collective-permute-done | bytes 32800 | tf_op jit(solution)/shard_map/ppermute | solution.py:48
  34.3 1.9 %attend.1 = (bf16[8,1536]{1,0:T(8,128)(2,1)S(1)}, bf16[8,1536]{1,0:T(8,128)(2,1)S(1)}, bf16[8,1536]{1,0:T(8,128)(2,1)S(1)}, bf16[8,1536]{1,0:T(8,128)(2,1)S(1)}) custom-call(s32[1,4]{1,0:T(1,128)S(1)} %bitcast.5, bf16[8,2048]{1,0:T(8,128)(2,1)S(1)} %collective-permute-done.5.refs_0_, bf16[8,2048]{1,0:T(8,128)(2,1)S(1)} %collective-permute-done.6.refs_1_, ...), custom_call_target="tpu_custom_call" | custom-call | flops 5000000000 | tf_op jit(solution)/shard_map/attend/pallas_call | solution.py:22
  36.2 1.5 %collective-permute-start.8 = (bf16[8,1536]{1,0:T(8,128)(2,1)S(1)}, bf16[8,1536]{1,0:T(8,128)(2,1)S(1)}, u32[]{:S(2)}, u32[]{:S(2)}) collective-permute-start(bf16[8,1536]{1,0:T(8,128)(2,1)S(1)} %get-tuple-element.37), channel_id=1, source_target_pairs={{0,3},{1,2},{2,1},{3,0},{4,7},{5,6},{6,5},{7,4},{8,11},{9,10},{10,... | collective-permute-start | bytes 73736 | tf_op jit(solution)/shard_map/ppermute | solution.py:48
  37.7 0.6 collective-permute-start.9
  38.4 2.3 %collective-permute-start.10 = (bf16[8,1536]{1,0:T(8,128)(2,1)S(1)}, bf16[8,1536]{1,0:T(8,128)(2,1)S(1)}, u32[]{:S(2)}, u32[]{:S(2)}) collective-permute-start(bf16[8,1536]{1,0:T(8,128)(2,1)S(1)} %get-tuple-element.39), channel_id=1, source_target_pairs={{0,1},{1,0},{2,3},{3,2},{4,5},{5,4},{6,7},{7,6},{8,9},{9,8},{10,11... | collective-permute-start | bytes 73736 | tf_op jit(solution)/shard_map/ppermute | solution.py:48
  40.7 1.2 %collective-permute-done.8.refs_0_ = bf16[8,1536]{1,0:T(8,128)(2,1)S(1)} collective-permute-done((bf16[8,1536]{1,0:T(8,128)(2,1)S(1)}, bf16[8,1536]{1,0:T(8,128)(2,1)S(1)}, u32[]{:S(2)}, u32[]{:S(2)}) %collective-permute-start.8) | collective-permute-done | bytes 24608 | tf_op jit(solution)/shard_map/ppermute | solution.py:48
  42.8 1.3 %collective-permute-start.12 = (bf16[16,3072]{1,0:T(8,128)(2,1)S(1)}, bf16[16,3072]{1,0:T(8,128)(2,1)S(1)}, u32[]{:S(2)}, u32[]{:S(2)}) collective-permute-start(bf16[16,3072]{1,0:T(8,128)(2,1)S(1)} %join.1.refs_0_), channel_id=1, source_target_pairs={{0,8},{4,12},{8,0},{12,4},{1,9},{5,13},{9,1},{13,5},{2,10},{6,14},... | collective-permute-start | bytes 294920 | tf_op jit(solution)/shard_map/ppermute | solution.py:48
  44.1 3.4 %collective-permute-done.12.refs_2_ = bf16[16,3072]{1,0:T(8,128)(2,1)S(1)} collective-permute-done((bf16[16,3072]{1,0:T(8,128)(2,1)S(1)}, bf16[16,3072]{1,0:T(8,128)(2,1)S(1)}, u32[]{:S(2)}, u32[]{:S(2)}) %collective-permute-start.12) | collective-permute-done | bytes 98336 | tf_op jit(solution)/shard_map/ppermute | solution.py:48
  47.5 1.3 %collective-permute-done.13.refs_3_ = bf16[16,3072]{1,0:T(8,128)(2,1)S(1)} collective-permute-done((bf16[16,3072]{1,0:T(8,128)(2,1)S(1)}, bf16[16,3072]{1,0:T(8,128)(2,1)S(1)}, u32[]{:S(2)}, u32[]{:S(2)}) %collective-permute-start.13) | collective-permute-done | bytes 98336 | tf_op jit(solution)/shard_map/ppermute | solution.py:48
  48.8 2.4 %output_part.3 = (f32[64,2048]{1,0:T(8,128)S(1)}, s16[32,2176]{1,0:T(8,128)(2,1)S(1)}) custom-call(bf16[16,3072]{1,0:T(8,128)(2,1)S(1)} %join.1.refs_0_, bf16[16,3072]{1,0:T(8,128)(2,1)S(1)} %collective-permute-done.11.refs_1_, bf16[16,3072]{1,0:T(8,128)(2,1)S(1)} %collective-permute-done.12.refs_2_, bf16[16,3072]{1,0:T(8,128)(2,1)S(1)} %collective-permute-done.13.refs_3_, ...), custom_call_target="tpu_custom_call" | custom-call | flops 805306368 | bytes 393216 | tf_op jit(solution)/shard_map/output_part/pallas_call | solution.py:22
  51.2 1.8 %collective-permute-start.14 = (s16[32,2176]{1,0:T(8,128)(2,1)S(1)}, s16[32,2176]{1,0:T(8,128)(2,1)S(1)}, u32[]{:S(2)}, u32[]{:S(2)}) collective-permute-start(s16[32,2176]{1,0:T(8,128)(2,1)S(1)} %get-tuple-element.42), channel_id=1, source_target_pairs={{0,1},{1,0},{2,3},{3,2},{4,5},{5,4},{6,7},{7,6},{8,9},{9,8},{10,11... | collective-permute-start | bytes 417800 | tf_op jit(solution)/shard_map/ppermute | solution.py:48
  53.1 2.1 %output_part.4 = (f32[64,1792]{1,0:T(8,128)S(1)}, s16[32,1920]{1,0:T(8,128)(2,1)S(1)}) custom-call(bf16[16,3072]{1,0:T(8,128)(2,1)S(1)} %join.1.refs_0_, bf16[16,3072]{1,0:T(8,128)(2,1)S(1)} %collective-permute-done.11.refs_1_, bf16[16,3072]{1,0:T(8,128)(2,1)S(1)} %collective-permute-done.12.refs_2_, bf16[16,3072]{1,0:T(8,128)(2,1)S(1)} %collective-permute-done.13.refs_3_, ...), custom_call_target="tpu_custom_call" | custom-call | flops 704643072 | bytes 393216 | tf_op jit(solution)/shard_map/output_part/pallas_call | solution.py:22
  55.5 1.5 %collective-permute-done.14.came_ref = s16[32,2176]{1,0:T(8,128)(2,1)S(1)} collective-permute-done((s16[32,2176]{1,0:T(8,128)(2,1)S(1)}, s16[32,2176]{1,0:T(8,128)(2,1)S(1)}, u32[]{:S(2)}, u32[]{:S(2)}) %collective-permute-start.14) | collective-permute-done | bytes 139296 | tf_op jit(solution)/shard_map/ppermute | solution.py:48
  57.3 1.8 %collective-permute-start.15 = (s16[16,2176]{1,0:T(8,128)(2,1)S(1)}, s16[16,2176]{1,0:T(8,128)(2,1)S(1)}, u32[]{:S(2)}, u32[]{:S(2)}) collective-permute-start(s16[16,2176]{1,0:T(8,128)(2,1)S(1)} %get-tuple-element.45), channel_id=1, source_target_pairs={{0,2},{1,3},{2,0},{3,1},{4,6},{5,7},{6,4},{7,5},{8,10},{9,11},{10,... | collective-permute-start | bytes 208904 | tf_op jit(solution)/shard_map/ppermute | solution.py:48
  59.0 1.0 %output_part.5 = (f32[64,768]{1,0:T(8,128)S(1)}, s16[32,896]{1,0:T(8,128)(2,1)S(1)}) custom-call(bf16[16,3072]{1,0:T(8,128)(2,1)S(1)} %join.1.refs_0_, bf16[16,3072]{1,0:T(8,128)(2,1)S(1)} %collective-permute-done.11.refs_1_, bf16[16,3072]{1,0:T(8,128)(2,1)S(1)} %collective-permute-done.12.refs_2_, bf16[16,3072]{1,0:T(8,128)(2,1)S(1)} %collective-permute-done.13.refs_3_, ...), custom_call_target="tpu_custom_call" | custom-call | flops 301989888 | bytes 393216 | tf_op jit(solution)/shard_map/output_part/pallas_call | solution.py:22
  60.1 1.4 %collective-permute-start.18 = (s16[32,896]{1,0:T(8,128)(2,1)S(1)}, s16[32,896]{1,0:T(8,128)(2,1)S(1)}, u32[]{:S(2)}, u32[]{:S(2)}) collective-permute-start(s16[32,896]{1,0:T(8,128)(2,1)S(1)} %get-tuple-element.50), channel_id=1, source_target_pairs={{0,1},{1,0},{2,3},{3,2},{4,5},{5,4},{6,7},{7,6},{8,9},{9,8},{10,11... | collective-permute-start | bytes 172040 | tf_op jit(solution)/shard_map/ppermute | solution.py:48
  61.7 2.4 %collective-permute-start.17 = (s16[16,1920]{1,0:T(8,128)(2,1)S(1)}, s16[16,1920]{1,0:T(8,128)(2,1)S(1)}, u32[]{:S(2)}, u32[]{:S(2)}) collective-permute-start(s16[16,1920]{1,0:T(8,128)(2,1)S(1)} %get-tuple-element.49), channel_id=1, source_target_pairs={{0,2},{1,3},{2,0},{3,1},{4,6},{5,7},{6,4},{7,5},{8,10},{9,11},{10,... | collective-permute-start | bytes 184328 | tf_op jit(solution)/shard_map/ppermute | solution.py:48
  64.6 1.9 %collective-permute-start.19 = (s16[16,896]{1,0:T(8,128)(2,1)S(1)}, s16[16,896]{1,0:T(8,128)(2,1)S(1)}, u32[]{:S(2)}, u32[]{:S(2)}) collective-permute-start(s16[16,896]{1,0:T(8,128)(2,1)S(1)} %get-tuple-element.52), channel_id=1, source_target_pairs={{0,2},{1,3},{2,0},{3,1},{4,6},{5,7},{6,4},{7,5},{8,10},{9,11},{10,... | collective-permute-start | bytes 86024 | tf_op jit(solution)/shard_map/ppermute | solution.py:48
  66.5 1.6 %collective-permute-done.17.refs_2_ = s16[16,1920]{1,0:T(8,128)(2,1)S(1)} collective-permute-done((s16[16,1920]{1,0:T(8,128)(2,1)S(1)}, s16[16,1920]{1,0:T(8,128)(2,1)S(1)}, u32[]{:S(2)}, u32[]{:S(2)}) %collective-permute-start.17) | collective-permute-done | bytes 61472 | tf_op jit(solution)/shard_map/ppermute | solution.py:48
  68.1 1.3 %collective-permute-done.19.refs_4_ = s16[16,896]{1,0:T(8,128)(2,1)S(1)} collective-permute-done((s16[16,896]{1,0:T(8,128)(2,1)S(1)}, s16[16,896]{1,0:T(8,128)(2,1)S(1)}, u32[]{:S(2)}, u32[]{:S(2)}) %collective-permute-start.19) | collective-permute-done | bytes 28704 | tf_op jit(solution)/shard_map/ppermute | solution.py:48
  69.4 0.8 %finish.3 = bf16[16,4608]{1,0:T(8,128)(2,1)} custom-call(bf16[16,2048]{1,0:T(8,128)(2,1)S(1)} %finish.2.refs_0_, f32[16,1792]{1,0:T(8,128)S(1)} %get-tuple-element.48.refs_1_, s16[16,1920]{1,0:T(8,128)(2,1)S(1)} %collective-permute-done.17.refs_2_, f32[16,768]{1,0:T(8,128)S(1)} %get-tuple-element.51.refs_3_, s16[16,896]{1,0:T(8,128)(2,1)S(1)} %collective-permute-done.19.refs_4_), custom_call_target="tpu_custom_call" | custom-call | bytes 589824 | tf_op jit(solution)/shard_map/finish/pallas_call | solution.py:22
  (49 shorter events, 2.9 us)
Async XLA Ops:
  1.3 6.1 %copy-start = (bf16[64,4608]{1,0:T(8,128)(2,1)S(1)}, bf16[64,4608]{1,0:T(8,128)(2,1)}, u32[]{:S(2)}) copy-start(bf16[64,4608]{1,0:T(8,128)(2,1)} %refs_4_.5) | copy-start | bytes 1769476
  1.3 6.1 %copy-start.1 = (bf16[1152,512]{1,0:T(8,128)(2,1)S(1)}, bf16[1152,512]{1,0:T(8,128)(2,1)}, u32[]{:S(2)}) copy-start(bf16[1152,512]{1,0:T(8,128)(2,1)} %refs_7_.1) | copy-start | bytes 3538948
  1.4 6.1 %copy-start.2 = (f32[4608]{0:T(1024)S(1)}, f32[4608]{0:T(1024)}, u32[]{:S(2)}) copy-start(f32[4608]{0:T(1024)} %refs_5_.1) | copy-start | bytes 55300
  1.4 5.5 %collective-permute-start.2 = (f32[2,64]{1,0:T(2,128)S(1)}, f32[2,64]{1,0:T(2,128)S(1)}, u32[]{:S(2)}, u32[]{:S(2)}) collective-permute-start(f32[2,64]{1,0:T(2,128)S(1)} %pad_maximum_fusion.refs_0_), channel_id=1, source_target_pairs={{0,12},{4,8},{8,4},{12,0},{1,13},{5,9},{9,5},{13,1},{2,14},{6,10},... | collective-permute-start | bytes 1544 | tf_op jit(solution)/shard_map/ppermute | solution.py:48
  3.8 3.6 %collective-permute-start.1 = (f32[2,64]{1,0:T(2,128)S(1)}, f32[2,64]{1,0:T(2,128)S(1)}, u32[]{:S(2)}, u32[]{:S(2)}) collective-permute-start(f32[2,64]{1,0:T(2,128)S(1)} %pad_maximum_fusion.refs_0_), channel_id=1, source_target_pairs={{0,8},{4,12},{8,0},{12,4},{1,9},{5,13},{9,1},{13,5},{2,10},{6,14},... | collective-permute-start | bytes 1544 | tf_op jit(solution)/shard_map/ppermute | solution.py:48
  4.5 2.9 %collective-permute-start = (f32[2,64]{1,0:T(2,128)S(1)}, f32[2,64]{1,0:T(2,128)S(1)}, u32[]{:S(2)}, u32[]{:S(2)}) collective-permute-start(f32[2,64]{1,0:T(2,128)S(1)} %pad_maximum_fusion.refs_0_), channel_id=1, source_target_pairs={{0,4},{4,0},{8,12},{12,8},{1,5},{5,1},{9,13},{13,9},{2,6},{6,2},{1... | collective-permute-start | bytes 1544 | tf_op jit(solution)/shard_map/ppermute | solution.py:48
  16.1 1.9 %collective-permute-start.3 = (f32[32,3584]{1,0:T(8,128)S(1)}, f32[32,3584]{1,0:T(8,128)S(1)}, u32[]{:S(2)}, u32[]{:S(2)}) collective-permute-start(f32[32,3584]{1,0:T(8,128)S(1)} %get-tuple-element.30), channel_id=1, source_target_pairs={{0,4},{4,0},{8,12},{12,8},{1,5},{5,1},{9,13},{13,9},{2,6},{6,2},{1... | collective-permute-start | bytes 1376264 | tf_op jit(solution)/shard_map/ppermute | solution.py:48
  18.0 7.7 %collective-permute-start.4 = (f32[16,3584]{1,0:T(8,128)S(1)}, f32[16,3584]{1,0:T(8,128)S(1)}, u32[]{:S(2)}, u32[]{:S(2)}) collective-permute-start(f32[16,3584]{1,0:T(8,128)S(1)} %get-tuple-element.32), channel_id=1, source_target_pairs={{0,8},{4,12},{8,0},{12,4},{1,9},{5,13},{9,1},{13,5},{2,10},{6,14},... | collective-permute-start | bytes 688136 | tf_op jit(solution)/shard_map/ppermute | solution.py:48
  25.7 8.6 %copy-start.3 = (bf16[4,1024,512]{2,1,0:T(8,128)(2,1)S(1)}, bf16[4,1024,512]{2,1,0:T(8,128)(2,1)}, u32[]{:S(2)}) copy-start(bf16[4,1024,512]{2,1,0:T(8,128)(2,1)} %refs_4_.6) | copy-start | bytes 12582916
  25.7 8.6 %copy-start.4 = (s32[4]{0:T(128)S(1)}, s32[4]{0:T(128)}, u32[]{:S(2)}) copy-start(s32[4]{0:T(128)} %param.13) | copy-start | bytes 52
  25.7 23.0 %slice-start = ((s8[28311552]{0:T(1024)(128)(4,1)}), s8[4194304]{0:T(1024)(128)(4,1)S(1)}, s32[]{:S(2)}) async-start(s8[28311552]{0:T(1024)(128)(4,1)} %bitcast.3), calls=%async_computation | async-start | bytes 8388608
  25.7 23.0 %slice-start.1 = ((s8[28311552]{0:T(1024)(128)(4,1)}), s8[4194304]{0:T(1024)(128)(4,1)S(1)}, s32[]{:S(2)}) async-start(s8[28311552]{0:T(1024)(128)(4,1)} %bitcast.3), calls=%async_computation.1 | async-start | bytes 8388608
  25.7 23.0 %slice-start.2 = ((s8[28311552]{0:T(1024)(128)(4,1)}), s8[4194304]{0:T(1024)(128)(4,1)S(1)}, s32[]{:S(2)}) async-start(s8[28311552]{0:T(1024)(128)(4,1)} %bitcast.3), calls=%async_computation.2 | async-start | bytes 8388608
  25.8 6.0 %collective-permute-start.5 = (bf16[8,2048]{1,0:T(8,128)(2,1)S(1)}, bf16[8,2048]{1,0:T(8,128)(2,1)S(1)}, u32[]{:S(2)}, u32[]{:S(2)}) collective-permute-start(bf16[8,2048]{1,0:T(8,128)(2,1)S(1)} %get-tuple-element.33), channel_id=1, source_target_pairs={{0,3},{1,2},{2,1},{3,0},{4,7},{5,6},{6,5},{7,4},{8,11},{9,10},{10,... | collective-permute-start | bytes 98312 | tf_op jit(solution)/shard_map/ppermute | solution.py:48
  29.5 4.8 %collective-permute-start.6 = (bf16[8,2048]{1,0:T(8,128)(2,1)S(1)}, bf16[8,2048]{1,0:T(8,128)(2,1)S(1)}, u32[]{:S(2)}, u32[]{:S(2)}) collective-permute-start(bf16[8,2048]{1,0:T(8,128)(2,1)S(1)} %get-tuple-element.34), channel_id=1, source_target_pairs={{0,2},{1,3},{2,0},{3,1},{4,6},{5,7},{6,4},{7,5},{8,10},{9,11},{10,... | collective-permute-start | bytes 98312 | tf_op jit(solution)/shard_map/ppermute | solution.py:48
  29.5 4.8 %collective-permute-start.7 = (bf16[8,2048]{1,0:T(8,128)(2,1)S(1)}, bf16[8,2048]{1,0:T(8,128)(2,1)S(1)}, u32[]{:S(2)}, u32[]{:S(2)}) collective-permute-start(bf16[8,2048]{1,0:T(8,128)(2,1)S(1)} %get-tuple-element.35), channel_id=1, source_target_pairs={{0,1},{1,0},{2,3},{3,2},{4,5},{5,4},{6,7},{7,6},{8,9},{9,8},{10,11... | collective-permute-start | bytes 98312 | tf_op jit(solution)/shard_map/ppermute | solution.py:48
  34.3 14.5 %slice-start.3 = ((s8[28311552]{0:T(1024)(128)(4,1)}), s8[4194304]{0:T(1024)(128)(4,1)S(1)}, s32[]{:S(2)}) async-start(s8[28311552]{0:T(1024)(128)(4,1)} %bitcast.3), calls=%async_computation.3 | async-start | bytes 8388608
  34.3 14.5 %slice-start.4 = ((s8[28311552]{0:T(1024)(128)(4,1)}), s8[4194304]{0:T(1024)(128)(4,1)S(1)}, s32[]{:S(2)}) async-start(s8[28311552]{0:T(1024)(128)(4,1)} %bitcast.3), calls=%async_computation.4 | async-start | bytes 8388608
  36.2 5.7 %collective-permute-start.8 = (bf16[8,1536]{1,0:T(8,128)(2,1)S(1)}, bf16[8,1536]{1,0:T(8,128)(2,1)S(1)}, u32[]{:S(2)}, u32[]{:S(2)}) collective-permute-start(bf16[8,1536]{1,0:T(8,128)(2,1)S(1)} %get-tuple-element.37), channel_id=1, source_target_pairs={{0,3},{1,2},{2,1},{3,0},{4,7},{5,6},{6,5},{7,4},{8,11},{9,10},{10,... | collective-permute-start | bytes 73736 | tf_op jit(solution)/shard_map/ppermute | solution.py:48
  37.7 4.7 %collective-permute-start.9 = (bf16[8,1536]{1,0:T(8,128)(2,1)S(1)}, bf16[8,1536]{1,0:T(8,128)(2,1)S(1)}, u32[]{:S(2)}, u32[]{:S(2)}) collective-permute-start(bf16[8,1536]{1,0:T(8,128)(2,1)S(1)} %get-tuple-element.38), channel_id=1, source_target_pairs={{0,2},{1,3},{2,0},{3,1},{4,6},{5,7},{6,4},{7,5},{8,10},{9,11},{10,... | collective-permute-start | bytes 73736 | tf_op jit(solution)/shard_map/ppermute | solution.py:48
  38.4 4.3 %collective-permute-start.10 = (bf16[8,1536]{1,0:T(8,128)(2,1)S(1)}, bf16[8,1536]{1,0:T(8,128)(2,1)S(1)}, u32[]{:S(2)}, u32[]{:S(2)}) collective-permute-start(bf16[8,1536]{1,0:T(8,128)(2,1)S(1)} %get-tuple-element.39), channel_id=1, source_target_pairs={{0,1},{1,0},{2,3},{3,2},{4,5},{5,4},{6,7},{7,6},{8,9},{9,8},{10,11... | collective-permute-start | bytes 73736 | tf_op jit(solution)/shard_map/ppermute | solution.py:48
  42.7 6.1 %slice-start.5 = ((s8[28311552]{0:T(1024)(128)(4,1)}), s8[4194304]{0:T(1024)(128)(4,1)S(1)}, s32[]{:S(2)}) async-start(s8[28311552]{0:T(1024)(128)(4,1)} %bitcast.3), calls=%async_computation.5 | async-start | bytes 8388608
  42.7 6.1 %slice-start.6 = ((s8[28311552]{0:T(1024)(128)(4,1)}), s8[3145728]{0:T(1024)(128)(4,1)S(1)}, s32[]{:S(2)}) async-start(s8[28311552]{0:T(1024)(128)(4,1)} %bitcast.3), calls=%async_computation.6 | async-start | bytes 6291456
  42.8 4.7 %collective-permute-start.12 = (bf16[16,3072]{1,0:T(8,128)(2,1)S(1)}, bf16[16,3072]{1,0:T(8,128)(2,1)S(1)}, u32[]{:S(2)}, u32[]{:S(2)}) collective-permute-start(bf16[16,3072]{1,0:T(8,128)(2,1)S(1)} %join.1.refs_0_), channel_id=1, source_target_pairs={{0,8},{4,12},{8,0},{12,4},{1,9},{5,13},{9,1},{13,5},{2,10},{6,14},... | collective-permute-start | bytes 294920 | tf_op jit(solution)/shard_map/ppermute | solution.py:48
  44.1 3.4 %collective-permute-start.11 = (bf16[16,3072]{1,0:T(8,128)(2,1)S(1)}, bf16[16,3072]{1,0:T(8,128)(2,1)S(1)}, u32[]{:S(2)}, u32[]{:S(2)}) collective-permute-start(bf16[16,3072]{1,0:T(8,128)(2,1)S(1)} %join.1.refs_0_), channel_id=1, source_target_pairs={{0,4},{4,0},{8,12},{12,8},{1,5},{5,1},{9,13},{13,9},{2,6},{6,2},{1... | collective-permute-start | bytes 294920 | tf_op jit(solution)/shard_map/ppermute | solution.py:48
  47.4 1.3 %collective-permute-start.13 = (bf16[16,3072]{1,0:T(8,128)(2,1)S(1)}, bf16[16,3072]{1,0:T(8,128)(2,1)S(1)}, u32[]{:S(2)}, u32[]{:S(2)}) collective-permute-start(bf16[16,3072]{1,0:T(8,128)(2,1)S(1)} %collective-permute-done.12.refs_2_), channel_id=1, source_target_pairs={{0,4},{4,0},{8,12},{12,8},{1,5},{5,1},{9,13},{13,9},{2,6},{6,2},{1... | collective-permute-start | bytes 294920 | tf_op jit(solution)/shard_map/ppermute | solution.py:48
  51.2 5.8 %collective-permute-start.14 = (s16[32,2176]{1,0:T(8,128)(2,1)S(1)}, s16[32,2176]{1,0:T(8,128)(2,1)S(1)}, u32[]{:S(2)}, u32[]{:S(2)}) collective-permute-start(s16[32,2176]{1,0:T(8,128)(2,1)S(1)} %get-tuple-element.42), channel_id=1, source_target_pairs={{0,1},{1,0},{2,3},{3,2},{4,5},{5,4},{6,7},{7,6},{8,9},{9,8},{10,11... | collective-permute-start | bytes 417800 | tf_op jit(solution)/shard_map/ppermute | solution.py:48
  55.2 6.3 %collective-permute-start.16 = (s16[32,1920]{1,0:T(8,128)(2,1)S(1)}, s16[32,1920]{1,0:T(8,128)(2,1)S(1)}, u32[]{:S(2)}, u32[]{:S(2)}) collective-permute-start(s16[32,1920]{1,0:T(8,128)(2,1)S(1)} %get-tuple-element.46), channel_id=1, source_target_pairs={{0,1},{1,0},{2,3},{3,2},{4,5},{5,4},{6,7},{7,6},{8,9},{9,8},{10,11... | collective-permute-start | bytes 368648 | tf_op jit(solution)/shard_map/ppermute | solution.py:48
  57.3 6.8 %collective-permute-start.15 = (s16[16,2176]{1,0:T(8,128)(2,1)S(1)}, s16[16,2176]{1,0:T(8,128)(2,1)S(1)}, u32[]{:S(2)}, u32[]{:S(2)}) collective-permute-start(s16[16,2176]{1,0:T(8,128)(2,1)S(1)} %get-tuple-element.45), channel_id=1, source_target_pairs={{0,2},{1,3},{2,0},{3,1},{4,6},{5,7},{6,4},{7,5},{8,10},{9,11},{10,... | collective-permute-start | bytes 208904 | tf_op jit(solution)/shard_map/ppermute | solution.py:48
  60.1 4.3 %collective-permute-start.18 = (s16[32,896]{1,0:T(8,128)(2,1)S(1)}, s16[32,896]{1,0:T(8,128)(2,1)S(1)}, u32[]{:S(2)}, u32[]{:S(2)}) collective-permute-start(s16[32,896]{1,0:T(8,128)(2,1)S(1)} %get-tuple-element.50), channel_id=1, source_target_pairs={{0,1},{1,0},{2,3},{3,2},{4,5},{5,4},{6,7},{7,6},{8,9},{9,8},{10,11... | collective-permute-start | bytes 172040 | tf_op jit(solution)/shard_map/ppermute | solution.py:48
  61.7 6.5 %collective-permute-start.17 = (s16[16,1920]{1,0:T(8,128)(2,1)S(1)}, s16[16,1920]{1,0:T(8,128)(2,1)S(1)}, u32[]{:S(2)}, u32[]{:S(2)}) collective-permute-start(s16[16,1920]{1,0:T(8,128)(2,1)S(1)} %get-tuple-element.49), channel_id=1, source_target_pairs={{0,2},{1,3},{2,0},{3,1},{4,6},{5,7},{6,4},{7,5},{8,10},{9,11},{10,... | collective-permute-start | bytes 184328 | tf_op jit(solution)/shard_map/ppermute | solution.py:48
  64.6 4.8 %collective-permute-start.19 = (s16[16,896]{1,0:T(8,128)(2,1)S(1)}, s16[16,896]{1,0:T(8,128)(2,1)S(1)}, u32[]{:S(2)}, u32[]{:S(2)}) collective-permute-start(s16[16,896]{1,0:T(8,128)(2,1)S(1)} %get-tuple-element.52), channel_id=1, source_target_pairs={{0,2},{1,3},{2,0},{3,1},{4,6},{5,7},{6,4},{7,5},{8,10},{9,11},{10,... | collective-permute-start | bytes 86024 | tf_op jit(solution)/shard_map/ppermute | solution.py:48

commit v14 on v13

--- a/solution.py
+++ b/solution.py
@@ -467,7 +467,7 @@
         flops=BESIDE,
     )
     gathered = gather(returned, "wide")
-    ends = [columns // LANES * k // 18 * LANES for k in (0, 8, 15, 18)]
+    ends = [columns // LANES * k // 18 * LANES for k in (0, 7, 15, 18)]
     cut_sums, halved, last = [], [], []
 
     def exchange_cut(kept, sent, after):

time: 70.3 us -> 69.8 us (level)
  starting transfers between devices: 24.4 us -> 22.4 us
  waiting for transfers between devices: 24.1 us -> 25.6 us
    ppermute x20, starting transfers between devices: 24.4 us -> 22.4 us  [swap(): return lax.ppermute(x, axis, [(i, i ^ distance) for i in range(count)])]
    ppermute x20, waiting for transfers between devices: 24.1 us -> 25.6 us  [swap(): return lax.ppermute(x, axis, [(i, i ^ distance) for i in range(count)])]
  transfers between devices with their start and end apart: 20 -> 20, of which waited for: 14 -> 15; matrix products, arithmetic and copies ran while one was open for 0% -> 0% of each run, Pallas kernels for 9% -> 9%
where the time goes in v14:
time: 69.8 us; the launch traced here: 69.6 us
  waiting for transfers between devices  25.6 us (37%)
  starting transfers between devices  22.4 us (32%)
  Pallas kernels  20 us (29%)
  other arithmetic  1.32 us (2%)
    ppermute x20, waiting for transfers between devices, swap(): return lax.ppermute(x, axis, [(i, i ^ distance) for i in range(count)])  25.6 us
    ppermute x20, starting transfers between devices, swap(): return lax.ppermute(x, axis, [(i, i ^ distance) for i in range(count)])  22.4 us
    pallas_call x14, Pallas kernels, call(): pl.pallas_call(kernel, out_shape=outs, in_specs=specs, out_specs=jax.tree...  20 us
  transfers between devices with their start and end apart: 20, of which 15 were waited for; matrix products, arithmetic and copies ran while one was open for 0% of the time, Pallas kernels for 9%

profile of v14, /device:TPU:0, one launch (start us, length us, event | category | flops | bytes accessed | tf_op | source)
XLA Modules:
  0.0 69.6 jit_solution(14581717865727322271)
XLA Ops:
  0.0 1.3 %convert_reduce_fusion = (f32[64]{0:T(128)S(1)}, f32[64]{0:T(128)S(1)}) fusion(bf16[64,4608]{1,0:T(8,128)(2,1)} %refs_4_.5), kind=kLoop, calls=%fused_computation.1 | loop fusion | flops 1179520 | bytes 590336 | tf_op jit(solution)/shard_map/reduce_sum | solution.py:433
  1.4 2.5 %collective-permute-start.2 = (f32[2,64]{1,0:T(2,128)S(1)}, f32[2,64]{1,0:T(2,128)S(1)}, u32[]{:S(2)}, u32[]{:S(2)}) collective-permute-start(f32[2,64]{1,0:T(2,128)S(1)} %pad_maximum_fusion.refs_0_), channel_id=1, source_target_pairs={{0,12},{4,8},{8,4},{12,0},{1,13},{5,9},{9,5},{13,1},{2,14},{6,10},... | collective-permute-start | bytes 1544 | tf_op jit(solution)/shard_map/ppermute | solution.py:48
  4.5 2.3 %fetch_query_weight.1.refs_8_ = bf16[768,3072]{1,0:T(8,128)(2,1)S(1)} custom-call(bf16[4608,3072]{1,0:T(8,128)(2,1)} %refs_6_.1, f32[2,64]{1,0:T(2,128)S(1)} %pad_maximum_fusion.refs_0_), custom_call_target="tpu_custom_call" | custom-call | bytes 4718592 | tf_op jit(solution)/shard_map/fetch_query_weight/pallas_call | solution.py:22
  7.4 8.6 %project.1 = (f32[32,3584]{1,0:T(8,128)S(1)}, f32[32,3584]{1,0:T(8,128)S(1)}) custom-call(f32[2,64]{1,0:T(2,128)S(1)} %pad_maximum_fusion.refs_0_, f32[2,64]{1,0:T(2,128)S(1)} %collective-permute-done.refs_1_, f32[2,64]{1,0:T(2,128)S(1)} %collective-permute-done.1.refs_2_, f32[2,64]{1,0:T(2,128)S(1)} %collective-permute-done.2.refs_3_, ...), custom_call_target="tpu_custom_call" | custom-call | flops 1811939328 | bytes 23592960 | tf_op jit(solution)/shard_map/project/pallas_call | solution.py:22
  16.2 1.8 %collective-permute-done.3.came_ref = f32[32,3584]{1,0:T(8,128)S(1)} collective-permute-done((f32[32,3584]{1,0:T(8,128)S(1)}, f32[32,3584]{1,0:T(8,128)S(1)}, u32[]{:S(2)}, u32[]{:S(2)}) %collective-permute-start.3) | collective-permute-done | bytes 458784 | tf_op jit(solution)/shard_map/ppermute | solution.py:48
  18.0 1.3 %collective-permute-start.4 = (f32[16,3584]{1,0:T(8,128)S(1)}, f32[16,3584]{1,0:T(8,128)S(1)}, u32[]{:S(2)}, u32[]{:S(2)}) collective-permute-start(f32[16,3584]{1,0:T(8,128)S(1)} %get-tuple-element.32), channel_id=1, source_target_pairs={{0,8},{4,12},{8,0},{12,4},{1,9},{5,13},{9,1},{13,5},{2,10},{6,14},... | collective-permute-start | bytes 688136 | tf_op jit(solution)/shard_map/ppermute | solution.py:48
  19.3 6.4 %collective-permute-done.4.came_ref = f32[16,3584]{1,0:T(8,128)S(1)} collective-permute-done((f32[16,3584]{1,0:T(8,128)S(1)}, f32[16,3584]{1,0:T(8,128)S(1)}, u32[]{:S(2)}, u32[]{:S(2)}) %collective-permute-start.4) | collective-permute-done | bytes 229408 | tf_op jit(solution)/shard_map/ppermute | solution.py:48
  25.8 3.7 %collective-permute-start.5 = (bf16[8,2048]{1,0:T(8,128)(2,1)S(1)}, bf16[8,2048]{1,0:T(8,128)(2,1)S(1)}, u32[]{:S(2)}, u32[]{:S(2)}) collective-permute-start(bf16[8,2048]{1,0:T(8,128)(2,1)S(1)} %get-tuple-element.33), channel_id=1, source_target_pairs={{0,3},{1,2},{2,1},{3,0},{4,7},{5,6},{6,5},{7,4},{8,11},{9,10},{10,... | collective-permute-start | bytes 98312 | tf_op jit(solution)/shard_map/ppermute | solution.py:48
  29.5 0.8 %collective-permute-start.7 = (bf16[8,2048]{1,0:T(8,128)(2,1)S(1)}, bf16[8,2048]{1,0:T(8,128)(2,1)S(1)}, u32[]{:S(2)}, u32[]{:S(2)}) collective-permute-start(bf16[8,2048]{1,0:T(8,128)(2,1)S(1)} %get-tuple-element.35), channel_id=1, source_target_pairs={{0,1},{1,0},{2,3},{3,2},{4,5},{5,4},{6,7},{7,6},{8,9},{9,8},{10,11... | collective-permute-start | bytes 98312 | tf_op jit(solution)/shard_map/ppermute | solution.py:48
  30.3 1.5 %collective-permute-done.5.refs_0_ = bf16[8,2048]{1,0:T(8,128)(2,1)S(1)} collective-permute-done((bf16[8,2048]{1,0:T(8,128)(2,1)S(1)}, bf16[8,2048]{1,0:T(8,128)(2,1)S(1)}, u32[]{:S(2)}, u32[]{:S(2)}) %collective-permute-start.5) | collective-permute-done | bytes 32800 | tf_op jit(solution)/shard_map/ppermute | solution.py:48
  31.8 2.5 %collective-permute-done.6.refs_1_ = bf16[8,2048]{1,0:T(8,128)(2,1)S(1)} collective-permute-done((bf16[8,2048]{1,0:T(8,128)(2,1)S(1)}, bf16[8,2048]{1,0:T(8,128)(2,1)S(1)}, u32[]{:S(2)}, u32[]{:S(2)}) %collective-permute-start.6) | collective-permute-done | bytes 32800 | tf_op jit(solution)/shard_map/ppermute | solution.py:48
  34.3 1.9 %attend.1 = (bf16[8,1536]{1,0:T(8,128)(2,1)S(1)}, bf16[8,1536]{1,0:T(8,128)(2,1)S(1)}, bf16[8,1536]{1,0:T(8,128)(2,1)S(1)}, bf16[8,1536]{1,0:T(8,128)(2,1)S(1)}) custom-call(s32[1,4]{1,0:T(1,128)S(1)} %bitcast.5, bf16[8,2048]{1,0:T(8,128)(2,1)S(1)} %collective-permute-done.5.refs_0_, bf16[8,2048]{1,0:T(8,128)(2,1)S(1)} %collective-permute-done.6.refs_1_, ...), custom_call_target="tpu_custom_call" | custom-call | flops 5000000000 | tf_op jit(solution)/shard_map/attend/pallas_call | solution.py:22
  36.2 1.5 %collective-permute-start.8 = (bf16[8,1536]{1,0:T(8,128)(2,1)S(1)}, bf16[8,1536]{1,0:T(8,128)(2,1)S(1)}, u32[]{:S(2)}, u32[]{:S(2)}) collective-permute-start(bf16[8,1536]{1,0:T(8,128)(2,1)S(1)} %get-tuple-element.37), channel_id=1, source_target_pairs={{0,3},{1,2},{2,1},{3,0},{4,7},{5,6},{6,5},{7,4},{8,11},{9,10},{10,... | collective-permute-start | bytes 73736 | tf_op jit(solution)/shard_map/ppermute | solution.py:48
  38.4 2.3 %collective-permute-start.10 = (bf16[8,1536]{1,0:T(8,128)(2,1)S(1)}, bf16[8,1536]{1,0:T(8,128)(2,1)S(1)}, u32[]{:S(2)}, u32[]{:S(2)}) collective-permute-start(bf16[8,1536]{1,0:T(8,128)(2,1)S(1)} %get-tuple-element.39), channel_id=1, source_target_pairs={{0,1},{1,0},{2,3},{3,2},{4,5},{5,4},{6,7},{7,6},{8,9},{9,8},{10,11... | collective-permute-start | bytes 73736 | tf_op jit(solution)/shard_map/ppermute | solution.py:48
  40.7 1.2 %collective-permute-done.8.refs_0_ = bf16[8,1536]{1,0:T(8,128)(2,1)S(1)} collective-permute-done((bf16[8,1536]{1,0:T(8,128)(2,1)S(1)}, bf16[8,1536]{1,0:T(8,128)(2,1)S(1)}, u32[]{:S(2)}, u32[]{:S(2)}) %collective-permute-start.8) | collective-permute-done | bytes 24608 | tf_op jit(solution)/shard_map/ppermute | solution.py:48
  42.8 1.3 %collective-permute-start.12 = (bf16[16,3072]{1,0:T(8,128)(2,1)S(1)}, bf16[16,3072]{1,0:T(8,128)(2,1)S(1)}, u32[]{:S(2)}, u32[]{:S(2)}) collective-permute-start(bf16[16,3072]{1,0:T(8,128)(2,1)S(1)} %join.1.refs_0_), channel_id=1, source_target_pairs={{0,8},{4,12},{8,0},{12,4},{1,9},{5,13},{9,1},{13,5},{2,10},{6,14},... | collective-permute-start | bytes 294920 | tf_op jit(solution)/shard_map/ppermute | solution.py:48
  44.1 3.4 %collective-permute-done.12.refs_2_ = bf16[16,3072]{1,0:T(8,128)(2,1)S(1)} collective-permute-done((bf16[16,3072]{1,0:T(8,128)(2,1)S(1)}, bf16[16,3072]{1,0:T(8,128)(2,1)S(1)}, u32[]{:S(2)}, u32[]{:S(2)}) %collective-permute-start.12) | collective-permute-done | bytes 98336 | tf_op jit(solution)/shard_map/ppermute | solution.py:48
  47.5 1.3 %collective-permute-done.13.refs_3_ = bf16[16,3072]{1,0:T(8,128)(2,1)S(1)} collective-permute-done((bf16[16,3072]{1,0:T(8,128)(2,1)S(1)}, bf16[16,3072]{1,0:T(8,128)(2,1)S(1)}, u32[]{:S(2)}, u32[]{:S(2)}) %collective-permute-start.13) | collective-permute-done | bytes 98336 | tf_op jit(solution)/shard_map/ppermute | solution.py:48
  48.8 2.1 %output_part.3 = (f32[64,1792]{1,0:T(8,128)S(1)}, s16[32,1920]{1,0:T(8,128)(2,1)S(1)}) custom-call(bf16[16,3072]{1,0:T(8,128)(2,1)S(1)} %join.1.refs_0_, bf16[16,3072]{1,0:T(8,128)(2,1)S(1)} %collective-permute-done.11.refs_1_, bf16[16,3072]{1,0:T(8,128)(2,1)S(1)} %collective-permute-done.12.refs_2_, bf16[16,3072]{1,0:T(8,128)(2,1)S(1)} %collective-permute-done.13.refs_3_, ...), custom_call_target="tpu_custom_call" | custom-call | flops 704643072 | bytes 393216 | tf_op jit(solution)/shard_map/output_part/pallas_call | solution.py:22
  51.0 1.8 %collective-permute-start.14 = (s16[32,1920]{1,0:T(8,128)(2,1)S(1)}, s16[32,1920]{1,0:T(8,128)(2,1)S(1)}, u32[]{:S(2)}, u32[]{:S(2)}) collective-permute-start(s16[32,1920]{1,0:T(8,128)(2,1)S(1)} %get-tuple-element.42), channel_id=1, source_target_pairs={{0,1},{1,0},{2,3},{3,2},{4,5},{5,4},{6,7},{7,6},{8,9},{9,8},{10,11... | collective-permute-start | bytes 368648 | tf_op jit(solution)/shard_map/ppermute | solution.py:48
  52.8 2.4 %output_part.4 = (f32[64,2048]{1,0:T(8,128)S(1)}, s16[32,2176]{1,0:T(8,128)(2,1)S(1)}) custom-call(bf16[16,3072]{1,0:T(8,128)(2,1)S(1)} %join.1.refs_0_, bf16[16,3072]{1,0:T(8,128)(2,1)S(1)} %collective-permute-done.11.refs_1_, bf16[16,3072]{1,0:T(8,128)(2,1)S(1)} %collective-permute-done.12.refs_2_, bf16[16,3072]{1,0:T(8,128)(2,1)S(1)} %collective-permute-done.13.refs_3_, ...), custom_call_target="tpu_custom_call" | custom-call | flops 805306368 | bytes 393216 | tf_op jit(solution)/shard_map/output_part/pallas_call | solution.py:22
  55.5 0.9 %collective-permute-done.14.came_ref = s16[32,1920]{1,0:T(8,128)(2,1)S(1)} collective-permute-done((s16[32,1920]{1,0:T(8,128)(2,1)S(1)}, s16[32,1920]{1,0:T(8,128)(2,1)S(1)}, u32[]{:S(2)}, u32[]{:S(2)}) %collective-permute-start.14) | collective-permute-done | bytes 122912 | tf_op jit(solution)/shard_map/ppermute | solution.py:48
  56.6 1.8 %collective-permute-start.15 = (s16[16,1920]{1,0:T(8,128)(2,1)S(1)}, s16[16,1920]{1,0:T(8,128)(2,1)S(1)}, u32[]{:S(2)}, u32[]{:S(2)}) collective-permute-start(s16[16,1920]{1,0:T(8,128)(2,1)S(1)} %get-tuple-element.45), channel_id=1, source_target_pairs={{0,2},{1,3},{2,0},{3,1},{4,6},{5,7},{6,4},{7,5},{8,10},{9,11},{10,... | collective-permute-start | bytes 184328 | tf_op jit(solution)/shard_map/ppermute | solution.py:48
  58.4 1.0 %output_part.5 = (f32[64,768]{1,0:T(8,128)S(1)}, s16[32,896]{1,0:T(8,128)(2,1)S(1)}) custom-call(bf16[16,3072]{1,0:T(8,128)(2,1)S(1)} %join.1.refs_0_, bf16[16,3072]{1,0:T(8,128)(2,1)S(1)} %collective-permute-done.11.refs_1_, bf16[16,3072]{1,0:T(8,128)(2,1)S(1)} %collective-permute-done.12.refs_2_, bf16[16,3072]{1,0:T(8,128)(2,1)S(1)} %collective-permute-done.13.refs_3_, ...), custom_call_target="tpu_custom_call" | custom-call | flops 301989888 | bytes 393216 | tf_op jit(solution)/shard_map/output_part/pallas_call | solution.py:22
  59.5 1.2 %collective-permute-start.18 = (s16[32,896]{1,0:T(8,128)(2,1)S(1)}, s16[32,896]{1,0:T(8,128)(2,1)S(1)}, u32[]{:S(2)}, u32[]{:S(2)}) collective-permute-start(s16[32,896]{1,0:T(8,128)(2,1)S(1)} %get-tuple-element.50), channel_id=1, source_target_pairs={{0,1},{1,0},{2,3},{3,2},{4,5},{5,4},{6,7},{7,6},{8,9},{9,8},{10,11... | collective-permute-start | bytes 172040 | tf_op jit(solution)/shard_map/ppermute | solution.py:48
  60.7 1.2 %collective-permute-done.16.came_ref = s16[32,2176]{1,0:T(8,128)(2,1)S(1)} collective-permute-done((s16[32,2176]{1,0:T(8,128)(2,1)S(1)}, s16[32,2176]{1,0:T(8,128)(2,1)S(1)}, u32[]{:S(2)}, u32[]{:S(2)}) %collective-permute-start.16) | collective-permute-done | bytes 139296 | tf_op jit(solution)/shard_map/ppermute | solution.py:48
  62.1 0.7 %collective-permute-start.17 = (s16[16,2176]{1,0:T(8,128)(2,1)S(1)}, s16[16,2176]{1,0:T(8,128)(2,1)S(1)}, u32[]{:S(2)}, u32[]{:S(2)}) collective-permute-start(s16[16,2176]{1,0:T(8,128)(2,1)S(1)} %get-tuple-element.49), channel_id=1, source_target_pairs={{0,2},{1,3},{2,0},{3,1},{4,6},{5,7},{6,4},{7,5},{8,10},{9,11},{10,... | collective-permute-start | bytes 208904 | tf_op jit(solution)/shard_map/ppermute | solution.py:48
  62.9 0.9 %collective-permute-done.18.came_ref = s16[32,896]{1,0:T(8,128)(2,1)S(1)} collective-permute-done((s16[32,896]{1,0:T(8,128)(2,1)S(1)}, s16[32,896]{1,0:T(8,128)(2,1)S(1)}, u32[]{:S(2)}, u32[]{:S(2)}) %collective-permute-start.18) | collective-permute-done | bytes 57376 | tf_op jit(solution)/shard_map/ppermute | solution.py:48
  64.0 1.7 %collective-permute-start.19 = (s16[16,896]{1,0:T(8,128)(2,1)S(1)}, s16[16,896]{1,0:T(8,128)(2,1)S(1)}, u32[]{:S(2)}, u32[]{:S(2)}) collective-permute-start(s16[16,896]{1,0:T(8,128)(2,1)S(1)} %get-tuple-element.52), channel_id=1, source_target_pairs={{0,2},{1,3},{2,0},{3,1},{4,6},{5,7},{6,4},{7,5},{8,10},{9,11},{10,... | collective-permute-start | bytes 86024 | tf_op jit(solution)/shard_map/ppermute | solution.py:48
  65.7 2.4 %collective-permute-done.17.refs_2_ = s16[16,2176]{1,0:T(8,128)(2,1)S(1)} collective-permute-done((s16[16,2176]{1,0:T(8,128)(2,1)S(1)}, s16[16,2176]{1,0:T(8,128)(2,1)S(1)}, u32[]{:S(2)}, u32[]{:S(2)}) %collective-permute-start.17) | collective-permute-done | bytes 69664 | tf_op jit(solution)/shard_map/ppermute | solution.py:48
  68.1 0.8 %collective-permute-done.19.refs_4_ = s16[16,896]{1,0:T(8,128)(2,1)S(1)} collective-permute-done((s16[16,896]{1,0:T(8,128)(2,1)S(1)}, s16[16,896]{1,0:T(8,128)(2,1)S(1)}, u32[]{:S(2)}, u32[]{:S(2)}) %collective-permute-start.19) | collective-permute-done | bytes 28704 | tf_op jit(solution)/shard_map/ppermute | solution.py:48
  68.8 0.8 %finish.3 = bf16[16,4608]{1,0:T(8,128)(2,1)} custom-call(bf16[16,1792]{1,0:T(8,128)(2,1)S(1)} %finish.2.refs_0_, f32[16,2048]{1,0:T(8,128)S(1)} %get-tuple-element.48.refs_1_, s16[16,2176]{1,0:T(8,128)(2,1)S(1)} %collective-permute-done.17.refs_2_, f32[16,768]{1,0:T(8,128)S(1)} %get-tuple-element.51.refs_3_, s16[16,896]{1,0:T(8,128)(2,1)S(1)} %collective-permute-done.19.refs_4_), custom_call_target="tpu_custom_call" | custom-call | bytes 589824 | tf_op jit(solution)/shard_map/finish/pallas_call | solution.py:22
  (49 shorter events, 3.9 us)
Async XLA Ops:
  1.3 6.1 %copy-start = (bf16[64,4608]{1,0:T(8,128)(2,1)S(1)}, bf16[64,4608]{1,0:T(8,128)(2,1)}, u32[]{:S(2)}) copy-start(bf16[64,4608]{1,0:T(8,128)(2,1)} %refs_4_.5) | copy-start | bytes 1769476
  1.3 6.1 %copy-start.1 = (bf16[1152,512]{1,0:T(8,128)(2,1)S(1)}, bf16[1152,512]{1,0:T(8,128)(2,1)}, u32[]{:S(2)}) copy-start(bf16[1152,512]{1,0:T(8,128)(2,1)} %refs_7_.1) | copy-start | bytes 3538948
  1.4 6.1 %copy-start.2 = (f32[4608]{0:T(1024)S(1)}, f32[4608]{0:T(1024)}, u32[]{:S(2)}) copy-start(f32[4608]{0:T(1024)} %refs_5_.1) | copy-start | bytes 55300
  1.4 5.5 %collective-permute-start.2 = (f32[2,64]{1,0:T(2,128)S(1)}, f32[2,64]{1,0:T(2,128)S(1)}, u32[]{:S(2)}, u32[]{:S(2)}) collective-permute-start(f32[2,64]{1,0:T(2,128)S(1)} %pad_maximum_fusion.refs_0_), channel_id=1, source_target_pairs={{0,12},{4,8},{8,4},{12,0},{1,13},{5,9},{9,5},{13,1},{2,14},{6,10},... | collective-permute-start | bytes 1544 | tf_op jit(solution)/shard_map/ppermute | solution.py:48
  3.8 3.6 %collective-permute-start.1 = (f32[2,64]{1,0:T(2,128)S(1)}, f32[2,64]{1,0:T(2,128)S(1)}, u32[]{:S(2)}, u32[]{:S(2)}) collective-permute-start(f32[2,64]{1,0:T(2,128)S(1)} %pad_maximum_fusion.refs_0_), channel_id=1, source_target_pairs={{0,8},{4,12},{8,0},{12,4},{1,9},{5,13},{9,1},{13,5},{2,10},{6,14},... | collective-permute-start | bytes 1544 | tf_op jit(solution)/shard_map/ppermute | solution.py:48
  4.5 2.9 %collective-permute-start = (f32[2,64]{1,0:T(2,128)S(1)}, f32[2,64]{1,0:T(2,128)S(1)}, u32[]{:S(2)}, u32[]{:S(2)}) collective-permute-start(f32[2,64]{1,0:T(2,128)S(1)} %pad_maximum_fusion.refs_0_), channel_id=1, source_target_pairs={{0,4},{4,0},{8,12},{12,8},{1,5},{5,1},{9,13},{13,9},{2,6},{6,2},{1... | collective-permute-start | bytes 1544 | tf_op jit(solution)/shard_map/ppermute | solution.py:48
  16.1 1.9 %collective-permute-start.3 = (f32[32,3584]{1,0:T(8,128)S(1)}, f32[32,3584]{1,0:T(8,128)S(1)}, u32[]{:S(2)}, u32[]{:S(2)}) collective-permute-start(f32[32,3584]{1,0:T(8,128)S(1)} %get-tuple-element.30), channel_id=1, source_target_pairs={{0,4},{4,0},{8,12},{12,8},{1,5},{5,1},{9,13},{13,9},{2,6},{6,2},{1... | collective-permute-start | bytes 1376264 | tf_op jit(solution)/shard_map/ppermute | solution.py:48
  18.0 7.7 %collective-permute-start.4 = (f32[16,3584]{1,0:T(8,128)S(1)}, f32[16,3584]{1,0:T(8,128)S(1)}, u32[]{:S(2)}, u32[]{:S(2)}) collective-permute-start(f32[16,3584]{1,0:T(8,128)S(1)} %get-tuple-element.32), channel_id=1, source_target_pairs={{0,8},{4,12},{8,0},{12,4},{1,9},{5,13},{9,1},{13,5},{2,10},{6,14},... | collective-permute-start | bytes 688136 | tf_op jit(solution)/shard_map/ppermute | solution.py:48
  25.7 8.6 %copy-start.3 = (bf16[4,1024,512]{2,1,0:T(8,128)(2,1)S(1)}, bf16[4,1024,512]{2,1,0:T(8,128)(2,1)}, u32[]{:S(2)}) copy-start(bf16[4,1024,512]{2,1,0:T(8,128)(2,1)} %refs_4_.6) | copy-start | bytes 12582916
  25.7 8.6 %copy-start.4 = (s32[4]{0:T(128)S(1)}, s32[4]{0:T(128)}, u32[]{:S(2)}) copy-start(s32[4]{0:T(128)} %param.13) | copy-start | bytes 52
  25.7 23.0 %slice-start = ((s8[28311552]{0:T(1024)(128)(4,1)}), s8[4194304]{0:T(1024)(128)(4,1)S(1)}, s32[]{:S(2)}) async-start(s8[28311552]{0:T(1024)(128)(4,1)} %bitcast.3), calls=%async_computation | async-start | bytes 8388608
  25.7 23.0 %slice-start.1 = ((s8[28311552]{0:T(1024)(128)(4,1)}), s8[4194304]{0:T(1024)(128)(4,1)S(1)}, s32[]{:S(2)}) async-start(s8[28311552]{0:T(1024)(128)(4,1)} %bitcast.3), calls=%async_computation.1 | async-start | bytes 8388608
  25.7 23.0 %slice-start.2 = ((s8[28311552]{0:T(1024)(128)(4,1)}), s8[4194304]{0:T(1024)(128)(4,1)S(1)}, s32[]{:S(2)}) async-start(s8[28311552]{0:T(1024)(128)(4,1)} %bitcast.3), calls=%async_computation.2 | async-start | bytes 8388608
  25.8 6.0 %collective-permute-start.5 = (bf16[8,2048]{1,0:T(8,128)(2,1)S(1)}, bf16[8,2048]{1,0:T(8,128)(2,1)S(1)}, u32[]{:S(2)}, u32[]{:S(2)}) collective-permute-start(bf16[8,2048]{1,0:T(8,128)(2,1)S(1)} %get-tuple-element.33), channel_id=1, source_target_pairs={{0,3},{1,2},{2,1},{3,0},{4,7},{5,6},{6,5},{7,4},{8,11},{9,10},{10,... | collective-permute-start | bytes 98312 | tf_op jit(solution)/shard_map/ppermute | solution.py:48
  29.5 4.8 %collective-permute-start.6 = (bf16[8,2048]{1,0:T(8,128)(2,1)S(1)}, bf16[8,2048]{1,0:T(8,128)(2,1)S(1)}, u32[]{:S(2)}, u32[]{:S(2)}) collective-permute-start(bf16[8,2048]{1,0:T(8,128)(2,1)S(1)} %get-tuple-element.34), channel_id=1, source_target_pairs={{0,2},{1,3},{2,0},{3,1},{4,6},{5,7},{6,4},{7,5},{8,10},{9,11},{10,... | collective-permute-start | bytes 98312 | tf_op jit(solution)/shard_map/ppermute | solution.py:48
  29.5 4.8 %collective-permute-start.7 = (bf16[8,2048]{1,0:T(8,128)(2,1)S(1)}, bf16[8,2048]{1,0:T(8,128)(2,1)S(1)}, u32[]{:S(2)}, u32[]{:S(2)}) collective-permute-start(bf16[8,2048]{1,0:T(8,128)(2,1)S(1)} %get-tuple-element.35), channel_id=1, source_target_pairs={{0,1},{1,0},{2,3},{3,2},{4,5},{5,4},{6,7},{7,6},{8,9},{9,8},{10,11... | collective-permute-start | bytes 98312 | tf_op jit(solution)/shard_map/ppermute | solution.py:48
  34.3 14.5 %slice-start.3 = ((s8[28311552]{0:T(1024)(128)(4,1)}), s8[4194304]{0:T(1024)(128)(4,1)S(1)}, s32[]{:S(2)}) async-start(s8[28311552]{0:T(1024)(128)(4,1)} %bitcast.3), calls=%async_computation.3 | async-start | bytes 8388608
  34.3 14.5 %slice-start.4 = ((s8[28311552]{0:T(1024)(128)(4,1)}), s8[4194304]{0:T(1024)(128)(4,1)S(1)}, s32[]{:S(2)}) async-start(s8[28311552]{0:T(1024)(128)(4,1)} %bitcast.3), calls=%async_computation.4 | async-start | bytes 8388608
  36.2 5.7 %collective-permute-start.8 = (bf16[8,1536]{1,0:T(8,128)(2,1)S(1)}, bf16[8,1536]{1,0:T(8,128)(2,1)S(1)}, u32[]{:S(2)}, u32[]{:S(2)}) collective-permute-start(bf16[8,1536]{1,0:T(8,128)(2,1)S(1)} %get-tuple-element.37), channel_id=1, source_target_pairs={{0,3},{1,2},{2,1},{3,0},{4,7},{5,6},{6,5},{7,4},{8,11},{9,10},{10,... | collective-permute-start | bytes 73736 | tf_op jit(solution)/shard_map/ppermute | solution.py:48
  37.7 4.7 %collective-permute-start.9 = (bf16[8,1536]{1,0:T(8,128)(2,1)S(1)}, bf16[8,1536]{1,0:T(8,128)(2,1)S(1)}, u32[]{:S(2)}, u32[]{:S(2)}) collective-permute-start(bf16[8,1536]{1,0:T(8,128)(2,1)S(1)} %get-tuple-element.38), channel_id=1, source_target_pairs={{0,2},{1,3},{2,0},{3,1},{4,6},{5,7},{6,4},{7,5},{8,10},{9,11},{10,... | collective-permute-start | bytes 73736 | tf_op jit(solution)/shard_map/ppermute | solution.py:48
  38.4 4.3 %collective-permute-start.10 = (bf16[8,1536]{1,0:T(8,128)(2,1)S(1)}, bf16[8,1536]{1,0:T(8,128)(2,1)S(1)}, u32[]{:S(2)}, u32[]{:S(2)}) collective-permute-start(bf16[8,1536]{1,0:T(8,128)(2,1)S(1)} %get-tuple-element.39), channel_id=1, source_target_pairs={{0,1},{1,0},{2,3},{3,2},{4,5},{5,4},{6,7},{7,6},{8,9},{9,8},{10,11... | collective-permute-start | bytes 73736 | tf_op jit(solution)/shard_map/ppermute | solution.py:48
  42.7 6.1 %slice-start.5 = ((s8[28311552]{0:T(1024)(128)(4,1)}), s8[4194304]{0:T(1024)(128)(4,1)S(1)}, s32[]{:S(2)}) async-start(s8[28311552]{0:T(1024)(128)(4,1)} %bitcast.3), calls=%async_computation.5 | async-start | bytes 8388608
  42.7 6.1 %slice-start.6 = ((s8[28311552]{0:T(1024)(128)(4,1)}), s8[3145728]{0:T(1024)(128)(4,1)S(1)}, s32[]{:S(2)}) async-start(s8[28311552]{0:T(1024)(128)(4,1)} %bitcast.3), calls=%async_computation.6 | async-start | bytes 6291456
  42.8 4.7 %collective-permute-start.12 = (bf16[16,3072]{1,0:T(8,128)(2,1)S(1)}, bf16[16,3072]{1,0:T(8,128)(2,1)S(1)}, u32[]{:S(2)}, u32[]{:S(2)}) collective-permute-start(bf16[16,3072]{1,0:T(8,128)(2,1)S(1)} %join.1.refs_0_), channel_id=1, source_target_pairs={{0,8},{4,12},{8,0},{12,4},{1,9},{5,13},{9,1},{13,5},{2,10},{6,14},... | collective-permute-start | bytes 294920 | tf_op jit(solution)/shard_map/ppermute | solution.py:48
  44.1 3.4 %collective-permute-start.11 = (bf16[16,3072]{1,0:T(8,128)(2,1)S(1)}, bf16[16,3072]{1,0:T(8,128)(2,1)S(1)}, u32[]{:S(2)}, u32[]{:S(2)}) collective-permute-start(bf16[16,3072]{1,0:T(8,128)(2,1)S(1)} %join.1.refs_0_), channel_id=1, source_target_pairs={{0,4},{4,0},{8,12},{12,8},{1,5},{5,1},{9,13},{13,9},{2,6},{6,2},{1... | collective-permute-start | bytes 294920 | tf_op jit(solution)/shard_map/ppermute | solution.py:48
  47.4 1.3 %collective-permute-start.13 = (bf16[16,3072]{1,0:T(8,128)(2,1)S(1)}, bf16[16,3072]{1,0:T(8,128)(2,1)S(1)}, u32[]{:S(2)}, u32[]{:S(2)}) collective-permute-start(bf16[16,3072]{1,0:T(8,128)(2,1)S(1)} %collective-permute-done.12.refs_2_), channel_id=1, source_target_pairs={{0,4},{4,0},{8,12},{12,8},{1,5},{5,1},{9,13},{13,9},{2,6},{6,2},{1... | collective-permute-start | bytes 294920 | tf_op jit(solution)/shard_map/ppermute | solution.py:48
  51.0 5.5 %collective-permute-start.14 = (s16[32,1920]{1,0:T(8,128)(2,1)S(1)}, s16[32,1920]{1,0:T(8,128)(2,1)S(1)}, u32[]{:S(2)}, u32[]{:S(2)}) collective-permute-start(s16[32,1920]{1,0:T(8,128)(2,1)S(1)} %get-tuple-element.42), channel_id=1, source_target_pairs={{0,1},{1,0},{2,3},{3,2},{4,5},{5,4},{6,7},{7,6},{8,9},{9,8},{10,11... | collective-permute-start | bytes 368648 | tf_op jit(solution)/shard_map/ppermute | solution.py:48
  55.2 6.7 %collective-permute-start.16 = (s16[32,2176]{1,0:T(8,128)(2,1)S(1)}, s16[32,2176]{1,0:T(8,128)(2,1)S(1)}, u32[]{:S(2)}, u32[]{:S(2)}) collective-permute-start(s16[32,2176]{1,0:T(8,128)(2,1)S(1)} %get-tuple-element.46), channel_id=1, source_target_pairs={{0,1},{1,0},{2,3},{3,2},{4,5},{5,4},{6,7},{7,6},{8,9},{9,8},{10,11... | collective-permute-start | bytes 417800 | tf_op jit(solution)/shard_map/ppermute | solution.py:48
  56.6 6.2 %collective-permute-start.15 = (s16[16,1920]{1,0:T(8,128)(2,1)S(1)}, s16[16,1920]{1,0:T(8,128)(2,1)S(1)}, u32[]{:S(2)}, u32[]{:S(2)}) collective-permute-start(s16[16,1920]{1,0:T(8,128)(2,1)S(1)} %get-tuple-element.45), channel_id=1, source_target_pairs={{0,2},{1,3},{2,0},{3,1},{4,6},{5,7},{6,4},{7,5},{8,10},{9,11},{10,... | collective-permute-start | bytes 184328 | tf_op jit(solution)/shard_map/ppermute | solution.py:48
  59.5 4.4 %collective-permute-start.18 = (s16[32,896]{1,0:T(8,128)(2,1)S(1)}, s16[32,896]{1,0:T(8,128)(2,1)S(1)}, u32[]{:S(2)}, u32[]{:S(2)}) collective-permute-start(s16[32,896]{1,0:T(8,128)(2,1)S(1)} %get-tuple-element.50), channel_id=1, source_target_pairs={{0,1},{1,0},{2,3},{3,2},{4,5},{5,4},{6,7},{7,6},{8,9},{9,8},{10,11... | collective-permute-start | bytes 172040 | tf_op jit(solution)/shard_map/ppermute | solution.py:48
  62.1 6.0 %collective-permute-start.17 = (s16[16,2176]{1,0:T(8,128)(2,1)S(1)}, s16[16,2176]{1,0:T(8,128)(2,1)S(1)}, u32[]{:S(2)}, u32[]{:S(2)}) collective-permute-start(s16[16,2176]{1,0:T(8,128)(2,1)S(1)} %get-tuple-element.49), channel_id=1, source_target_pairs={{0,2},{1,3},{2,0},{3,1},{4,6},{5,7},{6,4},{7,5},{8,10},{9,11},{10,... | collective-permute-start | bytes 208904 | tf_op jit(solution)/shard_map/ppermute | solution.py:48
  64.0 4.8 %collective-permute-start.19 = (s16[16,896]{1,0:T(8,128)(2,1)S(1)}, s16[16,896]{1,0:T(8,128)(2,1)S(1)}, u32[]{:S(2)}, u32[]{:S(2)}) collective-permute-start(s16[16,896]{1,0:T(8,128)(2,1)S(1)} %get-tuple-element.52), channel_id=1, source_target_pairs={{0,2},{1,3},{2,0},{3,1},{4,6},{5,7},{6,4},{7,5},{8,10},{9,11},{10,... | collective-permute-start | bytes 86024 | tf_op jit(solution)/shard_map/ppermute | solution.py:48

commit v15 on v11

--- a/solution.py
+++ b/solution.py
@@ -79,9 +79,26 @@
     return [sum(((k >> b) & 1) << (bits - 1 - b) for b in range(bits)) for k in range(count)]
 
 
+class Halves:
+    def __init__(self, source, start, target, sems, g):
+        half = target.shape[0] // 2
+        self.copies = [
+            pltpu.make_async_copy(source.at[start + k * half : start + (k + 1) * half], target.at[pl.ds(k * half, half)], sems.at[g, k])
+            for k in range(2)
+        ]
+
+    def start(self):
+        for k, copy in enumerate(self.copies):
+            copy.start(priority=k)
+
+    def wait(self):
+        for copy in self.copies:
+            copy.wait()
+
+
 def fetch_kernel(w_ref, *refs):
-    share_ref, sem = refs[-2:]
-    fetch = pltpu.make_async_copy(w_ref.at[: share_ref.shape[0]], share_ref, sem)
+    share_ref, sems = refs[-2:]
+    fetch = Halves(w_ref, 0, share_ref, sems, 0)
     fetch.start()
     fetch.wait()
 
@@ -93,7 +110,7 @@
         (in_hbm(w), *after),
         [ANY] * (1 + len(after)),
         "fetch_query_weight",
-        scratch=[pltpu.SemaphoreType.DMA],
+        scratch=[pltpu.SemaphoreType.DMA((1, 2))],
         moved=2 * rows * w.shape[1],
     )
 
@@ -118,10 +135,7 @@
     sub_width = width // narrow_count
     sizes = [ref.shape[0] for ref in (first_ref, *blocks)]
     starts = [sum(sizes[:g]) for g in range(len(sizes))]
-    fetches = [
-        pltpu.make_async_copy(w_ref.at[start : start + size], ref, sems.at[g])
-        for g, (start, size, ref) in enumerate(zip(starts[1:], sizes[1:], blocks))
-    ]
+    fetches = [Halves(w_ref, start, ref, sems, g) for g, (start, ref) in enumerate(zip(starts[1:], blocks))]
     ahead = 3
     for fetch in fetches[:ahead]:
         fetch.start()
@@ -188,7 +202,7 @@
             pltpu.VMEM((rows, width), jnp.bfloat16),
             pltpu.VMEM((rows, width // narrow_count), jnp.bfloat16),
             *[pltpu.VMEM((n, queries), jnp.bfloat16) for n in blocks],
-            pltpu.SemaphoreType.DMA((len(blocks),)),
+            pltpu.SemaphoreType.DMA((len(blocks), 2)),
         ],
         limit=36,
         flops=2 * rows * width * queries,

time: 69.7 us -> 70.3 us (level)
  no operation moved by 1% of the time
where the time goes in v15:
time: 70.3 us; the launch traced here: 70.1 us
  waiting for transfers between devices  23.7 us (34%)
  starting transfers between devices  22.8 us (32%)
  Pallas kernels  21.9 us (31%)
  other arithmetic  1.32 us (2%)
    ppermute x20, waiting for transfers between devices, swap(): return lax.ppermute(x, axis, [(i, i ^ distance) for i in range(count)])  23.7 us
    ppermute x20, starting transfers between devices, swap(): return lax.ppermute(x, axis, [(i, i ^ distance) for i in range(count)])  22.8 us
    pallas_call x12, Pallas kernels, call(): pl.pallas_call(kernel, out_shape=outs, in_specs=specs, out_specs=jax.tree...  19.7 us
    pallas_call x3, Pallas kernels, finish(): pl.pallas_call(functools.partial(finish_kernel, start), out_shape=pltpu.H...  2.15 us
  transfers between devices with their start and end apart: 20, of which 14 were waited for; matrix products, arithmetic and copies ran while one was open for 0% of the time, Pallas kernels for 11%

profile of v15, /device:TPU:0, one launch (start us, length us, event | category | flops | bytes accessed | tf_op | source)
XLA Modules:
  0.0 70.1 jit_solution(8402294769226753558)
XLA Ops:
  0.0 1.3 %convert_reduce_fusion = (f32[64]{0:T(128)S(1)}, f32[64]{0:T(128)S(1)}) fusion(bf16[64,4608]{1,0:T(8,128)(2,1)} %refs_4_.5), kind=kLoop, calls=%fused_computation.1 | loop fusion | flops 1179520 | bytes 590336 | tf_op jit(solution)/shard_map/reduce_sum | solution.py:446
  1.4 2.5 %collective-permute-start.2 = (f32[2,64]{1,0:T(2,128)S(1)}, f32[2,64]{1,0:T(2,128)S(1)}, u32[]{:S(2)}, u32[]{:S(2)}) collective-permute-start(f32[2,64]{1,0:T(2,128)S(1)} %pad_maximum_fusion.refs_0_), channel_id=1, source_target_pairs={{0,12},{4,8},{8,4},{12,0},{1,13},{5,9},{9,5},{13,1},{2,14},{6,10},... | collective-permute-start | bytes 1544 | tf_op jit(solution)/shard_map/ppermute | solution.py:48
  4.5 2.4 %fetch_query_weight.1.refs_8_ = bf16[768,3072]{1,0:T(8,128)(2,1)S(1)} custom-call(bf16[4608,3072]{1,0:T(8,128)(2,1)} %refs_6_.1, f32[2,64]{1,0:T(2,128)S(1)} %pad_maximum_fusion.refs_0_), custom_call_target="tpu_custom_call" | custom-call | bytes 4718592 | tf_op jit(solution)/shard_map/fetch_query_weight/pallas_call | solution.py:22
  7.4 9.2 %project.1 = (f32[32,3584]{1,0:T(8,128)S(1)}, f32[32,3584]{1,0:T(8,128)S(1)}) custom-call(f32[2,64]{1,0:T(2,128)S(1)} %pad_maximum_fusion.refs_0_, f32[2,64]{1,0:T(2,128)S(1)} %collective-permute-done.refs_1_, f32[2,64]{1,0:T(2,128)S(1)} %collective-permute-done.1.refs_2_, f32[2,64]{1,0:T(2,128)S(1)} %collective-permute-done.2.refs_3_, ...), custom_call_target="tpu_custom_call" | custom-call | flops 1811939328 | bytes 23592960 | tf_op jit(solution)/shard_map/project/pallas_call | solution.py:22
  16.7 1.8 %collective-permute-done.3.came_ref = f32[32,3584]{1,0:T(8,128)S(1)} collective-permute-done((f32[32,3584]{1,0:T(8,128)S(1)}, f32[32,3584]{1,0:T(8,128)S(1)}, u32[]{:S(2)}, u32[]{:S(2)}) %collective-permute-start.3) | collective-permute-done | bytes 458784 | tf_op jit(solution)/shard_map/ppermute | solution.py:48
  18.6 1.4 %collective-permute-start.4 = (f32[16,3584]{1,0:T(8,128)S(1)}, f32[16,3584]{1,0:T(8,128)S(1)}, u32[]{:S(2)}, u32[]{:S(2)}) collective-permute-start(f32[16,3584]{1,0:T(8,128)S(1)} %get-tuple-element.32), channel_id=1, source_target_pairs={{0,8},{4,12},{8,0},{12,4},{1,9},{5,13},{9,1},{13,5},{2,10},{6,14},... | collective-permute-start | bytes 688136 | tf_op jit(solution)/shard_map/ppermute | solution.py:48
  19.9 6.4 %collective-permute-done.4.came_ref = f32[16,3584]{1,0:T(8,128)S(1)} collective-permute-done((f32[16,3584]{1,0:T(8,128)S(1)}, f32[16,3584]{1,0:T(8,128)S(1)}, u32[]{:S(2)}, u32[]{:S(2)}) %collective-permute-start.4) | collective-permute-done | bytes 229408 | tf_op jit(solution)/shard_map/ppermute | solution.py:48
  26.4 3.7 %collective-permute-start.5 = (bf16[8,2048]{1,0:T(8,128)(2,1)S(1)}, bf16[8,2048]{1,0:T(8,128)(2,1)S(1)}, u32[]{:S(2)}, u32[]{:S(2)}) collective-permute-start(bf16[8,2048]{1,0:T(8,128)(2,1)S(1)} %get-tuple-element.33), channel_id=1, source_target_pairs={{0,3},{1,2},{2,1},{3,0},{4,7},{5,6},{6,5},{7,4},{8,11},{9,10},{10,... | collective-permute-start | bytes 98312 | tf_op jit(solution)/shard_map/ppermute | solution.py:48
  30.1 0.8 %collective-permute-start.7 = (bf16[8,2048]{1,0:T(8,128)(2,1)S(1)}, bf16[8,2048]{1,0:T(8,128)(2,1)S(1)}, u32[]{:S(2)}, u32[]{:S(2)}) collective-permute-start(bf16[8,2048]{1,0:T(8,128)(2,1)S(1)} %get-tuple-element.35), channel_id=1, source_target_pairs={{0,1},{1,0},{2,3},{3,2},{4,5},{5,4},{6,7},{7,6},{8,9},{9,8},{10,11... | collective-permute-start | bytes 98312 | tf_op jit(solution)/shard_map/ppermute | solution.py:48
  30.8 1.5 %collective-permute-done.5.refs_0_ = bf16[8,2048]{1,0:T(8,128)(2,1)S(1)} collective-permute-done((bf16[8,2048]{1,0:T(8,128)(2,1)S(1)}, bf16[8,2048]{1,0:T(8,128)(2,1)S(1)}, u32[]{:S(2)}, u32[]{:S(2)}) %collective-permute-start.5) | collective-permute-done | bytes 32800 | tf_op jit(solution)/shard_map/ppermute | solution.py:48
  32.4 2.5 %collective-permute-done.6.refs_1_ = bf16[8,2048]{1,0:T(8,128)(2,1)S(1)} collective-permute-done((bf16[8,2048]{1,0:T(8,128)(2,1)S(1)}, bf16[8,2048]{1,0:T(8,128)(2,1)S(1)}, u32[]{:S(2)}, u32[]{:S(2)}) %collective-permute-start.6) | collective-permute-done | bytes 32800 | tf_op jit(solution)/shard_map/ppermute | solution.py:48
  34.9 1.9 %attend.1 = (bf16[8,1536]{1,0:T(8,128)(2,1)S(1)}, bf16[8,1536]{1,0:T(8,128)(2,1)S(1)}, bf16[8,1536]{1,0:T(8,128)(2,1)S(1)}, bf16[8,1536]{1,0:T(8,128)(2,1)S(1)}) custom-call(s32[1,4]{1,0:T(1,128)S(1)} %bitcast.5, bf16[8,2048]{1,0:T(8,128)(2,1)S(1)} %collective-permute-done.5.refs_0_, bf16[8,2048]{1,0:T(8,128)(2,1)S(1)} %collective-permute-done.6.refs_1_, ...), custom_call_target="tpu_custom_call" | custom-call | flops 5000000000 | tf_op jit(solution)/shard_map/attend/pallas_call | solution.py:22
  36.8 1.5 %collective-permute-start.8 = (bf16[8,1536]{1,0:T(8,128)(2,1)S(1)}, bf16[8,1536]{1,0:T(8,128)(2,1)S(1)}, u32[]{:S(2)}, u32[]{:S(2)}) collective-permute-start(bf16[8,1536]{1,0:T(8,128)(2,1)S(1)} %get-tuple-element.37), channel_id=1, source_target_pairs={{0,3},{1,2},{2,1},{3,0},{4,7},{5,6},{6,5},{7,4},{8,11},{9,10},{10,... | collective-permute-start | bytes 73736 | tf_op jit(solution)/shard_map/ppermute | solution.py:48
  38.9 2.3 %collective-permute-start.10 = (bf16[8,1536]{1,0:T(8,128)(2,1)S(1)}, bf16[8,1536]{1,0:T(8,128)(2,1)S(1)}, u32[]{:S(2)}, u32[]{:S(2)}) collective-permute-start(bf16[8,1536]{1,0:T(8,128)(2,1)S(1)} %get-tuple-element.39), channel_id=1, source_target_pairs={{0,1},{1,0},{2,3},{3,2},{4,5},{5,4},{6,7},{7,6},{8,9},{9,8},{10,11... | collective-permute-start | bytes 73736 | tf_op jit(solution)/shard_map/ppermute | solution.py:48
  41.2 1.2 %collective-permute-done.8.refs_0_ = bf16[8,1536]{1,0:T(8,128)(2,1)S(1)} collective-permute-done((bf16[8,1536]{1,0:T(8,128)(2,1)S(1)}, bf16[8,1536]{1,0:T(8,128)(2,1)S(1)}, u32[]{:S(2)}, u32[]{:S(2)}) %collective-permute-start.8) | collective-permute-done | bytes 24608 | tf_op jit(solution)/shard_map/ppermute | solution.py:48
  43.3 1.4 %collective-permute-start.12 = (bf16[16,3072]{1,0:T(8,128)(2,1)S(1)}, bf16[16,3072]{1,0:T(8,128)(2,1)S(1)}, u32[]{:S(2)}, u32[]{:S(2)}) collective-permute-start(bf16[16,3072]{1,0:T(8,128)(2,1)S(1)} %join.1.refs_0_), channel_id=1, source_target_pairs={{0,8},{4,12},{8,0},{12,4},{1,9},{5,13},{9,1},{13,5},{2,10},{6,14},... | collective-permute-start | bytes 294920 | tf_op jit(solution)/shard_map/ppermute | solution.py:48
  44.7 3.3 %collective-permute-done.12.refs_2_ = bf16[16,3072]{1,0:T(8,128)(2,1)S(1)} collective-permute-done((bf16[16,3072]{1,0:T(8,128)(2,1)S(1)}, bf16[16,3072]{1,0:T(8,128)(2,1)S(1)}, u32[]{:S(2)}, u32[]{:S(2)}) %collective-permute-start.12) | collective-permute-done | bytes 98336 | tf_op jit(solution)/shard_map/ppermute | solution.py:48
  48.0 1.3 %collective-permute-done.13.refs_3_ = bf16[16,3072]{1,0:T(8,128)(2,1)S(1)} collective-permute-done((bf16[16,3072]{1,0:T(8,128)(2,1)S(1)}, bf16[16,3072]{1,0:T(8,128)(2,1)S(1)}, u32[]{:S(2)}, u32[]{:S(2)}) %collective-permute-start.13) | collective-permute-done | bytes 98336 | tf_op jit(solution)/shard_map/ppermute | solution.py:48
  49.4 2.1 %output_part.3 = (f32[64,1792]{1,0:T(8,128)S(1)}, s16[32,1920]{1,0:T(8,128)(2,1)S(1)}) custom-call(bf16[16,3072]{1,0:T(8,128)(2,1)S(1)} %join.1.refs_0_, bf16[16,3072]{1,0:T(8,128)(2,1)S(1)} %collective-permute-done.11.refs_1_, bf16[16,3072]{1,0:T(8,128)(2,1)S(1)} %collective-permute-done.12.refs_2_, bf16[16,3072]{1,0:T(8,128)(2,1)S(1)} %collective-permute-done.13.refs_3_, ...), custom_call_target="tpu_custom_call" | custom-call | flops 704643072 | bytes 393216 | tf_op jit(solution)/shard_map/output_part/pallas_call | solution.py:22
  51.5 1.8 %collective-permute-start.14 = (s16[32,1920]{1,0:T(8,128)(2,1)S(1)}, s16[32,1920]{1,0:T(8,128)(2,1)S(1)}, u32[]{:S(2)}, u32[]{:S(2)}) collective-permute-start(s16[32,1920]{1,0:T(8,128)(2,1)S(1)} %get-tuple-element.42), channel_id=1, source_target_pairs={{0,1},{1,0},{2,3},{3,2},{4,5},{5,4},{6,7},{7,6},{8,9},{9,8},{10,11... | collective-permute-start | bytes 368648 | tf_op jit(solution)/shard_map/ppermute | solution.py:48
  53.4 2.4 %output_part.4 = (f32[64,2048]{1,0:T(8,128)S(1)}, s16[32,2176]{1,0:T(8,128)(2,1)S(1)}) custom-call(bf16[16,3072]{1,0:T(8,128)(2,1)S(1)} %join.1.refs_0_, bf16[16,3072]{1,0:T(8,128)(2,1)S(1)} %collective-permute-done.11.refs_1_, bf16[16,3072]{1,0:T(8,128)(2,1)S(1)} %collective-permute-done.12.refs_2_, bf16[16,3072]{1,0:T(8,128)(2,1)S(1)} %collective-permute-done.13.refs_3_, ...), custom_call_target="tpu_custom_call" | custom-call | flops 805306368 | bytes 393216 | tf_op jit(solution)/shard_map/output_part/pallas_call | solution.py:22
  56.1 0.9 %collective-permute-done.14.came_ref = s16[32,1920]{1,0:T(8,128)(2,1)S(1)} collective-permute-done((s16[32,1920]{1,0:T(8,128)(2,1)S(1)}, s16[32,1920]{1,0:T(8,128)(2,1)S(1)}, u32[]{:S(2)}, u32[]{:S(2)}) %collective-permute-start.14) | collective-permute-done | bytes 122912 | tf_op jit(solution)/shard_map/ppermute | solution.py:48
  57.2 1.8 %collective-permute-start.16 = (s16[16,1920]{1,0:T(8,128)(2,1)S(1)}, s16[16,1920]{1,0:T(8,128)(2,1)S(1)}, u32[]{:S(2)}, u32[]{:S(2)}) collective-permute-start(s16[16,1920]{1,0:T(8,128)(2,1)S(1)} %get-tuple-element.47), channel_id=1, source_target_pairs={{0,2},{1,3},{2,0},{3,1},{4,6},{5,7},{6,4},{7,5},{8,10},{9,11},{10,... | collective-permute-start | bytes 184328 | tf_op jit(solution)/shard_map/ppermute | solution.py:48
  59.0 1.0 %output_part.5 = (f32[64,768]{1,0:T(8,128)S(1)}, s16[32,896]{1,0:T(8,128)(2,1)S(1)}) custom-call(bf16[16,3072]{1,0:T(8,128)(2,1)S(1)} %join.1.refs_0_, bf16[16,3072]{1,0:T(8,128)(2,1)S(1)} %collective-permute-done.11.refs_1_, bf16[16,3072]{1,0:T(8,128)(2,1)S(1)} %collective-permute-done.12.refs_2_, bf16[16,3072]{1,0:T(8,128)(2,1)S(1)} %collective-permute-done.13.refs_3_, ...), custom_call_target="tpu_custom_call" | custom-call | flops 301989888 | bytes 393216 | tf_op jit(solution)/shard_map/output_part/pallas_call | solution.py:22
  60.0 1.2 %collective-permute-start.15 = (s16[32,896]{1,0:T(8,128)(2,1)S(1)}, s16[32,896]{1,0:T(8,128)(2,1)S(1)}, u32[]{:S(2)}, u32[]{:S(2)}) collective-permute-start(s16[32,896]{1,0:T(8,128)(2,1)S(1)} %get-tuple-element.46), channel_id=1, source_target_pairs={{0,1},{1,0},{2,3},{3,2},{4,5},{5,4},{6,7},{7,6},{8,9},{9,8},{10,11... | collective-permute-start | bytes 172040 | tf_op jit(solution)/shard_map/ppermute | solution.py:48
  61.3 1.2 %collective-permute-done.18.came_ref = s16[32,2176]{1,0:T(8,128)(2,1)S(1)} collective-permute-done((s16[32,2176]{1,0:T(8,128)(2,1)S(1)}, s16[32,2176]{1,0:T(8,128)(2,1)S(1)}, u32[]{:S(2)}, u32[]{:S(2)}) %collective-permute-start.18) | collective-permute-done | bytes 139296 | tf_op jit(solution)/shard_map/ppermute | solution.py:48
  62.6 0.7 %collective-permute-start.19 = (s16[16,2176]{1,0:T(8,128)(2,1)S(1)}, s16[16,2176]{1,0:T(8,128)(2,1)S(1)}, u32[]{:S(2)}, u32[]{:S(2)}) collective-permute-start(s16[16,2176]{1,0:T(8,128)(2,1)S(1)} %get-tuple-element.52), channel_id=1, source_target_pairs={{0,2},{1,3},{2,0},{3,1},{4,6},{5,7},{6,4},{7,5},{8,10},{9,11},{10,... | collective-permute-start | bytes 208904 | tf_op jit(solution)/shard_map/ppermute | solution.py:48
  63.4 0.7 %finish.3.refs_0_ = bf16[16,4608]{1,0:T(8,128)(2,1)} custom-call(f32[16,1792]{1,0:T(8,128)S(1)} %get-tuple-element.44.refs_5_.kept_ref, s16[16,1920]{1,0:T(8,128)(2,1)S(1)} %collective-permute-done.16.came_ref), custom_call_target="tpu_custom_call" | custom-call | bytes 229376 | tf_op jit(solution)/shard_map/finish/pallas_call | solution.py:424
  64.6 2.1 %collective-permute-start.17 = (s16[16,896]{1,0:T(8,128)(2,1)S(1)}, s16[16,896]{1,0:T(8,128)(2,1)S(1)}, u32[]{:S(2)}, u32[]{:S(2)}) collective-permute-start(s16[16,896]{1,0:T(8,128)(2,1)S(1)} %get-tuple-element.49), channel_id=1, source_target_pairs={{0,2},{1,3},{2,0},{3,1},{4,6},{5,7},{6,4},{7,5},{8,10},{9,11},{10,... | collective-permute-start | bytes 86024 | tf_op jit(solution)/shard_map/ppermute | solution.py:48
  66.6 2.0 %collective-permute-done.19.came_ref = s16[16,2176]{1,0:T(8,128)(2,1)S(1)} collective-permute-done((s16[16,2176]{1,0:T(8,128)(2,1)S(1)}, s16[16,2176]{1,0:T(8,128)(2,1)S(1)}, u32[]{:S(2)}, u32[]{:S(2)}) %collective-permute-start.19) | collective-permute-done | bytes 69664 | tf_op jit(solution)/shard_map/ppermute | solution.py:48
  68.7 0.7 %finish.4.refs_0_ = bf16[16,4608]{1,0:T(8,128)(2,1)} custom-call(f32[16,2048]{1,0:T(8,128)S(1)} %get-tuple-element.51.kept_ref, s16[16,2176]{1,0:T(8,128)(2,1)S(1)} %collective-permute-done.19.came_ref, bf16[16,4608]{1,0:T(8,128)(2,1)} %finish.3.refs_0_), custom_call_target="tpu_custom_call", output_to_operand_aliasing={{}: (2, {})} | custom-call | bytes 262144 | tf_op jit(solution)/shard_map/finish/pallas_call | solution.py:424
  69.4 0.7 finish.5
  (50 shorter events, 4.1 us)
Async XLA Ops:
  1.3 6.1 %copy-start = (bf16[64,4608]{1,0:T(8,128)(2,1)S(1)}, bf16[64,4608]{1,0:T(8,128)(2,1)}, u32[]{:S(2)}) copy-start(bf16[64,4608]{1,0:T(8,128)(2,1)} %refs_4_.5) | copy-start | bytes 1769476
  1.3 6.1 %copy-start.1 = (bf16[1152,512]{1,0:T(8,128)(2,1)S(1)}, bf16[1152,512]{1,0:T(8,128)(2,1)}, u32[]{:S(2)}) copy-start(bf16[1152,512]{1,0:T(8,128)(2,1)} %refs_7_.1) | copy-start | bytes 3538948
  1.4 6.1 %copy-start.2 = (f32[4608]{0:T(1024)S(1)}, f32[4608]{0:T(1024)}, u32[]{:S(2)}) copy-start(f32[4608]{0:T(1024)} %refs_5_.1) | copy-start | bytes 55300
  1.4 5.6 %collective-permute-start.2 = (f32[2,64]{1,0:T(2,128)S(1)}, f32[2,64]{1,0:T(2,128)S(1)}, u32[]{:S(2)}, u32[]{:S(2)}) collective-permute-start(f32[2,64]{1,0:T(2,128)S(1)} %pad_maximum_fusion.refs_0_), channel_id=1, source_target_pairs={{0,12},{4,8},{8,4},{12,0},{1,13},{5,9},{9,5},{13,1},{2,14},{6,10},... | collective-permute-start | bytes 1544 | tf_op jit(solution)/shard_map/ppermute | solution.py:48
  3.8 3.6 %collective-permute-start.1 = (f32[2,64]{1,0:T(2,128)S(1)}, f32[2,64]{1,0:T(2,128)S(1)}, u32[]{:S(2)}, u32[]{:S(2)}) collective-permute-start(f32[2,64]{1,0:T(2,128)S(1)} %pad_maximum_fusion.refs_0_), channel_id=1, source_target_pairs={{0,8},{4,12},{8,0},{12,4},{1,9},{5,13},{9,1},{13,5},{2,10},{6,14},... | collective-permute-start | bytes 1544 | tf_op jit(solution)/shard_map/ppermute | solution.py:48
  4.5 2.9 %collective-permute-start = (f32[2,64]{1,0:T(2,128)S(1)}, f32[2,64]{1,0:T(2,128)S(1)}, u32[]{:S(2)}, u32[]{:S(2)}) collective-permute-start(f32[2,64]{1,0:T(2,128)S(1)} %pad_maximum_fusion.refs_0_), channel_id=1, source_target_pairs={{0,4},{4,0},{8,12},{12,8},{1,5},{5,1},{9,13},{13,9},{2,6},{6,2},{1... | collective-permute-start | bytes 1544 | tf_op jit(solution)/shard_map/ppermute | solution.py:48
  16.6 1.9 %collective-permute-start.3 = (f32[32,3584]{1,0:T(8,128)S(1)}, f32[32,3584]{1,0:T(8,128)S(1)}, u32[]{:S(2)}, u32[]{:S(2)}) collective-permute-start(f32[32,3584]{1,0:T(8,128)S(1)} %get-tuple-element.30), channel_id=1, source_target_pairs={{0,4},{4,0},{8,12},{12,8},{1,5},{5,1},{9,13},{13,9},{2,6},{6,2},{1... | collective-permute-start | bytes 1376264 | tf_op jit(solution)/shard_map/ppermute | solution.py:48
  18.6 7.7 %collective-permute-start.4 = (f32[16,3584]{1,0:T(8,128)S(1)}, f32[16,3584]{1,0:T(8,128)S(1)}, u32[]{:S(2)}, u32[]{:S(2)}) collective-permute-start(f32[16,3584]{1,0:T(8,128)S(1)} %get-tuple-element.32), channel_id=1, source_target_pairs={{0,8},{4,12},{8,0},{12,4},{1,9},{5,13},{9,1},{13,5},{2,10},{6,14},... | collective-permute-start | bytes 688136 | tf_op jit(solution)/shard_map/ppermute | solution.py:48
  26.3 8.6 %copy-start.3 = (bf16[4,1024,512]{2,1,0:T(8,128)(2,1)S(1)}, bf16[4,1024,512]{2,1,0:T(8,128)(2,1)}, u32[]{:S(2)}) copy-start(bf16[4,1024,512]{2,1,0:T(8,128)(2,1)} %refs_4_.6) | copy-start | bytes 12582916
  26.3 8.6 %copy-start.4 = (s32[4]{0:T(128)S(1)}, s32[4]{0:T(128)}, u32[]{:S(2)}) copy-start(s32[4]{0:T(128)} %param.13) | copy-start | bytes 52
  26.3 23.0 %slice-start = ((s8[28311552]{0:T(1024)(128)(4,1)}), s8[4194304]{0:T(1024)(128)(4,1)S(1)}, s32[]{:S(2)}) async-start(s8[28311552]{0:T(1024)(128)(4,1)} %bitcast.3), calls=%async_computation | async-start | bytes 8388608
  26.3 23.0 %slice-start.1 = ((s8[28311552]{0:T(1024)(128)(4,1)}), s8[4194304]{0:T(1024)(128)(4,1)S(1)}, s32[]{:S(2)}) async-start(s8[28311552]{0:T(1024)(128)(4,1)} %bitcast.3), calls=%async_computation.1 | async-start | bytes 8388608
  26.3 23.0 %slice-start.2 = ((s8[28311552]{0:T(1024)(128)(4,1)}), s8[4194304]{0:T(1024)(128)(4,1)S(1)}, s32[]{:S(2)}) async-start(s8[28311552]{0:T(1024)(128)(4,1)} %bitcast.3), calls=%async_computation.2 | async-start | bytes 8388608
  26.4 6.0 %collective-permute-start.5 = (bf16[8,2048]{1,0:T(8,128)(2,1)S(1)}, bf16[8,2048]{1,0:T(8,128)(2,1)S(1)}, u32[]{:S(2)}, u32[]{:S(2)}) collective-permute-start(bf16[8,2048]{1,0:T(8,128)(2,1)S(1)} %get-tuple-element.33), channel_id=1, source_target_pairs={{0,3},{1,2},{2,1},{3,0},{4,7},{5,6},{6,5},{7,4},{8,11},{9,10},{10,... | collective-permute-start | bytes 98312 | tf_op jit(solution)/shard_map/ppermute | solution.py:48
  30.0 4.8 %collective-permute-start.6 = (bf16[8,2048]{1,0:T(8,128)(2,1)S(1)}, bf16[8,2048]{1,0:T(8,128)(2,1)S(1)}, u32[]{:S(2)}, u32[]{:S(2)}) collective-permute-start(bf16[8,2048]{1,0:T(8,128)(2,1)S(1)} %get-tuple-element.34), channel_id=1, source_target_pairs={{0,2},{1,3},{2,0},{3,1},{4,6},{5,7},{6,4},{7,5},{8,10},{9,11},{10,... | collective-permute-start | bytes 98312 | tf_op jit(solution)/shard_map/ppermute | solution.py:48
  30.1 4.8 %collective-permute-start.7 = (bf16[8,2048]{1,0:T(8,128)(2,1)S(1)}, bf16[8,2048]{1,0:T(8,128)(2,1)S(1)}, u32[]{:S(2)}, u32[]{:S(2)}) collective-permute-start(bf16[8,2048]{1,0:T(8,128)(2,1)S(1)} %get-tuple-element.35), channel_id=1, source_target_pairs={{0,1},{1,0},{2,3},{3,2},{4,5},{5,4},{6,7},{7,6},{8,9},{9,8},{10,11... | collective-permute-start | bytes 98312 | tf_op jit(solution)/shard_map/ppermute | solution.py:48
  34.9 14.5 %slice-start.3 = ((s8[28311552]{0:T(1024)(128)(4,1)}), s8[4194304]{0:T(1024)(128)(4,1)S(1)}, s32[]{:S(2)}) async-start(s8[28311552]{0:T(1024)(128)(4,1)} %bitcast.3), calls=%async_computation.3 | async-start | bytes 8388608
  34.9 14.5 %slice-start.4 = ((s8[28311552]{0:T(1024)(128)(4,1)}), s8[4194304]{0:T(1024)(128)(4,1)S(1)}, s32[]{:S(2)}) async-start(s8[28311552]{0:T(1024)(128)(4,1)} %bitcast.3), calls=%async_computation.4 | async-start | bytes 8388608
  36.8 5.7 %collective-permute-start.8 = (bf16[8,1536]{1,0:T(8,128)(2,1)S(1)}, bf16[8,1536]{1,0:T(8,128)(2,1)S(1)}, u32[]{:S(2)}, u32[]{:S(2)}) collective-permute-start(bf16[8,1536]{1,0:T(8,128)(2,1)S(1)} %get-tuple-element.37), channel_id=1, source_target_pairs={{0,3},{1,2},{2,1},{3,0},{4,7},{5,6},{6,5},{7,4},{8,11},{9,10},{10,... | collective-permute-start | bytes 73736 | tf_op jit(solution)/shard_map/ppermute | solution.py:48
  38.3 4.7 %collective-permute-start.9 = (bf16[8,1536]{1,0:T(8,128)(2,1)S(1)}, bf16[8,1536]{1,0:T(8,128)(2,1)S(1)}, u32[]{:S(2)}, u32[]{:S(2)}) collective-permute-start(bf16[8,1536]{1,0:T(8,128)(2,1)S(1)} %get-tuple-element.38), channel_id=1, source_target_pairs={{0,2},{1,3},{2,0},{3,1},{4,6},{5,7},{6,4},{7,5},{8,10},{9,11},{10,... | collective-permute-start | bytes 73736 | tf_op jit(solution)/shard_map/ppermute | solution.py:48
  38.9 4.3 %collective-permute-start.10 = (bf16[8,1536]{1,0:T(8,128)(2,1)S(1)}, bf16[8,1536]{1,0:T(8,128)(2,1)S(1)}, u32[]{:S(2)}, u32[]{:S(2)}) collective-permute-start(bf16[8,1536]{1,0:T(8,128)(2,1)S(1)} %get-tuple-element.39), channel_id=1, source_target_pairs={{0,1},{1,0},{2,3},{3,2},{4,5},{5,4},{6,7},{7,6},{8,9},{9,8},{10,11... | collective-permute-start | bytes 73736 | tf_op jit(solution)/shard_map/ppermute | solution.py:48
  43.3 6.1 %slice-start.5 = ((s8[28311552]{0:T(1024)(128)(4,1)}), s8[4194304]{0:T(1024)(128)(4,1)S(1)}, s32[]{:S(2)}) async-start(s8[28311552]{0:T(1024)(128)(4,1)} %bitcast.3), calls=%async_computation.5 | async-start | bytes 8388608
  43.3 6.1 %slice-start.6 = ((s8[28311552]{0:T(1024)(128)(4,1)}), s8[3145728]{0:T(1024)(128)(4,1)S(1)}, s32[]{:S(2)}) async-start(s8[28311552]{0:T(1024)(128)(4,1)} %bitcast.3), calls=%async_computation.6 | async-start | bytes 6291456
  43.3 4.7 %collective-permute-start.12 = (bf16[16,3072]{1,0:T(8,128)(2,1)S(1)}, bf16[16,3072]{1,0:T(8,128)(2,1)S(1)}, u32[]{:S(2)}, u32[]{:S(2)}) collective-permute-start(bf16[16,3072]{1,0:T(8,128)(2,1)S(1)} %join.1.refs_0_), channel_id=1, source_target_pairs={{0,8},{4,12},{8,0},{12,4},{1,9},{5,13},{9,1},{13,5},{2,10},{6,14},... | collective-permute-start | bytes 294920 | tf_op jit(solution)/shard_map/ppermute | solution.py:48
  44.7 3.3 %collective-permute-start.11 = (bf16[16,3072]{1,0:T(8,128)(2,1)S(1)}, bf16[16,3072]{1,0:T(8,128)(2,1)S(1)}, u32[]{:S(2)}, u32[]{:S(2)}) collective-permute-start(bf16[16,3072]{1,0:T(8,128)(2,1)S(1)} %join.1.refs_0_), channel_id=1, source_target_pairs={{0,4},{4,0},{8,12},{12,8},{1,5},{5,1},{9,13},{13,9},{2,6},{6,2},{1... | collective-permute-start | bytes 294920 | tf_op jit(solution)/shard_map/ppermute | solution.py:48
  48.0 1.3 %collective-permute-start.13 = (bf16[16,3072]{1,0:T(8,128)(2,1)S(1)}, bf16[16,3072]{1,0:T(8,128)(2,1)S(1)}, u32[]{:S(2)}, u32[]{:S(2)}) collective-permute-start(bf16[16,3072]{1,0:T(8,128)(2,1)S(1)} %collective-permute-done.12.refs_2_), channel_id=1, source_target_pairs={{0,4},{4,0},{8,12},{12,8},{1,5},{5,1},{9,13},{13,9},{2,6},{6,2},{1... | collective-permute-start | bytes 294920 | tf_op jit(solution)/shard_map/ppermute | solution.py:48
  51.5 5.5 %collective-permute-start.14 = (s16[32,1920]{1,0:T(8,128)(2,1)S(1)}, s16[32,1920]{1,0:T(8,128)(2,1)S(1)}, u32[]{:S(2)}, u32[]{:S(2)}) collective-permute-start(s16[32,1920]{1,0:T(8,128)(2,1)S(1)} %get-tuple-element.42), channel_id=1, source_target_pairs={{0,1},{1,0},{2,3},{3,2},{4,5},{5,4},{6,7},{7,6},{8,9},{9,8},{10,11... | collective-permute-start | bytes 368648 | tf_op jit(solution)/shard_map/ppermute | solution.py:48
  55.8 6.7 %collective-permute-start.18 = (s16[32,2176]{1,0:T(8,128)(2,1)S(1)}, s16[32,2176]{1,0:T(8,128)(2,1)S(1)}, u32[]{:S(2)}, u32[]{:S(2)}) collective-permute-start(s16[32,2176]{1,0:T(8,128)(2,1)S(1)} %get-tuple-element.50), channel_id=1, source_target_pairs={{0,1},{1,0},{2,3},{3,2},{4,5},{5,4},{6,7},{7,6},{8,9},{9,8},{10,11... | collective-permute-start | bytes 417800 | tf_op jit(solution)/shard_map/ppermute | solution.py:48
  57.2 6.2 %collective-permute-start.16 = (s16[16,1920]{1,0:T(8,128)(2,1)S(1)}, s16[16,1920]{1,0:T(8,128)(2,1)S(1)}, u32[]{:S(2)}, u32[]{:S(2)}) collective-permute-start(s16[16,1920]{1,0:T(8,128)(2,1)S(1)} %get-tuple-element.47), channel_id=1, source_target_pairs={{0,2},{1,3},{2,0},{3,1},{4,6},{5,7},{6,4},{7,5},{8,10},{9,11},{10,... | collective-permute-start | bytes 184328 | tf_op jit(solution)/shard_map/ppermute | solution.py:48
  60.0 4.4 %collective-permute-start.15 = (s16[32,896]{1,0:T(8,128)(2,1)S(1)}, s16[32,896]{1,0:T(8,128)(2,1)S(1)}, u32[]{:S(2)}, u32[]{:S(2)}) collective-permute-start(s16[32,896]{1,0:T(8,128)(2,1)S(1)} %get-tuple-element.46), channel_id=1, source_target_pairs={{0,1},{1,0},{2,3},{3,2},{4,5},{5,4},{6,7},{7,6},{8,9},{9,8},{10,11... | collective-permute-start | bytes 172040 | tf_op jit(solution)/shard_map/ppermute | solution.py:48
  62.6 6.0 %collective-permute-start.19 = (s16[16,2176]{1,0:T(8,128)(2,1)S(1)}, s16[16,2176]{1,0:T(8,128)(2,1)S(1)}, u32[]{:S(2)}, u32[]{:S(2)}) collective-permute-start(s16[16,2176]{1,0:T(8,128)(2,1)S(1)} %get-tuple-element.52), channel_id=1, source_target_pairs={{0,2},{1,3},{2,0},{3,1},{4,6},{5,7},{6,4},{7,5},{8,10},{9,11},{10,... | collective-permute-start | bytes 208904 | tf_op jit(solution)/shard_map/ppermute | solution.py:48
  64.6 4.8 %collective-permute-start.17 = (s16[16,896]{1,0:T(8,128)(2,1)S(1)}, s16[16,896]{1,0:T(8,128)(2,1)S(1)}, u32[]{:S(2)}, u32[]{:S(2)}) collective-permute-start(s16[16,896]{1,0:T(8,128)(2,1)S(1)} %get-tuple-element.49), channel_id=1, source_target_pairs={{0,2},{1,3},{2,0},{3,1},{4,6},{5,7},{6,4},{7,5},{8,10},{9,11},{10,... | collective-permute-start | bytes 86024 | tf_op jit(solution)/shard_map/ppermute | solution.py:48

commit v16 on v11

--- a/solution.py
+++ b/solution.py
@@ -59,9 +59,17 @@
     return [x]
 
 
+def start_order(count):
+    return sorted(range(1, count), key=lambda d: (d != count // 2, -d))
+
+
 def exchange(blocks, axis):
-    far_first = {d: swap(blocks[d], axis, d) for d in range(len(blocks) - 1, 0, -1)}
-    return [blocks[0]] + [far_first[d] for d in range(1, len(blocks))]
+    return [swap(blocks[d], axis, d) for d in start_order(len(blocks))] + [blocks[0]]
+
+
+def by_distance(came):
+    order = start_order(len(came)) + [0]
+    return [came[order.index(d)] for d in range(len(came))]
 
 
 def gather(x, axis):
@@ -233,7 +241,7 @@
 
 
 def attend_kernel(head_dim, count, lengths_ref, *refs):
-    came_refs, kv_ref = refs[:count][::-1], refs[count]
+    came_refs, kv_ref = by_distance(refs[:count]), refs[count]
     out_refs, (heads, contexts) = refs[count + 1 : 2 * count + 1], refs[2 * count + 1 :]
     rows, positions = kv_ref.shape[0], kv_ref.shape[1]
     half = came_refs[0].shape[1]
@@ -297,7 +305,7 @@
     return call(
         functools.partial(attend_kernel, head_dim, count),
         [jax.ShapeDtypeStruct((PAD, queries // 2), jnp.bfloat16)] * count,
-        (lengths, *came[::-1], in_vmem(kv)),
+        (lengths, *came, in_vmem(kv)),
         [FULL] * (count + 2),
         "attend",
         scratch=[
@@ -314,9 +322,9 @@
     out_ref, joined = refs[-2:]
     half = joined.shape[1]
     rows = out_ref.shape[0] // count
-    for d in range(count):
+    for d, ref in enumerate(by_distance(refs[:count])):
         at = pl.ds(pl.multiple_of((lax.axis_index("narrow") ^ d) * PAD, PAD), PAD)
-        joined[at, :] = refs[count - 1 - d][...].astype(jnp.float32)
+        joined[at, :] = ref[...].astype(jnp.float32)
     for side in range(2):
         came = [joined[j * PAD + side * rows : j * PAD + (side + 1) * rows, :] for j in range(count)]
         out_ref[:, side * half : (side + 1) * half] = jnp.concatenate(came, axis=0).astype(jnp.bfloat16)
@@ -459,7 +467,7 @@
     returned = call(
         join_kernel,
         jax.ShapeDtypeStruct((narrow_count * own_rows, queries), jnp.bfloat16),
-        exchange(context, "narrow")[::-1],
+        exchange(context, "narrow"),
         [FULL] * narrow_count,
         "join",
         scratch=[pltpu.VMEM((narrow_count * PAD, queries // 2), jnp.float32)],

time: 69.7 us -> 69.4 us (level)
  transfers between devices with their start and end apart: 20 -> 20, of which waited for: 14 -> 12; matrix products, arithmetic and copies ran while one was open for 0% -> 0% of each run, Pallas kernels for 11% -> 11%
where the time goes in v16:
time: 69.4 us; the launch traced here: 69.2 us
  waiting for transfers between devices  23.9 us (34%)
  starting transfers between devices  22.4 us (32%)
  Pallas kernels  21.3 us (31%)
  other arithmetic  1.32 us (2%)
    ppermute x20, waiting for transfers between devices, swap(): return lax.ppermute(x, axis, [(i, i ^ distance) for i in range(count)])  23.9 us
    ppermute x20, starting transfers between devices, swap(): return lax.ppermute(x, axis, [(i, i ^ distance) for i in range(count)])  22.4 us
    pallas_call x12, Pallas kernels, call(): pl.pallas_call(kernel, out_shape=outs, in_specs=specs, out_specs=jax.tree...  19.1 us
    pallas_call x3, Pallas kernels, finish(): pl.pallas_call(functools.partial(finish_kernel, start), out_shape=pltpu.H...  2.15 us
  transfers between devices with their start and end apart: 20, of which 12 were waited for; matrix products, arithmetic and copies ran while one was open for 0% of the time, Pallas kernels for 11%

profile of v16, /device:TPU:0, one launch (start us, length us, event | category | flops | bytes accessed | tf_op | source)
XLA Modules:
  0.0 69.2 jit_solution(7386063202071568348)
XLA Ops:
  0.0 1.3 %convert_reduce_fusion = (f32[64]{0:T(128)S(1)}, f32[64]{0:T(128)S(1)}) fusion(bf16[64,4608]{1,0:T(8,128)(2,1)} %refs_4_.5), kind=kLoop, calls=%fused_computation.1 | loop fusion | flops 1179520 | bytes 590336 | tf_op jit(solution)/shard_map/reduce_sum | solution.py:440
  1.4 2.5 %collective-permute-start.2 = (f32[2,64]{1,0:T(2,128)S(1)}, f32[2,64]{1,0:T(2,128)S(1)}, u32[]{:S(2)}, u32[]{:S(2)}) collective-permute-start(f32[2,64]{1,0:T(2,128)S(1)} %pad_maximum_fusion.refs_0_), channel_id=1, source_target_pairs={{0,12},{4,8},{8,4},{12,0},{1,13},{5,9},{9,5},{13,1},{2,14},{6,10},... | collective-permute-start | bytes 1544 | tf_op jit(solution)/shard_map/ppermute | solution.py:48
  4.5 2.3 %fetch_query_weight.1.refs_8_ = bf16[768,3072]{1,0:T(8,128)(2,1)S(1)} custom-call(bf16[4608,3072]{1,0:T(8,128)(2,1)} %refs_6_.1, f32[2,64]{1,0:T(2,128)S(1)} %pad_maximum_fusion.refs_0_), custom_call_target="tpu_custom_call" | custom-call | bytes 4718592 | tf_op jit(solution)/shard_map/fetch_query_weight/pallas_call | solution.py:22
  7.4 8.6 %project.1 = (f32[32,3584]{1,0:T(8,128)S(1)}, f32[32,3584]{1,0:T(8,128)S(1)}) custom-call(f32[2,64]{1,0:T(2,128)S(1)} %pad_maximum_fusion.refs_0_, f32[2,64]{1,0:T(2,128)S(1)} %collective-permute-done.refs_1_, f32[2,64]{1,0:T(2,128)S(1)} %collective-permute-done.1.refs_2_, f32[2,64]{1,0:T(2,128)S(1)} %collective-permute-done.2.refs_3_, ...), custom_call_target="tpu_custom_call" | custom-call | flops 1811939328 | bytes 23592960 | tf_op jit(solution)/shard_map/project/pallas_call | solution.py:22
  16.2 1.8 %collective-permute-done.3.came_ref = f32[32,3584]{1,0:T(8,128)S(1)} collective-permute-done((f32[32,3584]{1,0:T(8,128)S(1)}, f32[32,3584]{1,0:T(8,128)S(1)}, u32[]{:S(2)}, u32[]{:S(2)}) %collective-permute-start.3) | collective-permute-done | bytes 458784 | tf_op jit(solution)/shard_map/ppermute | solution.py:48
  18.0 1.3 %collective-permute-start.4 = (f32[16,3584]{1,0:T(8,128)S(1)}, f32[16,3584]{1,0:T(8,128)S(1)}, u32[]{:S(2)}, u32[]{:S(2)}) collective-permute-start(f32[16,3584]{1,0:T(8,128)S(1)} %get-tuple-element.32), channel_id=1, source_target_pairs={{0,8},{4,12},{8,0},{12,4},{1,9},{5,13},{9,1},{13,5},{2,10},{6,14},... | collective-permute-start | bytes 688136 | tf_op jit(solution)/shard_map/ppermute | solution.py:48
  19.3 6.4 %collective-permute-done.4.came_ref = f32[16,3584]{1,0:T(8,128)S(1)} collective-permute-done((f32[16,3584]{1,0:T(8,128)S(1)}, f32[16,3584]{1,0:T(8,128)S(1)}, u32[]{:S(2)}, u32[]{:S(2)}) %collective-permute-start.4) | collective-permute-done | bytes 229408 | tf_op jit(solution)/shard_map/ppermute | solution.py:48
  25.8 2.7 %collective-permute-start.5 = (bf16[8,2048]{1,0:T(8,128)(2,1)S(1)}, bf16[8,2048]{1,0:T(8,128)(2,1)S(1)}, u32[]{:S(2)}, u32[]{:S(2)}) collective-permute-start(bf16[8,2048]{1,0:T(8,128)(2,1)S(1)} %get-tuple-element.33), channel_id=1, source_target_pairs={{0,2},{1,3},{2,0},{3,1},{4,6},{5,7},{6,4},{7,5},{8,10},{9,11},{10,... | collective-permute-start | bytes 98312 | tf_op jit(solution)/shard_map/ppermute | solution.py:48
  28.5 1.3 %collective-permute-start.6 = (bf16[8,2048]{1,0:T(8,128)(2,1)S(1)}, bf16[8,2048]{1,0:T(8,128)(2,1)S(1)}, u32[]{:S(2)}, u32[]{:S(2)}) collective-permute-start(bf16[8,2048]{1,0:T(8,128)(2,1)S(1)} %get-tuple-element.34), channel_id=1, source_target_pairs={{0,3},{1,2},{2,1},{3,0},{4,7},{5,6},{6,5},{7,4},{8,11},{9,10},{10,... | collective-permute-start | bytes 98312 | tf_op jit(solution)/shard_map/ppermute | solution.py:48
  30.7 3.5 %collective-permute-done.6.refs_1_ = bf16[8,2048]{1,0:T(8,128)(2,1)S(1)} collective-permute-done((bf16[8,2048]{1,0:T(8,128)(2,1)S(1)}, bf16[8,2048]{1,0:T(8,128)(2,1)S(1)}, u32[]{:S(2)}, u32[]{:S(2)}) %collective-permute-start.6) | collective-permute-done | bytes 32800 | tf_op jit(solution)/shard_map/ppermute | solution.py:48
  34.2 1.9 %attend.1 = (bf16[8,1536]{1,0:T(8,128)(2,1)S(1)}, bf16[8,1536]{1,0:T(8,128)(2,1)S(1)}, bf16[8,1536]{1,0:T(8,128)(2,1)S(1)}, bf16[8,1536]{1,0:T(8,128)(2,1)S(1)}) custom-call(s32[1,4]{1,0:T(1,128)S(1)} %bitcast.5, bf16[8,2048]{1,0:T(8,128)(2,1)S(1)} %collective-permute-done.5.refs_0_, bf16[8,2048]{1,0:T(8,128)(2,1)S(1)} %collective-permute-done.6.refs_1_, ...), custom_call_target="tpu_custom_call" | custom-call | flops 5000000000 | tf_op jit(solution)/shard_map/attend/pallas_call | solution.py:22
  36.1 1.3 %collective-permute-start.8 = (bf16[8,1536]{1,0:T(8,128)(2,1)S(1)}, bf16[8,1536]{1,0:T(8,128)(2,1)S(1)}, u32[]{:S(2)}, u32[]{:S(2)}) collective-permute-start(bf16[8,1536]{1,0:T(8,128)(2,1)S(1)} %get-tuple-element.37), channel_id=1, source_target_pairs={{0,2},{1,3},{2,0},{3,1},{4,6},{5,7},{6,4},{7,5},{8,10},{9,11},{10,... | collective-permute-start | bytes 73736 | tf_op jit(solution)/shard_map/ppermute | solution.py:48
  37.4 1.0 %collective-permute-start.9 = (bf16[8,1536]{1,0:T(8,128)(2,1)S(1)}, bf16[8,1536]{1,0:T(8,128)(2,1)S(1)}, u32[]{:S(2)}, u32[]{:S(2)}) collective-permute-start(bf16[8,1536]{1,0:T(8,128)(2,1)S(1)} %get-tuple-element.38), channel_id=1, source_target_pairs={{0,3},{1,2},{2,1},{3,0},{4,7},{5,6},{6,5},{7,4},{8,11},{9,10},{10,... | collective-permute-start | bytes 73736 | tf_op jit(solution)/shard_map/ppermute | solution.py:48
  38.4 1.2 %collective-permute-start.10 = (bf16[8,1536]{1,0:T(8,128)(2,1)S(1)}, bf16[8,1536]{1,0:T(8,128)(2,1)S(1)}, u32[]{:S(2)}, u32[]{:S(2)}) collective-permute-start(bf16[8,1536]{1,0:T(8,128)(2,1)S(1)} %get-tuple-element.39), channel_id=1, source_target_pairs={{0,1},{1,0},{2,3},{3,2},{4,5},{5,4},{6,7},{7,6},{8,9},{9,8},{10,11... | collective-permute-start | bytes 73736 | tf_op jit(solution)/shard_map/ppermute | solution.py:48
  39.7 1.2 %collective-permute-done.8.refs_0_ = bf16[8,1536]{1,0:T(8,128)(2,1)S(1)} collective-permute-done((bf16[8,1536]{1,0:T(8,128)(2,1)S(1)}, bf16[8,1536]{1,0:T(8,128)(2,1)S(1)}, u32[]{:S(2)}, u32[]{:S(2)}) %collective-permute-start.8) | collective-permute-done | bytes 24608 | tf_op jit(solution)/shard_map/ppermute | solution.py:48
  40.9 2.1 %collective-permute-done.9.refs_1_ = bf16[8,1536]{1,0:T(8,128)(2,1)S(1)} collective-permute-done((bf16[8,1536]{1,0:T(8,128)(2,1)S(1)}, bf16[8,1536]{1,0:T(8,128)(2,1)S(1)}, u32[]{:S(2)}, u32[]{:S(2)}) %collective-permute-start.9) | collective-permute-done | bytes 24608 | tf_op jit(solution)/shard_map/ppermute | solution.py:48
  43.1 1.3 %collective-permute-start.12 = (bf16[16,3072]{1,0:T(8,128)(2,1)S(1)}, bf16[16,3072]{1,0:T(8,128)(2,1)S(1)}, u32[]{:S(2)}, u32[]{:S(2)}) collective-permute-start(bf16[16,3072]{1,0:T(8,128)(2,1)S(1)} %join.1.refs_0_), channel_id=1, source_target_pairs={{0,8},{4,12},{8,0},{12,4},{1,9},{5,13},{9,1},{13,5},{2,10},{6,14},... | collective-permute-start | bytes 294920 | tf_op jit(solution)/shard_map/ppermute | solution.py:48
  44.4 3.4 %collective-permute-done.12.refs_2_ = bf16[16,3072]{1,0:T(8,128)(2,1)S(1)} collective-permute-done((bf16[16,3072]{1,0:T(8,128)(2,1)S(1)}, bf16[16,3072]{1,0:T(8,128)(2,1)S(1)}, u32[]{:S(2)}, u32[]{:S(2)}) %collective-permute-start.12) | collective-permute-done | bytes 98336 | tf_op jit(solution)/shard_map/ppermute | solution.py:48
  47.8 1.3 %collective-permute-done.13.refs_3_ = bf16[16,3072]{1,0:T(8,128)(2,1)S(1)} collective-permute-done((bf16[16,3072]{1,0:T(8,128)(2,1)S(1)}, bf16[16,3072]{1,0:T(8,128)(2,1)S(1)}, u32[]{:S(2)}, u32[]{:S(2)}) %collective-permute-start.13) | collective-permute-done | bytes 98336 | tf_op jit(solution)/shard_map/ppermute | solution.py:48
  49.1 2.1 %output_part.3 = (f32[64,1792]{1,0:T(8,128)S(1)}, s16[32,1920]{1,0:T(8,128)(2,1)S(1)}) custom-call(bf16[16,3072]{1,0:T(8,128)(2,1)S(1)} %join.1.refs_0_, bf16[16,3072]{1,0:T(8,128)(2,1)S(1)} %collective-permute-done.11.refs_1_, bf16[16,3072]{1,0:T(8,128)(2,1)S(1)} %collective-permute-done.12.refs_2_, bf16[16,3072]{1,0:T(8,128)(2,1)S(1)} %collective-permute-done.13.refs_3_, ...), custom_call_target="tpu_custom_call" | custom-call | flops 704643072 | bytes 393216 | tf_op jit(solution)/shard_map/output_part/pallas_call | solution.py:22
  51.8 2.4 %output_part.4 = (f32[64,2048]{1,0:T(8,128)S(1)}, s16[32,2176]{1,0:T(8,128)(2,1)S(1)}) custom-call(bf16[16,3072]{1,0:T(8,128)(2,1)S(1)} %join.1.refs_0_, bf16[16,3072]{1,0:T(8,128)(2,1)S(1)} %collective-permute-done.11.refs_1_, bf16[16,3072]{1,0:T(8,128)(2,1)S(1)} %collective-permute-done.12.refs_2_, bf16[16,3072]{1,0:T(8,128)(2,1)S(1)} %collective-permute-done.13.refs_3_, ...), custom_call_target="tpu_custom_call" | custom-call | flops 805306368 | bytes 393216 | tf_op jit(solution)/shard_map/output_part/pallas_call | solution.py:22
  54.2 1.6 %collective-permute-start.18 = (s16[32,2176]{1,0:T(8,128)(2,1)S(1)}, s16[32,2176]{1,0:T(8,128)(2,1)S(1)}, u32[]{:S(2)}, u32[]{:S(2)}) collective-permute-start(s16[32,2176]{1,0:T(8,128)(2,1)S(1)} %get-tuple-element.50), channel_id=1, source_target_pairs={{0,1},{1,0},{2,3},{3,2},{4,5},{5,4},{6,7},{7,6},{8,9},{9,8},{10,11... | collective-permute-start | bytes 417800 | tf_op jit(solution)/shard_map/ppermute | solution.py:48
  55.8 0.9 %collective-permute-done.14.came_ref = s16[32,1920]{1,0:T(8,128)(2,1)S(1)} collective-permute-done((s16[32,1920]{1,0:T(8,128)(2,1)S(1)}, s16[32,1920]{1,0:T(8,128)(2,1)S(1)}, u32[]{:S(2)}, u32[]{:S(2)}) %collective-permute-start.14) | collective-permute-done | bytes 122912 | tf_op jit(solution)/shard_map/ppermute | solution.py:48
  56.9 1.1 %collective-permute-start.16 = (s16[16,1920]{1,0:T(8,128)(2,1)S(1)}, s16[16,1920]{1,0:T(8,128)(2,1)S(1)}, u32[]{:S(2)}, u32[]{:S(2)}) collective-permute-start(s16[16,1920]{1,0:T(8,128)(2,1)S(1)} %get-tuple-element.47), channel_id=1, source_target_pairs={{0,2},{1,3},{2,0},{3,1},{4,6},{5,7},{6,4},{7,5},{8,10},{9,11},{10,... | collective-permute-start | bytes 184328 | tf_op jit(solution)/shard_map/ppermute | solution.py:48
  58.0 1.0 %output_part.5 = (f32[64,768]{1,0:T(8,128)S(1)}, s16[32,896]{1,0:T(8,128)(2,1)S(1)}) custom-call(bf16[16,3072]{1,0:T(8,128)(2,1)S(1)} %join.1.refs_0_, bf16[16,3072]{1,0:T(8,128)(2,1)S(1)} %collective-permute-done.11.refs_1_, bf16[16,3072]{1,0:T(8,128)(2,1)S(1)} %collective-permute-done.12.refs_2_, bf16[16,3072]{1,0:T(8,128)(2,1)S(1)} %collective-permute-done.13.refs_3_, ...), custom_call_target="tpu_custom_call" | custom-call | flops 301989888 | bytes 393216 | tf_op jit(solution)/shard_map/output_part/pallas_call | solution.py:22
  59.0 1.6 %collective-permute-start.15 = (s16[32,896]{1,0:T(8,128)(2,1)S(1)}, s16[32,896]{1,0:T(8,128)(2,1)S(1)}, u32[]{:S(2)}, u32[]{:S(2)}) collective-permute-start(s16[32,896]{1,0:T(8,128)(2,1)S(1)} %get-tuple-element.46), channel_id=1, source_target_pairs={{0,1},{1,0},{2,3},{3,2},{4,5},{5,4},{6,7},{7,6},{8,9},{9,8},{10,11... | collective-permute-start | bytes 172040 | tf_op jit(solution)/shard_map/ppermute | solution.py:48
  60.9 1.9 %collective-permute-start.19 = (s16[16,2176]{1,0:T(8,128)(2,1)S(1)}, s16[16,2176]{1,0:T(8,128)(2,1)S(1)}, u32[]{:S(2)}, u32[]{:S(2)}) collective-permute-start(s16[16,2176]{1,0:T(8,128)(2,1)S(1)} %get-tuple-element.52), channel_id=1, source_target_pairs={{0,2},{1,3},{2,0},{3,1},{4,6},{5,7},{6,4},{7,5},{8,10},{9,11},{10,... | collective-permute-start | bytes 208904 | tf_op jit(solution)/shard_map/ppermute | solution.py:48
  62.7 0.7 %finish.3.refs_0_ = bf16[16,4608]{1,0:T(8,128)(2,1)} custom-call(f32[16,1792]{1,0:T(8,128)S(1)} %get-tuple-element.44.refs_5_.kept_ref, s16[16,1920]{1,0:T(8,128)(2,1)S(1)} %collective-permute-done.16.came_ref), custom_call_target="tpu_custom_call" | custom-call | bytes 229376 | tf_op jit(solution)/shard_map/finish/pallas_call | solution.py:418
  63.7 2.0 %collective-permute-start.17 = (s16[16,896]{1,0:T(8,128)(2,1)S(1)}, s16[16,896]{1,0:T(8,128)(2,1)S(1)}, u32[]{:S(2)}, u32[]{:S(2)}) collective-permute-start(s16[16,896]{1,0:T(8,128)(2,1)S(1)} %get-tuple-element.49), channel_id=1, source_target_pairs={{0,2},{1,3},{2,0},{3,1},{4,6},{5,7},{6,4},{7,5},{8,10},{9,11},{10,... | collective-permute-start | bytes 86024 | tf_op jit(solution)/shard_map/ppermute | solution.py:48
  65.6 1.8 %collective-permute-done.19.came_ref = s16[16,2176]{1,0:T(8,128)(2,1)S(1)} collective-permute-done((s16[16,2176]{1,0:T(8,128)(2,1)S(1)}, s16[16,2176]{1,0:T(8,128)(2,1)S(1)}, u32[]{:S(2)}, u32[]{:S(2)}) %collective-permute-start.19) | collective-permute-done | bytes 69664 | tf_op jit(solution)/shard_map/ppermute | solution.py:48
  67.4 0.7 %finish.4.refs_0_ = bf16[16,4608]{1,0:T(8,128)(2,1)} custom-call(f32[16,2048]{1,0:T(8,128)S(1)} %get-tuple-element.51.kept_ref, s16[16,2176]{1,0:T(8,128)(2,1)S(1)} %collective-permute-done.19.came_ref, bf16[16,4608]{1,0:T(8,128)(2,1)} %finish.3.refs_0_), custom_call_target="tpu_custom_call", output_to_operand_aliasing={{}: (2, {})} | custom-call | bytes 262144 | tf_op jit(solution)/shard_map/finish/pallas_call | solution.py:418
  68.5 0.7 %finish.5 = bf16[16,4608]{1,0:T(8,128)(2,1)} custom-call(f32[16,768]{1,0:T(8,128)S(1)} %get-tuple-element.48.kept_ref, s16[16,896]{1,0:T(8,128)(2,1)S(1)} %collective-permute-done.17.came_ref, bf16[16,4608]{1,0:T(8,128)(2,1)} %finish.4.refs_0_), custom_call_target="tpu_custom_call", output_to_operand_aliasing={{}: (2, {})} | custom-call | bytes 98304 | tf_op jit(solution)/shard_map/finish/pallas_call | solution.py:418
  (50 shorter events, 3.9 us)
Async XLA Ops:
  1.3 6.1 %copy-start = (bf16[64,4608]{1,0:T(8,128)(2,1)S(1)}, bf16[64,4608]{1,0:T(8,128)(2,1)}, u32[]{:S(2)}) copy-start(bf16[64,4608]{1,0:T(8,128)(2,1)} %refs_4_.5) | copy-start | bytes 1769476
  1.3 6.1 %copy-start.1 = (bf16[1152,512]{1,0:T(8,128)(2,1)S(1)}, bf16[1152,512]{1,0:T(8,128)(2,1)}, u32[]{:S(2)}) copy-start(bf16[1152,512]{1,0:T(8,128)(2,1)} %refs_7_.1) | copy-start | bytes 3538948
  1.4 6.1 %copy-start.2 = (f32[4608]{0:T(1024)S(1)}, f32[4608]{0:T(1024)}, u32[]{:S(2)}) copy-start(f32[4608]{0:T(1024)} %refs_5_.1) | copy-start | bytes 55300
  1.4 5.5 %collective-permute-start.2 = (f32[2,64]{1,0:T(2,128)S(1)}, f32[2,64]{1,0:T(2,128)S(1)}, u32[]{:S(2)}, u32[]{:S(2)}) collective-permute-start(f32[2,64]{1,0:T(2,128)S(1)} %pad_maximum_fusion.refs_0_), channel_id=1, source_target_pairs={{0,12},{4,8},{8,4},{12,0},{1,13},{5,9},{9,5},{13,1},{2,14},{6,10},... | collective-permute-start | bytes 1544 | tf_op jit(solution)/shard_map/ppermute | solution.py:48
  3.8 3.6 %collective-permute-start.1 = (f32[2,64]{1,0:T(2,128)S(1)}, f32[2,64]{1,0:T(2,128)S(1)}, u32[]{:S(2)}, u32[]{:S(2)}) collective-permute-start(f32[2,64]{1,0:T(2,128)S(1)} %pad_maximum_fusion.refs_0_), channel_id=1, source_target_pairs={{0,8},{4,12},{8,0},{12,4},{1,9},{5,13},{9,1},{13,5},{2,10},{6,14},... | collective-permute-start | bytes 1544 | tf_op jit(solution)/shard_map/ppermute | solution.py:48
  4.5 2.9 %collective-permute-start = (f32[2,64]{1,0:T(2,128)S(1)}, f32[2,64]{1,0:T(2,128)S(1)}, u32[]{:S(2)}, u32[]{:S(2)}) collective-permute-start(f32[2,64]{1,0:T(2,128)S(1)} %pad_maximum_fusion.refs_0_), channel_id=1, source_target_pairs={{0,4},{4,0},{8,12},{12,8},{1,5},{5,1},{9,13},{13,9},{2,6},{6,2},{1... | collective-permute-start | bytes 1544 | tf_op jit(solution)/shard_map/ppermute | solution.py:48
  16.1 1.9 %collective-permute-start.3 = (f32[32,3584]{1,0:T(8,128)S(1)}, f32[32,3584]{1,0:T(8,128)S(1)}, u32[]{:S(2)}, u32[]{:S(2)}) collective-permute-start(f32[32,3584]{1,0:T(8,128)S(1)} %get-tuple-element.30), channel_id=1, source_target_pairs={{0,4},{4,0},{8,12},{12,8},{1,5},{5,1},{9,13},{13,9},{2,6},{6,2},{1... | collective-permute-start | bytes 1376264 | tf_op jit(solution)/shard_map/ppermute | solution.py:48
  18.0 7.7 %collective-permute-start.4 = (f32[16,3584]{1,0:T(8,128)S(1)}, f32[16,3584]{1,0:T(8,128)S(1)}, u32[]{:S(2)}, u32[]{:S(2)}) collective-permute-start(f32[16,3584]{1,0:T(8,128)S(1)} %get-tuple-element.32), channel_id=1, source_target_pairs={{0,8},{4,12},{8,0},{12,4},{1,9},{5,13},{9,1},{13,5},{2,10},{6,14},... | collective-permute-start | bytes 688136 | tf_op jit(solution)/shard_map/ppermute | solution.py:48
  25.7 8.5 %copy-start.3 = (bf16[4,1024,512]{2,1,0:T(8,128)(2,1)S(1)}, bf16[4,1024,512]{2,1,0:T(8,128)(2,1)}, u32[]{:S(2)}) copy-start(bf16[4,1024,512]{2,1,0:T(8,128)(2,1)} %refs_4_.6) | copy-start | bytes 12582916
  25.7 8.5 %copy-start.4 = (s32[4]{0:T(128)S(1)}, s32[4]{0:T(128)}, u32[]{:S(2)}) copy-start(s32[4]{0:T(128)} %param.13) | copy-start | bytes 52
  25.7 23.3 %slice-start = ((s8[28311552]{0:T(1024)(128)(4,1)}), s8[4194304]{0:T(1024)(128)(4,1)S(1)}, s32[]{:S(2)}) async-start(s8[28311552]{0:T(1024)(128)(4,1)} %bitcast.3), calls=%async_computation | async-start | bytes 8388608
  25.7 23.3 %slice-start.1 = ((s8[28311552]{0:T(1024)(128)(4,1)}), s8[4194304]{0:T(1024)(128)(4,1)S(1)}, s32[]{:S(2)}) async-start(s8[28311552]{0:T(1024)(128)(4,1)} %bitcast.3), calls=%async_computation.1 | async-start | bytes 8388608
  25.7 23.3 %slice-start.2 = ((s8[28311552]{0:T(1024)(128)(4,1)}), s8[4194304]{0:T(1024)(128)(4,1)S(1)}, s32[]{:S(2)}) async-start(s8[28311552]{0:T(1024)(128)(4,1)} %bitcast.3), calls=%async_computation.2 | async-start | bytes 8388608
  25.8 4.9 %collective-permute-start.5 = (bf16[8,2048]{1,0:T(8,128)(2,1)S(1)}, bf16[8,2048]{1,0:T(8,128)(2,1)S(1)}, u32[]{:S(2)}, u32[]{:S(2)}) collective-permute-start(bf16[8,2048]{1,0:T(8,128)(2,1)S(1)} %get-tuple-element.33), channel_id=1, source_target_pairs={{0,2},{1,3},{2,0},{3,1},{4,6},{5,7},{6,4},{7,5},{8,10},{9,11},{10,... | collective-permute-start | bytes 98312 | tf_op jit(solution)/shard_map/ppermute | solution.py:48
  28.5 5.7 %collective-permute-start.6 = (bf16[8,2048]{1,0:T(8,128)(2,1)S(1)}, bf16[8,2048]{1,0:T(8,128)(2,1)S(1)}, u32[]{:S(2)}, u32[]{:S(2)}) collective-permute-start(bf16[8,2048]{1,0:T(8,128)(2,1)S(1)} %get-tuple-element.34), channel_id=1, source_target_pairs={{0,3},{1,2},{2,1},{3,0},{4,7},{5,6},{6,5},{7,4},{8,11},{9,10},{10,... | collective-permute-start | bytes 98312 | tf_op jit(solution)/shard_map/ppermute | solution.py:48
  29.8 4.4 %collective-permute-start.7 = (bf16[8,2048]{1,0:T(8,128)(2,1)S(1)}, bf16[8,2048]{1,0:T(8,128)(2,1)S(1)}, u32[]{:S(2)}, u32[]{:S(2)}) collective-permute-start(bf16[8,2048]{1,0:T(8,128)(2,1)S(1)} %get-tuple-element.35), channel_id=1, source_target_pairs={{0,1},{1,0},{2,3},{3,2},{4,5},{5,4},{6,7},{7,6},{8,9},{9,8},{10,11... | collective-permute-start | bytes 98312 | tf_op jit(solution)/shard_map/ppermute | solution.py:48
  34.2 14.9 %slice-start.3 = ((s8[28311552]{0:T(1024)(128)(4,1)}), s8[4194304]{0:T(1024)(128)(4,1)S(1)}, s32[]{:S(2)}) async-start(s8[28311552]{0:T(1024)(128)(4,1)} %bitcast.3), calls=%async_computation.3 | async-start | bytes 8388608
  34.2 14.9 %slice-start.4 = ((s8[28311552]{0:T(1024)(128)(4,1)}), s8[4194304]{0:T(1024)(128)(4,1)S(1)}, s32[]{:S(2)}) async-start(s8[28311552]{0:T(1024)(128)(4,1)} %bitcast.3), calls=%async_computation.4 | async-start | bytes 8388608
  36.1 4.8 %collective-permute-start.8 = (bf16[8,1536]{1,0:T(8,128)(2,1)S(1)}, bf16[8,1536]{1,0:T(8,128)(2,1)S(1)}, u32[]{:S(2)}, u32[]{:S(2)}) collective-permute-start(bf16[8,1536]{1,0:T(8,128)(2,1)S(1)} %get-tuple-element.37), channel_id=1, source_target_pairs={{0,2},{1,3},{2,0},{3,1},{4,6},{5,7},{6,4},{7,5},{8,10},{9,11},{10,... | collective-permute-start | bytes 73736 | tf_op jit(solution)/shard_map/ppermute | solution.py:48
  37.4 5.6 %collective-permute-start.9 = (bf16[8,1536]{1,0:T(8,128)(2,1)S(1)}, bf16[8,1536]{1,0:T(8,128)(2,1)S(1)}, u32[]{:S(2)}, u32[]{:S(2)}) collective-permute-start(bf16[8,1536]{1,0:T(8,128)(2,1)S(1)} %get-tuple-element.38), channel_id=1, source_target_pairs={{0,3},{1,2},{2,1},{3,0},{4,7},{5,6},{6,5},{7,4},{8,11},{9,10},{10,... | collective-permute-start | bytes 73736 | tf_op jit(solution)/shard_map/ppermute | solution.py:48
  38.4 4.6 %collective-permute-start.10 = (bf16[8,1536]{1,0:T(8,128)(2,1)S(1)}, bf16[8,1536]{1,0:T(8,128)(2,1)S(1)}, u32[]{:S(2)}, u32[]{:S(2)}) collective-permute-start(bf16[8,1536]{1,0:T(8,128)(2,1)S(1)} %get-tuple-element.39), channel_id=1, source_target_pairs={{0,1},{1,0},{2,3},{3,2},{4,5},{5,4},{6,7},{7,6},{8,9},{9,8},{10,11... | collective-permute-start | bytes 73736 | tf_op jit(solution)/shard_map/ppermute | solution.py:48
  43.0 6.1 %slice-start.5 = ((s8[28311552]{0:T(1024)(128)(4,1)}), s8[4194304]{0:T(1024)(128)(4,1)S(1)}, s32[]{:S(2)}) async-start(s8[28311552]{0:T(1024)(128)(4,1)} %bitcast.3), calls=%async_computation.5 | async-start | bytes 8388608
  43.0 6.1 %slice-start.6 = ((s8[28311552]{0:T(1024)(128)(4,1)}), s8[3145728]{0:T(1024)(128)(4,1)S(1)}, s32[]{:S(2)}) async-start(s8[28311552]{0:T(1024)(128)(4,1)} %bitcast.3), calls=%async_computation.6 | async-start | bytes 6291456
  43.1 4.7 %collective-permute-start.12 = (bf16[16,3072]{1,0:T(8,128)(2,1)S(1)}, bf16[16,3072]{1,0:T(8,128)(2,1)S(1)}, u32[]{:S(2)}, u32[]{:S(2)}) collective-permute-start(bf16[16,3072]{1,0:T(8,128)(2,1)S(1)} %join.1.refs_0_), channel_id=1, source_target_pairs={{0,8},{4,12},{8,0},{12,4},{1,9},{5,13},{9,1},{13,5},{2,10},{6,14},... | collective-permute-start | bytes 294920 | tf_op jit(solution)/shard_map/ppermute | solution.py:48
  44.4 3.4 %collective-permute-start.11 = (bf16[16,3072]{1,0:T(8,128)(2,1)S(1)}, bf16[16,3072]{1,0:T(8,128)(2,1)S(1)}, u32[]{:S(2)}, u32[]{:S(2)}) collective-permute-start(bf16[16,3072]{1,0:T(8,128)(2,1)S(1)} %join.1.refs_0_), channel_id=1, source_target_pairs={{0,4},{4,0},{8,12},{12,8},{1,5},{5,1},{9,13},{13,9},{2,6},{6,2},{1... | collective-permute-start | bytes 294920 | tf_op jit(solution)/shard_map/ppermute | solution.py:48
  47.8 1.3 %collective-permute-start.13 = (bf16[16,3072]{1,0:T(8,128)(2,1)S(1)}, bf16[16,3072]{1,0:T(8,128)(2,1)S(1)}, u32[]{:S(2)}, u32[]{:S(2)}) collective-permute-start(bf16[16,3072]{1,0:T(8,128)(2,1)S(1)} %collective-permute-done.12.refs_2_), channel_id=1, source_target_pairs={{0,4},{4,0},{8,12},{12,8},{1,5},{5,1},{9,13},{13,9},{2,6},{6,2},{1... | collective-permute-start | bytes 294920 | tf_op jit(solution)/shard_map/ppermute | solution.py:48
  51.3 5.4 %collective-permute-start.14 = (s16[32,1920]{1,0:T(8,128)(2,1)S(1)}, s16[32,1920]{1,0:T(8,128)(2,1)S(1)}, u32[]{:S(2)}, u32[]{:S(2)}) collective-permute-start(s16[32,1920]{1,0:T(8,128)(2,1)S(1)} %get-tuple-element.42), channel_id=1, source_target_pairs={{0,1},{1,0},{2,3},{3,2},{4,5},{5,4},{6,7},{7,6},{8,9},{9,8},{10,11... | collective-permute-start | bytes 368648 | tf_op jit(solution)/shard_map/ppermute | solution.py:48
  54.2 6.5 %collective-permute-start.18 = (s16[32,2176]{1,0:T(8,128)(2,1)S(1)}, s16[32,2176]{1,0:T(8,128)(2,1)S(1)}, u32[]{:S(2)}, u32[]{:S(2)}) collective-permute-start(s16[32,2176]{1,0:T(8,128)(2,1)S(1)} %get-tuple-element.50), channel_id=1, source_target_pairs={{0,1},{1,0},{2,3},{3,2},{4,5},{5,4},{6,7},{7,6},{8,9},{9,8},{10,11... | collective-permute-start | bytes 417800 | tf_op jit(solution)/shard_map/ppermute | solution.py:48
  56.9 5.9 %collective-permute-start.16 = (s16[16,1920]{1,0:T(8,128)(2,1)S(1)}, s16[16,1920]{1,0:T(8,128)(2,1)S(1)}, u32[]{:S(2)}, u32[]{:S(2)}) collective-permute-start(s16[16,1920]{1,0:T(8,128)(2,1)S(1)} %get-tuple-element.47), channel_id=1, source_target_pairs={{0,2},{1,3},{2,0},{3,1},{4,6},{5,7},{6,4},{7,5},{8,10},{9,11},{10,... | collective-permute-start | bytes 184328 | tf_op jit(solution)/shard_map/ppermute | solution.py:48
  59.0 4.5 %collective-permute-start.15 = (s16[32,896]{1,0:T(8,128)(2,1)S(1)}, s16[32,896]{1,0:T(8,128)(2,1)S(1)}, u32[]{:S(2)}, u32[]{:S(2)}) collective-permute-start(s16[32,896]{1,0:T(8,128)(2,1)S(1)} %get-tuple-element.46), channel_id=1, source_target_pairs={{0,1},{1,0},{2,3},{3,2},{4,5},{5,4},{6,7},{7,6},{8,9},{9,8},{10,11... | collective-permute-start | bytes 172040 | tf_op jit(solution)/shard_map/ppermute | solution.py:48
  60.9 6.5 %collective-permute-start.19 = (s16[16,2176]{1,0:T(8,128)(2,1)S(1)}, s16[16,2176]{1,0:T(8,128)(2,1)S(1)}, u32[]{:S(2)}, u32[]{:S(2)}) collective-permute-start(s16[16,2176]{1,0:T(8,128)(2,1)S(1)} %get-tuple-element.52), channel_id=1, source_target_pairs={{0,2},{1,3},{2,0},{3,1},{4,6},{5,7},{6,4},{7,5},{8,10},{9,11},{10,... | collective-permute-start | bytes 208904 | tf_op jit(solution)/shard_map/ppermute | solution.py:48
  63.7 4.8 %collective-permute-start.17 = (s16[16,896]{1,0:T(8,128)(2,1)S(1)}, s16[16,896]{1,0:T(8,128)(2,1)S(1)}, u32[]{:S(2)}, u32[]{:S(2)}) collective-permute-start(s16[16,896]{1,0:T(8,128)(2,1)S(1)} %get-tuple-element.49), channel_id=1, source_target_pairs={{0,2},{1,3},{2,0},{3,1},{4,6},{5,7},{6,4},{7,5},{8,10},{9,11},{10,... | collective-permute-start | bytes 86024 | tf_op jit(solution)/shard_map/ppermute | solution.py:48

commit v17 on v16

--- a/solution.py
+++ b/solution.py
@@ -59,16 +59,16 @@
     return [x]
 
 
-def start_order(count):
-    return sorted(range(1, count), key=lambda d: (d != count // 2, -d))
-
-
-def exchange(blocks, axis):
-    return [swap(blocks[d], axis, d) for d in start_order(len(blocks))] + [blocks[0]]
-
-
-def by_distance(came):
-    order = start_order(len(came)) + [0]
+def start_order(count, half_first):
+    return sorted(range(1, count), key=lambda d: (half_first and d != count // 2, -d))
+
+
+def exchange(blocks, axis, half_first=False):
+    return [swap(blocks[d], axis, d) for d in start_order(len(blocks), half_first)] + [blocks[0]]
+
+
+def by_distance(came, half_first=False):
+    order = start_order(len(came), half_first) + [0]
     return [came[order.index(d)] for d in range(len(came))]
 
 
@@ -322,7 +322,7 @@
     out_ref, joined = refs[-2:]
     half = joined.shape[1]
     rows = out_ref.shape[0] // count
-    for d, ref in enumerate(by_distance(refs[:count])):
+    for d, ref in enumerate(by_distance(refs[:count], half_first=True)):
         at = pl.ds(pl.multiple_of((lax.axis_index("narrow") ^ d) * PAD, PAD), PAD)
         joined[at, :] = ref[...].astype(jnp.float32)
     for side in range(2):
@@ -467,7 +467,7 @@
     returned = call(
         join_kernel,
         jax.ShapeDtypeStruct((narrow_count * own_rows, queries), jnp.bfloat16),
-        exchange(context, "narrow"),
+        exchange(context, "narrow", half_first=True),
         [FULL] * narrow_count,
         "join",
         scratch=[pltpu.VMEM((narrow_count * PAD, queries // 2), jnp.float32)],

time: 69.4 us -> 70.3 us (1.013)
  waiting for transfers between devices: 23.9 us -> 24.7 us
    ppermute x20, waiting for transfers between devices: 23.9 us -> 24.7 us  [swap(): return lax.ppermute(x, axis, [(i, i ^ distance) for i in range(count)])]
where the time goes in v17:
time: 70.3 us; the launch traced here: 70.1 us
  waiting for transfers between devices  24.7 us (35%)
  starting transfers between devices  22.5 us (32%)
  Pallas kernels  21.3 us (30%)
  other arithmetic  1.32 us (2%)
    ppermute x20, waiting for transfers between devices, swap(): return lax.ppermute(x, axis, [(i, i ^ distance) for i in range(count)])  24.7 us
    ppermute x20, starting transfers between devices, swap(): return lax.ppermute(x, axis, [(i, i ^ distance) for i in range(count)])  22.5 us
    pallas_call x12, Pallas kernels, call(): pl.pallas_call(kernel, out_shape=outs, in_specs=specs, out_specs=jax.tree...  19.1 us
    pallas_call x3, Pallas kernels, finish(): pl.pallas_call(functools.partial(finish_kernel, start), out_shape=pltpu.H...  2.15 us
  transfers between devices with their start and end apart: 20, of which 12 were waited for; matrix products, arithmetic and copies ran while one was open for 0% of the time, Pallas kernels for 11%

profile of v17, /device:TPU:0, one launch (start us, length us, event | category | flops | bytes accessed | tf_op | source)
XLA Modules:
  0.0 70.1 jit_solution(4276876358694935820)
XLA Ops:
  0.0 1.3 %convert_reduce_fusion = (f32[64]{0:T(128)S(1)}, f32[64]{0:T(128)S(1)}) fusion(bf16[64,4608]{1,0:T(8,128)(2,1)} %refs_4_.5), kind=kLoop, calls=%fused_computation.1 | loop fusion | flops 1179520 | bytes 590336 | tf_op jit(solution)/shard_map/reduce_sum | solution.py:440
  1.4 2.5 %collective-permute-start.2 = (f32[2,64]{1,0:T(2,128)S(1)}, f32[2,64]{1,0:T(2,128)S(1)}, u32[]{:S(2)}, u32[]{:S(2)}) collective-permute-start(f32[2,64]{1,0:T(2,128)S(1)} %pad_maximum_fusion.refs_0_), channel_id=1, source_target_pairs={{0,12},{4,8},{8,4},{12,0},{1,13},{5,9},{9,5},{13,1},{2,14},{6,10},... | collective-permute-start | bytes 1544 | tf_op jit(solution)/shard_map/ppermute | solution.py:48
  4.5 2.3 %fetch_query_weight.1.refs_8_ = bf16[768,3072]{1,0:T(8,128)(2,1)S(1)} custom-call(bf16[4608,3072]{1,0:T(8,128)(2,1)} %refs_6_.1, f32[2,64]{1,0:T(2,128)S(1)} %pad_maximum_fusion.refs_0_), custom_call_target="tpu_custom_call" | custom-call | bytes 4718592 | tf_op jit(solution)/shard_map/fetch_query_weight/pallas_call | solution.py:22
  7.4 8.6 %project.1 = (f32[32,3584]{1,0:T(8,128)S(1)}, f32[32,3584]{1,0:T(8,128)S(1)}) custom-call(f32[2,64]{1,0:T(2,128)S(1)} %pad_maximum_fusion.refs_0_, f32[2,64]{1,0:T(2,128)S(1)} %collective-permute-done.refs_1_, f32[2,64]{1,0:T(2,128)S(1)} %collective-permute-done.1.refs_2_, f32[2,64]{1,0:T(2,128)S(1)} %collective-permute-done.2.refs_3_, ...), custom_call_target="tpu_custom_call" | custom-call | flops 1811939328 | bytes 23592960 | tf_op jit(solution)/shard_map/project/pallas_call | solution.py:22
  16.2 1.8 %collective-permute-done.3.came_ref = f32[32,3584]{1,0:T(8,128)S(1)} collective-permute-done((f32[32,3584]{1,0:T(8,128)S(1)}, f32[32,3584]{1,0:T(8,128)S(1)}, u32[]{:S(2)}, u32[]{:S(2)}) %collective-permute-start.3) | collective-permute-done | bytes 458784 | tf_op jit(solution)/shard_map/ppermute | solution.py:48
  18.0 1.3 %collective-permute-start.4 = (f32[16,3584]{1,0:T(8,128)S(1)}, f32[16,3584]{1,0:T(8,128)S(1)}, u32[]{:S(2)}, u32[]{:S(2)}) collective-permute-start(f32[16,3584]{1,0:T(8,128)S(1)} %get-tuple-element.32), channel_id=1, source_target_pairs={{0,8},{4,12},{8,0},{12,4},{1,9},{5,13},{9,1},{13,5},{2,10},{6,14},... | collective-permute-start | bytes 688136 | tf_op jit(solution)/shard_map/ppermute | solution.py:48
  19.3 6.4 %collective-permute-done.4.came_ref = f32[16,3584]{1,0:T(8,128)S(1)} collective-permute-done((f32[16,3584]{1,0:T(8,128)S(1)}, f32[16,3584]{1,0:T(8,128)S(1)}, u32[]{:S(2)}, u32[]{:S(2)}) %collective-permute-start.4) | collective-permute-done | bytes 229408 | tf_op jit(solution)/shard_map/ppermute | solution.py:48
  25.8 3.7 %collective-permute-start.5 = (bf16[8,2048]{1,0:T(8,128)(2,1)S(1)}, bf16[8,2048]{1,0:T(8,128)(2,1)S(1)}, u32[]{:S(2)}, u32[]{:S(2)}) collective-permute-start(bf16[8,2048]{1,0:T(8,128)(2,1)S(1)} %get-tuple-element.33), channel_id=1, source_target_pairs={{0,3},{1,2},{2,1},{3,0},{4,7},{5,6},{6,5},{7,4},{8,11},{9,10},{10,... | collective-permute-start | bytes 98312 | tf_op jit(solution)/shard_map/ppermute | solution.py:48
  29.5 0.8 %collective-permute-start.7 = (bf16[8,2048]{1,0:T(8,128)(2,1)S(1)}, bf16[8,2048]{1,0:T(8,128)(2,1)S(1)}, u32[]{:S(2)}, u32[]{:S(2)}) collective-permute-start(bf16[8,2048]{1,0:T(8,128)(2,1)S(1)} %get-tuple-element.35), channel_id=1, source_target_pairs={{0,1},{1,0},{2,3},{3,2},{4,5},{5,4},{6,7},{7,6},{8,9},{9,8},{10,11... | collective-permute-start | bytes 98312 | tf_op jit(solution)/shard_map/ppermute | solution.py:48
  30.3 1.5 %collective-permute-done.5.refs_0_ = bf16[8,2048]{1,0:T(8,128)(2,1)S(1)} collective-permute-done((bf16[8,2048]{1,0:T(8,128)(2,1)S(1)}, bf16[8,2048]{1,0:T(8,128)(2,1)S(1)}, u32[]{:S(2)}, u32[]{:S(2)}) %collective-permute-start.5) | collective-permute-done | bytes 32800 | tf_op jit(solution)/shard_map/ppermute | solution.py:48
  31.8 2.5 %collective-permute-done.6.refs_1_ = bf16[8,2048]{1,0:T(8,128)(2,1)S(1)} collective-permute-done((bf16[8,2048]{1,0:T(8,128)(2,1)S(1)}, bf16[8,2048]{1,0:T(8,128)(2,1)S(1)}, u32[]{:S(2)}, u32[]{:S(2)}) %collective-permute-start.6) | collective-permute-done | bytes 32800 | tf_op jit(solution)/shard_map/ppermute | solution.py:48
  34.3 1.9 %attend.1 = (bf16[8,1536]{1,0:T(8,128)(2,1)S(1)}, bf16[8,1536]{1,0:T(8,128)(2,1)S(1)}, bf16[8,1536]{1,0:T(8,128)(2,1)S(1)}, bf16[8,1536]{1,0:T(8,128)(2,1)S(1)}) custom-call(s32[1,4]{1,0:T(1,128)S(1)} %bitcast.5, bf16[8,2048]{1,0:T(8,128)(2,1)S(1)} %collective-permute-done.5.refs_0_, bf16[8,2048]{1,0:T(8,128)(2,1)S(1)} %collective-permute-done.6.refs_1_, ...), custom_call_target="tpu_custom_call" | custom-call | flops 5000000000 | tf_op jit(solution)/shard_map/attend/pallas_call | solution.py:22
  36.2 2.1 %collective-permute-start.8 = (bf16[8,1536]{1,0:T(8,128)(2,1)S(1)}, bf16[8,1536]{1,0:T(8,128)(2,1)S(1)}, u32[]{:S(2)}, u32[]{:S(2)}) collective-permute-start(bf16[8,1536]{1,0:T(8,128)(2,1)S(1)} %get-tuple-element.37), channel_id=1, source_target_pairs={{0,2},{1,3},{2,0},{3,1},{4,6},{5,7},{6,4},{7,5},{8,10},{9,11},{10,... | collective-permute-start | bytes 73736 | tf_op jit(solution)/shard_map/ppermute | solution.py:48
  38.5 1.3 %collective-permute-start.10 = (bf16[8,1536]{1,0:T(8,128)(2,1)S(1)}, bf16[8,1536]{1,0:T(8,128)(2,1)S(1)}, u32[]{:S(2)}, u32[]{:S(2)}) collective-permute-start(bf16[8,1536]{1,0:T(8,128)(2,1)S(1)} %get-tuple-element.39), channel_id=1, source_target_pairs={{0,1},{1,0},{2,3},{3,2},{4,5},{5,4},{6,7},{7,6},{8,9},{9,8},{10,11... | collective-permute-start | bytes 73736 | tf_op jit(solution)/shard_map/ppermute | solution.py:48
  39.8 1.2 %collective-permute-done.8.refs_0_ = bf16[8,1536]{1,0:T(8,128)(2,1)S(1)} collective-permute-done((bf16[8,1536]{1,0:T(8,128)(2,1)S(1)}, bf16[8,1536]{1,0:T(8,128)(2,1)S(1)}, u32[]{:S(2)}, u32[]{:S(2)}) %collective-permute-start.8) | collective-permute-done | bytes 24608 | tf_op jit(solution)/shard_map/ppermute | solution.py:48
  41.0 2.9 %collective-permute-done.9.refs_1_ = bf16[8,1536]{1,0:T(8,128)(2,1)S(1)} collective-permute-done((bf16[8,1536]{1,0:T(8,128)(2,1)S(1)}, bf16[8,1536]{1,0:T(8,128)(2,1)S(1)}, u32[]{:S(2)}, u32[]{:S(2)}) %collective-permute-start.9) | collective-permute-done | bytes 24608 | tf_op jit(solution)/shard_map/ppermute | solution.py:48
  44.0 1.3 %collective-permute-start.12 = (bf16[16,3072]{1,0:T(8,128)(2,1)S(1)}, bf16[16,3072]{1,0:T(8,128)(2,1)S(1)}, u32[]{:S(2)}, u32[]{:S(2)}) collective-permute-start(bf16[16,3072]{1,0:T(8,128)(2,1)S(1)} %join.1.refs_0_), channel_id=1, source_target_pairs={{0,8},{4,12},{8,0},{12,4},{1,9},{5,13},{9,1},{13,5},{2,10},{6,14},... | collective-permute-start | bytes 294920 | tf_op jit(solution)/shard_map/ppermute | solution.py:48
  45.3 3.4 %collective-permute-done.12.refs_2_ = bf16[16,3072]{1,0:T(8,128)(2,1)S(1)} collective-permute-done((bf16[16,3072]{1,0:T(8,128)(2,1)S(1)}, bf16[16,3072]{1,0:T(8,128)(2,1)S(1)}, u32[]{:S(2)}, u32[]{:S(2)}) %collective-permute-start.12) | collective-permute-done | bytes 98336 | tf_op jit(solution)/shard_map/ppermute | solution.py:48
  48.7 1.3 %collective-permute-done.13.refs_3_ = bf16[16,3072]{1,0:T(8,128)(2,1)S(1)} collective-permute-done((bf16[16,3072]{1,0:T(8,128)(2,1)S(1)}, bf16[16,3072]{1,0:T(8,128)(2,1)S(1)}, u32[]{:S(2)}, u32[]{:S(2)}) %collective-permute-start.13) | collective-permute-done | bytes 98336 | tf_op jit(solution)/shard_map/ppermute | solution.py:48
  50.0 2.1 %output_part.3 = (f32[64,1792]{1,0:T(8,128)S(1)}, s16[32,1920]{1,0:T(8,128)(2,1)S(1)}) custom-call(bf16[16,3072]{1,0:T(8,128)(2,1)S(1)} %join.1.refs_0_, bf16[16,3072]{1,0:T(8,128)(2,1)S(1)} %collective-permute-done.11.refs_1_, bf16[16,3072]{1,0:T(8,128)(2,1)S(1)} %collective-permute-done.12.refs_2_, bf16[16,3072]{1,0:T(8,128)(2,1)S(1)} %collective-permute-done.13.refs_3_, ...), custom_call_target="tpu_custom_call" | custom-call | flops 704643072 | bytes 393216 | tf_op jit(solution)/shard_map/output_part/pallas_call | solution.py:22
  52.2 2.4 %output_part.4 = (f32[64,2048]{1,0:T(8,128)S(1)}, s16[32,2176]{1,0:T(8,128)(2,1)S(1)}) custom-call(bf16[16,3072]{1,0:T(8,128)(2,1)S(1)} %join.1.refs_0_, bf16[16,3072]{1,0:T(8,128)(2,1)S(1)} %collective-permute-done.11.refs_1_, bf16[16,3072]{1,0:T(8,128)(2,1)S(1)} %collective-permute-done.12.refs_2_, bf16[16,3072]{1,0:T(8,128)(2,1)S(1)} %collective-permute-done.13.refs_3_, ...), custom_call_target="tpu_custom_call" | custom-call | flops 805306368 | bytes 393216 | tf_op jit(solution)/shard_map/output_part/pallas_call | solution.py:22
  54.6 2.1 %collective-permute-start.18 = (s16[32,2176]{1,0:T(8,128)(2,1)S(1)}, s16[32,2176]{1,0:T(8,128)(2,1)S(1)}, u32[]{:S(2)}, u32[]{:S(2)}) collective-permute-start(s16[32,2176]{1,0:T(8,128)(2,1)S(1)} %get-tuple-element.50), channel_id=1, source_target_pairs={{0,1},{1,0},{2,3},{3,2},{4,5},{5,4},{6,7},{7,6},{8,9},{9,8},{10,11... | collective-permute-start | bytes 417800 | tf_op jit(solution)/shard_map/ppermute | solution.py:48
  56.7 1.0 %collective-permute-done.14.came_ref = s16[32,1920]{1,0:T(8,128)(2,1)S(1)} collective-permute-done((s16[32,1920]{1,0:T(8,128)(2,1)S(1)}, s16[32,1920]{1,0:T(8,128)(2,1)S(1)}, u32[]{:S(2)}, u32[]{:S(2)}) %collective-permute-start.14) | collective-permute-done | bytes 122912 | tf_op jit(solution)/shard_map/ppermute | solution.py:48
  57.9 0.8 %collective-permute-start.16 = (s16[16,1920]{1,0:T(8,128)(2,1)S(1)}, s16[16,1920]{1,0:T(8,128)(2,1)S(1)}, u32[]{:S(2)}, u32[]{:S(2)}) collective-permute-start(s16[16,1920]{1,0:T(8,128)(2,1)S(1)} %get-tuple-element.47), channel_id=1, source_target_pairs={{0,2},{1,3},{2,0},{3,1},{4,6},{5,7},{6,4},{7,5},{8,10},{9,11},{10,... | collective-permute-start | bytes 184328 | tf_op jit(solution)/shard_map/ppermute | solution.py:48
  58.7 1.0 %output_part.5 = (f32[64,768]{1,0:T(8,128)S(1)}, s16[32,896]{1,0:T(8,128)(2,1)S(1)}) custom-call(bf16[16,3072]{1,0:T(8,128)(2,1)S(1)} %join.1.refs_0_, bf16[16,3072]{1,0:T(8,128)(2,1)S(1)} %collective-permute-done.11.refs_1_, bf16[16,3072]{1,0:T(8,128)(2,1)S(1)} %collective-permute-done.12.refs_2_, bf16[16,3072]{1,0:T(8,128)(2,1)S(1)} %collective-permute-done.13.refs_3_, ...), custom_call_target="tpu_custom_call" | custom-call | flops 301989888 | bytes 393216 | tf_op jit(solution)/shard_map/output_part/pallas_call | solution.py:22
  59.7 1.9 %collective-permute-start.15 = (s16[32,896]{1,0:T(8,128)(2,1)S(1)}, s16[32,896]{1,0:T(8,128)(2,1)S(1)}, u32[]{:S(2)}, u32[]{:S(2)}) collective-permute-start(s16[32,896]{1,0:T(8,128)(2,1)S(1)} %get-tuple-element.46), channel_id=1, source_target_pairs={{0,1},{1,0},{2,3},{3,2},{4,5},{5,4},{6,7},{7,6},{8,9},{9,8},{10,11... | collective-permute-start | bytes 172040 | tf_op jit(solution)/shard_map/ppermute | solution.py:48
  61.8 1.8 %collective-permute-start.19 = (s16[16,2176]{1,0:T(8,128)(2,1)S(1)}, s16[16,2176]{1,0:T(8,128)(2,1)S(1)}, u32[]{:S(2)}, u32[]{:S(2)}) collective-permute-start(s16[16,2176]{1,0:T(8,128)(2,1)S(1)} %get-tuple-element.52), channel_id=1, source_target_pairs={{0,2},{1,3},{2,0},{3,1},{4,6},{5,7},{6,4},{7,5},{8,10},{9,11},{10,... | collective-permute-start | bytes 208904 | tf_op jit(solution)/shard_map/ppermute | solution.py:48
  63.6 0.7 %finish.3.refs_0_ = bf16[16,4608]{1,0:T(8,128)(2,1)} custom-call(f32[16,1792]{1,0:T(8,128)S(1)} %get-tuple-element.44.refs_5_.kept_ref, s16[16,1920]{1,0:T(8,128)(2,1)S(1)} %collective-permute-done.16.came_ref), custom_call_target="tpu_custom_call" | custom-call | bytes 229376 | tf_op jit(solution)/shard_map/finish/pallas_call | solution.py:418
  64.6 2.0 %collective-permute-start.17 = (s16[16,896]{1,0:T(8,128)(2,1)S(1)}, s16[16,896]{1,0:T(8,128)(2,1)S(1)}, u32[]{:S(2)}, u32[]{:S(2)}) collective-permute-start(s16[16,896]{1,0:T(8,128)(2,1)S(1)} %get-tuple-element.49), channel_id=1, source_target_pairs={{0,2},{1,3},{2,0},{3,1},{4,6},{5,7},{6,4},{7,5},{8,10},{9,11},{10,... | collective-permute-start | bytes 86024 | tf_op jit(solution)/shard_map/ppermute | solution.py:48
  66.5 1.8 %collective-permute-done.19.came_ref = s16[16,2176]{1,0:T(8,128)(2,1)S(1)} collective-permute-done((s16[16,2176]{1,0:T(8,128)(2,1)S(1)}, s16[16,2176]{1,0:T(8,128)(2,1)S(1)}, u32[]{:S(2)}, u32[]{:S(2)}) %collective-permute-start.19) | collective-permute-done | bytes 69664 | tf_op jit(solution)/shard_map/ppermute | solution.py:48
  68.3 0.7 %finish.4.refs_0_ = bf16[16,4608]{1,0:T(8,128)(2,1)} custom-call(f32[16,2048]{1,0:T(8,128)S(1)} %get-tuple-element.51.kept_ref, s16[16,2176]{1,0:T(8,128)(2,1)S(1)} %collective-permute-done.19.came_ref, bf16[16,4608]{1,0:T(8,128)(2,1)} %finish.3.refs_0_), custom_call_target="tpu_custom_call", output_to_operand_aliasing={{}: (2, {})} | custom-call | bytes 262144 | tf_op jit(solution)/shard_map/finish/pallas_call | solution.py:418
  69.4 0.7 finish.5
  (50 shorter events, 2.8 us)
Async XLA Ops:
  1.3 6.1 %copy-start = (bf16[64,4608]{1,0:T(8,128)(2,1)S(1)}, bf16[64,4608]{1,0:T(8,128)(2,1)}, u32[]{:S(2)}) copy-start(bf16[64,4608]{1,0:T(8,128)(2,1)} %refs_4_.5) | copy-start | bytes 1769476
  1.3 6.1 %copy-start.1 = (bf16[1152,512]{1,0:T(8,128)(2,1)S(1)}, bf16[1152,512]{1,0:T(8,128)(2,1)}, u32[]{:S(2)}) copy-start(bf16[1152,512]{1,0:T(8,128)(2,1)} %refs_7_.1) | copy-start | bytes 3538948
  1.4 6.1 %copy-start.2 = (f32[4608]{0:T(1024)S(1)}, f32[4608]{0:T(1024)}, u32[]{:S(2)}) copy-start(f32[4608]{0:T(1024)} %refs_5_.1) | copy-start | bytes 55300
  1.4 5.5 %collective-permute-start.2 = (f32[2,64]{1,0:T(2,128)S(1)}, f32[2,64]{1,0:T(2,128)S(1)}, u32[]{:S(2)}, u32[]{:S(2)}) collective-permute-start(f32[2,64]{1,0:T(2,128)S(1)} %pad_maximum_fusion.refs_0_), channel_id=1, source_target_pairs={{0,12},{4,8},{8,4},{12,0},{1,13},{5,9},{9,5},{13,1},{2,14},{6,10},... | collective-permute-start | bytes 1544 | tf_op jit(solution)/shard_map/ppermute | solution.py:48
  3.8 3.6 %collective-permute-start.1 = (f32[2,64]{1,0:T(2,128)S(1)}, f32[2,64]{1,0:T(2,128)S(1)}, u32[]{:S(2)}, u32[]{:S(2)}) collective-permute-start(f32[2,64]{1,0:T(2,128)S(1)} %pad_maximum_fusion.refs_0_), channel_id=1, source_target_pairs={{0,8},{4,12},{8,0},{12,4},{1,9},{5,13},{9,1},{13,5},{2,10},{6,14},... | collective-permute-start | bytes 1544 | tf_op jit(solution)/shard_map/ppermute | solution.py:48
  4.5 2.9 %collective-permute-start = (f32[2,64]{1,0:T(2,128)S(1)}, f32[2,64]{1,0:T(2,128)S(1)}, u32[]{:S(2)}, u32[]{:S(2)}) collective-permute-start(f32[2,64]{1,0:T(2,128)S(1)} %pad_maximum_fusion.refs_0_), channel_id=1, source_target_pairs={{0,4},{4,0},{8,12},{12,8},{1,5},{5,1},{9,13},{13,9},{2,6},{6,2},{1... | collective-permute-start | bytes 1544 | tf_op jit(solution)/shard_map/ppermute | solution.py:48
  16.1 1.9 %collective-permute-start.3 = (f32[32,3584]{1,0:T(8,128)S(1)}, f32[32,3584]{1,0:T(8,128)S(1)}, u32[]{:S(2)}, u32[]{:S(2)}) collective-permute-start(f32[32,3584]{1,0:T(8,128)S(1)} %get-tuple-element.30), channel_id=1, source_target_pairs={{0,4},{4,0},{8,12},{12,8},{1,5},{5,1},{9,13},{13,9},{2,6},{6,2},{1... | collective-permute-start | bytes 1376264 | tf_op jit(solution)/shard_map/ppermute | solution.py:48
  18.0 7.7 %collective-permute-start.4 = (f32[16,3584]{1,0:T(8,128)S(1)}, f32[16,3584]{1,0:T(8,128)S(1)}, u32[]{:S(2)}, u32[]{:S(2)}) collective-permute-start(f32[16,3584]{1,0:T(8,128)S(1)} %get-tuple-element.32), channel_id=1, source_target_pairs={{0,8},{4,12},{8,0},{12,4},{1,9},{5,13},{9,1},{13,5},{2,10},{6,14},... | collective-permute-start | bytes 688136 | tf_op jit(solution)/shard_map/ppermute | solution.py:48
  25.7 8.6 %copy-start.3 = (bf16[4,1024,512]{2,1,0:T(8,128)(2,1)S(1)}, bf16[4,1024,512]{2,1,0:T(8,128)(2,1)}, u32[]{:S(2)}) copy-start(bf16[4,1024,512]{2,1,0:T(8,128)(2,1)} %refs_4_.6) | copy-start | bytes 12582916
  25.7 8.6 %copy-start.4 = (s32[4]{0:T(128)S(1)}, s32[4]{0:T(128)}, u32[]{:S(2)}) copy-start(s32[4]{0:T(128)} %param.13) | copy-start | bytes 52
  25.7 24.2 %slice-start = ((s8[28311552]{0:T(1024)(128)(4,1)}), s8[4194304]{0:T(1024)(128)(4,1)S(1)}, s32[]{:S(2)}) async-start(s8[28311552]{0:T(1024)(128)(4,1)} %bitcast.3), calls=%async_computation | async-start | bytes 8388608
  25.7 24.2 %slice-start.1 = ((s8[28311552]{0:T(1024)(128)(4,1)}), s8[4194304]{0:T(1024)(128)(4,1)S(1)}, s32[]{:S(2)}) async-start(s8[28311552]{0:T(1024)(128)(4,1)} %bitcast.3), calls=%async_computation.1 | async-start | bytes 8388608
  25.7 24.2 %slice-start.2 = ((s8[28311552]{0:T(1024)(128)(4,1)}), s8[4194304]{0:T(1024)(128)(4,1)S(1)}, s32[]{:S(2)}) async-start(s8[28311552]{0:T(1024)(128)(4,1)} %bitcast.3), calls=%async_computation.2 | async-start | bytes 8388608
  25.8 6.0 %collective-permute-start.5 = (bf16[8,2048]{1,0:T(8,128)(2,1)S(1)}, bf16[8,2048]{1,0:T(8,128)(2,1)S(1)}, u32[]{:S(2)}, u32[]{:S(2)}) collective-permute-start(bf16[8,2048]{1,0:T(8,128)(2,1)S(1)} %get-tuple-element.33), channel_id=1, source_target_pairs={{0,3},{1,2},{2,1},{3,0},{4,7},{5,6},{6,5},{7,4},{8,11},{9,10},{10,... | collective-permute-start | bytes 98312 | tf_op jit(solution)/shard_map/ppermute | solution.py:48
  29.5 4.8 %collective-permute-start.6 = (bf16[8,2048]{1,0:T(8,128)(2,1)S(1)}, bf16[8,2048]{1,0:T(8,128)(2,1)S(1)}, u32[]{:S(2)}, u32[]{:S(2)}) collective-permute-start(bf16[8,2048]{1,0:T(8,128)(2,1)S(1)} %get-tuple-element.34), channel_id=1, source_target_pairs={{0,2},{1,3},{2,0},{3,1},{4,6},{5,7},{6,4},{7,5},{8,10},{9,11},{10,... | collective-permute-start | bytes 98312 | tf_op jit(solution)/shard_map/ppermute | solution.py:48
  29.5 4.8 %collective-permute-start.7 = (bf16[8,2048]{1,0:T(8,128)(2,1)S(1)}, bf16[8,2048]{1,0:T(8,128)(2,1)S(1)}, u32[]{:S(2)}, u32[]{:S(2)}) collective-permute-start(bf16[8,2048]{1,0:T(8,128)(2,1)S(1)} %get-tuple-element.35), channel_id=1, source_target_pairs={{0,1},{1,0},{2,3},{3,2},{4,5},{5,4},{6,7},{7,6},{8,9},{9,8},{10,11... | collective-permute-start | bytes 98312 | tf_op jit(solution)/shard_map/ppermute | solution.py:48
  34.3 15.7 %slice-start.3 = ((s8[28311552]{0:T(1024)(128)(4,1)}), s8[4194304]{0:T(1024)(128)(4,1)S(1)}, s32[]{:S(2)}) async-start(s8[28311552]{0:T(1024)(128)(4,1)} %bitcast.3), calls=%async_computation.3 | async-start | bytes 8388608
  34.3 15.7 %slice-start.4 = ((s8[28311552]{0:T(1024)(128)(4,1)}), s8[4194304]{0:T(1024)(128)(4,1)S(1)}, s32[]{:S(2)}) async-start(s8[28311552]{0:T(1024)(128)(4,1)} %bitcast.3), calls=%async_computation.4 | async-start | bytes 8388608
  36.2 4.8 %collective-permute-start.8 = (bf16[8,1536]{1,0:T(8,128)(2,1)S(1)}, bf16[8,1536]{1,0:T(8,128)(2,1)S(1)}, u32[]{:S(2)}, u32[]{:S(2)}) collective-permute-start(bf16[8,1536]{1,0:T(8,128)(2,1)S(1)} %get-tuple-element.37), channel_id=1, source_target_pairs={{0,2},{1,3},{2,0},{3,1},{4,6},{5,7},{6,4},{7,5},{8,10},{9,11},{10,... | collective-permute-start | bytes 73736 | tf_op jit(solution)/shard_map/ppermute | solution.py:48
  38.3 5.6 %collective-permute-start.9 = (bf16[8,1536]{1,0:T(8,128)(2,1)S(1)}, bf16[8,1536]{1,0:T(8,128)(2,1)S(1)}, u32[]{:S(2)}, u32[]{:S(2)}) collective-permute-start(bf16[8,1536]{1,0:T(8,128)(2,1)S(1)} %get-tuple-element.38), channel_id=1, source_target_pairs={{0,3},{1,2},{2,1},{3,0},{4,7},{5,6},{6,5},{7,4},{8,11},{9,10},{10,... | collective-permute-start | bytes 73736 | tf_op jit(solution)/shard_map/ppermute | solution.py:48
  38.5 5.4 %collective-permute-start.10 = (bf16[8,1536]{1,0:T(8,128)(2,1)S(1)}, bf16[8,1536]{1,0:T(8,128)(2,1)S(1)}, u32[]{:S(2)}, u32[]{:S(2)}) collective-permute-start(bf16[8,1536]{1,0:T(8,128)(2,1)S(1)} %get-tuple-element.39), channel_id=1, source_target_pairs={{0,1},{1,0},{2,3},{3,2},{4,5},{5,4},{6,7},{7,6},{8,9},{9,8},{10,11... | collective-permute-start | bytes 73736 | tf_op jit(solution)/shard_map/ppermute | solution.py:48
  43.9 6.1 %slice-start.5 = ((s8[28311552]{0:T(1024)(128)(4,1)}), s8[4194304]{0:T(1024)(128)(4,1)S(1)}, s32[]{:S(2)}) async-start(s8[28311552]{0:T(1024)(128)(4,1)} %bitcast.3), calls=%async_computation.5 | async-start | bytes 8388608
  43.9 6.1 %slice-start.6 = ((s8[28311552]{0:T(1024)(128)(4,1)}), s8[3145728]{0:T(1024)(128)(4,1)S(1)}, s32[]{:S(2)}) async-start(s8[28311552]{0:T(1024)(128)(4,1)} %bitcast.3), calls=%async_computation.6 | async-start | bytes 6291456
  44.0 4.7 %collective-permute-start.12 = (bf16[16,3072]{1,0:T(8,128)(2,1)S(1)}, bf16[16,3072]{1,0:T(8,128)(2,1)S(1)}, u32[]{:S(2)}, u32[]{:S(2)}) collective-permute-start(bf16[16,3072]{1,0:T(8,128)(2,1)S(1)} %join.1.refs_0_), channel_id=1, source_target_pairs={{0,8},{4,12},{8,0},{12,4},{1,9},{5,13},{9,1},{13,5},{2,10},{6,14},... | collective-permute-start | bytes 294920 | tf_op jit(solution)/shard_map/ppermute | solution.py:48
  45.3 3.4 %collective-permute-start.11 = (bf16[16,3072]{1,0:T(8,128)(2,1)S(1)}, bf16[16,3072]{1,0:T(8,128)(2,1)S(1)}, u32[]{:S(2)}, u32[]{:S(2)}) collective-permute-start(bf16[16,3072]{1,0:T(8,128)(2,1)S(1)} %join.1.refs_0_), channel_id=1, source_target_pairs={{0,4},{4,0},{8,12},{12,8},{1,5},{5,1},{9,13},{13,9},{2,6},{6,2},{1... | collective-permute-start | bytes 294920 | tf_op jit(solution)/shard_map/ppermute | solution.py:48
  48.6 1.3 %collective-permute-start.13 = (bf16[16,3072]{1,0:T(8,128)(2,1)S(1)}, bf16[16,3072]{1,0:T(8,128)(2,1)S(1)}, u32[]{:S(2)}, u32[]{:S(2)}) collective-permute-start(bf16[16,3072]{1,0:T(8,128)(2,1)S(1)} %collective-permute-done.12.refs_2_), channel_id=1, source_target_pairs={{0,4},{4,0},{8,12},{12,8},{1,5},{5,1},{9,13},{13,9},{2,6},{6,2},{1... | collective-permute-start | bytes 294920 | tf_op jit(solution)/shard_map/ppermute | solution.py:48
  52.2 5.5 %collective-permute-start.14 = (s16[32,1920]{1,0:T(8,128)(2,1)S(1)}, s16[32,1920]{1,0:T(8,128)(2,1)S(1)}, u32[]{:S(2)}, u32[]{:S(2)}) collective-permute-start(s16[32,1920]{1,0:T(8,128)(2,1)S(1)} %get-tuple-element.42), channel_id=1, source_target_pairs={{0,1},{1,0},{2,3},{3,2},{4,5},{5,4},{6,7},{7,6},{8,9},{9,8},{10,11... | collective-permute-start | bytes 368648 | tf_op jit(solution)/shard_map/ppermute | solution.py:48
  54.6 7.0 %collective-permute-start.18 = (s16[32,2176]{1,0:T(8,128)(2,1)S(1)}, s16[32,2176]{1,0:T(8,128)(2,1)S(1)}, u32[]{:S(2)}, u32[]{:S(2)}) collective-permute-start(s16[32,2176]{1,0:T(8,128)(2,1)S(1)} %get-tuple-element.50), channel_id=1, source_target_pairs={{0,1},{1,0},{2,3},{3,2},{4,5},{5,4},{6,7},{7,6},{8,9},{9,8},{10,11... | collective-permute-start | bytes 417800 | tf_op jit(solution)/shard_map/ppermute | solution.py:48
  57.9 5.8 %collective-permute-start.16 = (s16[16,1920]{1,0:T(8,128)(2,1)S(1)}, s16[16,1920]{1,0:T(8,128)(2,1)S(1)}, u32[]{:S(2)}, u32[]{:S(2)}) collective-permute-start(s16[16,1920]{1,0:T(8,128)(2,1)S(1)} %get-tuple-element.47), channel_id=1, source_target_pairs={{0,2},{1,3},{2,0},{3,1},{4,6},{5,7},{6,4},{7,5},{8,10},{9,11},{10,... | collective-permute-start | bytes 184328 | tf_op jit(solution)/shard_map/ppermute | solution.py:48
  59.7 4.6 %collective-permute-start.15 = (s16[32,896]{1,0:T(8,128)(2,1)S(1)}, s16[32,896]{1,0:T(8,128)(2,1)S(1)}, u32[]{:S(2)}, u32[]{:S(2)}) collective-permute-start(s16[32,896]{1,0:T(8,128)(2,1)S(1)} %get-tuple-element.46), channel_id=1, source_target_pairs={{0,1},{1,0},{2,3},{3,2},{4,5},{5,4},{6,7},{7,6},{8,9},{9,8},{10,11... | collective-permute-start | bytes 172040 | tf_op jit(solution)/shard_map/ppermute | solution.py:48
  61.8 6.5 %collective-permute-start.19 = (s16[16,2176]{1,0:T(8,128)(2,1)S(1)}, s16[16,2176]{1,0:T(8,128)(2,1)S(1)}, u32[]{:S(2)}, u32[]{:S(2)}) collective-permute-start(s16[16,2176]{1,0:T(8,128)(2,1)S(1)} %get-tuple-element.52), channel_id=1, source_target_pairs={{0,2},{1,3},{2,0},{3,1},{4,6},{5,7},{6,4},{7,5},{8,10},{9,11},{10,... | collective-permute-start | bytes 208904 | tf_op jit(solution)/shard_map/ppermute | solution.py:48
  64.6 4.8 %collective-permute-start.17 = (s16[16,896]{1,0:T(8,128)(2,1)S(1)}, s16[16,896]{1,0:T(8,128)(2,1)S(1)}, u32[]{:S(2)}, u32[]{:S(2)}) collective-permute-start(s16[16,896]{1,0:T(8,128)(2,1)S(1)} %get-tuple-element.49), channel_id=1, source_target_pairs={{0,2},{1,3},{2,0},{3,1},{4,6},{5,7},{6,4},{7,5},{8,10},{9,11},{10,... | collective-permute-start | bytes 86024 | tf_op jit(solution)/shard_map/ppermute | solution.py:48

commit v18 on v16

--- a/solution.py
+++ b/solution.py
@@ -117,9 +117,10 @@
     return [LANES * n for n in blocks]
 
 
-def project_kernel(many, width_all, count, narrow_count, *refs):
+def project_kernel(many, streamed, width_all, count, narrow_count, *refs):
     stat_refs, refs = refs[:many], refs[many:]
-    x_ref, gain_ref, w_ref, kv_ref, first_ref, kept_ref, sent_ref, normed, own, *blocks, sems = refs
+    x_ref, gain_ref, w_ref, kv_ref, first_ref, *sum_refs, normed, own = refs[: len(refs) - 1 - streamed]
+    blocks, sems = refs[len(refs) - 1 - streamed : -1], refs[-1]
     rows, width = x_ref.shape
     half = rows // 2
     block = rows // count
@@ -160,19 +161,20 @@
             own[...] = normed[:, j * sub_width : (j + 1) * sub_width]
 
     queries = w_ref.shape[1]
+    cut = queries // 2
 
     def products(source, start):
         got = jnp.dot(normed[:, start : start + source.shape[0]], source[...], preferred_element_type=jnp.float32)
-        if start:
-            kept_ref[:, :queries] += got[:half, :]
-            sent_ref[:, :queries] += got[half:, :]
-        else:
-            kept_ref[:, :queries] = got[:half, :]
-            sent_ref[:, :queries] = got[half:, :]
+        for ref, side, columns in zip(sum_refs, (0, 0, 1, 1), (slice(0, cut), slice(cut, queries)) * 2):
+            part = got[side * half : (side + 1) * half, columns]
+            if start:
+                ref[:, :cut] += part
+            else:
+                ref[:, :cut] = part
 
     fresh = jnp.dot(own[...], kv_ref[...], preferred_element_type=jnp.float32)
-    kept_ref[:, queries:] = fresh[:half, :]
-    sent_ref[:, queries:] = fresh[half:, :]
+    sum_refs[0][:, cut:] = fresh[:half, :]
+    sum_refs[2][:, cut:] = fresh[half:, :]
     products(first_ref, 0)
     for g, fetch in enumerate(fetches):
         fetch.wait()
@@ -185,10 +187,10 @@
     rows, width = x.shape
     queries = w.shape[1]
     blocks = row_blocks(width)[1:]
-    half = jax.ShapeDtypeStruct((rows // 2, queries + kv.shape[1]), jnp.float32)
+    halves = [jax.ShapeDtypeStruct((rows // 2, queries // 2 + n), jnp.float32) for n in (kv.shape[1], 0)]
     return call(
-        functools.partial(project_kernel, len(stats), width_all, count, narrow_count),
-        (half, half),
+        functools.partial(project_kernel, len(stats), len(blocks), width_all, count, narrow_count),
+        halves * 2,
         (*stats, x, gain, in_hbm(w), in_vmem(kv), in_vmem(first)),
         [FULL] * (len(stats) + 2) + [ANY] + [FULL] * 2,
         "project",
@@ -204,29 +206,32 @@
     )
 
 
-def fold_kernel(kept_ref, came_ref, still_ref, sent_ref):
+def fold_kernel(kept_ref, came_ref, *refs):
+    still_ref, sent_ref = refs[-2:]
     half = still_ref.shape[0]
     still_ref[...] = kept_ref[:half, :] + came_ref[:half, :]
     sent_ref[...] = kept_ref[half:, :] + came_ref[half:, :]
 
 
-def fold(kept, came):
+def fold(kept, came, after):
     half = jax.ShapeDtypeStruct((kept.shape[0] // 2, kept.shape[1]), jnp.float32)
     return call(
         fold_kernel,
         (half, half),
-        (kept, came),
-        [FULL] * 2,
+        (kept, came, *after),
+        [FULL] * 2 + [ANY] * len(after),
         "fold",
         flops=BESIDE,
     )
 
 
-def split_kernel(queries, kept_ref, came_ref, *refs):
+def split_kernel(queries, kept_ref, came_ref, kept_2_ref, came_2_ref, *refs):
     out_refs, slots = refs[:-1], refs[-1]
     count = len(out_refs)
     narrow = lax.axis_index("narrow")
-    total = kept_ref[...] + came_ref[...]
+    first, second = kept_ref[...] + came_ref[...], kept_2_ref[...] + came_2_ref[...]
+    cut = second.shape[1]
+    total = jnp.concatenate([first[:, :cut], second, first[:, cut:]], axis=1)
     rows, columns = total.shape[0] // count, total.shape[1]
     half = slots.shape[1]
     fresh = total[:, queries:]
@@ -439,7 +444,7 @@
     values = activations.astype(jnp.float32)
     stats = jnp.stack([jnp.sum(values, axis=1), jnp.sum(values * values, axis=1)])
     first_part = fetch(query_weight, row_blocks(width)[0], [stats])
-    kept, sent = project(
+    kept, kept_2, sent, sent_2 = project(
         sent_apart(stats, "wide"),
         activations,
         norm_gain,
@@ -452,13 +457,14 @@
     )
     d = 1
     while 2 * d < wide_count:
-        kept, sent = fold(kept, swap(sent, "wide", d))
+        kept, sent = fold(kept, swap(sent, "wide", d), [])
+        kept_2, sent_2 = fold(kept_2, swap(sent_2, "wide", d), [kept])
         d *= 2
     split = call(
         functools.partial(split_kernel, queries),
         [jax.ShapeDtypeStruct((PAD, queries // 2 + 2 * head_dim), jnp.bfloat16)] * narrow_count,
-        (kept, swap(sent, "wide", d)),
-        [FULL] * 2,
+        (kept, swap(sent, "wide", d), kept_2, swap(sent_2, "wide", d)),
+        [FULL] * 4,
         "split",
         scratch=[pltpu.VMEM((narrow_count * PAD, queries // 2 + 2 * head_dim), jnp.float32)],
         flops=BESIDE,

time: 69.4 us -> 69.1 us (level)
  waiting for transfers between devices: 23.9 us -> 22.3 us
  starting transfers between devices: 22.4 us -> 23.7 us
    ppermute x20 -> x22, waiting for transfers between devices: 23.9 us -> 22.3 us  [swap(): return lax.ppermute(x, axis, [(i, i ^ distance) for i in range(count)])]
    ppermute x20 -> x22, starting transfers between devices: 22.4 us -> 23.7 us  [swap(): return lax.ppermute(x, axis, [(i, i ^ distance) for i in range(count)])]
    pallas_call x12 -> x13, Pallas kernels: 19.1 us -> 19.1 us  [call(): pl.pallas_call(kernel, out_shape=outs, in_specs=specs, out_specs=jax.tree...]
  transfers between devices with their start and end apart: 20 -> 22, of which waited for: 12 -> 12; matrix products, arithmetic and copies ran while one was open for 0% -> 0% of each run, Pallas kernels for 11% -> 11%
where the time goes in v18:
time: 69.1 us; the launch traced here: 68.9 us
  starting transfers between devices  23.7 us (34%)
  waiting for transfers between devices  22.3 us (32%)
  Pallas kernels  21.2 us (31%)
  other arithmetic  1.32 us (2%)
    ppermute x22, starting transfers between devices, swap(): return lax.ppermute(x, axis, [(i, i ^ distance) for i in range(count)])  23.7 us
    ppermute x22, waiting for transfers between devices, swap(): return lax.ppermute(x, axis, [(i, i ^ distance) for i in range(count)])  22.3 us
    pallas_call x13, Pallas kernels, call(): pl.pallas_call(kernel, out_shape=outs, in_specs=specs, out_specs=jax.tree...  19.1 us
    pallas_call x3, Pallas kernels, finish(): pl.pallas_call(functools.partial(finish_kernel, start), out_shape=pltpu.H...  2.15 us
  transfers between devices with their start and end apart: 22, of which 12 were waited for; matrix products, arithmetic and copies ran while one was open for 0% of the time, Pallas kernels for 11%

profile of v18, /device:TPU:0, one launch (start us, length us, event | category | flops | bytes accessed | tf_op | source)
XLA Modules:
  0.0 68.9 jit_solution(9615244220293971783)
XLA Ops:
  0.0 1.3 %convert_reduce_fusion = (f32[64]{0:T(128)S(1)}, f32[64]{0:T(128)S(1)}) fusion(bf16[64,4608]{1,0:T(8,128)(2,1)} %refs_4_.5), kind=kLoop, calls=%fused_computation.1 | loop fusion | flops 1179520 | bytes 590336 | tf_op jit(solution)/shard_map/reduce_sum | solution.py:445
  1.4 2.5 %collective-permute-start.2 = (f32[2,64]{1,0:T(2,128)S(1)}, f32[2,64]{1,0:T(2,128)S(1)}, u32[]{:S(2)}, u32[]{:S(2)}) collective-permute-start(f32[2,64]{1,0:T(2,128)S(1)} %pad_maximum_fusion.refs_0_), channel_id=1, source_target_pairs={{0,12},{4,8},{8,4},{12,0},{1,13},{5,9},{9,5},{13,1},{2,14},{6,10},... | collective-permute-start | bytes 1544 | tf_op jit(solution)/shard_map/ppermute | solution.py:48
  4.5 2.3 %fetch_query_weight.1.refs_8_ = bf16[768,3072]{1,0:T(8,128)(2,1)S(1)} custom-call(bf16[4608,3072]{1,0:T(8,128)(2,1)} %refs_6_.1, f32[2,64]{1,0:T(2,128)S(1)} %pad_maximum_fusion.refs_0_), custom_call_target="tpu_custom_call" | custom-call | bytes 4718592 | tf_op jit(solution)/shard_map/fetch_query_weight/pallas_call | solution.py:22
  7.4 8.6 %project.1 = (f32[32,2048]{1,0:T(8,128)S(1)}, f32[32,1536]{1,0:T(8,128)S(1)}, f32[32,2048]{1,0:T(8,128)S(1)}, f32[32,1536]{1,0:T(8,128)S(1)}) custom-call(f32[2,64]{1,0:T(2,128)S(1)} %pad_maximum_fusion.refs_0_, f32[2,64]{1,0:T(2,128)S(1)} %collective-permute-done.refs_1_, f32[2,64]{1,0:T(2,128)S(1)} %collective-permute-done.1.refs_2_, ...), custom_call_target="tpu_custom_call" | custom-call | flops 1811939328 | bytes 23592960 | tf_op jit(solution)/shard_map/project/pallas_call | solution.py:22
  16.6 1.0 %collective-permute-done.3.came_ref = f32[32,2048]{1,0:T(8,128)S(1)} collective-permute-done((f32[32,2048]{1,0:T(8,128)S(1)}, f32[32,2048]{1,0:T(8,128)S(1)}, u32[]{:S(2)}, u32[]{:S(2)}) %collective-permute-start.3) | collective-permute-done | bytes 262176 | tf_op jit(solution)/shard_map/ppermute | solution.py:48
  17.7 1.3 %collective-permute-start.4 = (f32[16,2048]{1,0:T(8,128)S(1)}, f32[16,2048]{1,0:T(8,128)S(1)}, u32[]{:S(2)}, u32[]{:S(2)}) collective-permute-start(f32[16,2048]{1,0:T(8,128)S(1)} %get-tuple-element.36), channel_id=1, source_target_pairs={{0,8},{4,12},{8,0},{12,4},{1,9},{5,13},{9,1},{13,5},{2,10},{6,14},... | collective-permute-start | bytes 393224 | tf_op jit(solution)/shard_map/ppermute | solution.py:48
  19.0 0.8 %collective-permute-start.6 = (f32[16,1536]{1,0:T(8,128)S(1)}, f32[16,1536]{1,0:T(8,128)S(1)}, u32[]{:S(2)}, u32[]{:S(2)}) collective-permute-start(f32[16,1536]{1,0:T(8,128)S(1)} %get-tuple-element.40), channel_id=1, source_target_pairs={{0,8},{4,12},{8,0},{12,4},{1,9},{5,13},{9,1},{13,5},{2,10},{6,14},... | collective-permute-start | bytes 294920 | tf_op jit(solution)/shard_map/ppermute | solution.py:48
  19.9 5.5 %collective-permute-done.6.came_2_ref = f32[16,1536]{1,0:T(8,128)S(1)} collective-permute-done((f32[16,1536]{1,0:T(8,128)S(1)}, f32[16,1536]{1,0:T(8,128)S(1)}, u32[]{:S(2)}, u32[]{:S(2)}) %collective-permute-start.6) | collective-permute-done | bytes 98336 | tf_op jit(solution)/shard_map/ppermute | solution.py:48
  25.5 2.7 %collective-permute-start.7 = (bf16[8,2048]{1,0:T(8,128)(2,1)S(1)}, bf16[8,2048]{1,0:T(8,128)(2,1)S(1)}, u32[]{:S(2)}, u32[]{:S(2)}) collective-permute-start(bf16[8,2048]{1,0:T(8,128)(2,1)S(1)} %get-tuple-element.41), channel_id=1, source_target_pairs={{0,2},{1,3},{2,0},{3,1},{4,6},{5,7},{6,4},{7,5},{8,10},{9,11},{10,... | collective-permute-start | bytes 98312 | tf_op jit(solution)/shard_map/ppermute | solution.py:48
  28.1 1.3 %collective-permute-start.8 = (bf16[8,2048]{1,0:T(8,128)(2,1)S(1)}, bf16[8,2048]{1,0:T(8,128)(2,1)S(1)}, u32[]{:S(2)}, u32[]{:S(2)}) collective-permute-start(bf16[8,2048]{1,0:T(8,128)(2,1)S(1)} %get-tuple-element.42), channel_id=1, source_target_pairs={{0,3},{1,2},{2,1},{3,0},{4,7},{5,6},{6,5},{7,4},{8,11},{9,10},{10,... | collective-permute-start | bytes 98312 | tf_op jit(solution)/shard_map/ppermute | solution.py:48
  30.4 3.5 %collective-permute-done.8.refs_1_ = bf16[8,2048]{1,0:T(8,128)(2,1)S(1)} collective-permute-done((bf16[8,2048]{1,0:T(8,128)(2,1)S(1)}, bf16[8,2048]{1,0:T(8,128)(2,1)S(1)}, u32[]{:S(2)}, u32[]{:S(2)}) %collective-permute-start.8) | collective-permute-done | bytes 32800 | tf_op jit(solution)/shard_map/ppermute | solution.py:48
  33.9 1.9 %attend.1 = (bf16[8,1536]{1,0:T(8,128)(2,1)S(1)}, bf16[8,1536]{1,0:T(8,128)(2,1)S(1)}, bf16[8,1536]{1,0:T(8,128)(2,1)S(1)}, bf16[8,1536]{1,0:T(8,128)(2,1)S(1)}) custom-call(s32[1,4]{1,0:T(1,128)S(1)} %bitcast.5, bf16[8,2048]{1,0:T(8,128)(2,1)S(1)} %collective-permute-done.7.refs_0_, bf16[8,2048]{1,0:T(8,128)(2,1)S(1)} %collective-permute-done.8.refs_1_, ...), custom_call_target="tpu_custom_call" | custom-call | flops 5000000000 | tf_op jit(solution)/shard_map/attend/pallas_call | solution.py:22
  35.8 1.3 %collective-permute-start.10 = (bf16[8,1536]{1,0:T(8,128)(2,1)S(1)}, bf16[8,1536]{1,0:T(8,128)(2,1)S(1)}, u32[]{:S(2)}, u32[]{:S(2)}) collective-permute-start(bf16[8,1536]{1,0:T(8,128)(2,1)S(1)} %get-tuple-element.45), channel_id=1, source_target_pairs={{0,2},{1,3},{2,0},{3,1},{4,6},{5,7},{6,4},{7,5},{8,10},{9,11},{10,... | collective-permute-start | bytes 73736 | tf_op jit(solution)/shard_map/ppermute | solution.py:48
  37.1 1.0 %collective-permute-start.11 = (bf16[8,1536]{1,0:T(8,128)(2,1)S(1)}, bf16[8,1536]{1,0:T(8,128)(2,1)S(1)}, u32[]{:S(2)}, u32[]{:S(2)}) collective-permute-start(bf16[8,1536]{1,0:T(8,128)(2,1)S(1)} %get-tuple-element.46), channel_id=1, source_target_pairs={{0,3},{1,2},{2,1},{3,0},{4,7},{5,6},{6,5},{7,4},{8,11},{9,10},{10,... | collective-permute-start | bytes 73736 | tf_op jit(solution)/shard_map/ppermute | solution.py:48
  38.1 1.2 %collective-permute-start.12 = (bf16[8,1536]{1,0:T(8,128)(2,1)S(1)}, bf16[8,1536]{1,0:T(8,128)(2,1)S(1)}, u32[]{:S(2)}, u32[]{:S(2)}) collective-permute-start(bf16[8,1536]{1,0:T(8,128)(2,1)S(1)} %get-tuple-element.47), channel_id=1, source_target_pairs={{0,1},{1,0},{2,3},{3,2},{4,5},{5,4},{6,7},{7,6},{8,9},{9,8},{10,11... | collective-permute-start | bytes 73736 | tf_op jit(solution)/shard_map/ppermute | solution.py:48
  39.3 1.2 %collective-permute-done.10.refs_0_ = bf16[8,1536]{1,0:T(8,128)(2,1)S(1)} collective-permute-done((bf16[8,1536]{1,0:T(8,128)(2,1)S(1)}, bf16[8,1536]{1,0:T(8,128)(2,1)S(1)}, u32[]{:S(2)}, u32[]{:S(2)}) %collective-permute-start.10) | collective-permute-done | bytes 24608 | tf_op jit(solution)/shard_map/ppermute | solution.py:48
  40.6 2.1 %collective-permute-done.11.refs_1_ = bf16[8,1536]{1,0:T(8,128)(2,1)S(1)} collective-permute-done((bf16[8,1536]{1,0:T(8,128)(2,1)S(1)}, bf16[8,1536]{1,0:T(8,128)(2,1)S(1)}, u32[]{:S(2)}, u32[]{:S(2)}) %collective-permute-start.11) | collective-permute-done | bytes 24608 | tf_op jit(solution)/shard_map/ppermute | solution.py:48
  42.7 1.3 %collective-permute-start.14 = (bf16[16,3072]{1,0:T(8,128)(2,1)S(1)}, bf16[16,3072]{1,0:T(8,128)(2,1)S(1)}, u32[]{:S(2)}, u32[]{:S(2)}) collective-permute-start(bf16[16,3072]{1,0:T(8,128)(2,1)S(1)} %join.1.refs_0_), channel_id=1, source_target_pairs={{0,8},{4,12},{8,0},{12,4},{1,9},{5,13},{9,1},{13,5},{2,10},{6,14},... | collective-permute-start | bytes 294920 | tf_op jit(solution)/shard_map/ppermute | solution.py:48
  44.1 3.4 %collective-permute-done.14.refs_2_ = bf16[16,3072]{1,0:T(8,128)(2,1)S(1)} collective-permute-done((bf16[16,3072]{1,0:T(8,128)(2,1)S(1)}, bf16[16,3072]{1,0:T(8,128)(2,1)S(1)}, u32[]{:S(2)}, u32[]{:S(2)}) %collective-permute-start.14) | collective-permute-done | bytes 98336 | tf_op jit(solution)/shard_map/ppermute | solution.py:48
  47.4 1.3 %collective-permute-done.15.refs_3_ = bf16[16,3072]{1,0:T(8,128)(2,1)S(1)} collective-permute-done((bf16[16,3072]{1,0:T(8,128)(2,1)S(1)}, bf16[16,3072]{1,0:T(8,128)(2,1)S(1)}, u32[]{:S(2)}, u32[]{:S(2)}) %collective-permute-start.15) | collective-permute-done | bytes 98336 | tf_op jit(solution)/shard_map/ppermute | solution.py:48
  48.8 2.1 %output_part.3 = (f32[64,1792]{1,0:T(8,128)S(1)}, s16[32,1920]{1,0:T(8,128)(2,1)S(1)}) custom-call(bf16[16,3072]{1,0:T(8,128)(2,1)S(1)} %join.1.refs_0_, bf16[16,3072]{1,0:T(8,128)(2,1)S(1)} %collective-permute-done.13.refs_1_, bf16[16,3072]{1,0:T(8,128)(2,1)S(1)} %collective-permute-done.14.refs_2_, bf16[16,3072]{1,0:T(8,128)(2,1)S(1)} %collective-permute-done.15.refs_3_, ...), custom_call_target="tpu_custom_call" | custom-call | flops 704643072 | bytes 393216 | tf_op jit(solution)/shard_map/output_part/pallas_call | solution.py:22
  51.5 2.4 %output_part.4 = (f32[64,2048]{1,0:T(8,128)S(1)}, s16[32,2176]{1,0:T(8,128)(2,1)S(1)}) custom-call(bf16[16,3072]{1,0:T(8,128)(2,1)S(1)} %join.1.refs_0_, bf16[16,3072]{1,0:T(8,128)(2,1)S(1)} %collective-permute-done.13.refs_1_, bf16[16,3072]{1,0:T(8,128)(2,1)S(1)} %collective-permute-done.14.refs_2_, bf16[16,3072]{1,0:T(8,128)(2,1)S(1)} %collective-permute-done.15.refs_3_, ...), custom_call_target="tpu_custom_call" | custom-call | flops 805306368 | bytes 393216 | tf_op jit(solution)/shard_map/output_part/pallas_call | solution.py:22
  53.9 1.6 %collective-permute-start.20 = (s16[32,2176]{1,0:T(8,128)(2,1)S(1)}, s16[32,2176]{1,0:T(8,128)(2,1)S(1)}, u32[]{:S(2)}, u32[]{:S(2)}) collective-permute-start(s16[32,2176]{1,0:T(8,128)(2,1)S(1)} %get-tuple-element.58), channel_id=1, source_target_pairs={{0,1},{1,0},{2,3},{3,2},{4,5},{5,4},{6,7},{7,6},{8,9},{9,8},{10,11... | collective-permute-start | bytes 417800 | tf_op jit(solution)/shard_map/ppermute | solution.py:48
  55.5 0.9 %collective-permute-done.16.came_ref = s16[32,1920]{1,0:T(8,128)(2,1)S(1)} collective-permute-done((s16[32,1920]{1,0:T(8,128)(2,1)S(1)}, s16[32,1920]{1,0:T(8,128)(2,1)S(1)}, u32[]{:S(2)}, u32[]{:S(2)}) %collective-permute-start.16) | collective-permute-done | bytes 122912 | tf_op jit(solution)/shard_map/ppermute | solution.py:48
  56.6 1.1 %collective-permute-start.18 = (s16[16,1920]{1,0:T(8,128)(2,1)S(1)}, s16[16,1920]{1,0:T(8,128)(2,1)S(1)}, u32[]{:S(2)}, u32[]{:S(2)}) collective-permute-start(s16[16,1920]{1,0:T(8,128)(2,1)S(1)} %get-tuple-element.55), channel_id=1, source_target_pairs={{0,2},{1,3},{2,0},{3,1},{4,6},{5,7},{6,4},{7,5},{8,10},{9,11},{10,... | collective-permute-start | bytes 184328 | tf_op jit(solution)/shard_map/ppermute | solution.py:48
  57.6 1.0 %output_part.5 = (f32[64,768]{1,0:T(8,128)S(1)}, s16[32,896]{1,0:T(8,128)(2,1)S(1)}) custom-call(bf16[16,3072]{1,0:T(8,128)(2,1)S(1)} %join.1.refs_0_, bf16[16,3072]{1,0:T(8,128)(2,1)S(1)} %collective-permute-done.13.refs_1_, bf16[16,3072]{1,0:T(8,128)(2,1)S(1)} %collective-permute-done.14.refs_2_, bf16[16,3072]{1,0:T(8,128)(2,1)S(1)} %collective-permute-done.15.refs_3_, ...), custom_call_target="tpu_custom_call" | custom-call | flops 301989888 | bytes 393216 | tf_op jit(solution)/shard_map/output_part/pallas_call | solution.py:22
  58.7 1.6 %collective-permute-start.17 = (s16[32,896]{1,0:T(8,128)(2,1)S(1)}, s16[32,896]{1,0:T(8,128)(2,1)S(1)}, u32[]{:S(2)}, u32[]{:S(2)}) collective-permute-start(s16[32,896]{1,0:T(8,128)(2,1)S(1)} %get-tuple-element.54), channel_id=1, source_target_pairs={{0,1},{1,0},{2,3},{3,2},{4,5},{5,4},{6,7},{7,6},{8,9},{9,8},{10,11... | collective-permute-start | bytes 172040 | tf_op jit(solution)/shard_map/ppermute | solution.py:48
  60.5 1.9 %collective-permute-start.21 = (s16[16,2176]{1,0:T(8,128)(2,1)S(1)}, s16[16,2176]{1,0:T(8,128)(2,1)S(1)}, u32[]{:S(2)}, u32[]{:S(2)}) collective-permute-start(s16[16,2176]{1,0:T(8,128)(2,1)S(1)} %get-tuple-element.60), channel_id=1, source_target_pairs={{0,2},{1,3},{2,0},{3,1},{4,6},{5,7},{6,4},{7,5},{8,10},{9,11},{10,... | collective-permute-start | bytes 208904 | tf_op jit(solution)/shard_map/ppermute | solution.py:48
  62.4 0.7 %finish.3.refs_0_ = bf16[16,4608]{1,0:T(8,128)(2,1)} custom-call(f32[16,1792]{1,0:T(8,128)S(1)} %get-tuple-element.52.refs_5_.kept_ref, s16[16,1920]{1,0:T(8,128)(2,1)S(1)} %collective-permute-done.18.came_ref), custom_call_target="tpu_custom_call" | custom-call | bytes 229376 | tf_op jit(solution)/shard_map/finish/pallas_call | solution.py:423
  63.3 2.0 %collective-permute-start.19 = (s16[16,896]{1,0:T(8,128)(2,1)S(1)}, s16[16,896]{1,0:T(8,128)(2,1)S(1)}, u32[]{:S(2)}, u32[]{:S(2)}) collective-permute-start(s16[16,896]{1,0:T(8,128)(2,1)S(1)} %get-tuple-element.57), channel_id=1, source_target_pairs={{0,2},{1,3},{2,0},{3,1},{4,6},{5,7},{6,4},{7,5},{8,10},{9,11},{10,... | collective-permute-start | bytes 86024 | tf_op jit(solution)/shard_map/ppermute | solution.py:48
  65.3 1.8 %collective-permute-done.21.came_ref = s16[16,2176]{1,0:T(8,128)(2,1)S(1)} collective-permute-done((s16[16,2176]{1,0:T(8,128)(2,1)S(1)}, s16[16,2176]{1,0:T(8,128)(2,1)S(1)}, u32[]{:S(2)}, u32[]{:S(2)}) %collective-permute-start.21) | collective-permute-done | bytes 69664 | tf_op jit(solution)/shard_map/ppermute | solution.py:48
  67.1 0.7 %finish.4.refs_0_ = bf16[16,4608]{1,0:T(8,128)(2,1)} custom-call(f32[16,2048]{1,0:T(8,128)S(1)} %get-tuple-element.59.kept_ref, s16[16,2176]{1,0:T(8,128)(2,1)S(1)} %collective-permute-done.21.came_ref, bf16[16,4608]{1,0:T(8,128)(2,1)} %finish.3.refs_0_), custom_call_target="tpu_custom_call", output_to_operand_aliasing={{}: (2, {})} | custom-call | bytes 262144 | tf_op jit(solution)/shard_map/finish/pallas_call | solution.py:423
  (55 shorter events, 5.1 us)
Async XLA Ops:
  1.3 6.1 %copy-start = (bf16[64,4608]{1,0:T(8,128)(2,1)S(1)}, bf16[64,4608]{1,0:T(8,128)(2,1)}, u32[]{:S(2)}) copy-start(bf16[64,4608]{1,0:T(8,128)(2,1)} %refs_4_.5) | copy-start | bytes 1769476
  1.4 5.5 %collective-permute-start.2 = (f32[2,64]{1,0:T(2,128)S(1)}, f32[2,64]{1,0:T(2,128)S(1)}, u32[]{:S(2)}, u32[]{:S(2)}) collective-permute-start(f32[2,64]{1,0:T(2,128)S(1)} %pad_maximum_fusion.refs_0_), channel_id=1, source_target_pairs={{0,12},{4,8},{8,4},{12,0},{1,13},{5,9},{9,5},{13,1},{2,14},{6,10},... | collective-permute-start | bytes 1544 | tf_op jit(solution)/shard_map/ppermute | solution.py:48
  3.8 3.6 %collective-permute-start.1 = (f32[2,64]{1,0:T(2,128)S(1)}, f32[2,64]{1,0:T(2,128)S(1)}, u32[]{:S(2)}, u32[]{:S(2)}) collective-permute-start(f32[2,64]{1,0:T(2,128)S(1)} %pad_maximum_fusion.refs_0_), channel_id=1, source_target_pairs={{0,8},{4,12},{8,0},{12,4},{1,9},{5,13},{9,1},{13,5},{2,10},{6,14},... | collective-permute-start | bytes 1544 | tf_op jit(solution)/shard_map/ppermute | solution.py:48
  4.5 2.9 %collective-permute-start = (f32[2,64]{1,0:T(2,128)S(1)}, f32[2,64]{1,0:T(2,128)S(1)}, u32[]{:S(2)}, u32[]{:S(2)}) collective-permute-start(f32[2,64]{1,0:T(2,128)S(1)} %pad_maximum_fusion.refs_0_), channel_id=1, source_target_pairs={{0,4},{4,0},{8,12},{12,8},{1,5},{5,1},{9,13},{13,9},{2,6},{6,2},{1... | collective-permute-start | bytes 1544 | tf_op jit(solution)/shard_map/ppermute | solution.py:48
  16.0 1.6 %collective-permute-start.3 = (f32[32,2048]{1,0:T(8,128)S(1)}, f32[32,2048]{1,0:T(8,128)S(1)}, u32[]{:S(2)}, u32[]{:S(2)}) collective-permute-start(f32[32,2048]{1,0:T(8,128)S(1)} %get-tuple-element.34), channel_id=1, source_target_pairs={{0,4},{4,0},{8,12},{12,8},{1,5},{5,1},{9,13},{13,9},{2,6},{6,2},{1... | collective-permute-start | bytes 786440 | tf_op jit(solution)/shard_map/ppermute | solution.py:48
  16.1 2.9 %collective-permute-start.5 = (f32[32,1536]{1,0:T(8,128)S(1)}, f32[32,1536]{1,0:T(8,128)S(1)}, u32[]{:S(2)}, u32[]{:S(2)}) collective-permute-start(f32[32,1536]{1,0:T(8,128)S(1)} %get-tuple-element.38), channel_id=1, source_target_pairs={{0,4},{4,0},{8,12},{12,8},{1,5},{5,1},{9,13},{13,9},{2,6},{6,2},{1... | collective-permute-start | bytes 589832 | tf_op jit(solution)/shard_map/ppermute | solution.py:48
  17.7 7.7 %collective-permute-start.4 = (f32[16,2048]{1,0:T(8,128)S(1)}, f32[16,2048]{1,0:T(8,128)S(1)}, u32[]{:S(2)}, u32[]{:S(2)}) collective-permute-start(f32[16,2048]{1,0:T(8,128)S(1)} %get-tuple-element.36), channel_id=1, source_target_pairs={{0,8},{4,12},{8,0},{12,4},{1,9},{5,13},{9,1},{13,5},{2,10},{6,14},... | collective-permute-start | bytes 393224 | tf_op jit(solution)/shard_map/ppermute | solution.py:48
  19.0 6.4 %collective-permute-start.6 = (f32[16,1536]{1,0:T(8,128)S(1)}, f32[16,1536]{1,0:T(8,128)S(1)}, u32[]{:S(2)}, u32[]{:S(2)}) collective-permute-start(f32[16,1536]{1,0:T(8,128)S(1)} %get-tuple-element.40), channel_id=1, source_target_pairs={{0,8},{4,12},{8,0},{12,4},{1,9},{5,13},{9,1},{13,5},{2,10},{6,14},... | collective-permute-start | bytes 294920 | tf_op jit(solution)/shard_map/ppermute | solution.py:48
  25.4 8.5 %copy-start.3 = (bf16[4,1024,512]{2,1,0:T(8,128)(2,1)S(1)}, bf16[4,1024,512]{2,1,0:T(8,128)(2,1)}, u32[]{:S(2)}) copy-start(bf16[4,1024,512]{2,1,0:T(8,128)(2,1)} %refs_4_.6) | copy-start | bytes 12582916
  25.4 8.5 %copy-start.4 = (s32[4]{0:T(128)S(1)}, s32[4]{0:T(128)}, u32[]{:S(2)}) copy-start(s32[4]{0:T(128)} %param.13) | copy-start | bytes 52
  25.4 23.3 %slice-start = ((s8[28311552]{0:T(1024)(128)(4,1)}), s8[4194304]{0:T(1024)(128)(4,1)S(1)}, s32[]{:S(2)}) async-start(s8[28311552]{0:T(1024)(128)(4,1)} %bitcast.3), calls=%async_computation | async-start | bytes 8388608
  25.4 23.3 %slice-start.1 = ((s8[28311552]{0:T(1024)(128)(4,1)}), s8[4194304]{0:T(1024)(128)(4,1)S(1)}, s32[]{:S(2)}) async-start(s8[28311552]{0:T(1024)(128)(4,1)} %bitcast.3), calls=%async_computation.1 | async-start | bytes 8388608
  25.4 23.3 %slice-start.2 = ((s8[28311552]{0:T(1024)(128)(4,1)}), s8[4194304]{0:T(1024)(128)(4,1)S(1)}, s32[]{:S(2)}) async-start(s8[28311552]{0:T(1024)(128)(4,1)} %bitcast.3), calls=%async_computation.2 | async-start | bytes 8388608
  25.5 4.9 %collective-permute-start.7 = (bf16[8,2048]{1,0:T(8,128)(2,1)S(1)}, bf16[8,2048]{1,0:T(8,128)(2,1)S(1)}, u32[]{:S(2)}, u32[]{:S(2)}) collective-permute-start(bf16[8,2048]{1,0:T(8,128)(2,1)S(1)} %get-tuple-element.41), channel_id=1, source_target_pairs={{0,2},{1,3},{2,0},{3,1},{4,6},{5,7},{6,4},{7,5},{8,10},{9,11},{10,... | collective-permute-start | bytes 98312 | tf_op jit(solution)/shard_map/ppermute | solution.py:48
  28.1 5.7 %collective-permute-start.8 = (bf16[8,2048]{1,0:T(8,128)(2,1)S(1)}, bf16[8,2048]{1,0:T(8,128)(2,1)S(1)}, u32[]{:S(2)}, u32[]{:S(2)}) collective-permute-start(bf16[8,2048]{1,0:T(8,128)(2,1)S(1)} %get-tuple-element.42), channel_id=1, source_target_pairs={{0,3},{1,2},{2,1},{3,0},{4,7},{5,6},{6,5},{7,4},{8,11},{9,10},{10,... | collective-permute-start | bytes 98312 | tf_op jit(solution)/shard_map/ppermute | solution.py:48
  29.5 4.4 %collective-permute-start.9 = (bf16[8,2048]{1,0:T(8,128)(2,1)S(1)}, bf16[8,2048]{1,0:T(8,128)(2,1)S(1)}, u32[]{:S(2)}, u32[]{:S(2)}) collective-permute-start(bf16[8,2048]{1,0:T(8,128)(2,1)S(1)} %get-tuple-element.43), channel_id=1, source_target_pairs={{0,1},{1,0},{2,3},{3,2},{4,5},{5,4},{6,7},{7,6},{8,9},{9,8},{10,11... | collective-permute-start | bytes 98312 | tf_op jit(solution)/shard_map/ppermute | solution.py:48
  33.9 14.9 %slice-start.3 = ((s8[28311552]{0:T(1024)(128)(4,1)}), s8[4194304]{0:T(1024)(128)(4,1)S(1)}, s32[]{:S(2)}) async-start(s8[28311552]{0:T(1024)(128)(4,1)} %bitcast.3), calls=%async_computation.3 | async-start | bytes 8388608
  33.9 14.9 %slice-start.4 = ((s8[28311552]{0:T(1024)(128)(4,1)}), s8[4194304]{0:T(1024)(128)(4,1)S(1)}, s32[]{:S(2)}) async-start(s8[28311552]{0:T(1024)(128)(4,1)} %bitcast.3), calls=%async_computation.4 | async-start | bytes 8388608
  35.8 4.8 %collective-permute-start.10 = (bf16[8,1536]{1,0:T(8,128)(2,1)S(1)}, bf16[8,1536]{1,0:T(8,128)(2,1)S(1)}, u32[]{:S(2)}, u32[]{:S(2)}) collective-permute-start(bf16[8,1536]{1,0:T(8,128)(2,1)S(1)} %get-tuple-element.45), channel_id=1, source_target_pairs={{0,2},{1,3},{2,0},{3,1},{4,6},{5,7},{6,4},{7,5},{8,10},{9,11},{10,... | collective-permute-start | bytes 73736 | tf_op jit(solution)/shard_map/ppermute | solution.py:48
  37.1 5.6 %collective-permute-start.11 = (bf16[8,1536]{1,0:T(8,128)(2,1)S(1)}, bf16[8,1536]{1,0:T(8,128)(2,1)S(1)}, u32[]{:S(2)}, u32[]{:S(2)}) collective-permute-start(bf16[8,1536]{1,0:T(8,128)(2,1)S(1)} %get-tuple-element.46), channel_id=1, source_target_pairs={{0,3},{1,2},{2,1},{3,0},{4,7},{5,6},{6,5},{7,4},{8,11},{9,10},{10,... | collective-permute-start | bytes 73736 | tf_op jit(solution)/shard_map/ppermute | solution.py:48
  38.1 4.6 %collective-permute-start.12 = (bf16[8,1536]{1,0:T(8,128)(2,1)S(1)}, bf16[8,1536]{1,0:T(8,128)(2,1)S(1)}, u32[]{:S(2)}, u32[]{:S(2)}) collective-permute-start(bf16[8,1536]{1,0:T(8,128)(2,1)S(1)} %get-tuple-element.47), channel_id=1, source_target_pairs={{0,1},{1,0},{2,3},{3,2},{4,5},{5,4},{6,7},{7,6},{8,9},{9,8},{10,11... | collective-permute-start | bytes 73736 | tf_op jit(solution)/shard_map/ppermute | solution.py:48
  42.7 6.1 %slice-start.5 = ((s8[28311552]{0:T(1024)(128)(4,1)}), s8[4194304]{0:T(1024)(128)(4,1)S(1)}, s32[]{:S(2)}) async-start(s8[28311552]{0:T(1024)(128)(4,1)} %bitcast.3), calls=%async_computation.5 | async-start | bytes 8388608
  42.7 6.1 %slice-start.6 = ((s8[28311552]{0:T(1024)(128)(4,1)}), s8[3145728]{0:T(1024)(128)(4,1)S(1)}, s32[]{:S(2)}) async-start(s8[28311552]{0:T(1024)(128)(4,1)} %bitcast.3), calls=%async_computation.6 | async-start | bytes 6291456
  42.7 4.7 %collective-permute-start.14 = (bf16[16,3072]{1,0:T(8,128)(2,1)S(1)}, bf16[16,3072]{1,0:T(8,128)(2,1)S(1)}, u32[]{:S(2)}, u32[]{:S(2)}) collective-permute-start(bf16[16,3072]{1,0:T(8,128)(2,1)S(1)} %join.1.refs_0_), channel_id=1, source_target_pairs={{0,8},{4,12},{8,0},{12,4},{1,9},{5,13},{9,1},{13,5},{2,10},{6,14},... | collective-permute-start | bytes 294920 | tf_op jit(solution)/shard_map/ppermute | solution.py:48
  44.1 3.4 %collective-permute-start.13 = (bf16[16,3072]{1,0:T(8,128)(2,1)S(1)}, bf16[16,3072]{1,0:T(8,128)(2,1)S(1)}, u32[]{:S(2)}, u32[]{:S(2)}) collective-permute-start(bf16[16,3072]{1,0:T(8,128)(2,1)S(1)} %join.1.refs_0_), channel_id=1, source_target_pairs={{0,4},{4,0},{8,12},{12,8},{1,5},{5,1},{9,13},{13,9},{2,6},{6,2},{1... | collective-permute-start | bytes 294920 | tf_op jit(solution)/shard_map/ppermute | solution.py:48
  47.4 1.3 %collective-permute-start.15 = (bf16[16,3072]{1,0:T(8,128)(2,1)S(1)}, bf16[16,3072]{1,0:T(8,128)(2,1)S(1)}, u32[]{:S(2)}, u32[]{:S(2)}) collective-permute-start(bf16[16,3072]{1,0:T(8,128)(2,1)S(1)} %collective-permute-done.14.refs_2_), channel_id=1, source_target_pairs={{0,4},{4,0},{8,12},{12,8},{1,5},{5,1},{9,13},{13,9},{2,6},{6,2},{1... | collective-permute-start | bytes 294920 | tf_op jit(solution)/shard_map/ppermute | solution.py:48
  50.9 5.4 %collective-permute-start.16 = (s16[32,1920]{1,0:T(8,128)(2,1)S(1)}, s16[32,1920]{1,0:T(8,128)(2,1)S(1)}, u32[]{:S(2)}, u32[]{:S(2)}) collective-permute-start(s16[32,1920]{1,0:T(8,128)(2,1)S(1)} %get-tuple-element.50), channel_id=1, source_target_pairs={{0,1},{1,0},{2,3},{3,2},{4,5},{5,4},{6,7},{7,6},{8,9},{9,8},{10,11... | collective-permute-start | bytes 368648 | tf_op jit(solution)/shard_map/ppermute | solution.py:48
  53.9 6.5 %collective-permute-start.20 = (s16[32,2176]{1,0:T(8,128)(2,1)S(1)}, s16[32,2176]{1,0:T(8,128)(2,1)S(1)}, u32[]{:S(2)}, u32[]{:S(2)}) collective-permute-start(s16[32,2176]{1,0:T(8,128)(2,1)S(1)} %get-tuple-element.58), channel_id=1, source_target_pairs={{0,1},{1,0},{2,3},{3,2},{4,5},{5,4},{6,7},{7,6},{8,9},{9,8},{10,11... | collective-permute-start | bytes 417800 | tf_op jit(solution)/shard_map/ppermute | solution.py:48
  56.6 5.9 %collective-permute-start.18 = (s16[16,1920]{1,0:T(8,128)(2,1)S(1)}, s16[16,1920]{1,0:T(8,128)(2,1)S(1)}, u32[]{:S(2)}, u32[]{:S(2)}) collective-permute-start(s16[16,1920]{1,0:T(8,128)(2,1)S(1)} %get-tuple-element.55), channel_id=1, source_target_pairs={{0,2},{1,3},{2,0},{3,1},{4,6},{5,7},{6,4},{7,5},{8,10},{9,11},{10,... | collective-permute-start | bytes 184328 | tf_op jit(solution)/shard_map/ppermute | solution.py:48
  58.7 4.5 %collective-permute-start.17 = (s16[32,896]{1,0:T(8,128)(2,1)S(1)}, s16[32,896]{1,0:T(8,128)(2,1)S(1)}, u32[]{:S(2)}, u32[]{:S(2)}) collective-permute-start(s16[32,896]{1,0:T(8,128)(2,1)S(1)} %get-tuple-element.54), channel_id=1, source_target_pairs={{0,1},{1,0},{2,3},{3,2},{4,5},{5,4},{6,7},{7,6},{8,9},{9,8},{10,11... | collective-permute-start | bytes 172040 | tf_op jit(solution)/shard_map/ppermute | solution.py:48
  60.5 6.5 %collective-permute-start.21 = (s16[16,2176]{1,0:T(8,128)(2,1)S(1)}, s16[16,2176]{1,0:T(8,128)(2,1)S(1)}, u32[]{:S(2)}, u32[]{:S(2)}) collective-permute-start(s16[16,2176]{1,0:T(8,128)(2,1)S(1)} %get-tuple-element.60), channel_id=1, source_target_pairs={{0,2},{1,3},{2,0},{3,1},{4,6},{5,7},{6,4},{7,5},{8,10},{9,11},{10,... | collective-permute-start | bytes 208904 | tf_op jit(solution)/shard_map/ppermute | solution.py:48
  63.3 4.8 %collective-permute-start.19 = (s16[16,896]{1,0:T(8,128)(2,1)S(1)}, s16[16,896]{1,0:T(8,128)(2,1)S(1)}, u32[]{:S(2)}, u32[]{:S(2)}) collective-permute-start(s16[16,896]{1,0:T(8,128)(2,1)S(1)} %get-tuple-element.57), channel_id=1, source_target_pairs={{0,2},{1,3},{2,0},{3,1},{4,6},{5,7},{6,4},{7,5},{8,10},{9,11},{10,... | collective-permute-start | bytes 86024 | tf_op jit(solution)/shard_map/ppermute | solution.py:48
  (2 other events, 12.1 us)

commit v19 on v18

--- a/solution.py
+++ b/solution.py
@@ -12,9 +12,10 @@
 FULL = pl.BlockSpec(memory_space=pltpu.VMEM)
 ANY = pl.BlockSpec(memory_space=pl.ANY)
 STEPS = 32700.0
-TINY = 1e-37
+TINY = 1e-33
 LANES = 128
 PAD = 8
+PIECES = 4
 BESIDE = 5 * 10**9
 
 
@@ -48,13 +49,15 @@
     return lax.ppermute(x, axis, [(i, i ^ distance) for i in range(count)])
 
 
-def sent_apart(x, axis):
+def sent_apart(x, axis, entries):
     count = lax.axis_size(axis)
     if count <= 4:
         return [x] + [swap(x, axis, d) for d in range(1, count)]
     d = 1
     while d < count:
-        x = x + swap(x, axis, d)
+        other = swap(x, axis, d)
+        between = (x[0] - other[0]) * (x[0] - other[0]) / (2 * entries * d)
+        x = jnp.stack([x[0] + other[0], x[1] + other[1] + between])
         d *= 2
     return [x]
 
@@ -85,6 +88,41 @@
 def halving_order(count):
     bits = count.bit_length() - 1
     return [sum(((k >> b) & 1) << (bits - 1 - b) for b in range(bits)) for k in range(count)]
+
+
+def stats_kernel(x_ref, out_ref, copied, sems):
+    rows, width = x_ref.shape
+    step = rows // PIECES
+    pieces = [pl.ds(p * step, step) for p in range(PIECES)]
+    copies = [pltpu.make_async_copy(x_ref.at[at], copied.at[at], sems.at[p]) for p, at in enumerate(pieces)]
+    for copy in copies:
+        copy.start()
+    totals, squares = [], []
+    for copy, at in zip(copies, pieces):
+        copy.wait()
+        parts = [copied[at, c : c + LANES].astype(jnp.float32) for c in range(0, width, LANES)]
+        total = jnp.sum(functools.reduce(jnp.add, parts), axis=1, keepdims=True)
+        apart = [part - total / width for part in parts]
+        square = jnp.sum(functools.reduce(jnp.add, [part * part for part in apart]), axis=1, keepdims=True)
+        totals.append(total)
+        squares.append(square)
+    row = lax.broadcasted_iota(jnp.int32, (rows, rows), 0)
+    column = lax.broadcasted_iota(jnp.int32, (rows, rows), 1)
+    for k, sums in enumerate((totals, squares)):
+        sums = jnp.where(row == column, jnp.concatenate(sums, axis=0), 0.0)
+        out_ref[k : k + 1, :] = jnp.sum(sums, axis=0, keepdims=True)
+
+
+def row_sums(x):
+    return call(
+        stats_kernel,
+        jax.ShapeDtypeStruct((2, x.shape[0]), jnp.float32),
+        (in_hbm(x),),
+        [ANY],
+        "row_sums",
+        scratch=[pltpu.VMEM(x.shape, x.dtype), pltpu.SemaphoreType.DMA((PIECES,))],
+        moved=2 * x.size,
+    )
 
 
 def fetch_kernel(w_ref, *refs):
@@ -135,15 +173,17 @@
     for fetch in fetches[:ahead]:
         fetch.start()
     me, narrow = lax.axis_index("wide"), lax.axis_index("narrow")
-    stats = stat_refs[0][...]
-    for ref in stat_refs[1:]:
-        stats = stats + ref[...]
+    parts = [ref[...] for ref in stat_refs]
+    entries = width_all // many
+    centers = sum(part[0:1, :] for part in parts) / width_all
+    spreads = 0.0
+    for part in parts:
+        off = part[0:1, :] / entries - centers
+        spreads = spreads + part[1:2, :] + entries * (off * off)
     row = lax.broadcasted_iota(jnp.int32, (rows, rows), 0)
     column = lax.broadcasted_iota(jnp.int32, (rows, rows), 1)
-    sums = jnp.sum(jnp.where(row == column, stats[0:1, :], 0.0), axis=1, keepdims=True)
-    squares = jnp.sum(jnp.where(row == column, stats[1:2, :], 0.0), axis=1, keepdims=True)
-    center = sums / width_all
-    spread = squares / width_all - center * center
+    center = jnp.sum(jnp.where(row == column, centers, 0.0), axis=1, keepdims=True)
+    spread = jnp.sum(jnp.where(row == column, spreads / width_all, 0.0), axis=1, keepdims=True)
     inverse = lax.rsqrt(spread + 1e-05)
     gain = gain_ref[...].reshape(1, width)
     order = halving_order(count)
@@ -441,11 +481,10 @@
     rows, width = activations.shape
     queries = query_weight.shape[1]
     columns = out_weight.shape[1]
-    values = activations.astype(jnp.float32)
-    stats = jnp.stack([jnp.sum(values, axis=1), jnp.sum(values * values, axis=1)])
+    stats = row_sums(activations)
     first_part = fetch(query_weight, row_blocks(width)[0], [stats])
     kept, kept_2, sent, sent_2 = project(
-        sent_apart(stats, "wide"),
+        sent_apart(stats, "wide", width),
         activations,
         norm_gain,
         query_weight,

time: 69.1 us -> 69.7 us (level)
  Pallas kernels: 21.2 us -> 23.2 us
  other arithmetic: 1.32 us -> 0.01 us
    pallas_call x13 -> x14, Pallas kernels: 19.1 us -> 21.1 us  [call(): pl.pallas_call(kernel, out_shape=outs, in_specs=specs, out_specs=jax.tree...]
    reduce_sum x1 -> x0, other arithmetic: 1.31 us -> none  [local(): jnp.sum(values, axis=1)]
where the time goes in v19:
time: 69.7 us; the launch traced here: 69.5 us
  starting transfers between devices  23.7 us (34%)
  Pallas kernels  23.2 us (33%)
  waiting for transfers between devices  22.3 us (32%)
    ppermute x22, starting transfers between devices, swap(): return lax.ppermute(x, axis, [(i, i ^ distance) for i in range(count)])  23.7 us
    ppermute x22, waiting for transfers between devices, swap(): return lax.ppermute(x, axis, [(i, i ^ distance) for i in range(count)])  22.3 us
    pallas_call x14, Pallas kernels, call(): pl.pallas_call(kernel, out_shape=outs, in_specs=specs, out_specs=jax.tree...  21.1 us
    pallas_call x3, Pallas kernels, finish(): pl.pallas_call(functools.partial(finish_kernel, start), out_shape=pltpu.H...  2.15 us
  transfers between devices with their start and end apart: 22, of which 12 were waited for; matrix products, arithmetic and copies ran while one was open for 0% of the time, Pallas kernels for 11%

profile of v19, /device:TPU:0, one launch (start us, length us, event | category | flops | bytes accessed | tf_op | source)
XLA Modules:
  0.0 69.5 jit_solution(2524706358705571411)
XLA Ops:
  0.0 2.0 %row_sums.1.refs_0_ = f32[2,64]{1,0:T(2,128)S(1)} custom-call(bf16[64,4608]{1,0:T(8,128)(2,1)} %refs_4_.5), custom_call_target="tpu_custom_call" | custom-call | bytes 589824 | tf_op jit(solution)/shard_map/row_sums/pallas_call | solution.py:23
  2.0 2.5 %collective-permute-start.2 = (f32[2,64]{1,0:T(2,128)S(1)}, f32[2,64]{1,0:T(2,128)S(1)}, u32[]{:S(2)}, u32[]{:S(2)}) collective-permute-start(f32[2,64]{1,0:T(2,128)S(1)} %row_sums.1.refs_0_), channel_id=1, source_target_pairs={{0,12},{4,8},{8,4},{12,0},{1,13},{5,9},{9,5},{13,1},{2,14},{6,10},... | collective-permute-start | bytes 1544 | tf_op jit(solution)/shard_map/ppermute | solution.py:49
  5.2 2.3 %fetch_query_weight.1.refs_8_ = bf16[768,3072]{1,0:T(8,128)(2,1)S(1)} custom-call(bf16[4608,3072]{1,0:T(8,128)(2,1)} %refs_6_.1, f32[2,64]{1,0:T(2,128)S(1)} %row_sums.1.refs_0_), custom_call_target="tpu_custom_call" | custom-call | bytes 4718592 | tf_op jit(solution)/shard_map/fetch_query_weight/pallas_call | solution.py:23
  8.1 8.6 %project.1 = (f32[32,2048]{1,0:T(8,128)S(1)}, f32[32,1536]{1,0:T(8,128)S(1)}, f32[32,2048]{1,0:T(8,128)S(1)}, f32[32,1536]{1,0:T(8,128)S(1)}) custom-call(f32[2,64]{1,0:T(2,128)S(1)} %row_sums.1.refs_0_, f32[2,64]{1,0:T(2,128)S(1)} %collective-permute-done.refs_1_, f32[2,64]{1,0:T(2,128)S(1)} %collective-permute-done.1.refs_2_, ...), custom_call_target="tpu_custom_call" | custom-call | flops 1811939328 | bytes 23592960 | tf_op jit(solution)/shard_map/project/pallas_call | solution.py:23
  17.3 1.0 %collective-permute-done.3.came_ref = f32[32,2048]{1,0:T(8,128)S(1)} collective-permute-done((f32[32,2048]{1,0:T(8,128)S(1)}, f32[32,2048]{1,0:T(8,128)S(1)}, u32[]{:S(2)}, u32[]{:S(2)}) %collective-permute-start.3) | collective-permute-done | bytes 262176 | tf_op jit(solution)/shard_map/ppermute | solution.py:49
  18.3 1.3 %collective-permute-start.4 = (f32[16,2048]{1,0:T(8,128)S(1)}, f32[16,2048]{1,0:T(8,128)S(1)}, u32[]{:S(2)}, u32[]{:S(2)}) collective-permute-start(f32[16,2048]{1,0:T(8,128)S(1)} %get-tuple-element.36), channel_id=1, source_target_pairs={{0,8},{4,12},{8,0},{12,4},{1,9},{5,13},{9,1},{13,5},{2,10},{6,14},... | collective-permute-start | bytes 393224 | tf_op jit(solution)/shard_map/ppermute | solution.py:49
  19.7 0.8 %collective-permute-start.6 = (f32[16,1536]{1,0:T(8,128)S(1)}, f32[16,1536]{1,0:T(8,128)S(1)}, u32[]{:S(2)}, u32[]{:S(2)}) collective-permute-start(f32[16,1536]{1,0:T(8,128)S(1)} %get-tuple-element.40), channel_id=1, source_target_pairs={{0,8},{4,12},{8,0},{12,4},{1,9},{5,13},{9,1},{13,5},{2,10},{6,14},... | collective-permute-start | bytes 294920 | tf_op jit(solution)/shard_map/ppermute | solution.py:49
  20.5 5.5 %collective-permute-done.6.came_2_ref = f32[16,1536]{1,0:T(8,128)S(1)} collective-permute-done((f32[16,1536]{1,0:T(8,128)S(1)}, f32[16,1536]{1,0:T(8,128)S(1)}, u32[]{:S(2)}, u32[]{:S(2)}) %collective-permute-start.6) | collective-permute-done | bytes 98336 | tf_op jit(solution)/shard_map/ppermute | solution.py:49
  26.1 2.7 %collective-permute-start.7 = (bf16[8,2048]{1,0:T(8,128)(2,1)S(1)}, bf16[8,2048]{1,0:T(8,128)(2,1)S(1)}, u32[]{:S(2)}, u32[]{:S(2)}) collective-permute-start(bf16[8,2048]{1,0:T(8,128)(2,1)S(1)} %get-tuple-element.41), channel_id=1, source_target_pairs={{0,2},{1,3},{2,0},{3,1},{4,6},{5,7},{6,4},{7,5},{8,10},{9,11},{10,... | collective-permute-start | bytes 98312 | tf_op jit(solution)/shard_map/ppermute | solution.py:49
  28.8 1.3 %collective-permute-start.8 = (bf16[8,2048]{1,0:T(8,128)(2,1)S(1)}, bf16[8,2048]{1,0:T(8,128)(2,1)S(1)}, u32[]{:S(2)}, u32[]{:S(2)}) collective-permute-start(bf16[8,2048]{1,0:T(8,128)(2,1)S(1)} %get-tuple-element.42), channel_id=1, source_target_pairs={{0,3},{1,2},{2,1},{3,0},{4,7},{5,6},{6,5},{7,4},{8,11},{9,10},{10,... | collective-permute-start | bytes 98312 | tf_op jit(solution)/shard_map/ppermute | solution.py:49
  31.0 3.5 %collective-permute-done.8.refs_1_ = bf16[8,2048]{1,0:T(8,128)(2,1)S(1)} collective-permute-done((bf16[8,2048]{1,0:T(8,128)(2,1)S(1)}, bf16[8,2048]{1,0:T(8,128)(2,1)S(1)}, u32[]{:S(2)}, u32[]{:S(2)}) %collective-permute-start.8) | collective-permute-done | bytes 32800 | tf_op jit(solution)/shard_map/ppermute | solution.py:49
  34.5 1.9 %attend.1 = (bf16[8,1536]{1,0:T(8,128)(2,1)S(1)}, bf16[8,1536]{1,0:T(8,128)(2,1)S(1)}, bf16[8,1536]{1,0:T(8,128)(2,1)S(1)}, bf16[8,1536]{1,0:T(8,128)(2,1)S(1)}) custom-call(s32[1,4]{1,0:T(1,128)S(1)} %bitcast.3, bf16[8,2048]{1,0:T(8,128)(2,1)S(1)} %collective-permute-done.7.refs_0_, bf16[8,2048]{1,0:T(8,128)(2,1)S(1)} %collective-permute-done.8.refs_1_, ...), custom_call_target="tpu_custom_call" | custom-call | flops 5000000000 | tf_op jit(solution)/shard_map/attend/pallas_call | solution.py:23
  36.4 1.3 %collective-permute-start.10 = (bf16[8,1536]{1,0:T(8,128)(2,1)S(1)}, bf16[8,1536]{1,0:T(8,128)(2,1)S(1)}, u32[]{:S(2)}, u32[]{:S(2)}) collective-permute-start(bf16[8,1536]{1,0:T(8,128)(2,1)S(1)} %get-tuple-element.45), channel_id=1, source_target_pairs={{0,2},{1,3},{2,0},{3,1},{4,6},{5,7},{6,4},{7,5},{8,10},{9,11},{10,... | collective-permute-start | bytes 73736 | tf_op jit(solution)/shard_map/ppermute | solution.py:49
  37.7 1.0 %collective-permute-start.11 = (bf16[8,1536]{1,0:T(8,128)(2,1)S(1)}, bf16[8,1536]{1,0:T(8,128)(2,1)S(1)}, u32[]{:S(2)}, u32[]{:S(2)}) collective-permute-start(bf16[8,1536]{1,0:T(8,128)(2,1)S(1)} %get-tuple-element.46), channel_id=1, source_target_pairs={{0,3},{1,2},{2,1},{3,0},{4,7},{5,6},{6,5},{7,4},{8,11},{9,10},{10,... | collective-permute-start | bytes 73736 | tf_op jit(solution)/shard_map/ppermute | solution.py:49
  38.7 1.2 %collective-permute-start.12 = (bf16[8,1536]{1,0:T(8,128)(2,1)S(1)}, bf16[8,1536]{1,0:T(8,128)(2,1)S(1)}, u32[]{:S(2)}, u32[]{:S(2)}) collective-permute-start(bf16[8,1536]{1,0:T(8,128)(2,1)S(1)} %get-tuple-element.47), channel_id=1, source_target_pairs={{0,1},{1,0},{2,3},{3,2},{4,5},{5,4},{6,7},{7,6},{8,9},{9,8},{10,11... | collective-permute-start | bytes 73736 | tf_op jit(solution)/shard_map/ppermute | solution.py:49
  40.0 1.2 %collective-permute-done.10.refs_0_ = bf16[8,1536]{1,0:T(8,128)(2,1)S(1)} collective-permute-done((bf16[8,1536]{1,0:T(8,128)(2,1)S(1)}, bf16[8,1536]{1,0:T(8,128)(2,1)S(1)}, u32[]{:S(2)}, u32[]{:S(2)}) %collective-permute-start.10) | collective-permute-done | bytes 24608 | tf_op jit(solution)/shard_map/ppermute | solution.py:49
  41.2 2.1 %collective-permute-done.11.refs_1_ = bf16[8,1536]{1,0:T(8,128)(2,1)S(1)} collective-permute-done((bf16[8,1536]{1,0:T(8,128)(2,1)S(1)}, bf16[8,1536]{1,0:T(8,128)(2,1)S(1)}, u32[]{:S(2)}, u32[]{:S(2)}) %collective-permute-start.11) | collective-permute-done | bytes 24608 | tf_op jit(solution)/shard_map/ppermute | solution.py:49
  43.4 1.3 %collective-permute-start.14 = (bf16[16,3072]{1,0:T(8,128)(2,1)S(1)}, bf16[16,3072]{1,0:T(8,128)(2,1)S(1)}, u32[]{:S(2)}, u32[]{:S(2)}) collective-permute-start(bf16[16,3072]{1,0:T(8,128)(2,1)S(1)} %join.1.refs_0_), channel_id=1, source_target_pairs={{0,8},{4,12},{8,0},{12,4},{1,9},{5,13},{9,1},{13,5},{2,10},{6,14},... | collective-permute-start | bytes 294920 | tf_op jit(solution)/shard_map/ppermute | solution.py:49
  44.7 3.4 %collective-permute-done.14.refs_2_ = bf16[16,3072]{1,0:T(8,128)(2,1)S(1)} collective-permute-done((bf16[16,3072]{1,0:T(8,128)(2,1)S(1)}, bf16[16,3072]{1,0:T(8,128)(2,1)S(1)}, u32[]{:S(2)}, u32[]{:S(2)}) %collective-permute-start.14) | collective-permute-done | bytes 98336 | tf_op jit(solution)/shard_map/ppermute | solution.py:49
  48.1 1.3 %collective-permute-done.15.refs_3_ = bf16[16,3072]{1,0:T(8,128)(2,1)S(1)} collective-permute-done((bf16[16,3072]{1,0:T(8,128)(2,1)S(1)}, bf16[16,3072]{1,0:T(8,128)(2,1)S(1)}, u32[]{:S(2)}, u32[]{:S(2)}) %collective-permute-start.15) | collective-permute-done | bytes 98336 | tf_op jit(solution)/shard_map/ppermute | solution.py:49
  49.4 2.1 %output_part.3 = (f32[64,1792]{1,0:T(8,128)S(1)}, s16[32,1920]{1,0:T(8,128)(2,1)S(1)}) custom-call(bf16[16,3072]{1,0:T(8,128)(2,1)S(1)} %join.1.refs_0_, bf16[16,3072]{1,0:T(8,128)(2,1)S(1)} %collective-permute-done.13.refs_1_, bf16[16,3072]{1,0:T(8,128)(2,1)S(1)} %collective-permute-done.14.refs_2_, bf16[16,3072]{1,0:T(8,128)(2,1)S(1)} %collective-permute-done.15.refs_3_, ...), custom_call_target="tpu_custom_call" | custom-call | flops 704643072 | bytes 393216 | tf_op jit(solution)/shard_map/output_part/pallas_call | solution.py:23
  52.1 2.4 %output_part.4 = (f32[64,2048]{1,0:T(8,128)S(1)}, s16[32,2176]{1,0:T(8,128)(2,1)S(1)}) custom-call(bf16[16,3072]{1,0:T(8,128)(2,1)S(1)} %join.1.refs_0_, bf16[16,3072]{1,0:T(8,128)(2,1)S(1)} %collective-permute-done.13.refs_1_, bf16[16,3072]{1,0:T(8,128)(2,1)S(1)} %collective-permute-done.14.refs_2_, bf16[16,3072]{1,0:T(8,128)(2,1)S(1)} %collective-permute-done.15.refs_3_, ...), custom_call_target="tpu_custom_call" | custom-call | flops 805306368 | bytes 393216 | tf_op jit(solution)/shard_map/output_part/pallas_call | solution.py:23
  54.5 1.6 %collective-permute-start.20 = (s16[32,2176]{1,0:T(8,128)(2,1)S(1)}, s16[32,2176]{1,0:T(8,128)(2,1)S(1)}, u32[]{:S(2)}, u32[]{:S(2)}) collective-permute-start(s16[32,2176]{1,0:T(8,128)(2,1)S(1)} %get-tuple-element.58), channel_id=1, source_target_pairs={{0,1},{1,0},{2,3},{3,2},{4,5},{5,4},{6,7},{7,6},{8,9},{9,8},{10,11... | collective-permute-start | bytes 417800 | tf_op jit(solution)/shard_map/ppermute | solution.py:49
  56.1 0.9 %collective-permute-done.16.came_ref = s16[32,1920]{1,0:T(8,128)(2,1)S(1)} collective-permute-done((s16[32,1920]{1,0:T(8,128)(2,1)S(1)}, s16[32,1920]{1,0:T(8,128)(2,1)S(1)}, u32[]{:S(2)}, u32[]{:S(2)}) %collective-permute-start.16) | collective-permute-done | bytes 122912 | tf_op jit(solution)/shard_map/ppermute | solution.py:49
  57.2 1.1 %collective-permute-start.18 = (s16[16,1920]{1,0:T(8,128)(2,1)S(1)}, s16[16,1920]{1,0:T(8,128)(2,1)S(1)}, u32[]{:S(2)}, u32[]{:S(2)}) collective-permute-start(s16[16,1920]{1,0:T(8,128)(2,1)S(1)} %get-tuple-element.55), channel_id=1, source_target_pairs={{0,2},{1,3},{2,0},{3,1},{4,6},{5,7},{6,4},{7,5},{8,10},{9,11},{10,... | collective-permute-start | bytes 184328 | tf_op jit(solution)/shard_map/ppermute | solution.py:49
  58.3 1.0 %output_part.5 = (f32[64,768]{1,0:T(8,128)S(1)}, s16[32,896]{1,0:T(8,128)(2,1)S(1)}) custom-call(bf16[16,3072]{1,0:T(8,128)(2,1)S(1)} %join.1.refs_0_, bf16[16,3072]{1,0:T(8,128)(2,1)S(1)} %collective-permute-done.13.refs_1_, bf16[16,3072]{1,0:T(8,128)(2,1)S(1)} %collective-permute-done.14.refs_2_, bf16[16,3072]{1,0:T(8,128)(2,1)S(1)} %collective-permute-done.15.refs_3_, ...), custom_call_target="tpu_custom_call" | custom-call | flops 301989888 | bytes 393216 | tf_op jit(solution)/shard_map/output_part/pallas_call | solution.py:23
  59.3 1.6 %collective-permute-start.17 = (s16[32,896]{1,0:T(8,128)(2,1)S(1)}, s16[32,896]{1,0:T(8,128)(2,1)S(1)}, u32[]{:S(2)}, u32[]{:S(2)}) collective-permute-start(s16[32,896]{1,0:T(8,128)(2,1)S(1)} %get-tuple-element.54), channel_id=1, source_target_pairs={{0,1},{1,0},{2,3},{3,2},{4,5},{5,4},{6,7},{7,6},{8,9},{9,8},{10,11... | collective-permute-start | bytes 172040 | tf_op jit(solution)/shard_map/ppermute | solution.py:49
  61.2 1.9 %collective-permute-start.21 = (s16[16,2176]{1,0:T(8,128)(2,1)S(1)}, s16[16,2176]{1,0:T(8,128)(2,1)S(1)}, u32[]{:S(2)}, u32[]{:S(2)}) collective-permute-start(s16[16,2176]{1,0:T(8,128)(2,1)S(1)} %get-tuple-element.60), channel_id=1, source_target_pairs={{0,2},{1,3},{2,0},{3,1},{4,6},{5,7},{6,4},{7,5},{8,10},{9,11},{10,... | collective-permute-start | bytes 208904 | tf_op jit(solution)/shard_map/ppermute | solution.py:49
  63.1 0.7 %finish.3.refs_0_ = bf16[16,4608]{1,0:T(8,128)(2,1)} custom-call(f32[16,1792]{1,0:T(8,128)S(1)} %get-tuple-element.52.refs_5_.kept_ref, s16[16,1920]{1,0:T(8,128)(2,1)S(1)} %collective-permute-done.18.came_ref), custom_call_target="tpu_custom_call" | custom-call | bytes 229376 | tf_op jit(solution)/shard_map/finish/pallas_call | solution.py:463
  64.0 2.0 %collective-permute-start.19 = (s16[16,896]{1,0:T(8,128)(2,1)S(1)}, s16[16,896]{1,0:T(8,128)(2,1)S(1)}, u32[]{:S(2)}, u32[]{:S(2)}) collective-permute-start(s16[16,896]{1,0:T(8,128)(2,1)S(1)} %get-tuple-element.57), channel_id=1, source_target_pairs={{0,2},{1,3},{2,0},{3,1},{4,6},{5,7},{6,4},{7,5},{8,10},{9,11},{10,... | collective-permute-start | bytes 86024 | tf_op jit(solution)/shard_map/ppermute | solution.py:49
  65.9 1.8 %collective-permute-done.21.came_ref = s16[16,2176]{1,0:T(8,128)(2,1)S(1)} collective-permute-done((s16[16,2176]{1,0:T(8,128)(2,1)S(1)}, s16[16,2176]{1,0:T(8,128)(2,1)S(1)}, u32[]{:S(2)}, u32[]{:S(2)}) %collective-permute-start.21) | collective-permute-done | bytes 69664 | tf_op jit(solution)/shard_map/ppermute | solution.py:49
  67.7 0.7 %finish.4.refs_0_ = bf16[16,4608]{1,0:T(8,128)(2,1)} custom-call(f32[16,2048]{1,0:T(8,128)S(1)} %get-tuple-element.59.kept_ref, s16[16,2176]{1,0:T(8,128)(2,1)S(1)} %collective-permute-done.21.came_ref, bf16[16,4608]{1,0:T(8,128)(2,1)} %finish.3.refs_0_), custom_call_target="tpu_custom_call", output_to_operand_aliasing={{}: (2, {})} | custom-call | bytes 262144 | tf_op jit(solution)/shard_map/finish/pallas_call | solution.py:463
  (54 shorter events, 5.1 us)
Async XLA Ops:
  2.0 6.1 %copy-start = (bf16[64,4608]{1,0:T(8,128)(2,1)S(1)}, bf16[64,4608]{1,0:T(8,128)(2,1)}, u32[]{:S(2)}) copy-start(bf16[64,4608]{1,0:T(8,128)(2,1)} %refs_4_.5) | copy-start | bytes 1769476
  2.0 5.5 %collective-permute-start.2 = (f32[2,64]{1,0:T(2,128)S(1)}, f32[2,64]{1,0:T(2,128)S(1)}, u32[]{:S(2)}, u32[]{:S(2)}) collective-permute-start(f32[2,64]{1,0:T(2,128)S(1)} %row_sums.1.refs_0_), channel_id=1, source_target_pairs={{0,12},{4,8},{8,4},{12,0},{1,13},{5,9},{9,5},{13,1},{2,14},{6,10},... | collective-permute-start | bytes 1544 | tf_op jit(solution)/shard_map/ppermute | solution.py:49
  4.5 3.6 %collective-permute-start.1 = (f32[2,64]{1,0:T(2,128)S(1)}, f32[2,64]{1,0:T(2,128)S(1)}, u32[]{:S(2)}, u32[]{:S(2)}) collective-permute-start(f32[2,64]{1,0:T(2,128)S(1)} %row_sums.1.refs_0_), channel_id=1, source_target_pairs={{0,8},{4,12},{8,0},{12,4},{1,9},{5,13},{9,1},{13,5},{2,10},{6,14},... | collective-permute-start | bytes 1544 | tf_op jit(solution)/shard_map/ppermute | solution.py:49
  5.1 2.9 %collective-permute-start = (f32[2,64]{1,0:T(2,128)S(1)}, f32[2,64]{1,0:T(2,128)S(1)}, u32[]{:S(2)}, u32[]{:S(2)}) collective-permute-start(f32[2,64]{1,0:T(2,128)S(1)} %row_sums.1.refs_0_), channel_id=1, source_target_pairs={{0,4},{4,0},{8,12},{12,8},{1,5},{5,1},{9,13},{13,9},{2,6},{6,2},{1... | collective-permute-start | bytes 1544 | tf_op jit(solution)/shard_map/ppermute | solution.py:49
  16.7 1.6 %collective-permute-start.3 = (f32[32,2048]{1,0:T(8,128)S(1)}, f32[32,2048]{1,0:T(8,128)S(1)}, u32[]{:S(2)}, u32[]{:S(2)}) collective-permute-start(f32[32,2048]{1,0:T(8,128)S(1)} %get-tuple-element.34), channel_id=1, source_target_pairs={{0,4},{4,0},{8,12},{12,8},{1,5},{5,1},{9,13},{13,9},{2,6},{6,2},{1... | collective-permute-start | bytes 786440 | tf_op jit(solution)/shard_map/ppermute | solution.py:49
  16.8 2.9 %collective-permute-start.5 = (f32[32,1536]{1,0:T(8,128)S(1)}, f32[32,1536]{1,0:T(8,128)S(1)}, u32[]{:S(2)}, u32[]{:S(2)}) collective-permute-start(f32[32,1536]{1,0:T(8,128)S(1)} %get-tuple-element.38), channel_id=1, source_target_pairs={{0,4},{4,0},{8,12},{12,8},{1,5},{5,1},{9,13},{13,9},{2,6},{6,2},{1... | collective-permute-start | bytes 589832 | tf_op jit(solution)/shard_map/ppermute | solution.py:49
  18.3 7.7 %collective-permute-start.4 = (f32[16,2048]{1,0:T(8,128)S(1)}, f32[16,2048]{1,0:T(8,128)S(1)}, u32[]{:S(2)}, u32[]{:S(2)}) collective-permute-start(f32[16,2048]{1,0:T(8,128)S(1)} %get-tuple-element.36), channel_id=1, source_target_pairs={{0,8},{4,12},{8,0},{12,4},{1,9},{5,13},{9,1},{13,5},{2,10},{6,14},... | collective-permute-start | bytes 393224 | tf_op jit(solution)/shard_map/ppermute | solution.py:49
  19.7 6.4 %collective-permute-start.6 = (f32[16,1536]{1,0:T(8,128)S(1)}, f32[16,1536]{1,0:T(8,128)S(1)}, u32[]{:S(2)}, u32[]{:S(2)}) collective-permute-start(f32[16,1536]{1,0:T(8,128)S(1)} %get-tuple-element.40), channel_id=1, source_target_pairs={{0,8},{4,12},{8,0},{12,4},{1,9},{5,13},{9,1},{13,5},{2,10},{6,14},... | collective-permute-start | bytes 294920 | tf_op jit(solution)/shard_map/ppermute | solution.py:49
  26.0 8.5 %copy-start.3 = (bf16[4,1024,512]{2,1,0:T(8,128)(2,1)S(1)}, bf16[4,1024,512]{2,1,0:T(8,128)(2,1)}, u32[]{:S(2)}) copy-start(bf16[4,1024,512]{2,1,0:T(8,128)(2,1)} %refs_4_.6) | copy-start | bytes 12582916
  26.0 8.5 %copy-start.4 = (s32[4]{0:T(128)S(1)}, s32[4]{0:T(128)}, u32[]{:S(2)}) copy-start(s32[4]{0:T(128)} %param.13) | copy-start | bytes 52
  26.0 23.3 %slice-start = ((s8[28311552]{0:T(1024)(128)(4,1)}), s8[4194304]{0:T(1024)(128)(4,1)S(1)}, s32[]{:S(2)}) async-start(s8[28311552]{0:T(1024)(128)(4,1)} %bitcast.1), calls=%async_computation | async-start | bytes 8388608
  26.0 23.3 %slice-start.1 = ((s8[28311552]{0:T(1024)(128)(4,1)}), s8[4194304]{0:T(1024)(128)(4,1)S(1)}, s32[]{:S(2)}) async-start(s8[28311552]{0:T(1024)(128)(4,1)} %bitcast.1), calls=%async_computation.1 | async-start | bytes 8388608
  26.1 23.3 %slice-start.2 = ((s8[28311552]{0:T(1024)(128)(4,1)}), s8[4194304]{0:T(1024)(128)(4,1)S(1)}, s32[]{:S(2)}) async-start(s8[28311552]{0:T(1024)(128)(4,1)} %bitcast.1), calls=%async_computation.2 | async-start | bytes 8388608
  26.1 4.9 %collective-permute-start.7 = (bf16[8,2048]{1,0:T(8,128)(2,1)S(1)}, bf16[8,2048]{1,0:T(8,128)(2,1)S(1)}, u32[]{:S(2)}, u32[]{:S(2)}) collective-permute-start(bf16[8,2048]{1,0:T(8,128)(2,1)S(1)} %get-tuple-element.41), channel_id=1, source_target_pairs={{0,2},{1,3},{2,0},{3,1},{4,6},{5,7},{6,4},{7,5},{8,10},{9,11},{10,... | collective-permute-start | bytes 98312 | tf_op jit(solution)/shard_map/ppermute | solution.py:49
  28.8 5.7 %collective-permute-start.8 = (bf16[8,2048]{1,0:T(8,128)(2,1)S(1)}, bf16[8,2048]{1,0:T(8,128)(2,1)S(1)}, u32[]{:S(2)}, u32[]{:S(2)}) collective-permute-start(bf16[8,2048]{1,0:T(8,128)(2,1)S(1)} %get-tuple-element.42), channel_id=1, source_target_pairs={{0,3},{1,2},{2,1},{3,0},{4,7},{5,6},{6,5},{7,4},{8,11},{9,10},{10,... | collective-permute-start | bytes 98312 | tf_op jit(solution)/shard_map/ppermute | solution.py:49
  30.1 4.4 %collective-permute-start.9 = (bf16[8,2048]{1,0:T(8,128)(2,1)S(1)}, bf16[8,2048]{1,0:T(8,128)(2,1)S(1)}, u32[]{:S(2)}, u32[]{:S(2)}) collective-permute-start(bf16[8,2048]{1,0:T(8,128)(2,1)S(1)} %get-tuple-element.43), channel_id=1, source_target_pairs={{0,1},{1,0},{2,3},{3,2},{4,5},{5,4},{6,7},{7,6},{8,9},{9,8},{10,11... | collective-permute-start | bytes 98312 | tf_op jit(solution)/shard_map/ppermute | solution.py:49
  34.5 14.9 %slice-start.3 = ((s8[28311552]{0:T(1024)(128)(4,1)}), s8[4194304]{0:T(1024)(128)(4,1)S(1)}, s32[]{:S(2)}) async-start(s8[28311552]{0:T(1024)(128)(4,1)} %bitcast.1), calls=%async_computation.3 | async-start | bytes 8388608
  34.5 14.9 %slice-start.4 = ((s8[28311552]{0:T(1024)(128)(4,1)}), s8[4194304]{0:T(1024)(128)(4,1)S(1)}, s32[]{:S(2)}) async-start(s8[28311552]{0:T(1024)(128)(4,1)} %bitcast.1), calls=%async_computation.4 | async-start | bytes 8388608
  36.4 4.8 %collective-permute-start.10 = (bf16[8,1536]{1,0:T(8,128)(2,1)S(1)}, bf16[8,1536]{1,0:T(8,128)(2,1)S(1)}, u32[]{:S(2)}, u32[]{:S(2)}) collective-permute-start(bf16[8,1536]{1,0:T(8,128)(2,1)S(1)} %get-tuple-element.45), channel_id=1, source_target_pairs={{0,2},{1,3},{2,0},{3,1},{4,6},{5,7},{6,4},{7,5},{8,10},{9,11},{10,... | collective-permute-start | bytes 73736 | tf_op jit(solution)/shard_map/ppermute | solution.py:49
  37.7 5.6 %collective-permute-start.11 = (bf16[8,1536]{1,0:T(8,128)(2,1)S(1)}, bf16[8,1536]{1,0:T(8,128)(2,1)S(1)}, u32[]{:S(2)}, u32[]{:S(2)}) collective-permute-start(bf16[8,1536]{1,0:T(8,128)(2,1)S(1)} %get-tuple-element.46), channel_id=1, source_target_pairs={{0,3},{1,2},{2,1},{3,0},{4,7},{5,6},{6,5},{7,4},{8,11},{9,10},{10,... | collective-permute-start | bytes 73736 | tf_op jit(solution)/shard_map/ppermute | solution.py:49
  38.7 4.6 %collective-permute-start.12 = (bf16[8,1536]{1,0:T(8,128)(2,1)S(1)}, bf16[8,1536]{1,0:T(8,128)(2,1)S(1)}, u32[]{:S(2)}, u32[]{:S(2)}) collective-permute-start(bf16[8,1536]{1,0:T(8,128)(2,1)S(1)} %get-tuple-element.47), channel_id=1, source_target_pairs={{0,1},{1,0},{2,3},{3,2},{4,5},{5,4},{6,7},{7,6},{8,9},{9,8},{10,11... | collective-permute-start | bytes 73736 | tf_op jit(solution)/shard_map/ppermute | solution.py:49
  43.3 6.1 %slice-start.5 = ((s8[28311552]{0:T(1024)(128)(4,1)}), s8[4194304]{0:T(1024)(128)(4,1)S(1)}, s32[]{:S(2)}) async-start(s8[28311552]{0:T(1024)(128)(4,1)} %bitcast.1), calls=%async_computation.5 | async-start | bytes 8388608
  43.3 6.1 %slice-start.6 = ((s8[28311552]{0:T(1024)(128)(4,1)}), s8[3145728]{0:T(1024)(128)(4,1)S(1)}, s32[]{:S(2)}) async-start(s8[28311552]{0:T(1024)(128)(4,1)} %bitcast.1), calls=%async_computation.6 | async-start | bytes 6291456
  43.4 4.7 %collective-permute-start.14 = (bf16[16,3072]{1,0:T(8,128)(2,1)S(1)}, bf16[16,3072]{1,0:T(8,128)(2,1)S(1)}, u32[]{:S(2)}, u32[]{:S(2)}) collective-permute-start(bf16[16,3072]{1,0:T(8,128)(2,1)S(1)} %join.1.refs_0_), channel_id=1, source_target_pairs={{0,8},{4,12},{8,0},{12,4},{1,9},{5,13},{9,1},{13,5},{2,10},{6,14},... | collective-permute-start | bytes 294920 | tf_op jit(solution)/shard_map/ppermute | solution.py:49
  44.7 3.4 %collective-permute-start.13 = (bf16[16,3072]{1,0:T(8,128)(2,1)S(1)}, bf16[16,3072]{1,0:T(8,128)(2,1)S(1)}, u32[]{:S(2)}, u32[]{:S(2)}) collective-permute-start(bf16[16,3072]{1,0:T(8,128)(2,1)S(1)} %join.1.refs_0_), channel_id=1, source_target_pairs={{0,4},{4,0},{8,12},{12,8},{1,5},{5,1},{9,13},{13,9},{2,6},{6,2},{1... | collective-permute-start | bytes 294920 | tf_op jit(solution)/shard_map/ppermute | solution.py:49
  48.1 1.3 %collective-permute-start.15 = (bf16[16,3072]{1,0:T(8,128)(2,1)S(1)}, bf16[16,3072]{1,0:T(8,128)(2,1)S(1)}, u32[]{:S(2)}, u32[]{:S(2)}) collective-permute-start(bf16[16,3072]{1,0:T(8,128)(2,1)S(1)} %collective-permute-done.14.refs_2_), channel_id=1, source_target_pairs={{0,4},{4,0},{8,12},{12,8},{1,5},{5,1},{9,13},{13,9},{2,6},{6,2},{1... | collective-permute-start | bytes 294920 | tf_op jit(solution)/shard_map/ppermute | solution.py:49
  51.6 5.4 %collective-permute-start.16 = (s16[32,1920]{1,0:T(8,128)(2,1)S(1)}, s16[32,1920]{1,0:T(8,128)(2,1)S(1)}, u32[]{:S(2)}, u32[]{:S(2)}) collective-permute-start(s16[32,1920]{1,0:T(8,128)(2,1)S(1)} %get-tuple-element.50), channel_id=1, source_target_pairs={{0,1},{1,0},{2,3},{3,2},{4,5},{5,4},{6,7},{7,6},{8,9},{9,8},{10,11... | collective-permute-start | bytes 368648 | tf_op jit(solution)/shard_map/ppermute | solution.py:49
  54.5 6.5 %collective-permute-start.20 = (s16[32,2176]{1,0:T(8,128)(2,1)S(1)}, s16[32,2176]{1,0:T(8,128)(2,1)S(1)}, u32[]{:S(2)}, u32[]{:S(2)}) collective-permute-start(s16[32,2176]{1,0:T(8,128)(2,1)S(1)} %get-tuple-element.58), channel_id=1, source_target_pairs={{0,1},{1,0},{2,3},{3,2},{4,5},{5,4},{6,7},{7,6},{8,9},{9,8},{10,11... | collective-permute-start | bytes 417800 | tf_op jit(solution)/shard_map/ppermute | solution.py:49
  57.2 5.9 %collective-permute-start.18 = (s16[16,1920]{1,0:T(8,128)(2,1)S(1)}, s16[16,1920]{1,0:T(8,128)(2,1)S(1)}, u32[]{:S(2)}, u32[]{:S(2)}) collective-permute-start(s16[16,1920]{1,0:T(8,128)(2,1)S(1)} %get-tuple-element.55), channel_id=1, source_target_pairs={{0,2},{1,3},{2,0},{3,1},{4,6},{5,7},{6,4},{7,5},{8,10},{9,11},{10,... | collective-permute-start | bytes 184328 | tf_op jit(solution)/shard_map/ppermute | solution.py:49
  59.3 4.5 %collective-permute-start.17 = (s16[32,896]{1,0:T(8,128)(2,1)S(1)}, s16[32,896]{1,0:T(8,128)(2,1)S(1)}, u32[]{:S(2)}, u32[]{:S(2)}) collective-permute-start(s16[32,896]{1,0:T(8,128)(2,1)S(1)} %get-tuple-element.54), channel_id=1, source_target_pairs={{0,1},{1,0},{2,3},{3,2},{4,5},{5,4},{6,7},{7,6},{8,9},{9,8},{10,11... | collective-permute-start | bytes 172040 | tf_op jit(solution)/shard_map/ppermute | solution.py:49
  61.2 6.5 %collective-permute-start.21 = (s16[16,2176]{1,0:T(8,128)(2,1)S(1)}, s16[16,2176]{1,0:T(8,128)(2,1)S(1)}, u32[]{:S(2)}, u32[]{:S(2)}) collective-permute-start(s16[16,2176]{1,0:T(8,128)(2,1)S(1)} %get-tuple-element.60), channel_id=1, source_target_pairs={{0,2},{1,3},{2,0},{3,1},{4,6},{5,7},{6,4},{7,5},{8,10},{9,11},{10,... | collective-permute-start | bytes 208904 | tf_op jit(solution)/shard_map/ppermute | solution.py:49
  64.0 4.8 %collective-permute-start.19 = (s16[16,896]{1,0:T(8,128)(2,1)S(1)}, s16[16,896]{1,0:T(8,128)(2,1)S(1)}, u32[]{:S(2)}, u32[]{:S(2)}) collective-permute-start(s16[16,896]{1,0:T(8,128)(2,1)S(1)} %get-tuple-element.57), channel_id=1, source_target_pairs={{0,2},{1,3},{2,0},{3,1},{4,6},{5,7},{6,4},{7,5},{8,10},{9,11},{10,... | collective-permute-start | bytes 86024 | tf_op jit(solution)/shard_map/ppermute | solution.py:49
  (2 other events, 12.1 us)
